TPU v7x, 32 devices: a whole 2x2x4 slice. The times are simulated.
32 devices in a mesh: blk: 8 (over z, y), col: 4 (over x, core).
Axes of the slice: x: 2, y: 2, z: 4, core: 2. Of those that a mesh axis runs over, the one named last changes fastest.
Arguments:
- y_start: float32 [128, 16384], P('col', 'blk')
- tile_real: bfloat16 [768, 256, 256], P('blk'), may hold values from 0 to 1, as said below
- tile_imag: bfloat16 [768, 256, 256], P('blk'), may hold values from -1 to 1, as said below
- tile_rows: int32 [768], P('blk'), may hold values from 0 to 7
- tile_slots: int32 [768], P('blk'), may hold values from 0 to 15, as said below
- fetch_pick: int32 [8, 8], P('blk'), may hold values from 0 to 7
Outputs:
- encodings: float32 [128, 16384], P('col', 'blk')
Inputs may be any that keep to these rules, and one draw needn't show every extreme that they name: `tile_slots`: on each device the first 16 of its 96 tiles name an own row block (0 to 7); the others name 8 + p for an owning device p other than itself; every device reads from the devices 1, 4 and -1 places away along blk, modulo the axis. `tile_real`: entries are 0 or 1. `tile_imag`: entries are -1, 0 or 1, and never nonzero where tile_real is nonzero.
All inputs are finite; a program needn't handle non-finite values.
Results may differ from a plain program's by a relative error of at most 0.0031.
Values may be sent and summed in bfloat16 or wider, within the bound.
No kernel may reach another device: no remote copies, remote signals or barrier semaphores. Data moves between devices by JAX's collectives and lax.ppermute only.
A program may use at most 128 MiB of HBM per device.

v0:
```python
import functools
import math

import jax
import jax.numpy as jnp
from jax import lax
from jax.experimental import pallas as pl
from jax.experimental.pallas import tpu as pltpu
from jax.sharding import PartitionSpec as P

LOC_RB = 2
STEPS = 4
UNROLL = 4
CHUNK = 4
DIRECT = 8
MIB = 1 << 20

center = 1.25
half_width = 0.75

F32 = jnp.float32
BF16 = jnp.bfloat16
I32 = jnp.int32

VMEM = pl.BlockSpec(memory_space=pltpu.VMEM)
SMEM = pl.BlockSpec(memory_space=pltpu.SMEM)
ANY = pl.BlockSpec(memory_space=pl.ANY)

NT = (((1,), (1,)), ((), ()))
TN = (((0,), (0,)), ((), ()))


def sds(shape, dtype):
    return jax.ShapeDtypeStruct(shape, dtype)


def resident(x):
    return pltpu.with_memory_space_constraint(x, pltpu.VMEM)


def params(limit):
    return pltpu.CompilerParams(vmem_limit_bytes=limit * MIB)


def turn_rows(values):
    rows = values.shape[0]
    even = lax.broadcasted_iota(I32, values.shape, 0) % 2 == 0
    below = pltpu.roll(values, rows - 1, 0)
    above = pltpu.roll(values, 1, 0)
    return jnp.where(even, -below, above)


def turn_lanes(values):
    lanes = values.shape[1]
    even = lax.broadcasted_iota(I32, values.shape, 1) % 2 == 0
    after = pltpu.roll(values, lanes - 1, 1)
    before = pltpu.roll(values, 1, 1)
    return jnp.where(even, after, -before)


def tiles_kernel(
    near_count,
    direct,
    rows_ref,
    slots_ref,
    real_hbm,
    imag_hbm,
    real_ref,
    imag_ref,
    scale_ref,
    plan_ref,
    present_ref,
    first_ref,
    sems,
):
    tiles, order, _ = real_ref.shape
    rb_dev = present_ref.shape[0]
    me = lax.axis_index("blk")
    nblk = lax.axis_size("blk")
    slots = rb_dev + nblk
    chunks = tiles // CHUNK

    def copies(c):
        at = pl.ds(c * CHUNK, CHUNK)
        return (
            pltpu.make_async_copy(real_hbm.at[at], real_ref.at[at], sems.at[c, 0]),
            pltpu.make_async_copy(imag_hbm.at[at], imag_ref.at[at], sems.at[c, 1]),
        )

    for c in range(chunks):
        for copy in copies(c):
            copy.start()

    def clear(key, _):
        first_ref[key] = -1
        return _

    lax.fori_loop(0, rb_dev * slots, clear, 0)
    present_ref[...] = jnp.zeros_like(present_ref)

    def source(slot):
        owner = slot - rb_dev
        other = rb_dev + (owner ^ me if direct else owner)
        return jnp.where(slot < rb_dev, slot, other)

    def one(t, listed):
        row = rows_ref[t]
        slot = slots_ref[t]
        key = row * slots + slot
        seen = first_ref[key]
        real = real_ref[t]
        imag = imag_ref[t]
        present_ref[row] = present_ref[row] + (jnp.abs(real) + jnp.abs(imag))

        @pl.when(seen >= 0)
        def _():
            real_ref[seen] = real_ref[seen] + real_ref[t]
            imag_ref[seen] = imag_ref[seen] + imag_ref[t]

        @pl.when(seen < 0)
        def _():
            first_ref[key] = t
            plan_ref[listed] = t | (row << 8) | (source(slot) << 16)

        return listed + (seen < 0).astype(I32)

    def chunk(c, listed):
        for copy in copies(c):
            copy.wait()
        for j in range(CHUNK):
            listed = one(c * CHUNK + j, listed)
        return listed

    def pad(listed):
        short = (UNROLL - listed % UNROLL) % UNROLL
        for j in range(UNROLL - 1):

            @pl.when(j < short)
            def _():
                plan_ref[listed + j] = slots << 16

        return listed + short

    header = 2
    near = pad(lax.fori_loop(0, near_count // CHUNK, chunk, header - header))
    plan_ref[plan_ref.shape[0] - 2] = near // UNROLL
    both = pad(lax.fori_loop(near_count // CHUNK, chunks, chunk, near))
    plan_ref[plan_ref.shape[0] - 1] = both // UNROLL

    ones = jnp.ones((8, order), BF16)
    for r in range(rb_dev):
        degree = lax.dot_general(ones, present_ref[r], NT, preferred_element_type=F32)
        scale_ref[:, r * order : (r + 1) * order] = 1.0 / jnp.sqrt(jnp.maximum(degree, 1.0))


def tiles_call(rows, slots, real, imag, near_count, direct):
    tiles, order, _ = real.shape
    rb_dev = rows.shape[0] // 12
    nblk = lax.axis_size("blk")
    return pl.pallas_call(
        functools.partial(tiles_kernel, near_count, direct),
        name="tiles",
        out_shape=(
            pltpu.VMEM(real.shape, BF16),
            pltpu.VMEM(imag.shape, BF16),
            sds((8, rb_dev * order), F32),
            sds((tiles + 32,), I32),
        ),
        in_specs=[SMEM, SMEM, ANY, ANY],
        out_specs=(VMEM, VMEM, VMEM, SMEM),
        scratch_shapes=[
            pltpu.VMEM((rb_dev, order, order), BF16),
            pltpu.SMEM((rb_dev * (rb_dev + nblk),), I32),
            pltpu.SemaphoreType.DMA((tiles // CHUNK, 2)),
        ],
        compiler_params=params(12),
        cost_estimate=pl.CostEstimate(flops=1 << 28, bytes_accessed=2 * real.size * 2, transcendentals=0),
    )(rows, slots, real, imag)


def send_blocks(field, scale_ref, sent_ref, pick, out_refs):
    order = sent_ref.shape[2]
    for r in range(sent_ref.shape[0]):
        at = slice(r * order, (r + 1) * order)
        sent_ref[r] = (field[:, at] * scale_ref[0:1, at]).astype(BF16)
    if len(out_refs) == 1:
        out = out_refs[0]
        for p in range(out.shape[0]):
            out[p] = sent_ref[pick(p)]
    else:
        for s, out in enumerate(out_refs, 1):
            out[0] = sent_ref[pick(s)]


def first_kernel(pieces, y_ref, scale_ref, *refs):
    wanted = refs[:pieces]
    sent_ref, picks_ref = refs[pieces], refs[pieces + 1]
    out_refs = refs[pieces + 2 :]
    me = lax.axis_index("blk")
    if len(out_refs) == 1:
        for p in range(picks_ref.shape[0]):
            picks_ref[p] = wanted[0][0, p]
    else:
        picks_ref[0] = 0
        for s in range(1, len(out_refs) + 1):
            picks_ref[s] = wanted[s - 1][0, me]
    send_blocks(y_ref, scale_ref, sent_ref, lambda s: picks_ref[s], out_refs)


def multiply(plan_ref, lo, hi, real_ref, imag_ref, load, acc_re, acc_im):
    def group(i, _):
        done = []
        for j in range(UNROLL):
            code = plan_ref[i * UNROLL + j]
            tile = code & 255
            x = load(code >> 16)
            re = lax.dot_general(x, real_ref[tile], NT, preferred_element_type=F32)
            im = lax.dot_general(x, imag_ref[tile], NT, preferred_element_type=F32)
            done.append(((code >> 8) & 255, re, im))
        for row, re, im in done:
            acc_re[row] = acc_re[row] + re
            acc_im[row] = acc_im[row] + im
        return _

    lax.fori_loop(lo, hi, group, 0)


def near_kernel(plan_ref, real_ref, imag_ref, sent_ref, acc_re, acc_im, x_ref):
    rb_dev = sent_ref.shape[0]
    x_ref[0:rb_dev] = sent_ref[...]
    x_ref[rb_dev] = jnp.zeros_like(x_ref[rb_dev])
    acc_re[...] = jnp.zeros_like(acc_re)
    acc_im[...] = jnp.zeros_like(acc_im)
    end = plan_ref[plan_ref.shape[0] - 2]
    multiply(
        plan_ref, 0, end, real_ref, imag_ref, lambda c: x_ref[jnp.minimum(c, rb_dev)], acc_re, acc_im
    )


def step_kernel(pieces, step, rb_dev, *refs):
    (plan_ref, picks_ref, real_ref, imag_ref, scale_ref, near_re, near_im, now_ref, before_ref) = refs[:9]
    arrived = refs[9 : 9 + pieces]
    next_ref = refs[9 + pieces]
    last = step == STEPS - 1
    sent_ref = None if last else refs[10 + pieces]
    out_refs = refs[10 + pieces : -3] if last else refs[11 + pieces : -3]
    x_ref, acc_re, acc_im = refs[-3:]
    order = near_re.shape[2]
    if pieces == 1:
        count = arrived[0].shape[0]
        x_ref[0:count] = arrived[0][...]
    else:
        count = pieces + 1
        for s in range(1, count):
            x_ref[s] = arrived[s - 1][0]
    x_ref[count] = jnp.zeros_like(x_ref[count])
    acc_re[...] = near_re[...]
    acc_im[...] = near_im[...]
    lo = plan_ref[plan_ref.shape[0] - 2]
    hi = plan_ref[plan_ref.shape[0] - 1]
    multiply(plan_ref, lo, hi, real_ref, imag_ref, lambda c: x_ref[c - rb_dev], acc_re, acc_im)
    for r in range(rb_dev):
        at = slice(r * order, (r + 1) * order)
        now = now_ref[:, at]
        applied = scale_ref[0:1, at] * (acc_re[r] + turn_rows(acc_im[r]))
        moved = ((1.0 - center) * now - applied) / half_width
        next_ref[:, at] = moved if step == 0 else 2.0 * moved - before_ref[:, at]
    if not last:
        send_blocks(next_ref, scale_ref, sent_ref, lambda s: picks_ref[s], out_refs)


def all_rows(own_ref, arrived, all_ref):
    c = lax.axis_index("col")
    all_ref[c] = own_ref[...].astype(BF16)
    for s, ref in enumerate(arrived, 1):
        all_ref[c ^ s] = ref[...]
    n, group, rows = all_ref.shape
    return all_ref[...].reshape(n * group, rows)


def gram_kernel(own_ref, *refs):
    arrived, (gram_ref, all_ref, full_ref) = refs[:-3], refs[-3:]
    rows = all_rows(own_ref, arrived, all_ref)
    full_ref[...] = lax.dot_general(rows, rows, NT, preferred_element_type=F32)
    half = gram_ref.shape[0]
    even = full_ref[pl.ds(0, half, stride=2), :]
    odd = full_ref[pl.ds(1, half, stride=2), :]
    gram_ref[...] = even + turn_lanes(odd)


PANEL = 16


def factor_kernel(grams, nodes, own_ref, *refs):
    parts = refs[:grams]
    arrived = refs[grams:-4]
    out_ref, all_ref, work_ref, inverse_ref = refs[-4:]
    group = own_ref.shape[0]
    order = work_ref.shape[0]
    total = parts[0][...]
    for part in parts[1:]:
        total = total + part[...]
    half = total.shape[0]
    work_ref[pl.ds(0, half, stride=2), :] = total
    work_ref[pl.ds(1, half, stride=2), :] = -turn_lanes(total)
    row_at = lax.broadcasted_iota(I32, (order, order), 0)
    lane_at = lax.broadcasted_iota(I32, (order, order), 1)
    inverse_ref[...] = (row_at == lane_at).astype(F32)
    here = lax.broadcasted_iota(I32, (PANEL, 1), 0)
    for top in range(0, order, PANEL):
        panel = jnp.concatenate([work_ref[top : top + PANEL, :], inverse_ref[top : top + PANEL, :]], axis=1)
        for k in range(0, PANEL, 2):
            lane = top + k
            left = panel[:, lane : lane + 1]
            right = panel[:, lane + 1 : lane + 2]
            inv = lax.rsqrt(left[k : k + 1, :])
            inv2 = inv * inv
            below = here > k + 1
            pair = here - k
            a = jnp.where(below, left * inv2, 0.0)
            b = jnp.where(below, right * inv2, 0.0)
            keep = jnp.where((pair == 0) | (pair == 1), inv, 1.0)
            panel = panel * keep - (a * panel[k : k + 1, :] + b * panel[k + 1 : k + 2, :])
        inverse_ref[top : top + PANEL, :] = panel[:, order:]
        rest = top + PANEL
        if rest < order:
            cols = panel[:, 0:order]
            update = lax.dot_general(
                cols, panel, TN, precision=lax.Precision.HIGHEST, preferred_element_type=F32
            )
            work_ref[rest:, :] = work_ref[rest:, :] - update[rest:, :order]
            inverse_ref[rest:, :] = inverse_ref[rest:, :] - update[rest:, order:]
    c = lax.axis_index("col")
    mine = inverse_ref[pl.ds(pl.multiple_of(c * group, group), group), :]
    mine = mine * math.sqrt(nodes)
    high = mine.astype(BF16)
    low = (mine - high.astype(F32)).astype(BF16)
    rows = all_rows(own_ref, arrived, all_ref)
    both = lax.dot_general(
        jnp.concatenate([high, low], axis=0), rows, (((1,), (0,)), ((), ())), preferred_element_type=F32
    )
    own = own_ref[...]
    lost = own - own.astype(BF16).astype(F32)
    own_lanes = (
        lax.broadcasted_iota(I32, (order, group), 0)
        == lax.broadcasted_iota(I32, (order, group), 1) + c * group
    ).astype(BF16)
    square = jnp.dot(high, own_lanes, preferred_element_type=F32).astype(BF16)
    out_ref[...] = (
        both[:group] + both[group:] + jnp.dot(square, lost.astype(BF16), preferred_element_type=F32)
    )


def to_partner(x, axis, mask):
    n = lax.axis_size(axis)
    return lax.ppermute(x, axis, [(i, i ^ mask) for i in range(n)])


def per_device(y_start, tile_real, tile_imag, tile_rows, tile_slots, fetch_pick):
    group, rows = y_start.shape
    tiles, order, _ = tile_real.shape
    rb_dev = rows // order
    nblk = lax.axis_size("blk")
    ncol = lax.axis_size("col")
    direct = nblk <= DIRECT
    pieces = nblk - 1 if direct else 1
    near_count = LOC_RB * rb_dev

    if direct:
        wanted = [to_partner(fetch_pick, "blk", s) for s in range(1, nblk)]
        block_shapes = [sds((1, group, order), BF16)] * pieces
        sources = nblk
    else:
        wanted = [lax.all_to_all(fetch_pick, "blk", split_axis=1, concat_axis=1, tiled=True)]
        block_shapes = [sds((nblk, group, order), BF16)]
        sources = nblk

    def exchange(blocks):
        if direct:
            return [to_partner(b, "blk", s) for s, b in enumerate(blocks, 1)]
        return [lax.all_to_all(blocks[0], "blk", split_axis=0, concat_axis=0, tiled=True)]

    real, imag, scale, plan = tiles_call(tile_rows, tile_slots, tile_real, tile_imag, near_count, direct)

    out = pl.pallas_call(
        functools.partial(first_kernel, pieces),
        name="first",
        out_shape=(sds((rb_dev, group, order), BF16), sds((nblk,), I32), *block_shapes),
        in_specs=[VMEM, VMEM] + [SMEM] * pieces,
        out_specs=(VMEM, SMEM) + (VMEM,) * len(block_shapes),
        compiler_params=params(8),
    )(y_start, scale, *wanted)
    sent, picks, blocks = out[0], out[1], out[2:]

    acc = sds((rb_dev, group, order), F32)
    previous, current = y_start, y_start
    for step in range(STEPS):
        arrived = exchange(blocks)
        near_re, near_im = pl.pallas_call(
            near_kernel,
            name="near",
            out_shape=(acc, acc),
            in_specs=[SMEM, VMEM, VMEM, VMEM],
            out_specs=(VMEM, VMEM),
            scratch_shapes=[pltpu.VMEM((rb_dev + 1, group, order), BF16)],
            compiler_params=params(8),
            cost_estimate=pl.CostEstimate(flops=1 << 28, bytes_accessed=1 << 20, transcendentals=0),
        )(plan, resident(real), resident(imag), sent)
        last = step == STEPS - 1
        more = () if last else (sds((rb_dev, group, order), BF16), *block_shapes)
        out = pl.pallas_call(
            functools.partial(step_kernel, pieces, step, rb_dev),
            name="step",
            out_shape=(sds((group, rows), F32), *more),
            in_specs=[SMEM, SMEM] + [VMEM] * (7 + len(arrived)),
            out_specs=(VMEM,) * (1 + len(more)),
            scratch_shapes=[
                pltpu.VMEM((sources + 1, group, order), BF16),
                pltpu.VMEM((rb_dev, group, order), F32),
                pltpu.VMEM((rb_dev, group, order), F32),
            ],
            compiler_params=params(12),
        )(plan, picks, resident(real), resident(imag), scale, near_re, near_im, current, previous, *arrived)
        previous, current = current, out[0]
        if not last:
            sent, blocks = out[1], out[2:]

    rounded = current.astype(BF16)
    others = [to_partner(rounded, "col", s) for s in range(1, ncol)]
    vectors = group * ncol
    part = pl.pallas_call(
        gram_kernel,
        name="gram",
        out_shape=sds((vectors // 2, vectors), F32),
        in_specs=[VMEM] * (1 + len(others)),
        out_specs=VMEM,
        scratch_shapes=[pltpu.VMEM((ncol, group, rows), BF16), pltpu.VMEM((vectors, vectors), F32)],
        compiler_params=params(12),
    )(current, *others)
    wide = 1
    while wide < nblk:
        span = min(nblk // wide, DIRECT)
        parts = [part] + [to_partner(part, "blk", s * wide) for s in range(1, span)]
        wide *= span
        if wide < nblk:
            part = sum(parts[1:], parts[0])
    return pl.pallas_call(
        functools.partial(factor_kernel, len(parts), rows * nblk),
        name="factor",
        out_shape=sds((group, rows), F32),
        in_specs=[VMEM] * (1 + len(parts) + len(others)),
        out_specs=VMEM,
        scratch_shapes=[
            pltpu.VMEM((ncol, group, rows), BF16),
            pltpu.VMEM((vectors, vectors), F32),
            pltpu.VMEM((vectors, vectors), F32),
        ],
        compiler_params=params(12),
    )(current, *parts, *others)


def solution(mesh):
    return jax.shard_map(
        per_device,
        mesh=mesh,
        in_specs=(
            P("col", "blk"),
            P("blk", None, None),
            P("blk", None, None),
            P("blk"),
            P("blk"),
            P("blk", None),
        ),
        out_specs=P("col", "blk"),
        check_vma=False,
    )
```

profile of v0, /device:TPU:0, one launch (start us, length us, event | category | flops | bytes accessed | tf_op | source)
XLA Modules:
  0.0 156.9 jit_solution(9295861335731723745)
XLA Ops:
  0.0 5.0 %collective-permute-start.4 = (s32[1,8]{1,0:T(1,128)}, s32[1,8]{1,0:T(1,128)S(1)}, u32[]{:S(2)}, u32[]{:S(2)}) collective-permute-start(s32[1,8]{1,0:T(1,128)} %param.11), channel_id=1, source_target_pairs={{0,20},{4,16},{8,28},{12,24},{16,4},{20,0},{24,12},{28,8},{1,21},{... | collective-permute-start | bytes 104 | tf_op jit(solution)/shard_map/ppermute | solution.py:356
  8.8 4.6 %copy-done.2 = bf16[96,256,256]{2,1,0:T(8,128)(2,1)S(1)} copy-done((bf16[96,256,256]{2,1,0:T(8,128)(2,1)S(1)}, bf16[96,256,256]{2,1,0:T(8,128)(2,1)}, u32[]{:S(2)}) %copy-start.2) | copy-done | bytes 12582936
  14.7 8.0 %tiles.1 = (bf16[96,256,256]{2,1,0:T(8,128)(2,1)S(1)}, bf16[96,256,256]{2,1,0:T(8,128)(2,1)S(1)}, f32[8,2048]{1,0:T(8,128)S(1)}, s32[128]{0:T(128)S(1)}) custom-call(s32[96]{0:T(128)S(1)} %copy-done.4, s32[96]{0:T(128)S(1)} %copy-done.5, bf16[96,256,256]{2,1,0:T(8,128)(2,1)S(1)} %copy-done.2, bf16[96,256,256]{2,1,0:T(8,128)(2,1)} %imag_hbm.1), custom_call_target="tpu_custom_call" | custom-call | flops 268435456 | bytes 25165824 | tf_op jit(solution)/shard_map/tiles/pallas_call | solution.py:160
  22.8 3.5 %collective-permute-start.6 = (s32[1,8]{1,0:T(1,128)S(1)}, s32[1,8]{1,0:T(1,128)S(1)}, u32[]{:S(2)}, u32[]{:S(2)}) collective-permute-start(s32[1,8]{1,0:T(1,128)S(1)} %copy-done.6), channel_id=1, source_target_pairs={{0,28},{4,24},{8,20},{12,16},{16,12},{20,8},{24,4},{28,0},{1,29},{... | collective-permute-start | bytes 104 | tf_op jit(solution)/shard_map/ppermute | solution.py:356
  26.5 2.6 %collective-permute-done.6.refs_6_ = s32[1,8]{1,0:T(1,128)S(1)} collective-permute-done((s32[1,8]{1,0:T(1,128)S(1)}, s32[1,8]{1,0:T(1,128)S(1)}, u32[]{:S(2)}, u32[]{:S(2)}) %collective-permute-start.6) | collective-permute-done | bytes 64 | tf_op jit(solution)/shard_map/ppermute | solution.py:356
  36.4 3.9 %collective-permute-start.11 = (bf16[1,32,256]{2,1,0:T(8,128)(2,1)S(1)}, bf16[1,32,256]{2,1,0:T(8,128)(2,1)S(1)}, u32[]{:S(2)}, u32[]{:S(2)}) collective-permute-start(bf16[1,32,256]{2,1,0:T(8,128)(2,1)S(1)} %get-tuple-element.65), channel_id=1, source_target_pairs={{0,20},{4,16},{8,28},{12,24},{16,4},{20,0},{24,12},{28,8},{1,21},{... | collective-permute-start | bytes 49160 | tf_op jit(solution)/shard_map/ppermute | solution.py:356
  40.6 3.5 %collective-permute-start.13 = (bf16[1,32,256]{2,1,0:T(8,128)(2,1)S(1)}, bf16[1,32,256]{2,1,0:T(8,128)(2,1)S(1)}, u32[]{:S(2)}, u32[]{:S(2)}) collective-permute-start(bf16[1,32,256]{2,1,0:T(8,128)(2,1)S(1)} %get-tuple-element.67), channel_id=1, source_target_pairs={{0,28},{4,24},{8,20},{12,16},{16,12},{20,8},{24,4},{28,0},{1,29},{... | collective-permute-start | bytes 49160 | tf_op jit(solution)/shard_map/ppermute | solution.py:356
  47.0 4.6 %copy-done.1 = bf16[96,256,256]{2,1,0:T(8,128)(2,1)S(1)} copy-done((bf16[96,256,256]{2,1,0:T(8,128)(2,1)S(1)}, bf16[96,256,256]{2,1,0:T(8,128)(2,1)}, u32[]{:S(2)}) %copy-start.1) | copy-done | bytes 12582936
  51.6 5.4 %step.4 = (f32[32,2048]{1,0:T(8,128)S(1)}, bf16[8,32,256]{2,1,0:T(8,128)(2,1)S(1)}, bf16[1,32,256]{2,1,0:T(8,128)(2,1)S(1)}, bf16[1,32,256]{2,1,0:T(8,128)(2,1)S...) custom-call(s32[128]{0:T(128)S(1)} %get-tuple-element.53.plan_ref.re, ...), custom_call_target="tpu_custom_call" | custom-call | tf_op jit(solution)/shard_map/step/pallas_call | solution.py:411
  64.1 2.8 %collective-permute-start.19 = (bf16[1,32,256]{2,1,0:T(8,128)(2,1)S(1)}, bf16[1,32,256]{2,1,0:T(8,128)(2,1)S(1)}, u32[]{:S(2)}, u32[]{:S(2)}) collective-permute-start(bf16[1,32,256]{2,1,0:T(8,128)(2,1)S(1)} %get-tuple-element.77), channel_id=1, source_target_pairs={{0,24},{4,28},{8,16},{12,20},{16,8},{20,12},{24,0},{28,4},{1,25},{... | collective-permute-start | bytes 49160 | tf_op jit(solution)/shard_map/ppermute | solution.py:356
  70.1 3.3 %collective-permute-done.20.refs_15_ = bf16[1,32,256]{2,1,0:T(8,128)(2,1)S(1)} collective-permute-done((bf16[1,32,256]{2,1,0:T(8,128)(2,1)S(1)}, bf16[1,32,256]{2,1,0:T(8,128)(2,1)S(1)}, u32[]{:S(2)}, u32[]{:S(2)}) %collective-permute-start.20) | collective-permute-done | bytes 16416 | tf_op jit(solution)/shard_map/ppermute | solution.py:356
  73.4 5.4 %step.5 = (f32[32,2048]{1,0:T(8,128)S(1)}, bf16[8,32,256]{2,1,0:T(8,128)(2,1)S(1)}, bf16[1,32,256]{2,1,0:T(8,128)(2,1)S(1)}, bf16[1,32,256]{2,1,0:T(8,128)(2,1)S...) custom-call(s32[128]{0:T(128)S(1)} %get-tuple-element.53.plan_ref.re, ...), custom_call_target="tpu_custom_call" | custom-call | tf_op jit(solution)/shard_map/step/pallas_call | solution.py:411
  82.3 3.9 %collective-permute-start.25 = (bf16[1,32,256]{2,1,0:T(8,128)(2,1)S(1)}, bf16[1,32,256]{2,1,0:T(8,128)(2,1)S(1)}, u32[]{:S(2)}, u32[]{:S(2)}) collective-permute-start(bf16[1,32,256]{2,1,0:T(8,128)(2,1)S(1)} %get-tuple-element.87), channel_id=1, source_target_pairs={{0,20},{4,16},{8,28},{12,24},{16,4},{20,0},{24,12},{28,8},{1,21},{... | collective-permute-start | bytes 49160 | tf_op jit(solution)/shard_map/ppermute | solution.py:356
  86.5 3.4 %collective-permute-start.27 = (bf16[1,32,256]{2,1,0:T(8,128)(2,1)S(1)}, bf16[1,32,256]{2,1,0:T(8,128)(2,1)S(1)}, u32[]{:S(2)}, u32[]{:S(2)}) collective-permute-start(bf16[1,32,256]{2,1,0:T(8,128)(2,1)S(1)} %get-tuple-element.89), channel_id=1, source_target_pairs={{0,28},{4,24},{8,20},{12,16},{16,12},{20,8},{24,4},{28,0},{1,29},{... | collective-permute-start | bytes 49160 | tf_op jit(solution)/shard_map/ppermute | solution.py:356
  93.0 5.4 %step.6 = (f32[32,2048]{1,0:T(8,128)S(1)}, bf16[8,32,256]{2,1,0:T(8,128)(2,1)S(1)}, bf16[1,32,256]{2,1,0:T(8,128)(2,1)S(1)}, bf16[1,32,256]{2,1,0:T(8,128)(2,1)S...) custom-call(s32[128]{0:T(128)S(1)} %get-tuple-element.53.plan_ref.re, ...), custom_call_target="tpu_custom_call" | custom-call | tf_op jit(solution)/shard_map/step/pallas_call | solution.py:411
  105.5 2.8 %collective-permute-start.33 = (bf16[1,32,256]{2,1,0:T(8,128)(2,1)S(1)}, bf16[1,32,256]{2,1,0:T(8,128)(2,1)S(1)}, u32[]{:S(2)}, u32[]{:S(2)}) collective-permute-start(bf16[1,32,256]{2,1,0:T(8,128)(2,1)S(1)} %get-tuple-element.99), channel_id=1, source_target_pairs={{0,24},{4,28},{8,16},{12,20},{16,8},{20,12},{24,0},{28,4},{1,25},{... | collective-permute-start | bytes 49160 | tf_op jit(solution)/shard_map/ppermute | solution.py:356
  111.5 3.2 %collective-permute-done.34.refs_15_ = bf16[1,32,256]{2,1,0:T(8,128)(2,1)S(1)} collective-permute-done((bf16[1,32,256]{2,1,0:T(8,128)(2,1)S(1)}, bf16[1,32,256]{2,1,0:T(8,128)(2,1)S(1)}, u32[]{:S(2)}, u32[]{:S(2)}) %collective-permute-start.34) | collective-permute-done | bytes 16416 | tf_op jit(solution)/shard_map/ppermute | solution.py:356
  114.7 5.4 %step.7.own_ref = f32[32,2048]{1,0:T(8,128)S(1)} custom-call(s32[128]{0:T(128)S(1)} %get-tuple-element.53.plan_ref.refs_0_, s32[8]{0:T(128)S(1)} %get-tuple-element.55.refs_1_, bf16[96,256,256]{2,1,0:T(8,128)(2,1)S(1)} %get-tuple-element.56.real_ref.refs_2_, bf16[96,256,256]{2,1,0:T(8,128)(2,1)S(1)} %copy-done.1, ...), custom_call_target="tpu_custom_call" | custom-call | tf_op jit(solution)/shard_map/step/pallas_call | solution.py:411
  122.1 3.9 %collective-permute-done.37.refs_2_.refs_10_ = bf16[32,2048]{1,0:T(8,128)(2,1)S(1)} collective-permute-done((bf16[32,2048]{1,0:T(8,128)(2,1)S(1)}, bf16[32,2048]{1,0:T(8,128)(2,1)S(1)}, u32[]{:S(2)}, u32[]{:S(2)}) %collective-permute-start.37) | collective-permute-done | bytes 131104 | tf_op jit(solution)/shard_map/ppermute | solution.py:356
  126.0 2.9 %collective-permute-done.36.refs_1_.refs_9_ = bf16[32,2048]{1,0:T(8,128)(2,1)S(1)} collective-permute-done((bf16[32,2048]{1,0:T(8,128)(2,1)S(1)}, bf16[32,2048]{1,0:T(8,128)(2,1)S(1)}, u32[]{:S(2)}, u32[]{:S(2)}) %collective-permute-start.36) | collective-permute-done | bytes 131104 | tf_op jit(solution)/shard_map/ppermute | solution.py:356
  130.6 3.7 %collective-permute-start.43 = (f32[64,128]{1,0:T(8,128)S(1)}, f32[64,128]{1,0:T(8,128)S(1)}, u32[]{:S(2)}, u32[]{:S(2)}) collective-permute-start(f32[64,128]{1,0:T(8,128)S(1)} %gram.1.refs_0_), channel_id=1, source_target_pairs={{0,24},{4,28},{8,16},{12,20},{16,8},{20,12},{24,0},{28,4},{1,25},{... | collective-permute-start | bytes 98312 | tf_op jit(solution)/shard_map/ppermute | solution.py:356
  134.3 2.7 %collective-permute-start.41 = (f32[64,128]{1,0:T(8,128)S(1)}, f32[64,128]{1,0:T(8,128)S(1)}, u32[]{:S(2)}, u32[]{:S(2)}) collective-permute-start(f32[64,128]{1,0:T(8,128)S(1)} %gram.1.refs_0_), channel_id=1, source_target_pairs={{0,16},{4,20},{8,24},{12,28},{16,0},{20,4},{24,8},{28,12},{1,17},{... | collective-permute-start | bytes 98312 | tf_op jit(solution)/shard_map/ppermute | solution.py:356
  137.0 3.1 %collective-permute-start.39 = (f32[64,128]{1,0:T(8,128)S(1)}, f32[64,128]{1,0:T(8,128)S(1)}, u32[]{:S(2)}, u32[]{:S(2)}) collective-permute-start(f32[64,128]{1,0:T(8,128)S(1)} %gram.1.refs_0_), channel_id=1, source_target_pairs={{0,8},{4,12},{8,0},{12,4},{16,24},{20,28},{24,16},{28,20},{1,9},{5... | collective-permute-start | bytes 98312 | tf_op jit(solution)/shard_map/ppermute | solution.py:356
  144.0 12.8 %factor.1 = f32[32,2048]{1,0:T(8,128)} custom-call(f32[32,2048]{1,0:T(8,128)S(1)} %step.7.own_ref, f32[64,128]{1,0:T(8,128)S(1)} %gram.1.refs_0_, f32[64,128]{1,0:T(8,128)S(1)} %collective-permute-done.38.refs_1_, f32[64,128]{1,0:T(8,128)S(1)} %collective-permute-done.39.refs_2_, f32[64,128]{1,0:T(8,128)S(1)} %collective-permute-done.40.refs_3_, ...), custom_call_target="tpu_custom_call" | custom-call | tf_op jit(solution)/shard_map/factor/pallas_call | solution.py:447
  (93 shorter events, 50.8 us)
Async XLA Ops:
  0.0 22.7 %collective-permute-start.4 = (s32[1,8]{1,0:T(1,128)}, s32[1,8]{1,0:T(1,128)S(1)}, u32[]{:S(2)}, u32[]{:S(2)}) collective-permute-start(s32[1,8]{1,0:T(1,128)} %param.11), channel_id=1, source_target_pairs={{0,20},{4,16},{8,28},{12,24},{16,4},{20,0},{24,12},{28,8},{1,21},{... | collective-permute-start | bytes 104 | tf_op jit(solution)/shard_map/ppermute | solution.py:356
  5.0 21.3 %collective-permute-start.3 = (s32[1,8]{1,0:T(1,128)}, s32[1,8]{1,0:T(1,128)S(1)}, u32[]{:S(2)}, u32[]{:S(2)}) collective-permute-start(s32[1,8]{1,0:T(1,128)} %param.11), channel_id=1, source_target_pairs={{0,16},{4,20},{8,24},{12,28},{16,0},{20,4},{24,8},{28,12},{1,17},{... | collective-permute-start | bytes 104 | tf_op jit(solution)/shard_map/ppermute | solution.py:356
  5.3 21.1 %collective-permute-start.2 = (s32[1,8]{1,0:T(1,128)}, s32[1,8]{1,0:T(1,128)S(1)}, u32[]{:S(2)}, u32[]{:S(2)}) collective-permute-start(s32[1,8]{1,0:T(1,128)} %param.11), channel_id=1, source_target_pairs={{0,12},{4,8},{8,4},{12,0},{16,28},{20,24},{24,20},{28,16},{1,13},{... | collective-permute-start | bytes 104 | tf_op jit(solution)/shard_map/ppermute | solution.py:356
  6.8 19.6 %collective-permute-start.1 = (s32[1,8]{1,0:T(1,128)}, s32[1,8]{1,0:T(1,128)S(1)}, u32[]{:S(2)}, u32[]{:S(2)}) collective-permute-start(s32[1,8]{1,0:T(1,128)} %param.11), channel_id=1, source_target_pairs={{0,8},{4,12},{8,0},{12,4},{16,24},{20,28},{24,16},{28,20},{1,9},{5... | collective-permute-start | bytes 104 | tf_op jit(solution)/shard_map/ppermute | solution.py:356
  7.0 19.4 %collective-permute-start = (s32[1,8]{1,0:T(1,128)}, s32[1,8]{1,0:T(1,128)S(1)}, u32[]{:S(2)}, u32[]{:S(2)}) collective-permute-start(s32[1,8]{1,0:T(1,128)} %param.11), channel_id=1, source_target_pairs={{0,4},{4,0},{8,12},{12,8},{16,20},{20,16},{24,28},{28,24},{1,5},{5... | collective-permute-start | bytes 104 | tf_op jit(solution)/shard_map/ppermute | solution.py:356
  32.8 7.5 %collective-permute-start.7 = (bf16[1,32,256]{2,1,0:T(8,128)(2,1)S(1)}, bf16[1,32,256]{2,1,0:T(8,128)(2,1)S(1)}, u32[]{:S(2)}, u32[]{:S(2)}) collective-permute-start(bf16[1,32,256]{2,1,0:T(8,128)(2,1)S(1)} %get-tuple-element.61), channel_id=1, source_target_pairs={{0,4},{4,0},{8,12},{12,8},{16,20},{20,16},{24,28},{28,24},{1,5},{5... | collective-permute-start | bytes 49160 | tf_op jit(solution)/shard_map/ppermute | solution.py:356
  34.4 11.5 %collective-permute-start.9 = (bf16[1,32,256]{2,1,0:T(8,128)(2,1)S(1)}, bf16[1,32,256]{2,1,0:T(8,128)(2,1)S(1)}, u32[]{:S(2)}, u32[]{:S(2)}) collective-permute-start(bf16[1,32,256]{2,1,0:T(8,128)(2,1)S(1)} %get-tuple-element.63), channel_id=1, source_target_pairs={{0,12},{4,8},{8,4},{12,0},{16,28},{20,24},{24,20},{28,16},{1,13},{... | collective-permute-start | bytes 49160 | tf_op jit(solution)/shard_map/ppermute | solution.py:356
  36.4 9.6 %collective-permute-start.10 = (bf16[1,32,256]{2,1,0:T(8,128)(2,1)S(1)}, bf16[1,32,256]{2,1,0:T(8,128)(2,1)S(1)}, u32[]{:S(2)}, u32[]{:S(2)}) collective-permute-start(bf16[1,32,256]{2,1,0:T(8,128)(2,1)S(1)} %get-tuple-element.64), channel_id=1, source_target_pairs={{0,16},{4,20},{8,24},{12,28},{16,0},{20,4},{24,8},{28,12},{1,17},{... | collective-permute-start | bytes 49160 | tf_op jit(solution)/shard_map/ppermute | solution.py:356
  36.4 9.6 %collective-permute-start.11 = (bf16[1,32,256]{2,1,0:T(8,128)(2,1)S(1)}, bf16[1,32,256]{2,1,0:T(8,128)(2,1)S(1)}, u32[]{:S(2)}, u32[]{:S(2)}) collective-permute-start(bf16[1,32,256]{2,1,0:T(8,128)(2,1)S(1)} %get-tuple-element.65), channel_id=1, source_target_pairs={{0,20},{4,16},{8,28},{12,24},{16,4},{20,0},{24,12},{28,8},{1,21},{... | collective-permute-start | bytes 49160 | tf_op jit(solution)/shard_map/ppermute | solution.py:356
  58.2 8.7 %collective-permute-start.15 = (bf16[1,32,256]{2,1,0:T(8,128)(2,1)S(1)}, bf16[1,32,256]{2,1,0:T(8,128)(2,1)S(1)}, u32[]{:S(2)}, u32[]{:S(2)}) collective-permute-start(bf16[1,32,256]{2,1,0:T(8,128)(2,1)S(1)} %get-tuple-element.73), channel_id=1, source_target_pairs={{0,8},{4,12},{8,0},{12,4},{16,24},{20,28},{24,16},{28,20},{1,9},{5... | collective-permute-start | bytes 49160 | tf_op jit(solution)/shard_map/ppermute | solution.py:356
  58.2 11.8 %collective-permute-start.16 = (bf16[1,32,256]{2,1,0:T(8,128)(2,1)S(1)}, bf16[1,32,256]{2,1,0:T(8,128)(2,1)S(1)}, u32[]{:S(2)}, u32[]{:S(2)}) collective-permute-start(bf16[1,32,256]{2,1,0:T(8,128)(2,1)S(1)} %get-tuple-element.74), channel_id=1, source_target_pairs={{0,12},{4,8},{8,4},{12,0},{16,28},{20,24},{24,20},{28,16},{1,13},{... | collective-permute-start | bytes 49160 | tf_op jit(solution)/shard_map/ppermute | solution.py:356
  60.5 9.5 %collective-permute-start.17 = (bf16[1,32,256]{2,1,0:T(8,128)(2,1)S(1)}, bf16[1,32,256]{2,1,0:T(8,128)(2,1)S(1)}, u32[]{:S(2)}, u32[]{:S(2)}) collective-permute-start(bf16[1,32,256]{2,1,0:T(8,128)(2,1)S(1)} %get-tuple-element.75), channel_id=1, source_target_pairs={{0,16},{4,20},{8,24},{12,28},{16,0},{20,4},{24,8},{28,12},{1,17},{... | collective-permute-start | bytes 49160 | tf_op jit(solution)/shard_map/ppermute | solution.py:356
  62.6 7.5 %collective-permute-start.18 = (bf16[1,32,256]{2,1,0:T(8,128)(2,1)S(1)}, bf16[1,32,256]{2,1,0:T(8,128)(2,1)S(1)}, u32[]{:S(2)}, u32[]{:S(2)}) collective-permute-start(bf16[1,32,256]{2,1,0:T(8,128)(2,1)S(1)} %get-tuple-element.76), channel_id=1, source_target_pairs={{0,20},{4,16},{8,28},{12,24},{16,4},{20,0},{24,12},{28,8},{1,21},{... | collective-permute-start | bytes 49160 | tf_op jit(solution)/shard_map/ppermute | solution.py:356
  78.8 7.5 %collective-permute-start.21 = (bf16[1,32,256]{2,1,0:T(8,128)(2,1)S(1)}, bf16[1,32,256]{2,1,0:T(8,128)(2,1)S(1)}, u32[]{:S(2)}, u32[]{:S(2)}) collective-permute-start(bf16[1,32,256]{2,1,0:T(8,128)(2,1)S(1)} %get-tuple-element.83), channel_id=1, source_target_pairs={{0,4},{4,0},{8,12},{12,8},{16,20},{20,16},{24,28},{28,24},{1,5},{5... | collective-permute-start | bytes 49160 | tf_op jit(solution)/shard_map/ppermute | solution.py:356
  80.4 11.5 %collective-permute-start.23 = (bf16[1,32,256]{2,1,0:T(8,128)(2,1)S(1)}, bf16[1,32,256]{2,1,0:T(8,128)(2,1)S(1)}, u32[]{:S(2)}, u32[]{:S(2)}) collective-permute-start(bf16[1,32,256]{2,1,0:T(8,128)(2,1)S(1)} %get-tuple-element.85), channel_id=1, source_target_pairs={{0,12},{4,8},{8,4},{12,0},{16,28},{20,24},{24,20},{28,16},{1,13},{... | collective-permute-start | bytes 49160 | tf_op jit(solution)/shard_map/ppermute | solution.py:356
  82.3 9.5 %collective-permute-start.24 = (bf16[1,32,256]{2,1,0:T(8,128)(2,1)S(1)}, bf16[1,32,256]{2,1,0:T(8,128)(2,1)S(1)}, u32[]{:S(2)}, u32[]{:S(2)}) collective-permute-start(bf16[1,32,256]{2,1,0:T(8,128)(2,1)S(1)} %get-tuple-element.86), channel_id=1, source_target_pairs={{0,16},{4,20},{8,24},{12,28},{16,0},{20,4},{24,8},{28,12},{1,17},{... | collective-permute-start | bytes 49160 | tf_op jit(solution)/shard_map/ppermute | solution.py:356
  82.3 9.6 %collective-permute-start.25 = (bf16[1,32,256]{2,1,0:T(8,128)(2,1)S(1)}, bf16[1,32,256]{2,1,0:T(8,128)(2,1)S(1)}, u32[]{:S(2)}, u32[]{:S(2)}) collective-permute-start(bf16[1,32,256]{2,1,0:T(8,128)(2,1)S(1)} %get-tuple-element.87), channel_id=1, source_target_pairs={{0,20},{4,16},{8,28},{12,24},{16,4},{20,0},{24,12},{28,8},{1,21},{... | collective-permute-start | bytes 49160 | tf_op jit(solution)/shard_map/ppermute | solution.py:356
  99.6 8.7 %collective-permute-start.29 = (bf16[1,32,256]{2,1,0:T(8,128)(2,1)S(1)}, bf16[1,32,256]{2,1,0:T(8,128)(2,1)S(1)}, u32[]{:S(2)}, u32[]{:S(2)}) collective-permute-start(bf16[1,32,256]{2,1,0:T(8,128)(2,1)S(1)} %get-tuple-element.95), channel_id=1, source_target_pairs={{0,8},{4,12},{8,0},{12,4},{16,24},{20,28},{24,16},{28,20},{1,9},{5... | collective-permute-start | bytes 49160 | tf_op jit(solution)/shard_map/ppermute | solution.py:356
  99.6 11.9 %collective-permute-start.30 = (bf16[1,32,256]{2,1,0:T(8,128)(2,1)S(1)}, bf16[1,32,256]{2,1,0:T(8,128)(2,1)S(1)}, u32[]{:S(2)}, u32[]{:S(2)}) collective-permute-start(bf16[1,32,256]{2,1,0:T(8,128)(2,1)S(1)} %get-tuple-element.96), channel_id=1, source_target_pairs={{0,12},{4,8},{8,4},{12,0},{16,28},{20,24},{24,20},{28,16},{1,13},{... | collective-permute-start | bytes 49160 | tf_op jit(solution)/shard_map/ppermute | solution.py:356
  101.9 9.5 %collective-permute-start.31 = (bf16[1,32,256]{2,1,0:T(8,128)(2,1)S(1)}, bf16[1,32,256]{2,1,0:T(8,128)(2,1)S(1)}, u32[]{:S(2)}, u32[]{:S(2)}) collective-permute-start(bf16[1,32,256]{2,1,0:T(8,128)(2,1)S(1)} %get-tuple-element.97), channel_id=1, source_target_pairs={{0,16},{4,20},{8,24},{12,28},{16,0},{20,4},{24,8},{28,12},{1,17},{... | collective-permute-start | bytes 49160 | tf_op jit(solution)/shard_map/ppermute | solution.py:356
  104.1 7.4 %collective-permute-start.32 = (bf16[1,32,256]{2,1,0:T(8,128)(2,1)S(1)}, bf16[1,32,256]{2,1,0:T(8,128)(2,1)S(1)}, u32[]{:S(2)}, u32[]{:S(2)}) collective-permute-start(bf16[1,32,256]{2,1,0:T(8,128)(2,1)S(1)} %get-tuple-element.98), channel_id=1, source_target_pairs={{0,20},{4,16},{8,28},{12,24},{16,4},{20,0},{24,12},{28,8},{1,21},{... | collective-permute-start | bytes 49160 | tf_op jit(solution)/shard_map/ppermute | solution.py:356
  120.2 8.6 %collective-permute-start.36 = (bf16[32,2048]{1,0:T(8,128)(2,1)S(1)}, bf16[32,2048]{1,0:T(8,128)(2,1)S(1)}, u32[]{:S(2)}, u32[]{:S(2)}) collective-permute-start(bf16[32,2048]{1,0:T(8,128)(2,1)S(1)} %convert_element_type.3), channel_id=1, source_target_pairs={{0,2},{1,3},{2,0},{3,1},{4,6},{5,7},{6,4},{7,5},{8,10},{9,11},{10,... | collective-permute-start | bytes 393224 | tf_op jit(solution)/shard_map/ppermute | solution.py:356
  129.3 7.7 %collective-permute-start.44 = (f32[64,128]{1,0:T(8,128)S(1)}, f32[64,128]{1,0:T(8,128)S(1)}, u32[]{:S(2)}, u32[]{:S(2)}) collective-permute-start(f32[64,128]{1,0:T(8,128)S(1)} %gram.1.refs_0_), channel_id=1, source_target_pairs={{0,28},{4,24},{8,20},{12,16},{16,12},{20,8},{24,4},{28,0},{1,29},{... | collective-permute-start | bytes 98312 | tf_op jit(solution)/shard_map/ppermute | solution.py:356
  130.6 9.5 %collective-permute-start.43 = (f32[64,128]{1,0:T(8,128)S(1)}, f32[64,128]{1,0:T(8,128)S(1)}, u32[]{:S(2)}, u32[]{:S(2)}) collective-permute-start(f32[64,128]{1,0:T(8,128)S(1)} %gram.1.refs_0_), channel_id=1, source_target_pairs={{0,24},{4,28},{8,16},{12,20},{16,8},{20,12},{24,0},{28,4},{1,25},{... | collective-permute-start | bytes 98312 | tf_op jit(solution)/shard_map/ppermute | solution.py:356
  (28 other events, 185.3 us)
where the time goes:
time: 157 us
  starting transfers between devices  70.4 us (45%)
  Pallas kernels  51.5 us (33%)
  waiting for transfers between devices  24.2 us (15%)
  local copies, waits for them, and re-layouts  10.5 us (7%)
    ppermute x45, starting transfers between devices, to_partner(): return lax.ppermute(x, axis, [(i, i ^ mask) for i in range(n)])  70.4 us
    ppermute x45, waiting for transfers between devices, to_partner(): return lax.ppermute(x, axis, [(i, i ^ mask) for i in range(n)])  24.2 us
    pallas_call x4, Pallas kernels, per_device(): pl.pallas_call(functools.partial(step_kernel, pieces, step, rb_dev), name...  21.5 us
    pallas_call x1, Pallas kernels, per_device(): pl.pallas_call(functools.partial(factor_kernel, len(parts), rows * nblk),...  12.8 us
    unnamed x14, local copies, waits for them, and re-layouts  10.5 us
    pallas_call x1, Pallas kernels, tiles_call(): pl.pallas_call(functools.partial(tiles_kernel, near_count, direct), name=...  8 us
    pallas_call x4, Pallas kernels, per_device(): pl.pallas_call(near_kernel, name='near', out_shape=(acc, acc), in_specs=[...  7.49 us
  transfers between devices with their start and end apart: 45, of which 11 were waited for; matrix products, arithmetic and copies ran while one was open for 0% of the time, Pallas kernels for 10%

commit v1 on v0

--- a/solution.py
+++ b/solution.py
@@ -12,7 +12,7 @@
 STEPS = 4
 UNROLL = 4
 CHUNK = 4
-DIRECT = 8
+DIRECT = 1
 MIB = 1 << 20
 
 center = 1.25
@@ -175,7 +175,12 @@
         ],
         compiler_params=params(12),
         cost_estimate=pl.CostEstimate(flops=1 << 28, bytes_accessed=2 * real.size * 2, transcendentals=0),
-    )(rows, slots, real, imag)
+    )(
+        rows,
+        slots,
+        pltpu.with_memory_space_constraint(real, pltpu.HBM),
+        pltpu.with_memory_space_constraint(imag, pltpu.HBM),
+    )
 
 
 def send_blocks(field, scale_ref, sent_ref, pick, out_refs):
@@ -291,15 +296,14 @@
 PANEL = 16
 
 
-def factor_kernel(grams, nodes, own_ref, *refs):
-    parts = refs[:grams]
-    arrived = refs[grams:-4]
+def factor_kernel(nodes, own_ref, parts_ref, *refs):
+    arrived = refs[:-4]
     out_ref, all_ref, work_ref, inverse_ref = refs[-4:]
     group = own_ref.shape[0]
     order = work_ref.shape[0]
-    total = parts[0][...]
-    for part in parts[1:]:
-        total = total + part[...]
+    total = parts_ref[0]
+    for p in range(1, parts_ref.shape[0]):
+        total = total + parts_ref[p]
     half = total.shape[0]
     work_ref[pl.ds(0, half, stride=2), :] = total
     work_ref[pl.ds(1, half, stride=2), :] = -turn_lanes(total)
@@ -437,18 +441,13 @@
         scratch_shapes=[pltpu.VMEM((ncol, group, rows), BF16), pltpu.VMEM((vectors, vectors), F32)],
         compiler_params=params(12),
     )(current, *others)
-    wide = 1
-    while wide < nblk:
-        span = min(nblk // wide, DIRECT)
-        parts = [part] + [to_partner(part, "blk", s * wide) for s in range(1, span)]
-        wide *= span
-        if wide < nblk:
-            part = sum(parts[1:], parts[0])
+    spread = jnp.broadcast_to(part[None], (nblk,) + part.shape)
+    parts = lax.all_to_all(spread, "blk", split_axis=0, concat_axis=0, tiled=True)
     return pl.pallas_call(
-        functools.partial(factor_kernel, len(parts), rows * nblk),
+        functools.partial(factor_kernel, rows * nblk),
         name="factor",
         out_shape=sds((group, rows), F32),
-        in_specs=[VMEM] * (1 + len(parts) + len(others)),
+        in_specs=[VMEM] * (2 + len(others)),
         out_specs=VMEM,
         scratch_shapes=[
             pltpu.VMEM((ncol, group, rows), BF16),
@@ -456,7 +455,7 @@
             pltpu.VMEM((vectors, vectors), F32),
         ],
         compiler_params=params(12),
-    )(current, *parts, *others)
+    )(current, parts, *others)
 
 
 def solution(mesh):

time: 157 us -> 199 us (1.27)
  local copies, waits for them, and re-layouts: 10.5 us -> 84.9 us
  starting transfers between devices: 70.4 us -> 33.2 us
  waiting for transfers between devices: 24.2 us -> 6.77 us
  blocking collectives: 0 us -> 15 us
  Pallas kernels: 51.5 us -> 56.7 us
    unnamed x14 -> x42, local copies, waits for them, and re-layouts: 10.5 us -> 83.5 us
    ppermute x45 -> x3, starting transfers between devices: 70.4 us -> 1.92 us  [to_partner(): return lax.ppermute(x, axis, [(i, i ^ mask) for i in range(n)])]
    all_to_all x0 -> x5, starting transfers between devices: none -> 31.3 us  [the longest x4 24 us: exchange(): lax.all_to_all(blocks[0], 'blk', split_axis=0, concat_axis=0, tiled=True)]
    ppermute x45 -> x3, waiting for transfers between devices: 24.2 us -> 6.75 us  [to_partner(): return lax.ppermute(x, axis, [(i, i ^ mask) for i in range(n)])]
    all_to_all x0 -> x1, blocking collectives: none -> 15 us  [per_device(): lax.all_to_all(spread, 'blk', split_axis=0, concat_axis=0, tiled=True)]
  transfers between devices with their start and end apart: 45 -> 8, of which waited for: 11 -> 2; matrix products, arithmetic and copies ran while one was open for 0% -> 0% of each run, Pallas kernels for 10% -> 10%
where the time goes in v1:
time: 199 us; the launch traced here: 197 us
  local copies, waits for them, and re-layouts  84.9 us (43%)
  Pallas kernels  56.7 us (28%)
  starting transfers between devices  33.2 us (17%)
  blocking collectives  15 us (8%)
  waiting for transfers between devices  6.77 us (3%)
    unnamed x42, local copies, waits for them, and re-layouts  83.5 us
    all_to_all x4, starting transfers between devices, exchange(): lax.all_to_all(blocks[0], 'blk', split_axis=0, concat_axis=0, tiled=True)  24 us
    pallas_call x4, Pallas kernels, per_device(): pl.pallas_call(functools.partial(step_kernel, pieces, step, rb_dev), name...  23.3 us
    all_to_all x1, blocking collectives, per_device(): lax.all_to_all(spread, 'blk', split_axis=0, concat_axis=0, tiled=True)  15 us
    pallas_call x1, Pallas kernels, per_device(): pl.pallas_call(functools.partial(factor_kernel, rows * nblk), name='facto...  12.8 us
    pallas_call x1, Pallas kernels, tiles_call(): pl.pallas_call(functools.partial(tiles_kernel, near_count, direct), name=...  9.97 us
    pallas_call x4, Pallas kernels, per_device(): pl.pallas_call(near_kernel, name='near', out_shape=(acc, acc), in_specs=[...  9.02 us
    all_to_all x1, starting transfers between devices, per_device(): lax.all_to_all(fetch_pick, 'blk', split_axis=1, concat_axis=1, tiled=True)  7.28 us
  transfers between devices with their start and end apart: 8, of which 2 were waited for; matrix products, arithmetic and copies ran while one was open for 0% of the time, Pallas kernels for 10%

profile of v1, /device:TPU:0, one launch (start us, length us, event | category | flops | bytes accessed | tf_op | source)
XLA Modules:
  0.0 196.9 jit_solution(870266751540012791)
XLA Ops:
  1.3 7.3 %all-to-all-start = ((s32[1,8,1]{2,0,1:T(1,128)}), s32[1,8,1]{2,0,1:T(1,128)S(1)}, u32[]{:S(2)}, u32[]{:S(2)}) async-start(s32[1,8,1]{2,0,1:T(1,128)} %copy.8), calls=%async_computation | async-start | bytes 8192 | tf_op jit(solution)/shard_map/all_to_all | solution.py:378
  9.9 10.0 %tiles.1 = (bf16[96,256,256]{2,1,0:T(8,128)(2,1)S(1)}, bf16[96,256,256]{2,1,0:T(8,128)(2,1)S(1)}, f32[8,2048]{1,0:T(8,128)S(1)}, s32[128]{0:T(128)S(1)}) custom-call(s32[96]{0:T(128)S(1)} %copy-done.19, s32[96]{0:T(128)S(1)} %copy-done.20, bf16[96,256,256]{2,1,0:T(8,128)(2,1)} %real_hbm.1, bf16[96,256,256]{2,1,0:T(8,128)(2,1)} %imag_hbm.1), custom_call_target="tpu_custom_call" | custom-call | flops 268435456 | bytes 25165824 | tf_op jit(solution)/shard_map/tiles/pallas_call | solution.py:160
  30.4 6.0 %all-to-all-start.1 = ((bf16[8,32,256]{2,1,0:T(8,128)(2,1)}), bf16[8,32,256]{2,1,0:T(8,128)(2,1)S(1)}, u32[]{:S(2)}, u32[]{:S(2)}) async-start(bf16[8,32,256]{2,1,0:T(8,128)(2,1)} %get-tuple-element.37), calls=%async_computation.1 | async-start | bytes 262144 | tf_op jit(solution)/shard_map/all_to_all | solution.py:385
  36.4 4.6 %copy-done.1 = bf16[96,256,256]{2,1,0:T(8,128)(2,1)S(1)} copy-done((bf16[96,256,256]{2,1,0:T(8,128)(2,1)S(1)}, bf16[96,256,256]{2,1,0:T(8,128)(2,1)}, u32[]{:S(2)}) %copy-start.1) | copy-done | bytes 12582936
  41.0 4.6 %copy-done.10 = bf16[96,256,256]{2,1,0:T(8,128)(2,1)S(1)} copy-done((bf16[96,256,256]{2,1,0:T(8,128)(2,1)S(1)}, bf16[96,256,256]{2,1,0:T(8,128)(2,1)}, u32[]{:S(2)}) %copy-start.10) | copy-done | bytes 12582936
  52.4 4.6 %copy-done.11 = bf16[96,256,256]{2,1,0:T(8,128)(2,1)S(1)} copy-done((bf16[96,256,256]{2,1,0:T(8,128)(2,1)S(1)}, bf16[96,256,256]{2,1,0:T(8,128)(2,1)}, u32[]{:S(2)}) %copy-start.11) | copy-done | bytes 12582936
  57.0 6.0 %step.4 = (f32[32,2048]{1,0:T(8,128)S(1)}, bf16[8,32,256]{2,1,0:T(8,128)(2,1)S(1)}, bf16[8,32,256]{2,1,0:T(8,128)(2,1)}) custom-call(s32[128]{0:T(128)S(1)} %get-tuple-element.29.plan_ref.refs_0_, s32[8]{0:T(128)S(1)} %get-tuple-element.31.refs_1_, bf16[96,256,256]{2,1,0:T(8,128)(2,1)S(1)} %copy-done.2, bf16[96,256,256]{2,1,0:T(8,128)(2,1)S(1)} %copy-done.11, ...), custom_call_target="tpu_custom_call" | custom-call | tf_op jit(solution)/shard_map/step/pallas_call | solution.py:415
  63.0 6.0 %all-to-all-start.2 = ((bf16[8,32,256]{2,1,0:T(8,128)(2,1)}), bf16[8,32,256]{2,1,0:T(8,128)(2,1)S(1)}, u32[]{:S(2)}, u32[]{:S(2)}) async-start(bf16[8,32,256]{2,1,0:T(8,128)(2,1)} %get-tuple-element.42), calls=%async_computation.2 | async-start | bytes 262144 | tf_op jit(solution)/shard_map/all_to_all | solution.py:385
  69.0 4.6 %copy-done.3 = bf16[96,256,256]{2,1,0:T(8,128)(2,1)S(1)} copy-done((bf16[96,256,256]{2,1,0:T(8,128)(2,1)S(1)}, bf16[96,256,256]{2,1,0:T(8,128)(2,1)}, u32[]{:S(2)}) %copy-start.3) | copy-done | bytes 12582936
  73.6 4.6 %copy-done.12 = bf16[96,256,256]{2,1,0:T(8,128)(2,1)S(1)} copy-done((bf16[96,256,256]{2,1,0:T(8,128)(2,1)S(1)}, bf16[96,256,256]{2,1,0:T(8,128)(2,1)}, u32[]{:S(2)}) %copy-start.12) | copy-done | bytes 12582936
  85.0 4.6 %copy-done.13 = bf16[96,256,256]{2,1,0:T(8,128)(2,1)S(1)} copy-done((bf16[96,256,256]{2,1,0:T(8,128)(2,1)S(1)}, bf16[96,256,256]{2,1,0:T(8,128)(2,1)}, u32[]{:S(2)}) %copy-start.13) | copy-done | bytes 12582936
  89.6 6.0 %step.5 = (f32[32,2048]{1,0:T(8,128)S(1)}, bf16[8,32,256]{2,1,0:T(8,128)(2,1)S(1)}, bf16[8,32,256]{2,1,0:T(8,128)(2,1)}) custom-call(s32[128]{0:T(128)S(1)} %get-tuple-element.29.plan_ref.refs_0_, s32[8]{0:T(128)S(1)} %get-tuple-element.31.refs_1_, bf16[96,256,256]{2,1,0:T(8,128)(2,1)S(1)} %copy-done.4, bf16[96,256,256]{2,1,0:T(8,128)(2,1)S(1)} %copy-done.13, ...), custom_call_target="tpu_custom_call" | custom-call | tf_op jit(solution)/shard_map/step/pallas_call | solution.py:415
  95.5 6.0 %all-to-all-start.3 = ((bf16[8,32,256]{2,1,0:T(8,128)(2,1)}), bf16[8,32,256]{2,1,0:T(8,128)(2,1)S(1)}, u32[]{:S(2)}, u32[]{:S(2)}) async-start(bf16[8,32,256]{2,1,0:T(8,128)(2,1)} %get-tuple-element.47), calls=%async_computation.3 | async-start | bytes 262144 | tf_op jit(solution)/shard_map/all_to_all | solution.py:385
  101.5 4.6 %copy-done.5 = bf16[96,256,256]{2,1,0:T(8,128)(2,1)S(1)} copy-done((bf16[96,256,256]{2,1,0:T(8,128)(2,1)S(1)}, bf16[96,256,256]{2,1,0:T(8,128)(2,1)}, u32[]{:S(2)}) %copy-start.5) | copy-done | bytes 12582936
  106.1 4.6 %copy-done.14 = bf16[96,256,256]{2,1,0:T(8,128)(2,1)S(1)} copy-done((bf16[96,256,256]{2,1,0:T(8,128)(2,1)S(1)}, bf16[96,256,256]{2,1,0:T(8,128)(2,1)}, u32[]{:S(2)}) %copy-start.14) | copy-done | bytes 12582936
  117.5 4.6 %copy-done.15 = bf16[96,256,256]{2,1,0:T(8,128)(2,1)S(1)} copy-done((bf16[96,256,256]{2,1,0:T(8,128)(2,1)S(1)}, bf16[96,256,256]{2,1,0:T(8,128)(2,1)}, u32[]{:S(2)}) %copy-start.15) | copy-done | bytes 12582936
  122.1 6.0 %step.6 = (f32[32,2048]{1,0:T(8,128)S(1)}, bf16[8,32,256]{2,1,0:T(8,128)(2,1)S(1)}, bf16[8,32,256]{2,1,0:T(8,128)(2,1)}) custom-call(s32[128]{0:T(128)S(1)} %get-tuple-element.29.plan_ref.refs_0_, s32[8]{0:T(128)S(1)} %get-tuple-element.31.refs_1_, bf16[96,256,256]{2,1,0:T(8,128)(2,1)S(1)} %copy-done.6, bf16[96,256,256]{2,1,0:T(8,128)(2,1)S(1)} %copy-done.15, ...), custom_call_target="tpu_custom_call" | custom-call | tf_op jit(solution)/shard_map/step/pallas_call | solution.py:415
  128.1 6.0 %all-to-all-start.4 = ((bf16[8,32,256]{2,1,0:T(8,128)(2,1)}), bf16[8,32,256]{2,1,0:T(8,128)(2,1)S(1)}, u32[]{:S(2)}, u32[]{:S(2)}) async-start(bf16[8,32,256]{2,1,0:T(8,128)(2,1)} %get-tuple-element.52), calls=%async_computation.4 | async-start | bytes 262144 | tf_op jit(solution)/shard_map/all_to_all | solution.py:385
  134.1 4.6 %copy-done.7 = bf16[96,256,256]{2,1,0:T(8,128)(2,1)S(1)} copy-done((bf16[96,256,256]{2,1,0:T(8,128)(2,1)S(1)}, bf16[96,256,256]{2,1,0:T(8,128)(2,1)}, u32[]{:S(2)}) %copy-start.7) | copy-done | bytes 12582936
  138.7 4.6 %copy-done.16 = bf16[96,256,256]{2,1,0:T(8,128)(2,1)S(1)} copy-done((bf16[96,256,256]{2,1,0:T(8,128)(2,1)S(1)}, bf16[96,256,256]{2,1,0:T(8,128)(2,1)}, u32[]{:S(2)}) %copy-start.16) | copy-done | bytes 12582936
  150.1 4.6 %copy-done.17 = bf16[96,256,256]{2,1,0:T(8,128)(2,1)S(1)} copy-done((bf16[96,256,256]{2,1,0:T(8,128)(2,1)S(1)}, bf16[96,256,256]{2,1,0:T(8,128)(2,1)}, u32[]{:S(2)}) %copy-start.17) | copy-done | bytes 12582936
  154.7 5.3 %step.7.own_ref = f32[32,2048]{1,0:T(8,128)S(1)} custom-call(s32[128]{0:T(128)S(1)} %get-tuple-element.29.plan_ref.refs_0_, s32[8]{0:T(128)S(1)} %get-tuple-element.31.refs_1_, bf16[96,256,256]{2,1,0:T(8,128)(2,1)S(1)} %copy-done.8, bf16[96,256,256]{2,1,0:T(8,128)(2,1)S(1)} %copy-done.17, f32[8,2048]{1,0:T(8,128)S(1)} %get-tuple-element.30.scale_ref.refs_4_, ...), custom_call_target="tpu_custom_call" | custom-call | tf_op jit(solution)/shard_map/step/pallas_call | solution.py:415
  169.2 15.0 %all_to_all.36.parts_ref = f32[8,64,128]{2,1,0:T(8,128)S(1)} all-to-all(f32[8,64,128]{2,1,0:T(8,128)S(1)} %broadcast_in_dim.2), channel_id=1, replica_groups=mesh['blk'=8,'col'=4] {'blk'}, dimensions={0} | all-to-all | bytes 524288 | tf_op jit(solution)/shard_map/all_to_all | solution.py:445
  184.1 12.8 %factor.1 = f32[32,2048]{1,0:T(8,128)} custom-call(f32[32,2048]{1,0:T(8,128)S(1)} %step.7.own_ref, f32[8,64,128]{2,1,0:T(8,128)S(1)} %all_to_all.36.parts_ref, bf16[32,2048]{1,0:T(8,128)(2,1)S(1)} %collective-permute-done.refs_0_, bf16[32,2048]{1,0:T(8,128)(2,1)S(1)} %collective-permute-done.1.refs_1_, bf16[32,2048]{1,0:T(8,128)(2,1)S(1)} %collective-permute-done.2.refs_2_), custom_call_target="tpu_custom_call" | custom-call | tf_op jit(solution)/shard_map/factor/pallas_call | solution.py:446
  (51 shorter events, 49.6 us)
Async XLA Ops:
  1.3 27.6 %all-to-all-start = ((s32[1,8,1]{2,0,1:T(1,128)}), s32[1,8,1]{2,0,1:T(1,128)S(1)}, u32[]{:S(2)}, u32[]{:S(2)}) async-start(s32[1,8,1]{2,0,1:T(1,128)} %copy.8), calls=%async_computation | async-start | bytes 8192 | tf_op jit(solution)/shard_map/all_to_all | solution.py:378
  9.9 19.3 %copy-start.18 = (f32[32,2048]{1,0:T(8,128)S(1)}, f32[32,2048]{1,0:T(8,128)}, u32[]{:S(2)}) copy-start(f32[32,2048]{1,0:T(8,128)} %refs_8_.3) | copy-start | bytes 786436
  30.4 17.4 %all-to-all-start.1 = ((bf16[8,32,256]{2,1,0:T(8,128)(2,1)}), bf16[8,32,256]{2,1,0:T(8,128)(2,1)S(1)}, u32[]{:S(2)}, u32[]{:S(2)}) async-start(bf16[8,32,256]{2,1,0:T(8,128)(2,1)} %get-tuple-element.37), calls=%async_computation.1 | async-start | bytes 262144 | tf_op jit(solution)/shard_map/all_to_all | solution.py:385
  36.4 4.6 %copy-start.1 = (bf16[96,256,256]{2,1,0:T(8,128)(2,1)S(1)}, bf16[96,256,256]{2,1,0:T(8,128)(2,1)}, u32[]{:S(2)}) copy-start(bf16[96,256,256]{2,1,0:T(8,128)(2,1)} %copy-done) | copy-start | bytes 37748740
  41.0 4.6 %copy-start.10 = (bf16[96,256,256]{2,1,0:T(8,128)(2,1)S(1)}, bf16[96,256,256]{2,1,0:T(8,128)(2,1)}, u32[]{:S(2)}) copy-start(bf16[96,256,256]{2,1,0:T(8,128)(2,1)} %copy-done.9) | copy-start | bytes 37748740
  47.9 4.6 %copy-start.2 = (bf16[96,256,256]{2,1,0:T(8,128)(2,1)S(1)}, bf16[96,256,256]{2,1,0:T(8,128)(2,1)}, u32[]{:S(2)}) copy-start(bf16[96,256,256]{2,1,0:T(8,128)(2,1)} %copy-done) | copy-start | bytes 37748740
  52.4 4.6 %copy-start.11 = (bf16[96,256,256]{2,1,0:T(8,128)(2,1)S(1)}, bf16[96,256,256]{2,1,0:T(8,128)(2,1)}, u32[]{:S(2)}) copy-start(bf16[96,256,256]{2,1,0:T(8,128)(2,1)} %copy-done.9) | copy-start | bytes 37748740
  63.0 17.4 %all-to-all-start.2 = ((bf16[8,32,256]{2,1,0:T(8,128)(2,1)}), bf16[8,32,256]{2,1,0:T(8,128)(2,1)S(1)}, u32[]{:S(2)}, u32[]{:S(2)}) async-start(bf16[8,32,256]{2,1,0:T(8,128)(2,1)} %get-tuple-element.42), calls=%async_computation.2 | async-start | bytes 262144 | tf_op jit(solution)/shard_map/all_to_all | solution.py:385
  69.0 4.6 %copy-start.3 = (bf16[96,256,256]{2,1,0:T(8,128)(2,1)S(1)}, bf16[96,256,256]{2,1,0:T(8,128)(2,1)}, u32[]{:S(2)}) copy-start(bf16[96,256,256]{2,1,0:T(8,128)(2,1)} %copy-done) | copy-start | bytes 37748740
  73.6 4.6 %copy-start.12 = (bf16[96,256,256]{2,1,0:T(8,128)(2,1)S(1)}, bf16[96,256,256]{2,1,0:T(8,128)(2,1)}, u32[]{:S(2)}) copy-start(bf16[96,256,256]{2,1,0:T(8,128)(2,1)} %copy-done.9) | copy-start | bytes 37748740
  80.4 4.6 %copy-start.4 = (bf16[96,256,256]{2,1,0:T(8,128)(2,1)S(1)}, bf16[96,256,256]{2,1,0:T(8,128)(2,1)}, u32[]{:S(2)}) copy-start(bf16[96,256,256]{2,1,0:T(8,128)(2,1)} %copy-done) | copy-start | bytes 37748740
  85.0 4.6 %copy-start.13 = (bf16[96,256,256]{2,1,0:T(8,128)(2,1)S(1)}, bf16[96,256,256]{2,1,0:T(8,128)(2,1)}, u32[]{:S(2)}) copy-start(bf16[96,256,256]{2,1,0:T(8,128)(2,1)} %copy-done.9) | copy-start | bytes 37748740
  95.5 17.4 %all-to-all-start.3 = ((bf16[8,32,256]{2,1,0:T(8,128)(2,1)}), bf16[8,32,256]{2,1,0:T(8,128)(2,1)S(1)}, u32[]{:S(2)}, u32[]{:S(2)}) async-start(bf16[8,32,256]{2,1,0:T(8,128)(2,1)} %get-tuple-element.47), calls=%async_computation.3 | async-start | bytes 262144 | tf_op jit(solution)/shard_map/all_to_all | solution.py:385
  101.5 4.6 %copy-start.5 = (bf16[96,256,256]{2,1,0:T(8,128)(2,1)S(1)}, bf16[96,256,256]{2,1,0:T(8,128)(2,1)}, u32[]{:S(2)}) copy-start(bf16[96,256,256]{2,1,0:T(8,128)(2,1)} %copy-done) | copy-start | bytes 37748740
  106.1 4.6 %copy-start.14 = (bf16[96,256,256]{2,1,0:T(8,128)(2,1)S(1)}, bf16[96,256,256]{2,1,0:T(8,128)(2,1)}, u32[]{:S(2)}) copy-start(bf16[96,256,256]{2,1,0:T(8,128)(2,1)} %copy-done.9) | copy-start | bytes 37748740
  113.0 4.6 %copy-start.6 = (bf16[96,256,256]{2,1,0:T(8,128)(2,1)S(1)}, bf16[96,256,256]{2,1,0:T(8,128)(2,1)}, u32[]{:S(2)}) copy-start(bf16[96,256,256]{2,1,0:T(8,128)(2,1)} %copy-done) | copy-start | bytes 37748740
  117.5 4.6 %copy-start.15 = (bf16[96,256,256]{2,1,0:T(8,128)(2,1)S(1)}, bf16[96,256,256]{2,1,0:T(8,128)(2,1)}, u32[]{:S(2)}) copy-start(bf16[96,256,256]{2,1,0:T(8,128)(2,1)} %copy-done.9) | copy-start | bytes 37748740
  128.1 17.4 %all-to-all-start.4 = ((bf16[8,32,256]{2,1,0:T(8,128)(2,1)}), bf16[8,32,256]{2,1,0:T(8,128)(2,1)S(1)}, u32[]{:S(2)}, u32[]{:S(2)}) async-start(bf16[8,32,256]{2,1,0:T(8,128)(2,1)} %get-tuple-element.52), calls=%async_computation.4 | async-start | bytes 262144 | tf_op jit(solution)/shard_map/all_to_all | solution.py:385
  138.7 4.6 %copy-start.16 = (bf16[96,256,256]{2,1,0:T(8,128)(2,1)S(1)}, bf16[96,256,256]{2,1,0:T(8,128)(2,1)}, u32[]{:S(2)}) copy-start(bf16[96,256,256]{2,1,0:T(8,128)(2,1)} %copy-done.9) | copy-start | bytes 37748740
  145.5 4.6 %copy-start.8 = (bf16[96,256,256]{2,1,0:T(8,128)(2,1)S(1)}, bf16[96,256,256]{2,1,0:T(8,128)(2,1)}, u32[]{:S(2)}) copy-start(bf16[96,256,256]{2,1,0:T(8,128)(2,1)} %copy-done) | copy-start | bytes 37748740
  150.1 4.6 %copy-start.17 = (bf16[96,256,256]{2,1,0:T(8,128)(2,1)S(1)}, bf16[96,256,256]{2,1,0:T(8,128)(2,1)}, u32[]{:S(2)}) copy-start(bf16[96,256,256]{2,1,0:T(8,128)(2,1)} %copy-done.9) | copy-start | bytes 37748740
  160.0 5.8 %collective-permute-start.2 = (bf16[32,2048]{1,0:T(8,128)(2,1)S(1)}, bf16[32,2048]{1,0:T(8,128)(2,1)S(1)}, u32[]{:S(2)}, u32[]{:S(2)}) collective-permute-start(bf16[32,2048]{1,0:T(8,128)(2,1)S(1)} %convert_element_type.3), channel_id=1, source_target_pairs={{0,3},{1,2},{2,1},{3,0},{4,7},{5,6},{6,5},{7,4},{8,11},{9,10},{10,... | collective-permute-start | bytes 393224 | tf_op jit(solution)/shard_map/ppermute | solution.py:360
  160.1 8.6 %collective-permute-start.1 = (bf16[32,2048]{1,0:T(8,128)(2,1)S(1)}, bf16[32,2048]{1,0:T(8,128)(2,1)S(1)}, u32[]{:S(2)}, u32[]{:S(2)}) collective-permute-start(bf16[32,2048]{1,0:T(8,128)(2,1)S(1)} %convert_element_type.3), channel_id=1, source_target_pairs={{0,2},{1,3},{2,0},{3,1},{4,6},{5,7},{6,4},{7,5},{8,10},{9,11},{10,... | collective-permute-start | bytes 393224 | tf_op jit(solution)/shard_map/ppermute | solution.py:360
  161.7 7.0 %collective-permute-start = (bf16[32,2048]{1,0:T(8,128)(2,1)S(1)}, bf16[32,2048]{1,0:T(8,128)(2,1)S(1)}, u32[]{:S(2)}, u32[]{:S(2)}) collective-permute-start(bf16[32,2048]{1,0:T(8,128)(2,1)S(1)} %convert_element_type.3), channel_id=1, source_target_pairs={{0,1},{1,0},{2,3},{3,2},{4,5},{5,4},{6,7},{7,6},{8,9},{9,8},{10,11... | collective-permute-start | bytes 393224 | tf_op jit(solution)/shard_map/ppermute | solution.py:360
  (5 other events, 14.9 us)

commit v2 on v0

--- a/solution.py
+++ b/solution.py
@@ -12,8 +12,9 @@
 STEPS = 4
 UNROLL = 4
 CHUNK = 4
-DIRECT = 8
+STAGED = 8
 MIB = 1 << 20
+LIMIT = 8
 
 center = 1.25
 half_width = 0.75
@@ -65,15 +66,14 @@
     slots_ref,
     real_hbm,
     imag_hbm,
-    real_ref,
-    imag_ref,
+    both_ref,
     scale_ref,
     plan_ref,
     present_ref,
     first_ref,
     sems,
 ):
-    tiles, order, _ = real_ref.shape
+    tiles, order, _ = both_ref.shape
     rb_dev = present_ref.shape[0]
     me = lax.axis_index("blk")
     nblk = lax.axis_size("blk")
@@ -83,8 +83,8 @@
     def copies(c):
         at = pl.ds(c * CHUNK, CHUNK)
         return (
-            pltpu.make_async_copy(real_hbm.at[at], real_ref.at[at], sems.at[c, 0]),
-            pltpu.make_async_copy(imag_hbm.at[at], imag_ref.at[at], sems.at[c, 1]),
+            pltpu.make_async_copy(real_hbm.at[at], both_ref.at[at, :, 0:order], sems.at[c, 0]),
+            pltpu.make_async_copy(imag_hbm.at[at], both_ref.at[at, :, order : 2 * order], sems.at[c, 1]),
         )
 
     for c in range(chunks):
@@ -108,14 +108,12 @@
         slot = slots_ref[t]
         key = row * slots + slot
         seen = first_ref[key]
-        real = real_ref[t]
-        imag = imag_ref[t]
-        present_ref[row] = present_ref[row] + (jnp.abs(real) + jnp.abs(imag))
+        both = jnp.abs(both_ref[t])
+        present_ref[row] = present_ref[row] + (both[:, :order] + both[:, order:])
 
         @pl.when(seen >= 0)
         def _():
-            real_ref[seen] = real_ref[seen] + real_ref[t]
-            imag_ref[seen] = imag_ref[seen] + imag_ref[t]
+            both_ref[seen] = both_ref[seen] + both_ref[t]
 
         @pl.when(seen < 0)
         def _():
@@ -161,21 +159,25 @@
         functools.partial(tiles_kernel, near_count, direct),
         name="tiles",
         out_shape=(
-            pltpu.VMEM(real.shape, BF16),
-            pltpu.VMEM(imag.shape, BF16),
+            pltpu.VMEM((tiles, order, 2 * order), BF16),
             sds((8, rb_dev * order), F32),
             sds((tiles + 32,), I32),
         ),
         in_specs=[SMEM, SMEM, ANY, ANY],
-        out_specs=(VMEM, VMEM, VMEM, SMEM),
+        out_specs=(VMEM, VMEM, SMEM),
         scratch_shapes=[
             pltpu.VMEM((rb_dev, order, order), BF16),
             pltpu.SMEM((rb_dev * (rb_dev + nblk),), I32),
             pltpu.SemaphoreType.DMA((tiles // CHUNK, 2)),
         ],
-        compiler_params=params(12),
+        compiler_params=params(LIMIT),
         cost_estimate=pl.CostEstimate(flops=1 << 28, bytes_accessed=2 * real.size * 2, transcendentals=0),
-    )(rows, slots, real, imag)
+    )(
+        pltpu.with_memory_space_constraint(rows, pltpu.HBM),
+        pltpu.with_memory_space_constraint(slots, pltpu.HBM),
+        pltpu.with_memory_space_constraint(real, pltpu.HBM),
+        pltpu.with_memory_space_constraint(imag, pltpu.HBM),
+    )
 
 
 def send_blocks(field, scale_ref, sent_ref, pick, out_refs):
@@ -184,89 +186,94 @@
         at = slice(r * order, (r + 1) * order)
         sent_ref[r] = (field[:, at] * scale_ref[0:1, at]).astype(BF16)
     if len(out_refs) == 1:
-        out = out_refs[0]
+        (out,) = out_refs
         for p in range(out.shape[0]):
             out[p] = sent_ref[pick(p)]
     else:
-        for s, out in enumerate(out_refs, 1):
-            out[0] = sent_ref[pick(s)]
-
-
-def first_kernel(pieces, y_ref, scale_ref, *refs):
-    wanted = refs[:pieces]
-    sent_ref, picks_ref = refs[pieces], refs[pieces + 1]
-    out_refs = refs[pieces + 2 :]
+        beside, across = out_refs
+        me = lax.axis_index("blk")
+        for h in range(beside.shape[0]):
+            beside[h] = sent_ref[pick(me ^ (2 * h + 1))]
+        for h in range(1, beside.shape[0]):
+            across[h - 1] = sent_ref[pick(me ^ (2 * h))]
+
+
+def first_kernel(y_ref, scale_ref, wanted_ref, sent_ref, picks_ref, *out_refs):
     me = lax.axis_index("blk")
-    if len(out_refs) == 1:
-        for p in range(picks_ref.shape[0]):
-            picks_ref[p] = wanted[0][0, p]
-    else:
-        picks_ref[0] = 0
-        for s in range(1, len(out_refs) + 1):
-            picks_ref[s] = wanted[s - 1][0, me]
-    send_blocks(y_ref, scale_ref, sent_ref, lambda s: picks_ref[s], out_refs)
-
-
-def multiply(plan_ref, lo, hi, real_ref, imag_ref, load, acc_re, acc_im):
+    for p in range(picks_ref.shape[0]):
+        picks_ref[p] = wanted_ref[p, me]
+    send_blocks(y_ref, scale_ref, sent_ref, lambda p: picks_ref[p], out_refs)
+
+
+def merge_kernel(across_ref, passed_ref, *out_refs):
+    for h, out in enumerate(out_refs, 1):
+        out[0] = across_ref[h - 1]
+        out[1] = passed_ref[h]
+
+
+def put_source(x_ref, at, block):
+    order = block.shape[1]
+    x_ref[at, :, :order] = block
+    x_ref[at, :, order:] = turn_rows(block.astype(F32)).astype(BF16)
+
+
+def multiply(plan_ref, lo, hi, both_ref, load, acc_ref):
     def group(i, _):
         done = []
         for j in range(UNROLL):
             code = plan_ref[i * UNROLL + j]
             tile = code & 255
-            x = load(code >> 16)
-            re = lax.dot_general(x, real_ref[tile], NT, preferred_element_type=F32)
-            im = lax.dot_general(x, imag_ref[tile], NT, preferred_element_type=F32)
-            done.append(((code >> 8) & 255, re, im))
-        for row, re, im in done:
-            acc_re[row] = acc_re[row] + re
-            acc_im[row] = acc_im[row] + im
+            product = lax.dot_general(both_ref[tile], load(code >> 16), NT, preferred_element_type=F32)
+            done.append(((code >> 8) & 255, product))
+        for row, product in done:
+            acc_ref[row] = acc_ref[row] + product
         return _
 
     lax.fori_loop(lo, hi, group, 0)
 
 
-def near_kernel(plan_ref, real_ref, imag_ref, sent_ref, acc_re, acc_im, x_ref):
+def near_kernel(plan_ref, both_ref, sent_ref, acc_ref, x_ref):
     rb_dev = sent_ref.shape[0]
-    x_ref[0:rb_dev] = sent_ref[...]
+    for r in range(rb_dev):
+        put_source(x_ref, r, sent_ref[r])
     x_ref[rb_dev] = jnp.zeros_like(x_ref[rb_dev])
-    acc_re[...] = jnp.zeros_like(acc_re)
-    acc_im[...] = jnp.zeros_like(acc_im)
+    acc_ref[...] = jnp.zeros_like(acc_ref)
     end = plan_ref[plan_ref.shape[0] - 2]
-    multiply(
-        plan_ref, 0, end, real_ref, imag_ref, lambda c: x_ref[jnp.minimum(c, rb_dev)], acc_re, acc_im
-    )
+    multiply(plan_ref, 0, end, both_ref, lambda c: x_ref[jnp.minimum(c, rb_dev)], acc_ref)
 
 
 def step_kernel(pieces, step, rb_dev, *refs):
-    (plan_ref, picks_ref, real_ref, imag_ref, scale_ref, near_re, near_im, now_ref, before_ref) = refs[:9]
-    arrived = refs[9 : 9 + pieces]
-    next_ref = refs[9 + pieces]
+    (plan_ref, picks_ref, both_ref, scale_ref, near_ref, now_ref, before_ref) = refs[:7]
+    arrived = refs[7 : 7 + pieces]
+    next_ref = refs[7 + pieces]
     last = step == STEPS - 1
-    sent_ref = None if last else refs[10 + pieces]
-    out_refs = refs[10 + pieces : -3] if last else refs[11 + pieces : -3]
-    x_ref, acc_re, acc_im = refs[-3:]
-    order = near_re.shape[2]
+    sent_ref = None if last else refs[8 + pieces]
+    out_refs = () if last else refs[9 + pieces : -2]
+    x_ref, acc_ref = refs[-2:]
+    order = near_ref.shape[1]
     if pieces == 1:
         count = arrived[0].shape[0]
-        x_ref[0:count] = arrived[0][...]
+        for p in range(count):
+            put_source(x_ref, p, arrived[0][p])
     else:
-        count = pieces + 1
-        for s in range(1, count):
-            x_ref[s] = arrived[s - 1][0]
+        count = 2 * pieces
+        put_source(x_ref, 1, arrived[0][0])
+        for h in range(1, pieces):
+            put_source(x_ref, 2 * h, arrived[h][0])
+            put_source(x_ref, 2 * h + 1, arrived[h][1])
     x_ref[count] = jnp.zeros_like(x_ref[count])
-    acc_re[...] = near_re[...]
-    acc_im[...] = near_im[...]
+    acc_ref[...] = near_ref[...]
     lo = plan_ref[plan_ref.shape[0] - 2]
     hi = plan_ref[plan_ref.shape[0] - 1]
-    multiply(plan_ref, lo, hi, real_ref, imag_ref, lambda c: x_ref[c - rb_dev], acc_re, acc_im)
+    multiply(plan_ref, lo, hi, both_ref, lambda c: x_ref[c - rb_dev], acc_ref)
     for r in range(rb_dev):
         at = slice(r * order, (r + 1) * order)
         now = now_ref[:, at]
-        applied = scale_ref[0:1, at] * (acc_re[r] + turn_rows(acc_im[r]))
+        applied = scale_ref[0:1, at] * acc_ref[r].T
         moved = ((1.0 - center) * now - applied) / half_width
         next_ref[:, at] = moved if step == 0 else 2.0 * moved - before_ref[:, at]
     if not last:
-        send_blocks(next_ref, scale_ref, sent_ref, lambda s: picks_ref[s], out_refs)
+        send_blocks(next_ref, scale_ref, sent_ref, lambda p: picks_ref[p], out_refs)
 
 
 def all_rows(own_ref, arrived, all_ref):
@@ -362,71 +369,78 @@
     rb_dev = rows // order
     nblk = lax.axis_size("blk")
     ncol = lax.axis_size("col")
-    direct = nblk <= DIRECT
-    pieces = nblk - 1 if direct else 1
+    staged = nblk == STAGED
     near_count = LOC_RB * rb_dev
-
-    if direct:
-        wanted = [to_partner(fetch_pick, "blk", s) for s in range(1, nblk)]
-        block_shapes = [sds((1, group, order), BF16)] * pieces
-        sources = nblk
+    wanted = lax.all_gather(fetch_pick, "blk", axis=0, tiled=True)
+    half = nblk // 2
+    if staged:
+        block_shapes = [sds((half, group, order), BF16), sds((half - 1, group, order), BF16)]
+        pieces = half
     else:
-        wanted = [lax.all_to_all(fetch_pick, "blk", split_axis=1, concat_axis=1, tiled=True)]
         block_shapes = [sds((nblk, group, order), BF16)]
-        sources = nblk
+        pieces = 1
 
     def exchange(blocks):
-        if direct:
-            return [to_partner(b, "blk", s) for s, b in enumerate(blocks, 1)]
-        return [lax.all_to_all(blocks[0], "blk", split_axis=0, concat_axis=0, tiled=True)]
-
-    real, imag, scale, plan = tiles_call(tile_rows, tile_slots, tile_real, tile_imag, near_count, direct)
+        if not staged:
+            return [lax.all_to_all(blocks[0], "blk", split_axis=0, concat_axis=0, tiled=True)]
+        passed = to_partner(blocks[0], "blk", 1)
+        pairs = pl.pallas_call(
+            merge_kernel,
+            name="merge",
+            out_shape=[sds((2, group, order), BF16)] * (half - 1),
+            in_specs=[VMEM, VMEM],
+            out_specs=[VMEM] * (half - 1),
+            compiler_params=params(LIMIT),
+        )(blocks[1], passed)
+        return [passed] + [to_partner(pair, "blk", 2 * h) for h, pair in enumerate(pairs, 1)]
+
+    both, scale, plan = tiles_call(tile_rows, tile_slots, tile_real, tile_imag, near_count, staged)
 
     out = pl.pallas_call(
-        functools.partial(first_kernel, pieces),
+        first_kernel,
         name="first",
         out_shape=(sds((rb_dev, group, order), BF16), sds((nblk,), I32), *block_shapes),
-        in_specs=[VMEM, VMEM] + [SMEM] * pieces,
+        in_specs=[VMEM, VMEM, SMEM],
         out_specs=(VMEM, SMEM) + (VMEM,) * len(block_shapes),
-        compiler_params=params(8),
-    )(y_start, scale, *wanted)
+        compiler_params=params(LIMIT),
+    )(y_start, scale, pltpu.with_memory_space_constraint(wanted, pltpu.HBM))
     sent, picks, blocks = out[0], out[1], out[2:]
 
-    acc = sds((rb_dev, group, order), F32)
+    acc = (rb_dev, order, group)
     previous, current = y_start, y_start
     for step in range(STEPS):
         arrived = exchange(blocks)
-        near_re, near_im = pl.pallas_call(
+        near = pl.pallas_call(
             near_kernel,
             name="near",
-            out_shape=(acc, acc),
-            in_specs=[SMEM, VMEM, VMEM, VMEM],
-            out_specs=(VMEM, VMEM),
-            scratch_shapes=[pltpu.VMEM((rb_dev + 1, group, order), BF16)],
-            compiler_params=params(8),
+            out_shape=sds(acc, F32),
+            in_specs=[SMEM, VMEM, VMEM],
+            out_specs=VMEM,
+            scratch_shapes=[pltpu.VMEM((rb_dev + 1, group, 2 * order), BF16)],
+            compiler_params=params(LIMIT),
             cost_estimate=pl.CostEstimate(flops=1 << 28, bytes_accessed=1 << 20, transcendentals=0),
-        )(plan, resident(real), resident(imag), sent)
+        )(plan, resident(both), sent)
         last = step == STEPS - 1
         more = () if last else (sds((rb_dev, group, order), BF16), *block_shapes)
         out = pl.pallas_call(
             functools.partial(step_kernel, pieces, step, rb_dev),
             name="step",
             out_shape=(sds((group, rows), F32), *more),
-            in_specs=[SMEM, SMEM] + [VMEM] * (7 + len(arrived)),
+            in_specs=[SMEM, SMEM] + [VMEM] * (5 + len(arrived)),
             out_specs=(VMEM,) * (1 + len(more)),
-            scratch_shapes=[
-                pltpu.VMEM((sources + 1, group, order), BF16),
-                pltpu.VMEM((rb_dev, group, order), F32),
-                pltpu.VMEM((rb_dev, group, order), F32),
-            ],
-            compiler_params=params(12),
-        )(plan, picks, resident(real), resident(imag), scale, near_re, near_im, current, previous, *arrived)
+            scratch_shapes=[pltpu.VMEM((nblk + 1, group, 2 * order), BF16), pltpu.VMEM(acc, F32)],
+            compiler_params=params(LIMIT),
+        )(plan, picks, resident(both), scale, near, current, previous, *arrived)
         previous, current = current, out[0]
         if not last:
             sent, blocks = out[1], out[2:]
 
     rounded = current.astype(BF16)
-    others = [to_partner(rounded, "col", s) for s in range(1, ncol)]
+    if ncol == 4:
+        beside, across = to_partner(rounded, "col", 1), to_partner(rounded, "col", 2)
+        others = [beside, across, to_partner(across, "col", 1)]
+    else:
+        others = [to_partner(rounded, "col", s) for s in range(1, ncol)]
     vectors = group * ncol
     part = pl.pallas_call(
         gram_kernel,
@@ -435,15 +449,13 @@
         in_specs=[VMEM] * (1 + len(others)),
         out_specs=VMEM,
         scratch_shapes=[pltpu.VMEM((ncol, group, rows), BF16), pltpu.VMEM((vectors, vectors), F32)],
-        compiler_params=params(12),
+        compiler_params=params(LIMIT),
     )(current, *others)
     wide = 1
-    while wide < nblk:
-        span = min(nblk // wide, DIRECT)
-        parts = [part] + [to_partner(part, "blk", s * wide) for s in range(1, span)]
-        wide *= span
-        if wide < nblk:
-            part = sum(parts[1:], parts[0])
+    while 2 * wide < nblk:
+        part = part + to_partner(part, "blk", wide)
+        wide *= 2
+    parts = [part, to_partner(part, "blk", wide)] if wide < nblk else [part]
     return pl.pallas_call(
         functools.partial(factor_kernel, len(parts), rows * nblk),
         name="factor",
@@ -455,7 +467,7 @@
             pltpu.VMEM((vectors, vectors), F32),
             pltpu.VMEM((vectors, vectors), F32),
         ],
-        compiler_params=params(12),
+        compiler_params=params(LIMIT),
     )(current, *parts, *others)
 
 

time: 157 us -> 141 us (0.90)
  starting transfers between devices: 70.4 us -> 19.8 us
  blocking collectives: 0 us -> 22.9 us
  waiting for transfers between devices: 24.2 us -> 41 us
  local copies, waits for them, and re-layouts: 10.5 us -> 0.01 us
  Pallas kernels: 51.5 us -> 56.4 us
    ppermute x45 -> x22, starting transfers between devices: 70.4 us -> 19.8 us  [to_partner(): return lax.ppermute(x, axis, [(i, i ^ mask) for i in range(n)])]
    all_gather x0 -> x1, blocking collectives: none -> 22.9 us  [per_device(): wanted = lax.all_gather(fetch_pick, 'blk', axis=0, tiled=True)]
    ppermute x45 -> x22, waiting for transfers between devices: 24.2 us -> 41 us  [to_partner(): return lax.ppermute(x, axis, [(i, i ^ mask) for i in range(n)])]
    unnamed x14 -> x2, local copies, waits for them, and re-layouts: 10.5 us -> 0.01 us
    pallas_call x1, Pallas kernels: 8 us -> 10.2 us  [tiles_call(): pl.pallas_call(functools.partial(tiles_kernel, near_count, direct), name=...]
    pallas_call x5 -> x9, Pallas kernels: 8.69 us -> 10.6 us  [the longest x4 9.27 us: per_device(): pl.pallas_call(near_kernel, name='near', out_shape=sds(acc, F32), in_spec...]
  transfers between devices with their start and end apart: 45 -> 22, of which waited for: 11 -> 12; matrix products, arithmetic and copies ran while one was open for 0% -> 0% of each run, Pallas kernels for 10% -> 7%
where the time goes in v2:
time: 141 us; the launch traced here: 140 us
  Pallas kernels  56.4 us (40%)
  waiting for transfers between devices  41 us (29%)
  blocking collectives  22.9 us (16%)
  starting transfers between devices  19.8 us (14%)
    ppermute x22, waiting for transfers between devices, to_partner(): return lax.ppermute(x, axis, [(i, i ^ mask) for i in range(n)])  41 us
    all_gather x1, blocking collectives, per_device(): wanted = lax.all_gather(fetch_pick, 'blk', axis=0, tiled=True)  22.9 us
    pallas_call x4, Pallas kernels, per_device(): pl.pallas_call(functools.partial(step_kernel, pieces, step, rb_dev), name...  22.3 us
    ppermute x22, starting transfers between devices, to_partner(): return lax.ppermute(x, axis, [(i, i ^ mask) for i in range(n)])  19.8 us
    pallas_call x1, Pallas kernels, per_device(): pl.pallas_call(functools.partial(factor_kernel, len(parts), rows * nblk),...  12.8 us
    pallas_call x1, Pallas kernels, tiles_call(): pl.pallas_call(functools.partial(tiles_kernel, near_count, direct), name=...  10.2 us
    pallas_call x4, Pallas kernels, per_device(): pl.pallas_call(near_kernel, name='near', out_shape=sds(acc, F32), in_spec...  9.27 us
  transfers between devices with their start and end apart: 22, of which 12 were waited for; matrix products, arithmetic and copies ran while one was open for 0% of the time, Pallas kernels for 7%

profile of v2, /device:TPU:0, one launch (start us, length us, event | category | flops | bytes accessed | tf_op | source)
XLA Modules:
  0.0 140.4 jit_solution(13441533947711073241)
XLA Ops:
  0.0 22.9 %all-gather = s32[8,1,8]{2,1,0:T(1,128)} all-gather(s32[1,1,8]{2,1,0:T(1,128)} %bitcast.3), channel_id=1, replica_groups=mesh['blk'=8,'col'=4] {'blk'}, dimensions={0}, use_global_device_ids=true | all-gather | bytes 288 | tf_op jit(solution)/shard_map/all_gather | solution.py:374
  22.9 10.2 %tiles.1 = (bf16[96,256,512]{2,1,0:T(8,128)(2,1)S(1)}, f32[8,2048]{1,0:T(8,128)S(1)}, s32[128]{0:T(128)S(1)}) custom-call(s32[96]{0:T(128)} %rows_ref.1, s32[96]{0:T(128)} %slots_ref.1, bf16[96,256,256]{2,1,0:T(8,128)(2,1)} %real_hbm.1, bf16[96,256,256]{2,1,0:T(8,128)(2,1)} %imag_hbm.1), custom_call_target="tpu_custom_call" | custom-call | flops 268435456 | bytes 25165824 | tf_op jit(solution)/shard_map/tiles/pallas_call | solution.py:158
  34.6 4.3 %collective-permute-done.passed_ref.refs_7_ = bf16[4,32,256]{2,1,0:T(8,128)(2,1)S(1)} collective-permute-done((bf16[4,32,256]{2,1,0:T(8,128)(2,1)S(1)}, bf16[4,32,256]{2,1,0:T(8,128)(2,1)S(1)}, u32[]{:S(2)}, u32[]{:S(2)}) %collective-permute-start) | collective-permute-done | bytes 65568 | tf_op jit(solution)/shard_map/ppermute | solution.py:363
  39.0 4.3 %collective-permute-start.3 = (bf16[2,32,256]{2,1,0:T(8,128)(2,1)S(1)}, bf16[2,32,256]{2,1,0:T(8,128)(2,1)S(1)}, u32[]{:S(2)}, u32[]{:S(2)}) collective-permute-start(bf16[2,32,256]{2,1,0:T(8,128)(2,1)S(1)} %get-tuple-element.45), channel_id=1, source_target_pairs={{0,24},{4,28},{8,16},{12,20},{16,8},{20,12},{24,0},{28,4},{1,25},{... | collective-permute-start | bytes 98312 | tf_op jit(solution)/shard_map/ppermute | solution.py:363
  45.6 5.6 %step.4 = (f32[32,2048]{1,0:T(8,128)S(1)}, bf16[8,32,256]{2,1,0:T(8,128)(2,1)S(1)}, bf16[4,32,256]{2,1,0:T(8,128)(2,1)S(1)}, bf16[3,32,256]{2,1,0:T(8,128)(2,1)S(1)}) custom-call(s32[128]{0:T(128)S(1)} %get-tuple-element.36.plan_ref.refs_0_, s32[8]{0:T(128)S(1)} %get-tuple-element.38.refs_1_, bf16[96,256,512]{2,1,0:T(8,128)(2,1)S(1)} %get-tuple-element.39.both_ref.refs_2_, ...), custom_call_target="tpu_custom_call" | custom-call | tf_op jit(solution)/shard_map/step/pallas_call | solution.py:425
  51.3 4.3 %collective-permute-done.4.passed_ref.refs_7_ = bf16[4,32,256]{2,1,0:T(8,128)(2,1)S(1)} collective-permute-done((bf16[4,32,256]{2,1,0:T(8,128)(2,1)S(1)}, bf16[4,32,256]{2,1,0:T(8,128)(2,1)S(1)}, u32[]{:S(2)}, u32[]{:S(2)}) %collective-permute-start.4) | collective-permute-done | bytes 65568 | tf_op jit(solution)/shard_map/ppermute | solution.py:363
  56.2 3.8 %collective-permute-start.6 = (bf16[2,32,256]{2,1,0:T(8,128)(2,1)S(1)}, bf16[2,32,256]{2,1,0:T(8,128)(2,1)S(1)}, u32[]{:S(2)}, u32[]{:S(2)}) collective-permute-start(bf16[2,32,256]{2,1,0:T(8,128)(2,1)S(1)} %get-tuple-element.51), channel_id=1, source_target_pairs={{0,16},{4,20},{8,24},{12,28},{16,0},{20,4},{24,8},{28,12},{1,17},{... | collective-permute-start | bytes 98312 | tf_op jit(solution)/shard_map/ppermute | solution.py:363
  60.0 2.3 %near.5.refs_4_ = f32[8,256,32]{2,1,0:T(8,128)S(1)} custom-call(s32[128]{0:T(128)S(1)} %get-tuple-element.36.plan_ref.refs_0_, bf16[96,256,512]{2,1,0:T(8,128)(2,1)S(1)} %get-tuple-element.39.both_ref.refs_2_, bf16[8,32,256]{2,1,0:T(8,128)(2,1)S(1)} %get-tuple-element.46.sent_ref), custom_call_target="tpu_custom_call" | custom-call | flops 268435456 | bytes 1048576 | tf_op jit(solution)/shard_map/near/pallas_call | solution.py:413
  62.4 3.3 %collective-permute-done.7.refs_10_ = bf16[2,32,256]{2,1,0:T(8,128)(2,1)S(1)} collective-permute-done((bf16[2,32,256]{2,1,0:T(8,128)(2,1)S(1)}, bf16[2,32,256]{2,1,0:T(8,128)(2,1)S(1)}, u32[]{:S(2)}, u32[]{:S(2)}) %collective-permute-start.7) | collective-permute-done | bytes 32800 | tf_op jit(solution)/shard_map/ppermute | solution.py:363
  65.7 5.6 %step.5 = (f32[32,2048]{1,0:T(8,128)S(1)}, bf16[8,32,256]{2,1,0:T(8,128)(2,1)S(1)}, bf16[4,32,256]{2,1,0:T(8,128)(2,1)S(1)}, bf16[3,32,256]{2,1,0:T(8,128)(2,1)S(1)}) custom-call(s32[128]{0:T(128)S(1)} %get-tuple-element.36.plan_ref.refs_0_, s32[8]{0:T(128)S(1)} %get-tuple-element.38.refs_1_, bf16[96,256,512]{2,1,0:T(8,128)(2,1)S(1)} %get-tuple-element.39.both_ref.refs_2_, ...), custom_call_target="tpu_custom_call" | custom-call | tf_op jit(solution)/shard_map/step/pallas_call | solution.py:425
  71.4 4.3 %collective-permute-done.8.passed_ref.refs_7_ = bf16[4,32,256]{2,1,0:T(8,128)(2,1)S(1)} collective-permute-done((bf16[4,32,256]{2,1,0:T(8,128)(2,1)S(1)}, bf16[4,32,256]{2,1,0:T(8,128)(2,1)S(1)}, u32[]{:S(2)}, u32[]{:S(2)}) %collective-permute-start.8) | collective-permute-done | bytes 65568 | tf_op jit(solution)/shard_map/ppermute | solution.py:363
  77.2 3.0 %collective-permute-start.11 = (bf16[2,32,256]{2,1,0:T(8,128)(2,1)S(1)}, bf16[2,32,256]{2,1,0:T(8,128)(2,1)S(1)}, u32[]{:S(2)}, u32[]{:S(2)}) collective-permute-start(bf16[2,32,256]{2,1,0:T(8,128)(2,1)S(1)} %get-tuple-element.59), channel_id=1, source_target_pairs={{0,24},{4,28},{8,16},{12,20},{16,8},{20,12},{24,0},{28,4},{1,25},{... | collective-permute-start | bytes 98312 | tf_op jit(solution)/shard_map/ppermute | solution.py:363
  80.1 2.3 %near.6.refs_4_ = f32[8,256,32]{2,1,0:T(8,128)S(1)} custom-call(s32[128]{0:T(128)S(1)} %get-tuple-element.36.plan_ref.refs_0_, bf16[96,256,512]{2,1,0:T(8,128)(2,1)S(1)} %get-tuple-element.39.both_ref.refs_2_, bf16[8,32,256]{2,1,0:T(8,128)(2,1)S(1)} %get-tuple-element.53.sent_ref), custom_call_target="tpu_custom_call" | custom-call | flops 268435456 | bytes 1048576 | tf_op jit(solution)/shard_map/near/pallas_call | solution.py:413
  83.0 5.6 %step.6 = (f32[32,2048]{1,0:T(8,128)S(1)}, bf16[8,32,256]{2,1,0:T(8,128)(2,1)S(1)}, bf16[4,32,256]{2,1,0:T(8,128)(2,1)S(1)}, bf16[3,32,256]{2,1,0:T(8,128)(2,1)S(1)}) custom-call(s32[128]{0:T(128)S(1)} %get-tuple-element.36.plan_ref.refs_0_, s32[8]{0:T(128)S(1)} %get-tuple-element.38.refs_1_, bf16[96,256,512]{2,1,0:T(8,128)(2,1)S(1)} %get-tuple-element.39.both_ref.refs_2_, ...), custom_call_target="tpu_custom_call" | custom-call | tf_op jit(solution)/shard_map/step/pallas_call | solution.py:425
  88.6 4.3 %collective-permute-done.12.passed_ref.refs_7_ = bf16[4,32,256]{2,1,0:T(8,128)(2,1)S(1)} collective-permute-done((bf16[4,32,256]{2,1,0:T(8,128)(2,1)S(1)}, bf16[4,32,256]{2,1,0:T(8,128)(2,1)S(1)}, u32[]{:S(2)}, u32[]{:S(2)}) %collective-permute-start.12) | collective-permute-done | bytes 65568 | tf_op jit(solution)/shard_map/ppermute | solution.py:363
  93.0 3.8 %collective-permute-start.14 = (bf16[2,32,256]{2,1,0:T(8,128)(2,1)S(1)}, bf16[2,32,256]{2,1,0:T(8,128)(2,1)S(1)}, u32[]{:S(2)}, u32[]{:S(2)}) collective-permute-start(bf16[2,32,256]{2,1,0:T(8,128)(2,1)S(1)} %get-tuple-element.65), channel_id=1, source_target_pairs={{0,16},{4,20},{8,24},{12,28},{16,0},{20,4},{24,8},{28,12},{1,17},{... | collective-permute-start | bytes 98312 | tf_op jit(solution)/shard_map/ppermute | solution.py:363
  97.3 2.3 %near.7.refs_4_ = f32[8,256,32]{2,1,0:T(8,128)S(1)} custom-call(s32[128]{0:T(128)S(1)} %get-tuple-element.36.plan_ref.refs_0_, bf16[96,256,512]{2,1,0:T(8,128)(2,1)S(1)} %get-tuple-element.39.both_ref.refs_2_, bf16[8,32,256]{2,1,0:T(8,128)(2,1)S(1)} %get-tuple-element.60.sent_ref), custom_call_target="tpu_custom_call" | custom-call | flops 268435456 | bytes 1048576 | tf_op jit(solution)/shard_map/near/pallas_call | solution.py:413
  99.7 2.8 %collective-permute-done.15.refs_10_ = bf16[2,32,256]{2,1,0:T(8,128)(2,1)S(1)} collective-permute-done((bf16[2,32,256]{2,1,0:T(8,128)(2,1)S(1)}, bf16[2,32,256]{2,1,0:T(8,128)(2,1)S(1)}, u32[]{:S(2)}, u32[]{:S(2)}) %collective-permute-start.15) | collective-permute-done | bytes 32800 | tf_op jit(solution)/shard_map/ppermute | solution.py:363
  102.5 5.5 %step.7.own_ref = f32[32,2048]{1,0:T(8,128)S(1)} custom-call(s32[128]{0:T(128)S(1)} %get-tuple-element.36.plan_ref.refs_0_, s32[8]{0:T(128)S(1)} %get-tuple-element.38.refs_1_, bf16[96,256,512]{2,1,0:T(8,128)(2,1)S(1)} %get-tuple-element.39.both_ref.refs_2_, f32[8,2048]{1,0:T(8,128)S(1)} %get-tuple-element.37.scale_ref.refs_3_, ...), custom_call_target="tpu_custom_call" | custom-call | tf_op jit(solution)/shard_map/step/pallas_call | solution.py:425
  109.7 3.4 %collective-permute-done.17.refs_1_.refs_3_ = bf16[32,2048]{1,0:T(8,128)(2,1)S(1)} collective-permute-done((bf16[32,2048]{1,0:T(8,128)(2,1)S(1)}, bf16[32,2048]{1,0:T(8,128)(2,1)S(1)}, u32[]{:S(2)}, u32[]{:S(2)}) %collective-permute-start.17) | collective-permute-done | bytes 131104 | tf_op jit(solution)/shard_map/ppermute | solution.py:363
  115.0 3.9 %collective-permute-done.19 = f32[64,128]{1,0:T(8,128)S(1)} collective-permute-done((f32[64,128]{1,0:T(8,128)S(1)}, f32[64,128]{1,0:T(8,128)S(1)}, u32[]{:S(2)}, u32[]{:S(2)}) %collective-permute-start.19) | collective-permute-done | bytes 32800 | tf_op jit(solution)/shard_map/ppermute | solution.py:363
  118.9 3.9 %collective-permute-done.20 = f32[64,128]{1,0:T(8,128)S(1)} collective-permute-done((f32[64,128]{1,0:T(8,128)S(1)}, f32[64,128]{1,0:T(8,128)S(1)}, u32[]{:S(2)}, u32[]{:S(2)}) %collective-permute-start.20) | collective-permute-done | bytes 32800 | tf_op jit(solution)/shard_map/ppermute | solution.py:363
  122.8 4.8 %collective-permute-done.21.refs_1_ = f32[64,128]{1,0:T(8,128)S(1)} collective-permute-done((f32[64,128]{1,0:T(8,128)S(1)}, f32[64,128]{1,0:T(8,128)S(1)}, u32[]{:S(2)}, u32[]{:S(2)}) %collective-permute-start.21) | collective-permute-done | bytes 32800 | tf_op jit(solution)/shard_map/ppermute | solution.py:363
  127.6 12.8 %factor.1 = f32[32,2048]{1,0:T(8,128)} custom-call(f32[32,2048]{1,0:T(8,128)S(1)} %step.7.own_ref, f32[64,128]{1,0:T(8,128)S(1)} %add.7.refs_0_, f32[64,128]{1,0:T(8,128)S(1)} %collective-permute-done.21.refs_1_, bf16[32,2048]{1,0:T(8,128)(2,1)S(1)} %collective-permute-done.16.refs_0_.refs_2_, bf16[32,2048]{1,0:T(8,128)(2,1)S(1)} %collective-permute-done.17.refs_1_.refs_3_, ...), custom_call_target="tpu_custom_call" | custom-call | tf_op jit(solution)/shard_map/factor/pallas_call | solution.py:459
  (42 shorter events, 11.0 us)
Async XLA Ops:
  22.9 10.2 %copy-start = (f32[32,2048]{1,0:T(8,128)S(1)}, f32[32,2048]{1,0:T(8,128)}, u32[]{:S(2)}) copy-start(f32[32,2048]{1,0:T(8,128)} %refs_6_.3) | copy-start | bytes 786436
  34.5 4.3 %collective-permute-start = (bf16[4,32,256]{2,1,0:T(8,128)(2,1)S(1)}, bf16[4,32,256]{2,1,0:T(8,128)(2,1)S(1)}, u32[]{:S(2)}, u32[]{:S(2)}) collective-permute-start(bf16[4,32,256]{2,1,0:T(8,128)(2,1)S(1)} %get-tuple-element.41), channel_id=1, source_target_pairs={{0,4},{4,0},{8,12},{12,8},{16,20},{20,16},{24,28},{28,24},{1,5},{5... | collective-permute-start | bytes 196616 | tf_op jit(solution)/shard_map/ppermute | solution.py:363
  38.8 6.8 %collective-permute-start.1 = (bf16[2,32,256]{2,1,0:T(8,128)(2,1)S(1)}, bf16[2,32,256]{2,1,0:T(8,128)(2,1)S(1)}, u32[]{:S(2)}, u32[]{:S(2)}) collective-permute-start(bf16[2,32,256]{2,1,0:T(8,128)(2,1)S(1)} %get-tuple-element.43), channel_id=1, source_target_pairs={{0,8},{4,12},{8,0},{12,4},{16,24},{20,28},{24,16},{28,20},{1,9},{5... | collective-permute-start | bytes 98312 | tf_op jit(solution)/shard_map/ppermute | solution.py:363
  38.9 6.7 %collective-permute-start.2 = (bf16[2,32,256]{2,1,0:T(8,128)(2,1)S(1)}, bf16[2,32,256]{2,1,0:T(8,128)(2,1)S(1)}, u32[]{:S(2)}, u32[]{:S(2)}) collective-permute-start(bf16[2,32,256]{2,1,0:T(8,128)(2,1)S(1)} %get-tuple-element.44), channel_id=1, source_target_pairs={{0,16},{4,20},{8,24},{12,28},{16,0},{20,4},{24,8},{28,12},{1,17},{... | collective-permute-start | bytes 98312 | tf_op jit(solution)/shard_map/ppermute | solution.py:363
  39.0 6.6 %collective-permute-start.3 = (bf16[2,32,256]{2,1,0:T(8,128)(2,1)S(1)}, bf16[2,32,256]{2,1,0:T(8,128)(2,1)S(1)}, u32[]{:S(2)}, u32[]{:S(2)}) collective-permute-start(bf16[2,32,256]{2,1,0:T(8,128)(2,1)S(1)} %get-tuple-element.45), channel_id=1, source_target_pairs={{0,24},{4,28},{8,16},{12,20},{16,8},{20,12},{24,0},{28,4},{1,25},{... | collective-permute-start | bytes 98312 | tf_op jit(solution)/shard_map/ppermute | solution.py:363
  51.2 4.3 %collective-permute-start.4 = (bf16[4,32,256]{2,1,0:T(8,128)(2,1)S(1)}, bf16[4,32,256]{2,1,0:T(8,128)(2,1)S(1)}, u32[]{:S(2)}, u32[]{:S(2)}) collective-permute-start(bf16[4,32,256]{2,1,0:T(8,128)(2,1)S(1)} %get-tuple-element.48), channel_id=1, source_target_pairs={{0,4},{4,0},{8,12},{12,8},{16,20},{20,16},{24,28},{28,24},{1,5},{5... | collective-permute-start | bytes 196616 | tf_op jit(solution)/shard_map/ppermute | solution.py:363
  55.6 6.8 %collective-permute-start.5 = (bf16[2,32,256]{2,1,0:T(8,128)(2,1)S(1)}, bf16[2,32,256]{2,1,0:T(8,128)(2,1)S(1)}, u32[]{:S(2)}, u32[]{:S(2)}) collective-permute-start(bf16[2,32,256]{2,1,0:T(8,128)(2,1)S(1)} %get-tuple-element.50), channel_id=1, source_target_pairs={{0,8},{4,12},{8,0},{12,4},{16,24},{20,28},{24,16},{28,20},{1,9},{5... | collective-permute-start | bytes 98312 | tf_op jit(solution)/shard_map/ppermute | solution.py:363
  56.2 6.2 %collective-permute-start.6 = (bf16[2,32,256]{2,1,0:T(8,128)(2,1)S(1)}, bf16[2,32,256]{2,1,0:T(8,128)(2,1)S(1)}, u32[]{:S(2)}, u32[]{:S(2)}) collective-permute-start(bf16[2,32,256]{2,1,0:T(8,128)(2,1)S(1)} %get-tuple-element.51), channel_id=1, source_target_pairs={{0,16},{4,20},{8,24},{12,28},{16,0},{20,4},{24,8},{28,12},{1,17},{... | collective-permute-start | bytes 98312 | tf_op jit(solution)/shard_map/ppermute | solution.py:363
  60.0 5.7 %collective-permute-start.7 = (bf16[2,32,256]{2,1,0:T(8,128)(2,1)S(1)}, bf16[2,32,256]{2,1,0:T(8,128)(2,1)S(1)}, u32[]{:S(2)}, u32[]{:S(2)}) collective-permute-start(bf16[2,32,256]{2,1,0:T(8,128)(2,1)S(1)} %get-tuple-element.52), channel_id=1, source_target_pairs={{0,24},{4,28},{8,16},{12,20},{16,8},{20,12},{24,0},{28,4},{1,25},{... | collective-permute-start | bytes 98312 | tf_op jit(solution)/shard_map/ppermute | solution.py:363
  71.3 4.3 %collective-permute-start.8 = (bf16[4,32,256]{2,1,0:T(8,128)(2,1)S(1)}, bf16[4,32,256]{2,1,0:T(8,128)(2,1)S(1)}, u32[]{:S(2)}, u32[]{:S(2)}) collective-permute-start(bf16[4,32,256]{2,1,0:T(8,128)(2,1)S(1)} %get-tuple-element.55), channel_id=1, source_target_pairs={{0,4},{4,0},{8,12},{12,8},{16,20},{20,16},{24,28},{28,24},{1,5},{5... | collective-permute-start | bytes 196616 | tf_op jit(solution)/shard_map/ppermute | solution.py:363
  75.7 6.8 %collective-permute-start.9 = (bf16[2,32,256]{2,1,0:T(8,128)(2,1)S(1)}, bf16[2,32,256]{2,1,0:T(8,128)(2,1)S(1)}, u32[]{:S(2)}, u32[]{:S(2)}) collective-permute-start(bf16[2,32,256]{2,1,0:T(8,128)(2,1)S(1)} %get-tuple-element.57), channel_id=1, source_target_pairs={{0,8},{4,12},{8,0},{12,4},{16,24},{20,28},{24,16},{28,20},{1,9},{5... | collective-permute-start | bytes 98312 | tf_op jit(solution)/shard_map/ppermute | solution.py:363
  75.7 6.7 %collective-permute-start.10 = (bf16[2,32,256]{2,1,0:T(8,128)(2,1)S(1)}, bf16[2,32,256]{2,1,0:T(8,128)(2,1)S(1)}, u32[]{:S(2)}, u32[]{:S(2)}) collective-permute-start(bf16[2,32,256]{2,1,0:T(8,128)(2,1)S(1)} %get-tuple-element.58), channel_id=1, source_target_pairs={{0,16},{4,20},{8,24},{12,28},{16,0},{20,4},{24,8},{28,12},{1,17},{... | collective-permute-start | bytes 98312 | tf_op jit(solution)/shard_map/ppermute | solution.py:363
  77.2 5.8 %collective-permute-start.11 = (bf16[2,32,256]{2,1,0:T(8,128)(2,1)S(1)}, bf16[2,32,256]{2,1,0:T(8,128)(2,1)S(1)}, u32[]{:S(2)}, u32[]{:S(2)}) collective-permute-start(bf16[2,32,256]{2,1,0:T(8,128)(2,1)S(1)} %get-tuple-element.59), channel_id=1, source_target_pairs={{0,24},{4,28},{8,16},{12,20},{16,8},{20,12},{24,0},{28,4},{1,25},{... | collective-permute-start | bytes 98312 | tf_op jit(solution)/shard_map/ppermute | solution.py:363
  88.5 4.3 %collective-permute-start.12 = (bf16[4,32,256]{2,1,0:T(8,128)(2,1)S(1)}, bf16[4,32,256]{2,1,0:T(8,128)(2,1)S(1)}, u32[]{:S(2)}, u32[]{:S(2)}) collective-permute-start(bf16[4,32,256]{2,1,0:T(8,128)(2,1)S(1)} %get-tuple-element.62), channel_id=1, source_target_pairs={{0,4},{4,0},{8,12},{12,8},{16,20},{20,16},{24,28},{28,24},{1,5},{5... | collective-permute-start | bytes 196616 | tf_op jit(solution)/shard_map/ppermute | solution.py:363
  92.9 6.8 %collective-permute-start.13 = (bf16[2,32,256]{2,1,0:T(8,128)(2,1)S(1)}, bf16[2,32,256]{2,1,0:T(8,128)(2,1)S(1)}, u32[]{:S(2)}, u32[]{:S(2)}) collective-permute-start(bf16[2,32,256]{2,1,0:T(8,128)(2,1)S(1)} %get-tuple-element.64), channel_id=1, source_target_pairs={{0,8},{4,12},{8,0},{12,4},{16,24},{20,28},{24,16},{28,20},{1,9},{5... | collective-permute-start | bytes 98312 | tf_op jit(solution)/shard_map/ppermute | solution.py:363
  93.0 6.7 %collective-permute-start.14 = (bf16[2,32,256]{2,1,0:T(8,128)(2,1)S(1)}, bf16[2,32,256]{2,1,0:T(8,128)(2,1)S(1)}, u32[]{:S(2)}, u32[]{:S(2)}) collective-permute-start(bf16[2,32,256]{2,1,0:T(8,128)(2,1)S(1)} %get-tuple-element.65), channel_id=1, source_target_pairs={{0,16},{4,20},{8,24},{12,28},{16,0},{20,4},{24,8},{28,12},{1,17},{... | collective-permute-start | bytes 98312 | tf_op jit(solution)/shard_map/ppermute | solution.py:363
  96.8 5.7 %collective-permute-start.15 = (bf16[2,32,256]{2,1,0:T(8,128)(2,1)S(1)}, bf16[2,32,256]{2,1,0:T(8,128)(2,1)S(1)}, u32[]{:S(2)}, u32[]{:S(2)}) collective-permute-start(bf16[2,32,256]{2,1,0:T(8,128)(2,1)S(1)} %get-tuple-element.66), channel_id=1, source_target_pairs={{0,24},{4,28},{8,16},{12,20},{16,8},{20,12},{24,0},{28,4},{1,25},{... | collective-permute-start | bytes 98312 | tf_op jit(solution)/shard_map/ppermute | solution.py:363
  108.1 5.0 %collective-permute-start.17 = (bf16[32,2048]{1,0:T(8,128)(2,1)S(1)}, bf16[32,2048]{1,0:T(8,128)(2,1)S(1)}, u32[]{:S(2)}, u32[]{:S(2)}) collective-permute-start(bf16[32,2048]{1,0:T(8,128)(2,1)S(1)} %convert_element_type.3), channel_id=1, source_target_pairs={{0,2},{1,3},{2,0},{3,1},{4,6},{5,7},{6,4},{7,5},{8,10},{9,11},{10,... | collective-permute-start | bytes 393224 | tf_op jit(solution)/shard_map/ppermute | solution.py:363
  109.7 3.4 %collective-permute-start.16 = (bf16[32,2048]{1,0:T(8,128)(2,1)S(1)}, bf16[32,2048]{1,0:T(8,128)(2,1)S(1)}, u32[]{:S(2)}, u32[]{:S(2)}) collective-permute-start(bf16[32,2048]{1,0:T(8,128)(2,1)S(1)} %convert_element_type.3), channel_id=1, source_target_pairs={{0,1},{1,0},{2,3},{3,2},{4,5},{5,4},{6,7},{7,6},{8,9},{9,8},{10,11... | collective-permute-start | bytes 393224 | tf_op jit(solution)/shard_map/ppermute | solution.py:363
  113.1 1.3 collective-permute-start.18
  114.9 4.0 %collective-permute-start.19 = (f32[64,128]{1,0:T(8,128)S(1)}, f32[64,128]{1,0:T(8,128)S(1)}, u32[]{:S(2)}, u32[]{:S(2)}) collective-permute-start(f32[64,128]{1,0:T(8,128)S(1)} %gram.1), channel_id=1, source_target_pairs={{0,4},{4,0},{8,12},{12,8},{16,20},{20,16},{24,28},{28,24},{1,5},{5... | collective-permute-start | bytes 98312 | tf_op jit(solution)/shard_map/ppermute | solution.py:363
  118.8 3.9 %collective-permute-start.20 = (f32[64,128]{1,0:T(8,128)S(1)}, f32[64,128]{1,0:T(8,128)S(1)}, u32[]{:S(2)}, u32[]{:S(2)}) collective-permute-start(f32[64,128]{1,0:T(8,128)S(1)} %add.6), channel_id=1, source_target_pairs={{0,8},{4,12},{8,0},{12,4},{16,24},{20,28},{24,16},{28,20},{1,9},{5... | collective-permute-start | bytes 98312 | tf_op jit(solution)/shard_map/ppermute | solution.py:363
  122.8 4.8 %collective-permute-start.21 = (f32[64,128]{1,0:T(8,128)S(1)}, f32[64,128]{1,0:T(8,128)S(1)}, u32[]{:S(2)}, u32[]{:S(2)}) collective-permute-start(f32[64,128]{1,0:T(8,128)S(1)} %add.7.refs_0_), channel_id=1, source_target_pairs={{0,16},{4,20},{8,24},{12,28},{16,0},{20,4},{24,8},{28,12},{1,17},{... | collective-permute-start | bytes 98312 | tf_op jit(solution)/shard_map/ppermute | solution.py:363

commit v3 on v2

v3 whole, which is shorter than its diff:
```python
import functools
import math

import jax
import jax.numpy as jnp
from jax import lax
from jax.experimental import pallas as pl
from jax.experimental.pallas import tpu as pltpu
from jax.sharding import PartitionSpec as P

LOC_RB = 2
STEPS = 4
UNROLL = 4
CHUNK = 4
MERGE = 16
PARTS = 3
TOP = 256.0
FINER = 16.0
TINY = 1e-30
MIB = 1 << 20
LIMIT = 24

center = 1.25
half_width = 0.75

F32 = jnp.float32
BF16 = jnp.bfloat16
F8 = jnp.float8_e4m3fn
I32 = jnp.int32

VMEM = pl.BlockSpec(memory_space=pltpu.VMEM)
SMEM = pl.BlockSpec(memory_space=pltpu.SMEM)
ANY = pl.BlockSpec(memory_space=pl.ANY)

NT = (((1,), (1,)), ((), ()))
TN = (((0,), (0,)), ((), ()))


def sds(shape, dtype):
    return jax.ShapeDtypeStruct(shape, dtype)


def params(limit):
    return pltpu.CompilerParams(vmem_limit_bytes=limit * MIB)


def turn_rows(values):
    rows = values.shape[0]
    even = lax.broadcasted_iota(I32, values.shape, 0) % 2 == 0
    below = pltpu.roll(values, rows - 1, 0)
    above = pltpu.roll(values, 1, 0)
    return jnp.where(even, -below, above)


def turn_lanes(values):
    lanes = values.shape[1]
    even = lax.broadcasted_iota(I32, values.shape, 1) % 2 == 0
    after = pltpu.roll(values, lanes - 1, 1)
    before = pltpu.roll(values, 1, 1)
    return jnp.where(even, after, -before)


def tiles_kernel(
    near_count,
    rows_ref,
    slots_ref,
    real_hbm,
    imag_hbm,
    packed_hbm,
    scale_ref,
    plan_ref,
    both_ref,
    small_ref,
    present_ref,
    table_ref,
    back_ref,
    done_ref,
    in_sems,
    out_sems,
):
    tiles, order, _ = both_ref.shape
    rb_dev = present_ref.shape[0]
    slots = rb_dev + lax.axis_size("blk")
    chunks = tiles // CHUNK

    def copies(c):
        at = pl.ds(c * CHUNK, CHUNK)
        return (
            pltpu.make_async_copy(real_hbm.at[at], both_ref.at[at, :, 0:order], in_sems.at[c, 0]),
            pltpu.make_async_copy(imag_hbm.at[at], both_ref.at[at, :, order : 2 * order], in_sems.at[c, 1]),
        )

    def leave(e):
        return pltpu.make_async_copy(small_ref.at[e], packed_hbm.at[e], out_sems.at[e])

    for c in range(chunks):
        for copy in copies(c):
            copy.start()

    def clear(key, _):
        table_ref[key] = -1
        return _

    lax.fori_loop(0, rb_dev * slots, clear, 0)
    present_ref[...] = jnp.zeros_like(present_ref)

    def link(t, carry):
        key = rows_ref[t] * slots + slots_ref[t]
        seen = table_ref[key]
        before = seen & 255
        length = seen >> 8
        joins = (seen >= 0) & (length < MERGE)
        back_ref[t] = jnp.where(joins, before, -1)
        done_ref[t] = 1

        @pl.when(joins)
        def _():
            done_ref[before] = 0

        table_ref[key] = t | (jnp.where(joins, length + 1, 1) << 8)
        return carry

    lax.fori_loop(0, tiles, link, 0)

    def one(t, listed):
        row = rows_ref[t]
        both = both_ref[t]
        present_ref[row] = present_ref[row] + (both[:, :order] + jnp.abs(both[:, order:]))
        closes = done_ref[t]

        @pl.when(closes == 1)
        def _():
            def add(prior):
                both_ref[t] = both_ref[t] + both_ref[prior]
                return back_ref[prior]

            lax.while_loop(lambda prior: prior >= 0, add, back_ref[t])
            small_ref[listed] = both_ref[t].astype(F32).astype(F8)
            leave(listed).start()
            plan_ref[listed] = row | (slots_ref[t] << 8)

        return listed + closes

    def chunk(c, listed):
        for copy in copies(c):
            copy.wait()
        for j in range(CHUNK):
            listed = one(c * CHUNK + j, listed)
        return listed

    def pad(listed):
        short = (UNROLL - listed % UNROLL) % UNROLL
        for j in range(UNROLL - 1):

            @pl.when(j < short)
            def _():
                small_ref[listed + j] = jnp.zeros(small_ref.shape[1:], F8)
                leave(listed + j).start()
                plan_ref[listed + j] = slots << 8

        return listed + short

    near = pad(lax.fori_loop(0, near_count // CHUNK, chunk, 0))
    every = pad(lax.fori_loop(near_count // CHUNK, chunks, chunk, near))
    plan_ref[tiles] = near // UNROLL
    plan_ref[tiles + 1] = every // UNROLL

    ones = jnp.ones((8, order), BF16)
    for r in range(rb_dev):
        degree = lax.dot_general(ones, present_ref[r], NT, preferred_element_type=F32)
        scale_ref[:, r * order : (r + 1) * order] = 1.0 / jnp.sqrt(jnp.maximum(degree, 1.0))

    def left(e, _):
        leave(e).wait()
        return _

    lax.fori_loop(0, every, left, 0)


def in_hbm(x):
    return pltpu.with_memory_space_constraint(x, pltpu.HBM)


def tiles_call(rows, slots, real, imag, rb_dev, near_count):
    tiles, order, _ = real.shape
    nblk = lax.axis_size("blk")
    return pl.pallas_call(
        functools.partial(tiles_kernel, near_count),
        name="tiles",
        out_shape=(
            pltpu.HBM((tiles, order, 2 * order), F8),
            sds((8, rb_dev * order), F32),
            sds((tiles + 32,), I32),
        ),
        in_specs=[SMEM, SMEM, ANY, ANY],
        out_specs=(ANY, VMEM, SMEM),
        scratch_shapes=[
            pltpu.VMEM((tiles, order, 2 * order), BF16),
            pltpu.VMEM((tiles, order, 2 * order), F8),
            pltpu.VMEM((rb_dev, order, order), BF16),
            pltpu.SMEM((rb_dev * (rb_dev + nblk),), I32),
            pltpu.SMEM((tiles,), I32),
            pltpu.SMEM((tiles,), I32),
            pltpu.SemaphoreType.DMA((tiles // CHUNK, 2)),
            pltpu.SemaphoreType.DMA((tiles,)),
        ],
        compiler_params=params(48),
        cost_estimate=pl.CostEstimate(flops=1 << 28, bytes_accessed=2 * real.size * 2, transcendentals=0),
    )(in_hbm(rows), in_hbm(slots), in_hbm(real), in_hbm(imag))


def send_blocks(field, scale_ref, sent_ref, pick, out_ref):
    order = sent_ref.shape[2]
    for r in range(sent_ref.shape[0]):
        at = slice(r * order, (r + 1) * order)
        sent_ref[r] = (field[:, at] * scale_ref[0:1, at]).astype(BF16)
    for p in range(out_ref.shape[0]):
        out_ref[p] = sent_ref[pick(p)]


def first_kernel(y_ref, scale_ref, wanted_ref, sent_ref, out_ref):
    send_blocks(y_ref, scale_ref, sent_ref, lambda p: wanted_ref[p, 0], out_ref)


def load_groups(packed_hbm, tiles_ref, sems, lo, hi):
    def copy(g):
        at = pl.ds((g - lo) * UNROLL, UNROLL)
        return pltpu.make_async_copy(
            packed_hbm.at[pl.ds(g * UNROLL, UNROLL)], tiles_ref.at[at], sems.at[g - lo]
        )

    def begin(g, _):
        copy(g).start()
        return _

    lax.fori_loop(lo, hi, begin, 0)
    return copy


def split_sources(source, x_ref):
    count, group, order = source.shape
    most = jnp.zeros((group, order), F32)
    for p in range(count):
        most = jnp.maximum(most, jnp.abs(source[p].astype(F32)))
    most = jnp.broadcast_to(jnp.max(most, axis=1, keepdims=True), (group, 128))
    most = jnp.maximum(jnp.maximum(most, jnp.abs(turn_rows(most))), TINY)
    size = most[:, 0:1] / TOP
    inverse = TOP / most[:, 0:1]
    for p in range(count):
        scaled = source[p].astype(F32) * inverse
        for side, part in enumerate((scaled, turn_rows(scaled))):
            at = slice(side * order, (side + 1) * order)
            for k in range(PARTS):
                short = part.astype(F8)
                x_ref[p, k * group : (k + 1) * group, at] = short
                part = (part - short.astype(F32)) * FINER
    x_ref[count] = jnp.zeros_like(x_ref[count])
    return size


def multiply(plan_ref, lo, hi, copy, tiles_ref, load, acc_ref):
    def group(g, _):
        copy(g).wait()
        done = []
        for j in range(UNROLL):
            code = plan_ref[g * UNROLL + j]
            tile = tiles_ref[(g - lo) * UNROLL + j]
            product = lax.dot_general(tile, load(code >> 8), NT, preferred_element_type=F32)
            done.append((code & 255, product))
        for row, product in done:
            acc_ref[row] = acc_ref[row] + product
        return _

    lax.fori_loop(lo, hi, group, 0)


def collect(acc, size):
    group = size.shape[0]
    flat = acc.T
    total = flat[(PARTS - 1) * group : PARTS * group]
    for k in range(PARTS - 2, -1, -1):
        total = flat[k * group : (k + 1) * group] + total * (1.0 / FINER)
    return total * size


def near_kernel(plan_ref, packed_hbm, sent_ref, out_ref, tiles_ref, x_ref, acc_ref, sems):
    rb_dev = sent_ref.shape[0]
    at = plan_ref.shape[0] - 32
    hi = plan_ref[at]
    copy = load_groups(packed_hbm, tiles_ref, sems, 0, hi)
    acc_ref[...] = jnp.zeros_like(acc_ref)
    size = split_sources(sent_ref, x_ref)
    multiply(plan_ref, 0, hi, copy, tiles_ref, lambda c: x_ref[jnp.minimum(c, rb_dev)], acc_ref)
    for r in range(rb_dev):
        out_ref[r] = collect(acc_ref[r], size)


def step_kernel(step, plan_ref, wanted_ref, packed_hbm, scale_ref, near_ref, now_ref, before_ref, arrived_ref, *refs):
    last = step == STEPS - 1
    next_ref = refs[0]
    tiles_ref, x_ref, acc_ref, sems = refs[-4:]
    rb_dev, _, order = near_ref.shape
    at = plan_ref.shape[0] - 32
    lo, hi = plan_ref[at], plan_ref[at + 1]
    copy = load_groups(packed_hbm, tiles_ref, sems, lo, hi)
    acc_ref[...] = jnp.zeros_like(acc_ref)
    size = split_sources(arrived_ref, x_ref)
    multiply(plan_ref, lo, hi, copy, tiles_ref, lambda c: x_ref[c - rb_dev], acc_ref)
    for r in range(rb_dev):
        at = slice(r * order, (r + 1) * order)
        now = now_ref[:, at]
        applied = scale_ref[0:1, at] * (near_ref[r] + collect(acc_ref[r], size))
        moved = ((1.0 - center) * now - applied) / half_width
        next_ref[:, at] = moved if step == 0 else 2.0 * moved - before_ref[:, at]
    if not last:
        send_blocks(next_ref, scale_ref, refs[1], lambda p: wanted_ref[p, 0], refs[2])


def all_rows(own_ref, arrived, all_ref):
    c = lax.axis_index("col")
    all_ref[c] = own_ref[...].astype(BF16)
    for s, ref in enumerate(arrived, 1):
        all_ref[c ^ s] = ref[...]
    n, group, rows = all_ref.shape
    return all_ref[...].reshape(n * group, rows)


def gram_kernel(own_ref, *refs):
    arrived, (gram_ref, all_ref, full_ref) = refs[:-3], refs[-3:]
    rows = all_rows(own_ref, arrived, all_ref)
    full_ref[...] = lax.dot_general(rows, rows, NT, preferred_element_type=F32)
    half = gram_ref.shape[0]
    even = full_ref[pl.ds(0, half, stride=2), :]
    odd = full_ref[pl.ds(1, half, stride=2), :]
    gram_ref[...] = even + turn_lanes(odd)


PANEL = 16


def factor_kernel(grams, nodes, own_ref, *refs):
    parts = refs[:grams]
    arrived = refs[grams:-4]
    out_ref, all_ref, work_ref, inverse_ref = refs[-4:]
    group = own_ref.shape[0]
    order = work_ref.shape[0]
    total = parts[0][...]
    for part in parts[1:]:
        total = total + part[...]
    half = total.shape[0]
    work_ref[pl.ds(0, half, stride=2), :] = total
    work_ref[pl.ds(1, half, stride=2), :] = -turn_lanes(total)
    row_at = lax.broadcasted_iota(I32, (order, order), 0)
    lane_at = lax.broadcasted_iota(I32, (order, order), 1)
    inverse_ref[...] = (row_at == lane_at).astype(F32)
    here = lax.broadcasted_iota(I32, (PANEL, 1), 0)
    for top in range(0, order, PANEL):
        panel = jnp.concatenate([work_ref[top : top + PANEL, :], inverse_ref[top : top + PANEL, :]], axis=1)
        for k in range(0, PANEL, 2):
            lane = top + k
            left = panel[:, lane : lane + 1]
            right = panel[:, lane + 1 : lane + 2]
            inv = lax.rsqrt(left[k : k + 1, :])
            inv2 = inv * inv
            below = here > k + 1
            pair = here - k
            a = jnp.where(below, left * inv2, 0.0)
            b = jnp.where(below, right * inv2, 0.0)
            keep = jnp.where((pair == 0) | (pair == 1), inv, 1.0)
            panel = panel * keep - (a * panel[k : k + 1, :] + b * panel[k + 1 : k + 2, :])
        inverse_ref[top : top + PANEL, :] = panel[:, order:]
        rest = top + PANEL
        if rest < order:
            cols = panel[:, 0:order]
            update = lax.dot_general(
                cols, panel, TN, precision=lax.Precision.HIGHEST, preferred_element_type=F32
            )
            work_ref[rest:, :] = work_ref[rest:, :] - update[rest:, :order]
            inverse_ref[rest:, :] = inverse_ref[rest:, :] - update[rest:, order:]
    c = lax.axis_index("col")
    mine = inverse_ref[pl.ds(pl.multiple_of(c * group, group), group), :]
    mine = mine * math.sqrt(nodes)
    high = mine.astype(BF16)
    low = (mine - high.astype(F32)).astype(BF16)
    rows = all_rows(own_ref, arrived, all_ref)
    both = lax.dot_general(
        jnp.concatenate([high, low], axis=0), rows, (((1,), (0,)), ((), ())), preferred_element_type=F32
    )
    own = own_ref[...]
    lost = own - own.astype(BF16).astype(F32)
    own_lanes = (
        lax.broadcasted_iota(I32, (order, group), 0)
        == lax.broadcasted_iota(I32, (order, group), 1) + c * group
    ).astype(BF16)
    square = jnp.dot(high, own_lanes, preferred_element_type=F32).astype(BF16)
    out_ref[...] = (
        both[:group] + both[group:] + jnp.dot(square, lost.astype(BF16), preferred_element_type=F32)
    )


def to_partner(x, axis, mask):
    n = lax.axis_size(axis)
    return lax.ppermute(x, axis, [(i, i ^ mask) for i in range(n)])


def per_device(y_start, tile_real, tile_imag, tile_rows, tile_slots, fetch_pick):
    group, rows = y_start.shape
    tiles, order, _ = tile_real.shape
    rb_dev = rows // order
    nblk = lax.axis_size("blk")
    ncol = lax.axis_size("col")
    near_count = LOC_RB * rb_dev
    wanted = lax.all_to_all(
        fetch_pick.reshape(nblk, 1), "blk", split_axis=0, concat_axis=0, tiled=True
    )
    packed, scale, plan = tiles_call(tile_rows, tile_slots, tile_real, tile_imag, rb_dev, near_count)

    own_blocks = sds((rb_dev, group, order), BF16)
    out_blocks = sds((nblk, group, order), BF16)
    sent, blocks = pl.pallas_call(
        first_kernel,
        name="first",
        out_shape=(own_blocks, out_blocks),
        in_specs=[VMEM, VMEM, SMEM],
        out_specs=(VMEM, VMEM),
        compiler_params=params(LIMIT),
    )(y_start, scale, wanted)

    def scratch(entries, sources):
        return [
            pltpu.VMEM((entries, order, 2 * order), F8),
            pltpu.VMEM((sources + 1, PARTS * group, 2 * order), F8),
            pltpu.VMEM((rb_dev, order, PARTS * group), F32),
            pltpu.SemaphoreType.DMA((entries // UNROLL,)),
        ]

    previous, current = y_start, y_start
    for step in range(STEPS):
        arrived = lax.all_to_all(blocks, "blk", split_axis=0, concat_axis=0, tiled=True)
        near = pl.pallas_call(
            near_kernel,
            name="near",
            out_shape=sds((rb_dev, group, order), F32),
            in_specs=[SMEM, ANY, VMEM],
            out_specs=VMEM,
            scratch_shapes=scratch(near_count, rb_dev),
            compiler_params=params(LIMIT),
            cost_estimate=pl.CostEstimate(flops=1 << 28, bytes_accessed=1 << 21, transcendentals=0),
        )(plan, in_hbm(packed), sent)
        last = step == STEPS - 1
        more = () if last else (own_blocks, out_blocks)
        out = pl.pallas_call(
            functools.partial(step_kernel, step),
            name="step",
            out_shape=(sds((group, rows), F32), *more),
            in_specs=[SMEM, SMEM, ANY] + [VMEM] * 5,
            out_specs=(VMEM,) * (1 + len(more)),
            scratch_shapes=scratch(tiles - near_count, nblk),
            compiler_params=params(LIMIT),
        )(plan, wanted, in_hbm(packed), scale, near, current, previous, arrived)
        previous, current = current, out[0]
        if not last:
            sent, blocks = out[1:]

    rounded = current.astype(BF16)
    if ncol == 4:
        beside, across = to_partner(rounded, "col", 1), to_partner(rounded, "col", 2)
        others = [beside, across, to_partner(across, "col", 1)]
    else:
        others = [to_partner(rounded, "col", s) for s in range(1, ncol)]
    vectors = group * ncol
    part = pl.pallas_call(
        gram_kernel,
        name="gram",
        out_shape=sds((vectors // 2, vectors), F32),
        in_specs=[VMEM] * (1 + len(others)),
        out_specs=VMEM,
        scratch_shapes=[pltpu.VMEM((ncol, group, rows), BF16), pltpu.VMEM((vectors, vectors), F32)],
        compiler_params=params(LIMIT),
    )(current, *others)
    wide = 1
    while 2 * wide < nblk:
        part = part + to_partner(part, "blk", wide)
        wide *= 2
    parts = [part, to_partner(part, "blk", wide)] if wide < nblk else [part]
    return pl.pallas_call(
        functools.partial(factor_kernel, len(parts), rows * nblk),
        name="factor",
        out_shape=sds((group, rows), F32),
        in_specs=[VMEM] * (1 + len(parts) + len(others)),
        out_specs=VMEM,
        scratch_shapes=[
            pltpu.VMEM((ncol, group, rows), BF16),
            pltpu.VMEM((vectors, vectors), F32),
            pltpu.VMEM((vectors, vectors), F32),
        ],
        compiler_params=params(LIMIT),
    )(current, *parts, *others)


def solution(mesh):
    return jax.shard_map(
        per_device,
        mesh=mesh,
        in_specs=(
            P("col", "blk"),
            P("blk", None, None),
            P("blk", None, None),
            P("blk"),
            P("blk"),
            P("blk", None),
        ),
        out_specs=P("col", "blk"),
        check_vma=False,
    )
```

time: 141 us -> 126 us (0.89)
  blocking collectives: 22.9 us -> 0 us
  waiting for transfers between devices: 41 us -> 33.6 us
  Pallas kernels: 56.4 us -> 63.5 us
  starting transfers between devices: 19.8 us -> 25.8 us
    ppermute x22 -> x6, waiting for transfers between devices: 41 us -> 16.6 us  [to_partner(): return lax.ppermute(x, axis, [(i, i ^ mask) for i in range(n)])]
    all_to_all x0 -> x5, starting transfers between devices: none -> 23.3 us  [the longest x4 16 us: per_device(): lax.all_to_all(blocks, 'blk', split_axis=0, concat_axis=0, tiled=True)]
    all_gather x1 -> x0, blocking collectives: 22.9 us -> none  [per_device(): wanted = lax.all_gather(fetch_pick, 'blk', axis=0, tiled=True)]
    ppermute x22 -> x6, starting transfers between devices: 19.8 us -> 2.49 us  [to_partner(): return lax.ppermute(x, axis, [(i, i ^ mask) for i in range(n)])]
    all_to_all x0 -> x5, waiting for transfers between devices: none -> 17 us  [the longest x4 17 us: per_device(): lax.all_to_all(blocks, 'blk', split_axis=0, concat_axis=0, tiled=True)]
    pallas_call x14 -> x10, Pallas kernels: 43.2 us -> 50.2 us  [the longest x4 22.5 us: per_device(): pl.pallas_call(functools.partial(step_kernel, step), name='step', out_sha...]
  transfers between devices with their start and end apart: 22 -> 11, of which waited for: 12 -> 9; matrix products, arithmetic and copies ran while one was open for 0% -> 0% of each run, Pallas kernels for 7% -> 21%
where the time goes in v3:
time: 126 us; the launch traced here: 124 us
  Pallas kernels  63.5 us (50%)
  waiting for transfers between devices  33.6 us (27%)
  starting transfers between devices  25.8 us (20%)
  local copies, waits for them, and re-layouts  1.32 us (1%)
    pallas_call x4, Pallas kernels, per_device(): pl.pallas_call(functools.partial(step_kernel, step), name='step', out_sha...  22.5 us
    all_to_all x4, waiting for transfers between devices, per_device(): lax.all_to_all(blocks, 'blk', split_axis=0, concat_axis=0, tiled=True)  17 us
    ppermute x6, waiting for transfers between devices, to_partner(): return lax.ppermute(x, axis, [(i, i ^ mask) for i in range(n)])  16.6 us
    all_to_all x4, starting transfers between devices, per_device(): lax.all_to_all(blocks, 'blk', split_axis=0, concat_axis=0, tiled=True)  16 us
    pallas_call x1, Pallas kernels, tiles_call(): pl.pallas_call(functools.partial(tiles_kernel, near_count), name='tiles',...  14.2 us
    pallas_call x1, Pallas kernels, per_device(): pl.pallas_call(functools.partial(factor_kernel, len(parts), rows * nblk),...  12.8 us
    pallas_call x4, Pallas kernels, per_device(): pl.pallas_call(near_kernel, name='near', out_shape=sds((rb_dev, group, or...  12.2 us
    all_to_all x1, starting transfers between devices, per_device(): lax.all_to_all(fetch_pick.reshape(nblk, 1), 'blk', split_axis=0, concat_a...  7.28 us
  transfers between devices with their start and end apart: 11, of which 9 were waited for; matrix products, arithmetic and copies ran while one was open for 0% of the time, Pallas kernels for 21%

profile of v3, /device:TPU:0, one launch (start us, length us, event | category | flops | bytes accessed | tf_op | source)
XLA Modules:
  0.0 124.3 jit_solution(17232130048473547714)
XLA Ops:
  1.3 7.3 %all-to-all-start = ((s32[8,1,1]{2,1,0:T(1,128)}), s32[8,1,1]{2,1,0:T(1,128)S(1)}, u32[]{:S(2)}, u32[]{:S(2)}) async-start(s32[8,1,1]{2,1,0:T(1,128)} %copy.18), calls=%async_computation | async-start | bytes 8192 | tf_op jit(solution)/shard_map/all_to_all | solution.py:413
  8.6 14.2 %tiles.1 = (f8e4m3fn[96,256,512]{2,1,0:T(32,128)(4,1)}, f32[8,2048]{1,0:T(8,128)S(1)}, s32[128]{0:T(128)S(1)}) custom-call(s32[96]{0:T(128)} %rows_ref.1, s32[96]{0:T(128)} %slots_ref.1, bf16[96,256,256]{2,1,0:T(8,128)(2,1)} %real_hbm.1, bf16[96,256,256]{2,1,0:T(8,128)(2,1)} %imag_hbm.1), custom_call_target="tpu_custom_call" | custom-call | flops 268435456 | bytes 25165824 | tf_op jit(solution)/shard_map/tiles/pallas_call | solution.py:187
  24.2 5.8 %all-to-all-start.1 = ((bf16[8,32,256]{2,1,0:T(8,128)(2,1)}), bf16[8,32,256]{2,1,0:T(8,128)(2,1)S(1)}, u32[]{:S(2)}, u32[]{:S(2)}) async-start(bf16[8,32,256]{2,1,0:T(8,128)(2,1)} %get-tuple-element.23), calls=%async_computation.1 | async-start | bytes 262144 | tf_op jit(solution)/shard_map/all_to_all | solution.py:439
  30.0 3.0 %near.4.near_ref = f32[8,32,256]{2,1,0:T(8,128)S(1)} custom-call(s32[128]{0:T(128)S(1)} %get-tuple-element.19.plan_ref, f8e4m3fn[96,256,512]{2,1,0:T(32,128)(4,1)} %get-tuple-element.20.packed_hbm, bf16[8,32,256]{2,1,0:T(8,128)(2,1)S(1)} %get-tuple-element.22.sent_ref), custom_call_target="tpu_custom_call" | custom-call | flops 268435456 | bytes 2097152 | tf_op jit(solution)/shard_map/near/pallas_call | solution.py:440
  33.0 4.3 %all-to-all-done.1.arrived_ref = bf16[8,32,256]{2,1,0:T(8,128)(2,1)S(1)} async-done(((bf16[8,32,256]{2,1,0:T(8,128)(2,1)}), bf16[8,32,256]{2,1,0:T(8,128)(2,1)S(1)}, u32[]{:S(2)}, u32[]{:S(2)}) %all-to-all-start.1) | async-done | bytes 131104 | tf_op jit(solution)/shard_map/all_to_all | solution.py:439
  37.3 5.8 %step.4 = (f32[32,2048]{1,0:T(8,128)S(1)}, bf16[8,32,256]{2,1,0:T(8,128)(2,1)S(1)}, bf16[8,32,256]{2,1,0:T(8,128)(2,1)}) custom-call(s32[128]{0:T(128)S(1)} %get-tuple-element.19.plan_ref, s32[8,1]{1,0:T(8,128)S(1)} %bitcast.3, f8e4m3fn[96,256,512]{2,1,0:T(32,128)(4,1)} %get-tuple-element.20.packed_hbm, f32[8,2048]{1,0:T(8,128)S(1)} %get-tuple-element.21.scale_ref, ...), custom_call_target="tpu_custom_call" | custom-call | tf_op jit(solution)/shard_map/step/pallas_call | solution.py:452
  43.1 3.4 %all-to-all-start.2 = ((bf16[8,32,256]{2,1,0:T(8,128)(2,1)}), bf16[8,32,256]{2,1,0:T(8,128)(2,1)S(1)}, u32[]{:S(2)}, u32[]{:S(2)}) async-start(bf16[8,32,256]{2,1,0:T(8,128)(2,1)} %get-tuple-element.26), calls=%async_computation.2 | async-start | bytes 262144 | tf_op jit(solution)/shard_map/all_to_all | solution.py:439
  46.5 3.0 %near.5.near_ref = f32[8,32,256]{2,1,0:T(8,128)S(1)} custom-call(s32[128]{0:T(128)S(1)} %get-tuple-element.19.plan_ref, f8e4m3fn[96,256,512]{2,1,0:T(32,128)(4,1)} %get-tuple-element.20.packed_hbm, bf16[8,32,256]{2,1,0:T(8,128)(2,1)S(1)} %get-tuple-element.24.sent_ref), custom_call_target="tpu_custom_call" | custom-call | flops 268435456 | bytes 2097152 | tf_op jit(solution)/shard_map/near/pallas_call | solution.py:440
  49.5 4.2 %all-to-all-done.2.arrived_ref = bf16[8,32,256]{2,1,0:T(8,128)(2,1)S(1)} async-done(((bf16[8,32,256]{2,1,0:T(8,128)(2,1)}), bf16[8,32,256]{2,1,0:T(8,128)(2,1)S(1)}, u32[]{:S(2)}, u32[]{:S(2)}) %all-to-all-start.2) | async-done | bytes 131104 | tf_op jit(solution)/shard_map/all_to_all | solution.py:439
  53.8 5.8 %step.5 = (f32[32,2048]{1,0:T(8,128)S(1)}, bf16[8,32,256]{2,1,0:T(8,128)(2,1)S(1)}, bf16[8,32,256]{2,1,0:T(8,128)(2,1)}) custom-call(s32[128]{0:T(128)S(1)} %get-tuple-element.19.plan_ref, s32[8,1]{1,0:T(8,128)S(1)} %bitcast.4, f8e4m3fn[96,256,512]{2,1,0:T(32,128)(4,1)} %get-tuple-element.20.packed_hbm, f32[8,2048]{1,0:T(8,128)S(1)} %get-tuple-element.21.scale_ref, ...), custom_call_target="tpu_custom_call" | custom-call | tf_op jit(solution)/shard_map/step/pallas_call | solution.py:452
  59.5 3.4 %all-to-all-start.3 = ((bf16[8,32,256]{2,1,0:T(8,128)(2,1)}), bf16[8,32,256]{2,1,0:T(8,128)(2,1)S(1)}, u32[]{:S(2)}, u32[]{:S(2)}) async-start(bf16[8,32,256]{2,1,0:T(8,128)(2,1)} %get-tuple-element.29), calls=%async_computation.3 | async-start | bytes 262144 | tf_op jit(solution)/shard_map/all_to_all | solution.py:439
  62.9 3.0 %near.6.near_ref = f32[8,32,256]{2,1,0:T(8,128)S(1)} custom-call(s32[128]{0:T(128)S(1)} %get-tuple-element.19.plan_ref, f8e4m3fn[96,256,512]{2,1,0:T(32,128)(4,1)} %get-tuple-element.20.packed_hbm, bf16[8,32,256]{2,1,0:T(8,128)(2,1)S(1)} %get-tuple-element.27.sent_ref), custom_call_target="tpu_custom_call" | custom-call | flops 268435456 | bytes 2097152 | tf_op jit(solution)/shard_map/near/pallas_call | solution.py:440
  66.0 4.2 %all-to-all-done.3.arrived_ref = bf16[8,32,256]{2,1,0:T(8,128)(2,1)S(1)} async-done(((bf16[8,32,256]{2,1,0:T(8,128)(2,1)}), bf16[8,32,256]{2,1,0:T(8,128)(2,1)S(1)}, u32[]{:S(2)}, u32[]{:S(2)}) %all-to-all-start.3) | async-done | bytes 131104 | tf_op jit(solution)/shard_map/all_to_all | solution.py:439
  70.2 5.8 %step.6 = (f32[32,2048]{1,0:T(8,128)S(1)}, bf16[8,32,256]{2,1,0:T(8,128)(2,1)S(1)}, bf16[8,32,256]{2,1,0:T(8,128)(2,1)}) custom-call(s32[128]{0:T(128)S(1)} %get-tuple-element.19.plan_ref, s32[8,1]{1,0:T(8,128)S(1)} %bitcast.5, f8e4m3fn[96,256,512]{2,1,0:T(32,128)(4,1)} %get-tuple-element.20.packed_hbm, f32[8,2048]{1,0:T(8,128)S(1)} %get-tuple-element.21.scale_ref, ...), custom_call_target="tpu_custom_call" | custom-call | tf_op jit(solution)/shard_map/step/pallas_call | solution.py:452
  76.0 3.4 %all-to-all-start.4 = ((bf16[8,32,256]{2,1,0:T(8,128)(2,1)}), bf16[8,32,256]{2,1,0:T(8,128)(2,1)S(1)}, u32[]{:S(2)}, u32[]{:S(2)}) async-start(bf16[8,32,256]{2,1,0:T(8,128)(2,1)} %get-tuple-element.32), calls=%async_computation.4 | async-start | bytes 262144 | tf_op jit(solution)/shard_map/all_to_all | solution.py:439
  79.4 3.0 %near.7.near_ref = f32[8,32,256]{2,1,0:T(8,128)S(1)} custom-call(s32[128]{0:T(128)S(1)} %get-tuple-element.19.plan_ref, f8e4m3fn[96,256,512]{2,1,0:T(32,128)(4,1)} %get-tuple-element.20.packed_hbm, bf16[8,32,256]{2,1,0:T(8,128)(2,1)S(1)} %get-tuple-element.30.sent_ref), custom_call_target="tpu_custom_call" | custom-call | flops 268435456 | bytes 2097152 | tf_op jit(solution)/shard_map/near/pallas_call | solution.py:440
  82.4 4.2 %all-to-all-done.4.arrived_ref = bf16[8,32,256]{2,1,0:T(8,128)(2,1)S(1)} async-done(((bf16[8,32,256]{2,1,0:T(8,128)(2,1)}), bf16[8,32,256]{2,1,0:T(8,128)(2,1)S(1)}, u32[]{:S(2)}, u32[]{:S(2)}) %all-to-all-start.4) | async-done | bytes 131104 | tf_op jit(solution)/shard_map/all_to_all | solution.py:439
  86.7 5.3 %step.7.own_ref = f32[32,2048]{1,0:T(8,128)S(1)} custom-call(s32[128]{0:T(128)S(1)} %get-tuple-element.19.plan_ref, s32[8,1]{1,0:T(8,128)S(1)} %bitcast.6, f8e4m3fn[96,256,512]{2,1,0:T(32,128)(4,1)} %get-tuple-element.20.packed_hbm, f32[8,2048]{1,0:T(8,128)S(1)} %get-tuple-element.21.scale_ref, f32[8,32,256]{2,1,0:T(8,128)S(1)} %near.7.near_ref, ...), custom_call_target="tpu_custom_call" | custom-call | tf_op jit(solution)/shard_map/step/pallas_call | solution.py:452
  92.0 1.6 %collective-permute-start.1 = (bf16[32,2048]{1,0:T(8,128)(2,1)S(1)}, bf16[32,2048]{1,0:T(8,128)(2,1)S(1)}, u32[]{:S(2)}, u32[]{:S(2)}) collective-permute-start(bf16[32,2048]{1,0:T(8,128)(2,1)S(1)} %convert_element_type.3), channel_id=1, source_target_pairs={{0,2},{1,3},{2,0},{3,1},{4,6},{5,7},{6,4},{7,5},{8,10},{9,11},{10,... | collective-permute-start | bytes 393224 | tf_op jit(solution)/shard_map/ppermute | solution.py:403
  93.5 3.5 %collective-permute-done.1.refs_1_.refs_3_ = bf16[32,2048]{1,0:T(8,128)(2,1)S(1)} collective-permute-done((bf16[32,2048]{1,0:T(8,128)(2,1)S(1)}, bf16[32,2048]{1,0:T(8,128)(2,1)S(1)}, u32[]{:S(2)}, u32[]{:S(2)}) %collective-permute-start.1) | collective-permute-done | bytes 131104 | tf_op jit(solution)/shard_map/ppermute | solution.py:403
  99.3 3.4 %collective-permute-done.3 = f32[64,128]{1,0:T(8,128)S(1)} collective-permute-done((f32[64,128]{1,0:T(8,128)S(1)}, f32[64,128]{1,0:T(8,128)S(1)}, u32[]{:S(2)}, u32[]{:S(2)}) %collective-permute-start.3) | collective-permute-done | bytes 32800 | tf_op jit(solution)/shard_map/ppermute | solution.py:403
  102.8 3.9 %collective-permute-done.4 = f32[64,128]{1,0:T(8,128)S(1)} collective-permute-done((f32[64,128]{1,0:T(8,128)S(1)}, f32[64,128]{1,0:T(8,128)S(1)}, u32[]{:S(2)}, u32[]{:S(2)}) %collective-permute-start.4) | collective-permute-done | bytes 32800 | tf_op jit(solution)/shard_map/ppermute | solution.py:403
  107.1 4.4 %collective-permute-done.5.refs_1_ = f32[64,128]{1,0:T(8,128)S(1)} collective-permute-done((f32[64,128]{1,0:T(8,128)S(1)}, f32[64,128]{1,0:T(8,128)S(1)}, u32[]{:S(2)}, u32[]{:S(2)}) %collective-permute-start.5) | collective-permute-done | bytes 32800 | tf_op jit(solution)/shard_map/ppermute | solution.py:403
  111.5 12.8 %factor.1 = f32[32,2048]{1,0:T(8,128)} custom-call(f32[32,2048]{1,0:T(8,128)S(1)} %step.7.own_ref, f32[64,128]{1,0:T(8,128)S(1)} %add.7.refs_0_, f32[64,128]{1,0:T(8,128)S(1)} %collective-permute-done.5.refs_1_, bf16[32,2048]{1,0:T(8,128)(2,1)S(1)} %collective-permute-done.refs_0_.refs_2_, bf16[32,2048]{1,0:T(8,128)(2,1)S(1)} %collective-permute-done.1.refs_1_.refs_3_, ...), custom_call_target="tpu_custom_call" | custom-call | tf_op jit(solution)/shard_map/factor/pallas_call | solution.py:486
  (16 shorter events, 5.3 us)
Async XLA Ops:
  1.3 21.5 %all-to-all-start = ((s32[8,1,1]{2,1,0:T(1,128)}), s32[8,1,1]{2,1,0:T(1,128)S(1)}, u32[]{:S(2)}, u32[]{:S(2)}) async-start(s32[8,1,1]{2,1,0:T(1,128)} %copy.18), calls=%async_computation | async-start | bytes 8192 | tf_op jit(solution)/shard_map/all_to_all | solution.py:413
  8.6 14.3 %copy-start = (f32[32,2048]{1,0:T(8,128)S(1)}, f32[32,2048]{1,0:T(8,128)}, u32[]{:S(2)}) copy-start(f32[32,2048]{1,0:T(8,128)} %before_ref.3) | copy-start | bytes 786436
  24.2 13.2 %all-to-all-start.1 = ((bf16[8,32,256]{2,1,0:T(8,128)(2,1)}), bf16[8,32,256]{2,1,0:T(8,128)(2,1)S(1)}, u32[]{:S(2)}, u32[]{:S(2)}) async-start(bf16[8,32,256]{2,1,0:T(8,128)(2,1)} %get-tuple-element.23), calls=%async_computation.1 | async-start | bytes 262144 | tf_op jit(solution)/shard_map/all_to_all | solution.py:439
  43.1 10.7 %all-to-all-start.2 = ((bf16[8,32,256]{2,1,0:T(8,128)(2,1)}), bf16[8,32,256]{2,1,0:T(8,128)(2,1)S(1)}, u32[]{:S(2)}, u32[]{:S(2)}) async-start(bf16[8,32,256]{2,1,0:T(8,128)(2,1)} %get-tuple-element.26), calls=%async_computation.2 | async-start | bytes 262144 | tf_op jit(solution)/shard_map/all_to_all | solution.py:439
  59.5 10.7 %all-to-all-start.3 = ((bf16[8,32,256]{2,1,0:T(8,128)(2,1)}), bf16[8,32,256]{2,1,0:T(8,128)(2,1)S(1)}, u32[]{:S(2)}, u32[]{:S(2)}) async-start(bf16[8,32,256]{2,1,0:T(8,128)(2,1)} %get-tuple-element.29), calls=%async_computation.3 | async-start | bytes 262144 | tf_op jit(solution)/shard_map/all_to_all | solution.py:439
  76.0 10.7 %all-to-all-start.4 = ((bf16[8,32,256]{2,1,0:T(8,128)(2,1)}), bf16[8,32,256]{2,1,0:T(8,128)(2,1)S(1)}, u32[]{:S(2)}, u32[]{:S(2)}) async-start(bf16[8,32,256]{2,1,0:T(8,128)(2,1)} %get-tuple-element.32), calls=%async_computation.4 | async-start | bytes 262144 | tf_op jit(solution)/shard_map/all_to_all | solution.py:439
  92.0 5.0 %collective-permute-start.1 = (bf16[32,2048]{1,0:T(8,128)(2,1)S(1)}, bf16[32,2048]{1,0:T(8,128)(2,1)S(1)}, u32[]{:S(2)}, u32[]{:S(2)}) collective-permute-start(bf16[32,2048]{1,0:T(8,128)(2,1)S(1)} %convert_element_type.3), channel_id=1, source_target_pairs={{0,2},{1,3},{2,0},{3,1},{4,6},{5,7},{6,4},{7,5},{8,10},{9,11},{10,... | collective-permute-start | bytes 393224 | tf_op jit(solution)/shard_map/ppermute | solution.py:403
  93.5 3.5 %collective-permute-start = (bf16[32,2048]{1,0:T(8,128)(2,1)S(1)}, bf16[32,2048]{1,0:T(8,128)(2,1)S(1)}, u32[]{:S(2)}, u32[]{:S(2)}) collective-permute-start(bf16[32,2048]{1,0:T(8,128)(2,1)S(1)} %convert_element_type.3), channel_id=1, source_target_pairs={{0,1},{1,0},{2,3},{3,2},{4,5},{5,4},{6,7},{7,6},{8,9},{9,8},{10,11... | collective-permute-start | bytes 393224 | tf_op jit(solution)/shard_map/ppermute | solution.py:403
  97.0 1.3 %collective-permute-start.2 = (bf16[32,2048]{1,0:T(8,128)(2,1)S(1)}, bf16[32,2048]{1,0:T(8,128)(2,1)S(1)}, u32[]{:S(2)}, u32[]{:S(2)}) collective-permute-start(bf16[32,2048]{1,0:T(8,128)(2,1)S(1)} %collective-permute-done.1.refs_1_.refs_3_), channel_id=1, source_target_pairs={{0,1},{1,0},{2,3},{3,2},{4,5},{5,4},{6,7},{7,6},{8,9},{9,8},{10,11... | collective-permute-start | bytes 393224 | tf_op jit(solution)/shard_map/ppermute | solution.py:403
  98.8 4.0 %collective-permute-start.3 = (f32[64,128]{1,0:T(8,128)S(1)}, f32[64,128]{1,0:T(8,128)S(1)}, u32[]{:S(2)}, u32[]{:S(2)}) collective-permute-start(f32[64,128]{1,0:T(8,128)S(1)} %gram.1), channel_id=1, source_target_pairs={{0,4},{4,0},{8,12},{12,8},{16,20},{20,16},{24,28},{28,24},{1,5},{5... | collective-permute-start | bytes 98312 | tf_op jit(solution)/shard_map/ppermute | solution.py:403
  102.7 3.9 %collective-permute-start.4 = (f32[64,128]{1,0:T(8,128)S(1)}, f32[64,128]{1,0:T(8,128)S(1)}, u32[]{:S(2)}, u32[]{:S(2)}) collective-permute-start(f32[64,128]{1,0:T(8,128)S(1)} %add.6), channel_id=1, source_target_pairs={{0,8},{4,12},{8,0},{12,4},{16,24},{20,28},{24,16},{28,20},{1,9},{5... | collective-permute-start | bytes 98312 | tf_op jit(solution)/shard_map/ppermute | solution.py:403
  106.7 4.8 %collective-permute-start.5 = (f32[64,128]{1,0:T(8,128)S(1)}, f32[64,128]{1,0:T(8,128)S(1)}, u32[]{:S(2)}, u32[]{:S(2)}) collective-permute-start(f32[64,128]{1,0:T(8,128)S(1)} %add.7.refs_0_), channel_id=1, source_target_pairs={{0,16},{4,20},{8,24},{12,28},{16,0},{20,4},{24,8},{28,12},{1,17},{... | collective-permute-start | bytes 98312 | tf_op jit(solution)/shard_map/ppermute | solution.py:403

commit v4 on v3

--- a/solution.py
+++ b/solution.py
@@ -335,7 +335,7 @@
     gram_ref[...] = even + turn_lanes(odd)
 
 
-PANEL = 16
+PANEL = 32
 
 
 def factor_kernel(grams, nodes, own_ref, *refs):
@@ -353,27 +353,30 @@
     row_at = lax.broadcasted_iota(I32, (order, order), 0)
     lane_at = lax.broadcasted_iota(I32, (order, order), 1)
     inverse_ref[...] = (row_at == lane_at).astype(F32)
-    here = lax.broadcasted_iota(I32, (PANEL, 1), 0)
+    here = lax.broadcasted_iota(I32, (PANEL, order), 0)
     for top in range(0, order, PANEL):
-        panel = jnp.concatenate([work_ref[top : top + PANEL, :], inverse_ref[top : top + PANEL, :]], axis=1)
+        a = work_ref[top : top + PANEL, :]
+        m = inverse_ref[top : top + PANEL, :]
+        pivots = jnp.ones_like(a)
         for k in range(0, PANEL, 2):
             lane = top + k
-            left = panel[:, lane : lane + 1]
-            right = panel[:, lane + 1 : lane + 2]
-            inv = lax.rsqrt(left[k : k + 1, :])
-            inv2 = inv * inv
-            below = here > k + 1
-            pair = here - k
-            a = jnp.where(below, left * inv2, 0.0)
-            b = jnp.where(below, right * inv2, 0.0)
-            keep = jnp.where((pair == 0) | (pair == 1), inv, 1.0)
-            panel = panel * keep - (a * panel[k : k + 1, :] + b * panel[k + 1 : k + 2, :])
-        inverse_ref[top : top + PANEL, :] = panel[:, order:]
+            left = jnp.broadcast_to(a[:, lane : lane + 1], a.shape)
+            right = jnp.broadcast_to(a[:, lane + 1 : lane + 2], a.shape)
+            pivot = left[k : k + 1, :]
+            inverse = 1.0 / pivot
+            left = jnp.where(here > k + 1, left, 0.0) * inverse
+            right = jnp.where(here > k + 1, right, 0.0) * inverse
+            pivots = jnp.where((here == k) | (here == k + 1), pivot, pivots)
+            a, m = (
+                v - left * v[k : k + 1, :] - right * v[k + 1 : k + 2, :] for v in (a, m)
+            )
+        root = lax.rsqrt(pivots)
+        a, m = a * root, m * root
+        inverse_ref[top : top + PANEL, :] = m
         rest = top + PANEL
         if rest < order:
-            cols = panel[:, 0:order]
             update = lax.dot_general(
-                cols, panel, TN, precision=lax.Precision.HIGHEST, preferred_element_type=F32
+                a, jnp.concatenate([a, m], axis=1), TN, precision=lax.Precision.HIGHEST, preferred_element_type=F32
             )
             work_ref[rest:, :] = work_ref[rest:, :] - update[rest:, :order]
             inverse_ref[rest:, :] = inverse_ref[rest:, :] - update[rest:, order:]

time: 126 us -> 119 us (0.944)
  Pallas kernels: 63.5 us -> 57 us
    pallas_call x1, Pallas kernels: 12.8 us -> 7.63 us  [per_device(): pl.pallas_call(functools.partial(factor_kernel, len(parts), rows * nblk),...]
  transfers between devices with their start and end apart: 11 -> 11, of which waited for: 9 -> 9; matrix products, arithmetic and copies ran while one was open for 0% -> 0% of each run, Pallas kernels for 21% -> 22%
where the time goes in v4:
time: 119 us; the launch traced here: 118 us
  Pallas kernels  57 us (48%)
  waiting for transfers between devices  32.7 us (27%)
  starting transfers between devices  27 us (23%)
  local copies, waits for them, and re-layouts  1.32 us (1%)
    pallas_call x4, Pallas kernels, per_device(): pl.pallas_call(functools.partial(step_kernel, step), name='step', out_sha...  21.5 us
    all_to_all x4, waiting for transfers between devices, per_device(): lax.all_to_all(blocks, 'blk', split_axis=0, concat_axis=0, tiled=True)  17 us
    all_to_all x4, starting transfers between devices, per_device(): lax.all_to_all(blocks, 'blk', split_axis=0, concat_axis=0, tiled=True)  16.3 us
    ppermute x6, waiting for transfers between devices, to_partner(): return lax.ppermute(x, axis, [(i, i ^ mask) for i in range(n)])  15.7 us
    pallas_call x1, Pallas kernels, tiles_call(): pl.pallas_call(functools.partial(tiles_kernel, near_count), name='tiles',...  14 us
    pallas_call x4, Pallas kernels, per_device(): pl.pallas_call(near_kernel, name='near', out_shape=sds((rb_dev, group, or...  12.2 us
    pallas_call x1, Pallas kernels, per_device(): pl.pallas_call(functools.partial(factor_kernel, len(parts), rows * nblk),...  7.63 us
    all_to_all x1, starting transfers between devices, per_device(): lax.all_to_all(fetch_pick.reshape(nblk, 1), 'blk', split_axis=0, concat_a...  7.28 us
  transfers between devices with their start and end apart: 11, of which 9 were waited for; matrix products, arithmetic and copies ran while one was open for 0% of the time, Pallas kernels for 22%

profile of v4, /device:TPU:0, one launch (start us, length us, event | category | flops | bytes accessed | tf_op | source)
XLA Modules:
  0.0 118.1 jit_solution(5021529985275407053)
XLA Ops:
  1.3 7.3 %all-to-all-start = ((s32[8,1,1]{2,1,0:T(1,128)}), s32[8,1,1]{2,1,0:T(1,128)S(1)}, u32[]{:S(2)}, u32[]{:S(2)}) async-start(s32[8,1,1]{2,1,0:T(1,128)} %copy.18), calls=%async_computation | async-start | bytes 8192 | tf_op jit(solution)/shard_map/all_to_all | solution.py:416
  8.6 14.0 %tiles.1 = (f8e4m3fn[96,256,512]{2,1,0:T(32,128)(4,1)}, f32[8,2048]{1,0:T(8,128)S(1)}, s32[128]{0:T(128)S(1)}) custom-call(s32[96]{0:T(128)} %rows_ref.1, s32[96]{0:T(128)} %slots_ref.1, bf16[96,256,256]{2,1,0:T(8,128)(2,1)} %real_hbm.1, bf16[96,256,256]{2,1,0:T(8,128)(2,1)} %imag_hbm.1), custom_call_target="tpu_custom_call" | custom-call | flops 268435456 | bytes 25165824 | tf_op jit(solution)/shard_map/tiles/pallas_call | solution.py:187
  23.9 6.1 %all-to-all-start.1 = ((bf16[8,32,256]{2,1,0:T(8,128)(2,1)}), bf16[8,32,256]{2,1,0:T(8,128)(2,1)S(1)}, u32[]{:S(2)}, u32[]{:S(2)}) async-start(bf16[8,32,256]{2,1,0:T(8,128)(2,1)} %get-tuple-element.23), calls=%async_computation.1 | async-start | bytes 262144 | tf_op jit(solution)/shard_map/all_to_all | solution.py:442
  30.0 3.0 %near.4.near_ref = f32[8,32,256]{2,1,0:T(8,128)S(1)} custom-call(s32[128]{0:T(128)S(1)} %get-tuple-element.19.plan_ref, f8e4m3fn[96,256,512]{2,1,0:T(32,128)(4,1)} %get-tuple-element.20.packed_hbm, bf16[8,32,256]{2,1,0:T(8,128)(2,1)S(1)} %get-tuple-element.22.sent_ref), custom_call_target="tpu_custom_call" | custom-call | flops 268435456 | bytes 2097152 | tf_op jit(solution)/shard_map/near/pallas_call | solution.py:443
  33.1 4.3 %all-to-all-done.1.arrived_ref = bf16[8,32,256]{2,1,0:T(8,128)(2,1)S(1)} async-done(((bf16[8,32,256]{2,1,0:T(8,128)(2,1)}), bf16[8,32,256]{2,1,0:T(8,128)(2,1)S(1)}, u32[]{:S(2)}, u32[]{:S(2)}) %all-to-all-start.1) | async-done | bytes 131104 | tf_op jit(solution)/shard_map/all_to_all | solution.py:442
  37.4 5.5 %step.4 = (f32[32,2048]{1,0:T(8,128)S(1)}, bf16[8,32,256]{2,1,0:T(8,128)(2,1)S(1)}, bf16[8,32,256]{2,1,0:T(8,128)(2,1)}) custom-call(s32[128]{0:T(128)S(1)} %get-tuple-element.19.plan_ref, s32[8,1]{1,0:T(8,128)S(1)} %bitcast.3, f8e4m3fn[96,256,512]{2,1,0:T(32,128)(4,1)} %get-tuple-element.20.packed_hbm, f32[8,2048]{1,0:T(8,128)S(1)} %get-tuple-element.21.scale_ref, ...), custom_call_target="tpu_custom_call" | custom-call | tf_op jit(solution)/shard_map/step/pallas_call | solution.py:455
  42.9 3.4 %all-to-all-start.2 = ((bf16[8,32,256]{2,1,0:T(8,128)(2,1)}), bf16[8,32,256]{2,1,0:T(8,128)(2,1)S(1)}, u32[]{:S(2)}, u32[]{:S(2)}) async-start(bf16[8,32,256]{2,1,0:T(8,128)(2,1)} %get-tuple-element.26), calls=%async_computation.2 | async-start | bytes 262144 | tf_op jit(solution)/shard_map/all_to_all | solution.py:442
  46.3 3.0 %near.5.near_ref = f32[8,32,256]{2,1,0:T(8,128)S(1)} custom-call(s32[128]{0:T(128)S(1)} %get-tuple-element.19.plan_ref, f8e4m3fn[96,256,512]{2,1,0:T(32,128)(4,1)} %get-tuple-element.20.packed_hbm, bf16[8,32,256]{2,1,0:T(8,128)(2,1)S(1)} %get-tuple-element.24.sent_ref), custom_call_target="tpu_custom_call" | custom-call | flops 268435456 | bytes 2097152 | tf_op jit(solution)/shard_map/near/pallas_call | solution.py:443
  49.3 4.2 %all-to-all-done.2.arrived_ref = bf16[8,32,256]{2,1,0:T(8,128)(2,1)S(1)} async-done(((bf16[8,32,256]{2,1,0:T(8,128)(2,1)}), bf16[8,32,256]{2,1,0:T(8,128)(2,1)S(1)}, u32[]{:S(2)}, u32[]{:S(2)}) %all-to-all-start.2) | async-done | bytes 131104 | tf_op jit(solution)/shard_map/all_to_all | solution.py:442
  53.6 5.5 %step.5 = (f32[32,2048]{1,0:T(8,128)S(1)}, bf16[8,32,256]{2,1,0:T(8,128)(2,1)S(1)}, bf16[8,32,256]{2,1,0:T(8,128)(2,1)}) custom-call(s32[128]{0:T(128)S(1)} %get-tuple-element.19.plan_ref, s32[8,1]{1,0:T(8,128)S(1)} %bitcast.4, f8e4m3fn[96,256,512]{2,1,0:T(32,128)(4,1)} %get-tuple-element.20.packed_hbm, f32[8,2048]{1,0:T(8,128)S(1)} %get-tuple-element.21.scale_ref, ...), custom_call_target="tpu_custom_call" | custom-call | tf_op jit(solution)/shard_map/step/pallas_call | solution.py:455
  59.1 3.4 %all-to-all-start.3 = ((bf16[8,32,256]{2,1,0:T(8,128)(2,1)}), bf16[8,32,256]{2,1,0:T(8,128)(2,1)S(1)}, u32[]{:S(2)}, u32[]{:S(2)}) async-start(bf16[8,32,256]{2,1,0:T(8,128)(2,1)} %get-tuple-element.29), calls=%async_computation.3 | async-start | bytes 262144 | tf_op jit(solution)/shard_map/all_to_all | solution.py:442
  62.5 3.0 %near.6.near_ref = f32[8,32,256]{2,1,0:T(8,128)S(1)} custom-call(s32[128]{0:T(128)S(1)} %get-tuple-element.19.plan_ref, f8e4m3fn[96,256,512]{2,1,0:T(32,128)(4,1)} %get-tuple-element.20.packed_hbm, bf16[8,32,256]{2,1,0:T(8,128)(2,1)S(1)} %get-tuple-element.27.sent_ref), custom_call_target="tpu_custom_call" | custom-call | flops 268435456 | bytes 2097152 | tf_op jit(solution)/shard_map/near/pallas_call | solution.py:443
  65.5 4.2 %all-to-all-done.3.arrived_ref = bf16[8,32,256]{2,1,0:T(8,128)(2,1)S(1)} async-done(((bf16[8,32,256]{2,1,0:T(8,128)(2,1)}), bf16[8,32,256]{2,1,0:T(8,128)(2,1)S(1)}, u32[]{:S(2)}, u32[]{:S(2)}) %all-to-all-start.3) | async-done | bytes 131104 | tf_op jit(solution)/shard_map/all_to_all | solution.py:442
  69.7 5.5 %step.6 = (f32[32,2048]{1,0:T(8,128)S(1)}, bf16[8,32,256]{2,1,0:T(8,128)(2,1)S(1)}, bf16[8,32,256]{2,1,0:T(8,128)(2,1)}) custom-call(s32[128]{0:T(128)S(1)} %get-tuple-element.19.plan_ref, s32[8,1]{1,0:T(8,128)S(1)} %bitcast.5, f8e4m3fn[96,256,512]{2,1,0:T(32,128)(4,1)} %get-tuple-element.20.packed_hbm, f32[8,2048]{1,0:T(8,128)S(1)} %get-tuple-element.21.scale_ref, ...), custom_call_target="tpu_custom_call" | custom-call | tf_op jit(solution)/shard_map/step/pallas_call | solution.py:455
  75.2 3.4 %all-to-all-start.4 = ((bf16[8,32,256]{2,1,0:T(8,128)(2,1)}), bf16[8,32,256]{2,1,0:T(8,128)(2,1)S(1)}, u32[]{:S(2)}, u32[]{:S(2)}) async-start(bf16[8,32,256]{2,1,0:T(8,128)(2,1)} %get-tuple-element.32), calls=%async_computation.4 | async-start | bytes 262144 | tf_op jit(solution)/shard_map/all_to_all | solution.py:442
  78.6 3.0 %near.7.near_ref = f32[8,32,256]{2,1,0:T(8,128)S(1)} custom-call(s32[128]{0:T(128)S(1)} %get-tuple-element.19.plan_ref, f8e4m3fn[96,256,512]{2,1,0:T(32,128)(4,1)} %get-tuple-element.20.packed_hbm, bf16[8,32,256]{2,1,0:T(8,128)(2,1)S(1)} %get-tuple-element.30.sent_ref), custom_call_target="tpu_custom_call" | custom-call | flops 268435456 | bytes 2097152 | tf_op jit(solution)/shard_map/near/pallas_call | solution.py:443
  81.7 4.2 %all-to-all-done.4.arrived_ref = bf16[8,32,256]{2,1,0:T(8,128)(2,1)S(1)} async-done(((bf16[8,32,256]{2,1,0:T(8,128)(2,1)}), bf16[8,32,256]{2,1,0:T(8,128)(2,1)S(1)}, u32[]{:S(2)}, u32[]{:S(2)}) %all-to-all-start.4) | async-done | bytes 131104 | tf_op jit(solution)/shard_map/all_to_all | solution.py:442
  85.9 5.0 %step.7.own_ref = f32[32,2048]{1,0:T(8,128)S(1)} custom-call(s32[128]{0:T(128)S(1)} %get-tuple-element.19.plan_ref, s32[8,1]{1,0:T(8,128)S(1)} %bitcast.6, f8e4m3fn[96,256,512]{2,1,0:T(32,128)(4,1)} %get-tuple-element.20.packed_hbm, f32[8,2048]{1,0:T(8,128)S(1)} %get-tuple-element.21.scale_ref, f32[8,32,256]{2,1,0:T(8,128)S(1)} %near.7.near_ref, ...), custom_call_target="tpu_custom_call" | custom-call | tf_op jit(solution)/shard_map/step/pallas_call | solution.py:455
  90.9 1.6 %collective-permute-start.1 = (bf16[32,2048]{1,0:T(8,128)(2,1)S(1)}, bf16[32,2048]{1,0:T(8,128)(2,1)S(1)}, u32[]{:S(2)}, u32[]{:S(2)}) collective-permute-start(bf16[32,2048]{1,0:T(8,128)(2,1)S(1)} %convert_element_type.3), channel_id=1, source_target_pairs={{0,2},{1,3},{2,0},{3,1},{4,6},{5,7},{6,4},{7,5},{8,10},{9,11},{10,... | collective-permute-start | bytes 393224 | tf_op jit(solution)/shard_map/ppermute | solution.py:406
  92.5 3.5 %collective-permute-done.1.refs_1_.refs_3_ = bf16[32,2048]{1,0:T(8,128)(2,1)S(1)} collective-permute-done((bf16[32,2048]{1,0:T(8,128)(2,1)S(1)}, bf16[32,2048]{1,0:T(8,128)(2,1)S(1)}, u32[]{:S(2)}, u32[]{:S(2)}) %collective-permute-start.1) | collective-permute-done | bytes 131104 | tf_op jit(solution)/shard_map/ppermute | solution.py:406
  98.6 3.2 %collective-permute-done.3 = f32[64,128]{1,0:T(8,128)S(1)} collective-permute-done((f32[64,128]{1,0:T(8,128)S(1)}, f32[64,128]{1,0:T(8,128)S(1)}, u32[]{:S(2)}, u32[]{:S(2)}) %collective-permute-start.3) | collective-permute-done | bytes 32800 | tf_op jit(solution)/shard_map/ppermute | solution.py:406
  101.9 3.8 %collective-permute-done.4 = f32[64,128]{1,0:T(8,128)S(1)} collective-permute-done((f32[64,128]{1,0:T(8,128)S(1)}, f32[64,128]{1,0:T(8,128)S(1)}, u32[]{:S(2)}, u32[]{:S(2)}) %collective-permute-start.4) | collective-permute-done | bytes 32800 | tf_op jit(solution)/shard_map/ppermute | solution.py:406
  106.6 3.9 %collective-permute-done.5.refs_1_ = f32[64,128]{1,0:T(8,128)S(1)} collective-permute-done((f32[64,128]{1,0:T(8,128)S(1)}, f32[64,128]{1,0:T(8,128)S(1)}, u32[]{:S(2)}, u32[]{:S(2)}) %collective-permute-start.5) | collective-permute-done | bytes 32800 | tf_op jit(solution)/shard_map/ppermute | solution.py:406
  110.5 7.6 %factor.1 = f32[32,2048]{1,0:T(8,128)} custom-call(f32[32,2048]{1,0:T(8,128)S(1)} %step.7.own_ref, f32[64,128]{1,0:T(8,128)S(1)} %add.7.refs_0_, f32[64,128]{1,0:T(8,128)S(1)} %collective-permute-done.5.refs_1_, bf16[32,2048]{1,0:T(8,128)(2,1)S(1)} %collective-permute-done.refs_0_.refs_2_, bf16[32,2048]{1,0:T(8,128)(2,1)S(1)} %collective-permute-done.1.refs_1_.refs_3_, ...), custom_call_target="tpu_custom_call" | custom-call | tf_op jit(solution)/shard_map/factor/pallas_call | solution.py:489
  (16 shorter events, 6.3 us)
Async XLA Ops:
  1.3 21.3 %all-to-all-start = ((s32[8,1,1]{2,1,0:T(1,128)}), s32[8,1,1]{2,1,0:T(1,128)S(1)}, u32[]{:S(2)}, u32[]{:S(2)}) async-start(s32[8,1,1]{2,1,0:T(1,128)} %copy.18), calls=%async_computation | async-start | bytes 8192 | tf_op jit(solution)/shard_map/all_to_all | solution.py:416
  8.6 14.0 %copy-start = (f32[32,2048]{1,0:T(8,128)S(1)}, f32[32,2048]{1,0:T(8,128)}, u32[]{:S(2)}) copy-start(f32[32,2048]{1,0:T(8,128)} %before_ref.3) | copy-start | bytes 786436
  23.9 13.5 %all-to-all-start.1 = ((bf16[8,32,256]{2,1,0:T(8,128)(2,1)}), bf16[8,32,256]{2,1,0:T(8,128)(2,1)S(1)}, u32[]{:S(2)}, u32[]{:S(2)}) async-start(bf16[8,32,256]{2,1,0:T(8,128)(2,1)} %get-tuple-element.23), calls=%async_computation.1 | async-start | bytes 262144 | tf_op jit(solution)/shard_map/all_to_all | solution.py:442
  42.9 10.7 %all-to-all-start.2 = ((bf16[8,32,256]{2,1,0:T(8,128)(2,1)}), bf16[8,32,256]{2,1,0:T(8,128)(2,1)S(1)}, u32[]{:S(2)}, u32[]{:S(2)}) async-start(bf16[8,32,256]{2,1,0:T(8,128)(2,1)} %get-tuple-element.26), calls=%async_computation.2 | async-start | bytes 262144 | tf_op jit(solution)/shard_map/all_to_all | solution.py:442
  59.1 10.7 %all-to-all-start.3 = ((bf16[8,32,256]{2,1,0:T(8,128)(2,1)}), bf16[8,32,256]{2,1,0:T(8,128)(2,1)S(1)}, u32[]{:S(2)}, u32[]{:S(2)}) async-start(bf16[8,32,256]{2,1,0:T(8,128)(2,1)} %get-tuple-element.29), calls=%async_computation.3 | async-start | bytes 262144 | tf_op jit(solution)/shard_map/all_to_all | solution.py:442
  75.2 10.7 %all-to-all-start.4 = ((bf16[8,32,256]{2,1,0:T(8,128)(2,1)}), bf16[8,32,256]{2,1,0:T(8,128)(2,1)S(1)}, u32[]{:S(2)}, u32[]{:S(2)}) async-start(bf16[8,32,256]{2,1,0:T(8,128)(2,1)} %get-tuple-element.32), calls=%async_computation.4 | async-start | bytes 262144 | tf_op jit(solution)/shard_map/all_to_all | solution.py:442
  90.9 5.0 %collective-permute-start.1 = (bf16[32,2048]{1,0:T(8,128)(2,1)S(1)}, bf16[32,2048]{1,0:T(8,128)(2,1)S(1)}, u32[]{:S(2)}, u32[]{:S(2)}) collective-permute-start(bf16[32,2048]{1,0:T(8,128)(2,1)S(1)} %convert_element_type.3), channel_id=1, source_target_pairs={{0,2},{1,3},{2,0},{3,1},{4,6},{5,7},{6,4},{7,5},{8,10},{9,11},{10,... | collective-permute-start | bytes 393224 | tf_op jit(solution)/shard_map/ppermute | solution.py:406
  92.5 3.5 %collective-permute-start = (bf16[32,2048]{1,0:T(8,128)(2,1)S(1)}, bf16[32,2048]{1,0:T(8,128)(2,1)S(1)}, u32[]{:S(2)}, u32[]{:S(2)}) collective-permute-start(bf16[32,2048]{1,0:T(8,128)(2,1)S(1)} %convert_element_type.3), channel_id=1, source_target_pairs={{0,1},{1,0},{2,3},{3,2},{4,5},{5,4},{6,7},{7,6},{8,9},{9,8},{10,11... | collective-permute-start | bytes 393224 | tf_op jit(solution)/shard_map/ppermute | solution.py:406
  96.0 1.3 %collective-permute-start.2 = (bf16[32,2048]{1,0:T(8,128)(2,1)S(1)}, bf16[32,2048]{1,0:T(8,128)(2,1)S(1)}, u32[]{:S(2)}, u32[]{:S(2)}) collective-permute-start(bf16[32,2048]{1,0:T(8,128)(2,1)S(1)} %collective-permute-done.1.refs_1_.refs_3_), channel_id=1, source_target_pairs={{0,1},{1,0},{2,3},{3,2},{4,5},{5,4},{6,7},{7,6},{8,9},{9,8},{10,11... | collective-permute-start | bytes 393224 | tf_op jit(solution)/shard_map/ppermute | solution.py:406
  97.8 4.0 %collective-permute-start.3 = (f32[64,128]{1,0:T(8,128)S(1)}, f32[64,128]{1,0:T(8,128)S(1)}, u32[]{:S(2)}, u32[]{:S(2)}) collective-permute-start(f32[64,128]{1,0:T(8,128)S(1)} %gram.1), channel_id=1, source_target_pairs={{0,4},{4,0},{8,12},{12,8},{16,20},{20,16},{24,28},{28,24},{1,5},{5... | collective-permute-start | bytes 98312 | tf_op jit(solution)/shard_map/ppermute | solution.py:406
  101.7 3.9 %collective-permute-start.4 = (f32[64,128]{1,0:T(8,128)S(1)}, f32[64,128]{1,0:T(8,128)S(1)}, u32[]{:S(2)}, u32[]{:S(2)}) collective-permute-start(f32[64,128]{1,0:T(8,128)S(1)} %add.6), channel_id=1, source_target_pairs={{0,8},{4,12},{8,0},{12,4},{16,24},{20,28},{24,16},{28,20},{1,9},{5... | collective-permute-start | bytes 98312 | tf_op jit(solution)/shard_map/ppermute | solution.py:406
  105.7 4.8 %collective-permute-start.5 = (f32[64,128]{1,0:T(8,128)S(1)}, f32[64,128]{1,0:T(8,128)S(1)}, u32[]{:S(2)}, u32[]{:S(2)}) collective-permute-start(f32[64,128]{1,0:T(8,128)S(1)} %add.7.refs_0_), channel_id=1, source_target_pairs={{0,16},{4,20},{8,24},{12,28},{16,0},{20,4},{24,8},{28,12},{1,17},{... | collective-permute-start | bytes 98312 | tf_op jit(solution)/shard_map/ppermute | solution.py:406

commit v5 on v4

--- a/solution.py
+++ b/solution.py
@@ -13,9 +13,9 @@
 UNROLL = 4
 CHUNK = 4
 MERGE = 16
-PARTS = 3
-TOP = 256.0
+TOP = 7.0
 FINER = 16.0
+SPLIT = float((1 << 20) + 1)
 TINY = 1e-30
 MIB = 1 << 20
 LIMIT = 24
@@ -209,17 +209,22 @@
     )(in_hbm(rows), in_hbm(slots), in_hbm(real), in_hbm(imag))
 
 
-def send_blocks(field, scale_ref, sent_ref, pick, out_ref):
+def rounded_block(field, scale_ref, r, order):
+    at = slice(r * order, (r + 1) * order)
+    return (field[:, at] * scale_ref[0:1, at]).astype(BF16)
+
+
+def send_blocks(field, scale_ref, wanted_ref, out_ref, sent_ref):
     order = sent_ref.shape[2]
+    me = lax.axis_index("blk")
     for r in range(sent_ref.shape[0]):
-        at = slice(r * order, (r + 1) * order)
-        sent_ref[r] = (field[:, at] * scale_ref[0:1, at]).astype(BF16)
+        sent_ref[r] = rounded_block(field, scale_ref, r, order)
     for p in range(out_ref.shape[0]):
-        out_ref[p] = sent_ref[pick(p)]
-
-
-def first_kernel(y_ref, scale_ref, wanted_ref, sent_ref, out_ref):
-    send_blocks(y_ref, scale_ref, sent_ref, lambda p: wanted_ref[p, 0], out_ref)
+        out_ref[p] = sent_ref[wanted_ref[p, 0, me]]
+
+
+def first_kernel(y_ref, scale_ref, wanted_ref, out_ref, sent_ref):
+    send_blocks(y_ref, scale_ref, wanted_ref, out_ref, sent_ref)
 
 
 def load_groups(packed_hbm, tiles_ref, sems, lo, hi):
@@ -237,25 +242,28 @@
     return copy
 
 
-def split_sources(source, x_ref):
-    count, group, order = source.shape
+def split_sources(count, source, x_ref):
+    _, rows, width = x_ref.shape
+    group, order = rows // 2, width // 2
     most = jnp.zeros((group, order), F32)
     for p in range(count):
-        most = jnp.maximum(most, jnp.abs(source[p].astype(F32)))
+        most = jnp.maximum(most, jnp.abs(source(p).astype(F32)))
     most = jnp.broadcast_to(jnp.max(most, axis=1, keepdims=True), (group, 128))
     most = jnp.maximum(jnp.maximum(most, jnp.abs(turn_rows(most))), TINY)
-    size = most[:, 0:1] / TOP
-    inverse = TOP / most[:, 0:1]
+    power = jnp.floor(jnp.log2(most))
+    size = jnp.exp2(power - TOP)
+    inverse = jnp.exp2(TOP - power)[:, 0:1]
     for p in range(count):
-        scaled = source[p].astype(F32) * inverse
-        for side, part in enumerate((scaled, turn_rows(scaled))):
-            at = slice(side * order, (side + 1) * order)
-            for k in range(PARTS):
-                short = part.astype(F8)
-                x_ref[p, k * group : (k + 1) * group, at] = short
-                part = (part - short.astype(F32)) * FINER
+        scaled = source(p).astype(F32) * inverse
+        far = scaled * SPLIT
+        high = far - (far - scaled)
+        low = (scaled - high) * FINER
+        for k, part in enumerate((high, low)):
+            at = slice(k * group, (k + 1) * group)
+            x_ref[p, at, :order] = part.astype(F8)
+            x_ref[p, at, order:] = turn_rows(part).astype(F8)
     x_ref[count] = jnp.zeros_like(x_ref[count])
-    return size
+    return size[:, 0:1]
 
 
 def multiply(plan_ref, lo, hi, copy, tiles_ref, load, acc_ref):
@@ -265,7 +273,7 @@
         for j in range(UNROLL):
             code = plan_ref[g * UNROLL + j]
             tile = tiles_ref[(g - lo) * UNROLL + j]
-            product = lax.dot_general(tile, load(code >> 8), NT, preferred_element_type=F32)
+            product = lax.dot_general(load(code >> 8), tile, NT, preferred_element_type=F32)
             done.append((code & 255, product))
         for row, product in done:
             acc_ref[row] = acc_ref[row] + product
@@ -276,44 +284,41 @@
 
 def collect(acc, size):
     group = size.shape[0]
-    flat = acc.T
-    total = flat[(PARTS - 1) * group : PARTS * group]
-    for k in range(PARTS - 2, -1, -1):
-        total = flat[k * group : (k + 1) * group] + total * (1.0 / FINER)
-    return total * size
-
-
-def near_kernel(plan_ref, packed_hbm, sent_ref, out_ref, tiles_ref, x_ref, acc_ref, sems):
-    rb_dev = sent_ref.shape[0]
-    at = plan_ref.shape[0] - 32
-    hi = plan_ref[at]
+    return (acc[:group] + acc[group:] * (1.0 / FINER)) * size
+
+
+def near_kernel(step, plan_ref, packed_hbm, scale_ref, now_ref, before_ref, base_ref, tiles_ref, x_ref, acc_ref, sems):
+    rb_dev, _, order = acc_ref.shape
+    end = plan_ref.shape[0] - 32
+    hi = plan_ref[end]
     copy = load_groups(packed_hbm, tiles_ref, sems, 0, hi)
     acc_ref[...] = jnp.zeros_like(acc_ref)
-    size = split_sources(sent_ref, x_ref)
+    size = split_sources(rb_dev, lambda r: rounded_block(now_ref, scale_ref, r, order), x_ref)
     multiply(plan_ref, 0, hi, copy, tiles_ref, lambda c: x_ref[jnp.minimum(c, rb_dev)], acc_ref)
     for r in range(rb_dev):
-        out_ref[r] = collect(acc_ref[r], size)
-
-
-def step_kernel(step, plan_ref, wanted_ref, packed_hbm, scale_ref, near_ref, now_ref, before_ref, arrived_ref, *refs):
+        at = slice(r * order, (r + 1) * order)
+        applied = scale_ref[0:1, at] * collect(acc_ref[r], size)
+        moved = ((1.0 - center) * now_ref[:, at] - applied) / half_width
+        base_ref[:, at] = moved if step == 0 else 2.0 * moved - before_ref[:, at]
+
+
+def step_kernel(step, plan_ref, wanted_ref, packed_hbm, scale_ref, base_ref, arrived_ref, *refs):
     last = step == STEPS - 1
     next_ref = refs[0]
     tiles_ref, x_ref, acc_ref, sems = refs[-4:]
-    rb_dev, _, order = near_ref.shape
-    at = plan_ref.shape[0] - 32
-    lo, hi = plan_ref[at], plan_ref[at + 1]
+    rb_dev, _, order = acc_ref.shape
+    end = plan_ref.shape[0] - 32
+    lo, hi = plan_ref[end], plan_ref[end + 1]
     copy = load_groups(packed_hbm, tiles_ref, sems, lo, hi)
     acc_ref[...] = jnp.zeros_like(acc_ref)
-    size = split_sources(arrived_ref, x_ref)
+    size = split_sources(arrived_ref.shape[0], lambda p: arrived_ref[p], x_ref)
+    size = size * ((1.0 if step == 0 else 2.0) / half_width)
     multiply(plan_ref, lo, hi, copy, tiles_ref, lambda c: x_ref[c - rb_dev], acc_ref)
     for r in range(rb_dev):
         at = slice(r * order, (r + 1) * order)
-        now = now_ref[:, at]
-        applied = scale_ref[0:1, at] * (near_ref[r] + collect(acc_ref[r], size))
-        moved = ((1.0 - center) * now - applied) / half_width
-        next_ref[:, at] = moved if step == 0 else 2.0 * moved - before_ref[:, at]
+        next_ref[:, at] = base_ref[:, at] - scale_ref[0:1, at] * collect(acc_ref[r], size)
     if not last:
-        send_blocks(next_ref, scale_ref, refs[1], lambda p: wanted_ref[p, 0], refs[2])
+        send_blocks(next_ref, scale_ref, wanted_ref, refs[1], refs[2])
 
 
 def all_rows(own_ref, arrived, all_ref):
@@ -414,56 +419,57 @@
     ncol = lax.axis_size("col")
     near_count = LOC_RB * rb_dev
     wanted = lax.all_to_all(
-        fetch_pick.reshape(nblk, 1), "blk", split_axis=0, concat_axis=0, tiled=True
+        jnp.broadcast_to(fetch_pick[None], (nblk, 1, nblk)), "blk", split_axis=0, concat_axis=0, tiled=True
     )
     packed, scale, plan = tiles_call(tile_rows, tile_slots, tile_real, tile_imag, rb_dev, near_count)
 
-    own_blocks = sds((rb_dev, group, order), BF16)
     out_blocks = sds((nblk, group, order), BF16)
-    sent, blocks = pl.pallas_call(
+    sent_scratch = pltpu.VMEM((rb_dev, group, order), BF16)
+    blocks = pl.pallas_call(
         first_kernel,
         name="first",
-        out_shape=(own_blocks, out_blocks),
+        out_shape=out_blocks,
         in_specs=[VMEM, VMEM, SMEM],
-        out_specs=(VMEM, VMEM),
+        out_specs=VMEM,
+        scratch_shapes=[sent_scratch],
         compiler_params=params(LIMIT),
     )(y_start, scale, wanted)
 
     def scratch(entries, sources):
         return [
             pltpu.VMEM((entries, order, 2 * order), F8),
-            pltpu.VMEM((sources + 1, PARTS * group, 2 * order), F8),
-            pltpu.VMEM((rb_dev, order, PARTS * group), F32),
+            pltpu.VMEM((sources + 1, 2 * group, 2 * order), F8),
+            pltpu.VMEM((rb_dev, 2 * group, order), F32),
             pltpu.SemaphoreType.DMA((entries // UNROLL,)),
         ]
 
+    vectors_here = sds((group, rows), F32)
     previous, current = y_start, y_start
     for step in range(STEPS):
         arrived = lax.all_to_all(blocks, "blk", split_axis=0, concat_axis=0, tiled=True)
-        near = pl.pallas_call(
-            near_kernel,
+        base = pl.pallas_call(
+            functools.partial(near_kernel, step),
             name="near",
-            out_shape=sds((rb_dev, group, order), F32),
-            in_specs=[SMEM, ANY, VMEM],
+            out_shape=vectors_here,
+            in_specs=[SMEM, ANY] + [VMEM] * 3,
             out_specs=VMEM,
             scratch_shapes=scratch(near_count, rb_dev),
             compiler_params=params(LIMIT),
             cost_estimate=pl.CostEstimate(flops=1 << 28, bytes_accessed=1 << 21, transcendentals=0),
-        )(plan, in_hbm(packed), sent)
+        )(plan, in_hbm(packed), scale, current, previous)
         last = step == STEPS - 1
-        more = () if last else (own_blocks, out_blocks)
         out = pl.pallas_call(
             functools.partial(step_kernel, step),
             name="step",
-            out_shape=(sds((group, rows), F32), *more),
-            in_specs=[SMEM, SMEM, ANY] + [VMEM] * 5,
-            out_specs=(VMEM,) * (1 + len(more)),
-            scratch_shapes=scratch(tiles - near_count, nblk),
+            out_shape=[vectors_here] if last else [vectors_here, out_blocks],
+            in_specs=[SMEM, SMEM, ANY] + [VMEM] * 3,
+            out_specs=[VMEM] if last else [VMEM, VMEM],
+            scratch_shapes=([] if last else [sent_scratch]) + scratch(tiles - near_count, nblk),
             compiler_params=params(LIMIT),
-        )(plan, wanted, in_hbm(packed), scale, near, current, previous, arrived)
+        )(plan, wanted, in_hbm(packed), scale, base, arrived)
         previous, current = current, out[0]
         if not last:
-            sent, blocks = out[1:]
+            blocks = out[1]
 
     rounded = current.astype(BF16)
     if ncol == 4:
@@ -482,10 +488,10 @@
         compiler_params=params(LIMIT),
     )(current, *others)
     wide = 1
-    while 2 * wide < nblk:
+    while 4 * wide < nblk:
         part = part + to_partner(part, "blk", wide)
         wide *= 2
-    parts = [part, to_partner(part, "blk", wide)] if wide < nblk else [part]
+    parts = [part] + [to_partner(part, "blk", s * wide) for s in range(1, nblk // wide)]
     return pl.pallas_call(
         functools.partial(factor_kernel, len(parts), rows * nblk),
         name="factor",

time: 119 us -> 116 us (0.975); the launches traced: 118 us -> 116 us
  waiting for transfers between devices: 32.7 us -> 28.6 us
  starting transfers between devices: 27 us -> 29.4 us
    ppermute x6 -> x7, waiting for transfers between devices: 15.7 us -> 10.6 us  [to_partner(): return lax.ppermute(x, axis, [(i, i ^ mask) for i in range(n)])]
    ppermute x6 -> x7, starting transfers between devices: 3.41 us -> 6.02 us  [to_partner(): return lax.ppermute(x, axis, [(i, i ^ mask) for i in range(n)])]
    all_to_all x1 -> x0, local copies, waits for them, and re-layouts: 1.32 us -> none  [per_device(): lax.all_to_all(fetch_pick.reshape(nblk, 1), 'blk', split_axis=0, concat_a...]
    broadcast_in_dim x0 -> x1, local copies, waits for them, and re-layouts: none -> 1.25 us  [per_device(): jnp.broadcast_to(fetch_pick[None], (nblk, 1, nblk))]
  transfers between devices with their start and end apart: 11 -> 12, of which waited for: 9 -> 9; matrix products, arithmetic and copies ran while one was open for 0% -> 0% of each run, Pallas kernels for 22% -> 22%
where the time goes in v5:
time: 116 us
  Pallas kernels  57.1 us (49%)
  starting transfers between devices  29.4 us (25%)
  waiting for transfers between devices  28.6 us (25%)
  local copies, waits for them, and re-layouts  1.25 us (1%)
    pallas_call x4, Pallas kernels, per_device(): pl.pallas_call(functools.partial(step_kernel, step), name='step', out_sha...  22.3 us
    all_to_all x4, waiting for transfers between devices, per_device(): lax.all_to_all(blocks, 'blk', split_axis=0, concat_axis=0, tiled=True)  18 us
    all_to_all x4, starting transfers between devices, per_device(): lax.all_to_all(blocks, 'blk', split_axis=0, concat_axis=0, tiled=True)  16.1 us
    pallas_call x1, Pallas kernels, tiles_call(): pl.pallas_call(functools.partial(tiles_kernel, near_count), name='tiles',...  14.3 us
    pallas_call x4, Pallas kernels, per_device(): pl.pallas_call(functools.partial(near_kernel, step), name='near', out_sha...  11.2 us
    ppermute x7, waiting for transfers between devices, to_partner(): return lax.ppermute(x, axis, [(i, i ^ mask) for i in range(n)])  10.6 us
    pallas_call x1, Pallas kernels, per_device(): pl.pallas_call(functools.partial(factor_kernel, len(parts), rows * nblk),...  7.63 us
    all_to_all x1, starting transfers between devices, per_device(): lax.all_to_all(jnp.broadcast_to(fetch_pick[None], (nblk, 1, nblk)), 'blk'...  7.28 us
  transfers between devices with their start and end apart: 12, of which 9 were waited for; matrix products, arithmetic and copies ran while one was open for 0% of the time, Pallas kernels for 22%

profile of v5, /device:TPU:0, one launch (start us, length us, event | category | flops | bytes accessed | tf_op | source)
XLA Modules:
  0.0 116.5 jit_solution(13504953902083570529)
XLA Ops:
  1.2 7.3 %all-to-all-start = ((s32[8,1,8]{2,1,0:T(1,128)}), s32[8,1,8]{2,1,0:T(1,128)S(1)}, u32[]{:S(2)}, u32[]{:S(2)}) async-start(s32[8,1,8]{2,1,0:T(1,128)} %broadcast_in_dim.9), calls=%async_computation | async-start | bytes 8192 | tf_op jit(solution)/shard_map/all_to_all | solution.py:421
  8.5 14.3 %tiles.1 = (f8e4m3fn[96,256,512]{2,1,0:T(32,128)(4,1)}, f32[8,2048]{1,0:T(8,128)S(1)}, s32[128]{0:T(128)S(1)}) custom-call(s32[96]{0:T(128)} %rows_ref.1, s32[96]{0:T(128)} %slots_ref.1, bf16[96,256,256]{2,1,0:T(8,128)(2,1)} %real_hbm.1, bf16[96,256,256]{2,1,0:T(8,128)(2,1)} %imag_hbm.1), custom_call_target="tpu_custom_call" | custom-call | flops 268435456 | bytes 25165824 | tf_op jit(solution)/shard_map/tiles/pallas_call | solution.py:187
  24.2 5.9 %all-to-all-start.1 = ((bf16[8,32,256]{2,1,0:T(8,128)(2,1)}), bf16[8,32,256]{2,1,0:T(8,128)(2,1)S(1)}, u32[]{:S(2)}, u32[]{:S(2)}) async-start(bf16[8,32,256]{2,1,0:T(8,128)(2,1)} %first.1), calls=%async_computation.1 | async-start | bytes 262144 | tf_op jit(solution)/shard_map/all_to_all | solution.py:449
  30.1 2.8 %near.4.base_ref = f32[32,2048]{1,0:T(8,128)S(1)} custom-call(s32[128]{0:T(128)S(1)} %get-tuple-element.14.plan_ref, f8e4m3fn[96,256,512]{2,1,0:T(32,128)(4,1)} %get-tuple-element.15.packed_hbm, f32[8,2048]{1,0:T(8,128)S(1)} %get-tuple-element.16.scale_ref, f32[32,2048]{1,0:T(8,128)S(1)} %copy-done, f32[32,2048]{1,0:T(8,128)S(1)} %copy-done), custom_call_target="tpu_custom_call" | custom-call | flops 268435456 | bytes 2097152 | tf_op jit(solution)/shard_map/near/pallas_call | solution.py:450
  32.8 4.6 %all-to-all-done.1.arrived_ref = bf16[8,32,256]{2,1,0:T(8,128)(2,1)S(1)} async-done(((bf16[8,32,256]{2,1,0:T(8,128)(2,1)}), bf16[8,32,256]{2,1,0:T(8,128)(2,1)S(1)}, u32[]{:S(2)}, u32[]{:S(2)}) %all-to-all-start.1) | async-done | bytes 131104 | tf_op jit(solution)/shard_map/all_to_all | solution.py:449
  37.4 5.7 %step.4 = (f32[32,2048]{1,0:T(8,128)S(1)}, bf16[8,32,256]{2,1,0:T(8,128)(2,1)}) custom-call(s32[128]{0:T(128)S(1)} %get-tuple-element.14.plan_ref, s32[8,1,8]{2,1,0:T(1,128)S(1)} %all-to-all-done.wanted_ref, f8e4m3fn[96,256,512]{2,1,0:T(32,128)(4,1)} %get-tuple-element.15.packed_hbm, f32[8,2048]{1,0:T(8,128)S(1)} %get-tuple-element.16.scale_ref, ...), custom_call_target="tpu_custom_call" | custom-call | tf_op jit(solution)/shard_map/step/pallas_call | solution.py:461
  43.1 3.4 %all-to-all-start.2 = ((bf16[8,32,256]{2,1,0:T(8,128)(2,1)}), bf16[8,32,256]{2,1,0:T(8,128)(2,1)S(1)}, u32[]{:S(2)}, u32[]{:S(2)}) async-start(bf16[8,32,256]{2,1,0:T(8,128)(2,1)} %get-tuple-element.18), calls=%async_computation.2 | async-start | bytes 262144 | tf_op jit(solution)/shard_map/all_to_all | solution.py:449
  46.5 2.8 %near.5.base_ref = f32[32,2048]{1,0:T(8,128)S(1)} custom-call(s32[128]{0:T(128)S(1)} %get-tuple-element.14.plan_ref, f8e4m3fn[96,256,512]{2,1,0:T(32,128)(4,1)} %get-tuple-element.15.packed_hbm, f32[8,2048]{1,0:T(8,128)S(1)} %get-tuple-element.16.scale_ref, f32[32,2048]{1,0:T(8,128)S(1)} %get-tuple-element.17.now_ref.before_ref, f32[32,2048]{1,0:T(8,128)S(1)} %copy-done), custom_call_target="tpu_custom_call" | custom-call | flops 268435456 | bytes 2097152 | tf_op jit(solution)/shard_map/near/pallas_call | solution.py:450
  49.3 4.5 %all-to-all-done.2.arrived_ref = bf16[8,32,256]{2,1,0:T(8,128)(2,1)S(1)} async-done(((bf16[8,32,256]{2,1,0:T(8,128)(2,1)}), bf16[8,32,256]{2,1,0:T(8,128)(2,1)S(1)}, u32[]{:S(2)}, u32[]{:S(2)}) %all-to-all-start.2) | async-done | bytes 131104 | tf_op jit(solution)/shard_map/all_to_all | solution.py:449
  53.8 5.7 %step.5 = (f32[32,2048]{1,0:T(8,128)S(1)}, bf16[8,32,256]{2,1,0:T(8,128)(2,1)}) custom-call(s32[128]{0:T(128)S(1)} %get-tuple-element.14.plan_ref, s32[8,1,8]{2,1,0:T(1,128)S(1)} %all-to-all-done.wanted_ref, f8e4m3fn[96,256,512]{2,1,0:T(32,128)(4,1)} %get-tuple-element.15.packed_hbm, f32[8,2048]{1,0:T(8,128)S(1)} %get-tuple-element.16.scale_ref, ...), custom_call_target="tpu_custom_call" | custom-call | tf_op jit(solution)/shard_map/step/pallas_call | solution.py:461
  59.6 3.4 %all-to-all-start.3 = ((bf16[8,32,256]{2,1,0:T(8,128)(2,1)}), bf16[8,32,256]{2,1,0:T(8,128)(2,1)S(1)}, u32[]{:S(2)}, u32[]{:S(2)}) async-start(bf16[8,32,256]{2,1,0:T(8,128)(2,1)} %get-tuple-element.20), calls=%async_computation.3 | async-start | bytes 262144 | tf_op jit(solution)/shard_map/all_to_all | solution.py:449
  63.0 2.8 %near.6.base_ref = f32[32,2048]{1,0:T(8,128)S(1)} custom-call(s32[128]{0:T(128)S(1)} %get-tuple-element.14.plan_ref, f8e4m3fn[96,256,512]{2,1,0:T(32,128)(4,1)} %get-tuple-element.15.packed_hbm, f32[8,2048]{1,0:T(8,128)S(1)} %get-tuple-element.16.scale_ref, f32[32,2048]{1,0:T(8,128)S(1)} %get-tuple-element.19.now_ref.before_ref, ...), custom_call_target="tpu_custom_call" | custom-call | flops 268435456 | bytes 2097152 | tf_op jit(solution)/shard_map/near/pallas_call | solution.py:450
  65.8 4.5 %all-to-all-done.3.arrived_ref = bf16[8,32,256]{2,1,0:T(8,128)(2,1)S(1)} async-done(((bf16[8,32,256]{2,1,0:T(8,128)(2,1)}), bf16[8,32,256]{2,1,0:T(8,128)(2,1)S(1)}, u32[]{:S(2)}, u32[]{:S(2)}) %all-to-all-start.3) | async-done | bytes 131104 | tf_op jit(solution)/shard_map/all_to_all | solution.py:449
  70.2 5.7 %step.6 = (f32[32,2048]{1,0:T(8,128)S(1)}, bf16[8,32,256]{2,1,0:T(8,128)(2,1)}) custom-call(s32[128]{0:T(128)S(1)} %get-tuple-element.14.plan_ref, s32[8,1,8]{2,1,0:T(1,128)S(1)} %all-to-all-done.wanted_ref, f8e4m3fn[96,256,512]{2,1,0:T(32,128)(4,1)} %get-tuple-element.15.packed_hbm, f32[8,2048]{1,0:T(8,128)S(1)} %get-tuple-element.16.scale_ref, ...), custom_call_target="tpu_custom_call" | custom-call | tf_op jit(solution)/shard_map/step/pallas_call | solution.py:461
  76.0 3.4 %all-to-all-start.4 = ((bf16[8,32,256]{2,1,0:T(8,128)(2,1)}), bf16[8,32,256]{2,1,0:T(8,128)(2,1)S(1)}, u32[]{:S(2)}, u32[]{:S(2)}) async-start(bf16[8,32,256]{2,1,0:T(8,128)(2,1)} %get-tuple-element.22), calls=%async_computation.4 | async-start | bytes 262144 | tf_op jit(solution)/shard_map/all_to_all | solution.py:449
  79.4 2.8 %near.7.base_ref = f32[32,2048]{1,0:T(8,128)S(1)} custom-call(s32[128]{0:T(128)S(1)} %get-tuple-element.14.plan_ref, f8e4m3fn[96,256,512]{2,1,0:T(32,128)(4,1)} %get-tuple-element.15.packed_hbm, f32[8,2048]{1,0:T(8,128)S(1)} %get-tuple-element.16.scale_ref, f32[32,2048]{1,0:T(8,128)S(1)} %get-tuple-element.21.now_ref, ...), custom_call_target="tpu_custom_call" | custom-call | flops 268435456 | bytes 2097152 | tf_op jit(solution)/shard_map/near/pallas_call | solution.py:450
  82.2 4.5 %all-to-all-done.4.arrived_ref = bf16[8,32,256]{2,1,0:T(8,128)(2,1)S(1)} async-done(((bf16[8,32,256]{2,1,0:T(8,128)(2,1)}), bf16[8,32,256]{2,1,0:T(8,128)(2,1)S(1)}, u32[]{:S(2)}, u32[]{:S(2)}) %all-to-all-start.4) | async-done | bytes 131104 | tf_op jit(solution)/shard_map/all_to_all | solution.py:449
  86.7 5.1 %step.7.own_ref = f32[32,2048]{1,0:T(8,128)S(1)} custom-call(s32[128]{0:T(128)S(1)} %get-tuple-element.14.plan_ref, s32[8,1,8]{2,1,0:T(1,128)S(1)} %all-to-all-done.wanted_ref, f8e4m3fn[96,256,512]{2,1,0:T(32,128)(4,1)} %get-tuple-element.15.packed_hbm, f32[8,2048]{1,0:T(8,128)S(1)} %get-tuple-element.16.scale_ref, f32[32,2048]{1,0:T(8,128)S(1)} %near.7.base_ref, ...), custom_call_target="tpu_custom_call" | custom-call | tf_op jit(solution)/shard_map/step/pallas_call | solution.py:461
  91.8 1.6 %collective-permute-start.1 = (bf16[32,2048]{1,0:T(8,128)(2,1)S(1)}, bf16[32,2048]{1,0:T(8,128)(2,1)S(1)}, u32[]{:S(2)}, u32[]{:S(2)}) collective-permute-start(bf16[32,2048]{1,0:T(8,128)(2,1)S(1)} %convert_element_type.3), channel_id=1, source_target_pairs={{0,2},{1,3},{2,0},{3,1},{4,6},{5,7},{6,4},{7,5},{8,10},{9,11},{10,... | collective-permute-start | bytes 393224 | tf_op jit(solution)/shard_map/ppermute | solution.py:411
  93.3 3.5 %collective-permute-done.1.refs_1_.refs_5_ = bf16[32,2048]{1,0:T(8,128)(2,1)S(1)} collective-permute-done((bf16[32,2048]{1,0:T(8,128)(2,1)S(1)}, bf16[32,2048]{1,0:T(8,128)(2,1)S(1)}, u32[]{:S(2)}, u32[]{:S(2)}) %collective-permute-start.1) | collective-permute-done | bytes 131104 | tf_op jit(solution)/shard_map/ppermute | solution.py:411
  96.8 1.3 %collective-permute-done.2.refs_2_.refs_6_ = bf16[32,2048]{1,0:T(8,128)(2,1)S(1)} collective-permute-done((bf16[32,2048]{1,0:T(8,128)(2,1)S(1)}, bf16[32,2048]{1,0:T(8,128)(2,1)S(1)}, u32[]{:S(2)}, u32[]{:S(2)}) %collective-permute-start.2) | collective-permute-done | bytes 131104 | tf_op jit(solution)/shard_map/ppermute | solution.py:411
  98.6 3.9 %collective-permute-done.3 = f32[64,128]{1,0:T(8,128)S(1)} collective-permute-done((f32[64,128]{1,0:T(8,128)S(1)}, f32[64,128]{1,0:T(8,128)S(1)}, u32[]{:S(2)}, u32[]{:S(2)}) %collective-permute-start.3) | collective-permute-done | bytes 32800 | tf_op jit(solution)/shard_map/ppermute | solution.py:411
  103.9 3.1 %collective-permute-start.4 = (f32[64,128]{1,0:T(8,128)S(1)}, f32[64,128]{1,0:T(8,128)S(1)}, u32[]{:S(2)}, u32[]{:S(2)}) collective-permute-start(f32[64,128]{1,0:T(8,128)S(1)} %add.3.refs_0_), channel_id=1, source_target_pairs={{0,8},{4,12},{8,0},{12,4},{16,24},{20,28},{24,16},{28,20},{1,9},{5... | collective-permute-start | bytes 98312 | tf_op jit(solution)/shard_map/ppermute | solution.py:411
  108.8 7.6 %factor.1 = f32[32,2048]{1,0:T(8,128)} custom-call(f32[32,2048]{1,0:T(8,128)S(1)} %step.7.own_ref, f32[64,128]{1,0:T(8,128)S(1)} %add.3.refs_0_, f32[64,128]{1,0:T(8,128)S(1)} %collective-permute-done.4.refs_1_, f32[64,128]{1,0:T(8,128)S(1)} %collective-permute-done.5.refs_2_, f32[64,128]{1,0:T(8,128)S(1)} %collective-permute-done.6.refs_3_, ...), custom_call_target="tpu_custom_call" | custom-call | tf_op jit(solution)/shard_map/factor/pallas_call | solution.py:495
  (17 shorter events, 6.3 us)
Async XLA Ops:
  1.2 21.6 %all-to-all-start = ((s32[8,1,8]{2,1,0:T(1,128)}), s32[8,1,8]{2,1,0:T(1,128)S(1)}, u32[]{:S(2)}, u32[]{:S(2)}) async-start(s32[8,1,8]{2,1,0:T(1,128)} %broadcast_in_dim.9), calls=%async_computation | async-start | bytes 8192 | tf_op jit(solution)/shard_map/all_to_all | solution.py:421
  8.5 14.3 %copy-start = (f32[32,2048]{1,0:T(8,128)S(1)}, f32[32,2048]{1,0:T(8,128)}, u32[]{:S(2)}) copy-start(f32[32,2048]{1,0:T(8,128)} %before_ref.3) | copy-start | bytes 786436
  24.2 13.2 %all-to-all-start.1 = ((bf16[8,32,256]{2,1,0:T(8,128)(2,1)}), bf16[8,32,256]{2,1,0:T(8,128)(2,1)S(1)}, u32[]{:S(2)}, u32[]{:S(2)}) async-start(bf16[8,32,256]{2,1,0:T(8,128)(2,1)} %first.1), calls=%async_computation.1 | async-start | bytes 262144 | tf_op jit(solution)/shard_map/all_to_all | solution.py:449
  43.1 10.7 %all-to-all-start.2 = ((bf16[8,32,256]{2,1,0:T(8,128)(2,1)}), bf16[8,32,256]{2,1,0:T(8,128)(2,1)S(1)}, u32[]{:S(2)}, u32[]{:S(2)}) async-start(bf16[8,32,256]{2,1,0:T(8,128)(2,1)} %get-tuple-element.18), calls=%async_computation.2 | async-start | bytes 262144 | tf_op jit(solution)/shard_map/all_to_all | solution.py:449
  59.6 10.7 %all-to-all-start.3 = ((bf16[8,32,256]{2,1,0:T(8,128)(2,1)}), bf16[8,32,256]{2,1,0:T(8,128)(2,1)S(1)}, u32[]{:S(2)}, u32[]{:S(2)}) async-start(bf16[8,32,256]{2,1,0:T(8,128)(2,1)} %get-tuple-element.20), calls=%async_computation.3 | async-start | bytes 262144 | tf_op jit(solution)/shard_map/all_to_all | solution.py:449
  76.0 10.7 %all-to-all-start.4 = ((bf16[8,32,256]{2,1,0:T(8,128)(2,1)}), bf16[8,32,256]{2,1,0:T(8,128)(2,1)S(1)}, u32[]{:S(2)}, u32[]{:S(2)}) async-start(bf16[8,32,256]{2,1,0:T(8,128)(2,1)} %get-tuple-element.22), calls=%async_computation.4 | async-start | bytes 262144 | tf_op jit(solution)/shard_map/all_to_all | solution.py:449
  91.8 5.0 %collective-permute-start.1 = (bf16[32,2048]{1,0:T(8,128)(2,1)S(1)}, bf16[32,2048]{1,0:T(8,128)(2,1)S(1)}, u32[]{:S(2)}, u32[]{:S(2)}) collective-permute-start(bf16[32,2048]{1,0:T(8,128)(2,1)S(1)} %convert_element_type.3), channel_id=1, source_target_pairs={{0,2},{1,3},{2,0},{3,1},{4,6},{5,7},{6,4},{7,5},{8,10},{9,11},{10,... | collective-permute-start | bytes 393224 | tf_op jit(solution)/shard_map/ppermute | solution.py:411
  93.3 3.5 %collective-permute-start = (bf16[32,2048]{1,0:T(8,128)(2,1)S(1)}, bf16[32,2048]{1,0:T(8,128)(2,1)S(1)}, u32[]{:S(2)}, u32[]{:S(2)}) collective-permute-start(bf16[32,2048]{1,0:T(8,128)(2,1)S(1)} %convert_element_type.3), channel_id=1, source_target_pairs={{0,1},{1,0},{2,3},{3,2},{4,5},{5,4},{6,7},{7,6},{8,9},{9,8},{10,11... | collective-permute-start | bytes 393224 | tf_op jit(solution)/shard_map/ppermute | solution.py:411
  96.8 1.3 %collective-permute-start.2 = (bf16[32,2048]{1,0:T(8,128)(2,1)S(1)}, bf16[32,2048]{1,0:T(8,128)(2,1)S(1)}, u32[]{:S(2)}, u32[]{:S(2)}) collective-permute-start(bf16[32,2048]{1,0:T(8,128)(2,1)S(1)} %collective-permute-done.1.refs_1_.refs_5_), channel_id=1, source_target_pairs={{0,1},{1,0},{2,3},{3,2},{4,5},{5,4},{6,7},{7,6},{8,9},{9,8},{10,11... | collective-permute-start | bytes 393224 | tf_op jit(solution)/shard_map/ppermute | solution.py:411
  98.6 4.0 %collective-permute-start.3 = (f32[64,128]{1,0:T(8,128)S(1)}, f32[64,128]{1,0:T(8,128)S(1)}, u32[]{:S(2)}, u32[]{:S(2)}) collective-permute-start(f32[64,128]{1,0:T(8,128)S(1)} %gram.1), channel_id=1, source_target_pairs={{0,4},{4,0},{8,12},{12,8},{16,20},{20,16},{24,28},{28,24},{1,5},{5... | collective-permute-start | bytes 98312 | tf_op jit(solution)/shard_map/ppermute | solution.py:411
  102.5 5.7 %collective-permute-start.6 = (f32[64,128]{1,0:T(8,128)S(1)}, f32[64,128]{1,0:T(8,128)S(1)}, u32[]{:S(2)}, u32[]{:S(2)}) collective-permute-start(f32[64,128]{1,0:T(8,128)S(1)} %add.3.refs_0_), channel_id=1, source_target_pairs={{0,24},{4,28},{8,16},{12,20},{16,8},{20,12},{24,0},{28,4},{1,25},{... | collective-permute-start | bytes 98312 | tf_op jit(solution)/shard_map/ppermute | solution.py:411
  102.8 5.4 %collective-permute-start.5 = (f32[64,128]{1,0:T(8,128)S(1)}, f32[64,128]{1,0:T(8,128)S(1)}, u32[]{:S(2)}, u32[]{:S(2)}) collective-permute-start(f32[64,128]{1,0:T(8,128)S(1)} %add.3.refs_0_), channel_id=1, source_target_pairs={{0,16},{4,20},{8,24},{12,28},{16,0},{20,4},{24,8},{28,12},{1,17},{... | collective-permute-start | bytes 98312 | tf_op jit(solution)/shard_map/ppermute | solution.py:411
  103.9 5.0 %collective-permute-start.4 = (f32[64,128]{1,0:T(8,128)S(1)}, f32[64,128]{1,0:T(8,128)S(1)}, u32[]{:S(2)}, u32[]{:S(2)}) collective-permute-start(f32[64,128]{1,0:T(8,128)S(1)} %add.3.refs_0_), channel_id=1, source_target_pairs={{0,8},{4,12},{8,0},{12,4},{16,24},{20,28},{24,16},{28,20},{1,9},{5... | collective-permute-start | bytes 98312 | tf_op jit(solution)/shard_map/ppermute | solution.py:411

commit v6 on v5

--- a/solution.py
+++ b/solution.py
@@ -11,6 +11,7 @@
 LOC_RB = 2
 STEPS = 4
 UNROLL = 4
+KEPT = 16
 CHUNK = 4
 MERGE = 16
 TOP = 7.0
@@ -67,6 +68,7 @@
     real_hbm,
     imag_hbm,
     packed_hbm,
+    kept_ref,
     scale_ref,
     plan_ref,
     both_ref,
@@ -78,6 +80,7 @@
     in_sems,
     out_sems,
 ):
+    kept = kept_ref.shape[0]
     tiles, order, _ = both_ref.shape
     rb_dev = present_ref.shape[0]
     slots = rb_dev + lax.axis_size("blk")
@@ -122,7 +125,17 @@
 
     lax.fori_loop(0, tiles, link, 0)
 
-    def one(t, listed):
+    def put(e, skip, value):
+        @pl.when(e < skip)
+        def _():
+            kept_ref[e - skip + kept] = value()
+
+        @pl.when(e >= skip)
+        def _():
+            small_ref[e] = value()
+            leave(e).start()
+
+    def one(skip, t, listed):
         row = rows_ref[t]
         both = both_ref[t]
         present_ref[row] = present_ref[row] + (both[:, :order] + jnp.abs(both[:, order:]))
@@ -135,33 +148,32 @@
                 return back_ref[prior]
 
             lax.while_loop(lambda prior: prior >= 0, add, back_ref[t])
-            small_ref[listed] = both_ref[t].astype(F32).astype(F8)
-            leave(listed).start()
+            put(listed, skip, lambda: both_ref[t].astype(F8))
             plan_ref[listed] = row | (slots_ref[t] << 8)
 
         return listed + closes
 
-    def chunk(c, listed):
+    def chunk(skip, c, listed):
         for copy in copies(c):
             copy.wait()
         for j in range(CHUNK):
-            listed = one(c * CHUNK + j, listed)
+            listed = one(skip, c * CHUNK + j, listed)
         return listed
 
-    def pad(listed):
+    def pad(skip, listed):
         short = (UNROLL - listed % UNROLL) % UNROLL
         for j in range(UNROLL - 1):
 
             @pl.when(j < short)
             def _():
-                small_ref[listed + j] = jnp.zeros(small_ref.shape[1:], F8)
-                leave(listed + j).start()
+                put(listed + j, skip, lambda: jnp.zeros(small_ref.shape[1:], F8))
                 plan_ref[listed + j] = slots << 8
 
         return listed + short
 
-    near = pad(lax.fori_loop(0, near_count // CHUNK, chunk, 0))
-    every = pad(lax.fori_loop(near_count // CHUNK, chunks, chunk, near))
+    near = pad(0, lax.fori_loop(0, near_count // CHUNK, functools.partial(chunk, 0), 0))
+    skip = near + kept
+    every = pad(skip, lax.fori_loop(near_count // CHUNK, chunks, functools.partial(chunk, skip), near))
     plan_ref[tiles] = near // UNROLL
     plan_ref[tiles + 1] = every // UNROLL
 
@@ -174,7 +186,8 @@
         leave(e).wait()
         return _
 
-    lax.fori_loop(0, every, left, 0)
+    lax.fori_loop(0, near, left, 0)
+    lax.fori_loop(skip, every, left, 0)
 
 
 def in_hbm(x):
@@ -189,11 +202,12 @@
         name="tiles",
         out_shape=(
             pltpu.HBM((tiles, order, 2 * order), F8),
+            pltpu.VMEM((KEPT, order, 2 * order), F8),
             sds((8, rb_dev * order), F32),
             sds((tiles + 32,), I32),
         ),
         in_specs=[SMEM, SMEM, ANY, ANY],
-        out_specs=(ANY, VMEM, SMEM),
+        out_specs=(ANY, VMEM, VMEM, SMEM),
         scratch_shapes=[
             pltpu.VMEM((tiles, order, 2 * order), BF16),
             pltpu.VMEM((tiles, order, 2 * order), F8),
@@ -214,17 +228,16 @@
     return (field[:, at] * scale_ref[0:1, at]).astype(BF16)
 
 
-def send_blocks(field, scale_ref, wanted_ref, out_ref, sent_ref):
-    order = sent_ref.shape[2]
+def send_picked(wanted_ref, sent_ref, out_ref):
     me = lax.axis_index("blk")
-    for r in range(sent_ref.shape[0]):
-        sent_ref[r] = rounded_block(field, scale_ref, r, order)
     for p in range(out_ref.shape[0]):
         out_ref[p] = sent_ref[wanted_ref[p, 0, me]]
 
 
 def first_kernel(y_ref, scale_ref, wanted_ref, out_ref, sent_ref):
-    send_blocks(y_ref, scale_ref, wanted_ref, out_ref, sent_ref)
+    for r in range(sent_ref.shape[0]):
+        sent_ref[r] = rounded_block(y_ref, scale_ref, r, sent_ref.shape[2])
+    send_picked(wanted_ref, sent_ref, out_ref)
 
 
 def load_groups(packed_hbm, tiles_ref, sems, lo, hi):
@@ -266,20 +279,27 @@
     return size[:, 0:1]
 
 
-def multiply(plan_ref, lo, hi, copy, tiles_ref, load, acc_ref):
+def multiply(plan_ref, lo, hi, tile, load, acc_ref):
     def group(g, _):
-        copy(g).wait()
         done = []
         for j in range(UNROLL):
             code = plan_ref[g * UNROLL + j]
-            tile = tiles_ref[(g - lo) * UNROLL + j]
-            product = lax.dot_general(load(code >> 8), tile, NT, preferred_element_type=F32)
+            product = lax.dot_general(load(code >> 8), tile(g, j), NT, preferred_element_type=F32)
             done.append((code & 255, product))
         for row, product in done:
             acc_ref[row] = acc_ref[row] + product
         return _
 
     lax.fori_loop(lo, hi, group, 0)
+
+
+def loaded(copy, tiles_ref, lo):
+    def tile(g, j):
+        if j == 0:
+            copy(g).wait()
+        return tiles_ref[(g - lo) * UNROLL + j]
+
+    return tile
 
 
 def collect(acc, size):
@@ -294,7 +314,7 @@
     copy = load_groups(packed_hbm, tiles_ref, sems, 0, hi)
     acc_ref[...] = jnp.zeros_like(acc_ref)
     size = split_sources(rb_dev, lambda r: rounded_block(now_ref, scale_ref, r, order), x_ref)
-    multiply(plan_ref, 0, hi, copy, tiles_ref, lambda c: x_ref[jnp.minimum(c, rb_dev)], acc_ref)
+    multiply(plan_ref, 0, hi, loaded(copy, tiles_ref, 0), lambda c: x_ref[jnp.minimum(c, rb_dev)], acc_ref)
     for r in range(rb_dev):
         at = slice(r * order, (r + 1) * order)
         applied = scale_ref[0:1, at] * collect(acc_ref[r], size)
@@ -302,23 +322,31 @@
         base_ref[:, at] = moved if step == 0 else 2.0 * moved - before_ref[:, at]
 
 
-def step_kernel(step, plan_ref, wanted_ref, packed_hbm, scale_ref, base_ref, arrived_ref, *refs):
+def step_kernel(step, plan_ref, wanted_ref, packed_hbm, kept_ref, scale_ref, base_ref, arrived_ref, *refs):
     last = step == STEPS - 1
     next_ref = refs[0]
     tiles_ref, x_ref, acc_ref, sems = refs[-4:]
     rb_dev, _, order = acc_ref.shape
     end = plan_ref.shape[0] - 32
     lo, hi = plan_ref[end], plan_ref[end + 1]
-    copy = load_groups(packed_hbm, tiles_ref, sems, lo, hi)
+    stay = jnp.minimum(lo + KEPT // UNROLL, hi)
+    copy = load_groups(packed_hbm, tiles_ref, sems, stay, hi)
     acc_ref[...] = jnp.zeros_like(acc_ref)
     size = split_sources(arrived_ref.shape[0], lambda p: arrived_ref[p], x_ref)
     size = size * ((1.0 if step == 0 else 2.0) / half_width)
-    multiply(plan_ref, lo, hi, copy, tiles_ref, lambda c: x_ref[c - rb_dev], acc_ref)
+    multiply(
+        plan_ref, lo, stay, lambda g, j: kept_ref[(g - lo) * UNROLL + j], lambda c: x_ref[c - rb_dev], acc_ref
+    )
+    multiply(plan_ref, stay, hi, loaded(copy, tiles_ref, stay), lambda c: x_ref[c - rb_dev], acc_ref)
     for r in range(rb_dev):
         at = slice(r * order, (r + 1) * order)
-        next_ref[:, at] = base_ref[:, at] - scale_ref[0:1, at] * collect(acc_ref[r], size)
+        scale = scale_ref[0:1, at]
+        following = base_ref[:, at] - scale * collect(acc_ref[r], size)
+        next_ref[:, at] = following
+        if not last:
+            refs[2][r] = (following * scale).astype(BF16)
     if not last:
-        send_blocks(next_ref, scale_ref, wanted_ref, refs[1], refs[2])
+        send_picked(wanted_ref, refs[2], refs[1])
 
 
 def all_rows(own_ref, arrived, all_ref):
@@ -363,17 +391,26 @@
         a = work_ref[top : top + PANEL, :]
         m = inverse_ref[top : top + PANEL, :]
         pivots = jnp.ones_like(a)
-        for k in range(0, PANEL, 2):
-            lane = top + k
-            left = jnp.broadcast_to(a[:, lane : lane + 1], a.shape)
-            right = jnp.broadcast_to(a[:, lane + 1 : lane + 2], a.shape)
-            pivot = left[k : k + 1, :]
-            inverse = 1.0 / pivot
-            left = jnp.where(here > k + 1, left, 0.0) * inverse
-            right = jnp.where(here > k + 1, right, 0.0) * inverse
-            pivots = jnp.where((here == k) | (here == k + 1), pivot, pivots)
+        for k in range(0, PANEL, 4):
+            w = [jnp.broadcast_to(a[:, i : i + 1], a.shape) for i in range(top + k, top + k + 4)]
+            p, q = w[0][k : k + 1, :], w[2][k + 2 : k + 3, :]
+            u, v = w[2][k : k + 1, :], w[3][k : k + 1, :]
+            single = 1.0 / p
+            det = p * q - (u * u + v * v)
+            both = 1.0 / det
+            second = (here == k + 2) | (here == k + 3)
+            below = here > k + 3
+            coefficients = (
+                jnp.where(second, w[0] * single, (w[0] * q - w[2] * u - w[3] * v) * both),
+                jnp.where(second, w[1] * single, (w[1] * q + w[2] * v - w[3] * u) * both),
+                jnp.where(below, (w[2] * p - w[0] * u + w[1] * v) * both, 0.0),
+                jnp.where(below, (w[3] * p - w[0] * v - w[1] * u) * both, 0.0),
+            )
+            coefficients = [jnp.where(here > k + 1, c, 0.0) for c in coefficients]
+            pivots = jnp.where((here == k) | (here == k + 1), p, pivots)
+            pivots = jnp.where(second, det * single, pivots)
             a, m = (
-                v - left * v[k : k + 1, :] - right * v[k + 1 : k + 2, :] for v in (a, m)
+                x - sum(c * x[k + i : k + i + 1, :] for i, c in enumerate(coefficients)) for x in (a, m)
             )
         root = lax.rsqrt(pivots)
         a, m = a * root, m * root
@@ -411,6 +448,24 @@
     return lax.ppermute(x, axis, [(i, i ^ mask) for i in range(n)])
 
 
+def sum_parts(part, nblk, ncol):
+    if nblk == 8 and ncol % 2 == 0:
+        places = [(b, c) for b in range(nblk) for c in range(ncol)]
+
+        def collect_from(masks):
+            pairs = [(b * ncol + c, (b ^ masks[c % 2]) * ncol + c) for b, c in places if masks[c % 2]]
+            return lax.ppermute(part, ("blk", "col"), pairs)
+
+        got = [collect_from(masks) for masks in ((1, 4), (2, 5), (3, 6), (0, 7))]
+        total = jnp.where(lax.axis_index("col") % 2 == 0, part, got[3]) + got[0] + got[1] + got[2]
+        return [total, to_partner(total, "col", 1)]
+    wide = 1
+    while 4 * wide < nblk:
+        part = part + to_partner(part, "blk", wide)
+        wide *= 2
+    return [part] + [to_partner(part, "blk", s * wide) for s in range(1, nblk // wide)]
+
+
 def per_device(y_start, tile_real, tile_imag, tile_rows, tile_slots, fetch_pick):
     group, rows = y_start.shape
     tiles, order, _ = tile_real.shape
@@ -421,7 +476,7 @@
     wanted = lax.all_to_all(
         jnp.broadcast_to(fetch_pick[None], (nblk, 1, nblk)), "blk", split_axis=0, concat_axis=0, tiled=True
     )
-    packed, scale, plan = tiles_call(tile_rows, tile_slots, tile_real, tile_imag, rb_dev, near_count)
+    packed, kept, scale, plan = tiles_call(tile_rows, tile_slots, tile_real, tile_imag, rb_dev, near_count)
 
     out_blocks = sds((nblk, group, order), BF16)
     sent_scratch = pltpu.VMEM((rb_dev, group, order), BF16)
@@ -462,11 +517,11 @@
             functools.partial(step_kernel, step),
             name="step",
             out_shape=[vectors_here] if last else [vectors_here, out_blocks],
-            in_specs=[SMEM, SMEM, ANY] + [VMEM] * 3,
+            in_specs=[SMEM, SMEM, ANY] + [VMEM] * 4,
             out_specs=[VMEM] if last else [VMEM, VMEM],
-            scratch_shapes=([] if last else [sent_scratch]) + scratch(tiles - near_count, nblk),
+            scratch_shapes=([] if last else [sent_scratch]) + scratch(tiles - near_count - KEPT, nblk),
             compiler_params=params(LIMIT),
-        )(plan, wanted, in_hbm(packed), scale, base, arrived)
+        )(plan, wanted, in_hbm(packed), pltpu.with_memory_space_constraint(kept, pltpu.VMEM), scale, base, arrived)
         previous, current = current, out[0]
         if not last:
             blocks = out[1]
@@ -487,11 +542,7 @@
         scratch_shapes=[pltpu.VMEM((ncol, group, rows), BF16), pltpu.VMEM((vectors, vectors), F32)],
         compiler_params=params(LIMIT),
     )(current, *others)
-    wide = 1
-    while 4 * wide < nblk:
-        part = part + to_partner(part, "blk", wide)
-        wide *= 2
-    parts = [part] + [to_partner(part, "blk", s * wide) for s in range(1, nblk // wide)]
+    parts = sum_parts(part, nblk, ncol)
     return pl.pallas_call(
         functools.partial(factor_kernel, len(parts), rows * nblk),
         name="factor",

time: 116 us -> 113 us (0.974); the launches traced: 116 us -> 112 us
  Pallas kernels: 57.1 us -> 51.3 us
  starting transfers between devices: 29.4 us -> 32.8 us
  waiting for transfers between devices: 28.6 us -> 26.2 us
    ppermute x7 -> x4, waiting for transfers between devices: 10.6 us -> 5.68 us  [to_partner(): return lax.ppermute(x, axis, [(i, i ^ mask) for i in range(n)])]
    ppermute x0 -> x4, starting transfers between devices: none -> 4.22 us  [collect_from(): return lax.ppermute(part, ('blk', 'col'), pairs)]
    pallas_call x4, Pallas kernels: 22.3 us -> 18.8 us  [per_device(): pl.pallas_call(functools.partial(step_kernel, step), name='step', out_sha...]
    ppermute x0 -> x4, waiting for transfers between devices: none -> 2.64 us  [collect_from(): return lax.ppermute(part, ('blk', 'col'), pairs)]
    pallas_call x1, Pallas kernels: 7.63 us -> 6.24 us  [per_device(): pl.pallas_call(functools.partial(factor_kernel, len(parts), rows * nblk),...]
    ppermute x7 -> x4, starting transfers between devices: 6.02 us -> 5.07 us  [to_partner(): return lax.ppermute(x, axis, [(i, i ^ mask) for i in range(n)])]
  transfers between devices with their start and end apart: 12 -> 13, of which waited for: 9 -> 10; matrix products, arithmetic and copies ran while one was open for 0% -> 0% of each run, Pallas kernels for 22% -> 22%
where the time goes in v6:
time: 113 us; the launch traced here: 112 us
  Pallas kernels  51.3 us (45%)
  starting transfers between devices  32.8 us (29%)
  waiting for transfers between devices  26.2 us (23%)
  local copies, waits for them, and re-layouts  1.25 us (1%)
    pallas_call x4, Pallas kernels, per_device(): pl.pallas_call(functools.partial(step_kernel, step), name='step', out_sha...  18.8 us
    all_to_all x4, waiting for transfers between devices, per_device(): lax.all_to_all(blocks, 'blk', split_axis=0, concat_axis=0, tiled=True)  17.9 us
    all_to_all x4, starting transfers between devices, per_device(): lax.all_to_all(blocks, 'blk', split_axis=0, concat_axis=0, tiled=True)  16.3 us
    pallas_call x1, Pallas kernels, tiles_call(): pl.pallas_call(functools.partial(tiles_kernel, near_count), name='tiles',...  13.4 us
    pallas_call x4, Pallas kernels, per_device(): pl.pallas_call(functools.partial(near_kernel, step), name='near', out_sha...  11.2 us
    all_to_all x1, starting transfers between devices, per_device(): lax.all_to_all(jnp.broadcast_to(fetch_pick[None], (nblk, 1, nblk)), 'blk'...  7.28 us
    pallas_call x1, Pallas kernels, per_device(): pl.pallas_call(functools.partial(factor_kernel, len(parts), rows * nblk),...  6.24 us
    ppermute x4, waiting for transfers between devices, to_partner(): return lax.ppermute(x, axis, [(i, i ^ mask) for i in range(n)])  5.68 us
  transfers between devices with their start and end apart: 13, of which 10 were waited for; matrix products, arithmetic and copies ran while one was open for 0% of the time, Pallas kernels for 22%

profile of v6, /device:TPU:0, one launch (start us, length us, event | category | flops | bytes accessed | tf_op | source)
XLA Modules:
  0.0 111.8 jit_solution(7895458131640878107)
XLA Ops:
  1.2 7.3 %all-to-all-start = ((s32[8,1,8]{2,1,0:T(1,128)}), s32[8,1,8]{2,1,0:T(1,128)S(1)}, u32[]{:S(2)}, u32[]{:S(2)}) async-start(s32[8,1,8]{2,1,0:T(1,128)} %broadcast_in_dim.9), calls=%async_computation | async-start | bytes 8192 | tf_op jit(solution)/shard_map/all_to_all | solution.py:476
  8.5 13.4 %tiles.1 = (f8e4m3fn[96,256,512]{2,1,0:T(32,128)(4,1)}, f8e4m3fn[16,256,512]{2,1,0:T(32,128)(4,1)S(1)}, f32[8,2048]{1,0:T(8,128)S(1)}, s32[128]{0:T(128)S(1)}) custom-call(s32[96]{0:T(128)} %rows_ref.1, s32[96]{0:T(128)} %slots_ref.1, bf16[96,256,256]{2,1,0:T(8,128)(2,1)} %real_hbm.1, bf16[96,256,256]{2,1,0:T(8,128)(2,1)} %imag_hbm.1), custom_call_target="tpu_custom_call" | custom-call | flops 268435456 | bytes 25165824 | tf_op jit(solution)/shard_map/tiles/pallas_call | solution.py:200
  23.2 6.1 %all-to-all-start.1 = ((bf16[8,32,256]{2,1,0:T(8,128)(2,1)}), bf16[8,32,256]{2,1,0:T(8,128)(2,1)S(1)}, u32[]{:S(2)}, u32[]{:S(2)}) async-start(bf16[8,32,256]{2,1,0:T(8,128)(2,1)} %first.1), calls=%async_computation.1 | async-start | bytes 262144 | tf_op jit(solution)/shard_map/all_to_all | solution.py:504
  29.3 2.8 %near.4.base_ref = f32[32,2048]{1,0:T(8,128)S(1)} custom-call(s32[128]{0:T(128)S(1)} %get-tuple-element.15.plan_ref, f8e4m3fn[96,256,512]{2,1,0:T(32,128)(4,1)} %get-tuple-element.16.packed_hbm, f32[8,2048]{1,0:T(8,128)S(1)} %get-tuple-element.18.scale_ref, f32[32,2048]{1,0:T(8,128)S(1)} %copy-done, f32[32,2048]{1,0:T(8,128)S(1)} %copy-done), custom_call_target="tpu_custom_call" | custom-call | flops 268435456 | bytes 2097152 | tf_op jit(solution)/shard_map/near/pallas_call | solution.py:505
  32.1 4.5 %all-to-all-done.1.arrived_ref = bf16[8,32,256]{2,1,0:T(8,128)(2,1)S(1)} async-done(((bf16[8,32,256]{2,1,0:T(8,128)(2,1)}), bf16[8,32,256]{2,1,0:T(8,128)(2,1)S(1)}, u32[]{:S(2)}, u32[]{:S(2)}) %all-to-all-start.1) | async-done | bytes 131104 | tf_op jit(solution)/shard_map/all_to_all | solution.py:504
  36.7 4.9 %step.4 = (f32[32,2048]{1,0:T(8,128)S(1)}, bf16[8,32,256]{2,1,0:T(8,128)(2,1)}) custom-call(s32[128]{0:T(128)S(1)} %get-tuple-element.15.plan_ref, s32[8,1,8]{2,1,0:T(1,128)S(1)} %all-to-all-done.wanted_ref, f8e4m3fn[96,256,512]{2,1,0:T(32,128)(4,1)} %get-tuple-element.16.packed_hbm, f8e4m3fn[16,256,512]{2,1,0:T(32,128)(4,1)S(1)} %get-tuple-element.17.kept_ref, ...), custom_call_target="tpu_custom_call" | custom-call | tf_op jit(solution)/shard_map/step/pallas_call | solution.py:516
  41.5 3.4 %all-to-all-start.2 = ((bf16[8,32,256]{2,1,0:T(8,128)(2,1)}), bf16[8,32,256]{2,1,0:T(8,128)(2,1)S(1)}, u32[]{:S(2)}, u32[]{:S(2)}) async-start(bf16[8,32,256]{2,1,0:T(8,128)(2,1)} %get-tuple-element.20), calls=%async_computation.2 | async-start | bytes 262144 | tf_op jit(solution)/shard_map/all_to_all | solution.py:504
  44.9 2.8 %near.5.base_ref = f32[32,2048]{1,0:T(8,128)S(1)} custom-call(s32[128]{0:T(128)S(1)} %get-tuple-element.15.plan_ref, f8e4m3fn[96,256,512]{2,1,0:T(32,128)(4,1)} %get-tuple-element.16.packed_hbm, f32[8,2048]{1,0:T(8,128)S(1)} %get-tuple-element.18.scale_ref, f32[32,2048]{1,0:T(8,128)S(1)} %get-tuple-element.19.now_ref.before_ref, f32[32,2048]{1,0:T(8,128)S(1)} %copy-done), custom_call_target="tpu_custom_call" | custom-call | flops 268435456 | bytes 2097152 | tf_op jit(solution)/shard_map/near/pallas_call | solution.py:505
  47.8 4.5 %all-to-all-done.2.arrived_ref = bf16[8,32,256]{2,1,0:T(8,128)(2,1)S(1)} async-done(((bf16[8,32,256]{2,1,0:T(8,128)(2,1)}), bf16[8,32,256]{2,1,0:T(8,128)(2,1)S(1)}, u32[]{:S(2)}, u32[]{:S(2)}) %all-to-all-start.2) | async-done | bytes 131104 | tf_op jit(solution)/shard_map/all_to_all | solution.py:504
  52.2 4.9 %step.5 = (f32[32,2048]{1,0:T(8,128)S(1)}, bf16[8,32,256]{2,1,0:T(8,128)(2,1)}) custom-call(s32[128]{0:T(128)S(1)} %get-tuple-element.15.plan_ref, s32[8,1,8]{2,1,0:T(1,128)S(1)} %all-to-all-done.wanted_ref, f8e4m3fn[96,256,512]{2,1,0:T(32,128)(4,1)} %get-tuple-element.16.packed_hbm, f8e4m3fn[16,256,512]{2,1,0:T(32,128)(4,1)S(1)} %get-tuple-element.17.kept_ref, ...), custom_call_target="tpu_custom_call" | custom-call | tf_op jit(solution)/shard_map/step/pallas_call | solution.py:516
  57.1 3.4 %all-to-all-start.3 = ((bf16[8,32,256]{2,1,0:T(8,128)(2,1)}), bf16[8,32,256]{2,1,0:T(8,128)(2,1)S(1)}, u32[]{:S(2)}, u32[]{:S(2)}) async-start(bf16[8,32,256]{2,1,0:T(8,128)(2,1)} %get-tuple-element.22), calls=%async_computation.3 | async-start | bytes 262144 | tf_op jit(solution)/shard_map/all_to_all | solution.py:504
  60.5 2.8 %near.6.base_ref = f32[32,2048]{1,0:T(8,128)S(1)} custom-call(s32[128]{0:T(128)S(1)} %get-tuple-element.15.plan_ref, f8e4m3fn[96,256,512]{2,1,0:T(32,128)(4,1)} %get-tuple-element.16.packed_hbm, f32[8,2048]{1,0:T(8,128)S(1)} %get-tuple-element.18.scale_ref, f32[32,2048]{1,0:T(8,128)S(1)} %get-tuple-element.21.now_ref.before_ref, ...), custom_call_target="tpu_custom_call" | custom-call | flops 268435456 | bytes 2097152 | tf_op jit(solution)/shard_map/near/pallas_call | solution.py:505
  63.3 4.5 %all-to-all-done.3.arrived_ref = bf16[8,32,256]{2,1,0:T(8,128)(2,1)S(1)} async-done(((bf16[8,32,256]{2,1,0:T(8,128)(2,1)}), bf16[8,32,256]{2,1,0:T(8,128)(2,1)S(1)}, u32[]{:S(2)}, u32[]{:S(2)}) %all-to-all-start.3) | async-done | bytes 131104 | tf_op jit(solution)/shard_map/all_to_all | solution.py:504
  67.8 4.9 %step.6 = (f32[32,2048]{1,0:T(8,128)S(1)}, bf16[8,32,256]{2,1,0:T(8,128)(2,1)}) custom-call(s32[128]{0:T(128)S(1)} %get-tuple-element.15.plan_ref, s32[8,1,8]{2,1,0:T(1,128)S(1)} %all-to-all-done.wanted_ref, f8e4m3fn[96,256,512]{2,1,0:T(32,128)(4,1)} %get-tuple-element.16.packed_hbm, f8e4m3fn[16,256,512]{2,1,0:T(32,128)(4,1)S(1)} %get-tuple-element.17.kept_ref, ...), custom_call_target="tpu_custom_call" | custom-call | tf_op jit(solution)/shard_map/step/pallas_call | solution.py:516
  72.6 3.4 %all-to-all-start.4 = ((bf16[8,32,256]{2,1,0:T(8,128)(2,1)}), bf16[8,32,256]{2,1,0:T(8,128)(2,1)S(1)}, u32[]{:S(2)}, u32[]{:S(2)}) async-start(bf16[8,32,256]{2,1,0:T(8,128)(2,1)} %get-tuple-element.24), calls=%async_computation.4 | async-start | bytes 262144 | tf_op jit(solution)/shard_map/all_to_all | solution.py:504
  76.0 2.8 %near.7.base_ref = f32[32,2048]{1,0:T(8,128)S(1)} custom-call(s32[128]{0:T(128)S(1)} %get-tuple-element.15.plan_ref, f8e4m3fn[96,256,512]{2,1,0:T(32,128)(4,1)} %get-tuple-element.16.packed_hbm, f32[8,2048]{1,0:T(8,128)S(1)} %get-tuple-element.18.scale_ref, f32[32,2048]{1,0:T(8,128)S(1)} %get-tuple-element.23.now_ref, ...), custom_call_target="tpu_custom_call" | custom-call | flops 268435456 | bytes 2097152 | tf_op jit(solution)/shard_map/near/pallas_call | solution.py:505
  78.8 4.5 %all-to-all-done.4.arrived_ref = bf16[8,32,256]{2,1,0:T(8,128)(2,1)S(1)} async-done(((bf16[8,32,256]{2,1,0:T(8,128)(2,1)}), bf16[8,32,256]{2,1,0:T(8,128)(2,1)S(1)}, u32[]{:S(2)}, u32[]{:S(2)}) %all-to-all-start.4) | async-done | bytes 131104 | tf_op jit(solution)/shard_map/all_to_all | solution.py:504
  83.3 4.2 %step.7.own_ref = f32[32,2048]{1,0:T(8,128)S(1)} custom-call(s32[128]{0:T(128)S(1)} %get-tuple-element.15.plan_ref, s32[8,1,8]{2,1,0:T(1,128)S(1)} %all-to-all-done.wanted_ref, f8e4m3fn[96,256,512]{2,1,0:T(32,128)(4,1)} %get-tuple-element.16.packed_hbm, f8e4m3fn[16,256,512]{2,1,0:T(32,128)(4,1)S(1)} %get-tuple-element.17.kept_ref, ...), custom_call_target="tpu_custom_call" | custom-call | tf_op jit(solution)/shard_map/step/pallas_call | solution.py:516
  87.5 1.6 %collective-permute-start.1 = (bf16[32,2048]{1,0:T(8,128)(2,1)S(1)}, bf16[32,2048]{1,0:T(8,128)(2,1)S(1)}, u32[]{:S(2)}, u32[]{:S(2)}) collective-permute-start(bf16[32,2048]{1,0:T(8,128)(2,1)S(1)} %convert_element_type.3), channel_id=1, source_target_pairs={{0,2},{1,3},{2,0},{3,1},{4,6},{5,7},{6,4},{7,5},{8,10},{9,11},{10,... | collective-permute-start | bytes 393224 | tf_op jit(solution)/shard_map/ppermute | solution.py:448
  89.1 3.5 %collective-permute-done.1.refs_1_.refs_3_ = bf16[32,2048]{1,0:T(8,128)(2,1)S(1)} collective-permute-done((bf16[32,2048]{1,0:T(8,128)(2,1)S(1)}, bf16[32,2048]{1,0:T(8,128)(2,1)S(1)}, u32[]{:S(2)}, u32[]{:S(2)}) %collective-permute-start.1) | collective-permute-done | bytes 131104 | tf_op jit(solution)/shard_map/ppermute | solution.py:448
  96.4 2.2 %collective-permute-start.6 = (f32[64,128]{1,0:T(8,128)S(1)}, f32[64,128]{1,0:T(8,128)S(1)}, u32[]{:S(2)}, u32[]{:S(2)}) collective-permute-start(f32[64,128]{1,0:T(8,128)S(1)} %gram.1), channel_id=1, source_target_pairs={{0,12},{1,25},{2,14},{3,27},{4,8},{5,29},{6,10},{7,31},{8,4},{9,17... | collective-permute-start | bytes 98312 | tf_op jit(solution)/shard_map/ppermute | solution.py:457
  99.5 1.7 %collective-permute-done.6 = f32[64,128]{1,0:T(8,128)S(1)} collective-permute-done((f32[64,128]{1,0:T(8,128)S(1)}, f32[64,128]{1,0:T(8,128)S(1)}, u32[]{:S(2)}, u32[]{:S(2)}) %collective-permute-start.6) | collective-permute-done | bytes 32800 | tf_op jit(solution)/shard_map/ppermute | solution.py:457
  101.2 3.5 %collective-permute-start.7 = (f32[64,128]{1,0:T(8,128)S(1)}, f32[64,128]{1,0:T(8,128)S(1)}, u32[]{:S(2)}, u32[]{:S(2)}) collective-permute-start(f32[64,128]{1,0:T(8,128)S(1)} %add_add_fusion.refs_0_), channel_id=1, source_target_pairs={{0,1},{1,0},{2,3},{3,2},{4,5},{5,4},{6,7},{7,6},{8,9},{9,8},{10,11... | collective-permute-start | bytes 98312 | tf_op jit(solution)/shard_map/ppermute | solution.py:448
  105.6 6.2 %factor.1 = f32[32,2048]{1,0:T(8,128)} custom-call(f32[32,2048]{1,0:T(8,128)S(1)} %step.7.own_ref, f32[64,128]{1,0:T(8,128)S(1)} %add_add_fusion.refs_0_, f32[64,128]{1,0:T(8,128)S(1)} %collective-permute-done.7.refs_1_, bf16[32,2048]{1,0:T(8,128)(2,1)S(1)} %collective-permute-done.refs_0_.refs_2_, ...), custom_call_target="tpu_custom_call" | custom-call | tf_op jit(solution)/shard_map/factor/pallas_call | solution.py:546
  (19 shorter events, 8.1 us)
Async XLA Ops:
  1.2 20.7 %all-to-all-start = ((s32[8,1,8]{2,1,0:T(1,128)}), s32[8,1,8]{2,1,0:T(1,128)S(1)}, u32[]{:S(2)}, u32[]{:S(2)}) async-start(s32[8,1,8]{2,1,0:T(1,128)} %broadcast_in_dim.9), calls=%async_computation | async-start | bytes 8192 | tf_op jit(solution)/shard_map/all_to_all | solution.py:476
  8.5 13.4 %copy-start = (f32[32,2048]{1,0:T(8,128)S(1)}, f32[32,2048]{1,0:T(8,128)}, u32[]{:S(2)}) copy-start(f32[32,2048]{1,0:T(8,128)} %before_ref.3) | copy-start | bytes 786436
  23.2 13.5 %all-to-all-start.1 = ((bf16[8,32,256]{2,1,0:T(8,128)(2,1)}), bf16[8,32,256]{2,1,0:T(8,128)(2,1)S(1)}, u32[]{:S(2)}, u32[]{:S(2)}) async-start(bf16[8,32,256]{2,1,0:T(8,128)(2,1)} %first.1), calls=%async_computation.1 | async-start | bytes 262144 | tf_op jit(solution)/shard_map/all_to_all | solution.py:504
  41.5 10.7 %all-to-all-start.2 = ((bf16[8,32,256]{2,1,0:T(8,128)(2,1)}), bf16[8,32,256]{2,1,0:T(8,128)(2,1)S(1)}, u32[]{:S(2)}, u32[]{:S(2)}) async-start(bf16[8,32,256]{2,1,0:T(8,128)(2,1)} %get-tuple-element.20), calls=%async_computation.2 | async-start | bytes 262144 | tf_op jit(solution)/shard_map/all_to_all | solution.py:504
  57.1 10.7 %all-to-all-start.3 = ((bf16[8,32,256]{2,1,0:T(8,128)(2,1)}), bf16[8,32,256]{2,1,0:T(8,128)(2,1)S(1)}, u32[]{:S(2)}, u32[]{:S(2)}) async-start(bf16[8,32,256]{2,1,0:T(8,128)(2,1)} %get-tuple-element.22), calls=%async_computation.3 | async-start | bytes 262144 | tf_op jit(solution)/shard_map/all_to_all | solution.py:504
  72.6 10.7 %all-to-all-start.4 = ((bf16[8,32,256]{2,1,0:T(8,128)(2,1)}), bf16[8,32,256]{2,1,0:T(8,128)(2,1)S(1)}, u32[]{:S(2)}, u32[]{:S(2)}) async-start(bf16[8,32,256]{2,1,0:T(8,128)(2,1)} %get-tuple-element.24), calls=%async_computation.4 | async-start | bytes 262144 | tf_op jit(solution)/shard_map/all_to_all | solution.py:504
  87.5 5.0 %collective-permute-start.1 = (bf16[32,2048]{1,0:T(8,128)(2,1)S(1)}, bf16[32,2048]{1,0:T(8,128)(2,1)S(1)}, u32[]{:S(2)}, u32[]{:S(2)}) collective-permute-start(bf16[32,2048]{1,0:T(8,128)(2,1)S(1)} %convert_element_type.3), channel_id=1, source_target_pairs={{0,2},{1,3},{2,0},{3,1},{4,6},{5,7},{6,4},{7,5},{8,10},{9,11},{10,... | collective-permute-start | bytes 393224 | tf_op jit(solution)/shard_map/ppermute | solution.py:448
  89.1 3.5 %collective-permute-start = (bf16[32,2048]{1,0:T(8,128)(2,1)S(1)}, bf16[32,2048]{1,0:T(8,128)(2,1)S(1)}, u32[]{:S(2)}, u32[]{:S(2)}) collective-permute-start(bf16[32,2048]{1,0:T(8,128)(2,1)S(1)} %convert_element_type.3), channel_id=1, source_target_pairs={{0,1},{1,0},{2,3},{3,2},{4,5},{5,4},{6,7},{7,6},{8,9},{9,8},{10,11... | collective-permute-start | bytes 393224 | tf_op jit(solution)/shard_map/ppermute | solution.py:448
  92.6 1.3 %collective-permute-start.2 = (bf16[32,2048]{1,0:T(8,128)(2,1)S(1)}, bf16[32,2048]{1,0:T(8,128)(2,1)S(1)}, u32[]{:S(2)}, u32[]{:S(2)}) collective-permute-start(bf16[32,2048]{1,0:T(8,128)(2,1)S(1)} %collective-permute-done.1.refs_1_.refs_3_), channel_id=1, source_target_pairs={{0,1},{1,0},{2,3},{3,2},{4,5},{5,4},{6,7},{7,6},{8,9},{9,8},{10,11... | collective-permute-start | bytes 393224 | tf_op jit(solution)/shard_map/ppermute | solution.py:448
  94.3 4.2 %collective-permute-start.3 = (f32[64,128]{1,0:T(8,128)S(1)}, f32[64,128]{1,0:T(8,128)S(1)}, u32[]{:S(2)}, u32[]{:S(2)}) collective-permute-start(f32[64,128]{1,0:T(8,128)S(1)} %gram.1), channel_id=1, source_target_pairs={{1,29},{3,31},{5,25},{7,27},{9,21},{11,23},{13,17},{15,19},{17,13}... | collective-permute-start | bytes 98312 | tf_op jit(solution)/shard_map/ppermute | solution.py:457
  95.0 4.0 %collective-permute-start.4 = (f32[64,128]{1,0:T(8,128)S(1)}, f32[64,128]{1,0:T(8,128)S(1)}, u32[]{:S(2)}, u32[]{:S(2)}) collective-permute-start(f32[64,128]{1,0:T(8,128)S(1)} %gram.1), channel_id=1, source_target_pairs={{0,4},{1,17},{2,6},{3,19},{4,0},{5,21},{6,2},{7,23},{8,12},{9,25},... | collective-permute-start | bytes 98312 | tf_op jit(solution)/shard_map/ppermute | solution.py:457
  95.5 3.9 %collective-permute-start.5 = (f32[64,128]{1,0:T(8,128)S(1)}, f32[64,128]{1,0:T(8,128)S(1)}, u32[]{:S(2)}, u32[]{:S(2)}) collective-permute-start(f32[64,128]{1,0:T(8,128)S(1)} %gram.1), channel_id=1, source_target_pairs={{0,8},{1,21},{2,10},{3,23},{4,12},{5,17},{6,14},{7,19},{8,0},{9,29... | collective-permute-start | bytes 98312 | tf_op jit(solution)/shard_map/ppermute | solution.py:457
  96.4 4.8 %collective-permute-start.6 = (f32[64,128]{1,0:T(8,128)S(1)}, f32[64,128]{1,0:T(8,128)S(1)}, u32[]{:S(2)}, u32[]{:S(2)}) collective-permute-start(f32[64,128]{1,0:T(8,128)S(1)} %gram.1), channel_id=1, source_target_pairs={{0,12},{1,25},{2,14},{3,27},{4,8},{5,29},{6,10},{7,31},{8,4},{9,17... | collective-permute-start | bytes 98312 | tf_op jit(solution)/shard_map/ppermute | solution.py:457
  101.2 4.4 %collective-permute-start.7 = (f32[64,128]{1,0:T(8,128)S(1)}, f32[64,128]{1,0:T(8,128)S(1)}, u32[]{:S(2)}, u32[]{:S(2)}) collective-permute-start(f32[64,128]{1,0:T(8,128)S(1)} %add_add_fusion.refs_0_), channel_id=1, source_target_pairs={{0,1},{1,0},{2,3},{3,2},{4,5},{5,4},{6,7},{7,6},{8,9},{9,8},{10,11... | collective-permute-start | bytes 98312 | tf_op jit(solution)/shard_map/ppermute | solution.py:448

commit v7 on v6

--- a/solution.py
+++ b/solution.py
@@ -149,7 +149,9 @@
 
             lax.while_loop(lambda prior: prior >= 0, add, back_ref[t])
             put(listed, skip, lambda: both_ref[t].astype(F8))
-            plan_ref[listed] = row | (slots_ref[t] << 8)
+            slot = slots_ref[t]
+            place = rb_dev + ((slot - rb_dev) ^ central(slots - rb_dev))
+            plan_ref[listed] = row | (jnp.where(slot < rb_dev, slot, place) << 8)
 
         return listed + closes
 
@@ -443,22 +445,22 @@
     )
 
 
+def central(nblk):
+    return nblk // 4
+
+
+def exchange(x):
+    nblk = lax.axis_size("blk")
+    group = [i ^ central(nblk) for i in range(nblk)]
+    return lax.all_to_all(x, "blk", split_axis=0, concat_axis=0, tiled=True, axis_index_groups=[group])
+
+
 def to_partner(x, axis, mask):
     n = lax.axis_size(axis)
     return lax.ppermute(x, axis, [(i, i ^ mask) for i in range(n)])
 
 
-def sum_parts(part, nblk, ncol):
-    if nblk == 8 and ncol % 2 == 0:
-        places = [(b, c) for b in range(nblk) for c in range(ncol)]
-
-        def collect_from(masks):
-            pairs = [(b * ncol + c, (b ^ masks[c % 2]) * ncol + c) for b, c in places if masks[c % 2]]
-            return lax.ppermute(part, ("blk", "col"), pairs)
-
-        got = [collect_from(masks) for masks in ((1, 4), (2, 5), (3, 6), (0, 7))]
-        total = jnp.where(lax.axis_index("col") % 2 == 0, part, got[3]) + got[0] + got[1] + got[2]
-        return [total, to_partner(total, "col", 1)]
+def sum_parts(part, nblk):
     wide = 1
     while 4 * wide < nblk:
         part = part + to_partner(part, "blk", wide)
@@ -473,9 +475,7 @@
     nblk = lax.axis_size("blk")
     ncol = lax.axis_size("col")
     near_count = LOC_RB * rb_dev
-    wanted = lax.all_to_all(
-        jnp.broadcast_to(fetch_pick[None], (nblk, 1, nblk)), "blk", split_axis=0, concat_axis=0, tiled=True
-    )
+    wanted = exchange(jnp.broadcast_to(fetch_pick[None], (nblk, 1, nblk)))
     packed, kept, scale, plan = tiles_call(tile_rows, tile_slots, tile_real, tile_imag, rb_dev, near_count)
 
     out_blocks = sds((nblk, group, order), BF16)
@@ -501,7 +501,7 @@
     vectors_here = sds((group, rows), F32)
     previous, current = y_start, y_start
     for step in range(STEPS):
-        arrived = lax.all_to_all(blocks, "blk", split_axis=0, concat_axis=0, tiled=True)
+        arrived = exchange(blocks)
         base = pl.pallas_call(
             functools.partial(near_kernel, step),
             name="near",
@@ -542,7 +542,7 @@
         scratch_shapes=[pltpu.VMEM((ncol, group, rows), BF16), pltpu.VMEM((vectors, vectors), F32)],
         compiler_params=params(LIMIT),
     )(current, *others)
-    parts = sum_parts(part, nblk, ncol)
+    parts = sum_parts(part, nblk)
     return pl.pallas_call(
         functools.partial(factor_kernel, len(parts), rows * nblk),
         name="factor",

time: 113 us -> 106 us (0.938)
  waiting for transfers between devices: 26.2 us -> 21.9 us
  starting transfers between devices: 32.8 us -> 30.9 us
    all_to_all x5, waiting for transfers between devices: 17.9 us -> 11.6 us  [exchange(): lax.all_to_all(x, 'blk', split_axis=0, concat_axis=0, tiled=True, axis_in...]
    ppermute x4 -> x7, waiting for transfers between devices: 5.68 us -> 10.3 us  [to_partner(): return lax.ppermute(x, axis, [(i, i ^ mask) for i in range(n)])]
    ppermute x4 -> x0, starting transfers between devices: 4.22 us -> none  [collect_from(): return lax.ppermute(part, ('blk', 'col'), pairs)]
    ppermute x4 -> x0, waiting for transfers between devices: 2.64 us -> none  [collect_from(): return lax.ppermute(part, ('blk', 'col'), pairs)]
    ppermute x4 -> x7, starting transfers between devices: 5.07 us -> 6.77 us  [to_partner(): return lax.ppermute(x, axis, [(i, i ^ mask) for i in range(n)])]
  transfers between devices with their start and end apart: 13 -> 12, of which waited for: 10 -> 9; matrix products, arithmetic and copies ran while one was open for 0% -> 0% of each run, Pallas kernels for 22% -> 24%
where the time goes in v7:
time: 106 us; the launch traced here: 105 us
  Pallas kernels  50.4 us (48%)
  starting transfers between devices  30.9 us (29%)
  waiting for transfers between devices  21.9 us (21%)
  local copies, waits for them, and re-layouts  1.25 us (1%)
    all_to_all x5, starting transfers between devices, exchange(): lax.all_to_all(x, 'blk', split_axis=0, concat_axis=0, tiled=True, axis_in...  24.2 us
    pallas_call x4, Pallas kernels, per_device(): pl.pallas_call(functools.partial(step_kernel, step), name='step', out_sha...  17.7 us
    pallas_call x1, Pallas kernels, tiles_call(): pl.pallas_call(functools.partial(tiles_kernel, near_count), name='tiles',...  13.5 us
    all_to_all x5, waiting for transfers between devices, exchange(): lax.all_to_all(x, 'blk', split_axis=0, concat_axis=0, tiled=True, axis_in...  11.6 us
    pallas_call x4, Pallas kernels, per_device(): pl.pallas_call(functools.partial(near_kernel, step), name='near', out_sha...  11.2 us
    ppermute x7, waiting for transfers between devices, to_partner(): return lax.ppermute(x, axis, [(i, i ^ mask) for i in range(n)])  10.3 us
    ppermute x7, starting transfers between devices, to_partner(): return lax.ppermute(x, axis, [(i, i ^ mask) for i in range(n)])  6.77 us
    pallas_call x1, Pallas kernels, per_device(): pl.pallas_call(functools.partial(factor_kernel, len(parts), rows * nblk),...  6.24 us
  transfers between devices with their start and end apart: 12, of which 9 were waited for; matrix products, arithmetic and copies ran while one was open for 0% of the time, Pallas kernels for 24%

profile of v7, /device:TPU:0, one launch (start us, length us, event | category | flops | bytes accessed | tf_op | source)
XLA Modules:
  0.0 104.6 jit_solution(2574958111766681651)
XLA Ops:
  1.2 7.8 %all-to-all-start = ((s32[8,1,8]{2,1,0:T(1,128)}), s32[8,1,8]{2,1,0:T(1,128)S(1)}, u32[]{:S(2)}, u32[]{:S(2)}) async-start(s32[8,1,8]{2,1,0:T(1,128)} %broadcast_in_dim.9), calls=%async_computation | async-start | bytes 8192 | tf_op jit(solution)/shard_map/all_to_all | solution.py:455
  9.1 13.5 %tiles.1 = (f8e4m3fn[96,256,512]{2,1,0:T(32,128)(4,1)}, f8e4m3fn[16,256,512]{2,1,0:T(32,128)(4,1)S(1)}, f32[8,2048]{1,0:T(8,128)S(1)}, s32[128]{0:T(128)S(1)}) custom-call(s32[96]{0:T(128)} %rows_ref.1, s32[96]{0:T(128)} %slots_ref.1, bf16[96,256,256]{2,1,0:T(8,128)(2,1)} %real_hbm.1, bf16[96,256,256]{2,1,0:T(8,128)(2,1)} %imag_hbm.1), custom_call_target="tpu_custom_call" | custom-call | flops 268435456 | bytes 25165824 | tf_op jit(solution)/shard_map/tiles/pallas_call | solution.py:202
  24.0 5.0 %all-to-all-start.1 = ((bf16[8,32,256]{2,1,0:T(8,128)(2,1)}), bf16[8,32,256]{2,1,0:T(8,128)(2,1)S(1)}, u32[]{:S(2)}, u32[]{:S(2)}) async-start(bf16[8,32,256]{2,1,0:T(8,128)(2,1)} %first.1), calls=%async_computation.1 | async-start | bytes 262144 | tf_op jit(solution)/shard_map/all_to_all | solution.py:455
  29.0 2.8 %near.4.base_ref = f32[32,2048]{1,0:T(8,128)S(1)} custom-call(s32[128]{0:T(128)S(1)} %get-tuple-element.15.plan_ref, f8e4m3fn[96,256,512]{2,1,0:T(32,128)(4,1)} %get-tuple-element.16.packed_hbm, f32[8,2048]{1,0:T(8,128)S(1)} %get-tuple-element.18.scale_ref, f32[32,2048]{1,0:T(8,128)S(1)} %copy-done, f32[32,2048]{1,0:T(8,128)S(1)} %copy-done), custom_call_target="tpu_custom_call" | custom-call | flops 268435456 | bytes 2097152 | tf_op jit(solution)/shard_map/near/pallas_call | solution.py:505
  31.8 2.9 %all-to-all-done.1.arrived_ref = bf16[8,32,256]{2,1,0:T(8,128)(2,1)S(1)} async-done(((bf16[8,32,256]{2,1,0:T(8,128)(2,1)}), bf16[8,32,256]{2,1,0:T(8,128)(2,1)S(1)}, u32[]{:S(2)}, u32[]{:S(2)}) %all-to-all-start.1) | async-done | bytes 131104 | tf_op jit(solution)/shard_map/all_to_all | solution.py:455
  34.7 4.6 %step.4 = (f32[32,2048]{1,0:T(8,128)S(1)}, bf16[8,32,256]{2,1,0:T(8,128)(2,1)}) custom-call(s32[128]{0:T(128)S(1)} %get-tuple-element.15.plan_ref, s32[8,1,8]{2,1,0:T(1,128)S(1)} %all-to-all-done.wanted_ref, f8e4m3fn[96,256,512]{2,1,0:T(32,128)(4,1)} %get-tuple-element.16.packed_hbm, f8e4m3fn[16,256,512]{2,1,0:T(32,128)(4,1)S(1)} %get-tuple-element.17.kept_ref, ...), custom_call_target="tpu_custom_call" | custom-call | tf_op jit(solution)/shard_map/step/pallas_call | solution.py:516
  39.3 3.8 %all-to-all-start.2 = ((bf16[8,32,256]{2,1,0:T(8,128)(2,1)}), bf16[8,32,256]{2,1,0:T(8,128)(2,1)S(1)}, u32[]{:S(2)}, u32[]{:S(2)}) async-start(bf16[8,32,256]{2,1,0:T(8,128)(2,1)} %get-tuple-element.20), calls=%async_computation.2 | async-start | bytes 262144 | tf_op jit(solution)/shard_map/all_to_all | solution.py:455
  43.1 2.8 %near.5.base_ref = f32[32,2048]{1,0:T(8,128)S(1)} custom-call(s32[128]{0:T(128)S(1)} %get-tuple-element.15.plan_ref, f8e4m3fn[96,256,512]{2,1,0:T(32,128)(4,1)} %get-tuple-element.16.packed_hbm, f32[8,2048]{1,0:T(8,128)S(1)} %get-tuple-element.18.scale_ref, f32[32,2048]{1,0:T(8,128)S(1)} %get-tuple-element.19.now_ref.before_ref, f32[32,2048]{1,0:T(8,128)S(1)} %copy-done), custom_call_target="tpu_custom_call" | custom-call | flops 268435456 | bytes 2097152 | tf_op jit(solution)/shard_map/near/pallas_call | solution.py:505
  45.9 2.9 %all-to-all-done.2.arrived_ref = bf16[8,32,256]{2,1,0:T(8,128)(2,1)S(1)} async-done(((bf16[8,32,256]{2,1,0:T(8,128)(2,1)}), bf16[8,32,256]{2,1,0:T(8,128)(2,1)S(1)}, u32[]{:S(2)}, u32[]{:S(2)}) %all-to-all-start.2) | async-done | bytes 131104 | tf_op jit(solution)/shard_map/all_to_all | solution.py:455
  48.8 4.6 %step.5 = (f32[32,2048]{1,0:T(8,128)S(1)}, bf16[8,32,256]{2,1,0:T(8,128)(2,1)}) custom-call(s32[128]{0:T(128)S(1)} %get-tuple-element.15.plan_ref, s32[8,1,8]{2,1,0:T(1,128)S(1)} %all-to-all-done.wanted_ref, f8e4m3fn[96,256,512]{2,1,0:T(32,128)(4,1)} %get-tuple-element.16.packed_hbm, f8e4m3fn[16,256,512]{2,1,0:T(32,128)(4,1)S(1)} %get-tuple-element.17.kept_ref, ...), custom_call_target="tpu_custom_call" | custom-call | tf_op jit(solution)/shard_map/step/pallas_call | solution.py:516
  53.4 3.8 %all-to-all-start.3 = ((bf16[8,32,256]{2,1,0:T(8,128)(2,1)}), bf16[8,32,256]{2,1,0:T(8,128)(2,1)S(1)}, u32[]{:S(2)}, u32[]{:S(2)}) async-start(bf16[8,32,256]{2,1,0:T(8,128)(2,1)} %get-tuple-element.22), calls=%async_computation.3 | async-start | bytes 262144 | tf_op jit(solution)/shard_map/all_to_all | solution.py:455
  57.1 2.8 %near.6.base_ref = f32[32,2048]{1,0:T(8,128)S(1)} custom-call(s32[128]{0:T(128)S(1)} %get-tuple-element.15.plan_ref, f8e4m3fn[96,256,512]{2,1,0:T(32,128)(4,1)} %get-tuple-element.16.packed_hbm, f32[8,2048]{1,0:T(8,128)S(1)} %get-tuple-element.18.scale_ref, f32[32,2048]{1,0:T(8,128)S(1)} %get-tuple-element.21.now_ref.before_ref, ...), custom_call_target="tpu_custom_call" | custom-call | flops 268435456 | bytes 2097152 | tf_op jit(solution)/shard_map/near/pallas_call | solution.py:505
  59.9 2.9 %all-to-all-done.3.arrived_ref = bf16[8,32,256]{2,1,0:T(8,128)(2,1)S(1)} async-done(((bf16[8,32,256]{2,1,0:T(8,128)(2,1)}), bf16[8,32,256]{2,1,0:T(8,128)(2,1)S(1)}, u32[]{:S(2)}, u32[]{:S(2)}) %all-to-all-start.3) | async-done | bytes 131104 | tf_op jit(solution)/shard_map/all_to_all | solution.py:455
  62.8 4.6 %step.6 = (f32[32,2048]{1,0:T(8,128)S(1)}, bf16[8,32,256]{2,1,0:T(8,128)(2,1)}) custom-call(s32[128]{0:T(128)S(1)} %get-tuple-element.15.plan_ref, s32[8,1,8]{2,1,0:T(1,128)S(1)} %all-to-all-done.wanted_ref, f8e4m3fn[96,256,512]{2,1,0:T(32,128)(4,1)} %get-tuple-element.16.packed_hbm, f8e4m3fn[16,256,512]{2,1,0:T(32,128)(4,1)S(1)} %get-tuple-element.17.kept_ref, ...), custom_call_target="tpu_custom_call" | custom-call | tf_op jit(solution)/shard_map/step/pallas_call | solution.py:516
  67.4 3.8 %all-to-all-start.4 = ((bf16[8,32,256]{2,1,0:T(8,128)(2,1)}), bf16[8,32,256]{2,1,0:T(8,128)(2,1)S(1)}, u32[]{:S(2)}, u32[]{:S(2)}) async-start(bf16[8,32,256]{2,1,0:T(8,128)(2,1)} %get-tuple-element.24), calls=%async_computation.4 | async-start | bytes 262144 | tf_op jit(solution)/shard_map/all_to_all | solution.py:455
  71.2 2.8 %near.7.base_ref = f32[32,2048]{1,0:T(8,128)S(1)} custom-call(s32[128]{0:T(128)S(1)} %get-tuple-element.15.plan_ref, f8e4m3fn[96,256,512]{2,1,0:T(32,128)(4,1)} %get-tuple-element.16.packed_hbm, f32[8,2048]{1,0:T(8,128)S(1)} %get-tuple-element.18.scale_ref, f32[32,2048]{1,0:T(8,128)S(1)} %get-tuple-element.23.now_ref, ...), custom_call_target="tpu_custom_call" | custom-call | flops 268435456 | bytes 2097152 | tf_op jit(solution)/shard_map/near/pallas_call | solution.py:505
  74.0 2.9 %all-to-all-done.4.arrived_ref = bf16[8,32,256]{2,1,0:T(8,128)(2,1)S(1)} async-done(((bf16[8,32,256]{2,1,0:T(8,128)(2,1)}), bf16[8,32,256]{2,1,0:T(8,128)(2,1)S(1)}, u32[]{:S(2)}, u32[]{:S(2)}) %all-to-all-start.4) | async-done | bytes 131104 | tf_op jit(solution)/shard_map/all_to_all | solution.py:455
  76.9 3.9 %step.7.own_ref = f32[32,2048]{1,0:T(8,128)S(1)} custom-call(s32[128]{0:T(128)S(1)} %get-tuple-element.15.plan_ref, s32[8,1,8]{2,1,0:T(1,128)S(1)} %all-to-all-done.wanted_ref, f8e4m3fn[96,256,512]{2,1,0:T(32,128)(4,1)} %get-tuple-element.16.packed_hbm, f8e4m3fn[16,256,512]{2,1,0:T(32,128)(4,1)S(1)} %get-tuple-element.17.kept_ref, ...), custom_call_target="tpu_custom_call" | custom-call | tf_op jit(solution)/shard_map/step/pallas_call | solution.py:516
  82.4 3.5 %collective-permute-done.1.refs_1_.refs_5_ = bf16[32,2048]{1,0:T(8,128)(2,1)S(1)} collective-permute-done((bf16[32,2048]{1,0:T(8,128)(2,1)S(1)}, bf16[32,2048]{1,0:T(8,128)(2,1)S(1)}, u32[]{:S(2)}, u32[]{:S(2)}) %collective-permute-start.1) | collective-permute-done | bytes 131104 | tf_op jit(solution)/shard_map/ppermute | solution.py:460
  88.5 3.2 %collective-permute-done.3 = f32[64,128]{1,0:T(8,128)S(1)} collective-permute-done((f32[64,128]{1,0:T(8,128)S(1)}, f32[64,128]{1,0:T(8,128)S(1)}, u32[]{:S(2)}, u32[]{:S(2)}) %collective-permute-start.3) | collective-permute-done | bytes 32800 | tf_op jit(solution)/shard_map/ppermute | solution.py:460
  91.6 1.9 %collective-permute-start.6 = (f32[64,128]{1,0:T(8,128)S(1)}, f32[64,128]{1,0:T(8,128)S(1)}, u32[]{:S(2)}, u32[]{:S(2)}) collective-permute-start(f32[64,128]{1,0:T(8,128)S(1)} %add.3.refs_0_), channel_id=1, source_target_pairs={{0,24},{4,28},{8,16},{12,20},{16,8},{20,12},{24,0},{28,4},{1,25},{... | collective-permute-start | bytes 98312 | tf_op jit(solution)/shard_map/ppermute | solution.py:460
  93.6 2.5 %collective-permute-start.4 = (f32[64,128]{1,0:T(8,128)S(1)}, f32[64,128]{1,0:T(8,128)S(1)}, u32[]{:S(2)}, u32[]{:S(2)}) collective-permute-start(f32[64,128]{1,0:T(8,128)S(1)} %add.3.refs_0_), channel_id=1, source_target_pairs={{0,8},{4,12},{8,0},{12,4},{16,24},{20,28},{24,16},{28,20},{1,9},{5... | collective-permute-start | bytes 98312 | tf_op jit(solution)/shard_map/ppermute | solution.py:460
  96.0 1.7 %collective-permute-done.6.refs_3_ = f32[64,128]{1,0:T(8,128)S(1)} collective-permute-done((f32[64,128]{1,0:T(8,128)S(1)}, f32[64,128]{1,0:T(8,128)S(1)}, u32[]{:S(2)}, u32[]{:S(2)}) %collective-permute-start.6) | collective-permute-done | bytes 32800 | tf_op jit(solution)/shard_map/ppermute | solution.py:460
  98.4 6.2 %factor.1 = f32[32,2048]{1,0:T(8,128)} custom-call(f32[32,2048]{1,0:T(8,128)S(1)} %step.7.own_ref, f32[64,128]{1,0:T(8,128)S(1)} %add.3.refs_0_, f32[64,128]{1,0:T(8,128)S(1)} %collective-permute-done.4.refs_1_, f32[64,128]{1,0:T(8,128)S(1)} %collective-permute-done.5.refs_2_, f32[64,128]{1,0:T(8,128)S(1)} %collective-permute-done.6.refs_3_, ...), custom_call_target="tpu_custom_call" | custom-call | tf_op jit(solution)/shard_map/factor/pallas_call | solution.py:546
  (17 shorter events, 7.3 us)
Async XLA Ops:
  1.2 21.4 %all-to-all-start = ((s32[8,1,8]{2,1,0:T(1,128)}), s32[8,1,8]{2,1,0:T(1,128)S(1)}, u32[]{:S(2)}, u32[]{:S(2)}) async-start(s32[8,1,8]{2,1,0:T(1,128)} %broadcast_in_dim.9), calls=%async_computation | async-start | bytes 8192 | tf_op jit(solution)/shard_map/all_to_all | solution.py:455
  9.1 13.6 %copy-start = (f32[32,2048]{1,0:T(8,128)S(1)}, f32[32,2048]{1,0:T(8,128)}, u32[]{:S(2)}) copy-start(f32[32,2048]{1,0:T(8,128)} %before_ref.3) | copy-start | bytes 786436
  24.0 10.8 %all-to-all-start.1 = ((bf16[8,32,256]{2,1,0:T(8,128)(2,1)}), bf16[8,32,256]{2,1,0:T(8,128)(2,1)S(1)}, u32[]{:S(2)}, u32[]{:S(2)}) async-start(bf16[8,32,256]{2,1,0:T(8,128)(2,1)} %first.1), calls=%async_computation.1 | async-start | bytes 262144 | tf_op jit(solution)/shard_map/all_to_all | solution.py:455
  39.3 9.5 %all-to-all-start.2 = ((bf16[8,32,256]{2,1,0:T(8,128)(2,1)}), bf16[8,32,256]{2,1,0:T(8,128)(2,1)S(1)}, u32[]{:S(2)}, u32[]{:S(2)}) async-start(bf16[8,32,256]{2,1,0:T(8,128)(2,1)} %get-tuple-element.20), calls=%async_computation.2 | async-start | bytes 262144 | tf_op jit(solution)/shard_map/all_to_all | solution.py:455
  53.4 9.5 %all-to-all-start.3 = ((bf16[8,32,256]{2,1,0:T(8,128)(2,1)}), bf16[8,32,256]{2,1,0:T(8,128)(2,1)S(1)}, u32[]{:S(2)}, u32[]{:S(2)}) async-start(bf16[8,32,256]{2,1,0:T(8,128)(2,1)} %get-tuple-element.22), calls=%async_computation.3 | async-start | bytes 262144 | tf_op jit(solution)/shard_map/all_to_all | solution.py:455
  67.4 9.5 %all-to-all-start.4 = ((bf16[8,32,256]{2,1,0:T(8,128)(2,1)}), bf16[8,32,256]{2,1,0:T(8,128)(2,1)S(1)}, u32[]{:S(2)}, u32[]{:S(2)}) async-start(bf16[8,32,256]{2,1,0:T(8,128)(2,1)} %get-tuple-element.24), calls=%async_computation.4 | async-start | bytes 262144 | tf_op jit(solution)/shard_map/all_to_all | solution.py:455
  80.8 5.0 %collective-permute-start.1 = (bf16[32,2048]{1,0:T(8,128)(2,1)S(1)}, bf16[32,2048]{1,0:T(8,128)(2,1)S(1)}, u32[]{:S(2)}, u32[]{:S(2)}) collective-permute-start(bf16[32,2048]{1,0:T(8,128)(2,1)S(1)} %convert_element_type.3), channel_id=1, source_target_pairs={{0,2},{1,3},{2,0},{3,1},{4,6},{5,7},{6,4},{7,5},{8,10},{9,11},{10,... | collective-permute-start | bytes 393224 | tf_op jit(solution)/shard_map/ppermute | solution.py:460
  82.4 3.5 %collective-permute-start = (bf16[32,2048]{1,0:T(8,128)(2,1)S(1)}, bf16[32,2048]{1,0:T(8,128)(2,1)S(1)}, u32[]{:S(2)}, u32[]{:S(2)}) collective-permute-start(bf16[32,2048]{1,0:T(8,128)(2,1)S(1)} %convert_element_type.3), channel_id=1, source_target_pairs={{0,1},{1,0},{2,3},{3,2},{4,5},{5,4},{6,7},{7,6},{8,9},{9,8},{10,11... | collective-permute-start | bytes 393224 | tf_op jit(solution)/shard_map/ppermute | solution.py:460
  85.9 1.3 %collective-permute-start.2 = (bf16[32,2048]{1,0:T(8,128)(2,1)S(1)}, bf16[32,2048]{1,0:T(8,128)(2,1)S(1)}, u32[]{:S(2)}, u32[]{:S(2)}) collective-permute-start(bf16[32,2048]{1,0:T(8,128)(2,1)S(1)} %collective-permute-done.1.refs_1_.refs_5_), channel_id=1, source_target_pairs={{0,1},{1,0},{2,3},{3,2},{4,5},{5,4},{6,7},{7,6},{8,9},{9,8},{10,11... | collective-permute-start | bytes 393224 | tf_op jit(solution)/shard_map/ppermute | solution.py:460
  87.7 4.0 %collective-permute-start.3 = (f32[64,128]{1,0:T(8,128)S(1)}, f32[64,128]{1,0:T(8,128)S(1)}, u32[]{:S(2)}, u32[]{:S(2)}) collective-permute-start(f32[64,128]{1,0:T(8,128)S(1)} %gram.1), channel_id=1, source_target_pairs={{0,4},{4,0},{8,12},{12,8},{16,20},{20,16},{24,28},{28,24},{1,5},{5... | collective-permute-start | bytes 98312 | tf_op jit(solution)/shard_map/ppermute | solution.py:460
  91.6 6.1 %collective-permute-start.6 = (f32[64,128]{1,0:T(8,128)S(1)}, f32[64,128]{1,0:T(8,128)S(1)}, u32[]{:S(2)}, u32[]{:S(2)}) collective-permute-start(f32[64,128]{1,0:T(8,128)S(1)} %add.3.refs_0_), channel_id=1, source_target_pairs={{0,24},{4,28},{8,16},{12,20},{16,8},{20,12},{24,0},{28,4},{1,25},{... | collective-permute-start | bytes 98312 | tf_op jit(solution)/shard_map/ppermute | solution.py:460
  93.5 4.8 %collective-permute-start.5 = (f32[64,128]{1,0:T(8,128)S(1)}, f32[64,128]{1,0:T(8,128)S(1)}, u32[]{:S(2)}, u32[]{:S(2)}) collective-permute-start(f32[64,128]{1,0:T(8,128)S(1)} %add.3.refs_0_), channel_id=1, source_target_pairs={{0,16},{4,20},{8,24},{12,28},{16,0},{20,4},{24,8},{28,12},{1,17},{... | collective-permute-start | bytes 98312 | tf_op jit(solution)/shard_map/ppermute | solution.py:460
  93.6 4.8 %collective-permute-start.4 = (f32[64,128]{1,0:T(8,128)S(1)}, f32[64,128]{1,0:T(8,128)S(1)}, u32[]{:S(2)}, u32[]{:S(2)}) collective-permute-start(f32[64,128]{1,0:T(8,128)S(1)} %add.3.refs_0_), channel_id=1, source_target_pairs={{0,8},{4,12},{8,0},{12,4},{16,24},{20,28},{24,16},{28,20},{1,9},{5... | collective-permute-start | bytes 98312 | tf_op jit(solution)/shard_map/ppermute | solution.py:460

commit v8 on v7

--- a/solution.py
+++ b/solution.py
@@ -10,6 +10,7 @@
 
 LOC_RB = 2
 STEPS = 4
+WIDE = 8
 UNROLL = 4
 KEPT = 16
 CHUNK = 4
@@ -230,16 +231,24 @@
     return (field[:, at] * scale_ref[0:1, at]).astype(BF16)
 
 
-def send_picked(wanted_ref, sent_ref, out_ref):
-    me = lax.axis_index("blk")
-    for p in range(out_ref.shape[0]):
-        out_ref[p] = sent_ref[wanted_ref[p, 0, me]]
-
-
-def first_kernel(y_ref, scale_ref, wanted_ref, out_ref, sent_ref):
+def send_picked(picks_ref, sent_ref, out_ref):
+    for i in range(out_ref.shape[0]):
+        out_ref[i] = sent_ref[picks_ref[i]]
+
+
+def first_kernel(y_ref, scale_ref, wanted_hbm, out_ref, picks_ref, sent_ref, wanted_ref, sem):
+    nblk, rows, lanes = wanted_ref.shape
+    copy = pltpu.make_async_copy(wanted_hbm.at[:, 0:rows, 0:lanes], wanted_ref, sem)
+    copy.start()
     for r in range(sent_ref.shape[0]):
         sent_ref[r] = rounded_block(y_ref, scale_ref, r, sent_ref.shape[2])
-    send_picked(wanted_ref, sent_ref, out_ref)
+    copy.wait()
+    mine = lax.broadcasted_iota(I32, (rows, lanes), 1) == lax.axis_index("blk")
+    top = lax.broadcasted_iota(I32, (rows, lanes), 0) == 0
+    for i in range(nblk):
+        pick = jnp.sum(jnp.where(mine & top, wanted_ref[i ^ central(nblk)], 0.0))
+        picks_ref[i] = pick.astype(I32)
+    send_picked(picks_ref, sent_ref, out_ref)
 
 
 def load_groups(packed_hbm, tiles_ref, sems, lo, hi):
@@ -324,7 +333,7 @@
         base_ref[:, at] = moved if step == 0 else 2.0 * moved - before_ref[:, at]
 
 
-def step_kernel(step, plan_ref, wanted_ref, packed_hbm, kept_ref, scale_ref, base_ref, arrived_ref, *refs):
+def step_kernel(step, plan_ref, picks_ref, packed_hbm, kept_ref, scale_ref, base_ref, arrived_ref, *refs):
     last = step == STEPS - 1
     next_ref = refs[0]
     tiles_ref, x_ref, acc_ref, sems = refs[-4:]
@@ -348,7 +357,7 @@
         if not last:
             refs[2][r] = (following * scale).astype(BF16)
     if not last:
-        send_picked(wanted_ref, refs[2], refs[1])
+        send_picked(picks_ref, refs[2], refs[1])
 
 
 def all_rows(own_ref, arrived, all_ref):
@@ -373,10 +382,14 @@
 PANEL = 32
 
 
-def factor_kernel(grams, nodes, own_ref, *refs):
-    parts = refs[:grams]
-    arrived = refs[grams:-4]
-    out_ref, all_ref, work_ref, inverse_ref = refs[-4:]
+def finer_reciprocal(x):
+    guess = pl.reciprocal(x, approx=True)
+    guess = guess * (2.0 - x * guess)
+    return guess * (2.0 - x * guess)
+
+
+def factor_kernel(nodes, own_ref, all_ref, *refs):
+    parts, (out_ref, work_ref, inverse_ref) = refs[:-3], refs[-3:]
     group = own_ref.shape[0]
     order = work_ref.shape[0]
     total = parts[0][...]
@@ -397,9 +410,9 @@
             w = [jnp.broadcast_to(a[:, i : i + 1], a.shape) for i in range(top + k, top + k + 4)]
             p, q = w[0][k : k + 1, :], w[2][k + 2 : k + 3, :]
             u, v = w[2][k : k + 1, :], w[3][k : k + 1, :]
-            single = 1.0 / p
+            single = finer_reciprocal(p)
             det = p * q - (u * u + v * v)
-            both = 1.0 / det
+            both = finer_reciprocal(det)
             second = (here == k + 2) | (here == k + 3)
             below = here > k + 3
             coefficients = (
@@ -429,7 +442,7 @@
     mine = mine * math.sqrt(nodes)
     high = mine.astype(BF16)
     low = (mine - high.astype(F32)).astype(BF16)
-    rows = all_rows(own_ref, arrived, all_ref)
+    rows = all_ref[...].reshape(order, own_ref.shape[1])
     both = lax.dot_general(
         jnp.concatenate([high, low], axis=0), rows, (((1,), (0,)), ((), ())), preferred_element_type=F32
     )
@@ -475,20 +488,22 @@
     nblk = lax.axis_size("blk")
     ncol = lax.axis_size("col")
     near_count = LOC_RB * rb_dev
-    wanted = exchange(jnp.broadcast_to(fetch_pick[None], (nblk, 1, nblk)))
+    picked = jnp.pad(fetch_pick.astype(F32), ((0, 0), (0, rows - nblk)))
+    top = lax.broadcasted_iota(I32, (WIDE, rows), 0) == 0
+    wanted = lax.all_gather(jnp.where(top, picked, y_start[:WIDE]), "blk", axis=0, tiled=False)
     packed, kept, scale, plan = tiles_call(tile_rows, tile_slots, tile_real, tile_imag, rb_dev, near_count)
 
     out_blocks = sds((nblk, group, order), BF16)
     sent_scratch = pltpu.VMEM((rb_dev, group, order), BF16)
-    blocks = pl.pallas_call(
+    blocks, picks = pl.pallas_call(
         first_kernel,
         name="first",
-        out_shape=out_blocks,
-        in_specs=[VMEM, VMEM, SMEM],
-        out_specs=VMEM,
-        scratch_shapes=[sent_scratch],
+        out_shape=(out_blocks, sds((nblk,), I32)),
+        in_specs=[VMEM, VMEM, ANY],
+        out_specs=(VMEM, SMEM),
+        scratch_shapes=[sent_scratch, pltpu.VMEM((nblk, 8, 128), F32), pltpu.SemaphoreType.DMA],
         compiler_params=params(LIMIT),
-    )(y_start, scale, wanted)
+    )(y_start, scale, in_hbm(wanted))
 
     def scratch(entries, sources):
         return [
@@ -521,7 +536,7 @@
             out_specs=[VMEM] if last else [VMEM, VMEM],
             scratch_shapes=([] if last else [sent_scratch]) + scratch(tiles - near_count - KEPT, nblk),
             compiler_params=params(LIMIT),
-        )(plan, wanted, in_hbm(packed), pltpu.with_memory_space_constraint(kept, pltpu.VMEM), scale, base, arrived)
+        )(plan, picks, in_hbm(packed), pltpu.with_memory_space_constraint(kept, pltpu.VMEM), scale, base, arrived)
         previous, current = current, out[0]
         if not last:
             blocks = out[1]
@@ -533,29 +548,25 @@
     else:
         others = [to_partner(rounded, "col", s) for s in range(1, ncol)]
     vectors = group * ncol
-    part = pl.pallas_call(
+    part, gathered = pl.pallas_call(
         gram_kernel,
         name="gram",
-        out_shape=sds((vectors // 2, vectors), F32),
+        out_shape=(sds((vectors // 2, vectors), F32), sds((ncol, group, rows), BF16)),
         in_specs=[VMEM] * (1 + len(others)),
-        out_specs=VMEM,
-        scratch_shapes=[pltpu.VMEM((ncol, group, rows), BF16), pltpu.VMEM((vectors, vectors), F32)],
+        out_specs=(VMEM, VMEM),
+        scratch_shapes=[pltpu.VMEM((vectors, vectors), F32)],
         compiler_params=params(LIMIT),
     )(current, *others)
     parts = sum_parts(part, nblk)
     return pl.pallas_call(
-        functools.partial(factor_kernel, len(parts), rows * nblk),
+        functools.partial(factor_kernel, rows * nblk),
         name="factor",
         out_shape=sds((group, rows), F32),
-        in_specs=[VMEM] * (1 + len(parts) + len(others)),
+        in_specs=[VMEM] * (2 + len(parts)),
         out_specs=VMEM,
-        scratch_shapes=[
-            pltpu.VMEM((ncol, group, rows), BF16),
-            pltpu.VMEM((vectors, vectors), F32),
-            pltpu.VMEM((vectors, vectors), F32),
-        ],
+        scratch_shapes=[pltpu.VMEM((vectors, vectors), F32)] * 2,
         compiler_params=params(LIMIT),
-    )(current, *parts, *others)
+    )(current, gathered, *parts)
 
 
 def solution(mesh):

time: 106 us -> 134 us (1.26)
  blocking collectives: 0 us -> 35.2 us
  starting transfers between devices: 30.9 us -> 22.9 us
  waiting for transfers between devices: 21.9 us -> 23.6 us
  other arithmetic: 0.02 us -> 1.6 us
    all_gather x0 -> x1, blocking collectives: none -> 35.2 us  [per_device(): lax.all_gather(jnp.where(top, picked, y_start[:WIDE]), 'blk', axis=0, til...]
    all_to_all x5 -> x4, starting transfers between devices: 24.2 us -> 16.9 us  [exchange(): lax.all_to_all(x, 'blk', split_axis=0, concat_axis=0, tiled=True, axis_in...]
    all_to_all x5 -> x4, waiting for transfers between devices: 11.6 us -> 12.7 us  [exchange(): lax.all_to_all(x, 'blk', split_axis=0, concat_axis=0, tiled=True, axis_in...]
  transfers between devices with their start and end apart: 12 -> 11, of which waited for: 9 -> 10; matrix products, arithmetic and copies ran while one was open for 0% -> 0% of each run, Pallas kernels for 24% -> 8%
where the time goes in v8:
time: 134 us
  Pallas kernels  50.2 us (37%)
  blocking collectives  35.2 us (26%)
  waiting for transfers between devices  23.6 us (18%)
  starting transfers between devices  22.9 us (17%)
  other arithmetic  1.6 us (1%)
    all_gather x1, blocking collectives, per_device(): lax.all_gather(jnp.where(top, picked, y_start[:WIDE]), 'blk', axis=0, til...  35.2 us
    pallas_call x4, Pallas kernels, per_device(): pl.pallas_call(functools.partial(step_kernel, step), name='step', out_sha...  18.5 us
    all_to_all x4, starting transfers between devices, exchange(): lax.all_to_all(x, 'blk', split_axis=0, concat_axis=0, tiled=True, axis_in...  16.9 us
    pallas_call x1, Pallas kernels, tiles_call(): pl.pallas_call(functools.partial(tiles_kernel, near_count), name='tiles',...  13.3 us
    all_to_all x4, waiting for transfers between devices, exchange(): lax.all_to_all(x, 'blk', split_axis=0, concat_axis=0, tiled=True, axis_in...  12.7 us
    ppermute x7, waiting for transfers between devices, to_partner(): return lax.ppermute(x, axis, [(i, i ^ mask) for i in range(n)])  11 us
    pallas_call x4, Pallas kernels, per_device(): pl.pallas_call(functools.partial(near_kernel, step), name='near', out_sha...  10.1 us
    pallas_call x1, Pallas kernels, per_device(): pl.pallas_call(functools.partial(factor_kernel, rows * nblk), name='facto...  6.25 us
  transfers between devices with their start and end apart: 11, of which 10 were waited for; matrix products, arithmetic and copies ran while one was open for 0% of the time, Pallas kernels for 8%

profile of v8, /device:TPU:0, one launch (start us, length us, event | category | flops | bytes accessed | tf_op | source)
XLA Modules:
  0.0 133.7 jit_solution(13843773662973125256)
XLA Ops:
  1.6 35.2 %all-gather = f32[64,2048]{1,0:T(8,128)} all-gather(f32[8,2048]{1,0:T(8,128)S(1)} %slice_select_fusion), channel_id=2, replica_groups=mesh['blk'=8,'col'=4] {'blk'}, dimensions={0}, use_global_device_ids=true | all-gather | bytes 589824 | tf_op jit(solution)/shard_map/all_gather | solution.py:493
  36.8 13.3 %tiles.1 = (f8e4m3fn[96,256,512]{2,1,0:T(32,128)(4,1)}, f8e4m3fn[16,256,512]{2,1,0:T(32,128)(4,1)S(1)}, f32[8,2048]{1,0:T(8,128)S(1)}, s32[128]{0:T(128)S(1)}) custom-call(s32[96]{0:T(128)} %rows_ref.1, s32[96]{0:T(128)} %slots_ref.1, bf16[96,256,256]{2,1,0:T(8,128)(2,1)} %real_hbm.1, bf16[96,256,256]{2,1,0:T(8,128)(2,1)} %imag_hbm.1), custom_call_target="tpu_custom_call" | custom-call | flops 268435456 | bytes 25165824 | tf_op jit(solution)/shard_map/tiles/pallas_call | solution.py:203
  50.1 1.6 %first.1 = (bf16[8,32,256]{2,1,0:T(8,128)(2,1)}, s32[8]{0:T(128)S(1)}) custom-call(f32[32,2048]{1,0:T(8,128)S(1)} %copy-done, f32[8,2048]{1,0:T(8,128)S(1)} %get-tuple-element.20.scale_ref, f32[8,8,2048]{2,1,0:T(8,128)} %bitcast.2), custom_call_target="tpu_custom_call" | custom-call | tf_op jit(solution)/shard_map/first/pallas_call | solution.py:498
  51.7 6.4 %all-to-all-start = ((bf16[8,32,256]{2,1,0:T(8,128)(2,1)}), bf16[8,32,256]{2,1,0:T(8,128)(2,1)S(1)}, u32[]{:S(2)}, u32[]{:S(2)}) async-start(bf16[8,32,256]{2,1,0:T(8,128)(2,1)} %get-tuple-element.24), calls=%async_computation | async-start | bytes 262144 | tf_op jit(solution)/shard_map/all_to_all | solution.py:468
  58.1 2.5 %near.4.base_ref = f32[32,2048]{1,0:T(8,128)S(1)} custom-call(s32[128]{0:T(128)S(1)} %get-tuple-element.19.plan_ref, f8e4m3fn[96,256,512]{2,1,0:T(32,128)(4,1)} %get-tuple-element.22.packed_hbm, f32[8,2048]{1,0:T(8,128)S(1)} %get-tuple-element.20.scale_ref, f32[32,2048]{1,0:T(8,128)S(1)} %copy-done, f32[32,2048]{1,0:T(8,128)S(1)} %copy-done), custom_call_target="tpu_custom_call" | custom-call | flops 268435456 | bytes 2097152 | tf_op jit(solution)/shard_map/near/pallas_call | solution.py:520
  60.7 3.2 %all-to-all-done.arrived_ref = bf16[8,32,256]{2,1,0:T(8,128)(2,1)S(1)} async-done(((bf16[8,32,256]{2,1,0:T(8,128)(2,1)}), bf16[8,32,256]{2,1,0:T(8,128)(2,1)S(1)}, u32[]{:S(2)}, u32[]{:S(2)}) %all-to-all-start) | async-done | bytes 131104 | tf_op jit(solution)/shard_map/all_to_all | solution.py:468
  63.8 4.8 %step.4 = (f32[32,2048]{1,0:T(8,128)S(1)}, bf16[8,32,256]{2,1,0:T(8,128)(2,1)}) custom-call(s32[128]{0:T(128)S(1)} %get-tuple-element.19.plan_ref, s32[8]{0:T(128)S(1)} %get-tuple-element.21.picks_ref, f8e4m3fn[96,256,512]{2,1,0:T(32,128)(4,1)} %get-tuple-element.22.packed_hbm, f8e4m3fn[16,256,512]{2,1,0:T(32,128)(4,1)S(1)} %get-tuple-element.23.kept_ref, ...), custom_call_target="tpu_custom_call" | custom-call | tf_op jit(solution)/shard_map/step/pallas_call | solution.py:531
  68.6 3.5 %all-to-all-start.1 = ((bf16[8,32,256]{2,1,0:T(8,128)(2,1)}), bf16[8,32,256]{2,1,0:T(8,128)(2,1)S(1)}, u32[]{:S(2)}, u32[]{:S(2)}) async-start(bf16[8,32,256]{2,1,0:T(8,128)(2,1)} %get-tuple-element.26), calls=%async_computation.1 | async-start | bytes 262144 | tf_op jit(solution)/shard_map/all_to_all | solution.py:468
  72.1 2.5 %near.5.base_ref = f32[32,2048]{1,0:T(8,128)S(1)} custom-call(s32[128]{0:T(128)S(1)} %get-tuple-element.19.plan_ref, f8e4m3fn[96,256,512]{2,1,0:T(32,128)(4,1)} %get-tuple-element.22.packed_hbm, f32[8,2048]{1,0:T(8,128)S(1)} %get-tuple-element.20.scale_ref, f32[32,2048]{1,0:T(8,128)S(1)} %get-tuple-element.25.now_ref.before_ref, f32[32,2048]{1,0:T(8,128)S(1)} %copy-done), custom_call_target="tpu_custom_call" | custom-call | flops 268435456 | bytes 2097152 | tf_op jit(solution)/shard_map/near/pallas_call | solution.py:520
  74.7 3.2 %all-to-all-done.1.arrived_ref = bf16[8,32,256]{2,1,0:T(8,128)(2,1)S(1)} async-done(((bf16[8,32,256]{2,1,0:T(8,128)(2,1)}), bf16[8,32,256]{2,1,0:T(8,128)(2,1)S(1)}, u32[]{:S(2)}, u32[]{:S(2)}) %all-to-all-start.1) | async-done | bytes 131104 | tf_op jit(solution)/shard_map/all_to_all | solution.py:468
  77.8 4.8 %step.5 = (f32[32,2048]{1,0:T(8,128)S(1)}, bf16[8,32,256]{2,1,0:T(8,128)(2,1)}) custom-call(s32[128]{0:T(128)S(1)} %get-tuple-element.19.plan_ref, s32[8]{0:T(128)S(1)} %get-tuple-element.21.picks_ref, f8e4m3fn[96,256,512]{2,1,0:T(32,128)(4,1)} %get-tuple-element.22.packed_hbm, f8e4m3fn[16,256,512]{2,1,0:T(32,128)(4,1)S(1)} %get-tuple-element.23.kept_ref, ...), custom_call_target="tpu_custom_call" | custom-call | tf_op jit(solution)/shard_map/step/pallas_call | solution.py:531
  82.6 3.5 %all-to-all-start.2 = ((bf16[8,32,256]{2,1,0:T(8,128)(2,1)}), bf16[8,32,256]{2,1,0:T(8,128)(2,1)S(1)}, u32[]{:S(2)}, u32[]{:S(2)}) async-start(bf16[8,32,256]{2,1,0:T(8,128)(2,1)} %get-tuple-element.28), calls=%async_computation.2 | async-start | bytes 262144 | tf_op jit(solution)/shard_map/all_to_all | solution.py:468
  86.1 2.5 %near.6.base_ref = f32[32,2048]{1,0:T(8,128)S(1)} custom-call(s32[128]{0:T(128)S(1)} %get-tuple-element.19.plan_ref, f8e4m3fn[96,256,512]{2,1,0:T(32,128)(4,1)} %get-tuple-element.22.packed_hbm, f32[8,2048]{1,0:T(8,128)S(1)} %get-tuple-element.20.scale_ref, f32[32,2048]{1,0:T(8,128)S(1)} %get-tuple-element.27.now_ref.before_ref, ...), custom_call_target="tpu_custom_call" | custom-call | flops 268435456 | bytes 2097152 | tf_op jit(solution)/shard_map/near/pallas_call | solution.py:520
  88.7 3.2 %all-to-all-done.2.arrived_ref = bf16[8,32,256]{2,1,0:T(8,128)(2,1)S(1)} async-done(((bf16[8,32,256]{2,1,0:T(8,128)(2,1)}), bf16[8,32,256]{2,1,0:T(8,128)(2,1)S(1)}, u32[]{:S(2)}, u32[]{:S(2)}) %all-to-all-start.2) | async-done | bytes 131104 | tf_op jit(solution)/shard_map/all_to_all | solution.py:468
  91.8 4.8 %step.6 = (f32[32,2048]{1,0:T(8,128)S(1)}, bf16[8,32,256]{2,1,0:T(8,128)(2,1)}) custom-call(s32[128]{0:T(128)S(1)} %get-tuple-element.19.plan_ref, s32[8]{0:T(128)S(1)} %get-tuple-element.21.picks_ref, f8e4m3fn[96,256,512]{2,1,0:T(32,128)(4,1)} %get-tuple-element.22.packed_hbm, f8e4m3fn[16,256,512]{2,1,0:T(32,128)(4,1)S(1)} %get-tuple-element.23.kept_ref, ...), custom_call_target="tpu_custom_call" | custom-call | tf_op jit(solution)/shard_map/step/pallas_call | solution.py:531
  96.6 3.5 %all-to-all-start.3 = ((bf16[8,32,256]{2,1,0:T(8,128)(2,1)}), bf16[8,32,256]{2,1,0:T(8,128)(2,1)S(1)}, u32[]{:S(2)}, u32[]{:S(2)}) async-start(bf16[8,32,256]{2,1,0:T(8,128)(2,1)} %get-tuple-element.30), calls=%async_computation.3 | async-start | bytes 262144 | tf_op jit(solution)/shard_map/all_to_all | solution.py:468
  100.1 2.5 %near.7.base_ref = f32[32,2048]{1,0:T(8,128)S(1)} custom-call(s32[128]{0:T(128)S(1)} %get-tuple-element.19.plan_ref, f8e4m3fn[96,256,512]{2,1,0:T(32,128)(4,1)} %get-tuple-element.22.packed_hbm, f32[8,2048]{1,0:T(8,128)S(1)} %get-tuple-element.20.scale_ref, f32[32,2048]{1,0:T(8,128)S(1)} %get-tuple-element.29.now_ref, ...), custom_call_target="tpu_custom_call" | custom-call | flops 268435456 | bytes 2097152 | tf_op jit(solution)/shard_map/near/pallas_call | solution.py:520
  102.7 3.2 %all-to-all-done.3.arrived_ref = bf16[8,32,256]{2,1,0:T(8,128)(2,1)S(1)} async-done(((bf16[8,32,256]{2,1,0:T(8,128)(2,1)}), bf16[8,32,256]{2,1,0:T(8,128)(2,1)S(1)}, u32[]{:S(2)}, u32[]{:S(2)}) %all-to-all-start.3) | async-done | bytes 131104 | tf_op jit(solution)/shard_map/all_to_all | solution.py:468
  105.8 4.1 %step.7.own_ref = f32[32,2048]{1,0:T(8,128)S(1)} custom-call(s32[128]{0:T(128)S(1)} %get-tuple-element.19.plan_ref, s32[8]{0:T(128)S(1)} %get-tuple-element.21.picks_ref, f8e4m3fn[96,256,512]{2,1,0:T(32,128)(4,1)} %get-tuple-element.22.packed_hbm, f8e4m3fn[16,256,512]{2,1,0:T(32,128)(4,1)S(1)} %get-tuple-element.23.kept_ref, ...), custom_call_target="tpu_custom_call" | custom-call | tf_op jit(solution)/shard_map/step/pallas_call | solution.py:531
  111.6 3.5 %collective-permute-done.1.refs_1_ = bf16[32,2048]{1,0:T(8,128)(2,1)S(1)} collective-permute-done((bf16[32,2048]{1,0:T(8,128)(2,1)S(1)}, bf16[32,2048]{1,0:T(8,128)(2,1)S(1)}, u32[]{:S(2)}, u32[]{:S(2)}) %collective-permute-start.1) | collective-permute-done | bytes 131104 | tf_op jit(solution)/shard_map/ppermute | solution.py:473
  116.9 3.9 %collective-permute-done.3 = f32[64,128]{1,0:T(8,128)S(1)} collective-permute-done((f32[64,128]{1,0:T(8,128)S(1)}, f32[64,128]{1,0:T(8,128)S(1)}, u32[]{:S(2)}, u32[]{:S(2)}) %collective-permute-start.3) | collective-permute-done | bytes 32800 | tf_op jit(solution)/shard_map/ppermute | solution.py:473
  120.8 1.6 %collective-permute-start.6 = (f32[64,128]{1,0:T(8,128)S(1)}, f32[64,128]{1,0:T(8,128)S(1)}, u32[]{:S(2)}, u32[]{:S(2)}) collective-permute-start(f32[64,128]{1,0:T(8,128)S(1)} %add.5.refs_0_), channel_id=1, source_target_pairs={{0,24},{4,28},{8,16},{12,20},{16,8},{20,12},{24,0},{28,4},{1,25},{... | collective-permute-start | bytes 98312 | tf_op jit(solution)/shard_map/ppermute | solution.py:473
  122.4 2.7 %collective-permute-start.4 = (f32[64,128]{1,0:T(8,128)S(1)}, f32[64,128]{1,0:T(8,128)S(1)}, u32[]{:S(2)}, u32[]{:S(2)}) collective-permute-start(f32[64,128]{1,0:T(8,128)S(1)} %add.5.refs_0_), channel_id=1, source_target_pairs={{0,8},{4,12},{8,0},{12,4},{16,24},{20,28},{24,16},{28,20},{1,9},{5... | collective-permute-start | bytes 98312 | tf_op jit(solution)/shard_map/ppermute | solution.py:473
  127.4 6.2 %factor.1 = f32[32,2048]{1,0:T(8,128)} custom-call(f32[32,2048]{1,0:T(8,128)S(1)} %step.7.own_ref, bf16[4,32,2048]{2,1,0:T(8,128)(2,1)S(1)} %get-tuple-element.31.all_ref, f32[64,128]{1,0:T(8,128)S(1)} %add.5.refs_0_, f32[64,128]{1,0:T(8,128)S(1)} %collective-permute-done.4.refs_1_, f32[64,128]{1,0:T(8,128)S(1)} %collective-permute-done.5.refs_2_, ...), custom_call_target="tpu_custom_call" | custom-call | tf_op jit(solution)/shard_map/factor/pallas_call | solution.py:561
  (19 shorter events, 7.3 us)
Async XLA Ops:
  36.8 13.3 %copy-start = (f32[32,2048]{1,0:T(8,128)S(1)}, f32[32,2048]{1,0:T(8,128)}, u32[]{:S(2)}) copy-start(f32[32,2048]{1,0:T(8,128)} %before_ref.3) | copy-start | bytes 786436
  51.7 12.1 %all-to-all-start = ((bf16[8,32,256]{2,1,0:T(8,128)(2,1)}), bf16[8,32,256]{2,1,0:T(8,128)(2,1)S(1)}, u32[]{:S(2)}, u32[]{:S(2)}) async-start(bf16[8,32,256]{2,1,0:T(8,128)(2,1)} %get-tuple-element.24), calls=%async_computation | async-start | bytes 262144 | tf_op jit(solution)/shard_map/all_to_all | solution.py:468
  68.6 9.2 %all-to-all-start.1 = ((bf16[8,32,256]{2,1,0:T(8,128)(2,1)}), bf16[8,32,256]{2,1,0:T(8,128)(2,1)S(1)}, u32[]{:S(2)}, u32[]{:S(2)}) async-start(bf16[8,32,256]{2,1,0:T(8,128)(2,1)} %get-tuple-element.26), calls=%async_computation.1 | async-start | bytes 262144 | tf_op jit(solution)/shard_map/all_to_all | solution.py:468
  82.6 9.2 %all-to-all-start.2 = ((bf16[8,32,256]{2,1,0:T(8,128)(2,1)}), bf16[8,32,256]{2,1,0:T(8,128)(2,1)S(1)}, u32[]{:S(2)}, u32[]{:S(2)}) async-start(bf16[8,32,256]{2,1,0:T(8,128)(2,1)} %get-tuple-element.28), calls=%async_computation.2 | async-start | bytes 262144 | tf_op jit(solution)/shard_map/all_to_all | solution.py:468
  96.6 9.2 %all-to-all-start.3 = ((bf16[8,32,256]{2,1,0:T(8,128)(2,1)}), bf16[8,32,256]{2,1,0:T(8,128)(2,1)S(1)}, u32[]{:S(2)}, u32[]{:S(2)}) async-start(bf16[8,32,256]{2,1,0:T(8,128)(2,1)} %get-tuple-element.30), calls=%async_computation.3 | async-start | bytes 262144 | tf_op jit(solution)/shard_map/all_to_all | solution.py:468
  110.0 5.0 %collective-permute-start.1 = (bf16[32,2048]{1,0:T(8,128)(2,1)S(1)}, bf16[32,2048]{1,0:T(8,128)(2,1)S(1)}, u32[]{:S(2)}, u32[]{:S(2)}) collective-permute-start(bf16[32,2048]{1,0:T(8,128)(2,1)S(1)} %convert_element_type.9), channel_id=1, source_target_pairs={{0,2},{1,3},{2,0},{3,1},{4,6},{5,7},{6,4},{7,5},{8,10},{9,11},{10,... | collective-permute-start | bytes 393224 | tf_op jit(solution)/shard_map/ppermute | solution.py:473
  111.6 3.5 %collective-permute-start = (bf16[32,2048]{1,0:T(8,128)(2,1)S(1)}, bf16[32,2048]{1,0:T(8,128)(2,1)S(1)}, u32[]{:S(2)}, u32[]{:S(2)}) collective-permute-start(bf16[32,2048]{1,0:T(8,128)(2,1)S(1)} %convert_element_type.9), channel_id=1, source_target_pairs={{0,1},{1,0},{2,3},{3,2},{4,5},{5,4},{6,7},{7,6},{8,9},{9,8},{10,11... | collective-permute-start | bytes 393224 | tf_op jit(solution)/shard_map/ppermute | solution.py:473
  115.0 1.3 %collective-permute-start.2 = (bf16[32,2048]{1,0:T(8,128)(2,1)S(1)}, bf16[32,2048]{1,0:T(8,128)(2,1)S(1)}, u32[]{:S(2)}, u32[]{:S(2)}) collective-permute-start(bf16[32,2048]{1,0:T(8,128)(2,1)S(1)} %collective-permute-done.1.refs_1_), channel_id=1, source_target_pairs={{0,1},{1,0},{2,3},{3,2},{4,5},{5,4},{6,7},{7,6},{8,9},{9,8},{10,11... | collective-permute-start | bytes 393224 | tf_op jit(solution)/shard_map/ppermute | solution.py:473
  116.8 4.0 %collective-permute-start.3 = (f32[64,128]{1,0:T(8,128)S(1)}, f32[64,128]{1,0:T(8,128)S(1)}, u32[]{:S(2)}, u32[]{:S(2)}) collective-permute-start(f32[64,128]{1,0:T(8,128)S(1)} %get-tuple-element.32), channel_id=1, source_target_pairs={{0,4},{4,0},{8,12},{12,8},{16,20},{20,16},{24,28},{28,24},{1,5},{5... | collective-permute-start | bytes 98312 | tf_op jit(solution)/shard_map/ppermute | solution.py:473
  120.8 5.7 %collective-permute-start.6 = (f32[64,128]{1,0:T(8,128)S(1)}, f32[64,128]{1,0:T(8,128)S(1)}, u32[]{:S(2)}, u32[]{:S(2)}) collective-permute-start(f32[64,128]{1,0:T(8,128)S(1)} %add.5.refs_0_), channel_id=1, source_target_pairs={{0,24},{4,28},{8,16},{12,20},{16,8},{20,12},{24,0},{28,4},{1,25},{... | collective-permute-start | bytes 98312 | tf_op jit(solution)/shard_map/ppermute | solution.py:473
  122.4 4.9 %collective-permute-start.5 = (f32[64,128]{1,0:T(8,128)S(1)}, f32[64,128]{1,0:T(8,128)S(1)}, u32[]{:S(2)}, u32[]{:S(2)}) collective-permute-start(f32[64,128]{1,0:T(8,128)S(1)} %add.5.refs_0_), channel_id=1, source_target_pairs={{0,16},{4,20},{8,24},{12,28},{16,0},{20,4},{24,8},{28,12},{1,17},{... | collective-permute-start | bytes 98312 | tf_op jit(solution)/shard_map/ppermute | solution.py:473
  122.4 5.0 %collective-permute-start.4 = (f32[64,128]{1,0:T(8,128)S(1)}, f32[64,128]{1,0:T(8,128)S(1)}, u32[]{:S(2)}, u32[]{:S(2)}) collective-permute-start(f32[64,128]{1,0:T(8,128)S(1)} %add.5.refs_0_), channel_id=1, source_target_pairs={{0,8},{4,12},{8,0},{12,4},{16,24},{20,28},{24,16},{28,20},{1,9},{5... | collective-permute-start | bytes 98312 | tf_op jit(solution)/shard_map/ppermute | solution.py:473

commit v9 on v8

--- a/solution.py
+++ b/solution.py
@@ -10,7 +10,6 @@
 
 LOC_RB = 2
 STEPS = 4
-WIDE = 8
 UNROLL = 4
 KEPT = 16
 CHUNK = 4
@@ -64,13 +63,16 @@
 
 def tiles_kernel(
     near_count,
-    rows_ref,
-    slots_ref,
+    rows_hbm,
+    slots_hbm,
     real_hbm,
     imag_hbm,
     packed_hbm,
     kept_ref,
     scale_ref,
+    plan_hbm,
+    rows_ref,
+    slots_ref,
     plan_ref,
     both_ref,
     small_ref,
@@ -80,6 +82,7 @@
     done_ref,
     in_sems,
     out_sems,
+    list_sems,
 ):
     kept = kept_ref.shape[0]
     tiles, order, _ = both_ref.shape
@@ -97,6 +100,12 @@
     def leave(e):
         return pltpu.make_async_copy(small_ref.at[e], packed_hbm.at[e], out_sems.at[e])
 
+    lists = (
+        pltpu.make_async_copy(rows_hbm, rows_ref, list_sems.at[0]),
+        pltpu.make_async_copy(slots_hbm, slots_ref, list_sems.at[1]),
+    )
+    for copy in lists:
+        copy.start()
     for c in range(chunks):
         for copy in copies(c):
             copy.start()
@@ -107,6 +116,8 @@
 
     lax.fori_loop(0, rb_dev * slots, clear, 0)
     present_ref[...] = jnp.zeros_like(present_ref)
+    for copy in lists:
+        copy.wait()
 
     def link(t, carry):
         key = rows_ref[t] * slots + slots_ref[t]
@@ -179,6 +190,8 @@
     every = pad(skip, lax.fori_loop(near_count // CHUNK, chunks, functools.partial(chunk, skip), near))
     plan_ref[tiles] = near // UNROLL
     plan_ref[tiles + 1] = every // UNROLL
+    plan_copy = pltpu.make_async_copy(plan_ref, plan_hbm, list_sems.at[2])
+    plan_copy.start()
 
     ones = jnp.ones((8, order), BF16)
     for r in range(rb_dev):
@@ -191,6 +204,7 @@
 
     lax.fori_loop(0, near, left, 0)
     lax.fori_loop(skip, every, left, 0)
+    plan_copy.wait()
 
 
 def in_hbm(x):
@@ -207,11 +221,14 @@
             pltpu.HBM((tiles, order, 2 * order), F8),
             pltpu.VMEM((KEPT, order, 2 * order), F8),
             sds((8, rb_dev * order), F32),
-            sds((tiles + 32,), I32),
+            pltpu.HBM((tiles + 32,), I32),
         ),
-        in_specs=[SMEM, SMEM, ANY, ANY],
-        out_specs=(ANY, VMEM, VMEM, SMEM),
+        in_specs=[ANY] * 4,
+        out_specs=(ANY, VMEM, VMEM, ANY),
         scratch_shapes=[
+            pltpu.SMEM((tiles,), I32),
+            pltpu.SMEM((tiles,), I32),
+            pltpu.SMEM((tiles + 32,), I32),
             pltpu.VMEM((tiles, order, 2 * order), BF16),
             pltpu.VMEM((tiles, order, 2 * order), F8),
             pltpu.VMEM((rb_dev, order, order), BF16),
@@ -220,6 +237,7 @@
             pltpu.SMEM((tiles,), I32),
             pltpu.SemaphoreType.DMA((tiles // CHUNK, 2)),
             pltpu.SemaphoreType.DMA((tiles,)),
+            pltpu.SemaphoreType.DMA((3,)),
         ],
         compiler_params=params(48),
         cost_estimate=pl.CostEstimate(flops=1 << 28, bytes_accessed=2 * real.size * 2, transcendentals=0),
@@ -231,24 +249,19 @@
     return (field[:, at] * scale_ref[0:1, at]).astype(BF16)
 
 
-def send_picked(picks_ref, sent_ref, out_ref):
+def send_picked(wanted_ref, sent_ref, out_ref):
+    me = lax.axis_index("blk")
     for i in range(out_ref.shape[0]):
-        out_ref[i] = sent_ref[picks_ref[i]]
-
-
-def first_kernel(y_ref, scale_ref, wanted_hbm, out_ref, picks_ref, sent_ref, wanted_ref, sem):
-    nblk, rows, lanes = wanted_ref.shape
-    copy = pltpu.make_async_copy(wanted_hbm.at[:, 0:rows, 0:lanes], wanted_ref, sem)
+        out_ref[i] = sent_ref[wanted_ref[i, 0, me]]
+
+
+def first_kernel(y_ref, scale_ref, wanted_hbm, out_ref, sent_ref, wanted_ref, sem):
+    copy = pltpu.make_async_copy(wanted_hbm, wanted_ref, sem)
     copy.start()
     for r in range(sent_ref.shape[0]):
         sent_ref[r] = rounded_block(y_ref, scale_ref, r, sent_ref.shape[2])
     copy.wait()
-    mine = lax.broadcasted_iota(I32, (rows, lanes), 1) == lax.axis_index("blk")
-    top = lax.broadcasted_iota(I32, (rows, lanes), 0) == 0
-    for i in range(nblk):
-        pick = jnp.sum(jnp.where(mine & top, wanted_ref[i ^ central(nblk)], 0.0))
-        picks_ref[i] = pick.astype(I32)
-    send_picked(picks_ref, sent_ref, out_ref)
+    send_picked(wanted_ref, sent_ref, out_ref)
 
 
 def load_groups(packed_hbm, tiles_ref, sems, lo, hi):
@@ -318,12 +331,17 @@
     return (acc[:group] + acc[group:] * (1.0 / FINER)) * size
 
 
-def near_kernel(step, plan_ref, packed_hbm, scale_ref, now_ref, before_ref, base_ref, tiles_ref, x_ref, acc_ref, sems):
+def near_kernel(
+    step, plan_hbm, packed_hbm, scale_ref, now_ref, before_ref, base_ref, tiles_ref, x_ref, acc_ref, sems, plan_ref, plan_sem
+):
+    plan_copy = pltpu.make_async_copy(plan_hbm, plan_ref, plan_sem)
+    plan_copy.start()
     rb_dev, _, order = acc_ref.shape
+    acc_ref[...] = jnp.zeros_like(acc_ref)
+    plan_copy.wait()
     end = plan_ref.shape[0] - 32
     hi = plan_ref[end]
     copy = load_groups(packed_hbm, tiles_ref, sems, 0, hi)
-    acc_ref[...] = jnp.zeros_like(acc_ref)
     size = split_sources(rb_dev, lambda r: rounded_block(now_ref, scale_ref, r, order), x_ref)
     multiply(plan_ref, 0, hi, loaded(copy, tiles_ref, 0), lambda c: x_ref[jnp.minimum(c, rb_dev)], acc_ref)
     for r in range(rb_dev):
@@ -333,16 +351,23 @@
         base_ref[:, at] = moved if step == 0 else 2.0 * moved - before_ref[:, at]
 
 
-def step_kernel(step, plan_ref, picks_ref, packed_hbm, kept_ref, scale_ref, base_ref, arrived_ref, *refs):
+def step_kernel(step, plan_hbm, wanted_hbm, packed_hbm, kept_ref, scale_ref, base_ref, arrived_ref, *refs):
     last = step == STEPS - 1
     next_ref = refs[0]
-    tiles_ref, x_ref, acc_ref, sems = refs[-4:]
+    tiles_ref, x_ref, acc_ref, sems, plan_ref, plan_sem = refs[-6:]
+    plan_copy = pltpu.make_async_copy(plan_hbm, plan_ref, plan_sem)
+    plan_copy.start()
+    if not last:
+        out_ref, sent_ref, wanted_ref, wanted_sem = refs[1:5]
+        wanted_copy = pltpu.make_async_copy(wanted_hbm, wanted_ref, wanted_sem)
+        wanted_copy.start()
     rb_dev, _, order = acc_ref.shape
+    acc_ref[...] = jnp.zeros_like(acc_ref)
+    plan_copy.wait()
     end = plan_ref.shape[0] - 32
     lo, hi = plan_ref[end], plan_ref[end + 1]
     stay = jnp.minimum(lo + KEPT // UNROLL, hi)
     copy = load_groups(packed_hbm, tiles_ref, sems, stay, hi)
-    acc_ref[...] = jnp.zeros_like(acc_ref)
     size = split_sources(arrived_ref.shape[0], lambda p: arrived_ref[p], x_ref)
     size = size * ((1.0 if step == 0 else 2.0) / half_width)
     multiply(
@@ -355,9 +380,10 @@
         following = base_ref[:, at] - scale * collect(acc_ref[r], size)
         next_ref[:, at] = following
         if not last:
-            refs[2][r] = (following * scale).astype(BF16)
+            sent_ref[r] = (following * scale).astype(BF16)
     if not last:
-        send_picked(picks_ref, refs[2], refs[1])
+        wanted_copy.wait()
+        send_picked(wanted_ref, sent_ref, out_ref)
 
 
 def all_rows(own_ref, arrived, all_ref):
@@ -380,12 +406,6 @@
 
 
 PANEL = 32
-
-
-def finer_reciprocal(x):
-    guess = pl.reciprocal(x, approx=True)
-    guess = guess * (2.0 - x * guess)
-    return guess * (2.0 - x * guess)
 
 
 def factor_kernel(nodes, own_ref, all_ref, *refs):
@@ -410,9 +430,9 @@
             w = [jnp.broadcast_to(a[:, i : i + 1], a.shape) for i in range(top + k, top + k + 4)]
             p, q = w[0][k : k + 1, :], w[2][k + 2 : k + 3, :]
             u, v = w[2][k : k + 1, :], w[3][k : k + 1, :]
-            single = finer_reciprocal(p)
+            single = 1.0 / p
             det = p * q - (u * u + v * v)
-            both = finer_reciprocal(det)
+            both = 1.0 / det
             second = (here == k + 2) | (here == k + 3)
             below = here > k + 3
             coefficients = (
@@ -488,20 +508,19 @@
     nblk = lax.axis_size("blk")
     ncol = lax.axis_size("col")
     near_count = LOC_RB * rb_dev
-    picked = jnp.pad(fetch_pick.astype(F32), ((0, 0), (0, rows - nblk)))
-    top = lax.broadcasted_iota(I32, (WIDE, rows), 0) == 0
-    wanted = lax.all_gather(jnp.where(top, picked, y_start[:WIDE]), "blk", axis=0, tiled=False)
+    wanted = exchange(jnp.broadcast_to(fetch_pick[None], (nblk, 1, nblk)))
     packed, kept, scale, plan = tiles_call(tile_rows, tile_slots, tile_real, tile_imag, rb_dev, near_count)
 
     out_blocks = sds((nblk, group, order), BF16)
     sent_scratch = pltpu.VMEM((rb_dev, group, order), BF16)
-    blocks, picks = pl.pallas_call(
+    wanted_scratch = pltpu.SMEM(wanted.shape, I32)
+    blocks = pl.pallas_call(
         first_kernel,
         name="first",
-        out_shape=(out_blocks, sds((nblk,), I32)),
+        out_shape=out_blocks,
         in_specs=[VMEM, VMEM, ANY],
-        out_specs=(VMEM, SMEM),
-        scratch_shapes=[sent_scratch, pltpu.VMEM((nblk, 8, 128), F32), pltpu.SemaphoreType.DMA],
+        out_specs=VMEM,
+        scratch_shapes=[sent_scratch, wanted_scratch, pltpu.SemaphoreType.DMA],
         compiler_params=params(LIMIT),
     )(y_start, scale, in_hbm(wanted))
 
@@ -511,6 +530,8 @@
             pltpu.VMEM((sources + 1, 2 * group, 2 * order), F8),
             pltpu.VMEM((rb_dev, 2 * group, order), F32),
             pltpu.SemaphoreType.DMA((entries // UNROLL,)),
+            pltpu.SMEM(plan.shape, I32),
+            pltpu.SemaphoreType.DMA,
         ]
 
     vectors_here = sds((group, rows), F32)
@@ -521,22 +542,23 @@
             functools.partial(near_kernel, step),
             name="near",
             out_shape=vectors_here,
-            in_specs=[SMEM, ANY] + [VMEM] * 3,
+            in_specs=[ANY, ANY] + [VMEM] * 3,
             out_specs=VMEM,
             scratch_shapes=scratch(near_count, rb_dev),
             compiler_params=params(LIMIT),
             cost_estimate=pl.CostEstimate(flops=1 << 28, bytes_accessed=1 << 21, transcendentals=0),
-        )(plan, in_hbm(packed), scale, current, previous)
+        )(in_hbm(plan), in_hbm(packed), scale, current, previous)
         last = step == STEPS - 1
         out = pl.pallas_call(
             functools.partial(step_kernel, step),
             name="step",
             out_shape=[vectors_here] if last else [vectors_here, out_blocks],
-            in_specs=[SMEM, SMEM, ANY] + [VMEM] * 4,
+            in_specs=[ANY] * 3 + [VMEM] * 4,
             out_specs=[VMEM] if last else [VMEM, VMEM],
-            scratch_shapes=([] if last else [sent_scratch]) + scratch(tiles - near_count - KEPT, nblk),
+            scratch_shapes=([] if last else [sent_scratch, wanted_scratch, pltpu.SemaphoreType.DMA])
+            + scratch(tiles - near_count - KEPT, nblk),
             compiler_params=params(LIMIT),
-        )(plan, picks, in_hbm(packed), pltpu.with_memory_space_constraint(kept, pltpu.VMEM), scale, base, arrived)
+        )(in_hbm(plan), in_hbm(wanted), in_hbm(packed), pltpu.with_memory_space_constraint(kept, pltpu.VMEM), scale, base, arrived)
         previous, current = current, out[0]
         if not last:
             blocks = out[1]

time: 134 us -> 106 us (0.79)
  blocking collectives: 35.2 us -> 0 us
  starting transfers between devices: 22.9 us -> 29.2 us
  Pallas kernels: 50.2 us -> 52.2 us
  waiting for transfers between devices: 23.6 us -> 21.7 us
  local copies, waits for them, and re-layouts: 0.01 us -> 1.83 us
  other arithmetic: 1.6 us -> 0.02 us
    all_gather x1 -> x0, blocking collectives: 35.2 us -> none  [per_device(): lax.all_gather(jnp.where(top, picked, y_start[:WIDE]), 'blk', axis=0, til...]
    all_to_all x4 -> x5, starting transfers between devices: 16.9 us -> 23 us  [exchange(): lax.all_to_all(x, 'blk', split_axis=0, concat_axis=0, tiled=True, axis_in...]
    all_to_all x4 -> x5, waiting for transfers between devices: 12.7 us -> 11 us  [exchange(): lax.all_to_all(x, 'blk', split_axis=0, concat_axis=0, tiled=True, axis_in...]
    pallas_call x4, Pallas kernels: 18.5 us -> 20.2 us  [per_device(): pl.pallas_call(functools.partial(step_kernel, step), name='step', out_sha...]
    pallas_call x4, Pallas kernels: 10.1 us -> 11.7 us  [per_device(): pl.pallas_call(functools.partial(near_kernel, step), name='near', out_sha...]
  transfers between devices with their start and end apart: 11 -> 12, of which waited for: 10 -> 10; matrix products, arithmetic and copies ran while one was open for 0% -> 0% of each run, Pallas kernels for 8% -> 23%
where the time goes in v9:
time: 106 us; the launch traced here: 105 us
  Pallas kernels  52.2 us (49%)
  starting transfers between devices  29.2 us (28%)
  waiting for transfers between devices  21.7 us (20%)
  local copies, waits for them, and re-layouts  1.83 us (2%)
    all_to_all x5, starting transfers between devices, exchange(): lax.all_to_all(x, 'blk', split_axis=0, concat_axis=0, tiled=True, axis_in...  23 us
    pallas_call x4, Pallas kernels, per_device(): pl.pallas_call(functools.partial(step_kernel, step), name='step', out_sha...  20.2 us
    pallas_call x1, Pallas kernels, tiles_call(): pl.pallas_call(functools.partial(tiles_kernel, near_count), name='tiles',...  12.1 us
    pallas_call x4, Pallas kernels, per_device(): pl.pallas_call(functools.partial(near_kernel, step), name='near', out_sha...  11.7 us
    all_to_all x5, waiting for transfers between devices, exchange(): lax.all_to_all(x, 'blk', split_axis=0, concat_axis=0, tiled=True, axis_in...  11 us
    ppermute x7, waiting for transfers between devices, to_partner(): return lax.ppermute(x, axis, [(i, i ^ mask) for i in range(n)])  10.8 us
    pallas_call x1, Pallas kernels, per_device(): pl.pallas_call(functools.partial(factor_kernel, rows * nblk), name='facto...  6.24 us
    ppermute x7, starting transfers between devices, to_partner(): return lax.ppermute(x, axis, [(i, i ^ mask) for i in range(n)])  6.23 us
  transfers between devices with their start and end apart: 12, of which 10 were waited for; matrix products, arithmetic and copies ran while one was open for 0% of the time, Pallas kernels for 23%

profile of v9, /device:TPU:0, one launch (start us, length us, event | category | flops | bytes accessed | tf_op | source)
XLA Modules:
  0.0 105.1 jit_solution(3669061985477901343)
XLA Ops:
  1.2 7.8 %all-to-all-start = ((s32[8,1,8]{2,1,0:T(1,128)}), s32[8,1,8]{2,1,0:T(1,128)S(1)}, u32[]{:S(2)}, u32[]{:S(2)}) async-start(s32[8,1,8]{2,1,0:T(1,128)} %broadcast_in_dim.9), calls=%async_computation | async-start | bytes 8192 | tf_op jit(solution)/shard_map/all_to_all | solution.py:488
  9.1 12.1 %tiles.1 = (f8e4m3fn[96,256,512]{2,1,0:T(32,128)(4,1)}, f8e4m3fn[16,256,512]{2,1,0:T(32,128)(4,1)S(1)}, f32[8,2048]{1,0:T(8,128)S(1)}, s32[128]{0:T(128)}) custom-call(s32[96]{0:T(128)} %rows_hbm.1, s32[96]{0:T(128)} %slots_hbm.1, bf16[96,256,256]{2,1,0:T(8,128)(2,1)} %real_hbm.1, bf16[96,256,256]{2,1,0:T(8,128)(2,1)} %imag_hbm.1), custom_call_target="tpu_custom_call" | custom-call | flops 268435456 | bytes 25165824 | tf_op jit(solution)/shard_map/tiles/pallas_call | solution.py:217
  21.8 1.4 %first.1 = bf16[8,32,256]{2,1,0:T(8,128)(2,1)} custom-call(f32[32,2048]{1,0:T(8,128)S(1)} %copy-done, f32[8,2048]{1,0:T(8,128)S(1)} %get-tuple-element.20.scale_ref, s32[8,1,8]{2,1,0:T(1,128)} %copy-done.1), custom_call_target="tpu_custom_call" | custom-call | tf_op jit(solution)/shard_map/first/pallas_call | solution.py:517
  23.3 5.2 %all-to-all-start.1 = ((bf16[8,32,256]{2,1,0:T(8,128)(2,1)}), bf16[8,32,256]{2,1,0:T(8,128)(2,1)S(1)}, u32[]{:S(2)}, u32[]{:S(2)}) async-start(bf16[8,32,256]{2,1,0:T(8,128)(2,1)} %first.1), calls=%async_computation.1 | async-start | bytes 262144 | tf_op jit(solution)/shard_map/all_to_all | solution.py:488
  28.4 2.9 %near.4.base_ref = f32[32,2048]{1,0:T(8,128)S(1)} custom-call(s32[128]{0:T(128)} %get-tuple-element.17.plan_hbm, f8e4m3fn[96,256,512]{2,1,0:T(32,128)(4,1)} %get-tuple-element.18.packed_hbm, f32[8,2048]{1,0:T(8,128)S(1)} %get-tuple-element.20.scale_ref, f32[32,2048]{1,0:T(8,128)S(1)} %copy-done, f32[32,2048]{1,0:T(8,128)S(1)} %copy-done), custom_call_target="tpu_custom_call" | custom-call | flops 268435456 | bytes 2097152 | tf_op jit(solution)/shard_map/near/pallas_call | solution.py:541
  31.3 2.8 %all-to-all-done.1.arrived_ref = bf16[8,32,256]{2,1,0:T(8,128)(2,1)S(1)} async-done(((bf16[8,32,256]{2,1,0:T(8,128)(2,1)}), bf16[8,32,256]{2,1,0:T(8,128)(2,1)S(1)}, u32[]{:S(2)}, u32[]{:S(2)}) %all-to-all-start.1) | async-done | bytes 131104 | tf_op jit(solution)/shard_map/all_to_all | solution.py:488
  34.1 5.2 %step.4 = (f32[32,2048]{1,0:T(8,128)S(1)}, bf16[8,32,256]{2,1,0:T(8,128)(2,1)}) custom-call(s32[128]{0:T(128)} %get-tuple-element.17.plan_hbm, s32[8,1,8]{2,1,0:T(1,128)} %copy-done.1, f8e4m3fn[96,256,512]{2,1,0:T(32,128)(4,1)} %get-tuple-element.18.packed_hbm, f8e4m3fn[16,256,512]{2,1,0:T(32,128)(4,1)S(1)} %get-tuple-element.19.kept_ref, ...), custom_call_target="tpu_custom_call" | custom-call | tf_op jit(solution)/shard_map/step/pallas_call | solution.py:552
  39.4 3.3 %all-to-all-start.2 = ((bf16[8,32,256]{2,1,0:T(8,128)(2,1)}), bf16[8,32,256]{2,1,0:T(8,128)(2,1)S(1)}, u32[]{:S(2)}, u32[]{:S(2)}) async-start(bf16[8,32,256]{2,1,0:T(8,128)(2,1)} %get-tuple-element.22), calls=%async_computation.2 | async-start | bytes 262144 | tf_op jit(solution)/shard_map/all_to_all | solution.py:488
  42.7 2.9 %near.5.base_ref = f32[32,2048]{1,0:T(8,128)S(1)} custom-call(s32[128]{0:T(128)} %get-tuple-element.17.plan_hbm, f8e4m3fn[96,256,512]{2,1,0:T(32,128)(4,1)} %get-tuple-element.18.packed_hbm, f32[8,2048]{1,0:T(8,128)S(1)} %get-tuple-element.20.scale_ref, f32[32,2048]{1,0:T(8,128)S(1)} %get-tuple-element.21.now_ref.before_ref, f32[32,2048]{1,0:T(8,128)S(1)} %copy-done), custom_call_target="tpu_custom_call" | custom-call | flops 268435456 | bytes 2097152 | tf_op jit(solution)/shard_map/near/pallas_call | solution.py:541
  45.7 2.7 %all-to-all-done.2.arrived_ref = bf16[8,32,256]{2,1,0:T(8,128)(2,1)S(1)} async-done(((bf16[8,32,256]{2,1,0:T(8,128)(2,1)}), bf16[8,32,256]{2,1,0:T(8,128)(2,1)S(1)}, u32[]{:S(2)}, u32[]{:S(2)}) %all-to-all-start.2) | async-done | bytes 131104 | tf_op jit(solution)/shard_map/all_to_all | solution.py:488
  48.4 5.2 %step.5 = (f32[32,2048]{1,0:T(8,128)S(1)}, bf16[8,32,256]{2,1,0:T(8,128)(2,1)}) custom-call(s32[128]{0:T(128)} %get-tuple-element.17.plan_hbm, s32[8,1,8]{2,1,0:T(1,128)} %copy-done.1, f8e4m3fn[96,256,512]{2,1,0:T(32,128)(4,1)} %get-tuple-element.18.packed_hbm, f8e4m3fn[16,256,512]{2,1,0:T(32,128)(4,1)S(1)} %get-tuple-element.19.kept_ref, ...), custom_call_target="tpu_custom_call" | custom-call | tf_op jit(solution)/shard_map/step/pallas_call | solution.py:552
  53.6 3.3 %all-to-all-start.3 = ((bf16[8,32,256]{2,1,0:T(8,128)(2,1)}), bf16[8,32,256]{2,1,0:T(8,128)(2,1)S(1)}, u32[]{:S(2)}, u32[]{:S(2)}) async-start(bf16[8,32,256]{2,1,0:T(8,128)(2,1)} %get-tuple-element.24), calls=%async_computation.3 | async-start | bytes 262144 | tf_op jit(solution)/shard_map/all_to_all | solution.py:488
  57.0 2.9 %near.6.base_ref = f32[32,2048]{1,0:T(8,128)S(1)} custom-call(s32[128]{0:T(128)} %get-tuple-element.17.plan_hbm, f8e4m3fn[96,256,512]{2,1,0:T(32,128)(4,1)} %get-tuple-element.18.packed_hbm, f32[8,2048]{1,0:T(8,128)S(1)} %get-tuple-element.20.scale_ref, f32[32,2048]{1,0:T(8,128)S(1)} %get-tuple-element.23.now_ref.before_ref, ...), custom_call_target="tpu_custom_call" | custom-call | flops 268435456 | bytes 2097152 | tf_op jit(solution)/shard_map/near/pallas_call | solution.py:541
  59.9 2.7 %all-to-all-done.3.arrived_ref = bf16[8,32,256]{2,1,0:T(8,128)(2,1)S(1)} async-done(((bf16[8,32,256]{2,1,0:T(8,128)(2,1)}), bf16[8,32,256]{2,1,0:T(8,128)(2,1)S(1)}, u32[]{:S(2)}, u32[]{:S(2)}) %all-to-all-start.3) | async-done | bytes 131104 | tf_op jit(solution)/shard_map/all_to_all | solution.py:488
  62.6 5.2 %step.6 = (f32[32,2048]{1,0:T(8,128)S(1)}, bf16[8,32,256]{2,1,0:T(8,128)(2,1)}) custom-call(s32[128]{0:T(128)} %get-tuple-element.17.plan_hbm, s32[8,1,8]{2,1,0:T(1,128)} %copy-done.1, f8e4m3fn[96,256,512]{2,1,0:T(32,128)(4,1)} %get-tuple-element.18.packed_hbm, f8e4m3fn[16,256,512]{2,1,0:T(32,128)(4,1)S(1)} %get-tuple-element.19.kept_ref, ...), custom_call_target="tpu_custom_call" | custom-call | tf_op jit(solution)/shard_map/step/pallas_call | solution.py:552
  67.9 3.3 %all-to-all-start.4 = ((bf16[8,32,256]{2,1,0:T(8,128)(2,1)}), bf16[8,32,256]{2,1,0:T(8,128)(2,1)S(1)}, u32[]{:S(2)}, u32[]{:S(2)}) async-start(bf16[8,32,256]{2,1,0:T(8,128)(2,1)} %get-tuple-element.26), calls=%async_computation.4 | async-start | bytes 262144 | tf_op jit(solution)/shard_map/all_to_all | solution.py:488
  71.2 2.9 %near.7.base_ref = f32[32,2048]{1,0:T(8,128)S(1)} custom-call(s32[128]{0:T(128)} %get-tuple-element.17.plan_hbm, f8e4m3fn[96,256,512]{2,1,0:T(32,128)(4,1)} %get-tuple-element.18.packed_hbm, f32[8,2048]{1,0:T(8,128)S(1)} %get-tuple-element.20.scale_ref, f32[32,2048]{1,0:T(8,128)S(1)} %get-tuple-element.25.now_ref, ...), custom_call_target="tpu_custom_call" | custom-call | flops 268435456 | bytes 2097152 | tf_op jit(solution)/shard_map/near/pallas_call | solution.py:541
  74.2 2.7 %all-to-all-done.4.arrived_ref = bf16[8,32,256]{2,1,0:T(8,128)(2,1)S(1)} async-done(((bf16[8,32,256]{2,1,0:T(8,128)(2,1)}), bf16[8,32,256]{2,1,0:T(8,128)(2,1)S(1)}, u32[]{:S(2)}, u32[]{:S(2)}) %all-to-all-start.4) | async-done | bytes 131104 | tf_op jit(solution)/shard_map/all_to_all | solution.py:488
  76.9 4.5 %step.7.own_ref = f32[32,2048]{1,0:T(8,128)S(1)} custom-call(s32[128]{0:T(128)} %get-tuple-element.17.plan_hbm, s32[8,1,8]{2,1,0:T(1,128)} %copy-done.1, f8e4m3fn[96,256,512]{2,1,0:T(32,128)(4,1)} %get-tuple-element.18.packed_hbm, f8e4m3fn[16,256,512]{2,1,0:T(32,128)(4,1)S(1)} %get-tuple-element.19.kept_ref, f32[8,2048]{1,0:T(8,128)S(1)} %get-tuple-element.20.scale_ref, ...), custom_call_target="tpu_custom_call" | custom-call | tf_op jit(solution)/shard_map/step/pallas_call | solution.py:552
  81.5 1.6 %collective-permute-start.1 = (bf16[32,2048]{1,0:T(8,128)(2,1)S(1)}, bf16[32,2048]{1,0:T(8,128)(2,1)S(1)}, u32[]{:S(2)}, u32[]{:S(2)}) collective-permute-start(bf16[32,2048]{1,0:T(8,128)(2,1)S(1)} %convert_element_type.3), channel_id=1, source_target_pairs={{0,2},{1,3},{2,0},{3,1},{4,6},{5,7},{6,4},{7,5},{8,10},{9,11},{10,... | collective-permute-start | bytes 393224 | tf_op jit(solution)/shard_map/ppermute | solution.py:493
  83.0 3.5 %collective-permute-done.1.refs_1_ = bf16[32,2048]{1,0:T(8,128)(2,1)S(1)} collective-permute-done((bf16[32,2048]{1,0:T(8,128)(2,1)S(1)}, bf16[32,2048]{1,0:T(8,128)(2,1)S(1)}, u32[]{:S(2)}, u32[]{:S(2)}) %collective-permute-start.1) | collective-permute-done | bytes 131104 | tf_op jit(solution)/shard_map/ppermute | solution.py:493
  88.6 3.7 %collective-permute-done.3 = f32[64,128]{1,0:T(8,128)S(1)} collective-permute-done((f32[64,128]{1,0:T(8,128)S(1)}, f32[64,128]{1,0:T(8,128)S(1)}, u32[]{:S(2)}, u32[]{:S(2)}) %collective-permute-start.3) | collective-permute-done | bytes 32800 | tf_op jit(solution)/shard_map/ppermute | solution.py:493
  93.6 3.0 %collective-permute-start.4 = (f32[64,128]{1,0:T(8,128)S(1)}, f32[64,128]{1,0:T(8,128)S(1)}, u32[]{:S(2)}, u32[]{:S(2)}) collective-permute-start(f32[64,128]{1,0:T(8,128)S(1)} %add.3.refs_0_), channel_id=1, source_target_pairs={{0,8},{4,12},{8,0},{12,4},{16,24},{20,28},{24,16},{28,20},{1,9},{5... | collective-permute-start | bytes 98312 | tf_op jit(solution)/shard_map/ppermute | solution.py:493
  98.9 6.2 %factor.1 = f32[32,2048]{1,0:T(8,128)} custom-call(f32[32,2048]{1,0:T(8,128)S(1)} %step.7.own_ref, bf16[4,32,2048]{2,1,0:T(8,128)(2,1)S(1)} %get-tuple-element.27.all_ref, f32[64,128]{1,0:T(8,128)S(1)} %add.3.refs_0_, f32[64,128]{1,0:T(8,128)S(1)} %collective-permute-done.4.refs_1_, f32[64,128]{1,0:T(8,128)S(1)} %collective-permute-done.5.refs_2_, ...), custom_call_target="tpu_custom_call" | custom-call | tf_op jit(solution)/shard_map/factor/pallas_call | solution.py:583
  (19 shorter events, 7.5 us)
Async XLA Ops:
  1.2 20.0 %all-to-all-start = ((s32[8,1,8]{2,1,0:T(1,128)}), s32[8,1,8]{2,1,0:T(1,128)S(1)}, u32[]{:S(2)}, u32[]{:S(2)}) async-start(s32[8,1,8]{2,1,0:T(1,128)} %broadcast_in_dim.9), calls=%async_computation | async-start | bytes 8192 | tf_op jit(solution)/shard_map/all_to_all | solution.py:488
  9.1 12.7 %copy-start = (f32[32,2048]{1,0:T(8,128)S(1)}, f32[32,2048]{1,0:T(8,128)}, u32[]{:S(2)}) copy-start(f32[32,2048]{1,0:T(8,128)} %before_ref.3) | copy-start | bytes 786436
  21.2 0.6 copy-start.1
  23.3 10.9 %all-to-all-start.1 = ((bf16[8,32,256]{2,1,0:T(8,128)(2,1)}), bf16[8,32,256]{2,1,0:T(8,128)(2,1)S(1)}, u32[]{:S(2)}, u32[]{:S(2)}) async-start(bf16[8,32,256]{2,1,0:T(8,128)(2,1)} %first.1), calls=%async_computation.1 | async-start | bytes 262144 | tf_op jit(solution)/shard_map/all_to_all | solution.py:488
  39.4 9.0 %all-to-all-start.2 = ((bf16[8,32,256]{2,1,0:T(8,128)(2,1)}), bf16[8,32,256]{2,1,0:T(8,128)(2,1)S(1)}, u32[]{:S(2)}, u32[]{:S(2)}) async-start(bf16[8,32,256]{2,1,0:T(8,128)(2,1)} %get-tuple-element.22), calls=%async_computation.2 | async-start | bytes 262144 | tf_op jit(solution)/shard_map/all_to_all | solution.py:488
  53.6 9.0 %all-to-all-start.3 = ((bf16[8,32,256]{2,1,0:T(8,128)(2,1)}), bf16[8,32,256]{2,1,0:T(8,128)(2,1)S(1)}, u32[]{:S(2)}, u32[]{:S(2)}) async-start(bf16[8,32,256]{2,1,0:T(8,128)(2,1)} %get-tuple-element.24), calls=%async_computation.3 | async-start | bytes 262144 | tf_op jit(solution)/shard_map/all_to_all | solution.py:488
  67.9 9.0 %all-to-all-start.4 = ((bf16[8,32,256]{2,1,0:T(8,128)(2,1)}), bf16[8,32,256]{2,1,0:T(8,128)(2,1)S(1)}, u32[]{:S(2)}, u32[]{:S(2)}) async-start(bf16[8,32,256]{2,1,0:T(8,128)(2,1)} %get-tuple-element.26), calls=%async_computation.4 | async-start | bytes 262144 | tf_op jit(solution)/shard_map/all_to_all | solution.py:488
  81.5 5.0 %collective-permute-start.1 = (bf16[32,2048]{1,0:T(8,128)(2,1)S(1)}, bf16[32,2048]{1,0:T(8,128)(2,1)S(1)}, u32[]{:S(2)}, u32[]{:S(2)}) collective-permute-start(bf16[32,2048]{1,0:T(8,128)(2,1)S(1)} %convert_element_type.3), channel_id=1, source_target_pairs={{0,2},{1,3},{2,0},{3,1},{4,6},{5,7},{6,4},{7,5},{8,10},{9,11},{10,... | collective-permute-start | bytes 393224 | tf_op jit(solution)/shard_map/ppermute | solution.py:493
  83.0 3.5 %collective-permute-start = (bf16[32,2048]{1,0:T(8,128)(2,1)S(1)}, bf16[32,2048]{1,0:T(8,128)(2,1)S(1)}, u32[]{:S(2)}, u32[]{:S(2)}) collective-permute-start(bf16[32,2048]{1,0:T(8,128)(2,1)S(1)} %convert_element_type.3), channel_id=1, source_target_pairs={{0,1},{1,0},{2,3},{3,2},{4,5},{5,4},{6,7},{7,6},{8,9},{9,8},{10,11... | collective-permute-start | bytes 393224 | tf_op jit(solution)/shard_map/ppermute | solution.py:493
  86.5 1.3 %collective-permute-start.2 = (bf16[32,2048]{1,0:T(8,128)(2,1)S(1)}, bf16[32,2048]{1,0:T(8,128)(2,1)S(1)}, u32[]{:S(2)}, u32[]{:S(2)}) collective-permute-start(bf16[32,2048]{1,0:T(8,128)(2,1)S(1)} %collective-permute-done.1.refs_1_), channel_id=1, source_target_pairs={{0,1},{1,0},{2,3},{3,2},{4,5},{5,4},{6,7},{7,6},{8,9},{9,8},{10,11... | collective-permute-start | bytes 393224 | tf_op jit(solution)/shard_map/ppermute | solution.py:493
  88.3 4.0 %collective-permute-start.3 = (f32[64,128]{1,0:T(8,128)S(1)}, f32[64,128]{1,0:T(8,128)S(1)}, u32[]{:S(2)}, u32[]{:S(2)}) collective-permute-start(f32[64,128]{1,0:T(8,128)S(1)} %get-tuple-element.28), channel_id=1, source_target_pairs={{0,4},{4,0},{8,12},{12,8},{16,20},{20,16},{24,28},{28,24},{1,5},{5... | collective-permute-start | bytes 98312 | tf_op jit(solution)/shard_map/ppermute | solution.py:493
  92.3 5.7 %collective-permute-start.6 = (f32[64,128]{1,0:T(8,128)S(1)}, f32[64,128]{1,0:T(8,128)S(1)}, u32[]{:S(2)}, u32[]{:S(2)}) collective-permute-start(f32[64,128]{1,0:T(8,128)S(1)} %add.3.refs_0_), channel_id=1, source_target_pairs={{0,24},{4,28},{8,16},{12,20},{16,8},{20,12},{24,0},{28,4},{1,25},{... | collective-permute-start | bytes 98312 | tf_op jit(solution)/shard_map/ppermute | solution.py:493
  93.6 5.2 %collective-permute-start.5 = (f32[64,128]{1,0:T(8,128)S(1)}, f32[64,128]{1,0:T(8,128)S(1)}, u32[]{:S(2)}, u32[]{:S(2)}) collective-permute-start(f32[64,128]{1,0:T(8,128)S(1)} %add.3.refs_0_), channel_id=1, source_target_pairs={{0,16},{4,20},{8,24},{12,28},{16,0},{20,4},{24,8},{28,12},{1,17},{... | collective-permute-start | bytes 98312 | tf_op jit(solution)/shard_map/ppermute | solution.py:493
  93.6 5.3 %collective-permute-start.4 = (f32[64,128]{1,0:T(8,128)S(1)}, f32[64,128]{1,0:T(8,128)S(1)}, u32[]{:S(2)}, u32[]{:S(2)}) collective-permute-start(f32[64,128]{1,0:T(8,128)S(1)} %add.3.refs_0_), channel_id=1, source_target_pairs={{0,8},{4,12},{8,0},{12,4},{16,24},{20,28},{24,16},{28,20},{1,9},{5... | collective-permute-start | bytes 98312 | tf_op jit(solution)/shard_map/ppermute | solution.py:493

commit v10 on v9

--- a/solution.py
+++ b/solution.py
@@ -137,6 +137,9 @@
 
     lax.fori_loop(0, tiles, link, 0)
 
+    def turned(tile):
+        return jnp.concatenate([tile[:, :order].T, tile[:, order:].T], axis=0).astype(F8)
+
     def put(e, skip, value):
         @pl.when(e < skip)
         def _():
@@ -160,7 +163,7 @@
                 return back_ref[prior]
 
             lax.while_loop(lambda prior: prior >= 0, add, back_ref[t])
-            put(listed, skip, lambda: both_ref[t].astype(F8))
+            put(listed, skip, lambda: turned(both_ref[t]))
             slot = slots_ref[t]
             place = rb_dev + ((slot - rb_dev) ^ central(slots - rb_dev))
             plan_ref[listed] = row | (jnp.where(slot < rb_dev, slot, place) << 8)
@@ -218,8 +221,8 @@
         functools.partial(tiles_kernel, near_count),
         name="tiles",
         out_shape=(
-            pltpu.HBM((tiles, order, 2 * order), F8),
-            pltpu.VMEM((KEPT, order, 2 * order), F8),
+            pltpu.HBM((tiles, 2 * order, order), F8),
+            pltpu.VMEM((KEPT, 2 * order, order), F8),
             sds((8, rb_dev * order), F32),
             pltpu.HBM((tiles + 32,), I32),
         ),
@@ -230,7 +233,7 @@
             pltpu.SMEM((tiles,), I32),
             pltpu.SMEM((tiles + 32,), I32),
             pltpu.VMEM((tiles, order, 2 * order), BF16),
-            pltpu.VMEM((tiles, order, 2 * order), F8),
+            pltpu.VMEM((tiles, 2 * order, order), F8),
             pltpu.VMEM((rb_dev, order, order), BF16),
             pltpu.SMEM((rb_dev * (rb_dev + nblk),), I32),
             pltpu.SMEM((tiles,), I32),
@@ -255,12 +258,9 @@
         out_ref[i] = sent_ref[wanted_ref[i, 0, me]]
 
 
-def first_kernel(y_ref, scale_ref, wanted_hbm, out_ref, sent_ref, wanted_ref, sem):
-    copy = pltpu.make_async_copy(wanted_hbm, wanted_ref, sem)
-    copy.start()
+def first_kernel(y_ref, scale_ref, wanted_ref, out_ref, sent_ref):
     for r in range(sent_ref.shape[0]):
         sent_ref[r] = rounded_block(y_ref, scale_ref, r, sent_ref.shape[2])
-    copy.wait()
     send_picked(wanted_ref, sent_ref, out_ref)
 
 
@@ -308,7 +308,7 @@
         done = []
         for j in range(UNROLL):
             code = plan_ref[g * UNROLL + j]
-            product = lax.dot_general(load(code >> 8), tile(g, j), NT, preferred_element_type=F32)
+            product = jnp.dot(load(code >> 8), tile(g, j), preferred_element_type=F32)
             done.append((code & 255, product))
         for row, product in done:
             acc_ref[row] = acc_ref[row] + product
@@ -331,17 +331,12 @@
     return (acc[:group] + acc[group:] * (1.0 / FINER)) * size
 
 
-def near_kernel(
-    step, plan_hbm, packed_hbm, scale_ref, now_ref, before_ref, base_ref, tiles_ref, x_ref, acc_ref, sems, plan_ref, plan_sem
-):
-    plan_copy = pltpu.make_async_copy(plan_hbm, plan_ref, plan_sem)
-    plan_copy.start()
+def near_kernel(step, plan_ref, packed_hbm, scale_ref, now_ref, before_ref, base_ref, tiles_ref, x_ref, acc_ref, sems):
     rb_dev, _, order = acc_ref.shape
-    acc_ref[...] = jnp.zeros_like(acc_ref)
-    plan_copy.wait()
     end = plan_ref.shape[0] - 32
     hi = plan_ref[end]
     copy = load_groups(packed_hbm, tiles_ref, sems, 0, hi)
+    acc_ref[...] = jnp.zeros_like(acc_ref)
     size = split_sources(rb_dev, lambda r: rounded_block(now_ref, scale_ref, r, order), x_ref)
     multiply(plan_ref, 0, hi, loaded(copy, tiles_ref, 0), lambda c: x_ref[jnp.minimum(c, rb_dev)], acc_ref)
     for r in range(rb_dev):
@@ -351,23 +346,18 @@
         base_ref[:, at] = moved if step == 0 else 2.0 * moved - before_ref[:, at]
 
 
-def step_kernel(step, plan_hbm, wanted_hbm, packed_hbm, kept_ref, scale_ref, base_ref, arrived_ref, *refs):
+def step_kernel(step, plan_ref, wanted_ref, packed_hbm, kept_ref, scale_ref, base_ref, arrived_ref, *refs):
     last = step == STEPS - 1
     next_ref = refs[0]
-    tiles_ref, x_ref, acc_ref, sems, plan_ref, plan_sem = refs[-6:]
-    plan_copy = pltpu.make_async_copy(plan_hbm, plan_ref, plan_sem)
-    plan_copy.start()
     if not last:
-        out_ref, sent_ref, wanted_ref, wanted_sem = refs[1:5]
-        wanted_copy = pltpu.make_async_copy(wanted_hbm, wanted_ref, wanted_sem)
-        wanted_copy.start()
+        out_ref, sent_ref = refs[1:3]
+    tiles_ref, x_ref, acc_ref, sems = refs[-4:]
     rb_dev, _, order = acc_ref.shape
-    acc_ref[...] = jnp.zeros_like(acc_ref)
-    plan_copy.wait()
     end = plan_ref.shape[0] - 32
     lo, hi = plan_ref[end], plan_ref[end + 1]
     stay = jnp.minimum(lo + KEPT // UNROLL, hi)
     copy = load_groups(packed_hbm, tiles_ref, sems, stay, hi)
+    acc_ref[...] = jnp.zeros_like(acc_ref)
     size = split_sources(arrived_ref.shape[0], lambda p: arrived_ref[p], x_ref)
     size = size * ((1.0 if step == 0 else 2.0) / half_width)
     multiply(
@@ -382,7 +372,6 @@
         if not last:
             sent_ref[r] = (following * scale).astype(BF16)
     if not last:
-        wanted_copy.wait()
         send_picked(wanted_ref, sent_ref, out_ref)
 
 
@@ -513,25 +502,22 @@
 
     out_blocks = sds((nblk, group, order), BF16)
     sent_scratch = pltpu.VMEM((rb_dev, group, order), BF16)
-    wanted_scratch = pltpu.SMEM(wanted.shape, I32)
     blocks = pl.pallas_call(
         first_kernel,
         name="first",
         out_shape=out_blocks,
-        in_specs=[VMEM, VMEM, ANY],
+        in_specs=[VMEM, VMEM, SMEM],
         out_specs=VMEM,
-        scratch_shapes=[sent_scratch, wanted_scratch, pltpu.SemaphoreType.DMA],
+        scratch_shapes=[sent_scratch],
         compiler_params=params(LIMIT),
-    )(y_start, scale, in_hbm(wanted))
+    )(y_start, scale, wanted)
 
     def scratch(entries, sources):
         return [
-            pltpu.VMEM((entries, order, 2 * order), F8),
+            pltpu.VMEM((entries, 2 * order, order), F8),
             pltpu.VMEM((sources + 1, 2 * group, 2 * order), F8),
             pltpu.VMEM((rb_dev, 2 * group, order), F32),
             pltpu.SemaphoreType.DMA((entries // UNROLL,)),
-            pltpu.SMEM(plan.shape, I32),
-            pltpu.SemaphoreType.DMA,
         ]
 
     vectors_here = sds((group, rows), F32)
@@ -542,7 +528,7 @@
             functools.partial(near_kernel, step),
             name="near",
             out_shape=vectors_here,
-            in_specs=[ANY, ANY] + [VMEM] * 3,
+            in_specs=[SMEM, ANY] + [VMEM] * 3,
             out_specs=VMEM,
             scratch_shapes=scratch(near_count, rb_dev),
             compiler_params=params(LIMIT),
@@ -553,12 +539,11 @@
             functools.partial(step_kernel, step),
             name="step",
             out_shape=[vectors_here] if last else [vectors_here, out_blocks],
-            in_specs=[ANY] * 3 + [VMEM] * 4,
+            in_specs=[SMEM, SMEM, ANY] + [VMEM] * 4,
             out_specs=[VMEM] if last else [VMEM, VMEM],
-            scratch_shapes=([] if last else [sent_scratch, wanted_scratch, pltpu.SemaphoreType.DMA])
-            + scratch(tiles - near_count - KEPT, nblk),
+            scratch_shapes=([] if last else [sent_scratch]) + scratch(tiles - near_count - KEPT, nblk),
             compiler_params=params(LIMIT),
-        )(in_hbm(plan), in_hbm(wanted), in_hbm(packed), pltpu.with_memory_space_constraint(kept, pltpu.VMEM), scale, base, arrived)
+        )(in_hbm(plan), wanted, in_hbm(packed), pltpu.with_memory_space_constraint(kept, pltpu.VMEM), scale, base, arrived)
         previous, current = current, out[0]
         if not last:
             blocks = out[1]

time: 106 us -> 105 us (level)
  Pallas kernels: 52.2 us -> 50 us
  waiting for transfers between devices: 21.7 us -> 23 us
    pallas_call x4, Pallas kernels: 20.2 us -> 16.1 us  [per_device(): pl.pallas_call(functools.partial(step_kernel, step), name='step', out_sha...]
    pallas_call x1, Pallas kernels: 12.1 us -> 15.3 us  [tiles_call(): pl.pallas_call(functools.partial(tiles_kernel, near_count), name='tiles',...]
    all_to_all x5, waiting for transfers between devices: 11 us -> 12.2 us  [exchange(): lax.all_to_all(x, 'blk', split_axis=0, concat_axis=0, tiled=True, axis_in...]
    pallas_call x4, Pallas kernels: 11.7 us -> 10.6 us  [per_device(): pl.pallas_call(functools.partial(near_kernel, step), name='near', out_sha...]
  transfers between devices with their start and end apart: 12 -> 12, of which waited for: 10 -> 10; matrix products, arithmetic and copies ran while one was open for 0% -> 0% of each run, Pallas kernels for 23% -> 25%
where the time goes in v10:
time: 105 us; the launch traced here: 104 us
  Pallas kernels  50 us (48%)
  starting transfers between devices  29.7 us (28%)
  waiting for transfers between devices  23 us (22%)
  local copies, waits for them, and re-layouts  1.25 us (1%)
    all_to_all x5, starting transfers between devices, exchange(): lax.all_to_all(x, 'blk', split_axis=0, concat_axis=0, tiled=True, axis_in...  23.5 us
    pallas_call x4, Pallas kernels, per_device(): pl.pallas_call(functools.partial(step_kernel, step), name='step', out_sha...  16.1 us
    pallas_call x1, Pallas kernels, tiles_call(): pl.pallas_call(functools.partial(tiles_kernel, near_count), name='tiles',...  15.3 us
    all_to_all x5, waiting for transfers between devices, exchange(): lax.all_to_all(x, 'blk', split_axis=0, concat_axis=0, tiled=True, axis_in...  12.2 us
    ppermute x7, waiting for transfers between devices, to_partner(): return lax.ppermute(x, axis, [(i, i ^ mask) for i in range(n)])  10.8 us
    pallas_call x4, Pallas kernels, per_device(): pl.pallas_call(functools.partial(near_kernel, step), name='near', out_sha...  10.6 us
    pallas_call x1, Pallas kernels, per_device(): pl.pallas_call(functools.partial(factor_kernel, rows * nblk), name='facto...  6.24 us
    ppermute x7, starting transfers between devices, to_partner(): return lax.ppermute(x, axis, [(i, i ^ mask) for i in range(n)])  6.23 us
  transfers between devices with their start and end apart: 12, of which 10 were waited for; matrix products, arithmetic and copies ran while one was open for 0% of the time, Pallas kernels for 25%

profile of v10, /device:TPU:0, one launch (start us, length us, event | category | flops | bytes accessed | tf_op | source)
XLA Modules:
  0.0 104.0 jit_solution(16992070151172325092)
XLA Ops:
  1.2 7.8 %all-to-all-start = ((s32[8,1,8]{2,1,0:T(1,128)}), s32[8,1,8]{2,1,0:T(1,128)S(1)}, u32[]{:S(2)}, u32[]{:S(2)}) async-start(s32[8,1,8]{2,1,0:T(1,128)} %broadcast_in_dim.9), calls=%async_computation | async-start | bytes 8192 | tf_op jit(solution)/shard_map/all_to_all | solution.py:477
  9.1 15.3 %tiles.1 = (f8e4m3fn[96,512,256]{2,1,0:T(32,128)(4,1)}, f8e4m3fn[16,512,256]{2,1,0:T(32,128)(4,1)S(1)}, f32[8,2048]{1,0:T(8,128)S(1)}, s32[128]{0:T(128)}) custom-call(s32[96]{0:T(128)} %rows_hbm.1, s32[96]{0:T(128)} %slots_hbm.1, bf16[96,256,256]{2,1,0:T(8,128)(2,1)} %real_hbm.1, bf16[96,256,256]{2,1,0:T(8,128)(2,1)} %imag_hbm.1), custom_call_target="tpu_custom_call" | custom-call | flops 268435456 | bytes 25165824 | tf_op jit(solution)/shard_map/tiles/pallas_call | solution.py:220
  25.7 5.0 %all-to-all-start.1 = ((bf16[8,32,256]{2,1,0:T(8,128)(2,1)}), bf16[8,32,256]{2,1,0:T(8,128)(2,1)S(1)}, u32[]{:S(2)}, u32[]{:S(2)}) async-start(bf16[8,32,256]{2,1,0:T(8,128)(2,1)} %first.1), calls=%async_computation.1 | async-start | bytes 262144 | tf_op jit(solution)/shard_map/all_to_all | solution.py:477
  30.8 2.6 %near.4.base_ref = f32[32,2048]{1,0:T(8,128)S(1)} custom-call(s32[128]{0:T(128)} %get-tuple-element.17.plan_ref, f8e4m3fn[96,512,256]{2,1,0:T(32,128)(4,1)} %get-tuple-element.18.packed_hbm, f32[8,2048]{1,0:T(8,128)S(1)} %get-tuple-element.20.scale_ref, f32[32,2048]{1,0:T(8,128)S(1)} %copy-done, f32[32,2048]{1,0:T(8,128)S(1)} %copy-done), custom_call_target="tpu_custom_call" | custom-call | flops 268435456 | bytes 2097152 | tf_op jit(solution)/shard_map/near/pallas_call | solution.py:527
  33.4 3.1 %all-to-all-done.1.arrived_ref = bf16[8,32,256]{2,1,0:T(8,128)(2,1)S(1)} async-done(((bf16[8,32,256]{2,1,0:T(8,128)(2,1)}), bf16[8,32,256]{2,1,0:T(8,128)(2,1)S(1)}, u32[]{:S(2)}, u32[]{:S(2)}) %all-to-all-start.1) | async-done | bytes 131104 | tf_op jit(solution)/shard_map/all_to_all | solution.py:477
  36.5 4.2 %step.4 = (f32[32,2048]{1,0:T(8,128)S(1)}, bf16[8,32,256]{2,1,0:T(8,128)(2,1)}) custom-call(s32[128]{0:T(128)} %get-tuple-element.17.plan_ref, s32[8,1,8]{2,1,0:T(1,128)S(1)} %all-to-all-done.wanted_ref, f8e4m3fn[96,512,256]{2,1,0:T(32,128)(4,1)} %get-tuple-element.18.packed_hbm, f8e4m3fn[16,512,256]{2,1,0:T(32,128)(4,1)S(1)} %get-tuple-element.19.kept_ref, ...), custom_call_target="tpu_custom_call" | custom-call | tf_op jit(solution)/shard_map/step/pallas_call | solution.py:538
  40.7 3.5 %all-to-all-start.2 = ((bf16[8,32,256]{2,1,0:T(8,128)(2,1)}), bf16[8,32,256]{2,1,0:T(8,128)(2,1)S(1)}, u32[]{:S(2)}, u32[]{:S(2)}) async-start(bf16[8,32,256]{2,1,0:T(8,128)(2,1)} %get-tuple-element.22), calls=%async_computation.2 | async-start | bytes 262144 | tf_op jit(solution)/shard_map/all_to_all | solution.py:477
  44.2 2.7 %near.5.base_ref = f32[32,2048]{1,0:T(8,128)S(1)} custom-call(s32[128]{0:T(128)} %get-tuple-element.17.plan_ref, f8e4m3fn[96,512,256]{2,1,0:T(32,128)(4,1)} %get-tuple-element.18.packed_hbm, f32[8,2048]{1,0:T(8,128)S(1)} %get-tuple-element.20.scale_ref, f32[32,2048]{1,0:T(8,128)S(1)} %get-tuple-element.21.now_ref.before_ref, f32[32,2048]{1,0:T(8,128)S(1)} %copy-done), custom_call_target="tpu_custom_call" | custom-call | flops 268435456 | bytes 2097152 | tf_op jit(solution)/shard_map/near/pallas_call | solution.py:527
  46.9 3.1 %all-to-all-done.2.arrived_ref = bf16[8,32,256]{2,1,0:T(8,128)(2,1)S(1)} async-done(((bf16[8,32,256]{2,1,0:T(8,128)(2,1)}), bf16[8,32,256]{2,1,0:T(8,128)(2,1)S(1)}, u32[]{:S(2)}, u32[]{:S(2)}) %all-to-all-start.2) | async-done | bytes 131104 | tf_op jit(solution)/shard_map/all_to_all | solution.py:477
  49.9 4.2 %step.5 = (f32[32,2048]{1,0:T(8,128)S(1)}, bf16[8,32,256]{2,1,0:T(8,128)(2,1)}) custom-call(s32[128]{0:T(128)} %get-tuple-element.17.plan_ref, s32[8,1,8]{2,1,0:T(1,128)S(1)} %all-to-all-done.wanted_ref, f8e4m3fn[96,512,256]{2,1,0:T(32,128)(4,1)} %get-tuple-element.18.packed_hbm, f8e4m3fn[16,512,256]{2,1,0:T(32,128)(4,1)S(1)} %get-tuple-element.19.kept_ref, ...), custom_call_target="tpu_custom_call" | custom-call | tf_op jit(solution)/shard_map/step/pallas_call | solution.py:538
  54.1 3.5 %all-to-all-start.3 = ((bf16[8,32,256]{2,1,0:T(8,128)(2,1)}), bf16[8,32,256]{2,1,0:T(8,128)(2,1)S(1)}, u32[]{:S(2)}, u32[]{:S(2)}) async-start(bf16[8,32,256]{2,1,0:T(8,128)(2,1)} %get-tuple-element.24), calls=%async_computation.3 | async-start | bytes 262144 | tf_op jit(solution)/shard_map/all_to_all | solution.py:477
  57.7 2.7 %near.6.base_ref = f32[32,2048]{1,0:T(8,128)S(1)} custom-call(s32[128]{0:T(128)} %get-tuple-element.17.plan_ref, f8e4m3fn[96,512,256]{2,1,0:T(32,128)(4,1)} %get-tuple-element.18.packed_hbm, f32[8,2048]{1,0:T(8,128)S(1)} %get-tuple-element.20.scale_ref, f32[32,2048]{1,0:T(8,128)S(1)} %get-tuple-element.23.now_ref.before_ref, ...), custom_call_target="tpu_custom_call" | custom-call | flops 268435456 | bytes 2097152 | tf_op jit(solution)/shard_map/near/pallas_call | solution.py:527
  60.3 3.1 %all-to-all-done.3.arrived_ref = bf16[8,32,256]{2,1,0:T(8,128)(2,1)S(1)} async-done(((bf16[8,32,256]{2,1,0:T(8,128)(2,1)}), bf16[8,32,256]{2,1,0:T(8,128)(2,1)S(1)}, u32[]{:S(2)}, u32[]{:S(2)}) %all-to-all-start.3) | async-done | bytes 131104 | tf_op jit(solution)/shard_map/all_to_all | solution.py:477
  63.4 4.2 %step.6 = (f32[32,2048]{1,0:T(8,128)S(1)}, bf16[8,32,256]{2,1,0:T(8,128)(2,1)}) custom-call(s32[128]{0:T(128)} %get-tuple-element.17.plan_ref, s32[8,1,8]{2,1,0:T(1,128)S(1)} %all-to-all-done.wanted_ref, f8e4m3fn[96,512,256]{2,1,0:T(32,128)(4,1)} %get-tuple-element.18.packed_hbm, f8e4m3fn[16,512,256]{2,1,0:T(32,128)(4,1)S(1)} %get-tuple-element.19.kept_ref, ...), custom_call_target="tpu_custom_call" | custom-call | tf_op jit(solution)/shard_map/step/pallas_call | solution.py:538
  67.6 3.5 %all-to-all-start.4 = ((bf16[8,32,256]{2,1,0:T(8,128)(2,1)}), bf16[8,32,256]{2,1,0:T(8,128)(2,1)S(1)}, u32[]{:S(2)}, u32[]{:S(2)}) async-start(bf16[8,32,256]{2,1,0:T(8,128)(2,1)} %get-tuple-element.26), calls=%async_computation.4 | async-start | bytes 262144 | tf_op jit(solution)/shard_map/all_to_all | solution.py:477
  71.1 2.7 %near.7.base_ref = f32[32,2048]{1,0:T(8,128)S(1)} custom-call(s32[128]{0:T(128)} %get-tuple-element.17.plan_ref, f8e4m3fn[96,512,256]{2,1,0:T(32,128)(4,1)} %get-tuple-element.18.packed_hbm, f32[8,2048]{1,0:T(8,128)S(1)} %get-tuple-element.20.scale_ref, f32[32,2048]{1,0:T(8,128)S(1)} %get-tuple-element.25.now_ref, ...), custom_call_target="tpu_custom_call" | custom-call | flops 268435456 | bytes 2097152 | tf_op jit(solution)/shard_map/near/pallas_call | solution.py:527
  73.8 3.1 %all-to-all-done.4.arrived_ref = bf16[8,32,256]{2,1,0:T(8,128)(2,1)S(1)} async-done(((bf16[8,32,256]{2,1,0:T(8,128)(2,1)}), bf16[8,32,256]{2,1,0:T(8,128)(2,1)S(1)}, u32[]{:S(2)}, u32[]{:S(2)}) %all-to-all-start.4) | async-done | bytes 131104 | tf_op jit(solution)/shard_map/all_to_all | solution.py:477
  76.8 3.5 %step.7.own_ref = f32[32,2048]{1,0:T(8,128)S(1)} custom-call(s32[128]{0:T(128)} %get-tuple-element.17.plan_ref, s32[8,1,8]{2,1,0:T(1,128)S(1)} %all-to-all-done.wanted_ref, f8e4m3fn[96,512,256]{2,1,0:T(32,128)(4,1)} %get-tuple-element.18.packed_hbm, f8e4m3fn[16,512,256]{2,1,0:T(32,128)(4,1)S(1)} %get-tuple-element.19.kept_ref, ...), custom_call_target="tpu_custom_call" | custom-call | tf_op jit(solution)/shard_map/step/pallas_call | solution.py:538
  80.4 1.6 %collective-permute-start.1 = (bf16[32,2048]{1,0:T(8,128)(2,1)S(1)}, bf16[32,2048]{1,0:T(8,128)(2,1)S(1)}, u32[]{:S(2)}, u32[]{:S(2)}) collective-permute-start(bf16[32,2048]{1,0:T(8,128)(2,1)S(1)} %convert_element_type.3), channel_id=1, source_target_pairs={{0,2},{1,3},{2,0},{3,1},{4,6},{5,7},{6,4},{7,5},{8,10},{9,11},{10,... | collective-permute-start | bytes 393224 | tf_op jit(solution)/shard_map/ppermute | solution.py:482
  81.9 3.5 %collective-permute-done.1.refs_1_ = bf16[32,2048]{1,0:T(8,128)(2,1)S(1)} collective-permute-done((bf16[32,2048]{1,0:T(8,128)(2,1)S(1)}, bf16[32,2048]{1,0:T(8,128)(2,1)S(1)}, u32[]{:S(2)}, u32[]{:S(2)}) %collective-permute-start.1) | collective-permute-done | bytes 131104 | tf_op jit(solution)/shard_map/ppermute | solution.py:482
  87.5 3.7 %collective-permute-done.3 = f32[64,128]{1,0:T(8,128)S(1)} collective-permute-done((f32[64,128]{1,0:T(8,128)S(1)}, f32[64,128]{1,0:T(8,128)S(1)}, u32[]{:S(2)}, u32[]{:S(2)}) %collective-permute-start.3) | collective-permute-done | bytes 32800 | tf_op jit(solution)/shard_map/ppermute | solution.py:482
  91.2 1.4 %collective-permute-start.6 = (f32[64,128]{1,0:T(8,128)S(1)}, f32[64,128]{1,0:T(8,128)S(1)}, u32[]{:S(2)}, u32[]{:S(2)}) collective-permute-start(f32[64,128]{1,0:T(8,128)S(1)} %add.3.refs_0_), channel_id=1, source_target_pairs={{0,24},{4,28},{8,16},{12,20},{16,8},{20,12},{24,0},{28,4},{1,25},{... | collective-permute-start | bytes 98312 | tf_op jit(solution)/shard_map/ppermute | solution.py:482
  92.9 2.7 %collective-permute-start.4 = (f32[64,128]{1,0:T(8,128)S(1)}, f32[64,128]{1,0:T(8,128)S(1)}, u32[]{:S(2)}, u32[]{:S(2)}) collective-permute-start(f32[64,128]{1,0:T(8,128)S(1)} %add.3.refs_0_), channel_id=1, source_target_pairs={{0,8},{4,12},{8,0},{12,4},{16,24},{20,28},{24,16},{28,20},{1,9},{5... | collective-permute-start | bytes 98312 | tf_op jit(solution)/shard_map/ppermute | solution.py:482
  97.8 6.2 %factor.1 = f32[32,2048]{1,0:T(8,128)} custom-call(f32[32,2048]{1,0:T(8,128)S(1)} %step.7.own_ref, bf16[4,32,2048]{2,1,0:T(8,128)(2,1)S(1)} %get-tuple-element.27.all_ref, f32[64,128]{1,0:T(8,128)S(1)} %add.3.refs_0_, f32[64,128]{1,0:T(8,128)S(1)} %collective-permute-done.4.refs_1_, f32[64,128]{1,0:T(8,128)S(1)} %collective-permute-done.5.refs_2_, ...), custom_call_target="tpu_custom_call" | custom-call | tf_op jit(solution)/shard_map/factor/pallas_call | solution.py:568
  (17 shorter events, 7.1 us)
Async XLA Ops:
  1.2 23.2 %all-to-all-start = ((s32[8,1,8]{2,1,0:T(1,128)}), s32[8,1,8]{2,1,0:T(1,128)S(1)}, u32[]{:S(2)}, u32[]{:S(2)}) async-start(s32[8,1,8]{2,1,0:T(1,128)} %broadcast_in_dim.9), calls=%async_computation | async-start | bytes 8192 | tf_op jit(solution)/shard_map/all_to_all | solution.py:477
  9.1 15.3 %copy-start = (f32[32,2048]{1,0:T(8,128)S(1)}, f32[32,2048]{1,0:T(8,128)}, u32[]{:S(2)}) copy-start(f32[32,2048]{1,0:T(8,128)} %before_ref.3) | copy-start | bytes 786436
  25.7 10.8 %all-to-all-start.1 = ((bf16[8,32,256]{2,1,0:T(8,128)(2,1)}), bf16[8,32,256]{2,1,0:T(8,128)(2,1)S(1)}, u32[]{:S(2)}, u32[]{:S(2)}) async-start(bf16[8,32,256]{2,1,0:T(8,128)(2,1)} %first.1), calls=%async_computation.1 | async-start | bytes 262144 | tf_op jit(solution)/shard_map/all_to_all | solution.py:477
  40.7 9.3 %all-to-all-start.2 = ((bf16[8,32,256]{2,1,0:T(8,128)(2,1)}), bf16[8,32,256]{2,1,0:T(8,128)(2,1)S(1)}, u32[]{:S(2)}, u32[]{:S(2)}) async-start(bf16[8,32,256]{2,1,0:T(8,128)(2,1)} %get-tuple-element.22), calls=%async_computation.2 | async-start | bytes 262144 | tf_op jit(solution)/shard_map/all_to_all | solution.py:477
  54.1 9.3 %all-to-all-start.3 = ((bf16[8,32,256]{2,1,0:T(8,128)(2,1)}), bf16[8,32,256]{2,1,0:T(8,128)(2,1)S(1)}, u32[]{:S(2)}, u32[]{:S(2)}) async-start(bf16[8,32,256]{2,1,0:T(8,128)(2,1)} %get-tuple-element.24), calls=%async_computation.3 | async-start | bytes 262144 | tf_op jit(solution)/shard_map/all_to_all | solution.py:477
  67.6 9.3 %all-to-all-start.4 = ((bf16[8,32,256]{2,1,0:T(8,128)(2,1)}), bf16[8,32,256]{2,1,0:T(8,128)(2,1)S(1)}, u32[]{:S(2)}, u32[]{:S(2)}) async-start(bf16[8,32,256]{2,1,0:T(8,128)(2,1)} %get-tuple-element.26), calls=%async_computation.4 | async-start | bytes 262144 | tf_op jit(solution)/shard_map/all_to_all | solution.py:477
  80.4 5.0 %collective-permute-start.1 = (bf16[32,2048]{1,0:T(8,128)(2,1)S(1)}, bf16[32,2048]{1,0:T(8,128)(2,1)S(1)}, u32[]{:S(2)}, u32[]{:S(2)}) collective-permute-start(bf16[32,2048]{1,0:T(8,128)(2,1)S(1)} %convert_element_type.3), channel_id=1, source_target_pairs={{0,2},{1,3},{2,0},{3,1},{4,6},{5,7},{6,4},{7,5},{8,10},{9,11},{10,... | collective-permute-start | bytes 393224 | tf_op jit(solution)/shard_map/ppermute | solution.py:482
  81.9 3.5 %collective-permute-start = (bf16[32,2048]{1,0:T(8,128)(2,1)S(1)}, bf16[32,2048]{1,0:T(8,128)(2,1)S(1)}, u32[]{:S(2)}, u32[]{:S(2)}) collective-permute-start(bf16[32,2048]{1,0:T(8,128)(2,1)S(1)} %convert_element_type.3), channel_id=1, source_target_pairs={{0,1},{1,0},{2,3},{3,2},{4,5},{5,4},{6,7},{7,6},{8,9},{9,8},{10,11... | collective-permute-start | bytes 393224 | tf_op jit(solution)/shard_map/ppermute | solution.py:482
  85.4 1.3 %collective-permute-start.2 = (bf16[32,2048]{1,0:T(8,128)(2,1)S(1)}, bf16[32,2048]{1,0:T(8,128)(2,1)S(1)}, u32[]{:S(2)}, u32[]{:S(2)}) collective-permute-start(bf16[32,2048]{1,0:T(8,128)(2,1)S(1)} %collective-permute-done.1.refs_1_), channel_id=1, source_target_pairs={{0,1},{1,0},{2,3},{3,2},{4,5},{5,4},{6,7},{7,6},{8,9},{9,8},{10,11... | collective-permute-start | bytes 393224 | tf_op jit(solution)/shard_map/ppermute | solution.py:482
  87.2 4.0 %collective-permute-start.3 = (f32[64,128]{1,0:T(8,128)S(1)}, f32[64,128]{1,0:T(8,128)S(1)}, u32[]{:S(2)}, u32[]{:S(2)}) collective-permute-start(f32[64,128]{1,0:T(8,128)S(1)} %get-tuple-element.28), channel_id=1, source_target_pairs={{0,4},{4,0},{8,12},{12,8},{16,20},{20,16},{24,28},{28,24},{1,5},{5... | collective-permute-start | bytes 98312 | tf_op jit(solution)/shard_map/ppermute | solution.py:482
  91.2 5.7 %collective-permute-start.6 = (f32[64,128]{1,0:T(8,128)S(1)}, f32[64,128]{1,0:T(8,128)S(1)}, u32[]{:S(2)}, u32[]{:S(2)}) collective-permute-start(f32[64,128]{1,0:T(8,128)S(1)} %add.3.refs_0_), channel_id=1, source_target_pairs={{0,24},{4,28},{8,16},{12,20},{16,8},{20,12},{24,0},{28,4},{1,25},{... | collective-permute-start | bytes 98312 | tf_op jit(solution)/shard_map/ppermute | solution.py:482
  92.6 5.1 %collective-permute-start.5 = (f32[64,128]{1,0:T(8,128)S(1)}, f32[64,128]{1,0:T(8,128)S(1)}, u32[]{:S(2)}, u32[]{:S(2)}) collective-permute-start(f32[64,128]{1,0:T(8,128)S(1)} %add.3.refs_0_), channel_id=1, source_target_pairs={{0,16},{4,20},{8,24},{12,28},{16,0},{20,4},{24,8},{28,12},{1,17},{... | collective-permute-start | bytes 98312 | tf_op jit(solution)/shard_map/ppermute | solution.py:482
  92.9 4.9 %collective-permute-start.4 = (f32[64,128]{1,0:T(8,128)S(1)}, f32[64,128]{1,0:T(8,128)S(1)}, u32[]{:S(2)}, u32[]{:S(2)}) collective-permute-start(f32[64,128]{1,0:T(8,128)S(1)} %add.3.refs_0_), channel_id=1, source_target_pairs={{0,8},{4,12},{8,0},{12,4},{16,24},{20,28},{24,16},{28,20},{1,9},{5... | collective-permute-start | bytes 98312 | tf_op jit(solution)/shard_map/ppermute | solution.py:482

commit v11 on v10

--- a/solution.py
+++ b/solution.py
@@ -85,7 +85,7 @@
     list_sems,
 ):
     kept = kept_ref.shape[0]
-    tiles, order, _ = both_ref.shape
+    tiles, order, _ = real_hbm.shape
     rb_dev = present_ref.shape[0]
     slots = rb_dev + lax.axis_size("blk")
     chunks = tiles // CHUNK
@@ -116,6 +116,8 @@
 
     lax.fori_loop(0, rb_dev * slots, clear, 0)
     present_ref[...] = jnp.zeros_like(present_ref)
+    both_ref[tiles] = jnp.zeros_like(both_ref[tiles])
+    back_ref[tiles] = -1
     for copy in lists:
         copy.wait()
 
@@ -137,33 +139,39 @@
 
     lax.fori_loop(0, tiles, link, 0)
 
-    def turned(tile):
-        return jnp.concatenate([tile[:, :order].T, tile[:, order:].T], axis=0).astype(F8)
+    def keep(e, skip):
+        return pltpu.make_async_copy(small_ref.at[e], kept_ref.at[e - skip + kept], out_sems.at[e])
 
     def put(e, skip, value):
+        small_ref[e] = value
+
         @pl.when(e < skip)
         def _():
-            kept_ref[e - skip + kept] = value()
+            keep(e, skip).start()
 
         @pl.when(e >= skip)
         def _():
-            small_ref[e] = value()
             leave(e).start()
 
     def one(skip, t, listed):
         row = rows_ref[t]
         both = both_ref[t]
-        present_ref[row] = present_ref[row] + (both[:, :order] + jnp.abs(both[:, order:]))
+        counted = both[:, :order] + jnp.abs(both[:, order:])
+        present_ref[row] = present_ref[row] + (counted[:, : order // 2] + counted[:, order // 2 :])
         closes = done_ref[t]
 
         @pl.when(closes == 1)
         def _():
-            def add(prior):
-                both_ref[t] = both_ref[t] + both_ref[prior]
-                return back_ref[prior]
-
-            lax.while_loop(lambda prior: prior >= 0, add, back_ref[t])
-            put(listed, skip, lambda: turned(both_ref[t]))
+            prior = back_ref[t]
+            partner = jnp.where(prior < 0, tiles, prior)
+
+            def add(earlier):
+                both_ref[partner] = both_ref[partner] + both_ref[earlier]
+                return back_ref[earlier]
+
+            lax.while_loop(lambda earlier: earlier >= 0, add, back_ref[partner])
+            small = (both_ref[t] + both_ref[partner]).astype(F8)
+            put(listed, skip, jnp.concatenate([small[:, :order].T, small[:, order:].T], axis=0))
             slot = slots_ref[t]
             place = rb_dev + ((slot - rb_dev) ^ central(slots - rb_dev))
             plan_ref[listed] = row | (jnp.where(slot < rb_dev, slot, place) << 8)
@@ -183,7 +191,7 @@
 
             @pl.when(j < short)
             def _():
-                put(listed + j, skip, lambda: jnp.zeros(small_ref.shape[1:], F8))
+                put(listed + j, skip, jnp.zeros(small_ref.shape[1:], F8))
                 plan_ref[listed + j] = slots << 8
 
         return listed + short
@@ -196,7 +204,7 @@
     plan_copy = pltpu.make_async_copy(plan_ref, plan_hbm, list_sems.at[2])
     plan_copy.start()
 
-    ones = jnp.ones((8, order), BF16)
+    ones = jnp.ones((8, order // 2), BF16)
     for r in range(rb_dev):
         degree = lax.dot_general(ones, present_ref[r], NT, preferred_element_type=F32)
         scale_ref[:, r * order : (r + 1) * order] = 1.0 / jnp.sqrt(jnp.maximum(degree, 1.0))
@@ -205,7 +213,12 @@
         leave(e).wait()
         return _
 
+    def stayed(e, _):
+        keep(e, skip).wait()
+        return _
+
     lax.fori_loop(0, near, left, 0)
+    lax.fori_loop(near, jnp.minimum(skip, every), stayed, 0)
     lax.fori_loop(skip, every, left, 0)
     plan_copy.wait()
 
@@ -232,11 +245,11 @@
             pltpu.SMEM((tiles,), I32),
             pltpu.SMEM((tiles,), I32),
             pltpu.SMEM((tiles + 32,), I32),
-            pltpu.VMEM((tiles, order, 2 * order), BF16),
+            pltpu.VMEM((tiles + 1, order, 2 * order), BF16),
             pltpu.VMEM((tiles, 2 * order, order), F8),
-            pltpu.VMEM((rb_dev, order, order), BF16),
+            pltpu.VMEM((rb_dev, order, order // 2), BF16),
             pltpu.SMEM((rb_dev * (rb_dev + nblk),), I32),
-            pltpu.SMEM((tiles,), I32),
+            pltpu.SMEM((tiles + 1,), I32),
             pltpu.SMEM((tiles,), I32),
             pltpu.SemaphoreType.DMA((tiles // CHUNK, 2)),
             pltpu.SemaphoreType.DMA((tiles,)),

time: 105 us -> 106 us (level)
  Pallas kernels: 50 us -> 51.2 us
    pallas_call x1, Pallas kernels: 15.3 us -> 16.5 us  [tiles_call(): pl.pallas_call(functools.partial(tiles_kernel, near_count), name='tiles',...]
  transfers between devices with their start and end apart: 12 -> 12, of which waited for: 10 -> 10; matrix products, arithmetic and copies ran while one was open for 0% -> 0% of each run, Pallas kernels for 25% -> 26%
where the time goes in v11:
time: 106 us; the launch traced here: 105 us
  Pallas kernels  51.2 us (48%)
  starting transfers between devices  29.5 us (28%)
  waiting for transfers between devices  22.9 us (22%)
  local copies, waits for them, and re-layouts  1.25 us (1%)
    all_to_all x5, starting transfers between devices, exchange(): lax.all_to_all(x, 'blk', split_axis=0, concat_axis=0, tiled=True, axis_in...  23.2 us
    pallas_call x1, Pallas kernels, tiles_call(): pl.pallas_call(functools.partial(tiles_kernel, near_count), name='tiles',...  16.5 us
    pallas_call x4, Pallas kernels, per_device(): pl.pallas_call(functools.partial(step_kernel, step), name='step', out_sha...  16.1 us
    all_to_all x5, waiting for transfers between devices, exchange(): lax.all_to_all(x, 'blk', split_axis=0, concat_axis=0, tiled=True, axis_in...  12.2 us
    ppermute x7, waiting for transfers between devices, to_partner(): return lax.ppermute(x, axis, [(i, i ^ mask) for i in range(n)])  10.8 us
    pallas_call x4, Pallas kernels, per_device(): pl.pallas_call(functools.partial(near_kernel, step), name='near', out_sha...  10.6 us
    pallas_call x1, Pallas kernels, per_device(): pl.pallas_call(functools.partial(factor_kernel, rows * nblk), name='facto...  6.24 us
    ppermute x7, starting transfers between devices, to_partner(): return lax.ppermute(x, axis, [(i, i ^ mask) for i in range(n)])  6.23 us
  transfers between devices with their start and end apart: 12, of which 10 were waited for; matrix products, arithmetic and copies ran while one was open for 0% of the time, Pallas kernels for 26%

profile of v11, /device:TPU:0, one launch (start us, length us, event | category | flops | bytes accessed | tf_op | source)
XLA Modules:
  0.0 105.0 jit_solution(14656644489872539762)
XLA Ops:
  1.2 7.8 %all-to-all-start = ((s32[8,1,8]{2,1,0:T(1,128)}), s32[8,1,8]{2,1,0:T(1,128)S(1)}, u32[]{:S(2)}, u32[]{:S(2)}) async-start(s32[8,1,8]{2,1,0:T(1,128)} %broadcast_in_dim.9), calls=%async_computation | async-start | bytes 8192 | tf_op jit(solution)/shard_map/all_to_all | solution.py:490
  9.1 16.5 %tiles.1 = (f8e4m3fn[96,512,256]{2,1,0:T(32,128)(4,1)}, f8e4m3fn[16,512,256]{2,1,0:T(32,128)(4,1)S(1)}, f32[8,2048]{1,0:T(8,128)S(1)}, s32[128]{0:T(128)}) custom-call(s32[96]{0:T(128)} %rows_hbm.1, s32[96]{0:T(128)} %slots_hbm.1, bf16[96,256,256]{2,1,0:T(8,128)(2,1)} %real_hbm.1, bf16[96,256,256]{2,1,0:T(8,128)(2,1)} %imag_hbm.1), custom_call_target="tpu_custom_call" | custom-call | flops 268435456 | bytes 25165824 | tf_op jit(solution)/shard_map/tiles/pallas_call | solution.py:233
  26.9 5.4 %all-to-all-start.1 = ((bf16[8,32,256]{2,1,0:T(8,128)(2,1)}), bf16[8,32,256]{2,1,0:T(8,128)(2,1)S(1)}, u32[]{:S(2)}, u32[]{:S(2)}) async-start(bf16[8,32,256]{2,1,0:T(8,128)(2,1)} %first.1), calls=%async_computation.1 | async-start | bytes 262144 | tf_op jit(solution)/shard_map/all_to_all | solution.py:490
  32.3 2.6 %near.4.base_ref = f32[32,2048]{1,0:T(8,128)S(1)} custom-call(s32[128]{0:T(128)} %get-tuple-element.17.plan_ref, f8e4m3fn[96,512,256]{2,1,0:T(32,128)(4,1)} %get-tuple-element.18.packed_hbm, f32[8,2048]{1,0:T(8,128)S(1)} %get-tuple-element.20.scale_ref, f32[32,2048]{1,0:T(8,128)S(1)} %copy-done, f32[32,2048]{1,0:T(8,128)S(1)} %copy-done), custom_call_target="tpu_custom_call" | custom-call | flops 268435456 | bytes 2097152 | tf_op jit(solution)/shard_map/near/pallas_call | solution.py:540
  35.0 3.1 %all-to-all-done.1.arrived_ref = bf16[8,32,256]{2,1,0:T(8,128)(2,1)S(1)} async-done(((bf16[8,32,256]{2,1,0:T(8,128)(2,1)}), bf16[8,32,256]{2,1,0:T(8,128)(2,1)S(1)}, u32[]{:S(2)}, u32[]{:S(2)}) %all-to-all-start.1) | async-done | bytes 131104 | tf_op jit(solution)/shard_map/all_to_all | solution.py:490
  38.0 4.2 %step.4 = (f32[32,2048]{1,0:T(8,128)S(1)}, bf16[8,32,256]{2,1,0:T(8,128)(2,1)}) custom-call(s32[128]{0:T(128)} %get-tuple-element.17.plan_ref, s32[8,1,8]{2,1,0:T(1,128)S(1)} %all-to-all-done.wanted_ref, f8e4m3fn[96,512,256]{2,1,0:T(32,128)(4,1)} %get-tuple-element.18.packed_hbm, f8e4m3fn[16,512,256]{2,1,0:T(32,128)(4,1)S(1)} %get-tuple-element.19.kept_ref, ...), custom_call_target="tpu_custom_call" | custom-call | tf_op jit(solution)/shard_map/step/pallas_call | solution.py:551
  42.2 3.3 %all-to-all-start.2 = ((bf16[8,32,256]{2,1,0:T(8,128)(2,1)}), bf16[8,32,256]{2,1,0:T(8,128)(2,1)S(1)}, u32[]{:S(2)}, u32[]{:S(2)}) async-start(bf16[8,32,256]{2,1,0:T(8,128)(2,1)} %get-tuple-element.22), calls=%async_computation.2 | async-start | bytes 262144 | tf_op jit(solution)/shard_map/all_to_all | solution.py:490
  45.6 2.7 %near.5.base_ref = f32[32,2048]{1,0:T(8,128)S(1)} custom-call(s32[128]{0:T(128)} %get-tuple-element.17.plan_ref, f8e4m3fn[96,512,256]{2,1,0:T(32,128)(4,1)} %get-tuple-element.18.packed_hbm, f32[8,2048]{1,0:T(8,128)S(1)} %get-tuple-element.20.scale_ref, f32[32,2048]{1,0:T(8,128)S(1)} %get-tuple-element.21.now_ref.before_ref, f32[32,2048]{1,0:T(8,128)S(1)} %copy-done), custom_call_target="tpu_custom_call" | custom-call | flops 268435456 | bytes 2097152 | tf_op jit(solution)/shard_map/near/pallas_call | solution.py:540
  48.2 3.0 %all-to-all-done.2.arrived_ref = bf16[8,32,256]{2,1,0:T(8,128)(2,1)S(1)} async-done(((bf16[8,32,256]{2,1,0:T(8,128)(2,1)}), bf16[8,32,256]{2,1,0:T(8,128)(2,1)S(1)}, u32[]{:S(2)}, u32[]{:S(2)}) %all-to-all-start.2) | async-done | bytes 131104 | tf_op jit(solution)/shard_map/all_to_all | solution.py:490
  51.3 4.2 %step.5 = (f32[32,2048]{1,0:T(8,128)S(1)}, bf16[8,32,256]{2,1,0:T(8,128)(2,1)}) custom-call(s32[128]{0:T(128)} %get-tuple-element.17.plan_ref, s32[8,1,8]{2,1,0:T(1,128)S(1)} %all-to-all-done.wanted_ref, f8e4m3fn[96,512,256]{2,1,0:T(32,128)(4,1)} %get-tuple-element.18.packed_hbm, f8e4m3fn[16,512,256]{2,1,0:T(32,128)(4,1)S(1)} %get-tuple-element.19.kept_ref, ...), custom_call_target="tpu_custom_call" | custom-call | tf_op jit(solution)/shard_map/step/pallas_call | solution.py:551
  55.5 3.3 %all-to-all-start.3 = ((bf16[8,32,256]{2,1,0:T(8,128)(2,1)}), bf16[8,32,256]{2,1,0:T(8,128)(2,1)S(1)}, u32[]{:S(2)}, u32[]{:S(2)}) async-start(bf16[8,32,256]{2,1,0:T(8,128)(2,1)} %get-tuple-element.24), calls=%async_computation.3 | async-start | bytes 262144 | tf_op jit(solution)/shard_map/all_to_all | solution.py:490
  58.8 2.7 %near.6.base_ref = f32[32,2048]{1,0:T(8,128)S(1)} custom-call(s32[128]{0:T(128)} %get-tuple-element.17.plan_ref, f8e4m3fn[96,512,256]{2,1,0:T(32,128)(4,1)} %get-tuple-element.18.packed_hbm, f32[8,2048]{1,0:T(8,128)S(1)} %get-tuple-element.20.scale_ref, f32[32,2048]{1,0:T(8,128)S(1)} %get-tuple-element.23.now_ref.before_ref, ...), custom_call_target="tpu_custom_call" | custom-call | flops 268435456 | bytes 2097152 | tf_op jit(solution)/shard_map/near/pallas_call | solution.py:540
  61.5 3.0 %all-to-all-done.3.arrived_ref = bf16[8,32,256]{2,1,0:T(8,128)(2,1)S(1)} async-done(((bf16[8,32,256]{2,1,0:T(8,128)(2,1)}), bf16[8,32,256]{2,1,0:T(8,128)(2,1)S(1)}, u32[]{:S(2)}, u32[]{:S(2)}) %all-to-all-start.3) | async-done | bytes 131104 | tf_op jit(solution)/shard_map/all_to_all | solution.py:490
  64.5 4.2 %step.6 = (f32[32,2048]{1,0:T(8,128)S(1)}, bf16[8,32,256]{2,1,0:T(8,128)(2,1)}) custom-call(s32[128]{0:T(128)} %get-tuple-element.17.plan_ref, s32[8,1,8]{2,1,0:T(1,128)S(1)} %all-to-all-done.wanted_ref, f8e4m3fn[96,512,256]{2,1,0:T(32,128)(4,1)} %get-tuple-element.18.packed_hbm, f8e4m3fn[16,512,256]{2,1,0:T(32,128)(4,1)S(1)} %get-tuple-element.19.kept_ref, ...), custom_call_target="tpu_custom_call" | custom-call | tf_op jit(solution)/shard_map/step/pallas_call | solution.py:551
  68.7 3.3 %all-to-all-start.4 = ((bf16[8,32,256]{2,1,0:T(8,128)(2,1)}), bf16[8,32,256]{2,1,0:T(8,128)(2,1)S(1)}, u32[]{:S(2)}, u32[]{:S(2)}) async-start(bf16[8,32,256]{2,1,0:T(8,128)(2,1)} %get-tuple-element.26), calls=%async_computation.4 | async-start | bytes 262144 | tf_op jit(solution)/shard_map/all_to_all | solution.py:490
  72.1 2.7 %near.7.base_ref = f32[32,2048]{1,0:T(8,128)S(1)} custom-call(s32[128]{0:T(128)} %get-tuple-element.17.plan_ref, f8e4m3fn[96,512,256]{2,1,0:T(32,128)(4,1)} %get-tuple-element.18.packed_hbm, f32[8,2048]{1,0:T(8,128)S(1)} %get-tuple-element.20.scale_ref, f32[32,2048]{1,0:T(8,128)S(1)} %get-tuple-element.25.now_ref, ...), custom_call_target="tpu_custom_call" | custom-call | flops 268435456 | bytes 2097152 | tf_op jit(solution)/shard_map/near/pallas_call | solution.py:540
  74.7 3.0 %all-to-all-done.4.arrived_ref = bf16[8,32,256]{2,1,0:T(8,128)(2,1)S(1)} async-done(((bf16[8,32,256]{2,1,0:T(8,128)(2,1)}), bf16[8,32,256]{2,1,0:T(8,128)(2,1)S(1)}, u32[]{:S(2)}, u32[]{:S(2)}) %all-to-all-start.4) | async-done | bytes 131104 | tf_op jit(solution)/shard_map/all_to_all | solution.py:490
  77.8 3.5 %step.7.own_ref = f32[32,2048]{1,0:T(8,128)S(1)} custom-call(s32[128]{0:T(128)} %get-tuple-element.17.plan_ref, s32[8,1,8]{2,1,0:T(1,128)S(1)} %all-to-all-done.wanted_ref, f8e4m3fn[96,512,256]{2,1,0:T(32,128)(4,1)} %get-tuple-element.18.packed_hbm, f8e4m3fn[16,512,256]{2,1,0:T(32,128)(4,1)S(1)} %get-tuple-element.19.kept_ref, ...), custom_call_target="tpu_custom_call" | custom-call | tf_op jit(solution)/shard_map/step/pallas_call | solution.py:551
  81.3 1.6 %collective-permute-start.1 = (bf16[32,2048]{1,0:T(8,128)(2,1)S(1)}, bf16[32,2048]{1,0:T(8,128)(2,1)S(1)}, u32[]{:S(2)}, u32[]{:S(2)}) collective-permute-start(bf16[32,2048]{1,0:T(8,128)(2,1)S(1)} %convert_element_type.3), channel_id=1, source_target_pairs={{0,2},{1,3},{2,0},{3,1},{4,6},{5,7},{6,4},{7,5},{8,10},{9,11},{10,... | collective-permute-start | bytes 393224 | tf_op jit(solution)/shard_map/ppermute | solution.py:495
  82.9 3.5 %collective-permute-done.1.refs_1_ = bf16[32,2048]{1,0:T(8,128)(2,1)S(1)} collective-permute-done((bf16[32,2048]{1,0:T(8,128)(2,1)S(1)}, bf16[32,2048]{1,0:T(8,128)(2,1)S(1)}, u32[]{:S(2)}, u32[]{:S(2)}) %collective-permute-start.1) | collective-permute-done | bytes 131104 | tf_op jit(solution)/shard_map/ppermute | solution.py:495
  88.4 3.7 %collective-permute-done.3 = f32[64,128]{1,0:T(8,128)S(1)} collective-permute-done((f32[64,128]{1,0:T(8,128)S(1)}, f32[64,128]{1,0:T(8,128)S(1)}, u32[]{:S(2)}, u32[]{:S(2)}) %collective-permute-start.3) | collective-permute-done | bytes 32800 | tf_op jit(solution)/shard_map/ppermute | solution.py:495
  92.1 1.4 %collective-permute-start.6 = (f32[64,128]{1,0:T(8,128)S(1)}, f32[64,128]{1,0:T(8,128)S(1)}, u32[]{:S(2)}, u32[]{:S(2)}) collective-permute-start(f32[64,128]{1,0:T(8,128)S(1)} %add.3.refs_0_), channel_id=1, source_target_pairs={{0,24},{4,28},{8,16},{12,20},{16,8},{20,12},{24,0},{28,4},{1,25},{... | collective-permute-start | bytes 98312 | tf_op jit(solution)/shard_map/ppermute | solution.py:495
  93.6 2.9 %collective-permute-start.4 = (f32[64,128]{1,0:T(8,128)S(1)}, f32[64,128]{1,0:T(8,128)S(1)}, u32[]{:S(2)}, u32[]{:S(2)}) collective-permute-start(f32[64,128]{1,0:T(8,128)S(1)} %add.3.refs_0_), channel_id=1, source_target_pairs={{0,8},{4,12},{8,0},{12,4},{16,24},{20,28},{24,16},{28,20},{1,9},{5... | collective-permute-start | bytes 98312 | tf_op jit(solution)/shard_map/ppermute | solution.py:495
  98.8 6.2 %factor.1 = f32[32,2048]{1,0:T(8,128)} custom-call(f32[32,2048]{1,0:T(8,128)S(1)} %step.7.own_ref, bf16[4,32,2048]{2,1,0:T(8,128)(2,1)S(1)} %get-tuple-element.27.all_ref, f32[64,128]{1,0:T(8,128)S(1)} %add.3.refs_0_, f32[64,128]{1,0:T(8,128)S(1)} %collective-permute-done.4.refs_1_, f32[64,128]{1,0:T(8,128)S(1)} %collective-permute-done.5.refs_2_, ...), custom_call_target="tpu_custom_call" | custom-call | tf_op jit(solution)/shard_map/factor/pallas_call | solution.py:581
  (17 shorter events, 6.9 us)
Async XLA Ops:
  1.2 24.4 %all-to-all-start = ((s32[8,1,8]{2,1,0:T(1,128)}), s32[8,1,8]{2,1,0:T(1,128)S(1)}, u32[]{:S(2)}, u32[]{:S(2)}) async-start(s32[8,1,8]{2,1,0:T(1,128)} %broadcast_in_dim.9), calls=%async_computation | async-start | bytes 8192 | tf_op jit(solution)/shard_map/all_to_all | solution.py:490
  9.1 16.6 %copy-start = (f32[32,2048]{1,0:T(8,128)S(1)}, f32[32,2048]{1,0:T(8,128)}, u32[]{:S(2)}) copy-start(f32[32,2048]{1,0:T(8,128)} %before_ref.3) | copy-start | bytes 786436
  26.9 11.1 %all-to-all-start.1 = ((bf16[8,32,256]{2,1,0:T(8,128)(2,1)}), bf16[8,32,256]{2,1,0:T(8,128)(2,1)S(1)}, u32[]{:S(2)}, u32[]{:S(2)}) async-start(bf16[8,32,256]{2,1,0:T(8,128)(2,1)} %first.1), calls=%async_computation.1 | async-start | bytes 262144 | tf_op jit(solution)/shard_map/all_to_all | solution.py:490
  42.2 9.1 %all-to-all-start.2 = ((bf16[8,32,256]{2,1,0:T(8,128)(2,1)}), bf16[8,32,256]{2,1,0:T(8,128)(2,1)S(1)}, u32[]{:S(2)}, u32[]{:S(2)}) async-start(bf16[8,32,256]{2,1,0:T(8,128)(2,1)} %get-tuple-element.22), calls=%async_computation.2 | async-start | bytes 262144 | tf_op jit(solution)/shard_map/all_to_all | solution.py:490
  55.5 9.1 %all-to-all-start.3 = ((bf16[8,32,256]{2,1,0:T(8,128)(2,1)}), bf16[8,32,256]{2,1,0:T(8,128)(2,1)S(1)}, u32[]{:S(2)}, u32[]{:S(2)}) async-start(bf16[8,32,256]{2,1,0:T(8,128)(2,1)} %get-tuple-element.24), calls=%async_computation.3 | async-start | bytes 262144 | tf_op jit(solution)/shard_map/all_to_all | solution.py:490
  68.7 9.1 %all-to-all-start.4 = ((bf16[8,32,256]{2,1,0:T(8,128)(2,1)}), bf16[8,32,256]{2,1,0:T(8,128)(2,1)S(1)}, u32[]{:S(2)}, u32[]{:S(2)}) async-start(bf16[8,32,256]{2,1,0:T(8,128)(2,1)} %get-tuple-element.26), calls=%async_computation.4 | async-start | bytes 262144 | tf_op jit(solution)/shard_map/all_to_all | solution.py:490
  81.3 5.0 %collective-permute-start.1 = (bf16[32,2048]{1,0:T(8,128)(2,1)S(1)}, bf16[32,2048]{1,0:T(8,128)(2,1)S(1)}, u32[]{:S(2)}, u32[]{:S(2)}) collective-permute-start(bf16[32,2048]{1,0:T(8,128)(2,1)S(1)} %convert_element_type.3), channel_id=1, source_target_pairs={{0,2},{1,3},{2,0},{3,1},{4,6},{5,7},{6,4},{7,5},{8,10},{9,11},{10,... | collective-permute-start | bytes 393224 | tf_op jit(solution)/shard_map/ppermute | solution.py:495
  82.9 3.5 %collective-permute-start = (bf16[32,2048]{1,0:T(8,128)(2,1)S(1)}, bf16[32,2048]{1,0:T(8,128)(2,1)S(1)}, u32[]{:S(2)}, u32[]{:S(2)}) collective-permute-start(bf16[32,2048]{1,0:T(8,128)(2,1)S(1)} %convert_element_type.3), channel_id=1, source_target_pairs={{0,1},{1,0},{2,3},{3,2},{4,5},{5,4},{6,7},{7,6},{8,9},{9,8},{10,11... | collective-permute-start | bytes 393224 | tf_op jit(solution)/shard_map/ppermute | solution.py:495
  86.4 1.3 %collective-permute-start.2 = (bf16[32,2048]{1,0:T(8,128)(2,1)S(1)}, bf16[32,2048]{1,0:T(8,128)(2,1)S(1)}, u32[]{:S(2)}, u32[]{:S(2)}) collective-permute-start(bf16[32,2048]{1,0:T(8,128)(2,1)S(1)} %collective-permute-done.1.refs_1_), channel_id=1, source_target_pairs={{0,1},{1,0},{2,3},{3,2},{4,5},{5,4},{6,7},{7,6},{8,9},{9,8},{10,11... | collective-permute-start | bytes 393224 | tf_op jit(solution)/shard_map/ppermute | solution.py:495
  88.1 4.0 %collective-permute-start.3 = (f32[64,128]{1,0:T(8,128)S(1)}, f32[64,128]{1,0:T(8,128)S(1)}, u32[]{:S(2)}, u32[]{:S(2)}) collective-permute-start(f32[64,128]{1,0:T(8,128)S(1)} %get-tuple-element.28), channel_id=1, source_target_pairs={{0,4},{4,0},{8,12},{12,8},{16,20},{20,16},{24,28},{28,24},{1,5},{5... | collective-permute-start | bytes 98312 | tf_op jit(solution)/shard_map/ppermute | solution.py:495
  92.1 5.7 %collective-permute-start.6 = (f32[64,128]{1,0:T(8,128)S(1)}, f32[64,128]{1,0:T(8,128)S(1)}, u32[]{:S(2)}, u32[]{:S(2)}) collective-permute-start(f32[64,128]{1,0:T(8,128)S(1)} %add.3.refs_0_), channel_id=1, source_target_pairs={{0,24},{4,28},{8,16},{12,20},{16,8},{20,12},{24,0},{28,4},{1,25},{... | collective-permute-start | bytes 98312 | tf_op jit(solution)/shard_map/ppermute | solution.py:495
  93.5 5.1 %collective-permute-start.5 = (f32[64,128]{1,0:T(8,128)S(1)}, f32[64,128]{1,0:T(8,128)S(1)}, u32[]{:S(2)}, u32[]{:S(2)}) collective-permute-start(f32[64,128]{1,0:T(8,128)S(1)} %add.3.refs_0_), channel_id=1, source_target_pairs={{0,16},{4,20},{8,24},{12,28},{16,0},{20,4},{24,8},{28,12},{1,17},{... | collective-permute-start | bytes 98312 | tf_op jit(solution)/shard_map/ppermute | solution.py:495
  93.6 5.1 %collective-permute-start.4 = (f32[64,128]{1,0:T(8,128)S(1)}, f32[64,128]{1,0:T(8,128)S(1)}, u32[]{:S(2)}, u32[]{:S(2)}) collective-permute-start(f32[64,128]{1,0:T(8,128)S(1)} %add.3.refs_0_), channel_id=1, source_target_pairs={{0,8},{4,12},{8,0},{12,4},{16,24},{20,28},{24,16},{28,20},{1,9},{5... | collective-permute-start | bytes 98312 | tf_op jit(solution)/shard_map/ppermute | solution.py:495

commit v12 on v11

--- a/solution.py
+++ b/solution.py
@@ -170,8 +170,8 @@
                 return back_ref[earlier]
 
             lax.while_loop(lambda earlier: earlier >= 0, add, back_ref[partner])
-            small = (both_ref[t] + both_ref[partner]).astype(F8)
-            put(listed, skip, jnp.concatenate([small[:, :order].T, small[:, order:].T], axis=0))
+            total = both_ref[t] + both_ref[partner]
+            put(listed, skip, jnp.concatenate([total[:, :order].T, total[:, order:].T], axis=0).astype(F8))
             slot = slots_ref[t]
             place = rb_dev + ((slot - rb_dev) ^ central(slots - rb_dev))
             plan_ref[listed] = row | (jnp.where(slot < rb_dev, slot, place) << 8)

time: 106 us -> 108 us (1.019)
  starting transfers between devices: 29.5 us -> 31.3 us
    pallas_call x1, Pallas kernels: 16.5 us -> 18 us  [tiles_call(): pl.pallas_call(functools.partial(tiles_kernel, near_count), name='tiles',...]
    all_to_all x5, starting transfers between devices: 23.2 us -> 24.6 us  [exchange(): lax.all_to_all(x, 'blk', split_axis=0, concat_axis=0, tiled=True, axis_in...]
  transfers between devices with their start and end apart: 12 -> 12, of which waited for: 10 -> 9; matrix products, arithmetic and copies ran while one was open for 0% -> 0% of each run, Pallas kernels for 26% -> 27%
where the time goes in v12:
time: 108 us; the launch traced here: 107 us
  Pallas kernels  51.9 us (48%)
  starting transfers between devices  31.3 us (29%)
  waiting for transfers between devices  22.6 us (21%)
  local copies, waits for them, and re-layouts  1.25 us (1%)
    all_to_all x5, starting transfers between devices, exchange(): lax.all_to_all(x, 'blk', split_axis=0, concat_axis=0, tiled=True, axis_in...  24.6 us
    pallas_call x1, Pallas kernels, tiles_call(): pl.pallas_call(functools.partial(tiles_kernel, near_count), name='tiles',...  18 us
    pallas_call x4, Pallas kernels, per_device(): pl.pallas_call(functools.partial(step_kernel, step), name='step', out_sha...  15.2 us
    all_to_all x5, waiting for transfers between devices, exchange(): lax.all_to_all(x, 'blk', split_axis=0, concat_axis=0, tiled=True, axis_in...  12.2 us
    pallas_call x4, Pallas kernels, per_device(): pl.pallas_call(functools.partial(near_kernel, step), name='near', out_sha...  10.6 us
    ppermute x7, waiting for transfers between devices, to_partner(): return lax.ppermute(x, axis, [(i, i ^ mask) for i in range(n)])  10.4 us
    ppermute x7, starting transfers between devices, to_partner(): return lax.ppermute(x, axis, [(i, i ^ mask) for i in range(n)])  6.64 us
    pallas_call x1, Pallas kernels, per_device(): pl.pallas_call(functools.partial(factor_kernel, rows * nblk), name='facto...  6.24 us
  transfers between devices with their start and end apart: 12, of which 9 were waited for; matrix products, arithmetic and copies ran while one was open for 0% of the time, Pallas kernels for 27%

profile of v12, /device:TPU:0, one launch (start us, length us, event | category | flops | bytes accessed | tf_op | source)
XLA Modules:
  0.0 107.1 jit_solution(72152175857586129)
XLA Ops:
  1.2 7.8 %all-to-all-start = ((s32[8,1,8]{2,1,0:T(1,128)}), s32[8,1,8]{2,1,0:T(1,128)S(1)}, u32[]{:S(2)}, u32[]{:S(2)}) async-start(s32[8,1,8]{2,1,0:T(1,128)} %broadcast_in_dim.9), calls=%async_computation | async-start | bytes 8192 | tf_op jit(solution)/shard_map/all_to_all | solution.py:490
  9.1 18.0 %tiles.1 = (f8e4m3fn[96,512,256]{2,1,0:T(32,128)(4,1)}, f8e4m3fn[16,512,256]{2,1,0:T(32,128)(4,1)S(1)}, f32[8,2048]{1,0:T(8,128)S(1)}, s32[128]{0:T(128)}) custom-call(s32[96]{0:T(128)} %rows_hbm.1, s32[96]{0:T(128)} %slots_hbm.1, bf16[96,256,256]{2,1,0:T(8,128)(2,1)} %real_hbm.1, bf16[96,256,256]{2,1,0:T(8,128)(2,1)} %imag_hbm.1), custom_call_target="tpu_custom_call" | custom-call | flops 268435456 | bytes 25165824 | tf_op jit(solution)/shard_map/tiles/pallas_call | solution.py:233
  28.5 5.6 %all-to-all-start.1 = ((bf16[8,32,256]{2,1,0:T(8,128)(2,1)}), bf16[8,32,256]{2,1,0:T(8,128)(2,1)S(1)}, u32[]{:S(2)}, u32[]{:S(2)}) async-start(bf16[8,32,256]{2,1,0:T(8,128)(2,1)} %first.1), calls=%async_computation.1 | async-start | bytes 262144 | tf_op jit(solution)/shard_map/all_to_all | solution.py:490
  34.0 2.6 %near.4.base_ref = f32[32,2048]{1,0:T(8,128)S(1)} custom-call(s32[128]{0:T(128)} %get-tuple-element.17.plan_ref, f8e4m3fn[96,512,256]{2,1,0:T(32,128)(4,1)} %get-tuple-element.18.packed_hbm, f32[8,2048]{1,0:T(8,128)S(1)} %get-tuple-element.20.scale_ref, f32[32,2048]{1,0:T(8,128)S(1)} %copy-done, f32[32,2048]{1,0:T(8,128)S(1)} %copy-done), custom_call_target="tpu_custom_call" | custom-call | flops 268435456 | bytes 2097152 | tf_op jit(solution)/shard_map/near/pallas_call | solution.py:540
  36.7 3.1 %all-to-all-done.1.arrived_ref = bf16[8,32,256]{2,1,0:T(8,128)(2,1)S(1)} async-done(((bf16[8,32,256]{2,1,0:T(8,128)(2,1)}), bf16[8,32,256]{2,1,0:T(8,128)(2,1)S(1)}, u32[]{:S(2)}, u32[]{:S(2)}) %all-to-all-start.1) | async-done | bytes 131104 | tf_op jit(solution)/shard_map/all_to_all | solution.py:490
  39.8 4.0 %step.4 = (f32[32,2048]{1,0:T(8,128)S(1)}, bf16[8,32,256]{2,1,0:T(8,128)(2,1)}) custom-call(s32[128]{0:T(128)} %get-tuple-element.17.plan_ref, s32[8,1,8]{2,1,0:T(1,128)S(1)} %all-to-all-done.wanted_ref, f8e4m3fn[96,512,256]{2,1,0:T(32,128)(4,1)} %get-tuple-element.18.packed_hbm, f8e4m3fn[16,512,256]{2,1,0:T(32,128)(4,1)S(1)} %get-tuple-element.19.kept_ref, ...), custom_call_target="tpu_custom_call" | custom-call | tf_op jit(solution)/shard_map/step/pallas_call | solution.py:551
  43.7 3.7 %all-to-all-start.2 = ((bf16[8,32,256]{2,1,0:T(8,128)(2,1)}), bf16[8,32,256]{2,1,0:T(8,128)(2,1)S(1)}, u32[]{:S(2)}, u32[]{:S(2)}) async-start(bf16[8,32,256]{2,1,0:T(8,128)(2,1)} %get-tuple-element.22), calls=%async_computation.2 | async-start | bytes 262144 | tf_op jit(solution)/shard_map/all_to_all | solution.py:490
  47.5 2.7 %near.5.base_ref = f32[32,2048]{1,0:T(8,128)S(1)} custom-call(s32[128]{0:T(128)} %get-tuple-element.17.plan_ref, f8e4m3fn[96,512,256]{2,1,0:T(32,128)(4,1)} %get-tuple-element.18.packed_hbm, f32[8,2048]{1,0:T(8,128)S(1)} %get-tuple-element.20.scale_ref, f32[32,2048]{1,0:T(8,128)S(1)} %get-tuple-element.21.now_ref.before_ref, f32[32,2048]{1,0:T(8,128)S(1)} %copy-done), custom_call_target="tpu_custom_call" | custom-call | flops 268435456 | bytes 2097152 | tf_op jit(solution)/shard_map/near/pallas_call | solution.py:540
  50.1 3.1 %all-to-all-done.2.arrived_ref = bf16[8,32,256]{2,1,0:T(8,128)(2,1)S(1)} async-done(((bf16[8,32,256]{2,1,0:T(8,128)(2,1)}), bf16[8,32,256]{2,1,0:T(8,128)(2,1)S(1)}, u32[]{:S(2)}, u32[]{:S(2)}) %all-to-all-start.2) | async-done | bytes 131104 | tf_op jit(solution)/shard_map/all_to_all | solution.py:490
  53.2 4.0 %step.5 = (f32[32,2048]{1,0:T(8,128)S(1)}, bf16[8,32,256]{2,1,0:T(8,128)(2,1)}) custom-call(s32[128]{0:T(128)} %get-tuple-element.17.plan_ref, s32[8,1,8]{2,1,0:T(1,128)S(1)} %all-to-all-done.wanted_ref, f8e4m3fn[96,512,256]{2,1,0:T(32,128)(4,1)} %get-tuple-element.18.packed_hbm, f8e4m3fn[16,512,256]{2,1,0:T(32,128)(4,1)S(1)} %get-tuple-element.19.kept_ref, ...), custom_call_target="tpu_custom_call" | custom-call | tf_op jit(solution)/shard_map/step/pallas_call | solution.py:551
  57.2 3.7 %all-to-all-start.3 = ((bf16[8,32,256]{2,1,0:T(8,128)(2,1)}), bf16[8,32,256]{2,1,0:T(8,128)(2,1)S(1)}, u32[]{:S(2)}, u32[]{:S(2)}) async-start(bf16[8,32,256]{2,1,0:T(8,128)(2,1)} %get-tuple-element.24), calls=%async_computation.3 | async-start | bytes 262144 | tf_op jit(solution)/shard_map/all_to_all | solution.py:490
  60.9 2.7 %near.6.base_ref = f32[32,2048]{1,0:T(8,128)S(1)} custom-call(s32[128]{0:T(128)} %get-tuple-element.17.plan_ref, f8e4m3fn[96,512,256]{2,1,0:T(32,128)(4,1)} %get-tuple-element.18.packed_hbm, f32[8,2048]{1,0:T(8,128)S(1)} %get-tuple-element.20.scale_ref, f32[32,2048]{1,0:T(8,128)S(1)} %get-tuple-element.23.now_ref.before_ref, ...), custom_call_target="tpu_custom_call" | custom-call | flops 268435456 | bytes 2097152 | tf_op jit(solution)/shard_map/near/pallas_call | solution.py:540
  63.6 3.1 %all-to-all-done.3.arrived_ref = bf16[8,32,256]{2,1,0:T(8,128)(2,1)S(1)} async-done(((bf16[8,32,256]{2,1,0:T(8,128)(2,1)}), bf16[8,32,256]{2,1,0:T(8,128)(2,1)S(1)}, u32[]{:S(2)}, u32[]{:S(2)}) %all-to-all-start.3) | async-done | bytes 131104 | tf_op jit(solution)/shard_map/all_to_all | solution.py:490
  66.7 4.0 %step.6 = (f32[32,2048]{1,0:T(8,128)S(1)}, bf16[8,32,256]{2,1,0:T(8,128)(2,1)}) custom-call(s32[128]{0:T(128)} %get-tuple-element.17.plan_ref, s32[8,1,8]{2,1,0:T(1,128)S(1)} %all-to-all-done.wanted_ref, f8e4m3fn[96,512,256]{2,1,0:T(32,128)(4,1)} %get-tuple-element.18.packed_hbm, f8e4m3fn[16,512,256]{2,1,0:T(32,128)(4,1)S(1)} %get-tuple-element.19.kept_ref, ...), custom_call_target="tpu_custom_call" | custom-call | tf_op jit(solution)/shard_map/step/pallas_call | solution.py:551
  70.6 3.7 %all-to-all-start.4 = ((bf16[8,32,256]{2,1,0:T(8,128)(2,1)}), bf16[8,32,256]{2,1,0:T(8,128)(2,1)S(1)}, u32[]{:S(2)}, u32[]{:S(2)}) async-start(bf16[8,32,256]{2,1,0:T(8,128)(2,1)} %get-tuple-element.26), calls=%async_computation.4 | async-start | bytes 262144 | tf_op jit(solution)/shard_map/all_to_all | solution.py:490
  74.4 2.7 %near.7.base_ref = f32[32,2048]{1,0:T(8,128)S(1)} custom-call(s32[128]{0:T(128)} %get-tuple-element.17.plan_ref, f8e4m3fn[96,512,256]{2,1,0:T(32,128)(4,1)} %get-tuple-element.18.packed_hbm, f32[8,2048]{1,0:T(8,128)S(1)} %get-tuple-element.20.scale_ref, f32[32,2048]{1,0:T(8,128)S(1)} %get-tuple-element.25.now_ref, ...), custom_call_target="tpu_custom_call" | custom-call | flops 268435456 | bytes 2097152 | tf_op jit(solution)/shard_map/near/pallas_call | solution.py:540
  77.1 3.1 %all-to-all-done.4.arrived_ref = bf16[8,32,256]{2,1,0:T(8,128)(2,1)S(1)} async-done(((bf16[8,32,256]{2,1,0:T(8,128)(2,1)}), bf16[8,32,256]{2,1,0:T(8,128)(2,1)S(1)}, u32[]{:S(2)}, u32[]{:S(2)}) %all-to-all-start.4) | async-done | bytes 131104 | tf_op jit(solution)/shard_map/all_to_all | solution.py:490
  80.1 3.3 %step.7.own_ref = f32[32,2048]{1,0:T(8,128)S(1)} custom-call(s32[128]{0:T(128)} %get-tuple-element.17.plan_ref, s32[8,1,8]{2,1,0:T(1,128)S(1)} %all-to-all-done.wanted_ref, f8e4m3fn[96,512,256]{2,1,0:T(32,128)(4,1)} %get-tuple-element.18.packed_hbm, f8e4m3fn[16,512,256]{2,1,0:T(32,128)(4,1)S(1)} %get-tuple-element.19.kept_ref, ...), custom_call_target="tpu_custom_call" | custom-call | tf_op jit(solution)/shard_map/step/pallas_call | solution.py:551
  83.4 1.6 %collective-permute-start.1 = (bf16[32,2048]{1,0:T(8,128)(2,1)S(1)}, bf16[32,2048]{1,0:T(8,128)(2,1)S(1)}, u32[]{:S(2)}, u32[]{:S(2)}) collective-permute-start(bf16[32,2048]{1,0:T(8,128)(2,1)S(1)} %convert_element_type.3), channel_id=1, source_target_pairs={{0,2},{1,3},{2,0},{3,1},{4,6},{5,7},{6,4},{7,5},{8,10},{9,11},{10,... | collective-permute-start | bytes 393224 | tf_op jit(solution)/shard_map/ppermute | solution.py:495
  85.0 3.5 %collective-permute-done.1.refs_1_ = bf16[32,2048]{1,0:T(8,128)(2,1)S(1)} collective-permute-done((bf16[32,2048]{1,0:T(8,128)(2,1)S(1)}, bf16[32,2048]{1,0:T(8,128)(2,1)S(1)}, u32[]{:S(2)}, u32[]{:S(2)}) %collective-permute-start.1) | collective-permute-done | bytes 131104 | tf_op jit(solution)/shard_map/ppermute | solution.py:495
  90.9 3.3 %collective-permute-done.3 = f32[64,128]{1,0:T(8,128)S(1)} collective-permute-done((f32[64,128]{1,0:T(8,128)S(1)}, f32[64,128]{1,0:T(8,128)S(1)}, u32[]{:S(2)}, u32[]{:S(2)}) %collective-permute-start.3) | collective-permute-done | bytes 32800 | tf_op jit(solution)/shard_map/ppermute | solution.py:495
  94.2 1.8 %collective-permute-start.6 = (f32[64,128]{1,0:T(8,128)S(1)}, f32[64,128]{1,0:T(8,128)S(1)}, u32[]{:S(2)}, u32[]{:S(2)}) collective-permute-start(f32[64,128]{1,0:T(8,128)S(1)} %add.3.refs_0_), channel_id=1, source_target_pairs={{0,24},{4,28},{8,16},{12,20},{16,8},{20,12},{24,0},{28,4},{1,25},{... | collective-permute-start | bytes 98312 | tf_op jit(solution)/shard_map/ppermute | solution.py:495
  96.1 2.5 %collective-permute-start.4 = (f32[64,128]{1,0:T(8,128)S(1)}, f32[64,128]{1,0:T(8,128)S(1)}, u32[]{:S(2)}, u32[]{:S(2)}) collective-permute-start(f32[64,128]{1,0:T(8,128)S(1)} %add.3.refs_0_), channel_id=1, source_target_pairs={{0,8},{4,12},{8,0},{12,4},{16,24},{20,28},{24,16},{28,20},{1,9},{5... | collective-permute-start | bytes 98312 | tf_op jit(solution)/shard_map/ppermute | solution.py:495
  100.9 6.2 %factor.1 = f32[32,2048]{1,0:T(8,128)} custom-call(f32[32,2048]{1,0:T(8,128)S(1)} %step.7.own_ref, bf16[4,32,2048]{2,1,0:T(8,128)(2,1)S(1)} %get-tuple-element.27.all_ref, f32[64,128]{1,0:T(8,128)S(1)} %add.3.refs_0_, f32[64,128]{1,0:T(8,128)S(1)} %collective-permute-done.4.refs_1_, f32[64,128]{1,0:T(8,128)S(1)} %collective-permute-done.5.refs_2_, ...), custom_call_target="tpu_custom_call" | custom-call | tf_op jit(solution)/shard_map/factor/pallas_call | solution.py:581
  (17 shorter events, 7.4 us)
Async XLA Ops:
  1.2 25.9 %all-to-all-start = ((s32[8,1,8]{2,1,0:T(1,128)}), s32[8,1,8]{2,1,0:T(1,128)S(1)}, u32[]{:S(2)}, u32[]{:S(2)}) async-start(s32[8,1,8]{2,1,0:T(1,128)} %broadcast_in_dim.9), calls=%async_computation | async-start | bytes 8192 | tf_op jit(solution)/shard_map/all_to_all | solution.py:490
  9.1 18.1 %copy-start = (f32[32,2048]{1,0:T(8,128)S(1)}, f32[32,2048]{1,0:T(8,128)}, u32[]{:S(2)}) copy-start(f32[32,2048]{1,0:T(8,128)} %before_ref.3) | copy-start | bytes 786436
  28.5 11.3 %all-to-all-start.1 = ((bf16[8,32,256]{2,1,0:T(8,128)(2,1)}), bf16[8,32,256]{2,1,0:T(8,128)(2,1)S(1)}, u32[]{:S(2)}, u32[]{:S(2)}) async-start(bf16[8,32,256]{2,1,0:T(8,128)(2,1)} %first.1), calls=%async_computation.1 | async-start | bytes 262144 | tf_op jit(solution)/shard_map/all_to_all | solution.py:490
  43.7 9.5 %all-to-all-start.2 = ((bf16[8,32,256]{2,1,0:T(8,128)(2,1)}), bf16[8,32,256]{2,1,0:T(8,128)(2,1)S(1)}, u32[]{:S(2)}, u32[]{:S(2)}) async-start(bf16[8,32,256]{2,1,0:T(8,128)(2,1)} %get-tuple-element.22), calls=%async_computation.2 | async-start | bytes 262144 | tf_op jit(solution)/shard_map/all_to_all | solution.py:490
  57.2 9.5 %all-to-all-start.3 = ((bf16[8,32,256]{2,1,0:T(8,128)(2,1)}), bf16[8,32,256]{2,1,0:T(8,128)(2,1)S(1)}, u32[]{:S(2)}, u32[]{:S(2)}) async-start(bf16[8,32,256]{2,1,0:T(8,128)(2,1)} %get-tuple-element.24), calls=%async_computation.3 | async-start | bytes 262144 | tf_op jit(solution)/shard_map/all_to_all | solution.py:490
  70.6 9.5 %all-to-all-start.4 = ((bf16[8,32,256]{2,1,0:T(8,128)(2,1)}), bf16[8,32,256]{2,1,0:T(8,128)(2,1)S(1)}, u32[]{:S(2)}, u32[]{:S(2)}) async-start(bf16[8,32,256]{2,1,0:T(8,128)(2,1)} %get-tuple-element.26), calls=%async_computation.4 | async-start | bytes 262144 | tf_op jit(solution)/shard_map/all_to_all | solution.py:490
  83.4 5.0 %collective-permute-start.1 = (bf16[32,2048]{1,0:T(8,128)(2,1)S(1)}, bf16[32,2048]{1,0:T(8,128)(2,1)S(1)}, u32[]{:S(2)}, u32[]{:S(2)}) collective-permute-start(bf16[32,2048]{1,0:T(8,128)(2,1)S(1)} %convert_element_type.3), channel_id=1, source_target_pairs={{0,2},{1,3},{2,0},{3,1},{4,6},{5,7},{6,4},{7,5},{8,10},{9,11},{10,... | collective-permute-start | bytes 393224 | tf_op jit(solution)/shard_map/ppermute | solution.py:495
  85.0 3.5 %collective-permute-start = (bf16[32,2048]{1,0:T(8,128)(2,1)S(1)}, bf16[32,2048]{1,0:T(8,128)(2,1)S(1)}, u32[]{:S(2)}, u32[]{:S(2)}) collective-permute-start(bf16[32,2048]{1,0:T(8,128)(2,1)S(1)} %convert_element_type.3), channel_id=1, source_target_pairs={{0,1},{1,0},{2,3},{3,2},{4,5},{5,4},{6,7},{7,6},{8,9},{9,8},{10,11... | collective-permute-start | bytes 393224 | tf_op jit(solution)/shard_map/ppermute | solution.py:495
  88.5 1.3 %collective-permute-start.2 = (bf16[32,2048]{1,0:T(8,128)(2,1)S(1)}, bf16[32,2048]{1,0:T(8,128)(2,1)S(1)}, u32[]{:S(2)}, u32[]{:S(2)}) collective-permute-start(bf16[32,2048]{1,0:T(8,128)(2,1)S(1)} %collective-permute-done.1.refs_1_), channel_id=1, source_target_pairs={{0,1},{1,0},{2,3},{3,2},{4,5},{5,4},{6,7},{7,6},{8,9},{9,8},{10,11... | collective-permute-start | bytes 393224 | tf_op jit(solution)/shard_map/ppermute | solution.py:495
  90.3 4.0 %collective-permute-start.3 = (f32[64,128]{1,0:T(8,128)S(1)}, f32[64,128]{1,0:T(8,128)S(1)}, u32[]{:S(2)}, u32[]{:S(2)}) collective-permute-start(f32[64,128]{1,0:T(8,128)S(1)} %get-tuple-element.28), channel_id=1, source_target_pairs={{0,4},{4,0},{8,12},{12,8},{16,20},{20,16},{24,28},{28,24},{1,5},{5... | collective-permute-start | bytes 98312 | tf_op jit(solution)/shard_map/ppermute | solution.py:495
  94.2 5.9 %collective-permute-start.6 = (f32[64,128]{1,0:T(8,128)S(1)}, f32[64,128]{1,0:T(8,128)S(1)}, u32[]{:S(2)}, u32[]{:S(2)}) collective-permute-start(f32[64,128]{1,0:T(8,128)S(1)} %add.3.refs_0_), channel_id=1, source_target_pairs={{0,24},{4,28},{8,16},{12,20},{16,8},{20,12},{24,0},{28,4},{1,25},{... | collective-permute-start | bytes 98312 | tf_op jit(solution)/shard_map/ppermute | solution.py:495
  96.1 4.8 %collective-permute-start.5 = (f32[64,128]{1,0:T(8,128)S(1)}, f32[64,128]{1,0:T(8,128)S(1)}, u32[]{:S(2)}, u32[]{:S(2)}) collective-permute-start(f32[64,128]{1,0:T(8,128)S(1)} %add.3.refs_0_), channel_id=1, source_target_pairs={{0,16},{4,20},{8,24},{12,28},{16,0},{20,4},{24,8},{28,12},{1,17},{... | collective-permute-start | bytes 98312 | tf_op jit(solution)/shard_map/ppermute | solution.py:495
  96.1 4.7 %collective-permute-start.4 = (f32[64,128]{1,0:T(8,128)S(1)}, f32[64,128]{1,0:T(8,128)S(1)}, u32[]{:S(2)}, u32[]{:S(2)}) collective-permute-start(f32[64,128]{1,0:T(8,128)S(1)} %add.3.refs_0_), channel_id=1, source_target_pairs={{0,8},{4,12},{8,0},{12,4},{16,24},{20,28},{24,16},{28,20},{1,9},{5... | collective-permute-start | bytes 98312 | tf_op jit(solution)/shard_map/ppermute | solution.py:495

commit v13 on v10

--- a/solution.py
+++ b/solution.py
@@ -138,7 +138,8 @@
     lax.fori_loop(0, tiles, link, 0)
 
     def turned(tile):
-        return jnp.concatenate([tile[:, :order].T, tile[:, order:].T], axis=0).astype(F8)
+        small = tile.astype(F8)
+        return jnp.concatenate([small[:, :order].T, small[:, order:].T], axis=0)
 
     def put(e, skip, value):
         @pl.when(e < skip)
@@ -252,16 +253,22 @@
     return (field[:, at] * scale_ref[0:1, at]).astype(BF16)
 
 
-def send_picked(wanted_ref, sent_ref, out_ref):
+def send_picked(wanted_ref, sent_ref, out_hbm, sems):
     me = lax.axis_index("blk")
-    for i in range(out_ref.shape[0]):
-        out_ref[i] = sent_ref[wanted_ref[i, 0, me]]
-
-
-def first_kernel(y_ref, scale_ref, wanted_ref, out_ref, sent_ref):
+    copies = [
+        pltpu.make_async_copy(sent_ref.at[wanted_ref[i, 0, me]], out_hbm.at[i], sems.at[i])
+        for i in range(out_hbm.shape[0])
+    ]
+    for copy in copies:
+        copy.start()
+    for copy in copies:
+        copy.wait()
+
+
+def first_kernel(y_ref, scale_ref, wanted_ref, out_hbm, sent_ref, out_sems):
     for r in range(sent_ref.shape[0]):
         sent_ref[r] = rounded_block(y_ref, scale_ref, r, sent_ref.shape[2])
-    send_picked(wanted_ref, sent_ref, out_ref)
+    send_picked(wanted_ref, sent_ref, out_hbm, out_sems)
 
 
 def load_groups(packed_hbm, tiles_ref, sems, lo, hi):
@@ -350,7 +357,7 @@
     last = step == STEPS - 1
     next_ref = refs[0]
     if not last:
-        out_ref, sent_ref = refs[1:3]
+        out_hbm, sent_ref, out_sems = refs[1:4]
     tiles_ref, x_ref, acc_ref, sems = refs[-4:]
     rb_dev, _, order = acc_ref.shape
     end = plan_ref.shape[0] - 32
@@ -372,7 +379,7 @@
         if not last:
             sent_ref[r] = (following * scale).astype(BF16)
     if not last:
-        send_picked(wanted_ref, sent_ref, out_ref)
+        send_picked(wanted_ref, sent_ref, out_hbm, out_sems)
 
 
 def all_rows(own_ref, arrived, all_ref):
@@ -500,15 +507,15 @@
     wanted = exchange(jnp.broadcast_to(fetch_pick[None], (nblk, 1, nblk)))
     packed, kept, scale, plan = tiles_call(tile_rows, tile_slots, tile_real, tile_imag, rb_dev, near_count)
 
-    out_blocks = sds((nblk, group, order), BF16)
-    sent_scratch = pltpu.VMEM((rb_dev, group, order), BF16)
+    out_blocks = pltpu.HBM((nblk, group, order), BF16)
+    sent_scratch = [pltpu.VMEM((rb_dev, group, order), BF16), pltpu.SemaphoreType.DMA((nblk,))]
     blocks = pl.pallas_call(
         first_kernel,
         name="first",
         out_shape=out_blocks,
         in_specs=[VMEM, VMEM, SMEM],
-        out_specs=VMEM,
-        scratch_shapes=[sent_scratch],
+        out_specs=ANY,
+        scratch_shapes=sent_scratch,
         compiler_params=params(LIMIT),
     )(y_start, scale, wanted)
 
@@ -540,8 +547,8 @@
             name="step",
             out_shape=[vectors_here] if last else [vectors_here, out_blocks],
             in_specs=[SMEM, SMEM, ANY] + [VMEM] * 4,
-            out_specs=[VMEM] if last else [VMEM, VMEM],
-            scratch_shapes=([] if last else [sent_scratch]) + scratch(tiles - near_count - KEPT, nblk),
+            out_specs=[VMEM] if last else [VMEM, ANY],
+            scratch_shapes=([] if last else sent_scratch) + scratch(tiles - near_count - KEPT, nblk),
             compiler_params=params(LIMIT),
         )(in_hbm(plan), wanted, in_hbm(packed), pltpu.with_memory_space_constraint(kept, pltpu.VMEM), scale, base, arrived)
         previous, current = current, out[0]

time: 105 us -> 104 us (level)
  Pallas kernels: 50 us -> 47.6 us
    pallas_call x1, Pallas kernels: 15.3 us -> 13.6 us  [tiles_call(): pl.pallas_call(functools.partial(tiles_kernel, near_count), name='tiles',...]
  transfers between devices with their start and end apart: 12 -> 12, of which waited for: 10 -> 9; matrix products, arithmetic and copies ran while one was open for 0% -> 0% of each run, Pallas kernels for 25% -> 23%
where the time goes in v13:
time: 104 us; the launch traced here: 103 us
  Pallas kernels  47.6 us (46%)
  starting transfers between devices  30.2 us (29%)
  waiting for transfers between devices  23.8 us (23%)
  local copies, waits for them, and re-layouts  1.25 us (1%)
    all_to_all x5, starting transfers between devices, exchange(): lax.all_to_all(x, 'blk', split_axis=0, concat_axis=0, tiled=True, axis_in...  24 us
    pallas_call x4, Pallas kernels, per_device(): pl.pallas_call(functools.partial(step_kernel, step), name='step', out_sha...  16.2 us
    pallas_call x1, Pallas kernels, tiles_call(): pl.pallas_call(functools.partial(tiles_kernel, near_count), name='tiles',...  13.6 us
    all_to_all x5, waiting for transfers between devices, exchange(): lax.all_to_all(x, 'blk', split_axis=0, concat_axis=0, tiled=True, axis_in...  13 us
    ppermute x7, waiting for transfers between devices, to_partner(): return lax.ppermute(x, axis, [(i, i ^ mask) for i in range(n)])  10.8 us
    pallas_call x4, Pallas kernels, per_device(): pl.pallas_call(functools.partial(near_kernel, step), name='near', out_sha...  9.84 us
    pallas_call x1, Pallas kernels, per_device(): pl.pallas_call(functools.partial(factor_kernel, rows * nblk), name='facto...  6.24 us
    ppermute x7, starting transfers between devices, to_partner(): return lax.ppermute(x, axis, [(i, i ^ mask) for i in range(n)])  6.22 us
  transfers between devices with their start and end apart: 12, of which 9 were waited for; matrix products, arithmetic and copies ran while one was open for 0% of the time, Pallas kernels for 23%

profile of v13, /device:TPU:0, one launch (start us, length us, event | category | flops | bytes accessed | tf_op | source)
XLA Modules:
  0.0 103.0 jit_solution(9774073707762557981)
XLA Ops:
  1.2 7.8 %all-to-all-start = ((s32[8,1,8]{2,1,0:T(1,128)}), s32[8,1,8]{2,1,0:T(1,128)S(1)}, u32[]{:S(2)}, u32[]{:S(2)}) async-start(s32[8,1,8]{2,1,0:T(1,128)} %broadcast_in_dim.9), calls=%async_computation | async-start | bytes 8192 | tf_op jit(solution)/shard_map/all_to_all | solution.py:484
  9.1 13.6 %tiles.1 = (f8e4m3fn[96,512,256]{2,1,0:T(32,128)(4,1)}, f8e4m3fn[16,512,256]{2,1,0:T(32,128)(4,1)S(1)}, f32[8,2048]{1,0:T(8,128)S(1)}, s32[128]{0:T(128)}) custom-call(s32[96]{0:T(128)} %rows_hbm.1, s32[96]{0:T(128)} %slots_hbm.1, bf16[96,256,256]{2,1,0:T(8,128)(2,1)} %real_hbm.1, bf16[96,256,256]{2,1,0:T(8,128)(2,1)} %imag_hbm.1), custom_call_target="tpu_custom_call" | custom-call | flops 268435456 | bytes 25165824 | tf_op jit(solution)/shard_map/tiles/pallas_call | solution.py:221
  24.0 5.1 %all-to-all-start.1 = ((bf16[8,32,256]{2,1,0:T(8,128)(2,1)}), bf16[8,32,256]{2,1,0:T(8,128)(2,1)S(1)}, u32[]{:S(2)}, u32[]{:S(2)}) async-start(bf16[8,32,256]{2,1,0:T(8,128)(2,1)} %first.1), calls=%async_computation.1 | async-start | bytes 262144 | tf_op jit(solution)/shard_map/all_to_all | solution.py:484
  29.1 2.4 %near.4.base_ref = f32[32,2048]{1,0:T(8,128)S(1)} custom-call(s32[128]{0:T(128)} %get-tuple-element.17.plan_ref, f8e4m3fn[96,512,256]{2,1,0:T(32,128)(4,1)} %get-tuple-element.18.packed_hbm, f32[8,2048]{1,0:T(8,128)S(1)} %get-tuple-element.20.scale_ref, f32[32,2048]{1,0:T(8,128)S(1)} %copy-done, f32[32,2048]{1,0:T(8,128)S(1)} %copy-done), custom_call_target="tpu_custom_call" | custom-call | flops 268435456 | bytes 2097152 | tf_op jit(solution)/shard_map/near/pallas_call | solution.py:534
  31.6 3.3 %all-to-all-done.1.arrived_ref = bf16[8,32,256]{2,1,0:T(8,128)(2,1)S(1)} async-done(((bf16[8,32,256]{2,1,0:T(8,128)(2,1)}), bf16[8,32,256]{2,1,0:T(8,128)(2,1)S(1)}, u32[]{:S(2)}, u32[]{:S(2)}) %all-to-all-start.1) | async-done | bytes 131104 | tf_op jit(solution)/shard_map/all_to_all | solution.py:484
  34.8 4.2 %step.4 = (f32[32,2048]{1,0:T(8,128)S(1)}, bf16[8,32,256]{2,1,0:T(8,128)(2,1)}) custom-call(s32[128]{0:T(128)} %get-tuple-element.17.plan_ref, s32[8,1,8]{2,1,0:T(1,128)S(1)} %all-to-all-done.wanted_ref, f8e4m3fn[96,512,256]{2,1,0:T(32,128)(4,1)} %get-tuple-element.18.packed_hbm, f8e4m3fn[16,512,256]{2,1,0:T(32,128)(4,1)S(1)} %get-tuple-element.19.kept_ref, ...), custom_call_target="tpu_custom_call" | custom-call | tf_op jit(solution)/shard_map/step/pallas_call | solution.py:545
  39.0 3.7 %all-to-all-start.2 = ((bf16[8,32,256]{2,1,0:T(8,128)(2,1)}), bf16[8,32,256]{2,1,0:T(8,128)(2,1)S(1)}, u32[]{:S(2)}, u32[]{:S(2)}) async-start(bf16[8,32,256]{2,1,0:T(8,128)(2,1)} %get-tuple-element.22), calls=%async_computation.2 | async-start | bytes 262144 | tf_op jit(solution)/shard_map/all_to_all | solution.py:484
  42.7 2.5 %near.5.base_ref = f32[32,2048]{1,0:T(8,128)S(1)} custom-call(s32[128]{0:T(128)} %get-tuple-element.17.plan_ref, f8e4m3fn[96,512,256]{2,1,0:T(32,128)(4,1)} %get-tuple-element.18.packed_hbm, f32[8,2048]{1,0:T(8,128)S(1)} %get-tuple-element.20.scale_ref, f32[32,2048]{1,0:T(8,128)S(1)} %get-tuple-element.21.now_ref.before_ref, f32[32,2048]{1,0:T(8,128)S(1)} %copy-done), custom_call_target="tpu_custom_call" | custom-call | flops 268435456 | bytes 2097152 | tf_op jit(solution)/shard_map/near/pallas_call | solution.py:534
  45.2 3.2 %all-to-all-done.2.arrived_ref = bf16[8,32,256]{2,1,0:T(8,128)(2,1)S(1)} async-done(((bf16[8,32,256]{2,1,0:T(8,128)(2,1)}), bf16[8,32,256]{2,1,0:T(8,128)(2,1)S(1)}, u32[]{:S(2)}, u32[]{:S(2)}) %all-to-all-start.2) | async-done | bytes 131104 | tf_op jit(solution)/shard_map/all_to_all | solution.py:484
  48.4 4.2 %step.5 = (f32[32,2048]{1,0:T(8,128)S(1)}, bf16[8,32,256]{2,1,0:T(8,128)(2,1)}) custom-call(s32[128]{0:T(128)} %get-tuple-element.17.plan_ref, s32[8,1,8]{2,1,0:T(1,128)S(1)} %all-to-all-done.wanted_ref, f8e4m3fn[96,512,256]{2,1,0:T(32,128)(4,1)} %get-tuple-element.18.packed_hbm, f8e4m3fn[16,512,256]{2,1,0:T(32,128)(4,1)S(1)} %get-tuple-element.19.kept_ref, ...), custom_call_target="tpu_custom_call" | custom-call | tf_op jit(solution)/shard_map/step/pallas_call | solution.py:545
  52.7 3.7 %all-to-all-start.3 = ((bf16[8,32,256]{2,1,0:T(8,128)(2,1)}), bf16[8,32,256]{2,1,0:T(8,128)(2,1)S(1)}, u32[]{:S(2)}, u32[]{:S(2)}) async-start(bf16[8,32,256]{2,1,0:T(8,128)(2,1)} %get-tuple-element.24), calls=%async_computation.3 | async-start | bytes 262144 | tf_op jit(solution)/shard_map/all_to_all | solution.py:484
  56.4 2.5 %near.6.base_ref = f32[32,2048]{1,0:T(8,128)S(1)} custom-call(s32[128]{0:T(128)} %get-tuple-element.17.plan_ref, f8e4m3fn[96,512,256]{2,1,0:T(32,128)(4,1)} %get-tuple-element.18.packed_hbm, f32[8,2048]{1,0:T(8,128)S(1)} %get-tuple-element.20.scale_ref, f32[32,2048]{1,0:T(8,128)S(1)} %get-tuple-element.23.now_ref.before_ref, ...), custom_call_target="tpu_custom_call" | custom-call | flops 268435456 | bytes 2097152 | tf_op jit(solution)/shard_map/near/pallas_call | solution.py:534
  58.9 3.2 %all-to-all-done.3.arrived_ref = bf16[8,32,256]{2,1,0:T(8,128)(2,1)S(1)} async-done(((bf16[8,32,256]{2,1,0:T(8,128)(2,1)}), bf16[8,32,256]{2,1,0:T(8,128)(2,1)S(1)}, u32[]{:S(2)}, u32[]{:S(2)}) %all-to-all-start.3) | async-done | bytes 131104 | tf_op jit(solution)/shard_map/all_to_all | solution.py:484
  62.1 4.2 %step.6 = (f32[32,2048]{1,0:T(8,128)S(1)}, bf16[8,32,256]{2,1,0:T(8,128)(2,1)}) custom-call(s32[128]{0:T(128)} %get-tuple-element.17.plan_ref, s32[8,1,8]{2,1,0:T(1,128)S(1)} %all-to-all-done.wanted_ref, f8e4m3fn[96,512,256]{2,1,0:T(32,128)(4,1)} %get-tuple-element.18.packed_hbm, f8e4m3fn[16,512,256]{2,1,0:T(32,128)(4,1)S(1)} %get-tuple-element.19.kept_ref, ...), custom_call_target="tpu_custom_call" | custom-call | tf_op jit(solution)/shard_map/step/pallas_call | solution.py:545
  66.3 3.7 %all-to-all-start.4 = ((bf16[8,32,256]{2,1,0:T(8,128)(2,1)}), bf16[8,32,256]{2,1,0:T(8,128)(2,1)S(1)}, u32[]{:S(2)}, u32[]{:S(2)}) async-start(bf16[8,32,256]{2,1,0:T(8,128)(2,1)} %get-tuple-element.26), calls=%async_computation.4 | async-start | bytes 262144 | tf_op jit(solution)/shard_map/all_to_all | solution.py:484
  70.0 2.5 %near.7.base_ref = f32[32,2048]{1,0:T(8,128)S(1)} custom-call(s32[128]{0:T(128)} %get-tuple-element.17.plan_ref, f8e4m3fn[96,512,256]{2,1,0:T(32,128)(4,1)} %get-tuple-element.18.packed_hbm, f32[8,2048]{1,0:T(8,128)S(1)} %get-tuple-element.20.scale_ref, f32[32,2048]{1,0:T(8,128)S(1)} %get-tuple-element.25.now_ref, ...), custom_call_target="tpu_custom_call" | custom-call | flops 268435456 | bytes 2097152 | tf_op jit(solution)/shard_map/near/pallas_call | solution.py:534
  72.5 3.2 %all-to-all-done.4.arrived_ref = bf16[8,32,256]{2,1,0:T(8,128)(2,1)S(1)} async-done(((bf16[8,32,256]{2,1,0:T(8,128)(2,1)}), bf16[8,32,256]{2,1,0:T(8,128)(2,1)S(1)}, u32[]{:S(2)}, u32[]{:S(2)}) %all-to-all-start.4) | async-done | bytes 131104 | tf_op jit(solution)/shard_map/all_to_all | solution.py:484
  75.7 3.5 %step.7.own_ref = f32[32,2048]{1,0:T(8,128)S(1)} custom-call(s32[128]{0:T(128)} %get-tuple-element.17.plan_ref, s32[8,1,8]{2,1,0:T(1,128)S(1)} %all-to-all-done.wanted_ref, f8e4m3fn[96,512,256]{2,1,0:T(32,128)(4,1)} %get-tuple-element.18.packed_hbm, f8e4m3fn[16,512,256]{2,1,0:T(32,128)(4,1)S(1)} %get-tuple-element.19.kept_ref, ...), custom_call_target="tpu_custom_call" | custom-call | tf_op jit(solution)/shard_map/step/pallas_call | solution.py:545
  79.3 1.6 %collective-permute-start.1 = (bf16[32,2048]{1,0:T(8,128)(2,1)S(1)}, bf16[32,2048]{1,0:T(8,128)(2,1)S(1)}, u32[]{:S(2)}, u32[]{:S(2)}) collective-permute-start(bf16[32,2048]{1,0:T(8,128)(2,1)S(1)} %convert_element_type.3), channel_id=1, source_target_pairs={{0,2},{1,3},{2,0},{3,1},{4,6},{5,7},{6,4},{7,5},{8,10},{9,11},{10,... | collective-permute-start | bytes 393224 | tf_op jit(solution)/shard_map/ppermute | solution.py:489
  80.8 3.5 %collective-permute-done.1.refs_1_ = bf16[32,2048]{1,0:T(8,128)(2,1)S(1)} collective-permute-done((bf16[32,2048]{1,0:T(8,128)(2,1)S(1)}, bf16[32,2048]{1,0:T(8,128)(2,1)S(1)}, u32[]{:S(2)}, u32[]{:S(2)}) %collective-permute-start.1) | collective-permute-done | bytes 131104 | tf_op jit(solution)/shard_map/ppermute | solution.py:489
  86.4 3.7 %collective-permute-done.3 = f32[64,128]{1,0:T(8,128)S(1)} collective-permute-done((f32[64,128]{1,0:T(8,128)S(1)}, f32[64,128]{1,0:T(8,128)S(1)}, u32[]{:S(2)}, u32[]{:S(2)}) %collective-permute-start.3) | collective-permute-done | bytes 32800 | tf_op jit(solution)/shard_map/ppermute | solution.py:489
  90.1 1.8 %collective-permute-start.6 = (f32[64,128]{1,0:T(8,128)S(1)}, f32[64,128]{1,0:T(8,128)S(1)}, u32[]{:S(2)}, u32[]{:S(2)}) collective-permute-start(f32[64,128]{1,0:T(8,128)S(1)} %add.3.refs_0_), channel_id=1, source_target_pairs={{0,24},{4,28},{8,16},{12,20},{16,8},{20,12},{24,0},{28,4},{1,25},{... | collective-permute-start | bytes 98312 | tf_op jit(solution)/shard_map/ppermute | solution.py:489
  91.9 2.5 %collective-permute-start.4 = (f32[64,128]{1,0:T(8,128)S(1)}, f32[64,128]{1,0:T(8,128)S(1)}, u32[]{:S(2)}, u32[]{:S(2)}) collective-permute-start(f32[64,128]{1,0:T(8,128)S(1)} %add.3.refs_0_), channel_id=1, source_target_pairs={{0,8},{4,12},{8,0},{12,4},{16,24},{20,28},{24,16},{28,20},{1,9},{5... | collective-permute-start | bytes 98312 | tf_op jit(solution)/shard_map/ppermute | solution.py:489
  96.7 6.2 %factor.1 = f32[32,2048]{1,0:T(8,128)} custom-call(f32[32,2048]{1,0:T(8,128)S(1)} %step.7.own_ref, bf16[4,32,2048]{2,1,0:T(8,128)(2,1)S(1)} %get-tuple-element.27.all_ref, f32[64,128]{1,0:T(8,128)S(1)} %add.3.refs_0_, f32[64,128]{1,0:T(8,128)S(1)} %collective-permute-done.4.refs_1_, f32[64,128]{1,0:T(8,128)S(1)} %collective-permute-done.5.refs_2_, ...), custom_call_target="tpu_custom_call" | custom-call | tf_op jit(solution)/shard_map/factor/pallas_call | solution.py:575
  (17 shorter events, 6.9 us)
Async XLA Ops:
  1.2 21.4 %all-to-all-start = ((s32[8,1,8]{2,1,0:T(1,128)}), s32[8,1,8]{2,1,0:T(1,128)S(1)}, u32[]{:S(2)}, u32[]{:S(2)}) async-start(s32[8,1,8]{2,1,0:T(1,128)} %broadcast_in_dim.9), calls=%async_computation | async-start | bytes 8192 | tf_op jit(solution)/shard_map/all_to_all | solution.py:484
  9.1 13.6 %copy-start = (f32[32,2048]{1,0:T(8,128)S(1)}, f32[32,2048]{1,0:T(8,128)}, u32[]{:S(2)}) copy-start(f32[32,2048]{1,0:T(8,128)} %before_ref.3) | copy-start | bytes 786436
  24.0 10.8 %all-to-all-start.1 = ((bf16[8,32,256]{2,1,0:T(8,128)(2,1)}), bf16[8,32,256]{2,1,0:T(8,128)(2,1)S(1)}, u32[]{:S(2)}, u32[]{:S(2)}) async-start(bf16[8,32,256]{2,1,0:T(8,128)(2,1)} %first.1), calls=%async_computation.1 | async-start | bytes 262144 | tf_op jit(solution)/shard_map/all_to_all | solution.py:484
  39.0 9.4 %all-to-all-start.2 = ((bf16[8,32,256]{2,1,0:T(8,128)(2,1)}), bf16[8,32,256]{2,1,0:T(8,128)(2,1)S(1)}, u32[]{:S(2)}, u32[]{:S(2)}) async-start(bf16[8,32,256]{2,1,0:T(8,128)(2,1)} %get-tuple-element.22), calls=%async_computation.2 | async-start | bytes 262144 | tf_op jit(solution)/shard_map/all_to_all | solution.py:484
  52.7 9.4 %all-to-all-start.3 = ((bf16[8,32,256]{2,1,0:T(8,128)(2,1)}), bf16[8,32,256]{2,1,0:T(8,128)(2,1)S(1)}, u32[]{:S(2)}, u32[]{:S(2)}) async-start(bf16[8,32,256]{2,1,0:T(8,128)(2,1)} %get-tuple-element.24), calls=%async_computation.3 | async-start | bytes 262144 | tf_op jit(solution)/shard_map/all_to_all | solution.py:484
  66.3 9.4 %all-to-all-start.4 = ((bf16[8,32,256]{2,1,0:T(8,128)(2,1)}), bf16[8,32,256]{2,1,0:T(8,128)(2,1)S(1)}, u32[]{:S(2)}, u32[]{:S(2)}) async-start(bf16[8,32,256]{2,1,0:T(8,128)(2,1)} %get-tuple-element.26), calls=%async_computation.4 | async-start | bytes 262144 | tf_op jit(solution)/shard_map/all_to_all | solution.py:484
  79.3 5.0 %collective-permute-start.1 = (bf16[32,2048]{1,0:T(8,128)(2,1)S(1)}, bf16[32,2048]{1,0:T(8,128)(2,1)S(1)}, u32[]{:S(2)}, u32[]{:S(2)}) collective-permute-start(bf16[32,2048]{1,0:T(8,128)(2,1)S(1)} %convert_element_type.3), channel_id=1, source_target_pairs={{0,2},{1,3},{2,0},{3,1},{4,6},{5,7},{6,4},{7,5},{8,10},{9,11},{10,... | collective-permute-start | bytes 393224 | tf_op jit(solution)/shard_map/ppermute | solution.py:489
  80.8 3.5 %collective-permute-start = (bf16[32,2048]{1,0:T(8,128)(2,1)S(1)}, bf16[32,2048]{1,0:T(8,128)(2,1)S(1)}, u32[]{:S(2)}, u32[]{:S(2)}) collective-permute-start(bf16[32,2048]{1,0:T(8,128)(2,1)S(1)} %convert_element_type.3), channel_id=1, source_target_pairs={{0,1},{1,0},{2,3},{3,2},{4,5},{5,4},{6,7},{7,6},{8,9},{9,8},{10,11... | collective-permute-start | bytes 393224 | tf_op jit(solution)/shard_map/ppermute | solution.py:489
  84.3 1.3 %collective-permute-start.2 = (bf16[32,2048]{1,0:T(8,128)(2,1)S(1)}, bf16[32,2048]{1,0:T(8,128)(2,1)S(1)}, u32[]{:S(2)}, u32[]{:S(2)}) collective-permute-start(bf16[32,2048]{1,0:T(8,128)(2,1)S(1)} %collective-permute-done.1.refs_1_), channel_id=1, source_target_pairs={{0,1},{1,0},{2,3},{3,2},{4,5},{5,4},{6,7},{7,6},{8,9},{9,8},{10,11... | collective-permute-start | bytes 393224 | tf_op jit(solution)/shard_map/ppermute | solution.py:489
  86.1 4.0 %collective-permute-start.3 = (f32[64,128]{1,0:T(8,128)S(1)}, f32[64,128]{1,0:T(8,128)S(1)}, u32[]{:S(2)}, u32[]{:S(2)}) collective-permute-start(f32[64,128]{1,0:T(8,128)S(1)} %get-tuple-element.28), channel_id=1, source_target_pairs={{0,4},{4,0},{8,12},{12,8},{16,20},{20,16},{24,28},{28,24},{1,5},{5... | collective-permute-start | bytes 98312 | tf_op jit(solution)/shard_map/ppermute | solution.py:489
  90.1 5.9 %collective-permute-start.6 = (f32[64,128]{1,0:T(8,128)S(1)}, f32[64,128]{1,0:T(8,128)S(1)}, u32[]{:S(2)}, u32[]{:S(2)}) collective-permute-start(f32[64,128]{1,0:T(8,128)S(1)} %add.3.refs_0_), channel_id=1, source_target_pairs={{0,24},{4,28},{8,16},{12,20},{16,8},{20,12},{24,0},{28,4},{1,25},{... | collective-permute-start | bytes 98312 | tf_op jit(solution)/shard_map/ppermute | solution.py:489
  91.9 4.8 %collective-permute-start.5 = (f32[64,128]{1,0:T(8,128)S(1)}, f32[64,128]{1,0:T(8,128)S(1)}, u32[]{:S(2)}, u32[]{:S(2)}) collective-permute-start(f32[64,128]{1,0:T(8,128)S(1)} %add.3.refs_0_), channel_id=1, source_target_pairs={{0,16},{4,20},{8,24},{12,28},{16,0},{20,4},{24,8},{28,12},{1,17},{... | collective-permute-start | bytes 98312 | tf_op jit(solution)/shard_map/ppermute | solution.py:489
  91.9 4.8 %collective-permute-start.4 = (f32[64,128]{1,0:T(8,128)S(1)}, f32[64,128]{1,0:T(8,128)S(1)}, u32[]{:S(2)}, u32[]{:S(2)}) collective-permute-start(f32[64,128]{1,0:T(8,128)S(1)} %add.3.refs_0_), channel_id=1, source_target_pairs={{0,8},{4,12},{8,0},{12,4},{16,24},{20,28},{24,16},{28,20},{1,9},{5... | collective-permute-start | bytes 98312 | tf_op jit(solution)/shard_map/ppermute | solution.py:489

commit v14 on v13

--- a/solution.py
+++ b/solution.py
@@ -110,32 +110,30 @@
         for copy in copies(c):
             copy.start()
 
-    def clear(key, _):
-        table_ref[key] = -1
+    def clear(row, _):
+        for slot in range(slots):
+            table_ref[row * slots + slot] = -1
         return _
 
-    lax.fori_loop(0, rb_dev * slots, clear, 0)
+    lax.fori_loop(0, rb_dev, clear, 0)
     present_ref[...] = jnp.zeros_like(present_ref)
     for copy in lists:
         copy.wait()
 
-    def link(t, carry):
-        key = rows_ref[t] * slots + slots_ref[t]
-        seen = table_ref[key]
-        before = seen & 255
-        length = seen >> 8
-        joins = (seen >= 0) & (length < MERGE)
-        back_ref[t] = jnp.where(joins, before, -1)
-        done_ref[t] = 1
-
-        @pl.when(joins)
-        def _():
-            done_ref[before] = 0
-
-        table_ref[key] = t | (jnp.where(joins, length + 1, 1) << 8)
+    def link(c, carry):
+        for t in [c * CHUNK + j for j in range(CHUNK)]:
+            key = rows_ref[t] * slots + slots_ref[t]
+            seen = table_ref[key]
+            before = seen & 255
+            length = seen >> 8
+            joins = (seen >= 0) & (length < MERGE)
+            back_ref[t] = jnp.where(joins, before, -1)
+            done_ref[t] = 1
+            done_ref[jnp.where(joins, before, tiles)] = 0
+            table_ref[key] = t | (jnp.where(joins, length + 1, 1) << 8)
         return carry
 
-    lax.fori_loop(0, tiles, link, 0)
+    lax.fori_loop(0, chunks, link, 0)
 
     def turned(tile):
         small = tile.astype(F8)
@@ -154,7 +152,8 @@
     def one(skip, t, listed):
         row = rows_ref[t]
         both = both_ref[t]
-        present_ref[row] = present_ref[row] + (both[:, :order] + jnp.abs(both[:, order:]))
+        counted = both[:, :order] + jnp.abs(both[:, order:])
+        present_ref[row] = present_ref[row] + (counted[:, : order // 2] + counted[:, order // 2 :])
         closes = done_ref[t]
 
         @pl.when(closes == 1)
@@ -197,7 +196,7 @@
     plan_copy = pltpu.make_async_copy(plan_ref, plan_hbm, list_sems.at[2])
     plan_copy.start()
 
-    ones = jnp.ones((8, order), BF16)
+    ones = jnp.ones((8, order // 2), BF16)
     for r in range(rb_dev):
         degree = lax.dot_general(ones, present_ref[r], NT, preferred_element_type=F32)
         scale_ref[:, r * order : (r + 1) * order] = 1.0 / jnp.sqrt(jnp.maximum(degree, 1.0))
@@ -235,10 +234,10 @@
             pltpu.SMEM((tiles + 32,), I32),
             pltpu.VMEM((tiles, order, 2 * order), BF16),
             pltpu.VMEM((tiles, 2 * order, order), F8),
-            pltpu.VMEM((rb_dev, order, order), BF16),
+            pltpu.VMEM((rb_dev, order, order // 2), BF16),
             pltpu.SMEM((rb_dev * (rb_dev + nblk),), I32),
             pltpu.SMEM((tiles,), I32),
-            pltpu.SMEM((tiles,), I32),
+            pltpu.SMEM((tiles + 1,), I32),
             pltpu.SemaphoreType.DMA((tiles // CHUNK, 2)),
             pltpu.SemaphoreType.DMA((tiles,)),
             pltpu.SemaphoreType.DMA((3,)),
@@ -401,7 +400,7 @@
     gram_ref[...] = even + turn_lanes(odd)
 
 
-PANEL = 32
+PANEL = 64
 
 
 def factor_kernel(nodes, own_ref, all_ref, *refs):

time: 104 us -> 104 us (level)
  transfers between devices with their start and end apart: 12 -> 12, of which waited for: 9 -> 10; matrix products, arithmetic and copies ran while one was open for 0% -> 0% of each run, Pallas kernels for 23% -> 24%
where the time goes in v14:
time: 104 us; the launch traced here: 102 us
  Pallas kernels  48 us (46%)
  starting transfers between devices  30.2 us (29%)
  waiting for transfers between devices  22.8 us (22%)
  local copies, waits for them, and re-layouts  1.25 us (1%)
    all_to_all x5, starting transfers between devices, exchange(): lax.all_to_all(x, 'blk', split_axis=0, concat_axis=0, tiled=True, axis_in...  23.8 us
    pallas_call x4, Pallas kernels, per_device(): pl.pallas_call(functools.partial(step_kernel, step), name='step', out_sha...  16.2 us
    pallas_call x1, Pallas kernels, tiles_call(): pl.pallas_call(functools.partial(tiles_kernel, near_count), name='tiles',...  13.8 us
    all_to_all x5, waiting for transfers between devices, exchange(): lax.all_to_all(x, 'blk', split_axis=0, concat_axis=0, tiled=True, axis_in...  12.2 us
    pallas_call x4, Pallas kernels, per_device(): pl.pallas_call(functools.partial(near_kernel, step), name='near', out_sha...  10.6 us
    ppermute x7, waiting for transfers between devices, to_partner(): return lax.ppermute(x, axis, [(i, i ^ mask) for i in range(n)])  10.6 us
    ppermute x7, starting transfers between devices, to_partner(): return lax.ppermute(x, axis, [(i, i ^ mask) for i in range(n)])  6.44 us
    pallas_call x1, Pallas kernels, per_device(): pl.pallas_call(functools.partial(factor_kernel, rows * nblk), name='facto...  5.62 us
  transfers between devices with their start and end apart: 12, of which 10 were waited for; matrix products, arithmetic and copies ran while one was open for 0% of the time, Pallas kernels for 24%

profile of v14, /device:TPU:0, one launch (start us, length us, event | category | flops | bytes accessed | tf_op | source)
XLA Modules:
  0.0 102.4 jit_solution(16644375270351455317)
XLA Ops:
  1.2 7.8 %all-to-all-start = ((s32[8,1,8]{2,1,0:T(1,128)}), s32[8,1,8]{2,1,0:T(1,128)S(1)}, u32[]{:S(2)}, u32[]{:S(2)}) async-start(s32[8,1,8]{2,1,0:T(1,128)} %broadcast_in_dim.9), calls=%async_computation | async-start | bytes 8192 | tf_op jit(solution)/shard_map/all_to_all | solution.py:483
  9.1 13.8 %tiles.1 = (f8e4m3fn[96,512,256]{2,1,0:T(32,128)(4,1)}, f8e4m3fn[16,512,256]{2,1,0:T(32,128)(4,1)S(1)}, f32[8,2048]{1,0:T(8,128)S(1)}, s32[128]{0:T(128)}) custom-call(s32[96]{0:T(128)} %rows_hbm.1, s32[96]{0:T(128)} %slots_hbm.1, bf16[96,256,256]{2,1,0:T(8,128)(2,1)} %real_hbm.1, bf16[96,256,256]{2,1,0:T(8,128)(2,1)} %imag_hbm.1), custom_call_target="tpu_custom_call" | custom-call | flops 268435456 | bytes 25165824 | tf_op jit(solution)/shard_map/tiles/pallas_call | solution.py:220
  24.2 5.3 %all-to-all-start.1 = ((bf16[8,32,256]{2,1,0:T(8,128)(2,1)}), bf16[8,32,256]{2,1,0:T(8,128)(2,1)S(1)}, u32[]{:S(2)}, u32[]{:S(2)}) async-start(bf16[8,32,256]{2,1,0:T(8,128)(2,1)} %first.1), calls=%async_computation.1 | async-start | bytes 262144 | tf_op jit(solution)/shard_map/all_to_all | solution.py:483
  29.6 2.6 %near.4.base_ref = f32[32,2048]{1,0:T(8,128)S(1)} custom-call(s32[128]{0:T(128)} %get-tuple-element.17.plan_ref, f8e4m3fn[96,512,256]{2,1,0:T(32,128)(4,1)} %get-tuple-element.18.packed_hbm, f32[8,2048]{1,0:T(8,128)S(1)} %get-tuple-element.20.scale_ref, f32[32,2048]{1,0:T(8,128)S(1)} %copy-done, f32[32,2048]{1,0:T(8,128)S(1)} %copy-done), custom_call_target="tpu_custom_call" | custom-call | flops 268435456 | bytes 2097152 | tf_op jit(solution)/shard_map/near/pallas_call | solution.py:533
  32.2 3.1 %all-to-all-done.1.arrived_ref = bf16[8,32,256]{2,1,0:T(8,128)(2,1)S(1)} async-done(((bf16[8,32,256]{2,1,0:T(8,128)(2,1)}), bf16[8,32,256]{2,1,0:T(8,128)(2,1)S(1)}, u32[]{:S(2)}, u32[]{:S(2)}) %all-to-all-start.1) | async-done | bytes 131104 | tf_op jit(solution)/shard_map/all_to_all | solution.py:483
  35.3 4.2 %step.4 = (f32[32,2048]{1,0:T(8,128)S(1)}, bf16[8,32,256]{2,1,0:T(8,128)(2,1)}) custom-call(s32[128]{0:T(128)} %get-tuple-element.17.plan_ref, s32[8,1,8]{2,1,0:T(1,128)S(1)} %all-to-all-done.wanted_ref, f8e4m3fn[96,512,256]{2,1,0:T(32,128)(4,1)} %get-tuple-element.18.packed_hbm, f8e4m3fn[16,512,256]{2,1,0:T(32,128)(4,1)S(1)} %get-tuple-element.19.kept_ref, ...), custom_call_target="tpu_custom_call" | custom-call | tf_op jit(solution)/shard_map/step/pallas_call | solution.py:544
  39.5 3.5 %all-to-all-start.2 = ((bf16[8,32,256]{2,1,0:T(8,128)(2,1)}), bf16[8,32,256]{2,1,0:T(8,128)(2,1)S(1)}, u32[]{:S(2)}, u32[]{:S(2)}) async-start(bf16[8,32,256]{2,1,0:T(8,128)(2,1)} %get-tuple-element.22), calls=%async_computation.2 | async-start | bytes 262144 | tf_op jit(solution)/shard_map/all_to_all | solution.py:483
  43.0 2.7 %near.5.base_ref = f32[32,2048]{1,0:T(8,128)S(1)} custom-call(s32[128]{0:T(128)} %get-tuple-element.17.plan_ref, f8e4m3fn[96,512,256]{2,1,0:T(32,128)(4,1)} %get-tuple-element.18.packed_hbm, f32[8,2048]{1,0:T(8,128)S(1)} %get-tuple-element.20.scale_ref, f32[32,2048]{1,0:T(8,128)S(1)} %get-tuple-element.21.now_ref.before_ref, f32[32,2048]{1,0:T(8,128)S(1)} %copy-done), custom_call_target="tpu_custom_call" | custom-call | flops 268435456 | bytes 2097152 | tf_op jit(solution)/shard_map/near/pallas_call | solution.py:533
  45.7 3.1 %all-to-all-done.2.arrived_ref = bf16[8,32,256]{2,1,0:T(8,128)(2,1)S(1)} async-done(((bf16[8,32,256]{2,1,0:T(8,128)(2,1)}), bf16[8,32,256]{2,1,0:T(8,128)(2,1)S(1)}, u32[]{:S(2)}, u32[]{:S(2)}) %all-to-all-start.2) | async-done | bytes 131104 | tf_op jit(solution)/shard_map/all_to_all | solution.py:483
  48.8 4.2 %step.5 = (f32[32,2048]{1,0:T(8,128)S(1)}, bf16[8,32,256]{2,1,0:T(8,128)(2,1)}) custom-call(s32[128]{0:T(128)} %get-tuple-element.17.plan_ref, s32[8,1,8]{2,1,0:T(1,128)S(1)} %all-to-all-done.wanted_ref, f8e4m3fn[96,512,256]{2,1,0:T(32,128)(4,1)} %get-tuple-element.18.packed_hbm, f8e4m3fn[16,512,256]{2,1,0:T(32,128)(4,1)S(1)} %get-tuple-element.19.kept_ref, ...), custom_call_target="tpu_custom_call" | custom-call | tf_op jit(solution)/shard_map/step/pallas_call | solution.py:544
  53.0 3.5 %all-to-all-start.3 = ((bf16[8,32,256]{2,1,0:T(8,128)(2,1)}), bf16[8,32,256]{2,1,0:T(8,128)(2,1)S(1)}, u32[]{:S(2)}, u32[]{:S(2)}) async-start(bf16[8,32,256]{2,1,0:T(8,128)(2,1)} %get-tuple-element.24), calls=%async_computation.3 | async-start | bytes 262144 | tf_op jit(solution)/shard_map/all_to_all | solution.py:483
  56.5 2.7 %near.6.base_ref = f32[32,2048]{1,0:T(8,128)S(1)} custom-call(s32[128]{0:T(128)} %get-tuple-element.17.plan_ref, f8e4m3fn[96,512,256]{2,1,0:T(32,128)(4,1)} %get-tuple-element.18.packed_hbm, f32[8,2048]{1,0:T(8,128)S(1)} %get-tuple-element.20.scale_ref, f32[32,2048]{1,0:T(8,128)S(1)} %get-tuple-element.23.now_ref.before_ref, ...), custom_call_target="tpu_custom_call" | custom-call | flops 268435456 | bytes 2097152 | tf_op jit(solution)/shard_map/near/pallas_call | solution.py:533
  59.2 3.1 %all-to-all-done.3.arrived_ref = bf16[8,32,256]{2,1,0:T(8,128)(2,1)S(1)} async-done(((bf16[8,32,256]{2,1,0:T(8,128)(2,1)}), bf16[8,32,256]{2,1,0:T(8,128)(2,1)S(1)}, u32[]{:S(2)}, u32[]{:S(2)}) %all-to-all-start.3) | async-done | bytes 131104 | tf_op jit(solution)/shard_map/all_to_all | solution.py:483
  62.3 4.2 %step.6 = (f32[32,2048]{1,0:T(8,128)S(1)}, bf16[8,32,256]{2,1,0:T(8,128)(2,1)}) custom-call(s32[128]{0:T(128)} %get-tuple-element.17.plan_ref, s32[8,1,8]{2,1,0:T(1,128)S(1)} %all-to-all-done.wanted_ref, f8e4m3fn[96,512,256]{2,1,0:T(32,128)(4,1)} %get-tuple-element.18.packed_hbm, f8e4m3fn[16,512,256]{2,1,0:T(32,128)(4,1)S(1)} %get-tuple-element.19.kept_ref, ...), custom_call_target="tpu_custom_call" | custom-call | tf_op jit(solution)/shard_map/step/pallas_call | solution.py:544
  66.5 3.5 %all-to-all-start.4 = ((bf16[8,32,256]{2,1,0:T(8,128)(2,1)}), bf16[8,32,256]{2,1,0:T(8,128)(2,1)S(1)}, u32[]{:S(2)}, u32[]{:S(2)}) async-start(bf16[8,32,256]{2,1,0:T(8,128)(2,1)} %get-tuple-element.26), calls=%async_computation.4 | async-start | bytes 262144 | tf_op jit(solution)/shard_map/all_to_all | solution.py:483
  70.0 2.7 %near.7.base_ref = f32[32,2048]{1,0:T(8,128)S(1)} custom-call(s32[128]{0:T(128)} %get-tuple-element.17.plan_ref, f8e4m3fn[96,512,256]{2,1,0:T(32,128)(4,1)} %get-tuple-element.18.packed_hbm, f32[8,2048]{1,0:T(8,128)S(1)} %get-tuple-element.20.scale_ref, f32[32,2048]{1,0:T(8,128)S(1)} %get-tuple-element.25.now_ref, ...), custom_call_target="tpu_custom_call" | custom-call | flops 268435456 | bytes 2097152 | tf_op jit(solution)/shard_map/near/pallas_call | solution.py:533
  72.7 3.1 %all-to-all-done.4.arrived_ref = bf16[8,32,256]{2,1,0:T(8,128)(2,1)S(1)} async-done(((bf16[8,32,256]{2,1,0:T(8,128)(2,1)}), bf16[8,32,256]{2,1,0:T(8,128)(2,1)S(1)}, u32[]{:S(2)}, u32[]{:S(2)}) %all-to-all-start.4) | async-done | bytes 131104 | tf_op jit(solution)/shard_map/all_to_all | solution.py:483
  75.8 3.5 %step.7.own_ref = f32[32,2048]{1,0:T(8,128)S(1)} custom-call(s32[128]{0:T(128)} %get-tuple-element.17.plan_ref, s32[8,1,8]{2,1,0:T(1,128)S(1)} %all-to-all-done.wanted_ref, f8e4m3fn[96,512,256]{2,1,0:T(32,128)(4,1)} %get-tuple-element.18.packed_hbm, f8e4m3fn[16,512,256]{2,1,0:T(32,128)(4,1)S(1)} %get-tuple-element.19.kept_ref, ...), custom_call_target="tpu_custom_call" | custom-call | tf_op jit(solution)/shard_map/step/pallas_call | solution.py:544
  79.3 1.6 %collective-permute-start.1 = (bf16[32,2048]{1,0:T(8,128)(2,1)S(1)}, bf16[32,2048]{1,0:T(8,128)(2,1)S(1)}, u32[]{:S(2)}, u32[]{:S(2)}) collective-permute-start(bf16[32,2048]{1,0:T(8,128)(2,1)S(1)} %convert_element_type.3), channel_id=1, source_target_pairs={{0,2},{1,3},{2,0},{3,1},{4,6},{5,7},{6,4},{7,5},{8,10},{9,11},{10,... | collective-permute-start | bytes 393224 | tf_op jit(solution)/shard_map/ppermute | solution.py:488
  80.9 3.5 %collective-permute-done.1.refs_1_ = bf16[32,2048]{1,0:T(8,128)(2,1)S(1)} collective-permute-done((bf16[32,2048]{1,0:T(8,128)(2,1)S(1)}, bf16[32,2048]{1,0:T(8,128)(2,1)S(1)}, u32[]{:S(2)}, u32[]{:S(2)}) %collective-permute-start.1) | collective-permute-done | bytes 131104 | tf_op jit(solution)/shard_map/ppermute | solution.py:488
  86.6 3.5 %collective-permute-done.3 = f32[64,128]{1,0:T(8,128)S(1)} collective-permute-done((f32[64,128]{1,0:T(8,128)S(1)}, f32[64,128]{1,0:T(8,128)S(1)}, u32[]{:S(2)}, u32[]{:S(2)}) %collective-permute-start.3) | collective-permute-done | bytes 32800 | tf_op jit(solution)/shard_map/ppermute | solution.py:488
  90.1 1.6 %collective-permute-start.6 = (f32[64,128]{1,0:T(8,128)S(1)}, f32[64,128]{1,0:T(8,128)S(1)}, u32[]{:S(2)}, u32[]{:S(2)}) collective-permute-start(f32[64,128]{1,0:T(8,128)S(1)} %add.3.refs_0_), channel_id=1, source_target_pairs={{0,24},{4,28},{8,16},{12,20},{16,8},{20,12},{24,0},{28,4},{1,25},{... | collective-permute-start | bytes 98312 | tf_op jit(solution)/shard_map/ppermute | solution.py:488
  91.8 2.7 %collective-permute-start.4 = (f32[64,128]{1,0:T(8,128)S(1)}, f32[64,128]{1,0:T(8,128)S(1)}, u32[]{:S(2)}, u32[]{:S(2)}) collective-permute-start(f32[64,128]{1,0:T(8,128)S(1)} %add.3.refs_0_), channel_id=1, source_target_pairs={{0,8},{4,12},{8,0},{12,4},{16,24},{20,28},{24,16},{28,20},{1,9},{5... | collective-permute-start | bytes 98312 | tf_op jit(solution)/shard_map/ppermute | solution.py:488
  96.7 5.6 %factor.1 = f32[32,2048]{1,0:T(8,128)} custom-call(f32[32,2048]{1,0:T(8,128)S(1)} %step.7.own_ref, bf16[4,32,2048]{2,1,0:T(8,128)(2,1)S(1)} %get-tuple-element.27.all_ref, f32[64,128]{1,0:T(8,128)S(1)} %add.3.refs_0_, f32[64,128]{1,0:T(8,128)S(1)} %collective-permute-done.4.refs_1_, f32[64,128]{1,0:T(8,128)S(1)} %collective-permute-done.5.refs_2_, ...), custom_call_target="tpu_custom_call" | custom-call | tf_op jit(solution)/shard_map/factor/pallas_call | solution.py:574
  (17 shorter events, 7.2 us)
Async XLA Ops:
  1.2 21.6 %all-to-all-start = ((s32[8,1,8]{2,1,0:T(1,128)}), s32[8,1,8]{2,1,0:T(1,128)S(1)}, u32[]{:S(2)}, u32[]{:S(2)}) async-start(s32[8,1,8]{2,1,0:T(1,128)} %broadcast_in_dim.9), calls=%async_computation | async-start | bytes 8192 | tf_op jit(solution)/shard_map/all_to_all | solution.py:483
  9.1 13.8 %copy-start = (f32[32,2048]{1,0:T(8,128)S(1)}, f32[32,2048]{1,0:T(8,128)}, u32[]{:S(2)}) copy-start(f32[32,2048]{1,0:T(8,128)} %before_ref.3) | copy-start | bytes 786436
  24.2 11.0 %all-to-all-start.1 = ((bf16[8,32,256]{2,1,0:T(8,128)(2,1)}), bf16[8,32,256]{2,1,0:T(8,128)(2,1)S(1)}, u32[]{:S(2)}, u32[]{:S(2)}) async-start(bf16[8,32,256]{2,1,0:T(8,128)(2,1)} %first.1), calls=%async_computation.1 | async-start | bytes 262144 | tf_op jit(solution)/shard_map/all_to_all | solution.py:483
  39.5 9.3 %all-to-all-start.2 = ((bf16[8,32,256]{2,1,0:T(8,128)(2,1)}), bf16[8,32,256]{2,1,0:T(8,128)(2,1)S(1)}, u32[]{:S(2)}, u32[]{:S(2)}) async-start(bf16[8,32,256]{2,1,0:T(8,128)(2,1)} %get-tuple-element.22), calls=%async_computation.2 | async-start | bytes 262144 | tf_op jit(solution)/shard_map/all_to_all | solution.py:483
  53.0 9.3 %all-to-all-start.3 = ((bf16[8,32,256]{2,1,0:T(8,128)(2,1)}), bf16[8,32,256]{2,1,0:T(8,128)(2,1)S(1)}, u32[]{:S(2)}, u32[]{:S(2)}) async-start(bf16[8,32,256]{2,1,0:T(8,128)(2,1)} %get-tuple-element.24), calls=%async_computation.3 | async-start | bytes 262144 | tf_op jit(solution)/shard_map/all_to_all | solution.py:483
  66.5 9.3 %all-to-all-start.4 = ((bf16[8,32,256]{2,1,0:T(8,128)(2,1)}), bf16[8,32,256]{2,1,0:T(8,128)(2,1)S(1)}, u32[]{:S(2)}, u32[]{:S(2)}) async-start(bf16[8,32,256]{2,1,0:T(8,128)(2,1)} %get-tuple-element.26), calls=%async_computation.4 | async-start | bytes 262144 | tf_op jit(solution)/shard_map/all_to_all | solution.py:483
  79.3 5.0 %collective-permute-start.1 = (bf16[32,2048]{1,0:T(8,128)(2,1)S(1)}, bf16[32,2048]{1,0:T(8,128)(2,1)S(1)}, u32[]{:S(2)}, u32[]{:S(2)}) collective-permute-start(bf16[32,2048]{1,0:T(8,128)(2,1)S(1)} %convert_element_type.3), channel_id=1, source_target_pairs={{0,2},{1,3},{2,0},{3,1},{4,6},{5,7},{6,4},{7,5},{8,10},{9,11},{10,... | collective-permute-start | bytes 393224 | tf_op jit(solution)/shard_map/ppermute | solution.py:488
  80.9 3.5 %collective-permute-start = (bf16[32,2048]{1,0:T(8,128)(2,1)S(1)}, bf16[32,2048]{1,0:T(8,128)(2,1)S(1)}, u32[]{:S(2)}, u32[]{:S(2)}) collective-permute-start(bf16[32,2048]{1,0:T(8,128)(2,1)S(1)} %convert_element_type.3), channel_id=1, source_target_pairs={{0,1},{1,0},{2,3},{3,2},{4,5},{5,4},{6,7},{7,6},{8,9},{9,8},{10,11... | collective-permute-start | bytes 393224 | tf_op jit(solution)/shard_map/ppermute | solution.py:488
  84.3 1.3 %collective-permute-start.2 = (bf16[32,2048]{1,0:T(8,128)(2,1)S(1)}, bf16[32,2048]{1,0:T(8,128)(2,1)S(1)}, u32[]{:S(2)}, u32[]{:S(2)}) collective-permute-start(bf16[32,2048]{1,0:T(8,128)(2,1)S(1)} %collective-permute-done.1.refs_1_), channel_id=1, source_target_pairs={{0,1},{1,0},{2,3},{3,2},{4,5},{5,4},{6,7},{7,6},{8,9},{9,8},{10,11... | collective-permute-start | bytes 393224 | tf_op jit(solution)/shard_map/ppermute | solution.py:488
  86.1 4.0 %collective-permute-start.3 = (f32[64,128]{1,0:T(8,128)S(1)}, f32[64,128]{1,0:T(8,128)S(1)}, u32[]{:S(2)}, u32[]{:S(2)}) collective-permute-start(f32[64,128]{1,0:T(8,128)S(1)} %get-tuple-element.28), channel_id=1, source_target_pairs={{0,4},{4,0},{8,12},{12,8},{16,20},{20,16},{24,28},{28,24},{1,5},{5... | collective-permute-start | bytes 98312 | tf_op jit(solution)/shard_map/ppermute | solution.py:488
  90.1 5.7 %collective-permute-start.6 = (f32[64,128]{1,0:T(8,128)S(1)}, f32[64,128]{1,0:T(8,128)S(1)}, u32[]{:S(2)}, u32[]{:S(2)}) collective-permute-start(f32[64,128]{1,0:T(8,128)S(1)} %add.3.refs_0_), channel_id=1, source_target_pairs={{0,24},{4,28},{8,16},{12,20},{16,8},{20,12},{24,0},{28,4},{1,25},{... | collective-permute-start | bytes 98312 | tf_op jit(solution)/shard_map/ppermute | solution.py:488
  91.7 4.9 %collective-permute-start.5 = (f32[64,128]{1,0:T(8,128)S(1)}, f32[64,128]{1,0:T(8,128)S(1)}, u32[]{:S(2)}, u32[]{:S(2)}) collective-permute-start(f32[64,128]{1,0:T(8,128)S(1)} %add.3.refs_0_), channel_id=1, source_target_pairs={{0,16},{4,20},{8,24},{12,28},{16,0},{20,4},{24,8},{28,12},{1,17},{... | collective-permute-start | bytes 98312 | tf_op jit(solution)/shard_map/ppermute | solution.py:488
  91.8 4.9 %collective-permute-start.4 = (f32[64,128]{1,0:T(8,128)S(1)}, f32[64,128]{1,0:T(8,128)S(1)}, u32[]{:S(2)}, u32[]{:S(2)}) collective-permute-start(f32[64,128]{1,0:T(8,128)S(1)} %add.3.refs_0_), channel_id=1, source_target_pairs={{0,8},{4,12},{8,0},{12,4},{16,24},{20,28},{24,16},{28,20},{1,9},{5... | collective-permute-start | bytes 98312 | tf_op jit(solution)/shard_map/ppermute | solution.py:488

commit v15 on v14

--- a/solution.py
+++ b/solution.py
@@ -135,25 +135,25 @@
 
     lax.fori_loop(0, chunks, link, 0)
 
-    def turned(tile):
-        small = tile.astype(F8)
-        return jnp.concatenate([small[:, :order].T, small[:, order:].T], axis=0)
-
-    def put(e, skip, value):
+    def fill(ref, e, t):
+        for at in [slice(q, q + 128) for q in range(0, 2 * order, 128)]:
+            ref[e, at] = jnp.zeros((128, order), F8) if t is None else both_ref[t, :, at].astype(F8).T
+
+    def put(e, skip, t):
         @pl.when(e < skip)
         def _():
-            kept_ref[e - skip + kept] = value()
+            fill(kept_ref, e - skip + kept, t)
 
         @pl.when(e >= skip)
         def _():
-            small_ref[e] = value()
+            fill(small_ref, e, t)
             leave(e).start()
 
     def one(skip, t, listed):
         row = rows_ref[t]
-        both = both_ref[t]
-        counted = both[:, :order] + jnp.abs(both[:, order:])
-        present_ref[row] = present_ref[row] + (counted[:, : order // 2] + counted[:, order // 2 :])
+        for at in [slice(q, q + order // 4) for q in range(0, order, order // 4)]:
+            counted = both_ref[t, at, :order] + jnp.abs(both_ref[t, at, order:])
+            present_ref[row, at] = present_ref[row, at] + counted
         closes = done_ref[t]
 
         @pl.when(closes == 1)
@@ -163,7 +163,7 @@
                 return back_ref[prior]
 
             lax.while_loop(lambda prior: prior >= 0, add, back_ref[t])
-            put(listed, skip, lambda: turned(both_ref[t]))
+            put(listed, skip, t)
             slot = slots_ref[t]
             place = rb_dev + ((slot - rb_dev) ^ central(slots - rb_dev))
             plan_ref[listed] = row | (jnp.where(slot < rb_dev, slot, place) << 8)
@@ -183,7 +183,7 @@
 
             @pl.when(j < short)
             def _():
-                put(listed + j, skip, lambda: jnp.zeros(small_ref.shape[1:], F8))
+                put(listed + j, skip, None)
                 plan_ref[listed + j] = slots << 8
 
         return listed + short
@@ -196,7 +196,7 @@
     plan_copy = pltpu.make_async_copy(plan_ref, plan_hbm, list_sems.at[2])
     plan_copy.start()
 
-    ones = jnp.ones((8, order // 2), BF16)
+    ones = jnp.ones((8, order), BF16)
     for r in range(rb_dev):
         degree = lax.dot_general(ones, present_ref[r], NT, preferred_element_type=F32)
         scale_ref[:, r * order : (r + 1) * order] = 1.0 / jnp.sqrt(jnp.maximum(degree, 1.0))
@@ -234,7 +234,7 @@
             pltpu.SMEM((tiles + 32,), I32),
             pltpu.VMEM((tiles, order, 2 * order), BF16),
             pltpu.VMEM((tiles, 2 * order, order), F8),
-            pltpu.VMEM((rb_dev, order, order // 2), BF16),
+            pltpu.VMEM((rb_dev, order, order), BF16),
             pltpu.SMEM((rb_dev * (rb_dev + nblk),), I32),
             pltpu.SMEM((tiles,), I32),
             pltpu.SMEM((tiles + 1,), I32),
@@ -400,7 +400,7 @@
     gram_ref[...] = even + turn_lanes(odd)
 
 
-PANEL = 64
+PANEL = 128
 
 
 def factor_kernel(nodes, own_ref, all_ref, *refs):

time: 104 us -> 103 us (level)
  starting transfers between devices: 30.2 us -> 28.5 us
  Pallas kernels: 48 us -> 49.3 us
    all_to_all x5, starting transfers between devices: 23.8 us -> 22.5 us  [exchange(): lax.all_to_all(x, 'blk', split_axis=0, concat_axis=0, tiled=True, axis_in...]
where the time goes in v15:
time: 103 us; the launch traced here: 102 us
  Pallas kernels  49.3 us (48%)
  starting transfers between devices  28.5 us (28%)
  waiting for transfers between devices  23 us (22%)
  local copies, waits for them, and re-layouts  1.25 us (1%)
    all_to_all x5, starting transfers between devices, exchange(): lax.all_to_all(x, 'blk', split_axis=0, concat_axis=0, tiled=True, axis_in...  22.5 us
    pallas_call x4, Pallas kernels, per_device(): pl.pallas_call(functools.partial(step_kernel, step), name='step', out_sha...  17.2 us
    pallas_call x1, Pallas kernels, tiles_call(): pl.pallas_call(functools.partial(tiles_kernel, near_count), name='tiles',...  13.9 us
    all_to_all x5, waiting for transfers between devices, exchange(): lax.all_to_all(x, 'blk', split_axis=0, concat_axis=0, tiled=True, axis_in...  12.1 us
    ppermute x7, waiting for transfers between devices, to_partner(): return lax.ppermute(x, axis, [(i, i ^ mask) for i in range(n)])  11 us
    pallas_call x4, Pallas kernels, per_device(): pl.pallas_call(functools.partial(near_kernel, step), name='near', out_sha...  10.6 us
    ppermute x7, starting transfers between devices, to_partner(): return lax.ppermute(x, axis, [(i, i ^ mask) for i in range(n)])  6.02 us
    pallas_call x1, Pallas kernels, per_device(): pl.pallas_call(functools.partial(factor_kernel, rows * nblk), name='facto...  5.72 us
  transfers between devices with their start and end apart: 12, of which 10 were waited for; matrix products, arithmetic and copies ran while one was open for 0% of the time, Pallas kernels for 24%

profile of v15, /device:TPU:0, one launch (start us, length us, event | category | flops | bytes accessed | tf_op | source)
XLA Modules:
  0.0 102.2 jit_solution(10762538154454690412)
XLA Ops:
  1.2 7.8 %all-to-all-start = ((s32[8,1,8]{2,1,0:T(1,128)}), s32[8,1,8]{2,1,0:T(1,128)S(1)}, u32[]{:S(2)}, u32[]{:S(2)}) async-start(s32[8,1,8]{2,1,0:T(1,128)} %broadcast_in_dim.9), calls=%async_computation | async-start | bytes 8192 | tf_op jit(solution)/shard_map/all_to_all | solution.py:483
  9.1 13.9 %tiles.1 = (f8e4m3fn[96,512,256]{2,1,0:T(32,128)(4,1)}, f8e4m3fn[16,512,256]{2,1,0:T(32,128)(4,1)S(1)}, f32[8,2048]{1,0:T(8,128)S(1)}, s32[128]{0:T(128)}) custom-call(s32[96]{0:T(128)} %rows_hbm.1, s32[96]{0:T(128)} %slots_hbm.1, bf16[96,256,256]{2,1,0:T(8,128)(2,1)} %real_hbm.1, bf16[96,256,256]{2,1,0:T(8,128)(2,1)} %imag_hbm.1), custom_call_target="tpu_custom_call" | custom-call | flops 268435456 | bytes 25165824 | tf_op jit(solution)/shard_map/tiles/pallas_call | solution.py:220
  24.4 4.7 %all-to-all-start.1 = ((bf16[8,32,256]{2,1,0:T(8,128)(2,1)}), bf16[8,32,256]{2,1,0:T(8,128)(2,1)S(1)}, u32[]{:S(2)}, u32[]{:S(2)}) async-start(bf16[8,32,256]{2,1,0:T(8,128)(2,1)} %first.1), calls=%async_computation.1 | async-start | bytes 262144 | tf_op jit(solution)/shard_map/all_to_all | solution.py:483
  29.1 2.6 %near.4.base_ref = f32[32,2048]{1,0:T(8,128)S(1)} custom-call(s32[128]{0:T(128)} %get-tuple-element.17.plan_ref, f8e4m3fn[96,512,256]{2,1,0:T(32,128)(4,1)} %get-tuple-element.18.packed_hbm, f32[8,2048]{1,0:T(8,128)S(1)} %get-tuple-element.20.scale_ref, f32[32,2048]{1,0:T(8,128)S(1)} %copy-done, f32[32,2048]{1,0:T(8,128)S(1)} %copy-done), custom_call_target="tpu_custom_call" | custom-call | flops 268435456 | bytes 2097152 | tf_op jit(solution)/shard_map/near/pallas_call | solution.py:533
  31.7 3.1 %all-to-all-done.1.arrived_ref = bf16[8,32,256]{2,1,0:T(8,128)(2,1)S(1)} async-done(((bf16[8,32,256]{2,1,0:T(8,128)(2,1)}), bf16[8,32,256]{2,1,0:T(8,128)(2,1)S(1)}, u32[]{:S(2)}, u32[]{:S(2)}) %all-to-all-start.1) | async-done | bytes 131104 | tf_op jit(solution)/shard_map/all_to_all | solution.py:483
  34.8 4.4 %step.4 = (f32[32,2048]{1,0:T(8,128)S(1)}, bf16[8,32,256]{2,1,0:T(8,128)(2,1)}) custom-call(s32[128]{0:T(128)} %get-tuple-element.17.plan_ref, s32[8,1,8]{2,1,0:T(1,128)S(1)} %all-to-all-done.wanted_ref, f8e4m3fn[96,512,256]{2,1,0:T(32,128)(4,1)} %get-tuple-element.18.packed_hbm, f8e4m3fn[16,512,256]{2,1,0:T(32,128)(4,1)S(1)} %get-tuple-element.19.kept_ref, ...), custom_call_target="tpu_custom_call" | custom-call | tf_op jit(solution)/shard_map/step/pallas_call | solution.py:544
  39.2 3.3 %all-to-all-start.2 = ((bf16[8,32,256]{2,1,0:T(8,128)(2,1)}), bf16[8,32,256]{2,1,0:T(8,128)(2,1)S(1)}, u32[]{:S(2)}, u32[]{:S(2)}) async-start(bf16[8,32,256]{2,1,0:T(8,128)(2,1)} %get-tuple-element.22), calls=%async_computation.2 | async-start | bytes 262144 | tf_op jit(solution)/shard_map/all_to_all | solution.py:483
  42.6 2.7 %near.5.base_ref = f32[32,2048]{1,0:T(8,128)S(1)} custom-call(s32[128]{0:T(128)} %get-tuple-element.17.plan_ref, f8e4m3fn[96,512,256]{2,1,0:T(32,128)(4,1)} %get-tuple-element.18.packed_hbm, f32[8,2048]{1,0:T(8,128)S(1)} %get-tuple-element.20.scale_ref, f32[32,2048]{1,0:T(8,128)S(1)} %get-tuple-element.21.now_ref.before_ref, f32[32,2048]{1,0:T(8,128)S(1)} %copy-done), custom_call_target="tpu_custom_call" | custom-call | flops 268435456 | bytes 2097152 | tf_op jit(solution)/shard_map/near/pallas_call | solution.py:533
  45.2 3.0 %all-to-all-done.2.arrived_ref = bf16[8,32,256]{2,1,0:T(8,128)(2,1)S(1)} async-done(((bf16[8,32,256]{2,1,0:T(8,128)(2,1)}), bf16[8,32,256]{2,1,0:T(8,128)(2,1)S(1)}, u32[]{:S(2)}, u32[]{:S(2)}) %all-to-all-start.2) | async-done | bytes 131104 | tf_op jit(solution)/shard_map/all_to_all | solution.py:483
  48.2 4.4 %step.5 = (f32[32,2048]{1,0:T(8,128)S(1)}, bf16[8,32,256]{2,1,0:T(8,128)(2,1)}) custom-call(s32[128]{0:T(128)} %get-tuple-element.17.plan_ref, s32[8,1,8]{2,1,0:T(1,128)S(1)} %all-to-all-done.wanted_ref, f8e4m3fn[96,512,256]{2,1,0:T(32,128)(4,1)} %get-tuple-element.18.packed_hbm, f8e4m3fn[16,512,256]{2,1,0:T(32,128)(4,1)S(1)} %get-tuple-element.19.kept_ref, ...), custom_call_target="tpu_custom_call" | custom-call | tf_op jit(solution)/shard_map/step/pallas_call | solution.py:544
  52.7 3.3 %all-to-all-start.3 = ((bf16[8,32,256]{2,1,0:T(8,128)(2,1)}), bf16[8,32,256]{2,1,0:T(8,128)(2,1)S(1)}, u32[]{:S(2)}, u32[]{:S(2)}) async-start(bf16[8,32,256]{2,1,0:T(8,128)(2,1)} %get-tuple-element.24), calls=%async_computation.3 | async-start | bytes 262144 | tf_op jit(solution)/shard_map/all_to_all | solution.py:483
  56.0 2.7 %near.6.base_ref = f32[32,2048]{1,0:T(8,128)S(1)} custom-call(s32[128]{0:T(128)} %get-tuple-element.17.plan_ref, f8e4m3fn[96,512,256]{2,1,0:T(32,128)(4,1)} %get-tuple-element.18.packed_hbm, f32[8,2048]{1,0:T(8,128)S(1)} %get-tuple-element.20.scale_ref, f32[32,2048]{1,0:T(8,128)S(1)} %get-tuple-element.23.now_ref.before_ref, ...), custom_call_target="tpu_custom_call" | custom-call | flops 268435456 | bytes 2097152 | tf_op jit(solution)/shard_map/near/pallas_call | solution.py:533
  58.7 3.0 %all-to-all-done.3.arrived_ref = bf16[8,32,256]{2,1,0:T(8,128)(2,1)S(1)} async-done(((bf16[8,32,256]{2,1,0:T(8,128)(2,1)}), bf16[8,32,256]{2,1,0:T(8,128)(2,1)S(1)}, u32[]{:S(2)}, u32[]{:S(2)}) %all-to-all-start.3) | async-done | bytes 131104 | tf_op jit(solution)/shard_map/all_to_all | solution.py:483
  61.7 4.4 %step.6 = (f32[32,2048]{1,0:T(8,128)S(1)}, bf16[8,32,256]{2,1,0:T(8,128)(2,1)}) custom-call(s32[128]{0:T(128)} %get-tuple-element.17.plan_ref, s32[8,1,8]{2,1,0:T(1,128)S(1)} %all-to-all-done.wanted_ref, f8e4m3fn[96,512,256]{2,1,0:T(32,128)(4,1)} %get-tuple-element.18.packed_hbm, f8e4m3fn[16,512,256]{2,1,0:T(32,128)(4,1)S(1)} %get-tuple-element.19.kept_ref, ...), custom_call_target="tpu_custom_call" | custom-call | tf_op jit(solution)/shard_map/step/pallas_call | solution.py:544
  66.1 3.3 %all-to-all-start.4 = ((bf16[8,32,256]{2,1,0:T(8,128)(2,1)}), bf16[8,32,256]{2,1,0:T(8,128)(2,1)S(1)}, u32[]{:S(2)}, u32[]{:S(2)}) async-start(bf16[8,32,256]{2,1,0:T(8,128)(2,1)} %get-tuple-element.26), calls=%async_computation.4 | async-start | bytes 262144 | tf_op jit(solution)/shard_map/all_to_all | solution.py:483
  69.5 2.7 %near.7.base_ref = f32[32,2048]{1,0:T(8,128)S(1)} custom-call(s32[128]{0:T(128)} %get-tuple-element.17.plan_ref, f8e4m3fn[96,512,256]{2,1,0:T(32,128)(4,1)} %get-tuple-element.18.packed_hbm, f32[8,2048]{1,0:T(8,128)S(1)} %get-tuple-element.20.scale_ref, f32[32,2048]{1,0:T(8,128)S(1)} %get-tuple-element.25.now_ref, ...), custom_call_target="tpu_custom_call" | custom-call | flops 268435456 | bytes 2097152 | tf_op jit(solution)/shard_map/near/pallas_call | solution.py:533
  72.2 3.0 %all-to-all-done.4.arrived_ref = bf16[8,32,256]{2,1,0:T(8,128)(2,1)S(1)} async-done(((bf16[8,32,256]{2,1,0:T(8,128)(2,1)}), bf16[8,32,256]{2,1,0:T(8,128)(2,1)S(1)}, u32[]{:S(2)}, u32[]{:S(2)}) %all-to-all-start.4) | async-done | bytes 131104 | tf_op jit(solution)/shard_map/all_to_all | solution.py:483
  75.2 3.9 %step.7.own_ref = f32[32,2048]{1,0:T(8,128)S(1)} custom-call(s32[128]{0:T(128)} %get-tuple-element.17.plan_ref, s32[8,1,8]{2,1,0:T(1,128)S(1)} %all-to-all-done.wanted_ref, f8e4m3fn[96,512,256]{2,1,0:T(32,128)(4,1)} %get-tuple-element.18.packed_hbm, f8e4m3fn[16,512,256]{2,1,0:T(32,128)(4,1)S(1)} %get-tuple-element.19.kept_ref, ...), custom_call_target="tpu_custom_call" | custom-call | tf_op jit(solution)/shard_map/step/pallas_call | solution.py:544
  79.1 1.6 %collective-permute-start.1 = (bf16[32,2048]{1,0:T(8,128)(2,1)S(1)}, bf16[32,2048]{1,0:T(8,128)(2,1)S(1)}, u32[]{:S(2)}, u32[]{:S(2)}) collective-permute-start(bf16[32,2048]{1,0:T(8,128)(2,1)S(1)} %convert_element_type.3), channel_id=1, source_target_pairs={{0,2},{1,3},{2,0},{3,1},{4,6},{5,7},{6,4},{7,5},{8,10},{9,11},{10,... | collective-permute-start | bytes 393224 | tf_op jit(solution)/shard_map/ppermute | solution.py:488
  80.6 3.5 %collective-permute-done.1.refs_1_ = bf16[32,2048]{1,0:T(8,128)(2,1)S(1)} collective-permute-done((bf16[32,2048]{1,0:T(8,128)(2,1)S(1)}, bf16[32,2048]{1,0:T(8,128)(2,1)S(1)}, u32[]{:S(2)}, u32[]{:S(2)}) %collective-permute-start.1) | collective-permute-done | bytes 131104 | tf_op jit(solution)/shard_map/ppermute | solution.py:488
  86.0 3.9 %collective-permute-done.3 = f32[64,128]{1,0:T(8,128)S(1)} collective-permute-done((f32[64,128]{1,0:T(8,128)S(1)}, f32[64,128]{1,0:T(8,128)S(1)}, u32[]{:S(2)}, u32[]{:S(2)}) %collective-permute-start.3) | collective-permute-done | bytes 32800 | tf_op jit(solution)/shard_map/ppermute | solution.py:488
  89.9 1.4 %collective-permute-start.6 = (f32[64,128]{1,0:T(8,128)S(1)}, f32[64,128]{1,0:T(8,128)S(1)}, u32[]{:S(2)}, u32[]{:S(2)}) collective-permute-start(f32[64,128]{1,0:T(8,128)S(1)} %add.3.refs_0_), channel_id=1, source_target_pairs={{0,24},{4,28},{8,16},{12,20},{16,8},{20,12},{24,0},{28,4},{1,25},{... | collective-permute-start | bytes 98312 | tf_op jit(solution)/shard_map/ppermute | solution.py:488
  91.3 2.9 %collective-permute-start.4 = (f32[64,128]{1,0:T(8,128)S(1)}, f32[64,128]{1,0:T(8,128)S(1)}, u32[]{:S(2)}, u32[]{:S(2)}) collective-permute-start(f32[64,128]{1,0:T(8,128)S(1)} %add.3.refs_0_), channel_id=1, source_target_pairs={{0,8},{4,12},{8,0},{12,4},{16,24},{20,28},{24,16},{28,20},{1,9},{5... | collective-permute-start | bytes 98312 | tf_op jit(solution)/shard_map/ppermute | solution.py:488
  96.5 5.7 %factor.1 = f32[32,2048]{1,0:T(8,128)} custom-call(f32[32,2048]{1,0:T(8,128)S(1)} %step.7.own_ref, bf16[4,32,2048]{2,1,0:T(8,128)(2,1)S(1)} %get-tuple-element.27.all_ref, f32[64,128]{1,0:T(8,128)S(1)} %add.3.refs_0_, f32[64,128]{1,0:T(8,128)S(1)} %collective-permute-done.4.refs_1_, f32[64,128]{1,0:T(8,128)S(1)} %collective-permute-done.5.refs_2_, ...), custom_call_target="tpu_custom_call" | custom-call | tf_op jit(solution)/shard_map/factor/pallas_call | solution.py:574
  (17 shorter events, 6.7 us)
Async XLA Ops:
  1.2 21.8 %all-to-all-start = ((s32[8,1,8]{2,1,0:T(1,128)}), s32[8,1,8]{2,1,0:T(1,128)S(1)}, u32[]{:S(2)}, u32[]{:S(2)}) async-start(s32[8,1,8]{2,1,0:T(1,128)} %broadcast_in_dim.9), calls=%async_computation | async-start | bytes 8192 | tf_op jit(solution)/shard_map/all_to_all | solution.py:483
  9.1 14.0 %copy-start = (f32[32,2048]{1,0:T(8,128)S(1)}, f32[32,2048]{1,0:T(8,128)}, u32[]{:S(2)}) copy-start(f32[32,2048]{1,0:T(8,128)} %before_ref.3) | copy-start | bytes 786436
  24.4 10.4 %all-to-all-start.1 = ((bf16[8,32,256]{2,1,0:T(8,128)(2,1)}), bf16[8,32,256]{2,1,0:T(8,128)(2,1)S(1)}, u32[]{:S(2)}, u32[]{:S(2)}) async-start(bf16[8,32,256]{2,1,0:T(8,128)(2,1)} %first.1), calls=%async_computation.1 | async-start | bytes 262144 | tf_op jit(solution)/shard_map/all_to_all | solution.py:483
  39.2 9.0 %all-to-all-start.2 = ((bf16[8,32,256]{2,1,0:T(8,128)(2,1)}), bf16[8,32,256]{2,1,0:T(8,128)(2,1)S(1)}, u32[]{:S(2)}, u32[]{:S(2)}) async-start(bf16[8,32,256]{2,1,0:T(8,128)(2,1)} %get-tuple-element.22), calls=%async_computation.2 | async-start | bytes 262144 | tf_op jit(solution)/shard_map/all_to_all | solution.py:483
  52.7 9.0 %all-to-all-start.3 = ((bf16[8,32,256]{2,1,0:T(8,128)(2,1)}), bf16[8,32,256]{2,1,0:T(8,128)(2,1)S(1)}, u32[]{:S(2)}, u32[]{:S(2)}) async-start(bf16[8,32,256]{2,1,0:T(8,128)(2,1)} %get-tuple-element.24), calls=%async_computation.3 | async-start | bytes 262144 | tf_op jit(solution)/shard_map/all_to_all | solution.py:483
  66.1 9.0 %all-to-all-start.4 = ((bf16[8,32,256]{2,1,0:T(8,128)(2,1)}), bf16[8,32,256]{2,1,0:T(8,128)(2,1)S(1)}, u32[]{:S(2)}, u32[]{:S(2)}) async-start(bf16[8,32,256]{2,1,0:T(8,128)(2,1)} %get-tuple-element.26), calls=%async_computation.4 | async-start | bytes 262144 | tf_op jit(solution)/shard_map/all_to_all | solution.py:483
  79.1 5.0 %collective-permute-start.1 = (bf16[32,2048]{1,0:T(8,128)(2,1)S(1)}, bf16[32,2048]{1,0:T(8,128)(2,1)S(1)}, u32[]{:S(2)}, u32[]{:S(2)}) collective-permute-start(bf16[32,2048]{1,0:T(8,128)(2,1)S(1)} %convert_element_type.3), channel_id=1, source_target_pairs={{0,2},{1,3},{2,0},{3,1},{4,6},{5,7},{6,4},{7,5},{8,10},{9,11},{10,... | collective-permute-start | bytes 393224 | tf_op jit(solution)/shard_map/ppermute | solution.py:488
  80.6 3.5 %collective-permute-start = (bf16[32,2048]{1,0:T(8,128)(2,1)S(1)}, bf16[32,2048]{1,0:T(8,128)(2,1)S(1)}, u32[]{:S(2)}, u32[]{:S(2)}) collective-permute-start(bf16[32,2048]{1,0:T(8,128)(2,1)S(1)} %convert_element_type.3), channel_id=1, source_target_pairs={{0,1},{1,0},{2,3},{3,2},{4,5},{5,4},{6,7},{7,6},{8,9},{9,8},{10,11... | collective-permute-start | bytes 393224 | tf_op jit(solution)/shard_map/ppermute | solution.py:488
  84.1 1.3 %collective-permute-start.2 = (bf16[32,2048]{1,0:T(8,128)(2,1)S(1)}, bf16[32,2048]{1,0:T(8,128)(2,1)S(1)}, u32[]{:S(2)}, u32[]{:S(2)}) collective-permute-start(bf16[32,2048]{1,0:T(8,128)(2,1)S(1)} %collective-permute-done.1.refs_1_), channel_id=1, source_target_pairs={{0,1},{1,0},{2,3},{3,2},{4,5},{5,4},{6,7},{7,6},{8,9},{9,8},{10,11... | collective-permute-start | bytes 393224 | tf_op jit(solution)/shard_map/ppermute | solution.py:488
  85.9 4.0 %collective-permute-start.3 = (f32[64,128]{1,0:T(8,128)S(1)}, f32[64,128]{1,0:T(8,128)S(1)}, u32[]{:S(2)}, u32[]{:S(2)}) collective-permute-start(f32[64,128]{1,0:T(8,128)S(1)} %get-tuple-element.28), channel_id=1, source_target_pairs={{0,4},{4,0},{8,12},{12,8},{16,20},{20,16},{24,28},{28,24},{1,5},{5... | collective-permute-start | bytes 98312 | tf_op jit(solution)/shard_map/ppermute | solution.py:488
  89.9 5.7 %collective-permute-start.6 = (f32[64,128]{1,0:T(8,128)S(1)}, f32[64,128]{1,0:T(8,128)S(1)}, u32[]{:S(2)}, u32[]{:S(2)}) collective-permute-start(f32[64,128]{1,0:T(8,128)S(1)} %add.3.refs_0_), channel_id=1, source_target_pairs={{0,24},{4,28},{8,16},{12,20},{16,8},{20,12},{24,0},{28,4},{1,25},{... | collective-permute-start | bytes 98312 | tf_op jit(solution)/shard_map/ppermute | solution.py:488
  91.3 5.1 %collective-permute-start.5 = (f32[64,128]{1,0:T(8,128)S(1)}, f32[64,128]{1,0:T(8,128)S(1)}, u32[]{:S(2)}, u32[]{:S(2)}) collective-permute-start(f32[64,128]{1,0:T(8,128)S(1)} %add.3.refs_0_), channel_id=1, source_target_pairs={{0,16},{4,20},{8,24},{12,28},{16,0},{20,4},{24,8},{28,12},{1,17},{... | collective-permute-start | bytes 98312 | tf_op jit(solution)/shard_map/ppermute | solution.py:488
  91.3 5.2 %collective-permute-start.4 = (f32[64,128]{1,0:T(8,128)S(1)}, f32[64,128]{1,0:T(8,128)S(1)}, u32[]{:S(2)}, u32[]{:S(2)}) collective-permute-start(f32[64,128]{1,0:T(8,128)S(1)} %add.3.refs_0_), channel_id=1, source_target_pairs={{0,8},{4,12},{8,0},{12,4},{16,24},{20,28},{24,16},{28,20},{1,9},{5... | collective-permute-start | bytes 98312 | tf_op jit(solution)/shard_map/ppermute | solution.py:488

commit v16 on v15

--- a/solution.py
+++ b/solution.py
@@ -400,7 +400,50 @@
     gram_ref[...] = even + turn_lanes(odd)
 
 
-PANEL = 128
+PANEL = 64
+SUB = 8
+
+
+def eliminate(a, m, top):
+    shape = a[0].shape
+    here = lax.broadcasted_iota(I32, shape, 0)
+    pivots = [None] * len(a)
+
+    def column(rows, lane):
+        return jnp.broadcast_to(rows[:, lane : lane + 1], shape)
+
+    for step in range(0, len(a) * SUB, 4):
+        own, k = divmod(step, SUB)
+        head = [column(a[own], top + step + i) for i in range(4)]
+        p, q = head[0][k : k + 1, :], head[2][k + 2 : k + 3, :]
+        u, v = head[2][k : k + 1, :], head[3][k : k + 1, :]
+        single = 1.0 / p
+        det = p * q - (u * u + v * v)
+        both = 1.0 / det
+        pq, ub, vb, pb = q * both, u * both, v * both, p * both
+        second = (here == k + 2) | (here == k + 3)
+        last = det * single
+        pivot = jnp.where(second, last, jnp.broadcast_to(p, shape))
+        pivots[own] = pivot if k == 0 else jnp.where(here < k, pivots[own], pivot)
+        rows = [[x[own][k + i : k + i + 1, :] for i in range(4)] for x in (a, m)]
+        for g in range(own, len(a)):
+            w = head if g == own else [column(a[g], top + step + i) for i in range(4)]
+            c = [
+                w[0] * pq - w[2] * ub - w[3] * vb,
+                w[1] * pq + w[2] * vb - w[3] * ub,
+                w[2] * pb - w[0] * ub + w[1] * vb,
+                w[3] * pb - w[0] * vb - w[1] * ub,
+            ]
+            if g == own:
+                below = here > k + 3
+                c = [jnp.where(below, x, 0.0) for x in c]
+                c[0] = jnp.where(second, w[0] * single, c[0])
+                c[1] = jnp.where(second, w[1] * single, c[1])
+            a[g], m[g] = (
+                x[g] - (c[0] * r[0] + c[1] * r[1] + c[2] * r[2] + c[3] * r[3]) for x, r in zip((a, m), rows)
+            )
+    roots = [lax.rsqrt(x) for x in pivots]
+    return [x * r for x, r in zip(a, roots)], [x * r for x, r in zip(m, roots)]
 
 
 def factor_kernel(nodes, own_ref, all_ref, *refs):
@@ -416,34 +459,11 @@
     row_at = lax.broadcasted_iota(I32, (order, order), 0)
     lane_at = lax.broadcasted_iota(I32, (order, order), 1)
     inverse_ref[...] = (row_at == lane_at).astype(F32)
-    here = lax.broadcasted_iota(I32, (PANEL, order), 0)
     for top in range(0, order, PANEL):
-        a = work_ref[top : top + PANEL, :]
-        m = inverse_ref[top : top + PANEL, :]
-        pivots = jnp.ones_like(a)
-        for k in range(0, PANEL, 4):
-            w = [jnp.broadcast_to(a[:, i : i + 1], a.shape) for i in range(top + k, top + k + 4)]
-            p, q = w[0][k : k + 1, :], w[2][k + 2 : k + 3, :]
-            u, v = w[2][k : k + 1, :], w[3][k : k + 1, :]
-            single = 1.0 / p
-            det = p * q - (u * u + v * v)
-            both = 1.0 / det
-            second = (here == k + 2) | (here == k + 3)
-            below = here > k + 3
-            coefficients = (
-                jnp.where(second, w[0] * single, (w[0] * q - w[2] * u - w[3] * v) * both),
-                jnp.where(second, w[1] * single, (w[1] * q + w[2] * v - w[3] * u) * both),
-                jnp.where(below, (w[2] * p - w[0] * u + w[1] * v) * both, 0.0),
-                jnp.where(below, (w[3] * p - w[0] * v - w[1] * u) * both, 0.0),
-            )
-            coefficients = [jnp.where(here > k + 1, c, 0.0) for c in coefficients]
-            pivots = jnp.where((here == k) | (here == k + 1), p, pivots)
-            pivots = jnp.where(second, det * single, pivots)
-            a, m = (
-                x - sum(c * x[k + i : k + i + 1, :] for i, c in enumerate(coefficients)) for x in (a, m)
-            )
-        root = lax.rsqrt(pivots)
-        a, m = a * root, m * root
+        tops = range(top, top + PANEL, SUB)
+        a, m = ([ref[r : r + SUB, :] for r in tops] for ref in (work_ref, inverse_ref))
+        a, m = eliminate(a, m, top)
+        a, m = jnp.concatenate(a, axis=0), jnp.concatenate(m, axis=0)
         inverse_ref[top : top + PANEL, :] = m
         rest = top + PANEL
         if rest < order:

time: 103 us -> 102 us (level)
  Pallas kernels: 49.3 us -> 47.1 us
where the time goes in v16:
time: 102 us; the launch traced here: 101 us
  Pallas kernels  47.1 us (46%)
  starting transfers between devices  29.2 us (29%)
  waiting for transfers between devices  22.9 us (22%)
  local copies, waits for them, and re-layouts  1.25 us (1%)
    all_to_all x5, starting transfers between devices, exchange(): lax.all_to_all(x, 'blk', split_axis=0, concat_axis=0, tiled=True, axis_in...  23 us
    pallas_call x4, Pallas kernels, per_device(): pl.pallas_call(functools.partial(step_kernel, step), name='step', out_sha...  16.2 us
    pallas_call x1, Pallas kernels, tiles_call(): pl.pallas_call(functools.partial(tiles_kernel, near_count), name='tiles',...  13.8 us
    all_to_all x5, waiting for transfers between devices, exchange(): lax.all_to_all(x, 'blk', split_axis=0, concat_axis=0, tiled=True, axis_in...  12.2 us
    ppermute x7, waiting for transfers between devices, to_partner(): return lax.ppermute(x, axis, [(i, i ^ mask) for i in range(n)])  10.8 us
    pallas_call x4, Pallas kernels, per_device(): pl.pallas_call(functools.partial(near_kernel, step), name='near', out_sha...  10.6 us
    ppermute x7, starting transfers between devices, to_partner(): return lax.ppermute(x, axis, [(i, i ^ mask) for i in range(n)])  6.23 us
    pallas_call x1, Pallas kernels, per_device(): pl.pallas_call(functools.partial(factor_kernel, rows * nblk), name='facto...  4.73 us
  transfers between devices with their start and end apart: 12, of which 10 were waited for; matrix products, arithmetic and copies ran while one was open for 0% of the time, Pallas kernels for 24%

profile of v16, /device:TPU:0, one launch (start us, length us, event | category | flops | bytes accessed | tf_op | source)
XLA Modules:
  0.0 100.6 jit_solution(3281042954239451227)
XLA Ops:
  1.2 7.8 %all-to-all-start = ((s32[8,1,8]{2,1,0:T(1,128)}), s32[8,1,8]{2,1,0:T(1,128)S(1)}, u32[]{:S(2)}, u32[]{:S(2)}) async-start(s32[8,1,8]{2,1,0:T(1,128)} %broadcast_in_dim.9), calls=%async_computation | async-start | bytes 8192 | tf_op jit(solution)/shard_map/all_to_all | solution.py:503
  9.1 13.8 %tiles.1 = (f8e4m3fn[96,512,256]{2,1,0:T(32,128)(4,1)}, f8e4m3fn[16,512,256]{2,1,0:T(32,128)(4,1)S(1)}, f32[8,2048]{1,0:T(8,128)S(1)}, s32[128]{0:T(128)}) custom-call(s32[96]{0:T(128)} %rows_hbm.1, s32[96]{0:T(128)} %slots_hbm.1, bf16[96,256,256]{2,1,0:T(8,128)(2,1)} %real_hbm.1, bf16[96,256,256]{2,1,0:T(8,128)(2,1)} %imag_hbm.1), custom_call_target="tpu_custom_call" | custom-call | flops 268435456 | bytes 25165824 | tf_op jit(solution)/shard_map/tiles/pallas_call | solution.py:220
  24.3 4.7 %all-to-all-start.1 = ((bf16[8,32,256]{2,1,0:T(8,128)(2,1)}), bf16[8,32,256]{2,1,0:T(8,128)(2,1)S(1)}, u32[]{:S(2)}, u32[]{:S(2)}) async-start(bf16[8,32,256]{2,1,0:T(8,128)(2,1)} %first.1), calls=%async_computation.1 | async-start | bytes 262144 | tf_op jit(solution)/shard_map/all_to_all | solution.py:503
  28.9 2.6 %near.4.base_ref = f32[32,2048]{1,0:T(8,128)S(1)} custom-call(s32[128]{0:T(128)} %get-tuple-element.17.plan_ref, f8e4m3fn[96,512,256]{2,1,0:T(32,128)(4,1)} %get-tuple-element.18.packed_hbm, f32[8,2048]{1,0:T(8,128)S(1)} %get-tuple-element.20.scale_ref, f32[32,2048]{1,0:T(8,128)S(1)} %copy-done, f32[32,2048]{1,0:T(8,128)S(1)} %copy-done), custom_call_target="tpu_custom_call" | custom-call | flops 268435456 | bytes 2097152 | tf_op jit(solution)/shard_map/near/pallas_call | solution.py:553
  31.6 3.1 %all-to-all-done.1.arrived_ref = bf16[8,32,256]{2,1,0:T(8,128)(2,1)S(1)} async-done(((bf16[8,32,256]{2,1,0:T(8,128)(2,1)}), bf16[8,32,256]{2,1,0:T(8,128)(2,1)S(1)}, u32[]{:S(2)}, u32[]{:S(2)}) %all-to-all-start.1) | async-done | bytes 131104 | tf_op jit(solution)/shard_map/all_to_all | solution.py:503
  34.6 4.2 %step.4 = (f32[32,2048]{1,0:T(8,128)S(1)}, bf16[8,32,256]{2,1,0:T(8,128)(2,1)}) custom-call(s32[128]{0:T(128)} %get-tuple-element.17.plan_ref, s32[8,1,8]{2,1,0:T(1,128)S(1)} %all-to-all-done.wanted_ref, f8e4m3fn[96,512,256]{2,1,0:T(32,128)(4,1)} %get-tuple-element.18.packed_hbm, f8e4m3fn[16,512,256]{2,1,0:T(32,128)(4,1)S(1)} %get-tuple-element.19.kept_ref, ...), custom_call_target="tpu_custom_call" | custom-call | tf_op jit(solution)/shard_map/step/pallas_call | solution.py:564
  38.9 3.5 %all-to-all-start.2 = ((bf16[8,32,256]{2,1,0:T(8,128)(2,1)}), bf16[8,32,256]{2,1,0:T(8,128)(2,1)S(1)}, u32[]{:S(2)}, u32[]{:S(2)}) async-start(bf16[8,32,256]{2,1,0:T(8,128)(2,1)} %get-tuple-element.22), calls=%async_computation.2 | async-start | bytes 262144 | tf_op jit(solution)/shard_map/all_to_all | solution.py:503
  42.4 2.7 %near.5.base_ref = f32[32,2048]{1,0:T(8,128)S(1)} custom-call(s32[128]{0:T(128)} %get-tuple-element.17.plan_ref, f8e4m3fn[96,512,256]{2,1,0:T(32,128)(4,1)} %get-tuple-element.18.packed_hbm, f32[8,2048]{1,0:T(8,128)S(1)} %get-tuple-element.20.scale_ref, f32[32,2048]{1,0:T(8,128)S(1)} %get-tuple-element.21.now_ref.before_ref, f32[32,2048]{1,0:T(8,128)S(1)} %copy-done), custom_call_target="tpu_custom_call" | custom-call | flops 268435456 | bytes 2097152 | tf_op jit(solution)/shard_map/near/pallas_call | solution.py:553
  45.0 3.0 %all-to-all-done.2.arrived_ref = bf16[8,32,256]{2,1,0:T(8,128)(2,1)S(1)} async-done(((bf16[8,32,256]{2,1,0:T(8,128)(2,1)}), bf16[8,32,256]{2,1,0:T(8,128)(2,1)S(1)}, u32[]{:S(2)}, u32[]{:S(2)}) %all-to-all-start.2) | async-done | bytes 131104 | tf_op jit(solution)/shard_map/all_to_all | solution.py:503
  48.1 4.2 %step.5 = (f32[32,2048]{1,0:T(8,128)S(1)}, bf16[8,32,256]{2,1,0:T(8,128)(2,1)}) custom-call(s32[128]{0:T(128)} %get-tuple-element.17.plan_ref, s32[8,1,8]{2,1,0:T(1,128)S(1)} %all-to-all-done.wanted_ref, f8e4m3fn[96,512,256]{2,1,0:T(32,128)(4,1)} %get-tuple-element.18.packed_hbm, f8e4m3fn[16,512,256]{2,1,0:T(32,128)(4,1)S(1)} %get-tuple-element.19.kept_ref, ...), custom_call_target="tpu_custom_call" | custom-call | tf_op jit(solution)/shard_map/step/pallas_call | solution.py:564
  52.3 3.5 %all-to-all-start.3 = ((bf16[8,32,256]{2,1,0:T(8,128)(2,1)}), bf16[8,32,256]{2,1,0:T(8,128)(2,1)S(1)}, u32[]{:S(2)}, u32[]{:S(2)}) async-start(bf16[8,32,256]{2,1,0:T(8,128)(2,1)} %get-tuple-element.24), calls=%async_computation.3 | async-start | bytes 262144 | tf_op jit(solution)/shard_map/all_to_all | solution.py:503
  55.8 2.7 %near.6.base_ref = f32[32,2048]{1,0:T(8,128)S(1)} custom-call(s32[128]{0:T(128)} %get-tuple-element.17.plan_ref, f8e4m3fn[96,512,256]{2,1,0:T(32,128)(4,1)} %get-tuple-element.18.packed_hbm, f32[8,2048]{1,0:T(8,128)S(1)} %get-tuple-element.20.scale_ref, f32[32,2048]{1,0:T(8,128)S(1)} %get-tuple-element.23.now_ref.before_ref, ...), custom_call_target="tpu_custom_call" | custom-call | flops 268435456 | bytes 2097152 | tf_op jit(solution)/shard_map/near/pallas_call | solution.py:553
  58.5 3.0 %all-to-all-done.3.arrived_ref = bf16[8,32,256]{2,1,0:T(8,128)(2,1)S(1)} async-done(((bf16[8,32,256]{2,1,0:T(8,128)(2,1)}), bf16[8,32,256]{2,1,0:T(8,128)(2,1)S(1)}, u32[]{:S(2)}, u32[]{:S(2)}) %all-to-all-start.3) | async-done | bytes 131104 | tf_op jit(solution)/shard_map/all_to_all | solution.py:503
  61.5 4.2 %step.6 = (f32[32,2048]{1,0:T(8,128)S(1)}, bf16[8,32,256]{2,1,0:T(8,128)(2,1)}) custom-call(s32[128]{0:T(128)} %get-tuple-element.17.plan_ref, s32[8,1,8]{2,1,0:T(1,128)S(1)} %all-to-all-done.wanted_ref, f8e4m3fn[96,512,256]{2,1,0:T(32,128)(4,1)} %get-tuple-element.18.packed_hbm, f8e4m3fn[16,512,256]{2,1,0:T(32,128)(4,1)S(1)} %get-tuple-element.19.kept_ref, ...), custom_call_target="tpu_custom_call" | custom-call | tf_op jit(solution)/shard_map/step/pallas_call | solution.py:564
  65.8 3.5 %all-to-all-start.4 = ((bf16[8,32,256]{2,1,0:T(8,128)(2,1)}), bf16[8,32,256]{2,1,0:T(8,128)(2,1)S(1)}, u32[]{:S(2)}, u32[]{:S(2)}) async-start(bf16[8,32,256]{2,1,0:T(8,128)(2,1)} %get-tuple-element.26), calls=%async_computation.4 | async-start | bytes 262144 | tf_op jit(solution)/shard_map/all_to_all | solution.py:503
  69.2 2.7 %near.7.base_ref = f32[32,2048]{1,0:T(8,128)S(1)} custom-call(s32[128]{0:T(128)} %get-tuple-element.17.plan_ref, f8e4m3fn[96,512,256]{2,1,0:T(32,128)(4,1)} %get-tuple-element.18.packed_hbm, f32[8,2048]{1,0:T(8,128)S(1)} %get-tuple-element.20.scale_ref, f32[32,2048]{1,0:T(8,128)S(1)} %get-tuple-element.25.now_ref, ...), custom_call_target="tpu_custom_call" | custom-call | flops 268435456 | bytes 2097152 | tf_op jit(solution)/shard_map/near/pallas_call | solution.py:553
  71.9 3.0 %all-to-all-done.4.arrived_ref = bf16[8,32,256]{2,1,0:T(8,128)(2,1)S(1)} async-done(((bf16[8,32,256]{2,1,0:T(8,128)(2,1)}), bf16[8,32,256]{2,1,0:T(8,128)(2,1)S(1)}, u32[]{:S(2)}, u32[]{:S(2)}) %all-to-all-start.4) | async-done | bytes 131104 | tf_op jit(solution)/shard_map/all_to_all | solution.py:503
  75.0 3.5 %step.7.own_ref = f32[32,2048]{1,0:T(8,128)S(1)} custom-call(s32[128]{0:T(128)} %get-tuple-element.17.plan_ref, s32[8,1,8]{2,1,0:T(1,128)S(1)} %all-to-all-done.wanted_ref, f8e4m3fn[96,512,256]{2,1,0:T(32,128)(4,1)} %get-tuple-element.18.packed_hbm, f8e4m3fn[16,512,256]{2,1,0:T(32,128)(4,1)S(1)} %get-tuple-element.19.kept_ref, ...), custom_call_target="tpu_custom_call" | custom-call | tf_op jit(solution)/shard_map/step/pallas_call | solution.py:564
  78.5 1.6 %collective-permute-start.1 = (bf16[32,2048]{1,0:T(8,128)(2,1)S(1)}, bf16[32,2048]{1,0:T(8,128)(2,1)S(1)}, u32[]{:S(2)}, u32[]{:S(2)}) collective-permute-start(bf16[32,2048]{1,0:T(8,128)(2,1)S(1)} %convert_element_type.3), channel_id=1, source_target_pairs={{0,2},{1,3},{2,0},{3,1},{4,6},{5,7},{6,4},{7,5},{8,10},{9,11},{10,... | collective-permute-start | bytes 393224 | tf_op jit(solution)/shard_map/ppermute | solution.py:508
  80.1 3.5 %collective-permute-done.1.refs_1_ = bf16[32,2048]{1,0:T(8,128)(2,1)S(1)} collective-permute-done((bf16[32,2048]{1,0:T(8,128)(2,1)S(1)}, bf16[32,2048]{1,0:T(8,128)(2,1)S(1)}, u32[]{:S(2)}, u32[]{:S(2)}) %collective-permute-start.1) | collective-permute-done | bytes 131104 | tf_op jit(solution)/shard_map/ppermute | solution.py:508
  85.6 3.7 %collective-permute-done.3 = f32[64,128]{1,0:T(8,128)S(1)} collective-permute-done((f32[64,128]{1,0:T(8,128)S(1)}, f32[64,128]{1,0:T(8,128)S(1)}, u32[]{:S(2)}, u32[]{:S(2)}) %collective-permute-start.3) | collective-permute-done | bytes 32800 | tf_op jit(solution)/shard_map/ppermute | solution.py:508
  89.3 1.6 %collective-permute-start.6 = (f32[64,128]{1,0:T(8,128)S(1)}, f32[64,128]{1,0:T(8,128)S(1)}, u32[]{:S(2)}, u32[]{:S(2)}) collective-permute-start(f32[64,128]{1,0:T(8,128)S(1)} %add.3.refs_0_), channel_id=1, source_target_pairs={{0,24},{4,28},{8,16},{12,20},{16,8},{20,12},{24,0},{28,4},{1,25},{... | collective-permute-start | bytes 98312 | tf_op jit(solution)/shard_map/ppermute | solution.py:508
  90.9 2.7 %collective-permute-start.4 = (f32[64,128]{1,0:T(8,128)S(1)}, f32[64,128]{1,0:T(8,128)S(1)}, u32[]{:S(2)}, u32[]{:S(2)}) collective-permute-start(f32[64,128]{1,0:T(8,128)S(1)} %add.3.refs_0_), channel_id=1, source_target_pairs={{0,8},{4,12},{8,0},{12,4},{16,24},{20,28},{24,16},{28,20},{1,9},{5... | collective-permute-start | bytes 98312 | tf_op jit(solution)/shard_map/ppermute | solution.py:508
  95.9 4.7 %factor.1 = f32[32,2048]{1,0:T(8,128)} custom-call(f32[32,2048]{1,0:T(8,128)S(1)} %step.7.own_ref, bf16[4,32,2048]{2,1,0:T(8,128)(2,1)S(1)} %get-tuple-element.27.all_ref, f32[64,128]{1,0:T(8,128)S(1)} %add.3.refs_0_, f32[64,128]{1,0:T(8,128)S(1)} %collective-permute-done.4.refs_1_, f32[64,128]{1,0:T(8,128)S(1)} %collective-permute-done.5.refs_2_, ...), custom_call_target="tpu_custom_call" | custom-call | tf_op jit(solution)/shard_map/factor/pallas_call | solution.py:594
  (17 shorter events, 6.9 us)
Async XLA Ops:
  1.2 21.6 %all-to-all-start = ((s32[8,1,8]{2,1,0:T(1,128)}), s32[8,1,8]{2,1,0:T(1,128)S(1)}, u32[]{:S(2)}, u32[]{:S(2)}) async-start(s32[8,1,8]{2,1,0:T(1,128)} %broadcast_in_dim.9), calls=%async_computation | async-start | bytes 8192 | tf_op jit(solution)/shard_map/all_to_all | solution.py:503
  9.1 13.8 %copy-start = (f32[32,2048]{1,0:T(8,128)S(1)}, f32[32,2048]{1,0:T(8,128)}, u32[]{:S(2)}) copy-start(f32[32,2048]{1,0:T(8,128)} %before_ref.3) | copy-start | bytes 786436
  24.3 10.4 %all-to-all-start.1 = ((bf16[8,32,256]{2,1,0:T(8,128)(2,1)}), bf16[8,32,256]{2,1,0:T(8,128)(2,1)S(1)}, u32[]{:S(2)}, u32[]{:S(2)}) async-start(bf16[8,32,256]{2,1,0:T(8,128)(2,1)} %first.1), calls=%async_computation.1 | async-start | bytes 262144 | tf_op jit(solution)/shard_map/all_to_all | solution.py:503
  38.9 9.2 %all-to-all-start.2 = ((bf16[8,32,256]{2,1,0:T(8,128)(2,1)}), bf16[8,32,256]{2,1,0:T(8,128)(2,1)S(1)}, u32[]{:S(2)}, u32[]{:S(2)}) async-start(bf16[8,32,256]{2,1,0:T(8,128)(2,1)} %get-tuple-element.22), calls=%async_computation.2 | async-start | bytes 262144 | tf_op jit(solution)/shard_map/all_to_all | solution.py:503
  52.3 9.2 %all-to-all-start.3 = ((bf16[8,32,256]{2,1,0:T(8,128)(2,1)}), bf16[8,32,256]{2,1,0:T(8,128)(2,1)S(1)}, u32[]{:S(2)}, u32[]{:S(2)}) async-start(bf16[8,32,256]{2,1,0:T(8,128)(2,1)} %get-tuple-element.24), calls=%async_computation.3 | async-start | bytes 262144 | tf_op jit(solution)/shard_map/all_to_all | solution.py:503
  65.8 9.2 %all-to-all-start.4 = ((bf16[8,32,256]{2,1,0:T(8,128)(2,1)}), bf16[8,32,256]{2,1,0:T(8,128)(2,1)S(1)}, u32[]{:S(2)}, u32[]{:S(2)}) async-start(bf16[8,32,256]{2,1,0:T(8,128)(2,1)} %get-tuple-element.26), calls=%async_computation.4 | async-start | bytes 262144 | tf_op jit(solution)/shard_map/all_to_all | solution.py:503
  78.5 5.0 %collective-permute-start.1 = (bf16[32,2048]{1,0:T(8,128)(2,1)S(1)}, bf16[32,2048]{1,0:T(8,128)(2,1)S(1)}, u32[]{:S(2)}, u32[]{:S(2)}) collective-permute-start(bf16[32,2048]{1,0:T(8,128)(2,1)S(1)} %convert_element_type.3), channel_id=1, source_target_pairs={{0,2},{1,3},{2,0},{3,1},{4,6},{5,7},{6,4},{7,5},{8,10},{9,11},{10,... | collective-permute-start | bytes 393224 | tf_op jit(solution)/shard_map/ppermute | solution.py:508
  80.1 3.5 %collective-permute-start = (bf16[32,2048]{1,0:T(8,128)(2,1)S(1)}, bf16[32,2048]{1,0:T(8,128)(2,1)S(1)}, u32[]{:S(2)}, u32[]{:S(2)}) collective-permute-start(bf16[32,2048]{1,0:T(8,128)(2,1)S(1)} %convert_element_type.3), channel_id=1, source_target_pairs={{0,1},{1,0},{2,3},{3,2},{4,5},{5,4},{6,7},{7,6},{8,9},{9,8},{10,11... | collective-permute-start | bytes 393224 | tf_op jit(solution)/shard_map/ppermute | solution.py:508
  83.5 1.3 %collective-permute-start.2 = (bf16[32,2048]{1,0:T(8,128)(2,1)S(1)}, bf16[32,2048]{1,0:T(8,128)(2,1)S(1)}, u32[]{:S(2)}, u32[]{:S(2)}) collective-permute-start(bf16[32,2048]{1,0:T(8,128)(2,1)S(1)} %collective-permute-done.1.refs_1_), channel_id=1, source_target_pairs={{0,1},{1,0},{2,3},{3,2},{4,5},{5,4},{6,7},{7,6},{8,9},{9,8},{10,11... | collective-permute-start | bytes 393224 | tf_op jit(solution)/shard_map/ppermute | solution.py:508
  85.3 4.0 %collective-permute-start.3 = (f32[64,128]{1,0:T(8,128)S(1)}, f32[64,128]{1,0:T(8,128)S(1)}, u32[]{:S(2)}, u32[]{:S(2)}) collective-permute-start(f32[64,128]{1,0:T(8,128)S(1)} %get-tuple-element.28), channel_id=1, source_target_pairs={{0,4},{4,0},{8,12},{12,8},{16,20},{20,16},{24,28},{28,24},{1,5},{5... | collective-permute-start | bytes 98312 | tf_op jit(solution)/shard_map/ppermute | solution.py:508
  89.3 5.7 %collective-permute-start.6 = (f32[64,128]{1,0:T(8,128)S(1)}, f32[64,128]{1,0:T(8,128)S(1)}, u32[]{:S(2)}, u32[]{:S(2)}) collective-permute-start(f32[64,128]{1,0:T(8,128)S(1)} %add.3.refs_0_), channel_id=1, source_target_pairs={{0,24},{4,28},{8,16},{12,20},{16,8},{20,12},{24,0},{28,4},{1,25},{... | collective-permute-start | bytes 98312 | tf_op jit(solution)/shard_map/ppermute | solution.py:508
  90.9 4.9 %collective-permute-start.5 = (f32[64,128]{1,0:T(8,128)S(1)}, f32[64,128]{1,0:T(8,128)S(1)}, u32[]{:S(2)}, u32[]{:S(2)}) collective-permute-start(f32[64,128]{1,0:T(8,128)S(1)} %add.3.refs_0_), channel_id=1, source_target_pairs={{0,16},{4,20},{8,24},{12,28},{16,0},{20,4},{24,8},{28,12},{1,17},{... | collective-permute-start | bytes 98312 | tf_op jit(solution)/shard_map/ppermute | solution.py:508
  90.9 5.0 %collective-permute-start.4 = (f32[64,128]{1,0:T(8,128)S(1)}, f32[64,128]{1,0:T(8,128)S(1)}, u32[]{:S(2)}, u32[]{:S(2)}) collective-permute-start(f32[64,128]{1,0:T(8,128)S(1)} %add.3.refs_0_), channel_id=1, source_target_pairs={{0,8},{4,12},{8,0},{12,4},{16,24},{20,28},{24,16},{28,20},{1,9},{5... | collective-permute-start | bytes 98312 | tf_op jit(solution)/shard_map/ppermute | solution.py:508

commit v17 on v16

--- a/solution.py
+++ b/solution.py
@@ -133,27 +133,30 @@
             table_ref[key] = t | (jnp.where(joins, length + 1, 1) << 8)
         return carry
 
-    lax.fori_loop(0, chunks, link, 0)
+    lax.fori_loop(near_count // CHUNK, chunks, link, 0)
 
     def fill(ref, e, t):
         for at in [slice(q, q + 128) for q in range(0, 2 * order, 128)]:
             ref[e, at] = jnp.zeros((128, order), F8) if t is None else both_ref[t, :, at].astype(F8).T
 
-    def put(e, skip, t):
-        @pl.when(e < skip)
+    def put(e, t):
+        @pl.when(e < kept)
         def _():
-            fill(kept_ref, e - skip + kept, t)
-
-        @pl.when(e >= skip)
+            fill(kept_ref, e, t)
+
+        @pl.when(e >= kept)
         def _():
-            fill(small_ref, e, t)
-            leave(e).start()
-
-    def one(skip, t, listed):
+            fill(small_ref, e - kept, t)
+            leave(e - kept).start()
+
+    def count(t):
         row = rows_ref[t]
         for at in [slice(q, q + order // 4) for q in range(0, order, order // 4)]:
             counted = both_ref[t, at, :order] + jnp.abs(both_ref[t, at, order:])
             present_ref[row, at] = present_ref[row, at] + counted
+
+    def one(t, listed):
+        count(t)
         closes = done_ref[t]
 
         @pl.when(closes == 1)
@@ -163,36 +166,38 @@
                 return back_ref[prior]
 
             lax.while_loop(lambda prior: prior >= 0, add, back_ref[t])
-            put(listed, skip, t)
-            slot = slots_ref[t]
-            place = rb_dev + ((slot - rb_dev) ^ central(slots - rb_dev))
-            plan_ref[listed] = row | (jnp.where(slot < rb_dev, slot, place) << 8)
+            put(listed, t)
+            place = (slots_ref[t] - rb_dev) ^ central(slots - rb_dev)
+            plan_ref[listed] = rows_ref[t] | (place << 8)
 
         return listed + closes
 
-    def chunk(skip, c, listed):
+    def near_chunk(c, carry):
         for copy in copies(c):
             copy.wait()
         for j in range(CHUNK):
-            listed = one(skip, c * CHUNK + j, listed)
+            count(c * CHUNK + j)
+        return carry
+
+    def far_chunk(c, listed):
+        for copy in copies(c):
+            copy.wait()
+        for j in range(CHUNK):
+            listed = one(c * CHUNK + j, listed)
         return listed
 
-    def pad(skip, listed):
-        short = (UNROLL - listed % UNROLL) % UNROLL
-        for j in range(UNROLL - 1):
-
-            @pl.when(j < short)
-            def _():
-                put(listed + j, skip, None)
-                plan_ref[listed + j] = slots << 8
-
-        return listed + short
-
-    near = pad(0, lax.fori_loop(0, near_count // CHUNK, functools.partial(chunk, 0), 0))
-    skip = near + kept
-    every = pad(skip, lax.fori_loop(near_count // CHUNK, chunks, functools.partial(chunk, skip), near))
-    plan_ref[tiles] = near // UNROLL
-    plan_ref[tiles + 1] = every // UNROLL
+    lax.fori_loop(0, near_count // CHUNK, near_chunk, 0)
+    listed = lax.fori_loop(near_count // CHUNK, chunks, far_chunk, 0)
+    short = (UNROLL - listed % UNROLL) % UNROLL
+    for j in range(UNROLL - 1):
+
+        @pl.when(j < short)
+        def _():
+            put(listed + j, None)
+            plan_ref[listed + j] = (slots - rb_dev) << 8
+
+    every = listed + short
+    plan_ref[tiles] = every // UNROLL
     plan_copy = pltpu.make_async_copy(plan_ref, plan_hbm, list_sems.at[2])
     plan_copy.start()
 
@@ -202,11 +207,10 @@
         scale_ref[:, r * order : (r + 1) * order] = 1.0 / jnp.sqrt(jnp.maximum(degree, 1.0))
 
     def left(e, _):
-        leave(e).wait()
+        leave(e - kept).wait()
         return _
 
-    lax.fori_loop(0, near, left, 0)
-    lax.fori_loop(skip, every, left, 0)
+    lax.fori_loop(kept, every, left, 0)
     plan_copy.wait()
 
 
@@ -221,7 +225,7 @@
         functools.partial(tiles_kernel, near_count),
         name="tiles",
         out_shape=(
-            pltpu.HBM((tiles, 2 * order, order), F8),
+            pltpu.HBM((tiles - near_count - KEPT, 2 * order, order), F8),
             pltpu.VMEM((KEPT, 2 * order, order), F8),
             sds((8, rb_dev * order), F32),
             pltpu.HBM((tiles + 32,), I32),
@@ -233,7 +237,7 @@
             pltpu.SMEM((tiles,), I32),
             pltpu.SMEM((tiles + 32,), I32),
             pltpu.VMEM((tiles, order, 2 * order), BF16),
-            pltpu.VMEM((tiles, 2 * order, order), F8),
+            pltpu.VMEM((tiles - near_count - KEPT, 2 * order, order), F8),
             pltpu.VMEM((rb_dev, order, order), BF16),
             pltpu.SMEM((rb_dev * (rb_dev + nblk),), I32),
             pltpu.SMEM((tiles,), I32),
@@ -270,18 +274,16 @@
     send_picked(wanted_ref, sent_ref, out_hbm, out_sems)
 
 
-def load_groups(packed_hbm, tiles_ref, sems, lo, hi):
+def load_groups(packed_hbm, tiles_ref, sems, count):
     def copy(g):
-        at = pl.ds((g - lo) * UNROLL, UNROLL)
-        return pltpu.make_async_copy(
-            packed_hbm.at[pl.ds(g * UNROLL, UNROLL)], tiles_ref.at[at], sems.at[g - lo]
-        )
+        at = pl.ds(g * UNROLL, UNROLL)
+        return pltpu.make_async_copy(packed_hbm.at[at], tiles_ref.at[at], sems.at[g])
 
     def begin(g, _):
         copy(g).start()
         return _
 
-    lax.fori_loop(lo, hi, begin, 0)
+    lax.fori_loop(0, count, begin, 0)
     return copy
 
 
@@ -323,31 +325,48 @@
     lax.fori_loop(lo, hi, group, 0)
 
 
-def loaded(copy, tiles_ref, lo):
-    def tile(g, j):
-        if j == 0:
-            copy(g).wait()
-        return tiles_ref[(g - lo) * UNROLL + j]
-
-    return tile
-
-
 def collect(acc, size):
     group = size.shape[0]
     return (acc[:group] + acc[group:] * (1.0 / FINER)) * size
 
 
-def near_kernel(step, plan_ref, packed_hbm, scale_ref, now_ref, before_ref, base_ref, tiles_ref, x_ref, acc_ref, sems):
-    rb_dev, _, order = acc_ref.shape
-    end = plan_ref.shape[0] - 32
-    hi = plan_ref[end]
-    copy = load_groups(packed_hbm, tiles_ref, sems, 0, hi)
+def near_kernel(
+    step, rows_ref, slots_ref, real_hbm, imag_hbm, scale_ref, now_ref, before_ref, base_ref, tiles_ref, x_ref, acc_ref, sems
+):
+    rb_dev, _, order = x_ref.shape
+    groups = sems.shape[0]
+
+    def copies(g):
+        at = pl.ds(g * UNROLL, UNROLL)
+        return [
+            pltpu.make_async_copy(hbm.at[at], tiles_ref.at[i, at], sems.at[g, i])
+            for i, hbm in enumerate((real_hbm, imag_hbm))
+        ]
+
+    for g in range(groups):
+        for copy in copies(g):
+            copy.start()
     acc_ref[...] = jnp.zeros_like(acc_ref)
-    size = split_sources(rb_dev, lambda r: rounded_block(now_ref, scale_ref, r, order), x_ref)
-    multiply(plan_ref, 0, hi, loaded(copy, tiles_ref, 0), lambda c: x_ref[jnp.minimum(c, rb_dev)], acc_ref)
+    for r in range(rb_dev):
+        x_ref[r] = rounded_block(now_ref, scale_ref, r, order)
+
+    def group(g, _):
+        for copy in copies(g):
+            copy.wait()
+        done = []
+        for t in [g * UNROLL + j for j in range(UNROLL)]:
+            x = x_ref[slots_ref[t]]
+            done.append([lax.dot_general(x, tiles_ref[i, t], NT, preferred_element_type=F32) for i in range(2)])
+        for j, products in enumerate(done):
+            row = rows_ref[g * UNROLL + j]
+            for i, product in enumerate(products):
+                acc_ref[i, row] = acc_ref[i, row] + product
+        return _
+
+    lax.fori_loop(0, groups, group, 0)
     for r in range(rb_dev):
         at = slice(r * order, (r + 1) * order)
-        applied = scale_ref[0:1, at] * collect(acc_ref[r], size)
+        applied = scale_ref[0:1, at] * (acc_ref[0, r] + turn_rows(acc_ref[1, r]))
         moved = ((1.0 - center) * now_ref[:, at] - applied) / half_width
         base_ref[:, at] = moved if step == 0 else 2.0 * moved - before_ref[:, at]
 
@@ -359,17 +378,23 @@
         out_hbm, sent_ref, out_sems = refs[1:4]
     tiles_ref, x_ref, acc_ref, sems = refs[-4:]
     rb_dev, _, order = acc_ref.shape
-    end = plan_ref.shape[0] - 32
-    lo, hi = plan_ref[end], plan_ref[end + 1]
-    stay = jnp.minimum(lo + KEPT // UNROLL, hi)
-    copy = load_groups(packed_hbm, tiles_ref, sems, stay, hi)
+    stay = KEPT // UNROLL
+    groups = plan_ref[plan_ref.shape[0] - 32]
+    copy = load_groups(packed_hbm, tiles_ref, sems, groups - stay)
     acc_ref[...] = jnp.zeros_like(acc_ref)
     size = split_sources(arrived_ref.shape[0], lambda p: arrived_ref[p], x_ref)
     size = size * ((1.0 if step == 0 else 2.0) / half_width)
-    multiply(
-        plan_ref, lo, stay, lambda g, j: kept_ref[(g - lo) * UNROLL + j], lambda c: x_ref[c - rb_dev], acc_ref
-    )
-    multiply(plan_ref, stay, hi, loaded(copy, tiles_ref, stay), lambda c: x_ref[c - rb_dev], acc_ref)
+
+    def loaded(g, j):
+        if j == 0:
+            copy(g - stay).wait()
+        return tiles_ref[(g - stay) * UNROLL + j]
+
+    def load(place):
+        return x_ref[place]
+
+    multiply(plan_ref, 0, jnp.minimum(stay, groups), lambda g, j: kept_ref[g * UNROLL + j], load, acc_ref)
+    multiply(plan_ref, stay, groups, loaded, load, acc_ref)
     for r in range(rb_dev):
         at = slice(r * order, (r + 1) * order)
         scale = scale_ref[0:1, at]
@@ -401,6 +426,7 @@
 
 
 PANEL = 64
+PIECES = 4
 SUB = 8
 
 
@@ -447,7 +473,7 @@
 
 
 def factor_kernel(nodes, own_ref, all_ref, *refs):
-    parts, (out_ref, work_ref, inverse_ref) = refs[:-3], refs[-3:]
+    parts, (out_hbm, work_ref, inverse_ref, piece_ref, sems) = refs[:-5], refs[-5:]
     group = own_ref.shape[0]
     order = work_ref.shape[0]
     total = parts[0][...]
@@ -477,20 +503,25 @@
     mine = mine * math.sqrt(nodes)
     high = mine.astype(BF16)
     low = (mine - high.astype(F32)).astype(BF16)
-    rows = all_ref[...].reshape(order, own_ref.shape[1])
-    both = lax.dot_general(
-        jnp.concatenate([high, low], axis=0), rows, (((1,), (0,)), ((), ())), preferred_element_type=F32
-    )
-    own = own_ref[...]
-    lost = own - own.astype(BF16).astype(F32)
     own_lanes = (
         lax.broadcasted_iota(I32, (order, group), 0)
         == lax.broadcasted_iota(I32, (order, group), 1) + c * group
     ).astype(BF16)
     square = jnp.dot(high, own_lanes, preferred_element_type=F32).astype(BF16)
-    out_ref[...] = (
-        both[:group] + both[group:] + jnp.dot(square, lost.astype(BF16), preferred_element_type=F32)
-    )
+    left = jnp.concatenate([high, low], axis=0)
+    width = own_ref.shape[1] // PIECES
+    copies = []
+    for i in range(PIECES):
+        at = slice(i * width, (i + 1) * width)
+        rows = all_ref[:, :, at].reshape(order, width)
+        both = jnp.dot(left, rows, preferred_element_type=F32)
+        own = own_ref[:, at]
+        lost = (own - own.astype(BF16).astype(F32)).astype(BF16)
+        piece_ref[i] = both[:group] + both[group:] + jnp.dot(square, lost, preferred_element_type=F32)
+        copies.append(pltpu.make_async_copy(piece_ref.at[i], out_hbm.at[:, at], sems.at[i]))
+        copies[-1].start()
+    for copy in copies:
+        copy.wait()
 
 
 def central(nblk):
@@ -538,14 +569,6 @@
         compiler_params=params(LIMIT),
     )(y_start, scale, wanted)
 
-    def scratch(entries, sources):
-        return [
-            pltpu.VMEM((entries, 2 * order, order), F8),
-            pltpu.VMEM((sources + 1, 2 * group, 2 * order), F8),
-            pltpu.VMEM((rb_dev, 2 * group, order), F32),
-            pltpu.SemaphoreType.DMA((entries // UNROLL,)),
-        ]
-
     vectors_here = sds((group, rows), F32)
     previous, current = y_start, y_start
     for step in range(STEPS):
@@ -554,12 +577,17 @@
             functools.partial(near_kernel, step),
             name="near",
             out_shape=vectors_here,
-            in_specs=[SMEM, ANY] + [VMEM] * 3,
+            in_specs=[SMEM, SMEM, ANY, ANY] + [VMEM] * 3,
             out_specs=VMEM,
-            scratch_shapes=scratch(near_count, rb_dev),
+            scratch_shapes=[
+                pltpu.VMEM((2, near_count, order, order), BF16),
+                pltpu.VMEM((rb_dev, group, order), BF16),
+                pltpu.VMEM((2, rb_dev, group, order), F32),
+                pltpu.SemaphoreType.DMA((near_count // UNROLL, 2)),
+            ],
             compiler_params=params(LIMIT),
             cost_estimate=pl.CostEstimate(flops=1 << 28, bytes_accessed=1 << 21, transcendentals=0),
-        )(in_hbm(plan), in_hbm(packed), scale, current, previous)
+        )(in_hbm(tile_rows), in_hbm(tile_slots), in_hbm(tile_real), in_hbm(tile_imag), scale, current, previous)
         last = step == STEPS - 1
         out = pl.pallas_call(
             functools.partial(step_kernel, step),
@@ -567,7 +595,13 @@
             out_shape=[vectors_here] if last else [vectors_here, out_blocks],
             in_specs=[SMEM, SMEM, ANY] + [VMEM] * 4,
             out_specs=[VMEM] if last else [VMEM, ANY],
-            scratch_shapes=([] if last else sent_scratch) + scratch(tiles - near_count - KEPT, nblk),
+            scratch_shapes=([] if last else sent_scratch)
+            + [
+                pltpu.VMEM(packed.shape, F8),
+                pltpu.VMEM((nblk + 1, 2 * group, 2 * order), F8),
+                pltpu.VMEM((rb_dev, 2 * group, order), F32),
+                pltpu.SemaphoreType.DMA((packed.shape[0] // UNROLL,)),
+            ],
             compiler_params=params(LIMIT),
         )(in_hbm(plan), wanted, in_hbm(packed), pltpu.with_memory_space_constraint(kept, pltpu.VMEM), scale, base, arrived)
         previous, current = current, out[0]
@@ -594,10 +628,11 @@
     return pl.pallas_call(
         functools.partial(factor_kernel, rows * nblk),
         name="factor",
-        out_shape=sds((group, rows), F32),
+        out_shape=pltpu.HBM((group, rows), F32),
         in_specs=[VMEM] * (2 + len(parts)),
-        out_specs=VMEM,
-        scratch_shapes=[pltpu.VMEM((vectors, vectors), F32)] * 2,
+        out_specs=ANY,
+        scratch_shapes=[pltpu.VMEM((vectors, vectors), F32)] * 2
+        + [pltpu.VMEM((PIECES, group, rows // PIECES), F32), pltpu.SemaphoreType.DMA((PIECES,))],
         compiler_params=params(LIMIT),
     )(current, gathered, *parts)
 

time: 102 us -> 101 us (level)
  waiting for transfers between devices: 22.9 us -> 18.6 us
  Pallas kernels: 47.1 us -> 50.6 us
    pallas_call x4, Pallas kernels: 10.6 us -> 15 us  [per_device(): pl.pallas_call(functools.partial(near_kernel, step), name='near', out_sha...]
    all_to_all x5, waiting for transfers between devices: 12.2 us -> 7.82 us  [exchange(): lax.all_to_all(x, 'blk', split_axis=0, concat_axis=0, tiled=True, axis_in...]
  transfers between devices with their start and end apart: 12 -> 12, of which waited for: 10 -> 10; matrix products, arithmetic and copies ran while one was open for 0% -> 0% of each run, Pallas kernels for 24% -> 28%
where the time goes in v17:
time: 101 us; the launch traced here: 99.6 us
  Pallas kernels  50.6 us (50%)
  starting transfers between devices  29 us (29%)
  waiting for transfers between devices  18.6 us (18%)
  local copies, waits for them, and re-layouts  1.25 us (1%)
    all_to_all x5, starting transfers between devices, exchange(): lax.all_to_all(x, 'blk', split_axis=0, concat_axis=0, tiled=True, axis_in...  22.8 us
    pallas_call x4, Pallas kernels, per_device(): pl.pallas_call(functools.partial(step_kernel, step), name='step', out_sha...  16.2 us
    pallas_call x4, Pallas kernels, per_device(): pl.pallas_call(functools.partial(near_kernel, step), name='near', out_sha...  15 us
    pallas_call x1, Pallas kernels, tiles_call(): pl.pallas_call(functools.partial(tiles_kernel, near_count), name='tiles',...  12.8 us
    ppermute x7, waiting for transfers between devices, to_partner(): return lax.ppermute(x, axis, [(i, i ^ mask) for i in range(n)])  10.8 us
    all_to_all x5, waiting for transfers between devices, exchange(): lax.all_to_all(x, 'blk', split_axis=0, concat_axis=0, tiled=True, axis_in...  7.82 us
    ppermute x7, starting transfers between devices, to_partner(): return lax.ppermute(x, axis, [(i, i ^ mask) for i in range(n)])  6.23 us
    pallas_call x1, Pallas kernels, per_device(): pl.pallas_call(functools.partial(factor_kernel, rows * nblk), name='facto...  4.79 us
  transfers between devices with their start and end apart: 12, of which 10 were waited for; matrix products, arithmetic and copies ran while one was open for 0% of the time, Pallas kernels for 28%

profile of v17, /device:TPU:0, one launch (start us, length us, event | category | flops | bytes accessed | tf_op | source)
XLA Modules:
  0.0 99.6 jit_solution(17595500918888167734)
XLA Ops:
  1.2 7.8 %all-to-all-start = ((s32[8,1,8]{2,1,0:T(1,128)}), s32[8,1,8]{2,1,0:T(1,128)S(1)}, u32[]{:S(2)}, u32[]{:S(2)}) async-start(s32[8,1,8]{2,1,0:T(1,128)} %broadcast_in_dim.9), calls=%async_computation | async-start | bytes 8192 | tf_op jit(solution)/shard_map/all_to_all | solution.py:534
  9.1 12.8 %tiles.1 = (f8e4m3fn[64,512,256]{2,1,0:T(32,128)(4,1)}, f8e4m3fn[16,512,256]{2,1,0:T(32,128)(4,1)S(1)}, f32[8,2048]{1,0:T(8,128)S(1)}, s32[128]{0:T(128)}) custom-call(s32[96]{0:T(128)} %rows_ref.7, s32[96]{0:T(128)} %slots_ref.7, bf16[96,256,256]{2,1,0:T(8,128)(2,1)} %real_hbm.9, bf16[96,256,256]{2,1,0:T(8,128)(2,1)} %imag_hbm.9), custom_call_target="tpu_custom_call" | custom-call | flops 268435456 | bytes 25165824 | tf_op jit(solution)/shard_map/tiles/pallas_call | solution.py:224
  23.3 4.9 %all-to-all-start.1 = ((bf16[8,32,256]{2,1,0:T(8,128)(2,1)}), bf16[8,32,256]{2,1,0:T(8,128)(2,1)S(1)}, u32[]{:S(2)}, u32[]{:S(2)}) async-start(bf16[8,32,256]{2,1,0:T(8,128)(2,1)} %first.1), calls=%async_computation.1 | async-start | bytes 262144 | tf_op jit(solution)/shard_map/all_to_all | solution.py:534
  28.2 3.7 %near.4.base_ref = f32[32,2048]{1,0:T(8,128)S(1)} custom-call(s32[96]{0:T(128)} %rows_ref.7, s32[96]{0:T(128)} %slots_ref.7, bf16[96,256,256]{2,1,0:T(8,128)(2,1)} %real_hbm.9, bf16[96,256,256]{2,1,0:T(8,128)(2,1)} %imag_hbm.9, f32[8,2048]{1,0:T(8,128)S(1)} %get-tuple-element.20.scale_ref, f32[32,2048]{1,0:T(8,128)S(1)} %copy-done, f32[32,2048]{1,0:T(8,128)S(1)} %copy-done), custom_call_target="tpu_custom_call" | custom-call | flops 268435456 | bytes 2097152 | tf_op jit(solution)/shard_map/near/pallas_call | solution.py:576
  32.0 2.0 %all-to-all-done.1.arrived_ref = bf16[8,32,256]{2,1,0:T(8,128)(2,1)S(1)} async-done(((bf16[8,32,256]{2,1,0:T(8,128)(2,1)}), bf16[8,32,256]{2,1,0:T(8,128)(2,1)S(1)}, u32[]{:S(2)}, u32[]{:S(2)}) %all-to-all-start.1) | async-done | bytes 131104 | tf_op jit(solution)/shard_map/all_to_all | solution.py:534
  33.9 4.2 %step.4 = (f32[32,2048]{1,0:T(8,128)S(1)}, bf16[8,32,256]{2,1,0:T(8,128)(2,1)}) custom-call(s32[128]{0:T(128)} %get-tuple-element.17.plan_ref, s32[8,1,8]{2,1,0:T(1,128)S(1)} %all-to-all-done.wanted_ref, f8e4m3fn[64,512,256]{2,1,0:T(32,128)(4,1)} %get-tuple-element.18.packed_hbm, f8e4m3fn[16,512,256]{2,1,0:T(32,128)(4,1)S(1)} %get-tuple-element.19.kept_ref, ...), custom_call_target="tpu_custom_call" | custom-call | tf_op jit(solution)/shard_map/step/pallas_call | solution.py:592
  38.2 3.3 %all-to-all-start.2 = ((bf16[8,32,256]{2,1,0:T(8,128)(2,1)}), bf16[8,32,256]{2,1,0:T(8,128)(2,1)S(1)}, u32[]{:S(2)}, u32[]{:S(2)}) async-start(bf16[8,32,256]{2,1,0:T(8,128)(2,1)} %get-tuple-element.22), calls=%async_computation.2 | async-start | bytes 262144 | tf_op jit(solution)/shard_map/all_to_all | solution.py:534
  41.5 3.8 %near.5.base_ref = f32[32,2048]{1,0:T(8,128)S(1)} custom-call(s32[96]{0:T(128)} %rows_ref.7, s32[96]{0:T(128)} %slots_ref.7, bf16[96,256,256]{2,1,0:T(8,128)(2,1)} %real_hbm.9, bf16[96,256,256]{2,1,0:T(8,128)(2,1)} %imag_hbm.9, f32[8,2048]{1,0:T(8,128)S(1)} %get-tuple-element.20.scale_ref, f32[32,2048]{1,0:T(8,128)S(1)} %get-tuple-element.21.now_ref.before_ref, ...), custom_call_target="tpu_custom_call" | custom-call | flops 268435456 | bytes 2097152 | tf_op jit(solution)/shard_map/near/pallas_call | solution.py:576
  45.3 1.9 %all-to-all-done.2.arrived_ref = bf16[8,32,256]{2,1,0:T(8,128)(2,1)S(1)} async-done(((bf16[8,32,256]{2,1,0:T(8,128)(2,1)}), bf16[8,32,256]{2,1,0:T(8,128)(2,1)S(1)}, u32[]{:S(2)}, u32[]{:S(2)}) %all-to-all-start.2) | async-done | bytes 131104 | tf_op jit(solution)/shard_map/all_to_all | solution.py:534
  47.2 4.2 %step.5 = (f32[32,2048]{1,0:T(8,128)S(1)}, bf16[8,32,256]{2,1,0:T(8,128)(2,1)}) custom-call(s32[128]{0:T(128)} %get-tuple-element.17.plan_ref, s32[8,1,8]{2,1,0:T(1,128)S(1)} %all-to-all-done.wanted_ref, f8e4m3fn[64,512,256]{2,1,0:T(32,128)(4,1)} %get-tuple-element.18.packed_hbm, f8e4m3fn[16,512,256]{2,1,0:T(32,128)(4,1)S(1)} %get-tuple-element.19.kept_ref, ...), custom_call_target="tpu_custom_call" | custom-call | tf_op jit(solution)/shard_map/step/pallas_call | solution.py:592
  51.5 3.3 %all-to-all-start.3 = ((bf16[8,32,256]{2,1,0:T(8,128)(2,1)}), bf16[8,32,256]{2,1,0:T(8,128)(2,1)S(1)}, u32[]{:S(2)}, u32[]{:S(2)}) async-start(bf16[8,32,256]{2,1,0:T(8,128)(2,1)} %get-tuple-element.24), calls=%async_computation.3 | async-start | bytes 262144 | tf_op jit(solution)/shard_map/all_to_all | solution.py:534
  54.8 3.8 %near.6.base_ref = f32[32,2048]{1,0:T(8,128)S(1)} custom-call(s32[96]{0:T(128)} %rows_ref.7, s32[96]{0:T(128)} %slots_ref.7, bf16[96,256,256]{2,1,0:T(8,128)(2,1)} %real_hbm.9, bf16[96,256,256]{2,1,0:T(8,128)(2,1)} %imag_hbm.9, f32[8,2048]{1,0:T(8,128)S(1)} %get-tuple-element.20.scale_ref, f32[32,2048]{1,0:T(8,128)S(1)} %get-tuple-element.23.now_ref.before_ref, ...), custom_call_target="tpu_custom_call" | custom-call | flops 268435456 | bytes 2097152 | tf_op jit(solution)/shard_map/near/pallas_call | solution.py:576
  58.6 1.9 %all-to-all-done.3.arrived_ref = bf16[8,32,256]{2,1,0:T(8,128)(2,1)S(1)} async-done(((bf16[8,32,256]{2,1,0:T(8,128)(2,1)}), bf16[8,32,256]{2,1,0:T(8,128)(2,1)S(1)}, u32[]{:S(2)}, u32[]{:S(2)}) %all-to-all-start.3) | async-done | bytes 131104 | tf_op jit(solution)/shard_map/all_to_all | solution.py:534
  60.5 4.2 %step.6 = (f32[32,2048]{1,0:T(8,128)S(1)}, bf16[8,32,256]{2,1,0:T(8,128)(2,1)}) custom-call(s32[128]{0:T(128)} %get-tuple-element.17.plan_ref, s32[8,1,8]{2,1,0:T(1,128)S(1)} %all-to-all-done.wanted_ref, f8e4m3fn[64,512,256]{2,1,0:T(32,128)(4,1)} %get-tuple-element.18.packed_hbm, f8e4m3fn[16,512,256]{2,1,0:T(32,128)(4,1)S(1)} %get-tuple-element.19.kept_ref, ...), custom_call_target="tpu_custom_call" | custom-call | tf_op jit(solution)/shard_map/step/pallas_call | solution.py:592
  64.8 3.3 %all-to-all-start.4 = ((bf16[8,32,256]{2,1,0:T(8,128)(2,1)}), bf16[8,32,256]{2,1,0:T(8,128)(2,1)S(1)}, u32[]{:S(2)}, u32[]{:S(2)}) async-start(bf16[8,32,256]{2,1,0:T(8,128)(2,1)} %get-tuple-element.26), calls=%async_computation.4 | async-start | bytes 262144 | tf_op jit(solution)/shard_map/all_to_all | solution.py:534
  68.1 3.8 %near.7.base_ref = f32[32,2048]{1,0:T(8,128)S(1)} custom-call(s32[96]{0:T(128)} %rows_ref.7, s32[96]{0:T(128)} %slots_ref.7, bf16[96,256,256]{2,1,0:T(8,128)(2,1)} %real_hbm.9, bf16[96,256,256]{2,1,0:T(8,128)(2,1)} %imag_hbm.9, f32[8,2048]{1,0:T(8,128)S(1)} %get-tuple-element.20.scale_ref, f32[32,2048]{1,0:T(8,128)S(1)} %get-tuple-element.25.now_ref, ...), custom_call_target="tpu_custom_call" | custom-call | flops 268435456 | bytes 2097152 | tf_op jit(solution)/shard_map/near/pallas_call | solution.py:576
  71.9 2.0 %all-to-all-done.4.arrived_ref = bf16[8,32,256]{2,1,0:T(8,128)(2,1)S(1)} async-done(((bf16[8,32,256]{2,1,0:T(8,128)(2,1)}), bf16[8,32,256]{2,1,0:T(8,128)(2,1)S(1)}, u32[]{:S(2)}, u32[]{:S(2)}) %all-to-all-start.4) | async-done | bytes 131104 | tf_op jit(solution)/shard_map/all_to_all | solution.py:534
  73.8 3.5 %step.7.own_ref = f32[32,2048]{1,0:T(8,128)S(1)} custom-call(s32[128]{0:T(128)} %get-tuple-element.17.plan_ref, s32[8,1,8]{2,1,0:T(1,128)S(1)} %all-to-all-done.wanted_ref, f8e4m3fn[64,512,256]{2,1,0:T(32,128)(4,1)} %get-tuple-element.18.packed_hbm, f8e4m3fn[16,512,256]{2,1,0:T(32,128)(4,1)S(1)} %get-tuple-element.19.kept_ref, ...), custom_call_target="tpu_custom_call" | custom-call | tf_op jit(solution)/shard_map/step/pallas_call | solution.py:592
  77.4 1.6 %collective-permute-start.1 = (bf16[32,2048]{1,0:T(8,128)(2,1)S(1)}, bf16[32,2048]{1,0:T(8,128)(2,1)S(1)}, u32[]{:S(2)}, u32[]{:S(2)}) collective-permute-start(bf16[32,2048]{1,0:T(8,128)(2,1)S(1)} %convert_element_type.3), channel_id=1, source_target_pairs={{0,2},{1,3},{2,0},{3,1},{4,6},{5,7},{6,4},{7,5},{8,10},{9,11},{10,... | collective-permute-start | bytes 393224 | tf_op jit(solution)/shard_map/ppermute | solution.py:539
  78.9 3.5 %collective-permute-done.1.refs_1_ = bf16[32,2048]{1,0:T(8,128)(2,1)S(1)} collective-permute-done((bf16[32,2048]{1,0:T(8,128)(2,1)S(1)}, bf16[32,2048]{1,0:T(8,128)(2,1)S(1)}, u32[]{:S(2)}, u32[]{:S(2)}) %collective-permute-start.1) | collective-permute-done | bytes 131104 | tf_op jit(solution)/shard_map/ppermute | solution.py:539
  84.4 3.7 %collective-permute-done.3 = f32[64,128]{1,0:T(8,128)S(1)} collective-permute-done((f32[64,128]{1,0:T(8,128)S(1)}, f32[64,128]{1,0:T(8,128)S(1)}, u32[]{:S(2)}, u32[]{:S(2)}) %collective-permute-start.3) | collective-permute-done | bytes 32800 | tf_op jit(solution)/shard_map/ppermute | solution.py:539
  88.1 1.4 %collective-permute-start.6 = (f32[64,128]{1,0:T(8,128)S(1)}, f32[64,128]{1,0:T(8,128)S(1)}, u32[]{:S(2)}, u32[]{:S(2)}) collective-permute-start(f32[64,128]{1,0:T(8,128)S(1)} %add.3.refs_0_), channel_id=1, source_target_pairs={{0,24},{4,28},{8,16},{12,20},{16,8},{20,12},{24,0},{28,4},{1,25},{... | collective-permute-start | bytes 98312 | tf_op jit(solution)/shard_map/ppermute | solution.py:539
  89.6 2.9 %collective-permute-start.4 = (f32[64,128]{1,0:T(8,128)S(1)}, f32[64,128]{1,0:T(8,128)S(1)}, u32[]{:S(2)}, u32[]{:S(2)}) collective-permute-start(f32[64,128]{1,0:T(8,128)S(1)} %add.3.refs_0_), channel_id=1, source_target_pairs={{0,8},{4,12},{8,0},{12,4},{16,24},{20,28},{24,16},{28,20},{1,9},{5... | collective-permute-start | bytes 98312 | tf_op jit(solution)/shard_map/ppermute | solution.py:539
  94.8 4.8 %factor.1 = f32[32,2048]{1,0:T(8,128)} custom-call(f32[32,2048]{1,0:T(8,128)S(1)} %step.7.own_ref, bf16[4,32,2048]{2,1,0:T(8,128)(2,1)S(1)} %get-tuple-element.27.all_ref, f32[64,128]{1,0:T(8,128)S(1)} %add.3.refs_0_, f32[64,128]{1,0:T(8,128)S(1)} %collective-permute-done.4.refs_1_, f32[64,128]{1,0:T(8,128)S(1)} %collective-permute-done.5.refs_2_, ...), custom_call_target="tpu_custom_call" | custom-call | tf_op jit(solution)/shard_map/factor/pallas_call | solution.py:628
  (17 shorter events, 7.0 us)
Async XLA Ops:
  1.2 20.7 %all-to-all-start = ((s32[8,1,8]{2,1,0:T(1,128)}), s32[8,1,8]{2,1,0:T(1,128)S(1)}, u32[]{:S(2)}, u32[]{:S(2)}) async-start(s32[8,1,8]{2,1,0:T(1,128)} %broadcast_in_dim.9), calls=%async_computation | async-start | bytes 8192 | tf_op jit(solution)/shard_map/all_to_all | solution.py:534
  9.1 12.9 %copy-start = (f32[32,2048]{1,0:T(8,128)S(1)}, f32[32,2048]{1,0:T(8,128)}, u32[]{:S(2)}) copy-start(f32[32,2048]{1,0:T(8,128)} %before_ref.3) | copy-start | bytes 786436
  23.3 10.6 %all-to-all-start.1 = ((bf16[8,32,256]{2,1,0:T(8,128)(2,1)}), bf16[8,32,256]{2,1,0:T(8,128)(2,1)S(1)}, u32[]{:S(2)}, u32[]{:S(2)}) async-start(bf16[8,32,256]{2,1,0:T(8,128)(2,1)} %first.1), calls=%async_computation.1 | async-start | bytes 262144 | tf_op jit(solution)/shard_map/all_to_all | solution.py:534
  38.2 9.1 %all-to-all-start.2 = ((bf16[8,32,256]{2,1,0:T(8,128)(2,1)}), bf16[8,32,256]{2,1,0:T(8,128)(2,1)S(1)}, u32[]{:S(2)}, u32[]{:S(2)}) async-start(bf16[8,32,256]{2,1,0:T(8,128)(2,1)} %get-tuple-element.22), calls=%async_computation.2 | async-start | bytes 262144 | tf_op jit(solution)/shard_map/all_to_all | solution.py:534
  51.5 9.1 %all-to-all-start.3 = ((bf16[8,32,256]{2,1,0:T(8,128)(2,1)}), bf16[8,32,256]{2,1,0:T(8,128)(2,1)S(1)}, u32[]{:S(2)}, u32[]{:S(2)}) async-start(bf16[8,32,256]{2,1,0:T(8,128)(2,1)} %get-tuple-element.24), calls=%async_computation.3 | async-start | bytes 262144 | tf_op jit(solution)/shard_map/all_to_all | solution.py:534
  64.8 9.1 %all-to-all-start.4 = ((bf16[8,32,256]{2,1,0:T(8,128)(2,1)}), bf16[8,32,256]{2,1,0:T(8,128)(2,1)S(1)}, u32[]{:S(2)}, u32[]{:S(2)}) async-start(bf16[8,32,256]{2,1,0:T(8,128)(2,1)} %get-tuple-element.26), calls=%async_computation.4 | async-start | bytes 262144 | tf_op jit(solution)/shard_map/all_to_all | solution.py:534
  77.4 5.0 %collective-permute-start.1 = (bf16[32,2048]{1,0:T(8,128)(2,1)S(1)}, bf16[32,2048]{1,0:T(8,128)(2,1)S(1)}, u32[]{:S(2)}, u32[]{:S(2)}) collective-permute-start(bf16[32,2048]{1,0:T(8,128)(2,1)S(1)} %convert_element_type.3), channel_id=1, source_target_pairs={{0,2},{1,3},{2,0},{3,1},{4,6},{5,7},{6,4},{7,5},{8,10},{9,11},{10,... | collective-permute-start | bytes 393224 | tf_op jit(solution)/shard_map/ppermute | solution.py:539
  78.9 3.5 %collective-permute-start = (bf16[32,2048]{1,0:T(8,128)(2,1)S(1)}, bf16[32,2048]{1,0:T(8,128)(2,1)S(1)}, u32[]{:S(2)}, u32[]{:S(2)}) collective-permute-start(bf16[32,2048]{1,0:T(8,128)(2,1)S(1)} %convert_element_type.3), channel_id=1, source_target_pairs={{0,1},{1,0},{2,3},{3,2},{4,5},{5,4},{6,7},{7,6},{8,9},{9,8},{10,11... | collective-permute-start | bytes 393224 | tf_op jit(solution)/shard_map/ppermute | solution.py:539
  82.4 1.3 %collective-permute-start.2 = (bf16[32,2048]{1,0:T(8,128)(2,1)S(1)}, bf16[32,2048]{1,0:T(8,128)(2,1)S(1)}, u32[]{:S(2)}, u32[]{:S(2)}) collective-permute-start(bf16[32,2048]{1,0:T(8,128)(2,1)S(1)} %collective-permute-done.1.refs_1_), channel_id=1, source_target_pairs={{0,1},{1,0},{2,3},{3,2},{4,5},{5,4},{6,7},{7,6},{8,9},{9,8},{10,11... | collective-permute-start | bytes 393224 | tf_op jit(solution)/shard_map/ppermute | solution.py:539
  84.2 4.0 %collective-permute-start.3 = (f32[64,128]{1,0:T(8,128)S(1)}, f32[64,128]{1,0:T(8,128)S(1)}, u32[]{:S(2)}, u32[]{:S(2)}) collective-permute-start(f32[64,128]{1,0:T(8,128)S(1)} %get-tuple-element.28), channel_id=1, source_target_pairs={{0,4},{4,0},{8,12},{12,8},{16,20},{20,16},{24,28},{28,24},{1,5},{5... | collective-permute-start | bytes 98312 | tf_op jit(solution)/shard_map/ppermute | solution.py:539
  88.1 5.7 %collective-permute-start.6 = (f32[64,128]{1,0:T(8,128)S(1)}, f32[64,128]{1,0:T(8,128)S(1)}, u32[]{:S(2)}, u32[]{:S(2)}) collective-permute-start(f32[64,128]{1,0:T(8,128)S(1)} %add.3.refs_0_), channel_id=1, source_target_pairs={{0,24},{4,28},{8,16},{12,20},{16,8},{20,12},{24,0},{28,4},{1,25},{... | collective-permute-start | bytes 98312 | tf_op jit(solution)/shard_map/ppermute | solution.py:539
  89.6 5.1 %collective-permute-start.5 = (f32[64,128]{1,0:T(8,128)S(1)}, f32[64,128]{1,0:T(8,128)S(1)}, u32[]{:S(2)}, u32[]{:S(2)}) collective-permute-start(f32[64,128]{1,0:T(8,128)S(1)} %add.3.refs_0_), channel_id=1, source_target_pairs={{0,16},{4,20},{8,24},{12,28},{16,0},{20,4},{24,8},{28,12},{1,17},{... | collective-permute-start | bytes 98312 | tf_op jit(solution)/shard_map/ppermute | solution.py:539
  89.6 5.1 %collective-permute-start.4 = (f32[64,128]{1,0:T(8,128)S(1)}, f32[64,128]{1,0:T(8,128)S(1)}, u32[]{:S(2)}, u32[]{:S(2)}) collective-permute-start(f32[64,128]{1,0:T(8,128)S(1)} %add.3.refs_0_), channel_id=1, source_target_pairs={{0,8},{4,12},{8,0},{12,4},{16,24},{20,28},{24,16},{28,20},{1,9},{5... | collective-permute-start | bytes 98312 | tf_op jit(solution)/shard_map/ppermute | solution.py:539

commit v18 on v17

--- a/solution.py
+++ b/solution.py
@@ -10,7 +10,8 @@
 
 LOC_RB = 2
 STEPS = 4
-UNROLL = 4
+UNROLL = 8
+NEAR_UNROLL = 4
 KEPT = 16
 CHUNK = 4
 MERGE = 16
@@ -337,7 +338,7 @@
     groups = sems.shape[0]
 
     def copies(g):
-        at = pl.ds(g * UNROLL, UNROLL)
+        at = pl.ds(g * NEAR_UNROLL, NEAR_UNROLL)
         return [
             pltpu.make_async_copy(hbm.at[at], tiles_ref.at[i, at], sems.at[g, i])
             for i, hbm in enumerate((real_hbm, imag_hbm))
@@ -354,11 +355,11 @@
         for copy in copies(g):
             copy.wait()
         done = []
-        for t in [g * UNROLL + j for j in range(UNROLL)]:
+        for t in [g * NEAR_UNROLL + j for j in range(NEAR_UNROLL)]:
             x = x_ref[slots_ref[t]]
             done.append([lax.dot_general(x, tiles_ref[i, t], NT, preferred_element_type=F32) for i in range(2)])
         for j, products in enumerate(done):
-            row = rows_ref[g * UNROLL + j]
+            row = rows_ref[g * NEAR_UNROLL + j]
             for i, product in enumerate(products):
                 acc_ref[i, row] = acc_ref[i, row] + product
         return _
@@ -583,7 +584,7 @@
                 pltpu.VMEM((2, near_count, order, order), BF16),
                 pltpu.VMEM((rb_dev, group, order), BF16),
                 pltpu.VMEM((2, rb_dev, group, order), F32),
-                pltpu.SemaphoreType.DMA((near_count // UNROLL, 2)),
+                pltpu.SemaphoreType.DMA((near_count // NEAR_UNROLL, 2)),
             ],
             compiler_params=params(LIMIT),
             cost_estimate=pl.CostEstimate(flops=1 << 28, bytes_accessed=1 << 21, transcendentals=0),

time: 101 us -> 100 us (0.990)
  no operation moved by 1% of the time
where the time goes in v18:
time: 100 us; the launch traced here: 99.6 us
  Pallas kernels  49.9 us (50%)
  starting transfers between devices  29.7 us (30%)
  waiting for transfers between devices  18.6 us (19%)
  local copies, waits for them, and re-layouts  1.25 us (1%)
    all_to_all x5, starting transfers between devices, exchange(): lax.all_to_all(x, 'blk', split_axis=0, concat_axis=0, tiled=True, axis_in...  23.5 us
    pallas_call x4, Pallas kernels, per_device(): pl.pallas_call(functools.partial(step_kernel, step), name='step', out_sha...  15.3 us
    pallas_call x4, Pallas kernels, per_device(): pl.pallas_call(functools.partial(near_kernel, step), name='near', out_sha...  15 us
    pallas_call x1, Pallas kernels, tiles_call(): pl.pallas_call(functools.partial(tiles_kernel, near_count), name='tiles',...  13 us
    ppermute x7, waiting for transfers between devices, to_partner(): return lax.ppermute(x, axis, [(i, i ^ mask) for i in range(n)])  10.8 us
    all_to_all x5, waiting for transfers between devices, exchange(): lax.all_to_all(x, 'blk', split_axis=0, concat_axis=0, tiled=True, axis_in...  7.82 us
    ppermute x7, starting transfers between devices, to_partner(): return lax.ppermute(x, axis, [(i, i ^ mask) for i in range(n)])  6.23 us
    pallas_call x1, Pallas kernels, per_device(): pl.pallas_call(functools.partial(factor_kernel, rows * nblk), name='facto...  4.79 us
  transfers between devices with their start and end apart: 12, of which 10 were waited for; matrix products, arithmetic and copies ran while one was open for 0% of the time, Pallas kernels for 28%

profile of v18, /device:TPU:0, one launch (start us, length us, event | category | flops | bytes accessed | tf_op | source)
XLA Modules:
  0.0 99.6 jit_solution(3921216007531312854)
XLA Ops:
  1.2 7.8 %all-to-all-start = ((s32[8,1,8]{2,1,0:T(1,128)}), s32[8,1,8]{2,1,0:T(1,128)S(1)}, u32[]{:S(2)}, u32[]{:S(2)}) async-start(s32[8,1,8]{2,1,0:T(1,128)} %broadcast_in_dim.9), calls=%async_computation | async-start | bytes 8192 | tf_op jit(solution)/shard_map/all_to_all | solution.py:535
  9.1 13.0 %tiles.1 = (f8e4m3fn[64,512,256]{2,1,0:T(32,128)(4,1)}, f8e4m3fn[16,512,256]{2,1,0:T(32,128)(4,1)S(1)}, f32[8,2048]{1,0:T(8,128)S(1)}, s32[128]{0:T(128)}) custom-call(s32[96]{0:T(128)} %rows_ref.7, s32[96]{0:T(128)} %slots_ref.7, bf16[96,256,256]{2,1,0:T(8,128)(2,1)} %real_hbm.9, bf16[96,256,256]{2,1,0:T(8,128)(2,1)} %imag_hbm.9), custom_call_target="tpu_custom_call" | custom-call | flops 268435456 | bytes 25165824 | tf_op jit(solution)/shard_map/tiles/pallas_call | solution.py:225
  23.5 5.2 %all-to-all-start.1 = ((bf16[8,32,256]{2,1,0:T(8,128)(2,1)}), bf16[8,32,256]{2,1,0:T(8,128)(2,1)S(1)}, u32[]{:S(2)}, u32[]{:S(2)}) async-start(bf16[8,32,256]{2,1,0:T(8,128)(2,1)} %first.1), calls=%async_computation.1 | async-start | bytes 262144 | tf_op jit(solution)/shard_map/all_to_all | solution.py:535
  28.7 3.7 %near.4.base_ref = f32[32,2048]{1,0:T(8,128)S(1)} custom-call(s32[96]{0:T(128)} %rows_ref.7, s32[96]{0:T(128)} %slots_ref.7, bf16[96,256,256]{2,1,0:T(8,128)(2,1)} %real_hbm.9, bf16[96,256,256]{2,1,0:T(8,128)(2,1)} %imag_hbm.9, f32[8,2048]{1,0:T(8,128)S(1)} %get-tuple-element.20.scale_ref, f32[32,2048]{1,0:T(8,128)S(1)} %copy-done, f32[32,2048]{1,0:T(8,128)S(1)} %copy-done), custom_call_target="tpu_custom_call" | custom-call | flops 268435456 | bytes 2097152 | tf_op jit(solution)/shard_map/near/pallas_call | solution.py:577
  32.4 2.0 %all-to-all-done.1.arrived_ref = bf16[8,32,256]{2,1,0:T(8,128)(2,1)S(1)} async-done(((bf16[8,32,256]{2,1,0:T(8,128)(2,1)}), bf16[8,32,256]{2,1,0:T(8,128)(2,1)S(1)}, u32[]{:S(2)}, u32[]{:S(2)}) %all-to-all-start.1) | async-done | bytes 131104 | tf_op jit(solution)/shard_map/all_to_all | solution.py:535
  34.4 4.0 %step.4 = (f32[32,2048]{1,0:T(8,128)S(1)}, bf16[8,32,256]{2,1,0:T(8,128)(2,1)}) custom-call(s32[128]{0:T(128)} %get-tuple-element.17.plan_ref, s32[8,1,8]{2,1,0:T(1,128)S(1)} %all-to-all-done.wanted_ref, f8e4m3fn[64,512,256]{2,1,0:T(32,128)(4,1)} %get-tuple-element.18.packed_hbm, f8e4m3fn[16,512,256]{2,1,0:T(32,128)(4,1)S(1)} %get-tuple-element.19.kept_ref, ...), custom_call_target="tpu_custom_call" | custom-call | tf_op jit(solution)/shard_map/step/pallas_call | solution.py:593
  38.4 3.5 %all-to-all-start.2 = ((bf16[8,32,256]{2,1,0:T(8,128)(2,1)}), bf16[8,32,256]{2,1,0:T(8,128)(2,1)S(1)}, u32[]{:S(2)}, u32[]{:S(2)}) async-start(bf16[8,32,256]{2,1,0:T(8,128)(2,1)} %get-tuple-element.22), calls=%async_computation.2 | async-start | bytes 262144 | tf_op jit(solution)/shard_map/all_to_all | solution.py:535
  41.9 3.8 %near.5.base_ref = f32[32,2048]{1,0:T(8,128)S(1)} custom-call(s32[96]{0:T(128)} %rows_ref.7, s32[96]{0:T(128)} %slots_ref.7, bf16[96,256,256]{2,1,0:T(8,128)(2,1)} %real_hbm.9, bf16[96,256,256]{2,1,0:T(8,128)(2,1)} %imag_hbm.9, f32[8,2048]{1,0:T(8,128)S(1)} %get-tuple-element.20.scale_ref, f32[32,2048]{1,0:T(8,128)S(1)} %get-tuple-element.21.now_ref.before_ref, ...), custom_call_target="tpu_custom_call" | custom-call | flops 268435456 | bytes 2097152 | tf_op jit(solution)/shard_map/near/pallas_call | solution.py:577
  45.7 1.9 %all-to-all-done.2.arrived_ref = bf16[8,32,256]{2,1,0:T(8,128)(2,1)S(1)} async-done(((bf16[8,32,256]{2,1,0:T(8,128)(2,1)}), bf16[8,32,256]{2,1,0:T(8,128)(2,1)S(1)}, u32[]{:S(2)}, u32[]{:S(2)}) %all-to-all-start.2) | async-done | bytes 131104 | tf_op jit(solution)/shard_map/all_to_all | solution.py:535
  47.6 4.0 %step.5 = (f32[32,2048]{1,0:T(8,128)S(1)}, bf16[8,32,256]{2,1,0:T(8,128)(2,1)}) custom-call(s32[128]{0:T(128)} %get-tuple-element.17.plan_ref, s32[8,1,8]{2,1,0:T(1,128)S(1)} %all-to-all-done.wanted_ref, f8e4m3fn[64,512,256]{2,1,0:T(32,128)(4,1)} %get-tuple-element.18.packed_hbm, f8e4m3fn[16,512,256]{2,1,0:T(32,128)(4,1)S(1)} %get-tuple-element.19.kept_ref, ...), custom_call_target="tpu_custom_call" | custom-call | tf_op jit(solution)/shard_map/step/pallas_call | solution.py:593
  51.6 3.5 %all-to-all-start.3 = ((bf16[8,32,256]{2,1,0:T(8,128)(2,1)}), bf16[8,32,256]{2,1,0:T(8,128)(2,1)S(1)}, u32[]{:S(2)}, u32[]{:S(2)}) async-start(bf16[8,32,256]{2,1,0:T(8,128)(2,1)} %get-tuple-element.24), calls=%async_computation.3 | async-start | bytes 262144 | tf_op jit(solution)/shard_map/all_to_all | solution.py:535
  55.1 3.8 %near.6.base_ref = f32[32,2048]{1,0:T(8,128)S(1)} custom-call(s32[96]{0:T(128)} %rows_ref.7, s32[96]{0:T(128)} %slots_ref.7, bf16[96,256,256]{2,1,0:T(8,128)(2,1)} %real_hbm.9, bf16[96,256,256]{2,1,0:T(8,128)(2,1)} %imag_hbm.9, f32[8,2048]{1,0:T(8,128)S(1)} %get-tuple-element.20.scale_ref, f32[32,2048]{1,0:T(8,128)S(1)} %get-tuple-element.23.now_ref.before_ref, ...), custom_call_target="tpu_custom_call" | custom-call | flops 268435456 | bytes 2097152 | tf_op jit(solution)/shard_map/near/pallas_call | solution.py:577
  58.9 1.9 %all-to-all-done.3.arrived_ref = bf16[8,32,256]{2,1,0:T(8,128)(2,1)S(1)} async-done(((bf16[8,32,256]{2,1,0:T(8,128)(2,1)}), bf16[8,32,256]{2,1,0:T(8,128)(2,1)S(1)}, u32[]{:S(2)}, u32[]{:S(2)}) %all-to-all-start.3) | async-done | bytes 131104 | tf_op jit(solution)/shard_map/all_to_all | solution.py:535
  60.8 4.0 %step.6 = (f32[32,2048]{1,0:T(8,128)S(1)}, bf16[8,32,256]{2,1,0:T(8,128)(2,1)}) custom-call(s32[128]{0:T(128)} %get-tuple-element.17.plan_ref, s32[8,1,8]{2,1,0:T(1,128)S(1)} %all-to-all-done.wanted_ref, f8e4m3fn[64,512,256]{2,1,0:T(32,128)(4,1)} %get-tuple-element.18.packed_hbm, f8e4m3fn[16,512,256]{2,1,0:T(32,128)(4,1)S(1)} %get-tuple-element.19.kept_ref, ...), custom_call_target="tpu_custom_call" | custom-call | tf_op jit(solution)/shard_map/step/pallas_call | solution.py:593
  64.8 3.5 %all-to-all-start.4 = ((bf16[8,32,256]{2,1,0:T(8,128)(2,1)}), bf16[8,32,256]{2,1,0:T(8,128)(2,1)S(1)}, u32[]{:S(2)}, u32[]{:S(2)}) async-start(bf16[8,32,256]{2,1,0:T(8,128)(2,1)} %get-tuple-element.26), calls=%async_computation.4 | async-start | bytes 262144 | tf_op jit(solution)/shard_map/all_to_all | solution.py:535
  68.3 3.8 %near.7.base_ref = f32[32,2048]{1,0:T(8,128)S(1)} custom-call(s32[96]{0:T(128)} %rows_ref.7, s32[96]{0:T(128)} %slots_ref.7, bf16[96,256,256]{2,1,0:T(8,128)(2,1)} %real_hbm.9, bf16[96,256,256]{2,1,0:T(8,128)(2,1)} %imag_hbm.9, f32[8,2048]{1,0:T(8,128)S(1)} %get-tuple-element.20.scale_ref, f32[32,2048]{1,0:T(8,128)S(1)} %get-tuple-element.25.now_ref, ...), custom_call_target="tpu_custom_call" | custom-call | flops 268435456 | bytes 2097152 | tf_op jit(solution)/shard_map/near/pallas_call | solution.py:577
  72.1 1.9 %all-to-all-done.4.arrived_ref = bf16[8,32,256]{2,1,0:T(8,128)(2,1)S(1)} async-done(((bf16[8,32,256]{2,1,0:T(8,128)(2,1)}), bf16[8,32,256]{2,1,0:T(8,128)(2,1)S(1)}, u32[]{:S(2)}, u32[]{:S(2)}) %all-to-all-start.4) | async-done | bytes 131104 | tf_op jit(solution)/shard_map/all_to_all | solution.py:535
  74.0 3.3 %step.7.own_ref = f32[32,2048]{1,0:T(8,128)S(1)} custom-call(s32[128]{0:T(128)} %get-tuple-element.17.plan_ref, s32[8,1,8]{2,1,0:T(1,128)S(1)} %all-to-all-done.wanted_ref, f8e4m3fn[64,512,256]{2,1,0:T(32,128)(4,1)} %get-tuple-element.18.packed_hbm, f8e4m3fn[16,512,256]{2,1,0:T(32,128)(4,1)S(1)} %get-tuple-element.19.kept_ref, ...), custom_call_target="tpu_custom_call" | custom-call | tf_op jit(solution)/shard_map/step/pallas_call | solution.py:593
  77.3 1.6 %collective-permute-start.1 = (bf16[32,2048]{1,0:T(8,128)(2,1)S(1)}, bf16[32,2048]{1,0:T(8,128)(2,1)S(1)}, u32[]{:S(2)}, u32[]{:S(2)}) collective-permute-start(bf16[32,2048]{1,0:T(8,128)(2,1)S(1)} %convert_element_type.3), channel_id=1, source_target_pairs={{0,2},{1,3},{2,0},{3,1},{4,6},{5,7},{6,4},{7,5},{8,10},{9,11},{10,... | collective-permute-start | bytes 393224 | tf_op jit(solution)/shard_map/ppermute | solution.py:540
  78.9 3.5 %collective-permute-done.1.refs_1_ = bf16[32,2048]{1,0:T(8,128)(2,1)S(1)} collective-permute-done((bf16[32,2048]{1,0:T(8,128)(2,1)S(1)}, bf16[32,2048]{1,0:T(8,128)(2,1)S(1)}, u32[]{:S(2)}, u32[]{:S(2)}) %collective-permute-start.1) | collective-permute-done | bytes 131104 | tf_op jit(solution)/shard_map/ppermute | solution.py:540
  84.4 3.7 %collective-permute-done.3 = f32[64,128]{1,0:T(8,128)S(1)} collective-permute-done((f32[64,128]{1,0:T(8,128)S(1)}, f32[64,128]{1,0:T(8,128)S(1)}, u32[]{:S(2)}, u32[]{:S(2)}) %collective-permute-start.3) | collective-permute-done | bytes 32800 | tf_op jit(solution)/shard_map/ppermute | solution.py:540
  88.1 1.6 %collective-permute-start.6 = (f32[64,128]{1,0:T(8,128)S(1)}, f32[64,128]{1,0:T(8,128)S(1)}, u32[]{:S(2)}, u32[]{:S(2)}) collective-permute-start(f32[64,128]{1,0:T(8,128)S(1)} %add.3.refs_0_), channel_id=1, source_target_pairs={{0,24},{4,28},{8,16},{12,20},{16,8},{20,12},{24,0},{28,4},{1,25},{... | collective-permute-start | bytes 98312 | tf_op jit(solution)/shard_map/ppermute | solution.py:540
  89.8 2.8 %collective-permute-start.4 = (f32[64,128]{1,0:T(8,128)S(1)}, f32[64,128]{1,0:T(8,128)S(1)}, u32[]{:S(2)}, u32[]{:S(2)}) collective-permute-start(f32[64,128]{1,0:T(8,128)S(1)} %add.3.refs_0_), channel_id=1, source_target_pairs={{0,8},{4,12},{8,0},{12,4},{16,24},{20,28},{24,16},{28,20},{1,9},{5... | collective-permute-start | bytes 98312 | tf_op jit(solution)/shard_map/ppermute | solution.py:540
  94.8 4.8 %factor.1 = f32[32,2048]{1,0:T(8,128)} custom-call(f32[32,2048]{1,0:T(8,128)S(1)} %step.7.own_ref, bf16[4,32,2048]{2,1,0:T(8,128)(2,1)S(1)} %get-tuple-element.27.all_ref, f32[64,128]{1,0:T(8,128)S(1)} %add.3.refs_0_, f32[64,128]{1,0:T(8,128)S(1)} %collective-permute-done.4.refs_1_, f32[64,128]{1,0:T(8,128)S(1)} %collective-permute-done.5.refs_2_, ...), custom_call_target="tpu_custom_call" | custom-call | tf_op jit(solution)/shard_map/factor/pallas_call | solution.py:629
  (17 shorter events, 6.9 us)
Async XLA Ops:
  1.2 20.9 %all-to-all-start = ((s32[8,1,8]{2,1,0:T(1,128)}), s32[8,1,8]{2,1,0:T(1,128)S(1)}, u32[]{:S(2)}, u32[]{:S(2)}) async-start(s32[8,1,8]{2,1,0:T(1,128)} %broadcast_in_dim.9), calls=%async_computation | async-start | bytes 8192 | tf_op jit(solution)/shard_map/all_to_all | solution.py:535
  9.1 13.1 %copy-start = (f32[32,2048]{1,0:T(8,128)S(1)}, f32[32,2048]{1,0:T(8,128)}, u32[]{:S(2)}) copy-start(f32[32,2048]{1,0:T(8,128)} %before_ref.3) | copy-start | bytes 786436
  23.5 10.9 %all-to-all-start.1 = ((bf16[8,32,256]{2,1,0:T(8,128)(2,1)}), bf16[8,32,256]{2,1,0:T(8,128)(2,1)S(1)}, u32[]{:S(2)}, u32[]{:S(2)}) async-start(bf16[8,32,256]{2,1,0:T(8,128)(2,1)} %first.1), calls=%async_computation.1 | async-start | bytes 262144 | tf_op jit(solution)/shard_map/all_to_all | solution.py:535
  38.4 9.2 %all-to-all-start.2 = ((bf16[8,32,256]{2,1,0:T(8,128)(2,1)}), bf16[8,32,256]{2,1,0:T(8,128)(2,1)S(1)}, u32[]{:S(2)}, u32[]{:S(2)}) async-start(bf16[8,32,256]{2,1,0:T(8,128)(2,1)} %get-tuple-element.22), calls=%async_computation.2 | async-start | bytes 262144 | tf_op jit(solution)/shard_map/all_to_all | solution.py:535
  51.6 9.2 %all-to-all-start.3 = ((bf16[8,32,256]{2,1,0:T(8,128)(2,1)}), bf16[8,32,256]{2,1,0:T(8,128)(2,1)S(1)}, u32[]{:S(2)}, u32[]{:S(2)}) async-start(bf16[8,32,256]{2,1,0:T(8,128)(2,1)} %get-tuple-element.24), calls=%async_computation.3 | async-start | bytes 262144 | tf_op jit(solution)/shard_map/all_to_all | solution.py:535
  64.8 9.2 %all-to-all-start.4 = ((bf16[8,32,256]{2,1,0:T(8,128)(2,1)}), bf16[8,32,256]{2,1,0:T(8,128)(2,1)S(1)}, u32[]{:S(2)}, u32[]{:S(2)}) async-start(bf16[8,32,256]{2,1,0:T(8,128)(2,1)} %get-tuple-element.26), calls=%async_computation.4 | async-start | bytes 262144 | tf_op jit(solution)/shard_map/all_to_all | solution.py:535
  77.3 5.0 %collective-permute-start.1 = (bf16[32,2048]{1,0:T(8,128)(2,1)S(1)}, bf16[32,2048]{1,0:T(8,128)(2,1)S(1)}, u32[]{:S(2)}, u32[]{:S(2)}) collective-permute-start(bf16[32,2048]{1,0:T(8,128)(2,1)S(1)} %convert_element_type.3), channel_id=1, source_target_pairs={{0,2},{1,3},{2,0},{3,1},{4,6},{5,7},{6,4},{7,5},{8,10},{9,11},{10,... | collective-permute-start | bytes 393224 | tf_op jit(solution)/shard_map/ppermute | solution.py:540
  78.9 3.5 %collective-permute-start = (bf16[32,2048]{1,0:T(8,128)(2,1)S(1)}, bf16[32,2048]{1,0:T(8,128)(2,1)S(1)}, u32[]{:S(2)}, u32[]{:S(2)}) collective-permute-start(bf16[32,2048]{1,0:T(8,128)(2,1)S(1)} %convert_element_type.3), channel_id=1, source_target_pairs={{0,1},{1,0},{2,3},{3,2},{4,5},{5,4},{6,7},{7,6},{8,9},{9,8},{10,11... | collective-permute-start | bytes 393224 | tf_op jit(solution)/shard_map/ppermute | solution.py:540
  82.4 1.3 %collective-permute-start.2 = (bf16[32,2048]{1,0:T(8,128)(2,1)S(1)}, bf16[32,2048]{1,0:T(8,128)(2,1)S(1)}, u32[]{:S(2)}, u32[]{:S(2)}) collective-permute-start(bf16[32,2048]{1,0:T(8,128)(2,1)S(1)} %collective-permute-done.1.refs_1_), channel_id=1, source_target_pairs={{0,1},{1,0},{2,3},{3,2},{4,5},{5,4},{6,7},{7,6},{8,9},{9,8},{10,11... | collective-permute-start | bytes 393224 | tf_op jit(solution)/shard_map/ppermute | solution.py:540
  84.2 4.0 %collective-permute-start.3 = (f32[64,128]{1,0:T(8,128)S(1)}, f32[64,128]{1,0:T(8,128)S(1)}, u32[]{:S(2)}, u32[]{:S(2)}) collective-permute-start(f32[64,128]{1,0:T(8,128)S(1)} %get-tuple-element.28), channel_id=1, source_target_pairs={{0,4},{4,0},{8,12},{12,8},{16,20},{20,16},{24,28},{28,24},{1,5},{5... | collective-permute-start | bytes 98312 | tf_op jit(solution)/shard_map/ppermute | solution.py:540
  88.1 5.7 %collective-permute-start.6 = (f32[64,128]{1,0:T(8,128)S(1)}, f32[64,128]{1,0:T(8,128)S(1)}, u32[]{:S(2)}, u32[]{:S(2)}) collective-permute-start(f32[64,128]{1,0:T(8,128)S(1)} %add.3.refs_0_), channel_id=1, source_target_pairs={{0,24},{4,28},{8,16},{12,20},{16,8},{20,12},{24,0},{28,4},{1,25},{... | collective-permute-start | bytes 98312 | tf_op jit(solution)/shard_map/ppermute | solution.py:540
  89.8 4.9 %collective-permute-start.5 = (f32[64,128]{1,0:T(8,128)S(1)}, f32[64,128]{1,0:T(8,128)S(1)}, u32[]{:S(2)}, u32[]{:S(2)}) collective-permute-start(f32[64,128]{1,0:T(8,128)S(1)} %add.3.refs_0_), channel_id=1, source_target_pairs={{0,16},{4,20},{8,24},{12,28},{16,0},{20,4},{24,8},{28,12},{1,17},{... | collective-permute-start | bytes 98312 | tf_op jit(solution)/shard_map/ppermute | solution.py:540
  89.8 5.0 %collective-permute-start.4 = (f32[64,128]{1,0:T(8,128)S(1)}, f32[64,128]{1,0:T(8,128)S(1)}, u32[]{:S(2)}, u32[]{:S(2)}) collective-permute-start(f32[64,128]{1,0:T(8,128)S(1)} %add.3.refs_0_), channel_id=1, source_target_pairs={{0,8},{4,12},{8,0},{12,4},{16,24},{20,28},{24,16},{28,20},{1,9},{5... | collective-permute-start | bytes 98312 | tf_op jit(solution)/shard_map/ppermute | solution.py:540

commit v19 on v18

--- a/solution.py
+++ b/solution.py
@@ -10,7 +10,8 @@
 
 LOC_RB = 2
 STEPS = 4
-UNROLL = 8
+UNROLL = 16
+LOAD = 8
 NEAR_UNROLL = 4
 KEPT = 16
 CHUNK = 4
@@ -168,7 +169,7 @@
 
             lax.while_loop(lambda prior: prior >= 0, add, back_ref[t])
             put(listed, t)
-            place = (slots_ref[t] - rb_dev) ^ central(slots - rb_dev)
+            place = place_of(slots_ref[t] - rb_dev, slots - rb_dev)
             plan_ref[listed] = rows_ref[t] | (place << 8)
 
         return listed + closes
@@ -275,13 +276,13 @@
     send_picked(wanted_ref, sent_ref, out_hbm, out_sems)
 
 
-def load_groups(packed_hbm, tiles_ref, sems, count):
-    def copy(g):
-        at = pl.ds(g * UNROLL, UNROLL)
-        return pltpu.make_async_copy(packed_hbm.at[at], tiles_ref.at[at], sems.at[g])
-
-    def begin(g, _):
-        copy(g).start()
+def load_tiles(packed_hbm, tiles_ref, sems, count):
+    def copy(part):
+        at = pl.ds(part * LOAD, LOAD)
+        return pltpu.make_async_copy(packed_hbm.at[at], tiles_ref.at[at], sems.at[part])
+
+    def begin(part, _):
+        copy(part).start()
         return _
 
     lax.fori_loop(0, count, begin, 0)
@@ -381,14 +382,14 @@
     rb_dev, _, order = acc_ref.shape
     stay = KEPT // UNROLL
     groups = plan_ref[plan_ref.shape[0] - 32]
-    copy = load_groups(packed_hbm, tiles_ref, sems, groups - stay)
+    copy = load_tiles(packed_hbm, tiles_ref, sems, (groups - stay) * (UNROLL // LOAD))
     acc_ref[...] = jnp.zeros_like(acc_ref)
     size = split_sources(arrived_ref.shape[0], lambda p: arrived_ref[p], x_ref)
     size = size * ((1.0 if step == 0 else 2.0) / half_width)
 
     def loaded(g, j):
-        if j == 0:
-            copy(g - stay).wait()
+        if j % LOAD == 0:
+            copy(((g - stay) * UNROLL + j) // LOAD).wait()
         return tiles_ref[(g - stay) * UNROLL + j]
 
     def load(place):
@@ -525,13 +526,18 @@
         copy.wait()
 
 
-def central(nblk):
-    return nblk // 4
+def place_of(device, nblk):
+    if nblk != 8:
+        return device ^ (nblk // 4)
+    z, y = device >> 1, device & 1
+    half = z >> 1
+    outer = (z & 1) ^ 1 ^ half
+    return half | (y << 1) | (outer << 2)
 
 
 def exchange(x):
     nblk = lax.axis_size("blk")
-    group = [i ^ central(nblk) for i in range(nblk)]
+    group = sorted(range(nblk), key=lambda device: place_of(device, nblk))
     return lax.all_to_all(x, "blk", split_axis=0, concat_axis=0, tiled=True, axis_index_groups=[group])
 
 
@@ -601,7 +607,7 @@
                 pltpu.VMEM(packed.shape, F8),
                 pltpu.VMEM((nblk + 1, 2 * group, 2 * order), F8),
                 pltpu.VMEM((rb_dev, 2 * group, order), F32),
-                pltpu.SemaphoreType.DMA((packed.shape[0] // UNROLL,)),
+                pltpu.SemaphoreType.DMA((packed.shape[0] // LOAD,)),
             ],
             compiler_params=params(LIMIT),
         )(in_hbm(plan), wanted, in_hbm(packed), pltpu.with_memory_space_constraint(kept, pltpu.VMEM), scale, base, arrived)

time: 100 us -> 102 us (1.020)
  starting transfers between devices: 29.7 us -> 31.7 us
    all_to_all x5, starting transfers between devices: 23.5 us -> 25 us  [exchange(): lax.all_to_all(x, 'blk', split_axis=0, concat_axis=0, tiled=True, axis_in...]
where the time goes in v19:
time: 102 us; the launch traced here: 101 us
  Pallas kernels  50.1 us (49%)
  starting transfers between devices  31.7 us (31%)
  waiting for transfers between devices  18.1 us (18%)
  local copies, waits for them, and re-layouts  1.25 us (1%)
    all_to_all x5, starting transfers between devices, exchange(): lax.all_to_all(x, 'blk', split_axis=0, concat_axis=0, tiled=True, axis_in...  25 us
    pallas_call x4, Pallas kernels, per_device(): pl.pallas_call(functools.partial(step_kernel, step), name='step', out_sha...  15.6 us
    pallas_call x4, Pallas kernels, per_device(): pl.pallas_call(functools.partial(near_kernel, step), name='near', out_sha...  15 us
    pallas_call x1, Pallas kernels, tiles_call(): pl.pallas_call(functools.partial(tiles_kernel, near_count), name='tiles',...  13 us
    ppermute x7, waiting for transfers between devices, to_partner(): return lax.ppermute(x, axis, [(i, i ^ mask) for i in range(n)])  10.2 us
    all_to_all x5, waiting for transfers between devices, exchange(): lax.all_to_all(x, 'blk', split_axis=0, concat_axis=0, tiled=True, axis_in...  7.87 us
    ppermute x7, starting transfers between devices, to_partner(): return lax.ppermute(x, axis, [(i, i ^ mask) for i in range(n)])  6.74 us
    pallas_call x1, Pallas kernels, per_device(): pl.pallas_call(functools.partial(factor_kernel, rows * nblk), name='facto...  4.79 us
  transfers between devices with their start and end apart: 12, of which 10 were waited for; matrix products, arithmetic and copies ran while one was open for 0% of the time, Pallas kernels for 28%

profile of v19, /device:TPU:0, one launch (start us, length us, event | category | flops | bytes accessed | tf_op | source)
XLA Modules:
  0.0 101.5 jit_solution(1252224470557074301)
XLA Ops:
  1.2 7.8 %all-to-all-start = ((s32[8,1,8]{2,1,0:T(1,128)}), s32[8,1,8]{2,1,0:T(1,128)S(1)}, u32[]{:S(2)}, u32[]{:S(2)}) async-start(s32[8,1,8]{2,1,0:T(1,128)} %broadcast_in_dim.9), calls=%async_computation | async-start | bytes 8192 | tf_op jit(solution)/shard_map/all_to_all | solution.py:541
  9.1 13.0 %tiles.1 = (f8e4m3fn[64,512,256]{2,1,0:T(32,128)(4,1)}, f8e4m3fn[16,512,256]{2,1,0:T(32,128)(4,1)S(1)}, f32[8,2048]{1,0:T(8,128)S(1)}, s32[128]{0:T(128)}) custom-call(s32[96]{0:T(128)} %rows_ref.7, s32[96]{0:T(128)} %slots_ref.7, bf16[96,256,256]{2,1,0:T(8,128)(2,1)} %real_hbm.9, bf16[96,256,256]{2,1,0:T(8,128)(2,1)} %imag_hbm.9), custom_call_target="tpu_custom_call" | custom-call | flops 268435456 | bytes 25165824 | tf_op jit(solution)/shard_map/tiles/pallas_call | solution.py:226
  23.4 5.0 %all-to-all-start.1 = ((bf16[8,32,256]{2,1,0:T(8,128)(2,1)}), bf16[8,32,256]{2,1,0:T(8,128)(2,1)S(1)}, u32[]{:S(2)}, u32[]{:S(2)}) async-start(bf16[8,32,256]{2,1,0:T(8,128)(2,1)} %first.1), calls=%async_computation.1 | async-start | bytes 262144 | tf_op jit(solution)/shard_map/all_to_all | solution.py:541
  28.5 3.7 %near.4.base_ref = f32[32,2048]{1,0:T(8,128)S(1)} custom-call(s32[96]{0:T(128)} %rows_ref.7, s32[96]{0:T(128)} %slots_ref.7, bf16[96,256,256]{2,1,0:T(8,128)(2,1)} %real_hbm.9, bf16[96,256,256]{2,1,0:T(8,128)(2,1)} %imag_hbm.9, f32[8,2048]{1,0:T(8,128)S(1)} %get-tuple-element.20.scale_ref, f32[32,2048]{1,0:T(8,128)S(1)} %copy-done, f32[32,2048]{1,0:T(8,128)S(1)} %copy-done), custom_call_target="tpu_custom_call" | custom-call | flops 268435456 | bytes 2097152 | tf_op jit(solution)/shard_map/near/pallas_call | solution.py:583
  32.2 2.0 %all-to-all-done.1.arrived_ref = bf16[8,32,256]{2,1,0:T(8,128)(2,1)S(1)} async-done(((bf16[8,32,256]{2,1,0:T(8,128)(2,1)}), bf16[8,32,256]{2,1,0:T(8,128)(2,1)S(1)}, u32[]{:S(2)}, u32[]{:S(2)}) %all-to-all-start.1) | async-done | bytes 131104 | tf_op jit(solution)/shard_map/all_to_all | solution.py:541
  34.2 4.0 %step.4 = (f32[32,2048]{1,0:T(8,128)S(1)}, bf16[8,32,256]{2,1,0:T(8,128)(2,1)}) custom-call(s32[128]{0:T(128)} %get-tuple-element.17.plan_ref, s32[8,1,8]{2,1,0:T(1,128)S(1)} %all-to-all-done.wanted_ref, f8e4m3fn[64,512,256]{2,1,0:T(32,128)(4,1)} %get-tuple-element.18.packed_hbm, f8e4m3fn[16,512,256]{2,1,0:T(32,128)(4,1)S(1)} %get-tuple-element.19.kept_ref, ...), custom_call_target="tpu_custom_call" | custom-call | tf_op jit(solution)/shard_map/step/pallas_call | solution.py:599
  38.2 4.0 %all-to-all-start.2 = ((bf16[8,32,256]{2,1,0:T(8,128)(2,1)}), bf16[8,32,256]{2,1,0:T(8,128)(2,1)S(1)}, u32[]{:S(2)}, u32[]{:S(2)}) async-start(bf16[8,32,256]{2,1,0:T(8,128)(2,1)} %get-tuple-element.22), calls=%async_computation.2 | async-start | bytes 262144 | tf_op jit(solution)/shard_map/all_to_all | solution.py:541
  42.3 3.8 %near.5.base_ref = f32[32,2048]{1,0:T(8,128)S(1)} custom-call(s32[96]{0:T(128)} %rows_ref.7, s32[96]{0:T(128)} %slots_ref.7, bf16[96,256,256]{2,1,0:T(8,128)(2,1)} %real_hbm.9, bf16[96,256,256]{2,1,0:T(8,128)(2,1)} %imag_hbm.9, f32[8,2048]{1,0:T(8,128)S(1)} %get-tuple-element.20.scale_ref, f32[32,2048]{1,0:T(8,128)S(1)} %get-tuple-element.21.now_ref.before_ref, ...), custom_call_target="tpu_custom_call" | custom-call | flops 268435456 | bytes 2097152 | tf_op jit(solution)/shard_map/near/pallas_call | solution.py:583
  46.0 2.0 %all-to-all-done.2.arrived_ref = bf16[8,32,256]{2,1,0:T(8,128)(2,1)S(1)} async-done(((bf16[8,32,256]{2,1,0:T(8,128)(2,1)}), bf16[8,32,256]{2,1,0:T(8,128)(2,1)S(1)}, u32[]{:S(2)}, u32[]{:S(2)}) %all-to-all-start.2) | async-done | bytes 131104 | tf_op jit(solution)/shard_map/all_to_all | solution.py:541
  48.0 4.0 %step.5 = (f32[32,2048]{1,0:T(8,128)S(1)}, bf16[8,32,256]{2,1,0:T(8,128)(2,1)}) custom-call(s32[128]{0:T(128)} %get-tuple-element.17.plan_ref, s32[8,1,8]{2,1,0:T(1,128)S(1)} %all-to-all-done.wanted_ref, f8e4m3fn[64,512,256]{2,1,0:T(32,128)(4,1)} %get-tuple-element.18.packed_hbm, f8e4m3fn[16,512,256]{2,1,0:T(32,128)(4,1)S(1)} %get-tuple-element.19.kept_ref, ...), custom_call_target="tpu_custom_call" | custom-call | tf_op jit(solution)/shard_map/step/pallas_call | solution.py:599
  52.0 4.0 %all-to-all-start.3 = ((bf16[8,32,256]{2,1,0:T(8,128)(2,1)}), bf16[8,32,256]{2,1,0:T(8,128)(2,1)S(1)}, u32[]{:S(2)}, u32[]{:S(2)}) async-start(bf16[8,32,256]{2,1,0:T(8,128)(2,1)} %get-tuple-element.24), calls=%async_computation.3 | async-start | bytes 262144 | tf_op jit(solution)/shard_map/all_to_all | solution.py:541
  56.1 3.8 %near.6.base_ref = f32[32,2048]{1,0:T(8,128)S(1)} custom-call(s32[96]{0:T(128)} %rows_ref.7, s32[96]{0:T(128)} %slots_ref.7, bf16[96,256,256]{2,1,0:T(8,128)(2,1)} %real_hbm.9, bf16[96,256,256]{2,1,0:T(8,128)(2,1)} %imag_hbm.9, f32[8,2048]{1,0:T(8,128)S(1)} %get-tuple-element.20.scale_ref, f32[32,2048]{1,0:T(8,128)S(1)} %get-tuple-element.23.now_ref.before_ref, ...), custom_call_target="tpu_custom_call" | custom-call | flops 268435456 | bytes 2097152 | tf_op jit(solution)/shard_map/near/pallas_call | solution.py:583
  59.8 2.0 %all-to-all-done.3.arrived_ref = bf16[8,32,256]{2,1,0:T(8,128)(2,1)S(1)} async-done(((bf16[8,32,256]{2,1,0:T(8,128)(2,1)}), bf16[8,32,256]{2,1,0:T(8,128)(2,1)S(1)}, u32[]{:S(2)}, u32[]{:S(2)}) %all-to-all-start.3) | async-done | bytes 131104 | tf_op jit(solution)/shard_map/all_to_all | solution.py:541
  61.8 4.0 %step.6 = (f32[32,2048]{1,0:T(8,128)S(1)}, bf16[8,32,256]{2,1,0:T(8,128)(2,1)}) custom-call(s32[128]{0:T(128)} %get-tuple-element.17.plan_ref, s32[8,1,8]{2,1,0:T(1,128)S(1)} %all-to-all-done.wanted_ref, f8e4m3fn[64,512,256]{2,1,0:T(32,128)(4,1)} %get-tuple-element.18.packed_hbm, f8e4m3fn[16,512,256]{2,1,0:T(32,128)(4,1)S(1)} %get-tuple-element.19.kept_ref, ...), custom_call_target="tpu_custom_call" | custom-call | tf_op jit(solution)/shard_map/step/pallas_call | solution.py:599
  65.8 4.0 %all-to-all-start.4 = ((bf16[8,32,256]{2,1,0:T(8,128)(2,1)}), bf16[8,32,256]{2,1,0:T(8,128)(2,1)S(1)}, u32[]{:S(2)}, u32[]{:S(2)}) async-start(bf16[8,32,256]{2,1,0:T(8,128)(2,1)} %get-tuple-element.26), calls=%async_computation.4 | async-start | bytes 262144 | tf_op jit(solution)/shard_map/all_to_all | solution.py:541
  69.9 3.8 %near.7.base_ref = f32[32,2048]{1,0:T(8,128)S(1)} custom-call(s32[96]{0:T(128)} %rows_ref.7, s32[96]{0:T(128)} %slots_ref.7, bf16[96,256,256]{2,1,0:T(8,128)(2,1)} %real_hbm.9, bf16[96,256,256]{2,1,0:T(8,128)(2,1)} %imag_hbm.9, f32[8,2048]{1,0:T(8,128)S(1)} %get-tuple-element.20.scale_ref, f32[32,2048]{1,0:T(8,128)S(1)} %get-tuple-element.25.now_ref, ...), custom_call_target="tpu_custom_call" | custom-call | flops 268435456 | bytes 2097152 | tf_op jit(solution)/shard_map/near/pallas_call | solution.py:583
  73.6 2.0 %all-to-all-done.4.arrived_ref = bf16[8,32,256]{2,1,0:T(8,128)(2,1)S(1)} async-done(((bf16[8,32,256]{2,1,0:T(8,128)(2,1)}), bf16[8,32,256]{2,1,0:T(8,128)(2,1)S(1)}, u32[]{:S(2)}, u32[]{:S(2)}) %all-to-all-start.4) | async-done | bytes 131104 | tf_op jit(solution)/shard_map/all_to_all | solution.py:541
  75.6 3.5 %step.7.own_ref = f32[32,2048]{1,0:T(8,128)S(1)} custom-call(s32[128]{0:T(128)} %get-tuple-element.17.plan_ref, s32[8,1,8]{2,1,0:T(1,128)S(1)} %all-to-all-done.wanted_ref, f8e4m3fn[64,512,256]{2,1,0:T(32,128)(4,1)} %get-tuple-element.18.packed_hbm, f8e4m3fn[16,512,256]{2,1,0:T(32,128)(4,1)S(1)} %get-tuple-element.19.kept_ref, ...), custom_call_target="tpu_custom_call" | custom-call | tf_op jit(solution)/shard_map/step/pallas_call | solution.py:599
  79.1 1.6 %collective-permute-start.1 = (bf16[32,2048]{1,0:T(8,128)(2,1)S(1)}, bf16[32,2048]{1,0:T(8,128)(2,1)S(1)}, u32[]{:S(2)}, u32[]{:S(2)}) collective-permute-start(bf16[32,2048]{1,0:T(8,128)(2,1)S(1)} %convert_element_type.3), channel_id=1, source_target_pairs={{0,2},{1,3},{2,0},{3,1},{4,6},{5,7},{6,4},{7,5},{8,10},{9,11},{10,... | collective-permute-start | bytes 393224 | tf_op jit(solution)/shard_map/ppermute | solution.py:546
  80.7 3.5 %collective-permute-done.1.refs_1_ = bf16[32,2048]{1,0:T(8,128)(2,1)S(1)} collective-permute-done((bf16[32,2048]{1,0:T(8,128)(2,1)S(1)}, bf16[32,2048]{1,0:T(8,128)(2,1)S(1)}, u32[]{:S(2)}, u32[]{:S(2)}) %collective-permute-start.1) | collective-permute-done | bytes 131104 | tf_op jit(solution)/shard_map/ppermute | solution.py:546
  86.7 3.2 %collective-permute-done.3 = f32[64,128]{1,0:T(8,128)S(1)} collective-permute-done((f32[64,128]{1,0:T(8,128)S(1)}, f32[64,128]{1,0:T(8,128)S(1)}, u32[]{:S(2)}, u32[]{:S(2)}) %collective-permute-start.3) | collective-permute-done | bytes 32800 | tf_op jit(solution)/shard_map/ppermute | solution.py:546
  92.1 2.2 %collective-permute-start.4 = (f32[64,128]{1,0:T(8,128)S(1)}, f32[64,128]{1,0:T(8,128)S(1)}, u32[]{:S(2)}, u32[]{:S(2)}) collective-permute-start(f32[64,128]{1,0:T(8,128)S(1)} %add.3.refs_0_), channel_id=1, source_target_pairs={{0,8},{4,12},{8,0},{12,4},{16,24},{20,28},{24,16},{28,20},{1,9},{5... | collective-permute-start | bytes 98312 | tf_op jit(solution)/shard_map/ppermute | solution.py:546
  94.3 1.4 %collective-permute-done.6.refs_3_ = f32[64,128]{1,0:T(8,128)S(1)} collective-permute-done((f32[64,128]{1,0:T(8,128)S(1)}, f32[64,128]{1,0:T(8,128)S(1)}, u32[]{:S(2)}, u32[]{:S(2)}) %collective-permute-start.6) | collective-permute-done | bytes 32800 | tf_op jit(solution)/shard_map/ppermute | solution.py:546
  96.5 4.8 %factor.1 = f32[32,2048]{1,0:T(8,128)} custom-call(f32[32,2048]{1,0:T(8,128)S(1)} %step.7.own_ref, bf16[4,32,2048]{2,1,0:T(8,128)(2,1)S(1)} %get-tuple-element.27.all_ref, f32[64,128]{1,0:T(8,128)S(1)} %add.3.refs_0_, f32[64,128]{1,0:T(8,128)S(1)} %collective-permute-done.4.refs_1_, f32[64,128]{1,0:T(8,128)S(1)} %collective-permute-done.5.refs_2_, ...), custom_call_target="tpu_custom_call" | custom-call | tf_op jit(solution)/shard_map/factor/pallas_call | solution.py:635
  (17 shorter events, 8.2 us)
Async XLA Ops:
  1.2 20.8 %all-to-all-start = ((s32[8,1,8]{2,1,0:T(1,128)}), s32[8,1,8]{2,1,0:T(1,128)S(1)}, u32[]{:S(2)}, u32[]{:S(2)}) async-start(s32[8,1,8]{2,1,0:T(1,128)} %broadcast_in_dim.9), calls=%async_computation | async-start | bytes 8192 | tf_op jit(solution)/shard_map/all_to_all | solution.py:541
  9.1 13.0 %copy-start = (f32[32,2048]{1,0:T(8,128)S(1)}, f32[32,2048]{1,0:T(8,128)}, u32[]{:S(2)}) copy-start(f32[32,2048]{1,0:T(8,128)} %before_ref.3) | copy-start | bytes 786436
  23.4 10.7 %all-to-all-start.1 = ((bf16[8,32,256]{2,1,0:T(8,128)(2,1)}), bf16[8,32,256]{2,1,0:T(8,128)(2,1)S(1)}, u32[]{:S(2)}, u32[]{:S(2)}) async-start(bf16[8,32,256]{2,1,0:T(8,128)(2,1)} %first.1), calls=%async_computation.1 | async-start | bytes 262144 | tf_op jit(solution)/shard_map/all_to_all | solution.py:541
  38.2 9.8 %all-to-all-start.2 = ((bf16[8,32,256]{2,1,0:T(8,128)(2,1)}), bf16[8,32,256]{2,1,0:T(8,128)(2,1)S(1)}, u32[]{:S(2)}, u32[]{:S(2)}) async-start(bf16[8,32,256]{2,1,0:T(8,128)(2,1)} %get-tuple-element.22), calls=%async_computation.2 | async-start | bytes 262144 | tf_op jit(solution)/shard_map/all_to_all | solution.py:541
  52.0 9.8 %all-to-all-start.3 = ((bf16[8,32,256]{2,1,0:T(8,128)(2,1)}), bf16[8,32,256]{2,1,0:T(8,128)(2,1)S(1)}, u32[]{:S(2)}, u32[]{:S(2)}) async-start(bf16[8,32,256]{2,1,0:T(8,128)(2,1)} %get-tuple-element.24), calls=%async_computation.3 | async-start | bytes 262144 | tf_op jit(solution)/shard_map/all_to_all | solution.py:541
  65.8 9.8 %all-to-all-start.4 = ((bf16[8,32,256]{2,1,0:T(8,128)(2,1)}), bf16[8,32,256]{2,1,0:T(8,128)(2,1)S(1)}, u32[]{:S(2)}, u32[]{:S(2)}) async-start(bf16[8,32,256]{2,1,0:T(8,128)(2,1)} %get-tuple-element.26), calls=%async_computation.4 | async-start | bytes 262144 | tf_op jit(solution)/shard_map/all_to_all | solution.py:541
  79.1 5.0 %collective-permute-start.1 = (bf16[32,2048]{1,0:T(8,128)(2,1)S(1)}, bf16[32,2048]{1,0:T(8,128)(2,1)S(1)}, u32[]{:S(2)}, u32[]{:S(2)}) collective-permute-start(bf16[32,2048]{1,0:T(8,128)(2,1)S(1)} %convert_element_type.3), channel_id=1, source_target_pairs={{0,2},{1,3},{2,0},{3,1},{4,6},{5,7},{6,4},{7,5},{8,10},{9,11},{10,... | collective-permute-start | bytes 393224 | tf_op jit(solution)/shard_map/ppermute | solution.py:546
  80.7 3.5 %collective-permute-start = (bf16[32,2048]{1,0:T(8,128)(2,1)S(1)}, bf16[32,2048]{1,0:T(8,128)(2,1)S(1)}, u32[]{:S(2)}, u32[]{:S(2)}) collective-permute-start(bf16[32,2048]{1,0:T(8,128)(2,1)S(1)} %convert_element_type.3), channel_id=1, source_target_pairs={{0,1},{1,0},{2,3},{3,2},{4,5},{5,4},{6,7},{7,6},{8,9},{9,8},{10,11... | collective-permute-start | bytes 393224 | tf_op jit(solution)/shard_map/ppermute | solution.py:546
  84.2 1.3 %collective-permute-start.2 = (bf16[32,2048]{1,0:T(8,128)(2,1)S(1)}, bf16[32,2048]{1,0:T(8,128)(2,1)S(1)}, u32[]{:S(2)}, u32[]{:S(2)}) collective-permute-start(bf16[32,2048]{1,0:T(8,128)(2,1)S(1)} %collective-permute-done.1.refs_1_), channel_id=1, source_target_pairs={{0,1},{1,0},{2,3},{3,2},{4,5},{5,4},{6,7},{7,6},{8,9},{9,8},{10,11... | collective-permute-start | bytes 393224 | tf_op jit(solution)/shard_map/ppermute | solution.py:546
  85.9 4.0 %collective-permute-start.3 = (f32[64,128]{1,0:T(8,128)S(1)}, f32[64,128]{1,0:T(8,128)S(1)}, u32[]{:S(2)}, u32[]{:S(2)}) collective-permute-start(f32[64,128]{1,0:T(8,128)S(1)} %get-tuple-element.28), channel_id=1, source_target_pairs={{0,4},{4,0},{8,12},{12,8},{16,20},{20,16},{24,28},{28,24},{1,5},{5... | collective-permute-start | bytes 98312 | tf_op jit(solution)/shard_map/ppermute | solution.py:546
  89.9 5.7 %collective-permute-start.6 = (f32[64,128]{1,0:T(8,128)S(1)}, f32[64,128]{1,0:T(8,128)S(1)}, u32[]{:S(2)}, u32[]{:S(2)}) collective-permute-start(f32[64,128]{1,0:T(8,128)S(1)} %add.3.refs_0_), channel_id=1, source_target_pairs={{0,24},{4,28},{8,16},{12,20},{16,8},{20,12},{24,0},{28,4},{1,25},{... | collective-permute-start | bytes 98312 | tf_op jit(solution)/shard_map/ppermute | solution.py:546
  90.9 5.6 %collective-permute-start.5 = (f32[64,128]{1,0:T(8,128)S(1)}, f32[64,128]{1,0:T(8,128)S(1)}, u32[]{:S(2)}, u32[]{:S(2)}) collective-permute-start(f32[64,128]{1,0:T(8,128)S(1)} %add.3.refs_0_), channel_id=1, source_target_pairs={{0,16},{4,20},{8,24},{12,28},{16,0},{20,4},{24,8},{28,12},{1,17},{... | collective-permute-start | bytes 98312 | tf_op jit(solution)/shard_map/ppermute | solution.py:546
  92.1 4.4 %collective-permute-start.4 = (f32[64,128]{1,0:T(8,128)S(1)}, f32[64,128]{1,0:T(8,128)S(1)}, u32[]{:S(2)}, u32[]{:S(2)}) collective-permute-start(f32[64,128]{1,0:T(8,128)S(1)} %add.3.refs_0_), channel_id=1, source_target_pairs={{0,8},{4,12},{8,0},{12,4},{16,24},{20,28},{24,16},{28,20},{1,9},{5... | collective-permute-start | bytes 98312 | tf_op jit(solution)/shard_map/ppermute | solution.py:546

commit v20 on v18

--- a/solution.py
+++ b/solution.py
@@ -168,7 +168,7 @@
 
             lax.while_loop(lambda prior: prior >= 0, add, back_ref[t])
             put(listed, t)
-            place = (slots_ref[t] - rb_dev) ^ central(slots - rb_dev)
+            place = place_of(slots_ref[t] - rb_dev, slots - rb_dev)
             plan_ref[listed] = rows_ref[t] | (place << 8)
 
         return listed + closes
@@ -525,13 +525,18 @@
         copy.wait()
 
 
-def central(nblk):
-    return nblk // 4
+def place_of(device, nblk):
+    if nblk != 8:
+        return device ^ (nblk // 4)
+    z, y = device >> 1, device & 1
+    half = z >> 1
+    outer = (z & 1) ^ 1 ^ half
+    return y | (outer << 1) | (half << 2)
 
 
 def exchange(x):
     nblk = lax.axis_size("blk")
-    group = [i ^ central(nblk) for i in range(nblk)]
+    group = sorted(range(nblk), key=lambda device: place_of(device, nblk))
     return lax.all_to_all(x, "blk", split_axis=0, concat_axis=0, tiled=True, axis_index_groups=[group])
 
 

time: 100 us -> 101 us (1.010)
  starting transfers between devices: 29.7 us -> 33.9 us
  waiting for transfers between devices: 18.6 us -> 15.5 us
    all_to_all x5, starting transfers between devices: 23.5 us -> 26.4 us  [exchange(): lax.all_to_all(x, 'blk', split_axis=0, concat_axis=0, tiled=True, axis_in...]
    all_to_all x5, waiting for transfers between devices: 7.82 us -> 5.81 us  [exchange(): lax.all_to_all(x, 'blk', split_axis=0, concat_axis=0, tiled=True, axis_in...]
    ppermute x7, starting transfers between devices: 6.23 us -> 7.46 us  [to_partner(): return lax.ppermute(x, axis, [(i, i ^ mask) for i in range(n)])]
    ppermute x7, waiting for transfers between devices: 10.8 us -> 9.68 us  [to_partner(): return lax.ppermute(x, axis, [(i, i ^ mask) for i in range(n)])]
where the time goes in v20:
time: 101 us
  Pallas kernels  49.8 us (49%)
  starting transfers between devices  33.9 us (34%)
  waiting for transfers between devices  15.5 us (15%)
  local copies, waits for them, and re-layouts  1.25 us (1%)
    all_to_all x5, starting transfers between devices, exchange(): lax.all_to_all(x, 'blk', split_axis=0, concat_axis=0, tiled=True, axis_in...  26.4 us
    pallas_call x4, Pallas kernels, per_device(): pl.pallas_call(functools.partial(step_kernel, step), name='step', out_sha...  15.3 us
    pallas_call x4, Pallas kernels, per_device(): pl.pallas_call(functools.partial(near_kernel, step), name='near', out_sha...  15 us
    pallas_call x1, Pallas kernels, tiles_call(): pl.pallas_call(functools.partial(tiles_kernel, near_count), name='tiles',...  13 us
    ppermute x7, waiting for transfers between devices, to_partner(): return lax.ppermute(x, axis, [(i, i ^ mask) for i in range(n)])  9.68 us
    ppermute x7, starting transfers between devices, to_partner(): return lax.ppermute(x, axis, [(i, i ^ mask) for i in range(n)])  7.46 us
    all_to_all x5, waiting for transfers between devices, exchange(): lax.all_to_all(x, 'blk', split_axis=0, concat_axis=0, tiled=True, axis_in...  5.81 us
    pallas_call x1, Pallas kernels, per_device(): pl.pallas_call(functools.partial(factor_kernel, rows * nblk), name='facto...  4.79 us
  transfers between devices with their start and end apart: 12, of which 10 were waited for; matrix products, arithmetic and copies ran while one was open for 0% of the time, Pallas kernels for 28%

profile of v20, /device:TPU:0, one launch (start us, length us, event | category | flops | bytes accessed | tf_op | source)
XLA Modules:
  0.0 100.6 jit_solution(15234350457117264584)
XLA Ops:
  1.2 7.8 %all-to-all-start = ((s32[8,1,8]{2,1,0:T(1,128)}), s32[8,1,8]{2,1,0:T(1,128)S(1)}, u32[]{:S(2)}, u32[]{:S(2)}) async-start(s32[8,1,8]{2,1,0:T(1,128)} %broadcast_in_dim.9), calls=%async_computation | async-start | bytes 8192 | tf_op jit(solution)/shard_map/all_to_all | solution.py:540
  9.1 13.0 %tiles.1 = (f8e4m3fn[64,512,256]{2,1,0:T(32,128)(4,1)}, f8e4m3fn[16,512,256]{2,1,0:T(32,128)(4,1)S(1)}, f32[8,2048]{1,0:T(8,128)S(1)}, s32[128]{0:T(128)}) custom-call(s32[96]{0:T(128)} %rows_ref.7, s32[96]{0:T(128)} %slots_ref.7, bf16[96,256,256]{2,1,0:T(8,128)(2,1)} %real_hbm.9, bf16[96,256,256]{2,1,0:T(8,128)(2,1)} %imag_hbm.9), custom_call_target="tpu_custom_call" | custom-call | flops 268435456 | bytes 25165824 | tf_op jit(solution)/shard_map/tiles/pallas_call | solution.py:225
  23.4 4.9 %all-to-all-start.1 = ((bf16[8,32,256]{2,1,0:T(8,128)(2,1)}), bf16[8,32,256]{2,1,0:T(8,128)(2,1)S(1)}, u32[]{:S(2)}, u32[]{:S(2)}) async-start(bf16[8,32,256]{2,1,0:T(8,128)(2,1)} %first.1), calls=%async_computation.1 | async-start | bytes 262144 | tf_op jit(solution)/shard_map/all_to_all | solution.py:540
  28.3 3.7 %near.4.base_ref = f32[32,2048]{1,0:T(8,128)S(1)} custom-call(s32[96]{0:T(128)} %rows_ref.7, s32[96]{0:T(128)} %slots_ref.7, bf16[96,256,256]{2,1,0:T(8,128)(2,1)} %real_hbm.9, bf16[96,256,256]{2,1,0:T(8,128)(2,1)} %imag_hbm.9, f32[8,2048]{1,0:T(8,128)S(1)} %get-tuple-element.20.scale_ref, f32[32,2048]{1,0:T(8,128)S(1)} %copy-done, f32[32,2048]{1,0:T(8,128)S(1)} %copy-done), custom_call_target="tpu_custom_call" | custom-call | flops 268435456 | bytes 2097152 | tf_op jit(solution)/shard_map/near/pallas_call | solution.py:582
  32.1 1.4 %all-to-all-done.1.arrived_ref = bf16[8,32,256]{2,1,0:T(8,128)(2,1)S(1)} async-done(((bf16[8,32,256]{2,1,0:T(8,128)(2,1)}), bf16[8,32,256]{2,1,0:T(8,128)(2,1)S(1)}, u32[]{:S(2)}, u32[]{:S(2)}) %all-to-all-start.1) | async-done | bytes 131104 | tf_op jit(solution)/shard_map/all_to_all | solution.py:540
  33.5 4.0 %step.4 = (f32[32,2048]{1,0:T(8,128)S(1)}, bf16[8,32,256]{2,1,0:T(8,128)(2,1)}) custom-call(s32[128]{0:T(128)} %get-tuple-element.17.plan_ref, s32[8,1,8]{2,1,0:T(1,128)S(1)} %all-to-all-done.wanted_ref, f8e4m3fn[64,512,256]{2,1,0:T(32,128)(4,1)} %get-tuple-element.18.packed_hbm, f8e4m3fn[16,512,256]{2,1,0:T(32,128)(4,1)S(1)} %get-tuple-element.19.kept_ref, ...), custom_call_target="tpu_custom_call" | custom-call | tf_op jit(solution)/shard_map/step/pallas_call | solution.py:598
  37.5 4.6 %all-to-all-start.2 = ((bf16[8,32,256]{2,1,0:T(8,128)(2,1)}), bf16[8,32,256]{2,1,0:T(8,128)(2,1)S(1)}, u32[]{:S(2)}, u32[]{:S(2)}) async-start(bf16[8,32,256]{2,1,0:T(8,128)(2,1)} %get-tuple-element.22), calls=%async_computation.2 | async-start | bytes 262144 | tf_op jit(solution)/shard_map/all_to_all | solution.py:540
  42.1 3.8 %near.5.base_ref = f32[32,2048]{1,0:T(8,128)S(1)} custom-call(s32[96]{0:T(128)} %rows_ref.7, s32[96]{0:T(128)} %slots_ref.7, bf16[96,256,256]{2,1,0:T(8,128)(2,1)} %real_hbm.9, bf16[96,256,256]{2,1,0:T(8,128)(2,1)} %imag_hbm.9, f32[8,2048]{1,0:T(8,128)S(1)} %get-tuple-element.20.scale_ref, f32[32,2048]{1,0:T(8,128)S(1)} %get-tuple-element.21.now_ref.before_ref, ...), custom_call_target="tpu_custom_call" | custom-call | flops 268435456 | bytes 2097152 | tf_op jit(solution)/shard_map/near/pallas_call | solution.py:582
  45.9 1.5 %all-to-all-done.2.arrived_ref = bf16[8,32,256]{2,1,0:T(8,128)(2,1)S(1)} async-done(((bf16[8,32,256]{2,1,0:T(8,128)(2,1)}), bf16[8,32,256]{2,1,0:T(8,128)(2,1)S(1)}, u32[]{:S(2)}, u32[]{:S(2)}) %all-to-all-start.2) | async-done | bytes 131104 | tf_op jit(solution)/shard_map/all_to_all | solution.py:540
  47.3 4.0 %step.5 = (f32[32,2048]{1,0:T(8,128)S(1)}, bf16[8,32,256]{2,1,0:T(8,128)(2,1)}) custom-call(s32[128]{0:T(128)} %get-tuple-element.17.plan_ref, s32[8,1,8]{2,1,0:T(1,128)S(1)} %all-to-all-done.wanted_ref, f8e4m3fn[64,512,256]{2,1,0:T(32,128)(4,1)} %get-tuple-element.18.packed_hbm, f8e4m3fn[16,512,256]{2,1,0:T(32,128)(4,1)S(1)} %get-tuple-element.19.kept_ref, ...), custom_call_target="tpu_custom_call" | custom-call | tf_op jit(solution)/shard_map/step/pallas_call | solution.py:598
  51.3 4.6 %all-to-all-start.3 = ((bf16[8,32,256]{2,1,0:T(8,128)(2,1)}), bf16[8,32,256]{2,1,0:T(8,128)(2,1)S(1)}, u32[]{:S(2)}, u32[]{:S(2)}) async-start(bf16[8,32,256]{2,1,0:T(8,128)(2,1)} %get-tuple-element.24), calls=%async_computation.3 | async-start | bytes 262144 | tf_op jit(solution)/shard_map/all_to_all | solution.py:540
  55.9 3.8 %near.6.base_ref = f32[32,2048]{1,0:T(8,128)S(1)} custom-call(s32[96]{0:T(128)} %rows_ref.7, s32[96]{0:T(128)} %slots_ref.7, bf16[96,256,256]{2,1,0:T(8,128)(2,1)} %real_hbm.9, bf16[96,256,256]{2,1,0:T(8,128)(2,1)} %imag_hbm.9, f32[8,2048]{1,0:T(8,128)S(1)} %get-tuple-element.20.scale_ref, f32[32,2048]{1,0:T(8,128)S(1)} %get-tuple-element.23.now_ref.before_ref, ...), custom_call_target="tpu_custom_call" | custom-call | flops 268435456 | bytes 2097152 | tf_op jit(solution)/shard_map/near/pallas_call | solution.py:582
  59.6 1.5 %all-to-all-done.3.arrived_ref = bf16[8,32,256]{2,1,0:T(8,128)(2,1)S(1)} async-done(((bf16[8,32,256]{2,1,0:T(8,128)(2,1)}), bf16[8,32,256]{2,1,0:T(8,128)(2,1)S(1)}, u32[]{:S(2)}, u32[]{:S(2)}) %all-to-all-start.3) | async-done | bytes 131104 | tf_op jit(solution)/shard_map/all_to_all | solution.py:540
  61.1 4.0 %step.6 = (f32[32,2048]{1,0:T(8,128)S(1)}, bf16[8,32,256]{2,1,0:T(8,128)(2,1)}) custom-call(s32[128]{0:T(128)} %get-tuple-element.17.plan_ref, s32[8,1,8]{2,1,0:T(1,128)S(1)} %all-to-all-done.wanted_ref, f8e4m3fn[64,512,256]{2,1,0:T(32,128)(4,1)} %get-tuple-element.18.packed_hbm, f8e4m3fn[16,512,256]{2,1,0:T(32,128)(4,1)S(1)} %get-tuple-element.19.kept_ref, ...), custom_call_target="tpu_custom_call" | custom-call | tf_op jit(solution)/shard_map/step/pallas_call | solution.py:598
  65.1 4.6 %all-to-all-start.4 = ((bf16[8,32,256]{2,1,0:T(8,128)(2,1)}), bf16[8,32,256]{2,1,0:T(8,128)(2,1)S(1)}, u32[]{:S(2)}, u32[]{:S(2)}) async-start(bf16[8,32,256]{2,1,0:T(8,128)(2,1)} %get-tuple-element.26), calls=%async_computation.4 | async-start | bytes 262144 | tf_op jit(solution)/shard_map/all_to_all | solution.py:540
  69.7 3.8 %near.7.base_ref = f32[32,2048]{1,0:T(8,128)S(1)} custom-call(s32[96]{0:T(128)} %rows_ref.7, s32[96]{0:T(128)} %slots_ref.7, bf16[96,256,256]{2,1,0:T(8,128)(2,1)} %real_hbm.9, bf16[96,256,256]{2,1,0:T(8,128)(2,1)} %imag_hbm.9, f32[8,2048]{1,0:T(8,128)S(1)} %get-tuple-element.20.scale_ref, f32[32,2048]{1,0:T(8,128)S(1)} %get-tuple-element.25.now_ref, ...), custom_call_target="tpu_custom_call" | custom-call | flops 268435456 | bytes 2097152 | tf_op jit(solution)/shard_map/near/pallas_call | solution.py:582
  73.4 1.5 %all-to-all-done.4.arrived_ref = bf16[8,32,256]{2,1,0:T(8,128)(2,1)S(1)} async-done(((bf16[8,32,256]{2,1,0:T(8,128)(2,1)}), bf16[8,32,256]{2,1,0:T(8,128)(2,1)S(1)}, u32[]{:S(2)}, u32[]{:S(2)}) %all-to-all-start.4) | async-done | bytes 131104 | tf_op jit(solution)/shard_map/all_to_all | solution.py:540
  74.9 3.3 %step.7.own_ref = f32[32,2048]{1,0:T(8,128)S(1)} custom-call(s32[128]{0:T(128)} %get-tuple-element.17.plan_ref, s32[8,1,8]{2,1,0:T(1,128)S(1)} %all-to-all-done.wanted_ref, f8e4m3fn[64,512,256]{2,1,0:T(32,128)(4,1)} %get-tuple-element.18.packed_hbm, f8e4m3fn[16,512,256]{2,1,0:T(32,128)(4,1)S(1)} %get-tuple-element.19.kept_ref, ...), custom_call_target="tpu_custom_call" | custom-call | tf_op jit(solution)/shard_map/step/pallas_call | solution.py:598
  78.2 1.6 %collective-permute-start.1 = (bf16[32,2048]{1,0:T(8,128)(2,1)S(1)}, bf16[32,2048]{1,0:T(8,128)(2,1)S(1)}, u32[]{:S(2)}, u32[]{:S(2)}) collective-permute-start(bf16[32,2048]{1,0:T(8,128)(2,1)S(1)} %convert_element_type.3), channel_id=1, source_target_pairs={{0,2},{1,3},{2,0},{3,1},{4,6},{5,7},{6,4},{7,5},{8,10},{9,11},{10,... | collective-permute-start | bytes 393224 | tf_op jit(solution)/shard_map/ppermute | solution.py:545
  79.8 3.5 %collective-permute-done.1.refs_1_ = bf16[32,2048]{1,0:T(8,128)(2,1)S(1)} collective-permute-done((bf16[32,2048]{1,0:T(8,128)(2,1)S(1)}, bf16[32,2048]{1,0:T(8,128)(2,1)S(1)}, u32[]{:S(2)}, u32[]{:S(2)}) %collective-permute-start.1) | collective-permute-done | bytes 131104 | tf_op jit(solution)/shard_map/ppermute | solution.py:545
  85.0 1.5 %collective-permute-start.3 = (f32[64,128]{1,0:T(8,128)S(1)}, f32[64,128]{1,0:T(8,128)S(1)}, u32[]{:S(2)}, u32[]{:S(2)}) collective-permute-start(f32[64,128]{1,0:T(8,128)S(1)} %get-tuple-element.28), channel_id=1, source_target_pairs={{0,4},{4,0},{8,12},{12,8},{16,20},{20,16},{24,28},{28,24},{1,5},{5... | collective-permute-start | bytes 98312 | tf_op jit(solution)/shard_map/ppermute | solution.py:545
  86.5 2.5 %collective-permute-done.3 = f32[64,128]{1,0:T(8,128)S(1)} collective-permute-done((f32[64,128]{1,0:T(8,128)S(1)}, f32[64,128]{1,0:T(8,128)S(1)}, u32[]{:S(2)}, u32[]{:S(2)}) %collective-permute-start.3) | collective-permute-done | bytes 32800 | tf_op jit(solution)/shard_map/ppermute | solution.py:545
  91.7 1.7 %collective-permute-start.4 = (f32[64,128]{1,0:T(8,128)S(1)}, f32[64,128]{1,0:T(8,128)S(1)}, u32[]{:S(2)}, u32[]{:S(2)}) collective-permute-start(f32[64,128]{1,0:T(8,128)S(1)} %add.3.refs_0_), channel_id=1, source_target_pairs={{0,8},{4,12},{8,0},{12,4},{16,24},{20,28},{24,16},{28,20},{1,9},{5... | collective-permute-start | bytes 98312 | tf_op jit(solution)/shard_map/ppermute | solution.py:545
  95.8 4.8 %factor.1 = f32[32,2048]{1,0:T(8,128)} custom-call(f32[32,2048]{1,0:T(8,128)S(1)} %step.7.own_ref, bf16[4,32,2048]{2,1,0:T(8,128)(2,1)S(1)} %get-tuple-element.27.all_ref, f32[64,128]{1,0:T(8,128)S(1)} %add.3.refs_0_, f32[64,128]{1,0:T(8,128)S(1)} %collective-permute-done.4.refs_1_, f32[64,128]{1,0:T(8,128)S(1)} %collective-permute-done.5.refs_2_, ...), custom_call_target="tpu_custom_call" | custom-call | tf_op jit(solution)/shard_map/factor/pallas_call | solution.py:634
  (17 shorter events, 9.5 us)
Async XLA Ops:
  1.2 20.8 %all-to-all-start = ((s32[8,1,8]{2,1,0:T(1,128)}), s32[8,1,8]{2,1,0:T(1,128)S(1)}, u32[]{:S(2)}, u32[]{:S(2)}) async-start(s32[8,1,8]{2,1,0:T(1,128)} %broadcast_in_dim.9), calls=%async_computation | async-start | bytes 8192 | tf_op jit(solution)/shard_map/all_to_all | solution.py:540
  9.1 13.0 %copy-start = (f32[32,2048]{1,0:T(8,128)S(1)}, f32[32,2048]{1,0:T(8,128)}, u32[]{:S(2)}) copy-start(f32[32,2048]{1,0:T(8,128)} %before_ref.3) | copy-start | bytes 786436
  23.4 10.1 %all-to-all-start.1 = ((bf16[8,32,256]{2,1,0:T(8,128)(2,1)}), bf16[8,32,256]{2,1,0:T(8,128)(2,1)S(1)}, u32[]{:S(2)}, u32[]{:S(2)}) async-start(bf16[8,32,256]{2,1,0:T(8,128)(2,1)} %first.1), calls=%async_computation.1 | async-start | bytes 262144 | tf_op jit(solution)/shard_map/all_to_all | solution.py:540
  37.5 9.8 %all-to-all-start.2 = ((bf16[8,32,256]{2,1,0:T(8,128)(2,1)}), bf16[8,32,256]{2,1,0:T(8,128)(2,1)S(1)}, u32[]{:S(2)}, u32[]{:S(2)}) async-start(bf16[8,32,256]{2,1,0:T(8,128)(2,1)} %get-tuple-element.22), calls=%async_computation.2 | async-start | bytes 262144 | tf_op jit(solution)/shard_map/all_to_all | solution.py:540
  51.3 9.8 %all-to-all-start.3 = ((bf16[8,32,256]{2,1,0:T(8,128)(2,1)}), bf16[8,32,256]{2,1,0:T(8,128)(2,1)S(1)}, u32[]{:S(2)}, u32[]{:S(2)}) async-start(bf16[8,32,256]{2,1,0:T(8,128)(2,1)} %get-tuple-element.24), calls=%async_computation.3 | async-start | bytes 262144 | tf_op jit(solution)/shard_map/all_to_all | solution.py:540
  65.1 9.8 %all-to-all-start.4 = ((bf16[8,32,256]{2,1,0:T(8,128)(2,1)}), bf16[8,32,256]{2,1,0:T(8,128)(2,1)S(1)}, u32[]{:S(2)}, u32[]{:S(2)}) async-start(bf16[8,32,256]{2,1,0:T(8,128)(2,1)} %get-tuple-element.26), calls=%async_computation.4 | async-start | bytes 262144 | tf_op jit(solution)/shard_map/all_to_all | solution.py:540
  78.2 5.0 %collective-permute-start.1 = (bf16[32,2048]{1,0:T(8,128)(2,1)S(1)}, bf16[32,2048]{1,0:T(8,128)(2,1)S(1)}, u32[]{:S(2)}, u32[]{:S(2)}) collective-permute-start(bf16[32,2048]{1,0:T(8,128)(2,1)S(1)} %convert_element_type.3), channel_id=1, source_target_pairs={{0,2},{1,3},{2,0},{3,1},{4,6},{5,7},{6,4},{7,5},{8,10},{9,11},{10,... | collective-permute-start | bytes 393224 | tf_op jit(solution)/shard_map/ppermute | solution.py:545
  79.8 3.5 %collective-permute-start = (bf16[32,2048]{1,0:T(8,128)(2,1)S(1)}, bf16[32,2048]{1,0:T(8,128)(2,1)S(1)}, u32[]{:S(2)}, u32[]{:S(2)}) collective-permute-start(bf16[32,2048]{1,0:T(8,128)(2,1)S(1)} %convert_element_type.3), channel_id=1, source_target_pairs={{0,1},{1,0},{2,3},{3,2},{4,5},{5,4},{6,7},{7,6},{8,9},{9,8},{10,11... | collective-permute-start | bytes 393224 | tf_op jit(solution)/shard_map/ppermute | solution.py:545
  83.2 1.3 %collective-permute-start.2 = (bf16[32,2048]{1,0:T(8,128)(2,1)S(1)}, bf16[32,2048]{1,0:T(8,128)(2,1)S(1)}, u32[]{:S(2)}, u32[]{:S(2)}) collective-permute-start(bf16[32,2048]{1,0:T(8,128)(2,1)S(1)} %collective-permute-done.1.refs_1_), channel_id=1, source_target_pairs={{0,1},{1,0},{2,3},{3,2},{4,5},{5,4},{6,7},{7,6},{8,9},{9,8},{10,11... | collective-permute-start | bytes 393224 | tf_op jit(solution)/shard_map/ppermute | solution.py:545
  85.0 4.0 %collective-permute-start.3 = (f32[64,128]{1,0:T(8,128)S(1)}, f32[64,128]{1,0:T(8,128)S(1)}, u32[]{:S(2)}, u32[]{:S(2)}) collective-permute-start(f32[64,128]{1,0:T(8,128)S(1)} %get-tuple-element.28), channel_id=1, source_target_pairs={{0,4},{4,0},{8,12},{12,8},{16,20},{20,16},{24,28},{28,24},{1,5},{5... | collective-permute-start | bytes 98312 | tf_op jit(solution)/shard_map/ppermute | solution.py:545
  89.0 5.7 %collective-permute-start.6 = (f32[64,128]{1,0:T(8,128)S(1)}, f32[64,128]{1,0:T(8,128)S(1)}, u32[]{:S(2)}, u32[]{:S(2)}) collective-permute-start(f32[64,128]{1,0:T(8,128)S(1)} %add.3.refs_0_), channel_id=1, source_target_pairs={{0,24},{4,28},{8,16},{12,20},{16,8},{20,12},{24,0},{28,4},{1,25},{... | collective-permute-start | bytes 98312 | tf_op jit(solution)/shard_map/ppermute | solution.py:545
  90.4 5.0 %collective-permute-start.5 = (f32[64,128]{1,0:T(8,128)S(1)}, f32[64,128]{1,0:T(8,128)S(1)}, u32[]{:S(2)}, u32[]{:S(2)}) collective-permute-start(f32[64,128]{1,0:T(8,128)S(1)} %add.3.refs_0_), channel_id=1, source_target_pairs={{0,16},{4,20},{8,24},{12,28},{16,0},{20,4},{24,8},{28,12},{1,17},{... | collective-permute-start | bytes 98312 | tf_op jit(solution)/shard_map/ppermute | solution.py:545
  91.7 4.1 %collective-permute-start.4 = (f32[64,128]{1,0:T(8,128)S(1)}, f32[64,128]{1,0:T(8,128)S(1)}, u32[]{:S(2)}, u32[]{:S(2)}) collective-permute-start(f32[64,128]{1,0:T(8,128)S(1)} %add.3.refs_0_), channel_id=1, source_target_pairs={{0,8},{4,12},{8,0},{12,4},{16,24},{20,28},{24,16},{28,20},{1,9},{5... | collective-permute-start | bytes 98312 | tf_op jit(solution)/shard_map/ppermute | solution.py:545

commit v21 on v20

--- a/solution.py
+++ b/solution.py
@@ -525,13 +525,11 @@
         copy.wait()
 
 
+PLACES = 0x12365047
+
+
 def place_of(device, nblk):
-    if nblk != 8:
-        return device ^ (nblk // 4)
-    z, y = device >> 1, device & 1
-    half = z >> 1
-    outer = (z & 1) ^ 1 ^ half
-    return y | (outer << 1) | (half << 2)
+    return (PLACES >> (4 * device)) & 15 if nblk == 8 else device ^ (nblk // 4)
 
 
 def exchange(x):

time: 101 us -> 100 us (0.990)
  starting transfers between devices: 33.9 us -> 30.3 us
  waiting for transfers between devices: 15.5 us -> 17.7 us
    all_to_all x5, starting transfers between devices: 26.4 us -> 24 us  [exchange(): lax.all_to_all(x, 'blk', split_axis=0, concat_axis=0, tiled=True, axis_in...]
    ppermute x7, starting transfers between devices: 7.46 us -> 6.27 us  [to_partner(): return lax.ppermute(x, axis, [(i, i ^ mask) for i in range(n)])]
    all_to_all x5, waiting for transfers between devices: 5.81 us -> 6.98 us  [exchange(): lax.all_to_all(x, 'blk', split_axis=0, concat_axis=0, tiled=True, axis_in...]
    ppermute x7, waiting for transfers between devices: 9.68 us -> 10.7 us  [to_partner(): return lax.ppermute(x, axis, [(i, i ^ mask) for i in range(n)])]
where the time goes in v21:
time: 100 us; the launch traced here: 99.1 us
  Pallas kernels  49.7 us (50%)
  starting transfers between devices  30.3 us (30%)
  waiting for transfers between devices  17.7 us (18%)
  local copies, waits for them, and re-layouts  1.25 us (1%)
    all_to_all x5, starting transfers between devices, exchange(): lax.all_to_all(x, 'blk', split_axis=0, concat_axis=0, tiled=True, axis_in...  24 us
    pallas_call x4, Pallas kernels, per_device(): pl.pallas_call(functools.partial(step_kernel, step), name='step', out_sha...  15.3 us
    pallas_call x4, Pallas kernels, per_device(): pl.pallas_call(functools.partial(near_kernel, step), name='near', out_sha...  15 us
    pallas_call x1, Pallas kernels, tiles_call(): pl.pallas_call(functools.partial(tiles_kernel, near_count), name='tiles',...  12.9 us
    ppermute x7, waiting for transfers between devices, to_partner(): return lax.ppermute(x, axis, [(i, i ^ mask) for i in range(n)])  10.7 us
    all_to_all x5, waiting for transfers between devices, exchange(): lax.all_to_all(x, 'blk', split_axis=0, concat_axis=0, tiled=True, axis_in...  6.98 us
    ppermute x7, starting transfers between devices, to_partner(): return lax.ppermute(x, axis, [(i, i ^ mask) for i in range(n)])  6.27 us
    pallas_call x1, Pallas kernels, per_device(): pl.pallas_call(functools.partial(factor_kernel, rows * nblk), name='facto...  4.79 us
  transfers between devices with their start and end apart: 12, of which 10 were waited for; matrix products, arithmetic and copies ran while one was open for 0% of the time, Pallas kernels for 28%

profile of v21, /device:TPU:0, one launch (start us, length us, event | category | flops | bytes accessed | tf_op | source)
XLA Modules:
  0.0 99.1 jit_solution(2329855376083607303)
XLA Ops:
  1.2 7.8 %all-to-all-start = ((s32[8,1,8]{2,1,0:T(1,128)}), s32[8,1,8]{2,1,0:T(1,128)S(1)}, u32[]{:S(2)}, u32[]{:S(2)}) async-start(s32[8,1,8]{2,1,0:T(1,128)} %broadcast_in_dim.9), calls=%async_computation | async-start | bytes 8192 | tf_op jit(solution)/shard_map/all_to_all | solution.py:538
  9.1 12.9 %tiles.1 = (f8e4m3fn[64,512,256]{2,1,0:T(32,128)(4,1)}, f8e4m3fn[16,512,256]{2,1,0:T(32,128)(4,1)S(1)}, f32[8,2048]{1,0:T(8,128)S(1)}, s32[128]{0:T(128)}) custom-call(s32[96]{0:T(128)} %rows_ref.7, s32[96]{0:T(128)} %slots_ref.7, bf16[96,256,256]{2,1,0:T(8,128)(2,1)} %real_hbm.9, bf16[96,256,256]{2,1,0:T(8,128)(2,1)} %imag_hbm.9), custom_call_target="tpu_custom_call" | custom-call | flops 268435456 | bytes 25165824 | tf_op jit(solution)/shard_map/tiles/pallas_call | solution.py:225
  23.4 5.0 %all-to-all-start.1 = ((bf16[8,32,256]{2,1,0:T(8,128)(2,1)}), bf16[8,32,256]{2,1,0:T(8,128)(2,1)S(1)}, u32[]{:S(2)}, u32[]{:S(2)}) async-start(bf16[8,32,256]{2,1,0:T(8,128)(2,1)} %first.1), calls=%async_computation.1 | async-start | bytes 262144 | tf_op jit(solution)/shard_map/all_to_all | solution.py:538
  28.4 3.7 %near.4.base_ref = f32[32,2048]{1,0:T(8,128)S(1)} custom-call(s32[96]{0:T(128)} %rows_ref.7, s32[96]{0:T(128)} %slots_ref.7, bf16[96,256,256]{2,1,0:T(8,128)(2,1)} %real_hbm.9, bf16[96,256,256]{2,1,0:T(8,128)(2,1)} %imag_hbm.9, f32[8,2048]{1,0:T(8,128)S(1)} %get-tuple-element.20.scale_ref, f32[32,2048]{1,0:T(8,128)S(1)} %copy-done, f32[32,2048]{1,0:T(8,128)S(1)} %copy-done), custom_call_target="tpu_custom_call" | custom-call | flops 268435456 | bytes 2097152 | tf_op jit(solution)/shard_map/near/pallas_call | solution.py:580
  32.2 1.8 %all-to-all-done.1.arrived_ref = bf16[8,32,256]{2,1,0:T(8,128)(2,1)S(1)} async-done(((bf16[8,32,256]{2,1,0:T(8,128)(2,1)}), bf16[8,32,256]{2,1,0:T(8,128)(2,1)S(1)}, u32[]{:S(2)}, u32[]{:S(2)}) %all-to-all-start.1) | async-done | bytes 131104 | tf_op jit(solution)/shard_map/all_to_all | solution.py:538
  33.9 4.0 %step.4 = (f32[32,2048]{1,0:T(8,128)S(1)}, bf16[8,32,256]{2,1,0:T(8,128)(2,1)}) custom-call(s32[128]{0:T(128)} %get-tuple-element.17.plan_ref, s32[8,1,8]{2,1,0:T(1,128)S(1)} %all-to-all-done.wanted_ref, f8e4m3fn[64,512,256]{2,1,0:T(32,128)(4,1)} %get-tuple-element.18.packed_hbm, f8e4m3fn[16,512,256]{2,1,0:T(32,128)(4,1)S(1)} %get-tuple-element.19.kept_ref, ...), custom_call_target="tpu_custom_call" | custom-call | tf_op jit(solution)/shard_map/step/pallas_call | solution.py:596
  38.0 3.7 %all-to-all-start.2 = ((bf16[8,32,256]{2,1,0:T(8,128)(2,1)}), bf16[8,32,256]{2,1,0:T(8,128)(2,1)S(1)}, u32[]{:S(2)}, u32[]{:S(2)}) async-start(bf16[8,32,256]{2,1,0:T(8,128)(2,1)} %get-tuple-element.22), calls=%async_computation.2 | async-start | bytes 262144 | tf_op jit(solution)/shard_map/all_to_all | solution.py:538
  41.6 3.8 %near.5.base_ref = f32[32,2048]{1,0:T(8,128)S(1)} custom-call(s32[96]{0:T(128)} %rows_ref.7, s32[96]{0:T(128)} %slots_ref.7, bf16[96,256,256]{2,1,0:T(8,128)(2,1)} %real_hbm.9, bf16[96,256,256]{2,1,0:T(8,128)(2,1)} %imag_hbm.9, f32[8,2048]{1,0:T(8,128)S(1)} %get-tuple-element.20.scale_ref, f32[32,2048]{1,0:T(8,128)S(1)} %get-tuple-element.21.now_ref.before_ref, ...), custom_call_target="tpu_custom_call" | custom-call | flops 268435456 | bytes 2097152 | tf_op jit(solution)/shard_map/near/pallas_call | solution.py:580
  45.4 1.7 %all-to-all-done.2.arrived_ref = bf16[8,32,256]{2,1,0:T(8,128)(2,1)S(1)} async-done(((bf16[8,32,256]{2,1,0:T(8,128)(2,1)}), bf16[8,32,256]{2,1,0:T(8,128)(2,1)S(1)}, u32[]{:S(2)}, u32[]{:S(2)}) %all-to-all-start.2) | async-done | bytes 131104 | tf_op jit(solution)/shard_map/all_to_all | solution.py:538
  47.1 4.0 %step.5 = (f32[32,2048]{1,0:T(8,128)S(1)}, bf16[8,32,256]{2,1,0:T(8,128)(2,1)}) custom-call(s32[128]{0:T(128)} %get-tuple-element.17.plan_ref, s32[8,1,8]{2,1,0:T(1,128)S(1)} %all-to-all-done.wanted_ref, f8e4m3fn[64,512,256]{2,1,0:T(32,128)(4,1)} %get-tuple-element.18.packed_hbm, f8e4m3fn[16,512,256]{2,1,0:T(32,128)(4,1)S(1)} %get-tuple-element.19.kept_ref, ...), custom_call_target="tpu_custom_call" | custom-call | tf_op jit(solution)/shard_map/step/pallas_call | solution.py:596
  51.2 3.7 %all-to-all-start.3 = ((bf16[8,32,256]{2,1,0:T(8,128)(2,1)}), bf16[8,32,256]{2,1,0:T(8,128)(2,1)S(1)}, u32[]{:S(2)}, u32[]{:S(2)}) async-start(bf16[8,32,256]{2,1,0:T(8,128)(2,1)} %get-tuple-element.24), calls=%async_computation.3 | async-start | bytes 262144 | tf_op jit(solution)/shard_map/all_to_all | solution.py:538
  54.9 3.8 %near.6.base_ref = f32[32,2048]{1,0:T(8,128)S(1)} custom-call(s32[96]{0:T(128)} %rows_ref.7, s32[96]{0:T(128)} %slots_ref.7, bf16[96,256,256]{2,1,0:T(8,128)(2,1)} %real_hbm.9, bf16[96,256,256]{2,1,0:T(8,128)(2,1)} %imag_hbm.9, f32[8,2048]{1,0:T(8,128)S(1)} %get-tuple-element.20.scale_ref, f32[32,2048]{1,0:T(8,128)S(1)} %get-tuple-element.23.now_ref.before_ref, ...), custom_call_target="tpu_custom_call" | custom-call | flops 268435456 | bytes 2097152 | tf_op jit(solution)/shard_map/near/pallas_call | solution.py:580
  58.6 1.7 %all-to-all-done.3.arrived_ref = bf16[8,32,256]{2,1,0:T(8,128)(2,1)S(1)} async-done(((bf16[8,32,256]{2,1,0:T(8,128)(2,1)}), bf16[8,32,256]{2,1,0:T(8,128)(2,1)S(1)}, u32[]{:S(2)}, u32[]{:S(2)}) %all-to-all-start.3) | async-done | bytes 131104 | tf_op jit(solution)/shard_map/all_to_all | solution.py:538
  60.4 4.0 %step.6 = (f32[32,2048]{1,0:T(8,128)S(1)}, bf16[8,32,256]{2,1,0:T(8,128)(2,1)}) custom-call(s32[128]{0:T(128)} %get-tuple-element.17.plan_ref, s32[8,1,8]{2,1,0:T(1,128)S(1)} %all-to-all-done.wanted_ref, f8e4m3fn[64,512,256]{2,1,0:T(32,128)(4,1)} %get-tuple-element.18.packed_hbm, f8e4m3fn[16,512,256]{2,1,0:T(32,128)(4,1)S(1)} %get-tuple-element.19.kept_ref, ...), custom_call_target="tpu_custom_call" | custom-call | tf_op jit(solution)/shard_map/step/pallas_call | solution.py:596
  64.4 3.7 %all-to-all-start.4 = ((bf16[8,32,256]{2,1,0:T(8,128)(2,1)}), bf16[8,32,256]{2,1,0:T(8,128)(2,1)S(1)}, u32[]{:S(2)}, u32[]{:S(2)}) async-start(bf16[8,32,256]{2,1,0:T(8,128)(2,1)} %get-tuple-element.26), calls=%async_computation.4 | async-start | bytes 262144 | tf_op jit(solution)/shard_map/all_to_all | solution.py:538
  68.1 3.8 %near.7.base_ref = f32[32,2048]{1,0:T(8,128)S(1)} custom-call(s32[96]{0:T(128)} %rows_ref.7, s32[96]{0:T(128)} %slots_ref.7, bf16[96,256,256]{2,1,0:T(8,128)(2,1)} %real_hbm.9, bf16[96,256,256]{2,1,0:T(8,128)(2,1)} %imag_hbm.9, f32[8,2048]{1,0:T(8,128)S(1)} %get-tuple-element.20.scale_ref, f32[32,2048]{1,0:T(8,128)S(1)} %get-tuple-element.25.now_ref, ...), custom_call_target="tpu_custom_call" | custom-call | flops 268435456 | bytes 2097152 | tf_op jit(solution)/shard_map/near/pallas_call | solution.py:580
  71.8 1.7 %all-to-all-done.4.arrived_ref = bf16[8,32,256]{2,1,0:T(8,128)(2,1)S(1)} async-done(((bf16[8,32,256]{2,1,0:T(8,128)(2,1)}), bf16[8,32,256]{2,1,0:T(8,128)(2,1)S(1)}, u32[]{:S(2)}, u32[]{:S(2)}) %all-to-all-start.4) | async-done | bytes 131104 | tf_op jit(solution)/shard_map/all_to_all | solution.py:538
  73.6 3.3 %step.7.own_ref = f32[32,2048]{1,0:T(8,128)S(1)} custom-call(s32[128]{0:T(128)} %get-tuple-element.17.plan_ref, s32[8,1,8]{2,1,0:T(1,128)S(1)} %all-to-all-done.wanted_ref, f8e4m3fn[64,512,256]{2,1,0:T(32,128)(4,1)} %get-tuple-element.18.packed_hbm, f8e4m3fn[16,512,256]{2,1,0:T(32,128)(4,1)S(1)} %get-tuple-element.19.kept_ref, ...), custom_call_target="tpu_custom_call" | custom-call | tf_op jit(solution)/shard_map/step/pallas_call | solution.py:596
  76.9 1.6 %collective-permute-start.1 = (bf16[32,2048]{1,0:T(8,128)(2,1)S(1)}, bf16[32,2048]{1,0:T(8,128)(2,1)S(1)}, u32[]{:S(2)}, u32[]{:S(2)}) collective-permute-start(bf16[32,2048]{1,0:T(8,128)(2,1)S(1)} %convert_element_type.3), channel_id=1, source_target_pairs={{0,2},{1,3},{2,0},{3,1},{4,6},{5,7},{6,4},{7,5},{8,10},{9,11},{10,... | collective-permute-start | bytes 393224 | tf_op jit(solution)/shard_map/ppermute | solution.py:543
  78.5 3.5 %collective-permute-done.1.refs_1_ = bf16[32,2048]{1,0:T(8,128)(2,1)S(1)} collective-permute-done((bf16[32,2048]{1,0:T(8,128)(2,1)S(1)}, bf16[32,2048]{1,0:T(8,128)(2,1)S(1)}, u32[]{:S(2)}, u32[]{:S(2)}) %collective-permute-start.1) | collective-permute-done | bytes 131104 | tf_op jit(solution)/shard_map/ppermute | solution.py:543
  81.9 1.3 %collective-permute-done.2.refs_2_ = bf16[32,2048]{1,0:T(8,128)(2,1)S(1)} collective-permute-done((bf16[32,2048]{1,0:T(8,128)(2,1)S(1)}, bf16[32,2048]{1,0:T(8,128)(2,1)S(1)}, u32[]{:S(2)}, u32[]{:S(2)}) %collective-permute-start.2) | collective-permute-done | bytes 131104 | tf_op jit(solution)/shard_map/ppermute | solution.py:543
  84.0 3.7 %collective-permute-done.3 = f32[64,128]{1,0:T(8,128)S(1)} collective-permute-done((f32[64,128]{1,0:T(8,128)S(1)}, f32[64,128]{1,0:T(8,128)S(1)}, u32[]{:S(2)}, u32[]{:S(2)}) %collective-permute-start.3) | collective-permute-done | bytes 32800 | tf_op jit(solution)/shard_map/ppermute | solution.py:543
  89.5 2.5 %collective-permute-start.4 = (f32[64,128]{1,0:T(8,128)S(1)}, f32[64,128]{1,0:T(8,128)S(1)}, u32[]{:S(2)}, u32[]{:S(2)}) collective-permute-start(f32[64,128]{1,0:T(8,128)S(1)} %add.3.refs_0_), channel_id=1, source_target_pairs={{0,8},{4,12},{8,0},{12,4},{16,24},{20,28},{24,16},{28,20},{1,9},{5... | collective-permute-start | bytes 98312 | tf_op jit(solution)/shard_map/ppermute | solution.py:543
  94.3 4.8 %factor.1 = f32[32,2048]{1,0:T(8,128)} custom-call(f32[32,2048]{1,0:T(8,128)S(1)} %step.7.own_ref, bf16[4,32,2048]{2,1,0:T(8,128)(2,1)S(1)} %get-tuple-element.27.all_ref, f32[64,128]{1,0:T(8,128)S(1)} %add.3.refs_0_, f32[64,128]{1,0:T(8,128)S(1)} %collective-permute-done.4.refs_1_, f32[64,128]{1,0:T(8,128)S(1)} %collective-permute-done.5.refs_2_, ...), custom_call_target="tpu_custom_call" | custom-call | tf_op jit(solution)/shard_map/factor/pallas_call | solution.py:632
  (17 shorter events, 7.4 us)
Async XLA Ops:
  1.2 20.8 %all-to-all-start = ((s32[8,1,8]{2,1,0:T(1,128)}), s32[8,1,8]{2,1,0:T(1,128)S(1)}, u32[]{:S(2)}, u32[]{:S(2)}) async-start(s32[8,1,8]{2,1,0:T(1,128)} %broadcast_in_dim.9), calls=%async_computation | async-start | bytes 8192 | tf_op jit(solution)/shard_map/all_to_all | solution.py:538
  9.1 12.9 %copy-start = (f32[32,2048]{1,0:T(8,128)S(1)}, f32[32,2048]{1,0:T(8,128)}, u32[]{:S(2)}) copy-start(f32[32,2048]{1,0:T(8,128)} %before_ref.3) | copy-start | bytes 786436
  23.4 10.6 %all-to-all-start.1 = ((bf16[8,32,256]{2,1,0:T(8,128)(2,1)}), bf16[8,32,256]{2,1,0:T(8,128)(2,1)S(1)}, u32[]{:S(2)}, u32[]{:S(2)}) async-start(bf16[8,32,256]{2,1,0:T(8,128)(2,1)} %first.1), calls=%async_computation.1 | async-start | bytes 262144 | tf_op jit(solution)/shard_map/all_to_all | solution.py:538
  38.0 9.2 %all-to-all-start.2 = ((bf16[8,32,256]{2,1,0:T(8,128)(2,1)}), bf16[8,32,256]{2,1,0:T(8,128)(2,1)S(1)}, u32[]{:S(2)}, u32[]{:S(2)}) async-start(bf16[8,32,256]{2,1,0:T(8,128)(2,1)} %get-tuple-element.22), calls=%async_computation.2 | async-start | bytes 262144 | tf_op jit(solution)/shard_map/all_to_all | solution.py:538
  51.2 9.2 %all-to-all-start.3 = ((bf16[8,32,256]{2,1,0:T(8,128)(2,1)}), bf16[8,32,256]{2,1,0:T(8,128)(2,1)S(1)}, u32[]{:S(2)}, u32[]{:S(2)}) async-start(bf16[8,32,256]{2,1,0:T(8,128)(2,1)} %get-tuple-element.24), calls=%async_computation.3 | async-start | bytes 262144 | tf_op jit(solution)/shard_map/all_to_all | solution.py:538
  64.4 9.2 %all-to-all-start.4 = ((bf16[8,32,256]{2,1,0:T(8,128)(2,1)}), bf16[8,32,256]{2,1,0:T(8,128)(2,1)S(1)}, u32[]{:S(2)}, u32[]{:S(2)}) async-start(bf16[8,32,256]{2,1,0:T(8,128)(2,1)} %get-tuple-element.26), calls=%async_computation.4 | async-start | bytes 262144 | tf_op jit(solution)/shard_map/all_to_all | solution.py:538
  76.9 5.0 %collective-permute-start.1 = (bf16[32,2048]{1,0:T(8,128)(2,1)S(1)}, bf16[32,2048]{1,0:T(8,128)(2,1)S(1)}, u32[]{:S(2)}, u32[]{:S(2)}) collective-permute-start(bf16[32,2048]{1,0:T(8,128)(2,1)S(1)} %convert_element_type.3), channel_id=1, source_target_pairs={{0,2},{1,3},{2,0},{3,1},{4,6},{5,7},{6,4},{7,5},{8,10},{9,11},{10,... | collective-permute-start | bytes 393224 | tf_op jit(solution)/shard_map/ppermute | solution.py:543
  78.5 3.5 %collective-permute-start = (bf16[32,2048]{1,0:T(8,128)(2,1)S(1)}, bf16[32,2048]{1,0:T(8,128)(2,1)S(1)}, u32[]{:S(2)}, u32[]{:S(2)}) collective-permute-start(bf16[32,2048]{1,0:T(8,128)(2,1)S(1)} %convert_element_type.3), channel_id=1, source_target_pairs={{0,1},{1,0},{2,3},{3,2},{4,5},{5,4},{6,7},{7,6},{8,9},{9,8},{10,11... | collective-permute-start | bytes 393224 | tf_op jit(solution)/shard_map/ppermute | solution.py:543
  81.9 1.3 %collective-permute-start.2 = (bf16[32,2048]{1,0:T(8,128)(2,1)S(1)}, bf16[32,2048]{1,0:T(8,128)(2,1)S(1)}, u32[]{:S(2)}, u32[]{:S(2)}) collective-permute-start(bf16[32,2048]{1,0:T(8,128)(2,1)S(1)} %collective-permute-done.1.refs_1_), channel_id=1, source_target_pairs={{0,1},{1,0},{2,3},{3,2},{4,5},{5,4},{6,7},{7,6},{8,9},{9,8},{10,11... | collective-permute-start | bytes 393224 | tf_op jit(solution)/shard_map/ppermute | solution.py:543
  83.7 4.0 %collective-permute-start.3 = (f32[64,128]{1,0:T(8,128)S(1)}, f32[64,128]{1,0:T(8,128)S(1)}, u32[]{:S(2)}, u32[]{:S(2)}) collective-permute-start(f32[64,128]{1,0:T(8,128)S(1)} %get-tuple-element.28), channel_id=1, source_target_pairs={{0,4},{4,0},{8,12},{12,8},{16,20},{20,16},{24,28},{28,24},{1,5},{5... | collective-permute-start | bytes 98312 | tf_op jit(solution)/shard_map/ppermute | solution.py:543
  87.7 5.7 %collective-permute-start.6 = (f32[64,128]{1,0:T(8,128)S(1)}, f32[64,128]{1,0:T(8,128)S(1)}, u32[]{:S(2)}, u32[]{:S(2)}) collective-permute-start(f32[64,128]{1,0:T(8,128)S(1)} %add.3.refs_0_), channel_id=1, source_target_pairs={{0,24},{4,28},{8,16},{12,20},{16,8},{20,12},{24,0},{28,4},{1,25},{... | collective-permute-start | bytes 98312 | tf_op jit(solution)/shard_map/ppermute | solution.py:543
  89.0 5.2 %collective-permute-start.5 = (f32[64,128]{1,0:T(8,128)S(1)}, f32[64,128]{1,0:T(8,128)S(1)}, u32[]{:S(2)}, u32[]{:S(2)}) collective-permute-start(f32[64,128]{1,0:T(8,128)S(1)} %add.3.refs_0_), channel_id=1, source_target_pairs={{0,16},{4,20},{8,24},{12,28},{16,0},{20,4},{24,8},{28,12},{1,17},{... | collective-permute-start | bytes 98312 | tf_op jit(solution)/shard_map/ppermute | solution.py:543
  89.5 4.8 %collective-permute-start.4 = (f32[64,128]{1,0:T(8,128)S(1)}, f32[64,128]{1,0:T(8,128)S(1)}, u32[]{:S(2)}, u32[]{:S(2)}) collective-permute-start(f32[64,128]{1,0:T(8,128)S(1)} %add.3.refs_0_), channel_id=1, source_target_pairs={{0,8},{4,12},{8,0},{12,4},{16,24},{20,28},{24,16},{28,20},{1,9},{5... | collective-permute-start | bytes 98312 | tf_op jit(solution)/shard_map/ppermute | solution.py:543

commit v22 on v18

--- a/solution.py
+++ b/solution.py
@@ -121,7 +121,7 @@
     for copy in lists:
         copy.wait()
 
-    def link(c, carry):
+    def link(c, entries):
         for t in [c * CHUNK + j for j in range(CHUNK)]:
             key = rows_ref[t] * slots + slots_ref[t]
             seen = table_ref[key]
@@ -132,9 +132,10 @@
             done_ref[t] = 1
             done_ref[jnp.where(joins, before, tiles)] = 0
             table_ref[key] = t | (jnp.where(joins, length + 1, 1) << 8)
-        return carry
-
-    lax.fori_loop(near_count // CHUNK, chunks, link, 0)
+            entries = entries + jnp.where(joins, 0, 1)
+        return entries
+
+    entries = lax.fori_loop(near_count // CHUNK, chunks, link, 0)
 
     def fill(ref, e, t):
         for at in [slice(q, q + 128) for q in range(0, 2 * order, 128)]:
@@ -187,18 +188,18 @@
             listed = one(c * CHUNK + j, listed)
         return listed
 
-    lax.fori_loop(0, near_count // CHUNK, near_chunk, 0)
-    listed = lax.fori_loop(near_count // CHUNK, chunks, far_chunk, 0)
-    short = (UNROLL - listed % UNROLL) % UNROLL
+    short = (UNROLL - entries % UNROLL) % UNROLL
     for j in range(UNROLL - 1):
 
         @pl.when(j < short)
         def _():
-            put(listed + j, None)
-            plan_ref[listed + j] = (slots - rb_dev) << 8
-
-    every = listed + short
+            put(entries + j, None)
+            plan_ref[entries + j] = (slots - rb_dev) << 8
+
+    every = entries + short
     plan_ref[tiles] = every // UNROLL
+    lax.fori_loop(0, near_count // CHUNK, near_chunk, 0)
+    lax.fori_loop(near_count // CHUNK, chunks, far_chunk, 0)
     plan_copy = pltpu.make_async_copy(plan_ref, plan_hbm, list_sems.at[2])
     plan_copy.start()
 
@@ -263,6 +264,14 @@
         pltpu.make_async_copy(sent_ref.at[wanted_ref[i, 0, me]], out_hbm.at[i], sems.at[i])
         for i in range(out_hbm.shape[0])
     ]
+    for copy in copies:
+        copy.start()
+    for copy in copies:
+        copy.wait()
+
+
+def spread_kernel(picks_hbm, out_hbm, sems):
+    copies = [pltpu.make_async_copy(picks_hbm, out_hbm.at[i], sems.at[i]) for i in range(out_hbm.shape[0])]
     for copy in copies:
         copy.start()
     for copy in copies:
@@ -555,7 +564,16 @@
     nblk = lax.axis_size("blk")
     ncol = lax.axis_size("col")
     near_count = LOC_RB * rb_dev
-    wanted = exchange(jnp.broadcast_to(fetch_pick[None], (nblk, 1, nblk)))
+    asked = pl.pallas_call(
+        spread_kernel,
+        name="spread",
+        out_shape=pltpu.HBM((nblk, 1, nblk), I32),
+        in_specs=[ANY],
+        out_specs=ANY,
+        scratch_shapes=[pltpu.SemaphoreType.DMA((nblk,))],
+        compiler_params=params(LIMIT),
+    )(in_hbm(fetch_pick))
+    wanted = exchange(asked)
     packed, kept, scale, plan = tiles_call(tile_rows, tile_slots, tile_real, tile_imag, rb_dev, near_count)
 
     out_blocks = pltpu.HBM((nblk, group, order), BF16)

time: 100 us -> 100 us (level)
  Pallas kernels: 49.9 us -> 51.5 us
  local copies, waits for them, and re-layouts: 1.25 us -> 0.01 us
    pallas_call x0 -> x1, Pallas kernels: none -> 1.43 us  [per_device(): pl.pallas_call(spread_kernel, name='spread', out_shape=pltpu.HBM((nblk, 1...]
    broadcast_in_dim x1 -> x0, local copies, waits for them, and re-layouts: 1.25 us -> none  [per_device(): wanted = exchange(jnp.broadcast_to(fetch_pick[None], (nblk, 1, nblk)))]
where the time goes in v22:
time: 100 us; the launch traced here: 99.6 us
  Pallas kernels  51.5 us (52%)
  starting transfers between devices  29.4 us (29%)
  waiting for transfers between devices  18.6 us (19%)
    all_to_all x5, starting transfers between devices, exchange(): lax.all_to_all(x, 'blk', split_axis=0, concat_axis=0, tiled=True, axis_in...  23.2 us
    pallas_call x4, Pallas kernels, per_device(): pl.pallas_call(functools.partial(step_kernel, step), name='step', out_sha...  15.3 us
    pallas_call x4, Pallas kernels, per_device(): pl.pallas_call(functools.partial(near_kernel, step), name='near', out_sha...  15 us
    pallas_call x1, Pallas kernels, tiles_call(): pl.pallas_call(functools.partial(tiles_kernel, near_count), name='tiles',...  13.2 us
    ppermute x7, waiting for transfers between devices, to_partner(): return lax.ppermute(x, axis, [(i, i ^ mask) for i in range(n)])  10.8 us
    all_to_all x5, waiting for transfers between devices, exchange(): lax.all_to_all(x, 'blk', split_axis=0, concat_axis=0, tiled=True, axis_in...  7.82 us
    ppermute x7, starting transfers between devices, to_partner(): return lax.ppermute(x, axis, [(i, i ^ mask) for i in range(n)])  6.23 us
    pallas_call x1, Pallas kernels, per_device(): pl.pallas_call(functools.partial(factor_kernel, rows * nblk), name='facto...  4.79 us
  transfers between devices with their start and end apart: 12, of which 10 were waited for; matrix products, arithmetic and copies ran while one was open for 0% of the time, Pallas kernels for 28%

profile of v22, /device:TPU:0, one launch (start us, length us, event | category | flops | bytes accessed | tf_op | source)
XLA Modules:
  0.0 99.6 jit_solution(16222814356588408729)
XLA Ops:
  1.4 7.9 %all-to-all-start = ((s32[8,1,8]{2,1,0:T(1,128)}), s32[8,1,8]{2,1,0:T(1,128)S(1)}, u32[]{:S(2)}, u32[]{:S(2)}) async-start(s32[8,1,8]{2,1,0:T(1,128)} %spread.1), calls=%async_computation | async-start | bytes 8192 | tf_op jit(solution)/shard_map/all_to_all | solution.py:544
  9.3 13.2 %tiles.1 = (f8e4m3fn[64,512,256]{2,1,0:T(32,128)(4,1)}, f8e4m3fn[16,512,256]{2,1,0:T(32,128)(4,1)S(1)}, f32[8,2048]{1,0:T(8,128)S(1)}, s32[128]{0:T(128)}) custom-call(s32[96]{0:T(128)} %rows_ref.7, s32[96]{0:T(128)} %slots_ref.7, bf16[96,256,256]{2,1,0:T(8,128)(2,1)} %real_hbm.9, bf16[96,256,256]{2,1,0:T(8,128)(2,1)} %imag_hbm.9), custom_call_target="tpu_custom_call" | custom-call | flops 268435456 | bytes 25165824 | tf_op jit(solution)/shard_map/tiles/pallas_call | solution.py:226
  23.9 4.8 %all-to-all-start.1 = ((bf16[8,32,256]{2,1,0:T(8,128)(2,1)}), bf16[8,32,256]{2,1,0:T(8,128)(2,1)S(1)}, u32[]{:S(2)}, u32[]{:S(2)}) async-start(bf16[8,32,256]{2,1,0:T(8,128)(2,1)} %first.1), calls=%async_computation.1 | async-start | bytes 262144 | tf_op jit(solution)/shard_map/all_to_all | solution.py:544
  28.7 3.7 %near.4.base_ref = f32[32,2048]{1,0:T(8,128)S(1)} custom-call(s32[96]{0:T(128)} %rows_ref.7, s32[96]{0:T(128)} %slots_ref.7, bf16[96,256,256]{2,1,0:T(8,128)(2,1)} %real_hbm.9, bf16[96,256,256]{2,1,0:T(8,128)(2,1)} %imag_hbm.9, f32[8,2048]{1,0:T(8,128)S(1)} %get-tuple-element.20.scale_ref, f32[32,2048]{1,0:T(8,128)S(1)} %copy-done, f32[32,2048]{1,0:T(8,128)S(1)} %copy-done), custom_call_target="tpu_custom_call" | custom-call | flops 268435456 | bytes 2097152 | tf_op jit(solution)/shard_map/near/pallas_call | solution.py:595
  32.5 2.0 %all-to-all-done.1.arrived_ref = bf16[8,32,256]{2,1,0:T(8,128)(2,1)S(1)} async-done(((bf16[8,32,256]{2,1,0:T(8,128)(2,1)}), bf16[8,32,256]{2,1,0:T(8,128)(2,1)S(1)}, u32[]{:S(2)}, u32[]{:S(2)}) %all-to-all-start.1) | async-done | bytes 131104 | tf_op jit(solution)/shard_map/all_to_all | solution.py:544
  34.4 4.0 %step.4 = (f32[32,2048]{1,0:T(8,128)S(1)}, bf16[8,32,256]{2,1,0:T(8,128)(2,1)}) custom-call(s32[128]{0:T(128)} %get-tuple-element.17.plan_ref, s32[8,1,8]{2,1,0:T(1,128)S(1)} %all-to-all-done.wanted_ref, f8e4m3fn[64,512,256]{2,1,0:T(32,128)(4,1)} %get-tuple-element.18.packed_hbm, f8e4m3fn[16,512,256]{2,1,0:T(32,128)(4,1)S(1)} %get-tuple-element.19.kept_ref, ...), custom_call_target="tpu_custom_call" | custom-call | tf_op jit(solution)/shard_map/step/pallas_call | solution.py:611
  38.4 3.5 %all-to-all-start.2 = ((bf16[8,32,256]{2,1,0:T(8,128)(2,1)}), bf16[8,32,256]{2,1,0:T(8,128)(2,1)S(1)}, u32[]{:S(2)}, u32[]{:S(2)}) async-start(bf16[8,32,256]{2,1,0:T(8,128)(2,1)} %get-tuple-element.22), calls=%async_computation.2 | async-start | bytes 262144 | tf_op jit(solution)/shard_map/all_to_all | solution.py:544
  41.9 3.7 %near.5.base_ref = f32[32,2048]{1,0:T(8,128)S(1)} custom-call(s32[96]{0:T(128)} %rows_ref.7, s32[96]{0:T(128)} %slots_ref.7, bf16[96,256,256]{2,1,0:T(8,128)(2,1)} %real_hbm.9, bf16[96,256,256]{2,1,0:T(8,128)(2,1)} %imag_hbm.9, f32[8,2048]{1,0:T(8,128)S(1)} %get-tuple-element.20.scale_ref, f32[32,2048]{1,0:T(8,128)S(1)} %get-tuple-element.21.now_ref.before_ref, ...), custom_call_target="tpu_custom_call" | custom-call | flops 268435456 | bytes 2097152 | tf_op jit(solution)/shard_map/near/pallas_call | solution.py:595
  45.7 2.0 %all-to-all-done.2.arrived_ref = bf16[8,32,256]{2,1,0:T(8,128)(2,1)S(1)} async-done(((bf16[8,32,256]{2,1,0:T(8,128)(2,1)}), bf16[8,32,256]{2,1,0:T(8,128)(2,1)S(1)}, u32[]{:S(2)}, u32[]{:S(2)}) %all-to-all-start.2) | async-done | bytes 131104 | tf_op jit(solution)/shard_map/all_to_all | solution.py:544
  47.6 4.0 %step.5 = (f32[32,2048]{1,0:T(8,128)S(1)}, bf16[8,32,256]{2,1,0:T(8,128)(2,1)}) custom-call(s32[128]{0:T(128)} %get-tuple-element.17.plan_ref, s32[8,1,8]{2,1,0:T(1,128)S(1)} %all-to-all-done.wanted_ref, f8e4m3fn[64,512,256]{2,1,0:T(32,128)(4,1)} %get-tuple-element.18.packed_hbm, f8e4m3fn[16,512,256]{2,1,0:T(32,128)(4,1)S(1)} %get-tuple-element.19.kept_ref, ...), custom_call_target="tpu_custom_call" | custom-call | tf_op jit(solution)/shard_map/step/pallas_call | solution.py:611
  51.6 3.5 %all-to-all-start.3 = ((bf16[8,32,256]{2,1,0:T(8,128)(2,1)}), bf16[8,32,256]{2,1,0:T(8,128)(2,1)S(1)}, u32[]{:S(2)}, u32[]{:S(2)}) async-start(bf16[8,32,256]{2,1,0:T(8,128)(2,1)} %get-tuple-element.24), calls=%async_computation.3 | async-start | bytes 262144 | tf_op jit(solution)/shard_map/all_to_all | solution.py:544
  55.1 3.8 %near.6.base_ref = f32[32,2048]{1,0:T(8,128)S(1)} custom-call(s32[96]{0:T(128)} %rows_ref.7, s32[96]{0:T(128)} %slots_ref.7, bf16[96,256,256]{2,1,0:T(8,128)(2,1)} %real_hbm.9, bf16[96,256,256]{2,1,0:T(8,128)(2,1)} %imag_hbm.9, f32[8,2048]{1,0:T(8,128)S(1)} %get-tuple-element.20.scale_ref, f32[32,2048]{1,0:T(8,128)S(1)} %get-tuple-element.23.now_ref.before_ref, ...), custom_call_target="tpu_custom_call" | custom-call | flops 268435456 | bytes 2097152 | tf_op jit(solution)/shard_map/near/pallas_call | solution.py:595
  58.9 1.9 %all-to-all-done.3.arrived_ref = bf16[8,32,256]{2,1,0:T(8,128)(2,1)S(1)} async-done(((bf16[8,32,256]{2,1,0:T(8,128)(2,1)}), bf16[8,32,256]{2,1,0:T(8,128)(2,1)S(1)}, u32[]{:S(2)}, u32[]{:S(2)}) %all-to-all-start.3) | async-done | bytes 131104 | tf_op jit(solution)/shard_map/all_to_all | solution.py:544
  60.8 4.0 %step.6 = (f32[32,2048]{1,0:T(8,128)S(1)}, bf16[8,32,256]{2,1,0:T(8,128)(2,1)}) custom-call(s32[128]{0:T(128)} %get-tuple-element.17.plan_ref, s32[8,1,8]{2,1,0:T(1,128)S(1)} %all-to-all-done.wanted_ref, f8e4m3fn[64,512,256]{2,1,0:T(32,128)(4,1)} %get-tuple-element.18.packed_hbm, f8e4m3fn[16,512,256]{2,1,0:T(32,128)(4,1)S(1)} %get-tuple-element.19.kept_ref, ...), custom_call_target="tpu_custom_call" | custom-call | tf_op jit(solution)/shard_map/step/pallas_call | solution.py:611
  64.9 3.5 %all-to-all-start.4 = ((bf16[8,32,256]{2,1,0:T(8,128)(2,1)}), bf16[8,32,256]{2,1,0:T(8,128)(2,1)S(1)}, u32[]{:S(2)}, u32[]{:S(2)}) async-start(bf16[8,32,256]{2,1,0:T(8,128)(2,1)} %get-tuple-element.26), calls=%async_computation.4 | async-start | bytes 262144 | tf_op jit(solution)/shard_map/all_to_all | solution.py:544
  68.3 3.8 %near.7.base_ref = f32[32,2048]{1,0:T(8,128)S(1)} custom-call(s32[96]{0:T(128)} %rows_ref.7, s32[96]{0:T(128)} %slots_ref.7, bf16[96,256,256]{2,1,0:T(8,128)(2,1)} %real_hbm.9, bf16[96,256,256]{2,1,0:T(8,128)(2,1)} %imag_hbm.9, f32[8,2048]{1,0:T(8,128)S(1)} %get-tuple-element.20.scale_ref, f32[32,2048]{1,0:T(8,128)S(1)} %get-tuple-element.25.now_ref, ...), custom_call_target="tpu_custom_call" | custom-call | flops 268435456 | bytes 2097152 | tf_op jit(solution)/shard_map/near/pallas_call | solution.py:595
  72.1 1.9 %all-to-all-done.4.arrived_ref = bf16[8,32,256]{2,1,0:T(8,128)(2,1)S(1)} async-done(((bf16[8,32,256]{2,1,0:T(8,128)(2,1)}), bf16[8,32,256]{2,1,0:T(8,128)(2,1)S(1)}, u32[]{:S(2)}, u32[]{:S(2)}) %all-to-all-start.4) | async-done | bytes 131104 | tf_op jit(solution)/shard_map/all_to_all | solution.py:544
  74.0 3.3 %step.7.own_ref = f32[32,2048]{1,0:T(8,128)S(1)} custom-call(s32[128]{0:T(128)} %get-tuple-element.17.plan_ref, s32[8,1,8]{2,1,0:T(1,128)S(1)} %all-to-all-done.wanted_ref, f8e4m3fn[64,512,256]{2,1,0:T(32,128)(4,1)} %get-tuple-element.18.packed_hbm, f8e4m3fn[16,512,256]{2,1,0:T(32,128)(4,1)S(1)} %get-tuple-element.19.kept_ref, ...), custom_call_target="tpu_custom_call" | custom-call | tf_op jit(solution)/shard_map/step/pallas_call | solution.py:611
  77.4 1.6 %collective-permute-start.1 = (bf16[32,2048]{1,0:T(8,128)(2,1)S(1)}, bf16[32,2048]{1,0:T(8,128)(2,1)S(1)}, u32[]{:S(2)}, u32[]{:S(2)}) collective-permute-start(bf16[32,2048]{1,0:T(8,128)(2,1)S(1)} %convert_element_type.3), channel_id=1, source_target_pairs={{0,2},{1,3},{2,0},{3,1},{4,6},{5,7},{6,4},{7,5},{8,10},{9,11},{10,... | collective-permute-start | bytes 393224 | tf_op jit(solution)/shard_map/ppermute | solution.py:549
  78.9 3.5 %collective-permute-done.1.refs_1_ = bf16[32,2048]{1,0:T(8,128)(2,1)S(1)} collective-permute-done((bf16[32,2048]{1,0:T(8,128)(2,1)S(1)}, bf16[32,2048]{1,0:T(8,128)(2,1)S(1)}, u32[]{:S(2)}, u32[]{:S(2)}) %collective-permute-start.1) | collective-permute-done | bytes 131104 | tf_op jit(solution)/shard_map/ppermute | solution.py:549
  84.5 3.7 %collective-permute-done.3 = f32[64,128]{1,0:T(8,128)S(1)} collective-permute-done((f32[64,128]{1,0:T(8,128)S(1)}, f32[64,128]{1,0:T(8,128)S(1)}, u32[]{:S(2)}, u32[]{:S(2)}) %collective-permute-start.3) | collective-permute-done | bytes 32800 | tf_op jit(solution)/shard_map/ppermute | solution.py:549
  88.2 1.6 %collective-permute-start.6 = (f32[64,128]{1,0:T(8,128)S(1)}, f32[64,128]{1,0:T(8,128)S(1)}, u32[]{:S(2)}, u32[]{:S(2)}) collective-permute-start(f32[64,128]{1,0:T(8,128)S(1)} %add.3.refs_0_), channel_id=1, source_target_pairs={{0,24},{4,28},{8,16},{12,20},{16,8},{20,12},{24,0},{28,4},{1,25},{... | collective-permute-start | bytes 98312 | tf_op jit(solution)/shard_map/ppermute | solution.py:549
  89.8 2.7 %collective-permute-start.4 = (f32[64,128]{1,0:T(8,128)S(1)}, f32[64,128]{1,0:T(8,128)S(1)}, u32[]{:S(2)}, u32[]{:S(2)}) collective-permute-start(f32[64,128]{1,0:T(8,128)S(1)} %add.3.refs_0_), channel_id=1, source_target_pairs={{0,8},{4,12},{8,0},{12,4},{16,24},{20,28},{24,16},{28,20},{1,9},{5... | collective-permute-start | bytes 98312 | tf_op jit(solution)/shard_map/ppermute | solution.py:549
  94.8 4.8 %factor.1 = f32[32,2048]{1,0:T(8,128)} custom-call(f32[32,2048]{1,0:T(8,128)S(1)} %step.7.own_ref, bf16[4,32,2048]{2,1,0:T(8,128)(2,1)S(1)} %get-tuple-element.27.all_ref, f32[64,128]{1,0:T(8,128)S(1)} %add.3.refs_0_, f32[64,128]{1,0:T(8,128)S(1)} %collective-permute-done.4.refs_1_, f32[64,128]{1,0:T(8,128)S(1)} %collective-permute-done.5.refs_2_, ...), custom_call_target="tpu_custom_call" | custom-call | tf_op jit(solution)/shard_map/factor/pallas_call | solution.py:647
  (17 shorter events, 7.1 us)
Async XLA Ops:
  1.4 21.1 %all-to-all-start = ((s32[8,1,8]{2,1,0:T(1,128)}), s32[8,1,8]{2,1,0:T(1,128)S(1)}, u32[]{:S(2)}, u32[]{:S(2)}) async-start(s32[8,1,8]{2,1,0:T(1,128)} %spread.1), calls=%async_computation | async-start | bytes 8192 | tf_op jit(solution)/shard_map/all_to_all | solution.py:544
  9.3 13.2 %copy-start = (f32[32,2048]{1,0:T(8,128)S(1)}, f32[32,2048]{1,0:T(8,128)}, u32[]{:S(2)}) copy-start(f32[32,2048]{1,0:T(8,128)} %before_ref.3) | copy-start | bytes 786436
  23.9 10.6 %all-to-all-start.1 = ((bf16[8,32,256]{2,1,0:T(8,128)(2,1)}), bf16[8,32,256]{2,1,0:T(8,128)(2,1)S(1)}, u32[]{:S(2)}, u32[]{:S(2)}) async-start(bf16[8,32,256]{2,1,0:T(8,128)(2,1)} %first.1), calls=%async_computation.1 | async-start | bytes 262144 | tf_op jit(solution)/shard_map/all_to_all | solution.py:544
  38.4 9.2 %all-to-all-start.2 = ((bf16[8,32,256]{2,1,0:T(8,128)(2,1)}), bf16[8,32,256]{2,1,0:T(8,128)(2,1)S(1)}, u32[]{:S(2)}, u32[]{:S(2)}) async-start(bf16[8,32,256]{2,1,0:T(8,128)(2,1)} %get-tuple-element.22), calls=%async_computation.2 | async-start | bytes 262144 | tf_op jit(solution)/shard_map/all_to_all | solution.py:544
  51.6 9.2 %all-to-all-start.3 = ((bf16[8,32,256]{2,1,0:T(8,128)(2,1)}), bf16[8,32,256]{2,1,0:T(8,128)(2,1)S(1)}, u32[]{:S(2)}, u32[]{:S(2)}) async-start(bf16[8,32,256]{2,1,0:T(8,128)(2,1)} %get-tuple-element.24), calls=%async_computation.3 | async-start | bytes 262144 | tf_op jit(solution)/shard_map/all_to_all | solution.py:544
  64.9 9.2 %all-to-all-start.4 = ((bf16[8,32,256]{2,1,0:T(8,128)(2,1)}), bf16[8,32,256]{2,1,0:T(8,128)(2,1)S(1)}, u32[]{:S(2)}, u32[]{:S(2)}) async-start(bf16[8,32,256]{2,1,0:T(8,128)(2,1)} %get-tuple-element.26), calls=%async_computation.4 | async-start | bytes 262144 | tf_op jit(solution)/shard_map/all_to_all | solution.py:544
  77.4 5.0 %collective-permute-start.1 = (bf16[32,2048]{1,0:T(8,128)(2,1)S(1)}, bf16[32,2048]{1,0:T(8,128)(2,1)S(1)}, u32[]{:S(2)}, u32[]{:S(2)}) collective-permute-start(bf16[32,2048]{1,0:T(8,128)(2,1)S(1)} %convert_element_type.3), channel_id=1, source_target_pairs={{0,2},{1,3},{2,0},{3,1},{4,6},{5,7},{6,4},{7,5},{8,10},{9,11},{10,... | collective-permute-start | bytes 393224 | tf_op jit(solution)/shard_map/ppermute | solution.py:549
  78.9 3.5 %collective-permute-start = (bf16[32,2048]{1,0:T(8,128)(2,1)S(1)}, bf16[32,2048]{1,0:T(8,128)(2,1)S(1)}, u32[]{:S(2)}, u32[]{:S(2)}) collective-permute-start(bf16[32,2048]{1,0:T(8,128)(2,1)S(1)} %convert_element_type.3), channel_id=1, source_target_pairs={{0,1},{1,0},{2,3},{3,2},{4,5},{5,4},{6,7},{7,6},{8,9},{9,8},{10,11... | collective-permute-start | bytes 393224 | tf_op jit(solution)/shard_map/ppermute | solution.py:549
  82.4 1.3 %collective-permute-start.2 = (bf16[32,2048]{1,0:T(8,128)(2,1)S(1)}, bf16[32,2048]{1,0:T(8,128)(2,1)S(1)}, u32[]{:S(2)}, u32[]{:S(2)}) collective-permute-start(bf16[32,2048]{1,0:T(8,128)(2,1)S(1)} %collective-permute-done.1.refs_1_), channel_id=1, source_target_pairs={{0,1},{1,0},{2,3},{3,2},{4,5},{5,4},{6,7},{7,6},{8,9},{9,8},{10,11... | collective-permute-start | bytes 393224 | tf_op jit(solution)/shard_map/ppermute | solution.py:549
  84.2 4.0 %collective-permute-start.3 = (f32[64,128]{1,0:T(8,128)S(1)}, f32[64,128]{1,0:T(8,128)S(1)}, u32[]{:S(2)}, u32[]{:S(2)}) collective-permute-start(f32[64,128]{1,0:T(8,128)S(1)} %get-tuple-element.28), channel_id=1, source_target_pairs={{0,4},{4,0},{8,12},{12,8},{16,20},{20,16},{24,28},{28,24},{1,5},{5... | collective-permute-start | bytes 98312 | tf_op jit(solution)/shard_map/ppermute | solution.py:549
  88.2 5.7 %collective-permute-start.6 = (f32[64,128]{1,0:T(8,128)S(1)}, f32[64,128]{1,0:T(8,128)S(1)}, u32[]{:S(2)}, u32[]{:S(2)}) collective-permute-start(f32[64,128]{1,0:T(8,128)S(1)} %add.3.refs_0_), channel_id=1, source_target_pairs={{0,24},{4,28},{8,16},{12,20},{16,8},{20,12},{24,0},{28,4},{1,25},{... | collective-permute-start | bytes 98312 | tf_op jit(solution)/shard_map/ppermute | solution.py:549
  89.8 4.9 %collective-permute-start.5 = (f32[64,128]{1,0:T(8,128)S(1)}, f32[64,128]{1,0:T(8,128)S(1)}, u32[]{:S(2)}, u32[]{:S(2)}) collective-permute-start(f32[64,128]{1,0:T(8,128)S(1)} %add.3.refs_0_), channel_id=1, source_target_pairs={{0,16},{4,20},{8,24},{12,28},{16,0},{20,4},{24,8},{28,12},{1,17},{... | collective-permute-start | bytes 98312 | tf_op jit(solution)/shard_map/ppermute | solution.py:549
  89.8 5.0 %collective-permute-start.4 = (f32[64,128]{1,0:T(8,128)S(1)}, f32[64,128]{1,0:T(8,128)S(1)}, u32[]{:S(2)}, u32[]{:S(2)}) collective-permute-start(f32[64,128]{1,0:T(8,128)S(1)} %add.3.refs_0_), channel_id=1, source_target_pairs={{0,8},{4,12},{8,0},{12,4},{16,24},{20,28},{24,16},{28,20},{1,9},{5... | collective-permute-start | bytes 98312 | tf_op jit(solution)/shard_map/ppermute | solution.py:549

commit v23 on v22

--- a/solution.py
+++ b/solution.py
@@ -264,14 +264,6 @@
         pltpu.make_async_copy(sent_ref.at[wanted_ref[i, 0, me]], out_hbm.at[i], sems.at[i])
         for i in range(out_hbm.shape[0])
     ]
-    for copy in copies:
-        copy.start()
-    for copy in copies:
-        copy.wait()
-
-
-def spread_kernel(picks_hbm, out_hbm, sems):
-    copies = [pltpu.make_async_copy(picks_hbm, out_hbm.at[i], sems.at[i]) for i in range(out_hbm.shape[0])]
     for copy in copies:
         copy.start()
     for copy in copies:
@@ -535,7 +527,7 @@
 
 
 def central(nblk):
-    return nblk // 4
+    return nblk // 2 + nblk // 8
 
 
 def exchange(x):
@@ -564,16 +556,7 @@
     nblk = lax.axis_size("blk")
     ncol = lax.axis_size("col")
     near_count = LOC_RB * rb_dev
-    asked = pl.pallas_call(
-        spread_kernel,
-        name="spread",
-        out_shape=pltpu.HBM((nblk, 1, nblk), I32),
-        in_specs=[ANY],
-        out_specs=ANY,
-        scratch_shapes=[pltpu.SemaphoreType.DMA((nblk,))],
-        compiler_params=params(LIMIT),
-    )(in_hbm(fetch_pick))
-    wanted = exchange(asked)
+    wanted = exchange(jnp.broadcast_to(fetch_pick[None], (nblk, 1, nblk)))
     packed, kept, scale, plan = tiles_call(tile_rows, tile_slots, tile_real, tile_imag, rb_dev, near_count)
 
     out_blocks = pltpu.HBM((nblk, group, order), BF16)

time: 100 us -> 99.2 us (level)
  waiting for transfers between devices: 18.6 us -> 9.7 us
  starting transfers between devices: 29.4 us -> 37.4 us
  Pallas kernels: 51.5 us -> 49.8 us
  local copies, waits for them, and re-layouts: 0.01 us -> 1.25 us
    all_to_all x5, waiting for transfers between devices: 7.82 us -> 0.01 us  [exchange(): lax.all_to_all(x, 'blk', split_axis=0, concat_axis=0, tiled=True, axis_in...]
    all_to_all x5, starting transfers between devices: 23.2 us -> 29.6 us  [exchange(): lax.all_to_all(x, 'blk', split_axis=0, concat_axis=0, tiled=True, axis_in...]
    ppermute x7, starting transfers between devices: 6.23 us -> 7.79 us  [to_partner(): return lax.ppermute(x, axis, [(i, i ^ mask) for i in range(n)])]
    pallas_call x1 -> x0, Pallas kernels: 1.43 us -> none  [per_device(): pl.pallas_call(spread_kernel, name='spread', out_shape=pltpu.HBM((nblk, 1...]
    broadcast_in_dim x0 -> x1, local copies, waits for them, and re-layouts: none -> 1.25 us  [per_device(): wanted = exchange(jnp.broadcast_to(fetch_pick[None], (nblk, 1, nblk)))]
    ppermute x7, waiting for transfers between devices: 10.8 us -> 9.69 us  [to_partner(): return lax.ppermute(x, axis, [(i, i ^ mask) for i in range(n)])]
  transfers between devices with their start and end apart: 12 -> 12, of which waited for: 10 -> 5; matrix products, arithmetic and copies ran while one was open for 0% -> 0% of each run, Pallas kernels for 28% -> 28%
where the time goes in v23:
time: 99.2 us; the launch traced here: 98.3 us
  Pallas kernels  49.8 us (50%)
  starting transfers between devices  37.4 us (38%)
  waiting for transfers between devices  9.7 us (10%)
  local copies, waits for them, and re-layouts  1.25 us (1%)
    all_to_all x5, starting transfers between devices, exchange(): lax.all_to_all(x, 'blk', split_axis=0, concat_axis=0, tiled=True, axis_in...  29.6 us
    pallas_call x4, Pallas kernels, per_device(): pl.pallas_call(functools.partial(step_kernel, step), name='step', out_sha...  15.3 us
    pallas_call x4, Pallas kernels, per_device(): pl.pallas_call(functools.partial(near_kernel, step), name='near', out_sha...  15 us
    pallas_call x1, Pallas kernels, tiles_call(): pl.pallas_call(functools.partial(tiles_kernel, near_count), name='tiles',...  12.9 us
    ppermute x7, waiting for transfers between devices, to_partner(): return lax.ppermute(x, axis, [(i, i ^ mask) for i in range(n)])  9.69 us
    ppermute x7, starting transfers between devices, to_partner(): return lax.ppermute(x, axis, [(i, i ^ mask) for i in range(n)])  7.79 us
    pallas_call x1, Pallas kernels, per_device(): pl.pallas_call(functools.partial(factor_kernel, rows * nblk), name='facto...  4.79 us
  transfers between devices with their start and end apart: 12, of which 5 were waited for; matrix products, arithmetic and copies ran while one was open for 0% of the time, Pallas kernels for 28%

profile of v23, /device:TPU:0, one launch (start us, length us, event | category | flops | bytes accessed | tf_op | source)
XLA Modules:
  0.0 98.3 jit_solution(3762527750148415605)
XLA Ops:
  1.2 8.2 %all-to-all-start = ((s32[8,1,8]{2,1,0:T(1,128)}), s32[8,1,8]{2,1,0:T(1,128)S(1)}, u32[]{:S(2)}, u32[]{:S(2)}) async-start(s32[8,1,8]{2,1,0:T(1,128)} %broadcast_in_dim.9), calls=%async_computation | async-start | bytes 8192 | tf_op jit(solution)/shard_map/all_to_all | solution.py:536
  9.5 12.9 %tiles.1 = (f8e4m3fn[64,512,256]{2,1,0:T(32,128)(4,1)}, f8e4m3fn[16,512,256]{2,1,0:T(32,128)(4,1)S(1)}, f32[8,2048]{1,0:T(8,128)S(1)}, s32[128]{0:T(128)}) custom-call(s32[96]{0:T(128)} %rows_ref.7, s32[96]{0:T(128)} %slots_ref.7, bf16[96,256,256]{2,1,0:T(8,128)(2,1)} %real_hbm.9, bf16[96,256,256]{2,1,0:T(8,128)(2,1)} %imag_hbm.9), custom_call_target="tpu_custom_call" | custom-call | flops 268435456 | bytes 25165824 | tf_op jit(solution)/shard_map/tiles/pallas_call | solution.py:226
  22.5 1.3 %first.1 = bf16[8,32,256]{2,1,0:T(8,128)(2,1)} custom-call(f32[32,2048]{1,0:T(8,128)S(1)} %copy-done, f32[8,2048]{1,0:T(8,128)S(1)} %get-tuple-element.20.scale_ref, s32[8,1,8]{2,1,0:T(1,128)S(1)} %all-to-all-done.wanted_ref), custom_call_target="tpu_custom_call" | custom-call | tf_op jit(solution)/shard_map/first/pallas_call | solution.py:564
  23.8 5.1 %all-to-all-start.1 = ((bf16[8,32,256]{2,1,0:T(8,128)(2,1)}), bf16[8,32,256]{2,1,0:T(8,128)(2,1)S(1)}, u32[]{:S(2)}, u32[]{:S(2)}) async-start(bf16[8,32,256]{2,1,0:T(8,128)(2,1)} %first.1), calls=%async_computation.1 | async-start | bytes 262144 | tf_op jit(solution)/shard_map/all_to_all | solution.py:536
  28.9 3.7 %near.4.base_ref = f32[32,2048]{1,0:T(8,128)S(1)} custom-call(s32[96]{0:T(128)} %rows_ref.7, s32[96]{0:T(128)} %slots_ref.7, bf16[96,256,256]{2,1,0:T(8,128)(2,1)} %real_hbm.9, bf16[96,256,256]{2,1,0:T(8,128)(2,1)} %imag_hbm.9, f32[8,2048]{1,0:T(8,128)S(1)} %get-tuple-element.20.scale_ref, f32[32,2048]{1,0:T(8,128)S(1)} %copy-done, f32[32,2048]{1,0:T(8,128)S(1)} %copy-done), custom_call_target="tpu_custom_call" | custom-call | flops 268435456 | bytes 2097152 | tf_op jit(solution)/shard_map/near/pallas_call | solution.py:578
  32.7 4.0 %step.4 = (f32[32,2048]{1,0:T(8,128)S(1)}, bf16[8,32,256]{2,1,0:T(8,128)(2,1)}) custom-call(s32[128]{0:T(128)} %get-tuple-element.17.plan_ref, s32[8,1,8]{2,1,0:T(1,128)S(1)} %all-to-all-done.wanted_ref, f8e4m3fn[64,512,256]{2,1,0:T(32,128)(4,1)} %get-tuple-element.18.packed_hbm, f8e4m3fn[16,512,256]{2,1,0:T(32,128)(4,1)S(1)} %get-tuple-element.19.kept_ref, ...), custom_call_target="tpu_custom_call" | custom-call | tf_op jit(solution)/shard_map/step/pallas_call | solution.py:594
  36.7 5.4 %all-to-all-start.2 = ((bf16[8,32,256]{2,1,0:T(8,128)(2,1)}), bf16[8,32,256]{2,1,0:T(8,128)(2,1)S(1)}, u32[]{:S(2)}, u32[]{:S(2)}) async-start(bf16[8,32,256]{2,1,0:T(8,128)(2,1)} %get-tuple-element.22), calls=%async_computation.2 | async-start | bytes 262144 | tf_op jit(solution)/shard_map/all_to_all | solution.py:536
  42.1 3.7 %near.5.base_ref = f32[32,2048]{1,0:T(8,128)S(1)} custom-call(s32[96]{0:T(128)} %rows_ref.7, s32[96]{0:T(128)} %slots_ref.7, bf16[96,256,256]{2,1,0:T(8,128)(2,1)} %real_hbm.9, bf16[96,256,256]{2,1,0:T(8,128)(2,1)} %imag_hbm.9, f32[8,2048]{1,0:T(8,128)S(1)} %get-tuple-element.20.scale_ref, f32[32,2048]{1,0:T(8,128)S(1)} %get-tuple-element.21.now_ref.before_ref, ...), custom_call_target="tpu_custom_call" | custom-call | flops 268435456 | bytes 2097152 | tf_op jit(solution)/shard_map/near/pallas_call | solution.py:578
  45.9 4.0 %step.5 = (f32[32,2048]{1,0:T(8,128)S(1)}, bf16[8,32,256]{2,1,0:T(8,128)(2,1)}) custom-call(s32[128]{0:T(128)} %get-tuple-element.17.plan_ref, s32[8,1,8]{2,1,0:T(1,128)S(1)} %all-to-all-done.wanted_ref, f8e4m3fn[64,512,256]{2,1,0:T(32,128)(4,1)} %get-tuple-element.18.packed_hbm, f8e4m3fn[16,512,256]{2,1,0:T(32,128)(4,1)S(1)} %get-tuple-element.19.kept_ref, ...), custom_call_target="tpu_custom_call" | custom-call | tf_op jit(solution)/shard_map/step/pallas_call | solution.py:594
  49.9 5.4 %all-to-all-start.3 = ((bf16[8,32,256]{2,1,0:T(8,128)(2,1)}), bf16[8,32,256]{2,1,0:T(8,128)(2,1)S(1)}, u32[]{:S(2)}, u32[]{:S(2)}) async-start(bf16[8,32,256]{2,1,0:T(8,128)(2,1)} %get-tuple-element.24), calls=%async_computation.3 | async-start | bytes 262144 | tf_op jit(solution)/shard_map/all_to_all | solution.py:536
  55.3 3.8 %near.6.base_ref = f32[32,2048]{1,0:T(8,128)S(1)} custom-call(s32[96]{0:T(128)} %rows_ref.7, s32[96]{0:T(128)} %slots_ref.7, bf16[96,256,256]{2,1,0:T(8,128)(2,1)} %real_hbm.9, bf16[96,256,256]{2,1,0:T(8,128)(2,1)} %imag_hbm.9, f32[8,2048]{1,0:T(8,128)S(1)} %get-tuple-element.20.scale_ref, f32[32,2048]{1,0:T(8,128)S(1)} %get-tuple-element.23.now_ref.before_ref, ...), custom_call_target="tpu_custom_call" | custom-call | flops 268435456 | bytes 2097152 | tf_op jit(solution)/shard_map/near/pallas_call | solution.py:578
  59.1 4.0 %step.6 = (f32[32,2048]{1,0:T(8,128)S(1)}, bf16[8,32,256]{2,1,0:T(8,128)(2,1)}) custom-call(s32[128]{0:T(128)} %get-tuple-element.17.plan_ref, s32[8,1,8]{2,1,0:T(1,128)S(1)} %all-to-all-done.wanted_ref, f8e4m3fn[64,512,256]{2,1,0:T(32,128)(4,1)} %get-tuple-element.18.packed_hbm, f8e4m3fn[16,512,256]{2,1,0:T(32,128)(4,1)S(1)} %get-tuple-element.19.kept_ref, ...), custom_call_target="tpu_custom_call" | custom-call | tf_op jit(solution)/shard_map/step/pallas_call | solution.py:594
  63.1 5.4 %all-to-all-start.4 = ((bf16[8,32,256]{2,1,0:T(8,128)(2,1)}), bf16[8,32,256]{2,1,0:T(8,128)(2,1)S(1)}, u32[]{:S(2)}, u32[]{:S(2)}) async-start(bf16[8,32,256]{2,1,0:T(8,128)(2,1)} %get-tuple-element.26), calls=%async_computation.4 | async-start | bytes 262144 | tf_op jit(solution)/shard_map/all_to_all | solution.py:536
  68.5 3.8 %near.7.base_ref = f32[32,2048]{1,0:T(8,128)S(1)} custom-call(s32[96]{0:T(128)} %rows_ref.7, s32[96]{0:T(128)} %slots_ref.7, bf16[96,256,256]{2,1,0:T(8,128)(2,1)} %real_hbm.9, bf16[96,256,256]{2,1,0:T(8,128)(2,1)} %imag_hbm.9, f32[8,2048]{1,0:T(8,128)S(1)} %get-tuple-element.20.scale_ref, f32[32,2048]{1,0:T(8,128)S(1)} %get-tuple-element.25.now_ref, ...), custom_call_target="tpu_custom_call" | custom-call | flops 268435456 | bytes 2097152 | tf_op jit(solution)/shard_map/near/pallas_call | solution.py:578
  72.3 3.3 %step.7.own_ref = f32[32,2048]{1,0:T(8,128)S(1)} custom-call(s32[128]{0:T(128)} %get-tuple-element.17.plan_ref, s32[8,1,8]{2,1,0:T(1,128)S(1)} %all-to-all-done.wanted_ref, f8e4m3fn[64,512,256]{2,1,0:T(32,128)(4,1)} %get-tuple-element.18.packed_hbm, f8e4m3fn[16,512,256]{2,1,0:T(32,128)(4,1)S(1)} %get-tuple-element.19.kept_ref, ...), custom_call_target="tpu_custom_call" | custom-call | tf_op jit(solution)/shard_map/step/pallas_call | solution.py:594
  75.6 1.6 %collective-permute-start.1 = (bf16[32,2048]{1,0:T(8,128)(2,1)S(1)}, bf16[32,2048]{1,0:T(8,128)(2,1)S(1)}, u32[]{:S(2)}, u32[]{:S(2)}) collective-permute-start(bf16[32,2048]{1,0:T(8,128)(2,1)S(1)} %convert_element_type.3), channel_id=1, source_target_pairs={{0,2},{1,3},{2,0},{3,1},{4,6},{5,7},{6,4},{7,5},{8,10},{9,11},{10,... | collective-permute-start | bytes 393224 | tf_op jit(solution)/shard_map/ppermute | solution.py:541
  77.2 3.5 %collective-permute-done.1.refs_1_ = bf16[32,2048]{1,0:T(8,128)(2,1)S(1)} collective-permute-done((bf16[32,2048]{1,0:T(8,128)(2,1)S(1)}, bf16[32,2048]{1,0:T(8,128)(2,1)S(1)}, u32[]{:S(2)}, u32[]{:S(2)}) %collective-permute-start.1) | collective-permute-done | bytes 131104 | tf_op jit(solution)/shard_map/ppermute | solution.py:541
  80.7 1.3 %collective-permute-done.2.refs_2_ = bf16[32,2048]{1,0:T(8,128)(2,1)S(1)} collective-permute-done((bf16[32,2048]{1,0:T(8,128)(2,1)S(1)}, bf16[32,2048]{1,0:T(8,128)(2,1)S(1)}, u32[]{:S(2)}, u32[]{:S(2)}) %collective-permute-start.2) | collective-permute-done | bytes 131104 | tf_op jit(solution)/shard_map/ppermute | solution.py:541
  82.4 1.8 %collective-permute-start.3 = (f32[64,128]{1,0:T(8,128)S(1)}, f32[64,128]{1,0:T(8,128)S(1)}, u32[]{:S(2)}, u32[]{:S(2)}) collective-permute-start(f32[64,128]{1,0:T(8,128)S(1)} %get-tuple-element.28), channel_id=1, source_target_pairs={{0,4},{4,0},{8,12},{12,8},{16,20},{20,16},{24,28},{28,24},{1,5},{5... | collective-permute-start | bytes 98312 | tf_op jit(solution)/shard_map/ppermute | solution.py:541
  84.3 2.1 %collective-permute-done.3 = f32[64,128]{1,0:T(8,128)S(1)} collective-permute-done((f32[64,128]{1,0:T(8,128)S(1)}, f32[64,128]{1,0:T(8,128)S(1)}, u32[]{:S(2)}, u32[]{:S(2)}) %collective-permute-start.3) | collective-permute-done | bytes 32800 | tf_op jit(solution)/shard_map/ppermute | solution.py:541
  86.4 2.1 %collective-permute-start.6 = (f32[64,128]{1,0:T(8,128)S(1)}, f32[64,128]{1,0:T(8,128)S(1)}, u32[]{:S(2)}, u32[]{:S(2)}) collective-permute-start(f32[64,128]{1,0:T(8,128)S(1)} %add.3.refs_0_), channel_id=1, source_target_pairs={{0,24},{4,28},{8,16},{12,20},{16,8},{20,12},{24,0},{28,4},{1,25},{... | collective-permute-start | bytes 98312 | tf_op jit(solution)/shard_map/ppermute | solution.py:541
  88.9 1.9 %collective-permute-start.4 = (f32[64,128]{1,0:T(8,128)S(1)}, f32[64,128]{1,0:T(8,128)S(1)}, u32[]{:S(2)}, u32[]{:S(2)}) collective-permute-start(f32[64,128]{1,0:T(8,128)S(1)} %add.3.refs_0_), channel_id=1, source_target_pairs={{0,8},{4,12},{8,0},{12,4},{16,24},{20,28},{24,16},{28,20},{1,9},{5... | collective-permute-start | bytes 98312 | tf_op jit(solution)/shard_map/ppermute | solution.py:541
  90.8 1.5 %collective-permute-done.6.refs_3_ = f32[64,128]{1,0:T(8,128)S(1)} collective-permute-done((f32[64,128]{1,0:T(8,128)S(1)}, f32[64,128]{1,0:T(8,128)S(1)}, u32[]{:S(2)}, u32[]{:S(2)}) %collective-permute-start.6) | collective-permute-done | bytes 32800 | tf_op jit(solution)/shard_map/ppermute | solution.py:541
  93.5 4.8 %factor.1 = f32[32,2048]{1,0:T(8,128)} custom-call(f32[32,2048]{1,0:T(8,128)S(1)} %step.7.own_ref, bf16[4,32,2048]{2,1,0:T(8,128)(2,1)S(1)} %get-tuple-element.27.all_ref, f32[64,128]{1,0:T(8,128)S(1)} %add.3.refs_0_, f32[64,128]{1,0:T(8,128)S(1)} %collective-permute-done.4.refs_1_, f32[64,128]{1,0:T(8,128)S(1)} %collective-permute-done.5.refs_2_, ...), custom_call_target="tpu_custom_call" | custom-call | tf_op jit(solution)/shard_map/factor/pallas_call | solution.py:630
  (17 shorter events, 3.3 us)
Async XLA Ops:
  1.2 21.2 %all-to-all-start = ((s32[8,1,8]{2,1,0:T(1,128)}), s32[8,1,8]{2,1,0:T(1,128)S(1)}, u32[]{:S(2)}, u32[]{:S(2)}) async-start(s32[8,1,8]{2,1,0:T(1,128)} %broadcast_in_dim.9), calls=%async_computation | async-start | bytes 8192 | tf_op jit(solution)/shard_map/all_to_all | solution.py:536
  9.5 13.0 %copy-start = (f32[32,2048]{1,0:T(8,128)S(1)}, f32[32,2048]{1,0:T(8,128)}, u32[]{:S(2)}) copy-start(f32[32,2048]{1,0:T(8,128)} %before_ref.3) | copy-start | bytes 786436
  23.8 8.8 %all-to-all-start.1 = ((bf16[8,32,256]{2,1,0:T(8,128)(2,1)}), bf16[8,32,256]{2,1,0:T(8,128)(2,1)S(1)}, u32[]{:S(2)}, u32[]{:S(2)}) async-start(bf16[8,32,256]{2,1,0:T(8,128)(2,1)} %first.1), calls=%async_computation.1 | async-start | bytes 262144 | tf_op jit(solution)/shard_map/all_to_all | solution.py:536
  36.7 9.2 %all-to-all-start.2 = ((bf16[8,32,256]{2,1,0:T(8,128)(2,1)}), bf16[8,32,256]{2,1,0:T(8,128)(2,1)S(1)}, u32[]{:S(2)}, u32[]{:S(2)}) async-start(bf16[8,32,256]{2,1,0:T(8,128)(2,1)} %get-tuple-element.22), calls=%async_computation.2 | async-start | bytes 262144 | tf_op jit(solution)/shard_map/all_to_all | solution.py:536
  49.9 9.2 %all-to-all-start.3 = ((bf16[8,32,256]{2,1,0:T(8,128)(2,1)}), bf16[8,32,256]{2,1,0:T(8,128)(2,1)S(1)}, u32[]{:S(2)}, u32[]{:S(2)}) async-start(bf16[8,32,256]{2,1,0:T(8,128)(2,1)} %get-tuple-element.24), calls=%async_computation.3 | async-start | bytes 262144 | tf_op jit(solution)/shard_map/all_to_all | solution.py:536
  63.1 9.2 %all-to-all-start.4 = ((bf16[8,32,256]{2,1,0:T(8,128)(2,1)}), bf16[8,32,256]{2,1,0:T(8,128)(2,1)S(1)}, u32[]{:S(2)}, u32[]{:S(2)}) async-start(bf16[8,32,256]{2,1,0:T(8,128)(2,1)} %get-tuple-element.26), calls=%async_computation.4 | async-start | bytes 262144 | tf_op jit(solution)/shard_map/all_to_all | solution.py:536
  75.6 5.0 %collective-permute-start.1 = (bf16[32,2048]{1,0:T(8,128)(2,1)S(1)}, bf16[32,2048]{1,0:T(8,128)(2,1)S(1)}, u32[]{:S(2)}, u32[]{:S(2)}) collective-permute-start(bf16[32,2048]{1,0:T(8,128)(2,1)S(1)} %convert_element_type.3), channel_id=1, source_target_pairs={{0,2},{1,3},{2,0},{3,1},{4,6},{5,7},{6,4},{7,5},{8,10},{9,11},{10,... | collective-permute-start | bytes 393224 | tf_op jit(solution)/shard_map/ppermute | solution.py:541
  77.2 3.5 %collective-permute-start = (bf16[32,2048]{1,0:T(8,128)(2,1)S(1)}, bf16[32,2048]{1,0:T(8,128)(2,1)S(1)}, u32[]{:S(2)}, u32[]{:S(2)}) collective-permute-start(bf16[32,2048]{1,0:T(8,128)(2,1)S(1)} %convert_element_type.3), channel_id=1, source_target_pairs={{0,1},{1,0},{2,3},{3,2},{4,5},{5,4},{6,7},{7,6},{8,9},{9,8},{10,11... | collective-permute-start | bytes 393224 | tf_op jit(solution)/shard_map/ppermute | solution.py:541
  80.7 1.3 %collective-permute-start.2 = (bf16[32,2048]{1,0:T(8,128)(2,1)S(1)}, bf16[32,2048]{1,0:T(8,128)(2,1)S(1)}, u32[]{:S(2)}, u32[]{:S(2)}) collective-permute-start(bf16[32,2048]{1,0:T(8,128)(2,1)S(1)} %collective-permute-done.1.refs_1_), channel_id=1, source_target_pairs={{0,1},{1,0},{2,3},{3,2},{4,5},{5,4},{6,7},{7,6},{8,9},{9,8},{10,11... | collective-permute-start | bytes 393224 | tf_op jit(solution)/shard_map/ppermute | solution.py:541
  82.4 4.0 %collective-permute-start.3 = (f32[64,128]{1,0:T(8,128)S(1)}, f32[64,128]{1,0:T(8,128)S(1)}, u32[]{:S(2)}, u32[]{:S(2)}) collective-permute-start(f32[64,128]{1,0:T(8,128)S(1)} %get-tuple-element.28), channel_id=1, source_target_pairs={{0,4},{4,0},{8,12},{12,8},{16,20},{20,16},{24,28},{28,24},{1,5},{5... | collective-permute-start | bytes 98312 | tf_op jit(solution)/shard_map/ppermute | solution.py:541
  86.4 5.9 %collective-permute-start.6 = (f32[64,128]{1,0:T(8,128)S(1)}, f32[64,128]{1,0:T(8,128)S(1)}, u32[]{:S(2)}, u32[]{:S(2)}) collective-permute-start(f32[64,128]{1,0:T(8,128)S(1)} %add.3.refs_0_), channel_id=1, source_target_pairs={{0,24},{4,28},{8,16},{12,20},{16,8},{20,12},{24,0},{28,4},{1,25},{... | collective-permute-start | bytes 98312 | tf_op jit(solution)/shard_map/ppermute | solution.py:541
  88.6 5.0 %collective-permute-start.5 = (f32[64,128]{1,0:T(8,128)S(1)}, f32[64,128]{1,0:T(8,128)S(1)}, u32[]{:S(2)}, u32[]{:S(2)}) collective-permute-start(f32[64,128]{1,0:T(8,128)S(1)} %add.3.refs_0_), channel_id=1, source_target_pairs={{0,16},{4,20},{8,24},{12,28},{16,0},{20,4},{24,8},{28,12},{1,17},{... | collective-permute-start | bytes 98312 | tf_op jit(solution)/shard_map/ppermute | solution.py:541
  88.9 4.6 %collective-permute-start.4 = (f32[64,128]{1,0:T(8,128)S(1)}, f32[64,128]{1,0:T(8,128)S(1)}, u32[]{:S(2)}, u32[]{:S(2)}) collective-permute-start(f32[64,128]{1,0:T(8,128)S(1)} %add.3.refs_0_), channel_id=1, source_target_pairs={{0,8},{4,12},{8,0},{12,4},{16,24},{20,28},{24,16},{28,20},{1,9},{5... | collective-permute-start | bytes 98312 | tf_op jit(solution)/shard_map/ppermute | solution.py:541

commit v24 on v23

--- a/solution.py
+++ b/solution.py
@@ -107,7 +107,8 @@
     )
     for copy in lists:
         copy.start()
-    for c in range(chunks):
+    first_far = near_count // CHUNK
+    for c in [*range(first_far, chunks), *range(first_far)]:
         for copy in copies(c):
             copy.start()
 
@@ -135,7 +136,7 @@
             entries = entries + jnp.where(joins, 0, 1)
         return entries
 
-    entries = lax.fori_loop(near_count // CHUNK, chunks, link, 0)
+    entries = lax.fori_loop(first_far, chunks, link, 0)
 
     def fill(ref, e, t):
         for at in [slice(q, q + 128) for q in range(0, 2 * order, 128)]:
@@ -198,8 +199,8 @@
 
     every = entries + short
     plan_ref[tiles] = every // UNROLL
-    lax.fori_loop(0, near_count // CHUNK, near_chunk, 0)
-    lax.fori_loop(near_count // CHUNK, chunks, far_chunk, 0)
+    lax.fori_loop(first_far, chunks, far_chunk, 0)
+    lax.fori_loop(0, first_far, near_chunk, 0)
     plan_copy = pltpu.make_async_copy(plan_ref, plan_hbm, list_sems.at[2])
     plan_copy.start()
 

time: 99.2 us -> 98.1 us (0.989)
  Pallas kernels: 49.8 us -> 47.1 us
  starting transfers between devices: 37.4 us -> 38.7 us
    pallas_call x1, Pallas kernels: 12.9 us -> 11.6 us  [tiles_call(): pl.pallas_call(functools.partial(tiles_kernel, near_count), name='tiles',...]
    pallas_call x4, Pallas kernels: 15.3 us -> 14 us  [per_device(): pl.pallas_call(functools.partial(step_kernel, step), name='step', out_sha...]
  transfers between devices with their start and end apart: 12 -> 12, of which waited for: 5 -> 5; matrix products, arithmetic and copies ran while one was open for 0% -> 0% of each run, Pallas kernels for 28% -> 27%
where the time goes in v24:
time: 98.1 us; the launch traced here: 97 us
  Pallas kernels  47.1 us (48%)
  starting transfers between devices  38.7 us (39%)
  waiting for transfers between devices  9.7 us (10%)
  local copies, waits for them, and re-layouts  1.25 us (1%)
    all_to_all x5, starting transfers between devices, exchange(): lax.all_to_all(x, 'blk', split_axis=0, concat_axis=0, tiled=True, axis_in...  30.6 us
    pallas_call x4, Pallas kernels, per_device(): pl.pallas_call(functools.partial(near_kernel, step), name='near', out_sha...  15 us
    pallas_call x4, Pallas kernels, per_device(): pl.pallas_call(functools.partial(step_kernel, step), name='step', out_sha...  14 us
    pallas_call x1, Pallas kernels, tiles_call(): pl.pallas_call(functools.partial(tiles_kernel, near_count), name='tiles',...  11.6 us
    ppermute x7, waiting for transfers between devices, to_partner(): return lax.ppermute(x, axis, [(i, i ^ mask) for i in range(n)])  9.69 us
    ppermute x7, starting transfers between devices, to_partner(): return lax.ppermute(x, axis, [(i, i ^ mask) for i in range(n)])  8.11 us
    pallas_call x1, Pallas kernels, per_device(): pl.pallas_call(functools.partial(factor_kernel, rows * nblk), name='facto...  4.79 us
  transfers between devices with their start and end apart: 12, of which 5 were waited for; matrix products, arithmetic and copies ran while one was open for 0% of the time, Pallas kernels for 27%

profile of v24, /device:TPU:0, one launch (start us, length us, event | category | flops | bytes accessed | tf_op | source)
XLA Modules:
  0.0 97.0 jit_solution(10555996895809306163)
XLA Ops:
  1.2 8.2 %all-to-all-start = ((s32[8,1,8]{2,1,0:T(1,128)}), s32[8,1,8]{2,1,0:T(1,128)S(1)}, u32[]{:S(2)}, u32[]{:S(2)}) async-start(s32[8,1,8]{2,1,0:T(1,128)} %broadcast_in_dim.9), calls=%async_computation | async-start | bytes 8192 | tf_op jit(solution)/shard_map/all_to_all | solution.py:537
  9.5 11.6 %tiles.1 = (f8e4m3fn[64,512,256]{2,1,0:T(32,128)(4,1)}, f8e4m3fn[16,512,256]{2,1,0:T(32,128)(4,1)S(1)}, f32[8,2048]{1,0:T(8,128)S(1)}, s32[128]{0:T(128)}) custom-call(s32[96]{0:T(128)} %rows_ref.7, s32[96]{0:T(128)} %slots_ref.7, bf16[96,256,256]{2,1,0:T(8,128)(2,1)} %real_hbm.9, bf16[96,256,256]{2,1,0:T(8,128)(2,1)} %imag_hbm.9), custom_call_target="tpu_custom_call" | custom-call | flops 268435456 | bytes 25165824 | tf_op jit(solution)/shard_map/tiles/pallas_call | solution.py:227
  21.1 1.3 %first.1 = bf16[8,32,256]{2,1,0:T(8,128)(2,1)} custom-call(f32[32,2048]{1,0:T(8,128)S(1)} %copy-done, f32[8,2048]{1,0:T(8,128)S(1)} %get-tuple-element.20.scale_ref, s32[8,1,8]{2,1,0:T(1,128)S(1)} %all-to-all-done.wanted_ref), custom_call_target="tpu_custom_call" | custom-call | tf_op jit(solution)/shard_map/first/pallas_call | solution.py:565
  22.4 5.1 %all-to-all-start.1 = ((bf16[8,32,256]{2,1,0:T(8,128)(2,1)}), bf16[8,32,256]{2,1,0:T(8,128)(2,1)S(1)}, u32[]{:S(2)}, u32[]{:S(2)}) async-start(bf16[8,32,256]{2,1,0:T(8,128)(2,1)} %first.1), calls=%async_computation.1 | async-start | bytes 262144 | tf_op jit(solution)/shard_map/all_to_all | solution.py:537
  27.6 3.7 %near.4.base_ref = f32[32,2048]{1,0:T(8,128)S(1)} custom-call(s32[96]{0:T(128)} %rows_ref.7, s32[96]{0:T(128)} %slots_ref.7, bf16[96,256,256]{2,1,0:T(8,128)(2,1)} %real_hbm.9, bf16[96,256,256]{2,1,0:T(8,128)(2,1)} %imag_hbm.9, f32[8,2048]{1,0:T(8,128)S(1)} %get-tuple-element.20.scale_ref, f32[32,2048]{1,0:T(8,128)S(1)} %copy-done, f32[32,2048]{1,0:T(8,128)S(1)} %copy-done), custom_call_target="tpu_custom_call" | custom-call | flops 268435456 | bytes 2097152 | tf_op jit(solution)/shard_map/near/pallas_call | solution.py:579
  31.3 3.7 %step.4 = (f32[32,2048]{1,0:T(8,128)S(1)}, bf16[8,32,256]{2,1,0:T(8,128)(2,1)}) custom-call(s32[128]{0:T(128)} %get-tuple-element.17.plan_ref, s32[8,1,8]{2,1,0:T(1,128)S(1)} %all-to-all-done.wanted_ref, f8e4m3fn[64,512,256]{2,1,0:T(32,128)(4,1)} %get-tuple-element.18.packed_hbm, f8e4m3fn[16,512,256]{2,1,0:T(32,128)(4,1)S(1)} %get-tuple-element.19.kept_ref, ...), custom_call_target="tpu_custom_call" | custom-call | tf_op jit(solution)/shard_map/step/pallas_call | solution.py:595
  35.0 5.8 %all-to-all-start.2 = ((bf16[8,32,256]{2,1,0:T(8,128)(2,1)}), bf16[8,32,256]{2,1,0:T(8,128)(2,1)S(1)}, u32[]{:S(2)}, u32[]{:S(2)}) async-start(bf16[8,32,256]{2,1,0:T(8,128)(2,1)} %get-tuple-element.22), calls=%async_computation.2 | async-start | bytes 262144 | tf_op jit(solution)/shard_map/all_to_all | solution.py:537
  40.8 3.7 %near.5.base_ref = f32[32,2048]{1,0:T(8,128)S(1)} custom-call(s32[96]{0:T(128)} %rows_ref.7, s32[96]{0:T(128)} %slots_ref.7, bf16[96,256,256]{2,1,0:T(8,128)(2,1)} %real_hbm.9, bf16[96,256,256]{2,1,0:T(8,128)(2,1)} %imag_hbm.9, f32[8,2048]{1,0:T(8,128)S(1)} %get-tuple-element.20.scale_ref, f32[32,2048]{1,0:T(8,128)S(1)} %get-tuple-element.21.now_ref.before_ref, ...), custom_call_target="tpu_custom_call" | custom-call | flops 268435456 | bytes 2097152 | tf_op jit(solution)/shard_map/near/pallas_call | solution.py:579
  44.5 3.7 %step.5 = (f32[32,2048]{1,0:T(8,128)S(1)}, bf16[8,32,256]{2,1,0:T(8,128)(2,1)}) custom-call(s32[128]{0:T(128)} %get-tuple-element.17.plan_ref, s32[8,1,8]{2,1,0:T(1,128)S(1)} %all-to-all-done.wanted_ref, f8e4m3fn[64,512,256]{2,1,0:T(32,128)(4,1)} %get-tuple-element.18.packed_hbm, f8e4m3fn[16,512,256]{2,1,0:T(32,128)(4,1)S(1)} %get-tuple-element.19.kept_ref, ...), custom_call_target="tpu_custom_call" | custom-call | tf_op jit(solution)/shard_map/step/pallas_call | solution.py:595
  48.2 5.7 %all-to-all-start.3 = ((bf16[8,32,256]{2,1,0:T(8,128)(2,1)}), bf16[8,32,256]{2,1,0:T(8,128)(2,1)S(1)}, u32[]{:S(2)}, u32[]{:S(2)}) async-start(bf16[8,32,256]{2,1,0:T(8,128)(2,1)} %get-tuple-element.24), calls=%async_computation.3 | async-start | bytes 262144 | tf_op jit(solution)/shard_map/all_to_all | solution.py:537
  54.0 3.8 %near.6.base_ref = f32[32,2048]{1,0:T(8,128)S(1)} custom-call(s32[96]{0:T(128)} %rows_ref.7, s32[96]{0:T(128)} %slots_ref.7, bf16[96,256,256]{2,1,0:T(8,128)(2,1)} %real_hbm.9, bf16[96,256,256]{2,1,0:T(8,128)(2,1)} %imag_hbm.9, f32[8,2048]{1,0:T(8,128)S(1)} %get-tuple-element.20.scale_ref, f32[32,2048]{1,0:T(8,128)S(1)} %get-tuple-element.23.now_ref.before_ref, ...), custom_call_target="tpu_custom_call" | custom-call | flops 268435456 | bytes 2097152 | tf_op jit(solution)/shard_map/near/pallas_call | solution.py:579
  57.7 3.7 %step.6 = (f32[32,2048]{1,0:T(8,128)S(1)}, bf16[8,32,256]{2,1,0:T(8,128)(2,1)}) custom-call(s32[128]{0:T(128)} %get-tuple-element.17.plan_ref, s32[8,1,8]{2,1,0:T(1,128)S(1)} %all-to-all-done.wanted_ref, f8e4m3fn[64,512,256]{2,1,0:T(32,128)(4,1)} %get-tuple-element.18.packed_hbm, f8e4m3fn[16,512,256]{2,1,0:T(32,128)(4,1)S(1)} %get-tuple-element.19.kept_ref, ...), custom_call_target="tpu_custom_call" | custom-call | tf_op jit(solution)/shard_map/step/pallas_call | solution.py:595
  61.4 5.7 %all-to-all-start.4 = ((bf16[8,32,256]{2,1,0:T(8,128)(2,1)}), bf16[8,32,256]{2,1,0:T(8,128)(2,1)S(1)}, u32[]{:S(2)}, u32[]{:S(2)}) async-start(bf16[8,32,256]{2,1,0:T(8,128)(2,1)} %get-tuple-element.26), calls=%async_computation.4 | async-start | bytes 262144 | tf_op jit(solution)/shard_map/all_to_all | solution.py:537
  67.2 3.8 %near.7.base_ref = f32[32,2048]{1,0:T(8,128)S(1)} custom-call(s32[96]{0:T(128)} %rows_ref.7, s32[96]{0:T(128)} %slots_ref.7, bf16[96,256,256]{2,1,0:T(8,128)(2,1)} %real_hbm.9, bf16[96,256,256]{2,1,0:T(8,128)(2,1)} %imag_hbm.9, f32[8,2048]{1,0:T(8,128)S(1)} %get-tuple-element.20.scale_ref, f32[32,2048]{1,0:T(8,128)S(1)} %get-tuple-element.25.now_ref, ...), custom_call_target="tpu_custom_call" | custom-call | flops 268435456 | bytes 2097152 | tf_op jit(solution)/shard_map/near/pallas_call | solution.py:579
  70.9 3.0 %step.7.own_ref = f32[32,2048]{1,0:T(8,128)S(1)} custom-call(s32[128]{0:T(128)} %get-tuple-element.17.plan_ref, s32[8,1,8]{2,1,0:T(1,128)S(1)} %all-to-all-done.wanted_ref, f8e4m3fn[64,512,256]{2,1,0:T(32,128)(4,1)} %get-tuple-element.18.packed_hbm, f8e4m3fn[16,512,256]{2,1,0:T(32,128)(4,1)S(1)} %get-tuple-element.19.kept_ref, ...), custom_call_target="tpu_custom_call" | custom-call | tf_op jit(solution)/shard_map/step/pallas_call | solution.py:595
  73.9 1.6 %collective-permute-start.1 = (bf16[32,2048]{1,0:T(8,128)(2,1)S(1)}, bf16[32,2048]{1,0:T(8,128)(2,1)S(1)}, u32[]{:S(2)}, u32[]{:S(2)}) collective-permute-start(bf16[32,2048]{1,0:T(8,128)(2,1)S(1)} %convert_element_type.3), channel_id=1, source_target_pairs={{0,2},{1,3},{2,0},{3,1},{4,6},{5,7},{6,4},{7,5},{8,10},{9,11},{10,... | collective-permute-start | bytes 393224 | tf_op jit(solution)/shard_map/ppermute | solution.py:542
  75.5 3.5 %collective-permute-done.1.refs_1_ = bf16[32,2048]{1,0:T(8,128)(2,1)S(1)} collective-permute-done((bf16[32,2048]{1,0:T(8,128)(2,1)S(1)}, bf16[32,2048]{1,0:T(8,128)(2,1)S(1)}, u32[]{:S(2)}, u32[]{:S(2)}) %collective-permute-start.1) | collective-permute-done | bytes 131104 | tf_op jit(solution)/shard_map/ppermute | solution.py:542
  79.0 1.3 %collective-permute-done.2.refs_2_ = bf16[32,2048]{1,0:T(8,128)(2,1)S(1)} collective-permute-done((bf16[32,2048]{1,0:T(8,128)(2,1)S(1)}, bf16[32,2048]{1,0:T(8,128)(2,1)S(1)}, u32[]{:S(2)}, u32[]{:S(2)}) %collective-permute-start.2) | collective-permute-done | bytes 131104 | tf_op jit(solution)/shard_map/ppermute | solution.py:542
  80.8 2.2 %collective-permute-start.3 = (f32[64,128]{1,0:T(8,128)S(1)}, f32[64,128]{1,0:T(8,128)S(1)}, u32[]{:S(2)}, u32[]{:S(2)}) collective-permute-start(f32[64,128]{1,0:T(8,128)S(1)} %get-tuple-element.28), channel_id=1, source_target_pairs={{0,4},{4,0},{8,12},{12,8},{16,20},{20,16},{24,28},{28,24},{1,5},{5... | collective-permute-start | bytes 98312 | tf_op jit(solution)/shard_map/ppermute | solution.py:542
  82.9 1.9 %collective-permute-done.3 = f32[64,128]{1,0:T(8,128)S(1)} collective-permute-done((f32[64,128]{1,0:T(8,128)S(1)}, f32[64,128]{1,0:T(8,128)S(1)}, u32[]{:S(2)}, u32[]{:S(2)}) %collective-permute-start.3) | collective-permute-done | bytes 32800 | tf_op jit(solution)/shard_map/ppermute | solution.py:542
  84.8 2.4 %collective-permute-start.6 = (f32[64,128]{1,0:T(8,128)S(1)}, f32[64,128]{1,0:T(8,128)S(1)}, u32[]{:S(2)}, u32[]{:S(2)}) collective-permute-start(f32[64,128]{1,0:T(8,128)S(1)} %add.3.refs_0_), channel_id=1, source_target_pairs={{0,24},{4,28},{8,16},{12,20},{16,8},{20,12},{24,0},{28,4},{1,25},{... | collective-permute-start | bytes 98312 | tf_op jit(solution)/shard_map/ppermute | solution.py:542
  87.6 1.6 %collective-permute-start.4 = (f32[64,128]{1,0:T(8,128)S(1)}, f32[64,128]{1,0:T(8,128)S(1)}, u32[]{:S(2)}, u32[]{:S(2)}) collective-permute-start(f32[64,128]{1,0:T(8,128)S(1)} %add.3.refs_0_), channel_id=1, source_target_pairs={{0,8},{4,12},{8,0},{12,4},{16,24},{20,28},{24,16},{28,20},{1,9},{5... | collective-permute-start | bytes 98312 | tf_op jit(solution)/shard_map/ppermute | solution.py:542
  90.5 1.6 %collective-permute-done.5.refs_2_ = f32[64,128]{1,0:T(8,128)S(1)} collective-permute-done((f32[64,128]{1,0:T(8,128)S(1)}, f32[64,128]{1,0:T(8,128)S(1)}, u32[]{:S(2)}, u32[]{:S(2)}) %collective-permute-start.5) | collective-permute-done | bytes 32800 | tf_op jit(solution)/shard_map/ppermute | solution.py:542
  92.2 4.8 %factor.1 = f32[32,2048]{1,0:T(8,128)} custom-call(f32[32,2048]{1,0:T(8,128)S(1)} %step.7.own_ref, bf16[4,32,2048]{2,1,0:T(8,128)(2,1)S(1)} %get-tuple-element.27.all_ref, f32[64,128]{1,0:T(8,128)S(1)} %add.3.refs_0_, f32[64,128]{1,0:T(8,128)S(1)} %collective-permute-done.4.refs_1_, f32[64,128]{1,0:T(8,128)S(1)} %collective-permute-done.5.refs_2_, ...), custom_call_target="tpu_custom_call" | custom-call | tf_op jit(solution)/shard_map/factor/pallas_call | solution.py:631
  (17 shorter events, 3.4 us)
Async XLA Ops:
  1.2 19.8 %all-to-all-start = ((s32[8,1,8]{2,1,0:T(1,128)}), s32[8,1,8]{2,1,0:T(1,128)S(1)}, u32[]{:S(2)}, u32[]{:S(2)}) async-start(s32[8,1,8]{2,1,0:T(1,128)} %broadcast_in_dim.9), calls=%async_computation | async-start | bytes 8192 | tf_op jit(solution)/shard_map/all_to_all | solution.py:537
  9.5 11.6 %copy-start = (f32[32,2048]{1,0:T(8,128)S(1)}, f32[32,2048]{1,0:T(8,128)}, u32[]{:S(2)}) copy-start(f32[32,2048]{1,0:T(8,128)} %before_ref.3) | copy-start | bytes 786436
  22.4 8.8 %all-to-all-start.1 = ((bf16[8,32,256]{2,1,0:T(8,128)(2,1)}), bf16[8,32,256]{2,1,0:T(8,128)(2,1)S(1)}, u32[]{:S(2)}, u32[]{:S(2)}) async-start(bf16[8,32,256]{2,1,0:T(8,128)(2,1)} %first.1), calls=%async_computation.1 | async-start | bytes 262144 | tf_op jit(solution)/shard_map/all_to_all | solution.py:537
  35.0 9.5 %all-to-all-start.2 = ((bf16[8,32,256]{2,1,0:T(8,128)(2,1)}), bf16[8,32,256]{2,1,0:T(8,128)(2,1)S(1)}, u32[]{:S(2)}, u32[]{:S(2)}) async-start(bf16[8,32,256]{2,1,0:T(8,128)(2,1)} %get-tuple-element.22), calls=%async_computation.2 | async-start | bytes 262144 | tf_op jit(solution)/shard_map/all_to_all | solution.py:537
  48.2 9.5 %all-to-all-start.3 = ((bf16[8,32,256]{2,1,0:T(8,128)(2,1)}), bf16[8,32,256]{2,1,0:T(8,128)(2,1)S(1)}, u32[]{:S(2)}, u32[]{:S(2)}) async-start(bf16[8,32,256]{2,1,0:T(8,128)(2,1)} %get-tuple-element.24), calls=%async_computation.3 | async-start | bytes 262144 | tf_op jit(solution)/shard_map/all_to_all | solution.py:537
  61.4 9.5 %all-to-all-start.4 = ((bf16[8,32,256]{2,1,0:T(8,128)(2,1)}), bf16[8,32,256]{2,1,0:T(8,128)(2,1)S(1)}, u32[]{:S(2)}, u32[]{:S(2)}) async-start(bf16[8,32,256]{2,1,0:T(8,128)(2,1)} %get-tuple-element.26), calls=%async_computation.4 | async-start | bytes 262144 | tf_op jit(solution)/shard_map/all_to_all | solution.py:537
  73.9 5.0 %collective-permute-start.1 = (bf16[32,2048]{1,0:T(8,128)(2,1)S(1)}, bf16[32,2048]{1,0:T(8,128)(2,1)S(1)}, u32[]{:S(2)}, u32[]{:S(2)}) collective-permute-start(bf16[32,2048]{1,0:T(8,128)(2,1)S(1)} %convert_element_type.3), channel_id=1, source_target_pairs={{0,2},{1,3},{2,0},{3,1},{4,6},{5,7},{6,4},{7,5},{8,10},{9,11},{10,... | collective-permute-start | bytes 393224 | tf_op jit(solution)/shard_map/ppermute | solution.py:542
  75.5 3.5 %collective-permute-start = (bf16[32,2048]{1,0:T(8,128)(2,1)S(1)}, bf16[32,2048]{1,0:T(8,128)(2,1)S(1)}, u32[]{:S(2)}, u32[]{:S(2)}) collective-permute-start(bf16[32,2048]{1,0:T(8,128)(2,1)S(1)} %convert_element_type.3), channel_id=1, source_target_pairs={{0,1},{1,0},{2,3},{3,2},{4,5},{5,4},{6,7},{7,6},{8,9},{9,8},{10,11... | collective-permute-start | bytes 393224 | tf_op jit(solution)/shard_map/ppermute | solution.py:542
  79.0 1.3 %collective-permute-start.2 = (bf16[32,2048]{1,0:T(8,128)(2,1)S(1)}, bf16[32,2048]{1,0:T(8,128)(2,1)S(1)}, u32[]{:S(2)}, u32[]{:S(2)}) collective-permute-start(bf16[32,2048]{1,0:T(8,128)(2,1)S(1)} %collective-permute-done.1.refs_1_), channel_id=1, source_target_pairs={{0,1},{1,0},{2,3},{3,2},{4,5},{5,4},{6,7},{7,6},{8,9},{9,8},{10,11... | collective-permute-start | bytes 393224 | tf_op jit(solution)/shard_map/ppermute | solution.py:542
  80.8 4.1 %collective-permute-start.3 = (f32[64,128]{1,0:T(8,128)S(1)}, f32[64,128]{1,0:T(8,128)S(1)}, u32[]{:S(2)}, u32[]{:S(2)}) collective-permute-start(f32[64,128]{1,0:T(8,128)S(1)} %get-tuple-element.28), channel_id=1, source_target_pairs={{0,4},{4,0},{8,12},{12,8},{16,20},{20,16},{24,28},{28,24},{1,5},{5... | collective-permute-start | bytes 98312 | tf_op jit(solution)/shard_map/ppermute | solution.py:542
  84.8 5.7 %collective-permute-start.6 = (f32[64,128]{1,0:T(8,128)S(1)}, f32[64,128]{1,0:T(8,128)S(1)}, u32[]{:S(2)}, u32[]{:S(2)}) collective-permute-start(f32[64,128]{1,0:T(8,128)S(1)} %add.3.refs_0_), channel_id=1, source_target_pairs={{0,24},{4,28},{8,16},{12,20},{16,8},{20,12},{24,0},{28,4},{1,25},{... | collective-permute-start | bytes 98312 | tf_op jit(solution)/shard_map/ppermute | solution.py:542
  87.2 5.0 %collective-permute-start.5 = (f32[64,128]{1,0:T(8,128)S(1)}, f32[64,128]{1,0:T(8,128)S(1)}, u32[]{:S(2)}, u32[]{:S(2)}) collective-permute-start(f32[64,128]{1,0:T(8,128)S(1)} %add.3.refs_0_), channel_id=1, source_target_pairs={{0,16},{4,20},{8,24},{12,28},{16,0},{20,4},{24,8},{28,12},{1,17},{... | collective-permute-start | bytes 98312 | tf_op jit(solution)/shard_map/ppermute | solution.py:542
  87.6 4.6 %collective-permute-start.4 = (f32[64,128]{1,0:T(8,128)S(1)}, f32[64,128]{1,0:T(8,128)S(1)}, u32[]{:S(2)}, u32[]{:S(2)}) collective-permute-start(f32[64,128]{1,0:T(8,128)S(1)} %add.3.refs_0_), channel_id=1, source_target_pairs={{0,8},{4,12},{8,0},{12,4},{16,24},{20,28},{24,16},{28,20},{1,9},{5... | collective-permute-start | bytes 98312 | tf_op jit(solution)/shard_map/ppermute | solution.py:542

commit v25 on v24

--- a/solution.py
+++ b/solution.py
@@ -528,7 +528,7 @@
 
 
 def central(nblk):
-    return nblk // 2 + nblk // 8
+    return nblk // 2
 
 
 def exchange(x):

time: 98.1 us -> 98.9 us (level)
  starting transfers between devices: 38.7 us -> 32.1 us
  waiting for transfers between devices: 9.7 us -> 16 us
  Pallas kernels: 47.1 us -> 48.8 us
    all_to_all x5, waiting for transfers between devices: 0.01 us -> 4.92 us  [exchange(): lax.all_to_all(x, 'blk', split_axis=0, concat_axis=0, tiled=True, axis_in...]
    all_to_all x5, starting transfers between devices: 30.6 us -> 25.8 us  [exchange(): lax.all_to_all(x, 'blk', split_axis=0, concat_axis=0, tiled=True, axis_in...]
    ppermute x7, starting transfers between devices: 8.11 us -> 6.26 us  [to_partner(): return lax.ppermute(x, axis, [(i, i ^ mask) for i in range(n)])]
    ppermute x7, waiting for transfers between devices: 9.69 us -> 11.1 us  [to_partner(): return lax.ppermute(x, axis, [(i, i ^ mask) for i in range(n)])]
    pallas_call x4, Pallas kernels: 14 us -> 15.3 us  [per_device(): pl.pallas_call(functools.partial(step_kernel, step), name='step', out_sha...]
  transfers between devices with their start and end apart: 12 -> 12, of which waited for: 5 -> 9; matrix products, arithmetic and copies ran while one was open for 0% -> 0% of each run, Pallas kernels for 27% -> 27%
where the time goes in v25:
time: 98.9 us; the launch traced here: 98.2 us
  Pallas kernels  48.8 us (49%)
  starting transfers between devices  32.1 us (32%)
  waiting for transfers between devices  16 us (16%)
  local copies, waits for them, and re-layouts  1.25 us (1%)
    all_to_all x5, starting transfers between devices, exchange(): lax.all_to_all(x, 'blk', split_axis=0, concat_axis=0, tiled=True, axis_in...  25.8 us
    pallas_call x4, Pallas kernels, per_device(): pl.pallas_call(functools.partial(step_kernel, step), name='step', out_sha...  15.3 us
    pallas_call x4, Pallas kernels, per_device(): pl.pallas_call(functools.partial(near_kernel, step), name='near', out_sha...  15 us
    pallas_call x1, Pallas kernels, tiles_call(): pl.pallas_call(functools.partial(tiles_kernel, near_count), name='tiles',...  11.9 us
    ppermute x7, waiting for transfers between devices, to_partner(): return lax.ppermute(x, axis, [(i, i ^ mask) for i in range(n)])  11.1 us
    ppermute x7, starting transfers between devices, to_partner(): return lax.ppermute(x, axis, [(i, i ^ mask) for i in range(n)])  6.26 us
    all_to_all x5, waiting for transfers between devices, exchange(): lax.all_to_all(x, 'blk', split_axis=0, concat_axis=0, tiled=True, axis_in...  4.92 us
    pallas_call x1, Pallas kernels, per_device(): pl.pallas_call(functools.partial(factor_kernel, rows * nblk), name='facto...  4.79 us
  transfers between devices with their start and end apart: 12, of which 9 were waited for; matrix products, arithmetic and copies ran while one was open for 0% of the time, Pallas kernels for 27%

profile of v25, /device:TPU:0, one launch (start us, length us, event | category | flops | bytes accessed | tf_op | source)
XLA Modules:
  0.0 98.2 jit_solution(6468710394593821083)
XLA Ops:
  0.0 1.2 %broadcast_in_dim.9 = s32[8,1,8]{2,1,0:T(1,128)} broadcast(s32[8]{0:T(128)} %bitcast.1), dimensions={2} | broadcast | bytes 288 | tf_op jit(solution)/shard_map/broadcast_in_dim | solution.py:560
  1.2 7.8 %all-to-all-start = ((s32[8,1,8]{2,1,0:T(1,128)}), s32[8,1,8]{2,1,0:T(1,128)S(1)}, u32[]{:S(2)}, u32[]{:S(2)}) async-start(s32[8,1,8]{2,1,0:T(1,128)} %broadcast_in_dim.9), calls=%async_computation | async-start | bytes 8192 | tf_op jit(solution)/shard_map/all_to_all | solution.py:537
  9.1 11.9 %tiles.1 = (f8e4m3fn[64,512,256]{2,1,0:T(32,128)(4,1)}, f8e4m3fn[16,512,256]{2,1,0:T(32,128)(4,1)S(1)}, f32[8,2048]{1,0:T(8,128)S(1)}, s32[128]{0:T(128)}) custom-call(s32[96]{0:T(128)} %rows_ref.7, s32[96]{0:T(128)} %slots_ref.7, bf16[96,256,256]{2,1,0:T(8,128)(2,1)} %real_hbm.9, bf16[96,256,256]{2,1,0:T(8,128)(2,1)} %imag_hbm.9), custom_call_target="tpu_custom_call" | custom-call | flops 268435456 | bytes 25165824 | tf_op jit(solution)/shard_map/tiles/pallas_call | solution.py:227
  21.1 1.3 %first.1 = bf16[8,32,256]{2,1,0:T(8,128)(2,1)} custom-call(f32[32,2048]{1,0:T(8,128)S(1)} %copy-done, f32[8,2048]{1,0:T(8,128)S(1)} %get-tuple-element.20.scale_ref, s32[8,1,8]{2,1,0:T(1,128)S(1)} %all-to-all-done.wanted_ref), custom_call_target="tpu_custom_call" | custom-call | tf_op jit(solution)/shard_map/first/pallas_call | solution.py:565
  22.4 5.3 %all-to-all-start.1 = ((bf16[8,32,256]{2,1,0:T(8,128)(2,1)}), bf16[8,32,256]{2,1,0:T(8,128)(2,1)S(1)}, u32[]{:S(2)}, u32[]{:S(2)}) async-start(bf16[8,32,256]{2,1,0:T(8,128)(2,1)} %first.1), calls=%async_computation.1 | async-start | bytes 262144 | tf_op jit(solution)/shard_map/all_to_all | solution.py:537
  27.7 3.7 %near.4.base_ref = f32[32,2048]{1,0:T(8,128)S(1)} custom-call(s32[96]{0:T(128)} %rows_ref.7, s32[96]{0:T(128)} %slots_ref.7, bf16[96,256,256]{2,1,0:T(8,128)(2,1)} %real_hbm.9, bf16[96,256,256]{2,1,0:T(8,128)(2,1)} %imag_hbm.9, f32[8,2048]{1,0:T(8,128)S(1)} %get-tuple-element.20.scale_ref, f32[32,2048]{1,0:T(8,128)S(1)} %copy-done, f32[32,2048]{1,0:T(8,128)S(1)} %copy-done), custom_call_target="tpu_custom_call" | custom-call | flops 268435456 | bytes 2097152 | tf_op jit(solution)/shard_map/near/pallas_call | solution.py:579
  32.7 4.0 %step.4 = (f32[32,2048]{1,0:T(8,128)S(1)}, bf16[8,32,256]{2,1,0:T(8,128)(2,1)}) custom-call(s32[128]{0:T(128)} %get-tuple-element.17.plan_ref, s32[8,1,8]{2,1,0:T(1,128)S(1)} %all-to-all-done.wanted_ref, f8e4m3fn[64,512,256]{2,1,0:T(32,128)(4,1)} %get-tuple-element.18.packed_hbm, f8e4m3fn[16,512,256]{2,1,0:T(32,128)(4,1)S(1)} %get-tuple-element.19.kept_ref, ...), custom_call_target="tpu_custom_call" | custom-call | tf_op jit(solution)/shard_map/step/pallas_call | solution.py:595
  36.7 4.2 %all-to-all-start.2 = ((bf16[8,32,256]{2,1,0:T(8,128)(2,1)}), bf16[8,32,256]{2,1,0:T(8,128)(2,1)S(1)}, u32[]{:S(2)}, u32[]{:S(2)}) async-start(bf16[8,32,256]{2,1,0:T(8,128)(2,1)} %get-tuple-element.22), calls=%async_computation.2 | async-start | bytes 262144 | tf_op jit(solution)/shard_map/all_to_all | solution.py:537
  40.9 3.8 %near.5.base_ref = f32[32,2048]{1,0:T(8,128)S(1)} custom-call(s32[96]{0:T(128)} %rows_ref.7, s32[96]{0:T(128)} %slots_ref.7, bf16[96,256,256]{2,1,0:T(8,128)(2,1)} %real_hbm.9, bf16[96,256,256]{2,1,0:T(8,128)(2,1)} %imag_hbm.9, f32[8,2048]{1,0:T(8,128)S(1)} %get-tuple-element.20.scale_ref, f32[32,2048]{1,0:T(8,128)S(1)} %get-tuple-element.21.now_ref.before_ref, ...), custom_call_target="tpu_custom_call" | custom-call | flops 268435456 | bytes 2097152 | tf_op jit(solution)/shard_map/near/pallas_call | solution.py:579
  45.9 4.0 %step.5 = (f32[32,2048]{1,0:T(8,128)S(1)}, bf16[8,32,256]{2,1,0:T(8,128)(2,1)}) custom-call(s32[128]{0:T(128)} %get-tuple-element.17.plan_ref, s32[8,1,8]{2,1,0:T(1,128)S(1)} %all-to-all-done.wanted_ref, f8e4m3fn[64,512,256]{2,1,0:T(32,128)(4,1)} %get-tuple-element.18.packed_hbm, f8e4m3fn[16,512,256]{2,1,0:T(32,128)(4,1)S(1)} %get-tuple-element.19.kept_ref, ...), custom_call_target="tpu_custom_call" | custom-call | tf_op jit(solution)/shard_map/step/pallas_call | solution.py:595
  49.9 4.2 %all-to-all-start.3 = ((bf16[8,32,256]{2,1,0:T(8,128)(2,1)}), bf16[8,32,256]{2,1,0:T(8,128)(2,1)S(1)}, u32[]{:S(2)}, u32[]{:S(2)}) async-start(bf16[8,32,256]{2,1,0:T(8,128)(2,1)} %get-tuple-element.24), calls=%async_computation.3 | async-start | bytes 262144 | tf_op jit(solution)/shard_map/all_to_all | solution.py:537
  54.1 3.8 %near.6.base_ref = f32[32,2048]{1,0:T(8,128)S(1)} custom-call(s32[96]{0:T(128)} %rows_ref.7, s32[96]{0:T(128)} %slots_ref.7, bf16[96,256,256]{2,1,0:T(8,128)(2,1)} %real_hbm.9, bf16[96,256,256]{2,1,0:T(8,128)(2,1)} %imag_hbm.9, f32[8,2048]{1,0:T(8,128)S(1)} %get-tuple-element.20.scale_ref, f32[32,2048]{1,0:T(8,128)S(1)} %get-tuple-element.23.now_ref.before_ref, ...), custom_call_target="tpu_custom_call" | custom-call | flops 268435456 | bytes 2097152 | tf_op jit(solution)/shard_map/near/pallas_call | solution.py:579
  59.1 4.0 %step.6 = (f32[32,2048]{1,0:T(8,128)S(1)}, bf16[8,32,256]{2,1,0:T(8,128)(2,1)}) custom-call(s32[128]{0:T(128)} %get-tuple-element.17.plan_ref, s32[8,1,8]{2,1,0:T(1,128)S(1)} %all-to-all-done.wanted_ref, f8e4m3fn[64,512,256]{2,1,0:T(32,128)(4,1)} %get-tuple-element.18.packed_hbm, f8e4m3fn[16,512,256]{2,1,0:T(32,128)(4,1)S(1)} %get-tuple-element.19.kept_ref, ...), custom_call_target="tpu_custom_call" | custom-call | tf_op jit(solution)/shard_map/step/pallas_call | solution.py:595
  63.1 4.2 %all-to-all-start.4 = ((bf16[8,32,256]{2,1,0:T(8,128)(2,1)}), bf16[8,32,256]{2,1,0:T(8,128)(2,1)S(1)}, u32[]{:S(2)}, u32[]{:S(2)}) async-start(bf16[8,32,256]{2,1,0:T(8,128)(2,1)} %get-tuple-element.26), calls=%async_computation.4 | async-start | bytes 262144 | tf_op jit(solution)/shard_map/all_to_all | solution.py:537
  67.4 3.8 %near.7.base_ref = f32[32,2048]{1,0:T(8,128)S(1)} custom-call(s32[96]{0:T(128)} %rows_ref.7, s32[96]{0:T(128)} %slots_ref.7, bf16[96,256,256]{2,1,0:T(8,128)(2,1)} %real_hbm.9, bf16[96,256,256]{2,1,0:T(8,128)(2,1)} %imag_hbm.9, f32[8,2048]{1,0:T(8,128)S(1)} %get-tuple-element.20.scale_ref, f32[32,2048]{1,0:T(8,128)S(1)} %get-tuple-element.25.now_ref, ...), custom_call_target="tpu_custom_call" | custom-call | flops 268435456 | bytes 2097152 | tf_op jit(solution)/shard_map/near/pallas_call | solution.py:579
  72.3 3.3 %step.7.own_ref = f32[32,2048]{1,0:T(8,128)S(1)} custom-call(s32[128]{0:T(128)} %get-tuple-element.17.plan_ref, s32[8,1,8]{2,1,0:T(1,128)S(1)} %all-to-all-done.wanted_ref, f8e4m3fn[64,512,256]{2,1,0:T(32,128)(4,1)} %get-tuple-element.18.packed_hbm, f8e4m3fn[16,512,256]{2,1,0:T(32,128)(4,1)S(1)} %get-tuple-element.19.kept_ref, ...), custom_call_target="tpu_custom_call" | custom-call | tf_op jit(solution)/shard_map/step/pallas_call | solution.py:595
  75.7 1.6 %collective-permute-start.1 = (bf16[32,2048]{1,0:T(8,128)(2,1)S(1)}, bf16[32,2048]{1,0:T(8,128)(2,1)S(1)}, u32[]{:S(2)}, u32[]{:S(2)}) collective-permute-start(bf16[32,2048]{1,0:T(8,128)(2,1)S(1)} %convert_element_type.3), channel_id=1, source_target_pairs={{0,2},{1,3},{2,0},{3,1},{4,6},{5,7},{6,4},{7,5},{8,10},{9,11},{10,... | collective-permute-start | bytes 393224 | tf_op jit(solution)/shard_map/ppermute | solution.py:542
  77.2 3.5 %collective-permute-done.1.refs_1_ = bf16[32,2048]{1,0:T(8,128)(2,1)S(1)} collective-permute-done((bf16[32,2048]{1,0:T(8,128)(2,1)S(1)}, bf16[32,2048]{1,0:T(8,128)(2,1)S(1)}, u32[]{:S(2)}, u32[]{:S(2)}) %collective-permute-start.1) | collective-permute-done | bytes 131104 | tf_op jit(solution)/shard_map/ppermute | solution.py:542
  80.7 1.3 %collective-permute-done.2.refs_2_ = bf16[32,2048]{1,0:T(8,128)(2,1)S(1)} collective-permute-done((bf16[32,2048]{1,0:T(8,128)(2,1)S(1)}, bf16[32,2048]{1,0:T(8,128)(2,1)S(1)}, u32[]{:S(2)}, u32[]{:S(2)}) %collective-permute-start.2) | collective-permute-done | bytes 131104 | tf_op jit(solution)/shard_map/ppermute | solution.py:542
  82.8 3.7 %collective-permute-done.3 = f32[64,128]{1,0:T(8,128)S(1)} collective-permute-done((f32[64,128]{1,0:T(8,128)S(1)}, f32[64,128]{1,0:T(8,128)S(1)}, u32[]{:S(2)}, u32[]{:S(2)}) %collective-permute-start.3) | collective-permute-done | bytes 32800 | tf_op jit(solution)/shard_map/ppermute | solution.py:542
  86.5 2.2 %collective-permute-start.6 = (f32[64,128]{1,0:T(8,128)S(1)}, f32[64,128]{1,0:T(8,128)S(1)}, u32[]{:S(2)}, u32[]{:S(2)}) collective-permute-start(f32[64,128]{1,0:T(8,128)S(1)} %add.3.refs_0_), channel_id=1, source_target_pairs={{0,24},{4,28},{8,16},{12,20},{16,8},{20,12},{24,0},{28,4},{1,25},{... | collective-permute-start | bytes 98312 | tf_op jit(solution)/shard_map/ppermute | solution.py:542
  88.6 2.2 %collective-permute-start.4 = (f32[64,128]{1,0:T(8,128)S(1)}, f32[64,128]{1,0:T(8,128)S(1)}, u32[]{:S(2)}, u32[]{:S(2)}) collective-permute-start(f32[64,128]{1,0:T(8,128)S(1)} %add.3.refs_0_), channel_id=1, source_target_pairs={{0,8},{4,12},{8,0},{12,4},{16,24},{20,28},{24,16},{28,20},{1,9},{5... | collective-permute-start | bytes 98312 | tf_op jit(solution)/shard_map/ppermute | solution.py:542
  90.8 1.4 %collective-permute-done.6.refs_3_ = f32[64,128]{1,0:T(8,128)S(1)} collective-permute-done((f32[64,128]{1,0:T(8,128)S(1)}, f32[64,128]{1,0:T(8,128)S(1)}, u32[]{:S(2)}, u32[]{:S(2)}) %collective-permute-start.6) | collective-permute-done | bytes 32800 | tf_op jit(solution)/shard_map/ppermute | solution.py:542
  93.5 4.8 %factor.1 = f32[32,2048]{1,0:T(8,128)} custom-call(f32[32,2048]{1,0:T(8,128)S(1)} %step.7.own_ref, bf16[4,32,2048]{2,1,0:T(8,128)(2,1)S(1)} %get-tuple-element.27.all_ref, f32[64,128]{1,0:T(8,128)S(1)} %add.3.refs_0_, f32[64,128]{1,0:T(8,128)S(1)} %collective-permute-done.4.refs_1_, f32[64,128]{1,0:T(8,128)S(1)} %collective-permute-done.5.refs_2_, ...), custom_call_target="tpu_custom_call" | custom-call | tf_op jit(solution)/shard_map/factor/pallas_call | solution.py:631
  (17 shorter events, 6.9 us)
Async XLA Ops:
  1.2 19.8 %all-to-all-start = ((s32[8,1,8]{2,1,0:T(1,128)}), s32[8,1,8]{2,1,0:T(1,128)S(1)}, u32[]{:S(2)}, u32[]{:S(2)}) async-start(s32[8,1,8]{2,1,0:T(1,128)} %broadcast_in_dim.9), calls=%async_computation | async-start | bytes 8192 | tf_op jit(solution)/shard_map/all_to_all | solution.py:537
  9.1 12.0 %copy-start = (f32[32,2048]{1,0:T(8,128)S(1)}, f32[32,2048]{1,0:T(8,128)}, u32[]{:S(2)}) copy-start(f32[32,2048]{1,0:T(8,128)} %before_ref.3) | copy-start | bytes 786436
  22.4 10.3 %all-to-all-start.1 = ((bf16[8,32,256]{2,1,0:T(8,128)(2,1)}), bf16[8,32,256]{2,1,0:T(8,128)(2,1)S(1)}, u32[]{:S(2)}, u32[]{:S(2)}) async-start(bf16[8,32,256]{2,1,0:T(8,128)(2,1)} %first.1), calls=%async_computation.1 | async-start | bytes 262144 | tf_op jit(solution)/shard_map/all_to_all | solution.py:537
  36.7 9.2 %all-to-all-start.2 = ((bf16[8,32,256]{2,1,0:T(8,128)(2,1)}), bf16[8,32,256]{2,1,0:T(8,128)(2,1)S(1)}, u32[]{:S(2)}, u32[]{:S(2)}) async-start(bf16[8,32,256]{2,1,0:T(8,128)(2,1)} %get-tuple-element.22), calls=%async_computation.2 | async-start | bytes 262144 | tf_op jit(solution)/shard_map/all_to_all | solution.py:537
  49.9 9.2 %all-to-all-start.3 = ((bf16[8,32,256]{2,1,0:T(8,128)(2,1)}), bf16[8,32,256]{2,1,0:T(8,128)(2,1)S(1)}, u32[]{:S(2)}, u32[]{:S(2)}) async-start(bf16[8,32,256]{2,1,0:T(8,128)(2,1)} %get-tuple-element.24), calls=%async_computation.3 | async-start | bytes 262144 | tf_op jit(solution)/shard_map/all_to_all | solution.py:537
  63.1 9.2 %all-to-all-start.4 = ((bf16[8,32,256]{2,1,0:T(8,128)(2,1)}), bf16[8,32,256]{2,1,0:T(8,128)(2,1)S(1)}, u32[]{:S(2)}, u32[]{:S(2)}) async-start(bf16[8,32,256]{2,1,0:T(8,128)(2,1)} %get-tuple-element.26), calls=%async_computation.4 | async-start | bytes 262144 | tf_op jit(solution)/shard_map/all_to_all | solution.py:537
  75.7 5.0 %collective-permute-start.1 = (bf16[32,2048]{1,0:T(8,128)(2,1)S(1)}, bf16[32,2048]{1,0:T(8,128)(2,1)S(1)}, u32[]{:S(2)}, u32[]{:S(2)}) collective-permute-start(bf16[32,2048]{1,0:T(8,128)(2,1)S(1)} %convert_element_type.3), channel_id=1, source_target_pairs={{0,2},{1,3},{2,0},{3,1},{4,6},{5,7},{6,4},{7,5},{8,10},{9,11},{10,... | collective-permute-start | bytes 393224 | tf_op jit(solution)/shard_map/ppermute | solution.py:542
  77.2 3.5 %collective-permute-start = (bf16[32,2048]{1,0:T(8,128)(2,1)S(1)}, bf16[32,2048]{1,0:T(8,128)(2,1)S(1)}, u32[]{:S(2)}, u32[]{:S(2)}) collective-permute-start(bf16[32,2048]{1,0:T(8,128)(2,1)S(1)} %convert_element_type.3), channel_id=1, source_target_pairs={{0,1},{1,0},{2,3},{3,2},{4,5},{5,4},{6,7},{7,6},{8,9},{9,8},{10,11... | collective-permute-start | bytes 393224 | tf_op jit(solution)/shard_map/ppermute | solution.py:542
  80.7 1.3 %collective-permute-start.2 = (bf16[32,2048]{1,0:T(8,128)(2,1)S(1)}, bf16[32,2048]{1,0:T(8,128)(2,1)S(1)}, u32[]{:S(2)}, u32[]{:S(2)}) collective-permute-start(bf16[32,2048]{1,0:T(8,128)(2,1)S(1)} %collective-permute-done.1.refs_1_), channel_id=1, source_target_pairs={{0,1},{1,0},{2,3},{3,2},{4,5},{5,4},{6,7},{7,6},{8,9},{9,8},{10,11... | collective-permute-start | bytes 393224 | tf_op jit(solution)/shard_map/ppermute | solution.py:542
  82.5 4.0 %collective-permute-start.3 = (f32[64,128]{1,0:T(8,128)S(1)}, f32[64,128]{1,0:T(8,128)S(1)}, u32[]{:S(2)}, u32[]{:S(2)}) collective-permute-start(f32[64,128]{1,0:T(8,128)S(1)} %get-tuple-element.28), channel_id=1, source_target_pairs={{0,4},{4,0},{8,12},{12,8},{16,20},{20,16},{24,28},{28,24},{1,5},{5... | collective-permute-start | bytes 98312 | tf_op jit(solution)/shard_map/ppermute | solution.py:542
  86.5 5.8 %collective-permute-start.6 = (f32[64,128]{1,0:T(8,128)S(1)}, f32[64,128]{1,0:T(8,128)S(1)}, u32[]{:S(2)}, u32[]{:S(2)}) collective-permute-start(f32[64,128]{1,0:T(8,128)S(1)} %add.3.refs_0_), channel_id=1, source_target_pairs={{0,24},{4,28},{8,16},{12,20},{16,8},{20,12},{24,0},{28,4},{1,25},{... | collective-permute-start | bytes 98312 | tf_op jit(solution)/shard_map/ppermute | solution.py:542
  88.6 4.8 %collective-permute-start.5 = (f32[64,128]{1,0:T(8,128)S(1)}, f32[64,128]{1,0:T(8,128)S(1)}, u32[]{:S(2)}, u32[]{:S(2)}) collective-permute-start(f32[64,128]{1,0:T(8,128)S(1)} %add.3.refs_0_), channel_id=1, source_target_pairs={{0,16},{4,20},{8,24},{12,28},{16,0},{20,4},{24,8},{28,12},{1,17},{... | collective-permute-start | bytes 98312 | tf_op jit(solution)/shard_map/ppermute | solution.py:542
  88.6 4.8 %collective-permute-start.4 = (f32[64,128]{1,0:T(8,128)S(1)}, f32[64,128]{1,0:T(8,128)S(1)}, u32[]{:S(2)}, u32[]{:S(2)}) collective-permute-start(f32[64,128]{1,0:T(8,128)S(1)} %add.3.refs_0_), channel_id=1, source_target_pairs={{0,8},{4,12},{8,0},{12,4},{16,24},{20,28},{24,16},{28,20},{1,9},{5... | collective-permute-start | bytes 98312 | tf_op jit(solution)/shard_map/ppermute | solution.py:542

commit v26 on v24

--- a/solution.py
+++ b/solution.py
@@ -11,7 +11,7 @@
 LOC_RB = 2
 STEPS = 4
 UNROLL = 8
-NEAR_UNROLL = 4
+NEAR_UNROLL = 8
 KEPT = 16
 CHUNK = 4
 MERGE = 16

time: 98.1 us -> 98.4 us (level)
  Pallas kernels: 47.1 us -> 49.4 us
  starting transfers between devices: 38.7 us -> 37.1 us
    pallas_call x4, Pallas kernels: 14 us -> 15.3 us  [per_device(): pl.pallas_call(functools.partial(step_kernel, step), name='step', out_sha...]
    all_to_all x5, starting transfers between devices: 30.6 us -> 29.4 us  [exchange(): lax.all_to_all(x, 'blk', split_axis=0, concat_axis=0, tiled=True, axis_in...]
  transfers between devices with their start and end apart: 12 -> 12, of which waited for: 5 -> 5; matrix products, arithmetic and copies ran while one was open for 0% -> 0% of each run, Pallas kernels for 27% -> 28%
where the time goes in v26:
time: 98.4 us; the launch traced here: 97.8 us
  Pallas kernels  49.4 us (50%)
  starting transfers between devices  37.1 us (38%)
  waiting for transfers between devices  9.89 us (10%)
  local copies, waits for them, and re-layouts  1.25 us (1%)
    all_to_all x5, starting transfers between devices, exchange(): lax.all_to_all(x, 'blk', split_axis=0, concat_axis=0, tiled=True, axis_in...  29.4 us
    pallas_call x4, Pallas kernels, per_device(): pl.pallas_call(functools.partial(step_kernel, step), name='step', out_sha...  15.3 us
    pallas_call x4, Pallas kernels, per_device(): pl.pallas_call(functools.partial(near_kernel, step), name='near', out_sha...  15.3 us
    pallas_call x1, Pallas kernels, tiles_call(): pl.pallas_call(functools.partial(tiles_kernel, near_count), name='tiles',...  12.2 us
    ppermute x7, waiting for transfers between devices, to_partner(): return lax.ppermute(x, axis, [(i, i ^ mask) for i in range(n)])  9.88 us
    ppermute x7, starting transfers between devices, to_partner(): return lax.ppermute(x, axis, [(i, i ^ mask) for i in range(n)])  7.72 us
    pallas_call x1, Pallas kernels, per_device(): pl.pallas_call(functools.partial(factor_kernel, rows * nblk), name='facto...  4.79 us
  transfers between devices with their start and end apart: 12, of which 5 were waited for; matrix products, arithmetic and copies ran while one was open for 0% of the time, Pallas kernels for 28%

profile of v26, /device:TPU:0, one launch (start us, length us, event | category | flops | bytes accessed | tf_op | source)
XLA Modules:
  0.0 97.8 jit_solution(5969041202271422811)
XLA Ops:
  1.2 8.2 %all-to-all-start = ((s32[8,1,8]{2,1,0:T(1,128)}), s32[8,1,8]{2,1,0:T(1,128)S(1)}, u32[]{:S(2)}, u32[]{:S(2)}) async-start(s32[8,1,8]{2,1,0:T(1,128)} %broadcast_in_dim.9), calls=%async_computation | async-start | bytes 8192 | tf_op jit(solution)/shard_map/all_to_all | solution.py:537
  9.5 12.2 %tiles.1 = (f8e4m3fn[64,512,256]{2,1,0:T(32,128)(4,1)}, f8e4m3fn[16,512,256]{2,1,0:T(32,128)(4,1)S(1)}, f32[8,2048]{1,0:T(8,128)S(1)}, s32[128]{0:T(128)}) custom-call(s32[96]{0:T(128)} %rows_ref.7, s32[96]{0:T(128)} %slots_ref.7, bf16[96,256,256]{2,1,0:T(8,128)(2,1)} %real_hbm.9, bf16[96,256,256]{2,1,0:T(8,128)(2,1)} %imag_hbm.9), custom_call_target="tpu_custom_call" | custom-call | flops 268435456 | bytes 25165824 | tf_op jit(solution)/shard_map/tiles/pallas_call | solution.py:227
  23.1 5.1 %all-to-all-start.1 = ((bf16[8,32,256]{2,1,0:T(8,128)(2,1)}), bf16[8,32,256]{2,1,0:T(8,128)(2,1)S(1)}, u32[]{:S(2)}, u32[]{:S(2)}) async-start(bf16[8,32,256]{2,1,0:T(8,128)(2,1)} %first.1), calls=%async_computation.1 | async-start | bytes 262144 | tf_op jit(solution)/shard_map/all_to_all | solution.py:537
  28.2 3.8 %near.4.base_ref = f32[32,2048]{1,0:T(8,128)S(1)} custom-call(s32[96]{0:T(128)} %rows_ref.7, s32[96]{0:T(128)} %slots_ref.7, bf16[96,256,256]{2,1,0:T(8,128)(2,1)} %real_hbm.9, bf16[96,256,256]{2,1,0:T(8,128)(2,1)} %imag_hbm.9, f32[8,2048]{1,0:T(8,128)S(1)} %get-tuple-element.20.scale_ref, f32[32,2048]{1,0:T(8,128)S(1)} %copy-done, f32[32,2048]{1,0:T(8,128)S(1)} %copy-done), custom_call_target="tpu_custom_call" | custom-call | flops 268435456 | bytes 2097152 | tf_op jit(solution)/shard_map/near/pallas_call | solution.py:579
  32.0 4.0 %step.4 = (f32[32,2048]{1,0:T(8,128)S(1)}, bf16[8,32,256]{2,1,0:T(8,128)(2,1)}) custom-call(s32[128]{0:T(128)} %get-tuple-element.17.plan_ref, s32[8,1,8]{2,1,0:T(1,128)S(1)} %all-to-all-done.wanted_ref, f8e4m3fn[64,512,256]{2,1,0:T(32,128)(4,1)} %get-tuple-element.18.packed_hbm, f8e4m3fn[16,512,256]{2,1,0:T(32,128)(4,1)S(1)} %get-tuple-element.19.kept_ref, ...), custom_call_target="tpu_custom_call" | custom-call | tf_op jit(solution)/shard_map/step/pallas_call | solution.py:595
  36.0 5.4 %all-to-all-start.2 = ((bf16[8,32,256]{2,1,0:T(8,128)(2,1)}), bf16[8,32,256]{2,1,0:T(8,128)(2,1)S(1)}, u32[]{:S(2)}, u32[]{:S(2)}) async-start(bf16[8,32,256]{2,1,0:T(8,128)(2,1)} %get-tuple-element.22), calls=%async_computation.2 | async-start | bytes 262144 | tf_op jit(solution)/shard_map/all_to_all | solution.py:537
  41.4 3.8 %near.5.base_ref = f32[32,2048]{1,0:T(8,128)S(1)} custom-call(s32[96]{0:T(128)} %rows_ref.7, s32[96]{0:T(128)} %slots_ref.7, bf16[96,256,256]{2,1,0:T(8,128)(2,1)} %real_hbm.9, bf16[96,256,256]{2,1,0:T(8,128)(2,1)} %imag_hbm.9, f32[8,2048]{1,0:T(8,128)S(1)} %get-tuple-element.20.scale_ref, f32[32,2048]{1,0:T(8,128)S(1)} %get-tuple-element.21.now_ref.before_ref, ...), custom_call_target="tpu_custom_call" | custom-call | flops 268435456 | bytes 2097152 | tf_op jit(solution)/shard_map/near/pallas_call | solution.py:579
  45.2 4.0 %step.5 = (f32[32,2048]{1,0:T(8,128)S(1)}, bf16[8,32,256]{2,1,0:T(8,128)(2,1)}) custom-call(s32[128]{0:T(128)} %get-tuple-element.17.plan_ref, s32[8,1,8]{2,1,0:T(1,128)S(1)} %all-to-all-done.wanted_ref, f8e4m3fn[64,512,256]{2,1,0:T(32,128)(4,1)} %get-tuple-element.18.packed_hbm, f8e4m3fn[16,512,256]{2,1,0:T(32,128)(4,1)S(1)} %get-tuple-element.19.kept_ref, ...), custom_call_target="tpu_custom_call" | custom-call | tf_op jit(solution)/shard_map/step/pallas_call | solution.py:595
  49.3 5.3 %all-to-all-start.3 = ((bf16[8,32,256]{2,1,0:T(8,128)(2,1)}), bf16[8,32,256]{2,1,0:T(8,128)(2,1)S(1)}, u32[]{:S(2)}, u32[]{:S(2)}) async-start(bf16[8,32,256]{2,1,0:T(8,128)(2,1)} %get-tuple-element.24), calls=%async_computation.3 | async-start | bytes 262144 | tf_op jit(solution)/shard_map/all_to_all | solution.py:537
  54.6 3.8 %near.6.base_ref = f32[32,2048]{1,0:T(8,128)S(1)} custom-call(s32[96]{0:T(128)} %rows_ref.7, s32[96]{0:T(128)} %slots_ref.7, bf16[96,256,256]{2,1,0:T(8,128)(2,1)} %real_hbm.9, bf16[96,256,256]{2,1,0:T(8,128)(2,1)} %imag_hbm.9, f32[8,2048]{1,0:T(8,128)S(1)} %get-tuple-element.20.scale_ref, f32[32,2048]{1,0:T(8,128)S(1)} %get-tuple-element.23.now_ref.before_ref, ...), custom_call_target="tpu_custom_call" | custom-call | flops 268435456 | bytes 2097152 | tf_op jit(solution)/shard_map/near/pallas_call | solution.py:579
  58.5 4.0 %step.6 = (f32[32,2048]{1,0:T(8,128)S(1)}, bf16[8,32,256]{2,1,0:T(8,128)(2,1)}) custom-call(s32[128]{0:T(128)} %get-tuple-element.17.plan_ref, s32[8,1,8]{2,1,0:T(1,128)S(1)} %all-to-all-done.wanted_ref, f8e4m3fn[64,512,256]{2,1,0:T(32,128)(4,1)} %get-tuple-element.18.packed_hbm, f8e4m3fn[16,512,256]{2,1,0:T(32,128)(4,1)S(1)} %get-tuple-element.19.kept_ref, ...), custom_call_target="tpu_custom_call" | custom-call | tf_op jit(solution)/shard_map/step/pallas_call | solution.py:595
  62.5 5.3 %all-to-all-start.4 = ((bf16[8,32,256]{2,1,0:T(8,128)(2,1)}), bf16[8,32,256]{2,1,0:T(8,128)(2,1)S(1)}, u32[]{:S(2)}, u32[]{:S(2)}) async-start(bf16[8,32,256]{2,1,0:T(8,128)(2,1)} %get-tuple-element.26), calls=%async_computation.4 | async-start | bytes 262144 | tf_op jit(solution)/shard_map/all_to_all | solution.py:537
  67.8 3.8 %near.7.base_ref = f32[32,2048]{1,0:T(8,128)S(1)} custom-call(s32[96]{0:T(128)} %rows_ref.7, s32[96]{0:T(128)} %slots_ref.7, bf16[96,256,256]{2,1,0:T(8,128)(2,1)} %real_hbm.9, bf16[96,256,256]{2,1,0:T(8,128)(2,1)} %imag_hbm.9, f32[8,2048]{1,0:T(8,128)S(1)} %get-tuple-element.20.scale_ref, f32[32,2048]{1,0:T(8,128)S(1)} %get-tuple-element.25.now_ref, ...), custom_call_target="tpu_custom_call" | custom-call | flops 268435456 | bytes 2097152 | tf_op jit(solution)/shard_map/near/pallas_call | solution.py:579
  71.7 3.3 %step.7.own_ref = f32[32,2048]{1,0:T(8,128)S(1)} custom-call(s32[128]{0:T(128)} %get-tuple-element.17.plan_ref, s32[8,1,8]{2,1,0:T(1,128)S(1)} %all-to-all-done.wanted_ref, f8e4m3fn[64,512,256]{2,1,0:T(32,128)(4,1)} %get-tuple-element.18.packed_hbm, f8e4m3fn[16,512,256]{2,1,0:T(32,128)(4,1)S(1)} %get-tuple-element.19.kept_ref, ...), custom_call_target="tpu_custom_call" | custom-call | tf_op jit(solution)/shard_map/step/pallas_call | solution.py:595
  75.0 1.6 %collective-permute-start.1 = (bf16[32,2048]{1,0:T(8,128)(2,1)S(1)}, bf16[32,2048]{1,0:T(8,128)(2,1)S(1)}, u32[]{:S(2)}, u32[]{:S(2)}) collective-permute-start(bf16[32,2048]{1,0:T(8,128)(2,1)S(1)} %convert_element_type.3), channel_id=1, source_target_pairs={{0,2},{1,3},{2,0},{3,1},{4,6},{5,7},{6,4},{7,5},{8,10},{9,11},{10,... | collective-permute-start | bytes 393224 | tf_op jit(solution)/shard_map/ppermute | solution.py:542
  76.5 3.5 %collective-permute-done.1.refs_1_ = bf16[32,2048]{1,0:T(8,128)(2,1)S(1)} collective-permute-done((bf16[32,2048]{1,0:T(8,128)(2,1)S(1)}, bf16[32,2048]{1,0:T(8,128)(2,1)S(1)}, u32[]{:S(2)}, u32[]{:S(2)}) %collective-permute-start.1) | collective-permute-done | bytes 131104 | tf_op jit(solution)/shard_map/ppermute | solution.py:542
  80.0 1.3 %collective-permute-done.2.refs_2_ = bf16[32,2048]{1,0:T(8,128)(2,1)S(1)} collective-permute-done((bf16[32,2048]{1,0:T(8,128)(2,1)S(1)}, bf16[32,2048]{1,0:T(8,128)(2,1)S(1)}, u32[]{:S(2)}, u32[]{:S(2)}) %collective-permute-start.2) | collective-permute-done | bytes 131104 | tf_op jit(solution)/shard_map/ppermute | solution.py:542
  81.8 1.8 %collective-permute-start.3 = (f32[64,128]{1,0:T(8,128)S(1)}, f32[64,128]{1,0:T(8,128)S(1)}, u32[]{:S(2)}, u32[]{:S(2)}) collective-permute-start(f32[64,128]{1,0:T(8,128)S(1)} %get-tuple-element.28), channel_id=1, source_target_pairs={{0,4},{4,0},{8,12},{12,8},{16,20},{20,16},{24,28},{28,24},{1,5},{5... | collective-permute-start | bytes 98312 | tf_op jit(solution)/shard_map/ppermute | solution.py:542
  83.6 2.2 %collective-permute-done.3 = f32[64,128]{1,0:T(8,128)S(1)} collective-permute-done((f32[64,128]{1,0:T(8,128)S(1)}, f32[64,128]{1,0:T(8,128)S(1)}, u32[]{:S(2)}, u32[]{:S(2)}) %collective-permute-start.3) | collective-permute-done | bytes 32800 | tf_op jit(solution)/shard_map/ppermute | solution.py:542
  85.8 2.1 %collective-permute-start.6 = (f32[64,128]{1,0:T(8,128)S(1)}, f32[64,128]{1,0:T(8,128)S(1)}, u32[]{:S(2)}, u32[]{:S(2)}) collective-permute-start(f32[64,128]{1,0:T(8,128)S(1)} %add.3.refs_0_), channel_id=1, source_target_pairs={{0,24},{4,28},{8,16},{12,20},{16,8},{20,12},{24,0},{28,4},{1,25},{... | collective-permute-start | bytes 98312 | tf_op jit(solution)/shard_map/ppermute | solution.py:542
  88.2 1.9 %collective-permute-start.4 = (f32[64,128]{1,0:T(8,128)S(1)}, f32[64,128]{1,0:T(8,128)S(1)}, u32[]{:S(2)}, u32[]{:S(2)}) collective-permute-start(f32[64,128]{1,0:T(8,128)S(1)} %add.3.refs_0_), channel_id=1, source_target_pairs={{0,8},{4,12},{8,0},{12,4},{16,24},{20,28},{24,16},{28,20},{1,9},{5... | collective-permute-start | bytes 98312 | tf_op jit(solution)/shard_map/ppermute | solution.py:542
  90.2 1.5 %collective-permute-done.6.refs_3_ = f32[64,128]{1,0:T(8,128)S(1)} collective-permute-done((f32[64,128]{1,0:T(8,128)S(1)}, f32[64,128]{1,0:T(8,128)S(1)}, u32[]{:S(2)}, u32[]{:S(2)}) %collective-permute-start.6) | collective-permute-done | bytes 32800 | tf_op jit(solution)/shard_map/ppermute | solution.py:542
  91.6 1.4 %collective-permute-done.5.refs_2_ = f32[64,128]{1,0:T(8,128)S(1)} collective-permute-done((f32[64,128]{1,0:T(8,128)S(1)}, f32[64,128]{1,0:T(8,128)S(1)}, u32[]{:S(2)}, u32[]{:S(2)}) %collective-permute-start.5) | collective-permute-done | bytes 32800 | tf_op jit(solution)/shard_map/ppermute | solution.py:542
  93.0 4.8 %factor.1 = f32[32,2048]{1,0:T(8,128)} custom-call(f32[32,2048]{1,0:T(8,128)S(1)} %step.7.own_ref, bf16[4,32,2048]{2,1,0:T(8,128)(2,1)S(1)} %get-tuple-element.27.all_ref, f32[64,128]{1,0:T(8,128)S(1)} %add.3.refs_0_, f32[64,128]{1,0:T(8,128)S(1)} %collective-permute-done.4.refs_1_, f32[64,128]{1,0:T(8,128)S(1)} %collective-permute-done.5.refs_2_, ...), custom_call_target="tpu_custom_call" | custom-call | tf_op jit(solution)/shard_map/factor/pallas_call | solution.py:631
  (17 shorter events, 3.4 us)
Async XLA Ops:
  1.2 20.5 %all-to-all-start = ((s32[8,1,8]{2,1,0:T(1,128)}), s32[8,1,8]{2,1,0:T(1,128)S(1)}, u32[]{:S(2)}, u32[]{:S(2)}) async-start(s32[8,1,8]{2,1,0:T(1,128)} %broadcast_in_dim.9), calls=%async_computation | async-start | bytes 8192 | tf_op jit(solution)/shard_map/all_to_all | solution.py:537
  9.5 12.3 %copy-start = (f32[32,2048]{1,0:T(8,128)S(1)}, f32[32,2048]{1,0:T(8,128)}, u32[]{:S(2)}) copy-start(f32[32,2048]{1,0:T(8,128)} %before_ref.3) | copy-start | bytes 786436
  23.1 8.9 %all-to-all-start.1 = ((bf16[8,32,256]{2,1,0:T(8,128)(2,1)}), bf16[8,32,256]{2,1,0:T(8,128)(2,1)S(1)}, u32[]{:S(2)}, u32[]{:S(2)}) async-start(bf16[8,32,256]{2,1,0:T(8,128)(2,1)} %first.1), calls=%async_computation.1 | async-start | bytes 262144 | tf_op jit(solution)/shard_map/all_to_all | solution.py:537
  36.0 9.2 %all-to-all-start.2 = ((bf16[8,32,256]{2,1,0:T(8,128)(2,1)}), bf16[8,32,256]{2,1,0:T(8,128)(2,1)S(1)}, u32[]{:S(2)}, u32[]{:S(2)}) async-start(bf16[8,32,256]{2,1,0:T(8,128)(2,1)} %get-tuple-element.22), calls=%async_computation.2 | async-start | bytes 262144 | tf_op jit(solution)/shard_map/all_to_all | solution.py:537
  49.3 9.2 %all-to-all-start.3 = ((bf16[8,32,256]{2,1,0:T(8,128)(2,1)}), bf16[8,32,256]{2,1,0:T(8,128)(2,1)S(1)}, u32[]{:S(2)}, u32[]{:S(2)}) async-start(bf16[8,32,256]{2,1,0:T(8,128)(2,1)} %get-tuple-element.24), calls=%async_computation.3 | async-start | bytes 262144 | tf_op jit(solution)/shard_map/all_to_all | solution.py:537
  62.5 9.2 %all-to-all-start.4 = ((bf16[8,32,256]{2,1,0:T(8,128)(2,1)}), bf16[8,32,256]{2,1,0:T(8,128)(2,1)S(1)}, u32[]{:S(2)}, u32[]{:S(2)}) async-start(bf16[8,32,256]{2,1,0:T(8,128)(2,1)} %get-tuple-element.26), calls=%async_computation.4 | async-start | bytes 262144 | tf_op jit(solution)/shard_map/all_to_all | solution.py:537
  75.0 5.0 %collective-permute-start.1 = (bf16[32,2048]{1,0:T(8,128)(2,1)S(1)}, bf16[32,2048]{1,0:T(8,128)(2,1)S(1)}, u32[]{:S(2)}, u32[]{:S(2)}) collective-permute-start(bf16[32,2048]{1,0:T(8,128)(2,1)S(1)} %convert_element_type.3), channel_id=1, source_target_pairs={{0,2},{1,3},{2,0},{3,1},{4,6},{5,7},{6,4},{7,5},{8,10},{9,11},{10,... | collective-permute-start | bytes 393224 | tf_op jit(solution)/shard_map/ppermute | solution.py:542
  76.5 3.5 %collective-permute-start = (bf16[32,2048]{1,0:T(8,128)(2,1)S(1)}, bf16[32,2048]{1,0:T(8,128)(2,1)S(1)}, u32[]{:S(2)}, u32[]{:S(2)}) collective-permute-start(bf16[32,2048]{1,0:T(8,128)(2,1)S(1)} %convert_element_type.3), channel_id=1, source_target_pairs={{0,1},{1,0},{2,3},{3,2},{4,5},{5,4},{6,7},{7,6},{8,9},{9,8},{10,11... | collective-permute-start | bytes 393224 | tf_op jit(solution)/shard_map/ppermute | solution.py:542
  80.0 1.3 %collective-permute-start.2 = (bf16[32,2048]{1,0:T(8,128)(2,1)S(1)}, bf16[32,2048]{1,0:T(8,128)(2,1)S(1)}, u32[]{:S(2)}, u32[]{:S(2)}) collective-permute-start(bf16[32,2048]{1,0:T(8,128)(2,1)S(1)} %collective-permute-done.1.refs_1_), channel_id=1, source_target_pairs={{0,1},{1,0},{2,3},{3,2},{4,5},{5,4},{6,7},{7,6},{8,9},{9,8},{10,11... | collective-permute-start | bytes 393224 | tf_op jit(solution)/shard_map/ppermute | solution.py:542
  81.8 4.0 %collective-permute-start.3 = (f32[64,128]{1,0:T(8,128)S(1)}, f32[64,128]{1,0:T(8,128)S(1)}, u32[]{:S(2)}, u32[]{:S(2)}) collective-permute-start(f32[64,128]{1,0:T(8,128)S(1)} %get-tuple-element.28), channel_id=1, source_target_pairs={{0,4},{4,0},{8,12},{12,8},{16,20},{20,16},{24,28},{28,24},{1,5},{5... | collective-permute-start | bytes 98312 | tf_op jit(solution)/shard_map/ppermute | solution.py:542
  85.8 5.9 %collective-permute-start.6 = (f32[64,128]{1,0:T(8,128)S(1)}, f32[64,128]{1,0:T(8,128)S(1)}, u32[]{:S(2)}, u32[]{:S(2)}) collective-permute-start(f32[64,128]{1,0:T(8,128)S(1)} %add.3.refs_0_), channel_id=1, source_target_pairs={{0,24},{4,28},{8,16},{12,20},{16,8},{20,12},{24,0},{28,4},{1,25},{... | collective-permute-start | bytes 98312 | tf_op jit(solution)/shard_map/ppermute | solution.py:542
  87.8 5.2 %collective-permute-start.5 = (f32[64,128]{1,0:T(8,128)S(1)}, f32[64,128]{1,0:T(8,128)S(1)}, u32[]{:S(2)}, u32[]{:S(2)}) collective-permute-start(f32[64,128]{1,0:T(8,128)S(1)} %add.3.refs_0_), channel_id=1, source_target_pairs={{0,16},{4,20},{8,24},{12,28},{16,0},{20,4},{24,8},{28,12},{1,17},{... | collective-permute-start | bytes 98312 | tf_op jit(solution)/shard_map/ppermute | solution.py:542
  88.2 4.8 %collective-permute-start.4 = (f32[64,128]{1,0:T(8,128)S(1)}, f32[64,128]{1,0:T(8,128)S(1)}, u32[]{:S(2)}, u32[]{:S(2)}) collective-permute-start(f32[64,128]{1,0:T(8,128)S(1)} %add.3.refs_0_), channel_id=1, source_target_pairs={{0,8},{4,12},{8,0},{12,4},{16,24},{20,28},{24,16},{28,20},{1,9},{5... | collective-permute-start | bytes 98312 | tf_op jit(solution)/shard_map/ppermute | solution.py:542

commit v27 on v24

--- a/solution.py
+++ b/solution.py
@@ -13,7 +13,7 @@
 UNROLL = 8
 NEAR_UNROLL = 4
 KEPT = 16
-CHUNK = 4
+CHUNK = 8
 MERGE = 16
 TOP = 7.0
 FINER = 16.0

time: 98.1 us -> 98 us (level)
  no operation moved by 1% of the time
where the time goes in v27:
time: 98 us; the launch traced here: 97.1 us
  Pallas kernels  47.2 us (48%)
  starting transfers between devices  38.7 us (39%)
  waiting for transfers between devices  9.7 us (10%)
  local copies, waits for them, and re-layouts  1.25 us (1%)
    all_to_all x5, starting transfers between devices, exchange(): lax.all_to_all(x, 'blk', split_axis=0, concat_axis=0, tiled=True, axis_in...  30.6 us
    pallas_call x4, Pallas kernels, per_device(): pl.pallas_call(functools.partial(near_kernel, step), name='near', out_sha...  15 us
    pallas_call x4, Pallas kernels, per_device(): pl.pallas_call(functools.partial(step_kernel, step), name='step', out_sha...  14 us
    pallas_call x1, Pallas kernels, tiles_call(): pl.pallas_call(functools.partial(tiles_kernel, near_count), name='tiles',...  11.7 us
    ppermute x7, waiting for transfers between devices, to_partner(): return lax.ppermute(x, axis, [(i, i ^ mask) for i in range(n)])  9.68 us
    ppermute x7, starting transfers between devices, to_partner(): return lax.ppermute(x, axis, [(i, i ^ mask) for i in range(n)])  8.12 us
    pallas_call x1, Pallas kernels, per_device(): pl.pallas_call(functools.partial(factor_kernel, rows * nblk), name='facto...  4.79 us
  transfers between devices with their start and end apart: 12, of which 5 were waited for; matrix products, arithmetic and copies ran while one was open for 0% of the time, Pallas kernels for 27%

profile of v27, /device:TPU:0, one launch (start us, length us, event | category | flops | bytes accessed | tf_op | source)
XLA Modules:
  0.0 97.1 jit_solution(9914483337615641246)
XLA Ops:
  1.2 8.2 %all-to-all-start = ((s32[8,1,8]{2,1,0:T(1,128)}), s32[8,1,8]{2,1,0:T(1,128)S(1)}, u32[]{:S(2)}, u32[]{:S(2)}) async-start(s32[8,1,8]{2,1,0:T(1,128)} %broadcast_in_dim.9), calls=%async_computation | async-start | bytes 8192 | tf_op jit(solution)/shard_map/all_to_all | solution.py:537
  9.5 11.7 %tiles.1 = (f8e4m3fn[64,512,256]{2,1,0:T(32,128)(4,1)}, f8e4m3fn[16,512,256]{2,1,0:T(32,128)(4,1)S(1)}, f32[8,2048]{1,0:T(8,128)S(1)}, s32[128]{0:T(128)}) custom-call(s32[96]{0:T(128)} %rows_ref.7, s32[96]{0:T(128)} %slots_ref.7, bf16[96,256,256]{2,1,0:T(8,128)(2,1)} %real_hbm.9, bf16[96,256,256]{2,1,0:T(8,128)(2,1)} %imag_hbm.9), custom_call_target="tpu_custom_call" | custom-call | flops 268435456 | bytes 25165824 | tf_op jit(solution)/shard_map/tiles/pallas_call | solution.py:227
  21.2 1.3 %first.1 = bf16[8,32,256]{2,1,0:T(8,128)(2,1)} custom-call(f32[32,2048]{1,0:T(8,128)S(1)} %copy-done, f32[8,2048]{1,0:T(8,128)S(1)} %get-tuple-element.20.scale_ref, s32[8,1,8]{2,1,0:T(1,128)S(1)} %all-to-all-done.wanted_ref), custom_call_target="tpu_custom_call" | custom-call | tf_op jit(solution)/shard_map/first/pallas_call | solution.py:565
  22.5 5.1 %all-to-all-start.1 = ((bf16[8,32,256]{2,1,0:T(8,128)(2,1)}), bf16[8,32,256]{2,1,0:T(8,128)(2,1)S(1)}, u32[]{:S(2)}, u32[]{:S(2)}) async-start(bf16[8,32,256]{2,1,0:T(8,128)(2,1)} %first.1), calls=%async_computation.1 | async-start | bytes 262144 | tf_op jit(solution)/shard_map/all_to_all | solution.py:537
  27.6 3.7 %near.4.base_ref = f32[32,2048]{1,0:T(8,128)S(1)} custom-call(s32[96]{0:T(128)} %rows_ref.7, s32[96]{0:T(128)} %slots_ref.7, bf16[96,256,256]{2,1,0:T(8,128)(2,1)} %real_hbm.9, bf16[96,256,256]{2,1,0:T(8,128)(2,1)} %imag_hbm.9, f32[8,2048]{1,0:T(8,128)S(1)} %get-tuple-element.20.scale_ref, f32[32,2048]{1,0:T(8,128)S(1)} %copy-done, f32[32,2048]{1,0:T(8,128)S(1)} %copy-done), custom_call_target="tpu_custom_call" | custom-call | flops 268435456 | bytes 2097152 | tf_op jit(solution)/shard_map/near/pallas_call | solution.py:579
  31.4 3.7 %step.4 = (f32[32,2048]{1,0:T(8,128)S(1)}, bf16[8,32,256]{2,1,0:T(8,128)(2,1)}) custom-call(s32[128]{0:T(128)} %get-tuple-element.17.plan_ref, s32[8,1,8]{2,1,0:T(1,128)S(1)} %all-to-all-done.wanted_ref, f8e4m3fn[64,512,256]{2,1,0:T(32,128)(4,1)} %get-tuple-element.18.packed_hbm, f8e4m3fn[16,512,256]{2,1,0:T(32,128)(4,1)S(1)} %get-tuple-element.19.kept_ref, ...), custom_call_target="tpu_custom_call" | custom-call | tf_op jit(solution)/shard_map/step/pallas_call | solution.py:595
  35.1 5.8 %all-to-all-start.2 = ((bf16[8,32,256]{2,1,0:T(8,128)(2,1)}), bf16[8,32,256]{2,1,0:T(8,128)(2,1)S(1)}, u32[]{:S(2)}, u32[]{:S(2)}) async-start(bf16[8,32,256]{2,1,0:T(8,128)(2,1)} %get-tuple-element.22), calls=%async_computation.2 | async-start | bytes 262144 | tf_op jit(solution)/shard_map/all_to_all | solution.py:537
  40.8 3.8 %near.5.base_ref = f32[32,2048]{1,0:T(8,128)S(1)} custom-call(s32[96]{0:T(128)} %rows_ref.7, s32[96]{0:T(128)} %slots_ref.7, bf16[96,256,256]{2,1,0:T(8,128)(2,1)} %real_hbm.9, bf16[96,256,256]{2,1,0:T(8,128)(2,1)} %imag_hbm.9, f32[8,2048]{1,0:T(8,128)S(1)} %get-tuple-element.20.scale_ref, f32[32,2048]{1,0:T(8,128)S(1)} %get-tuple-element.21.now_ref.before_ref, ...), custom_call_target="tpu_custom_call" | custom-call | flops 268435456 | bytes 2097152 | tf_op jit(solution)/shard_map/near/pallas_call | solution.py:579
  44.6 3.7 %step.5 = (f32[32,2048]{1,0:T(8,128)S(1)}, bf16[8,32,256]{2,1,0:T(8,128)(2,1)}) custom-call(s32[128]{0:T(128)} %get-tuple-element.17.plan_ref, s32[8,1,8]{2,1,0:T(1,128)S(1)} %all-to-all-done.wanted_ref, f8e4m3fn[64,512,256]{2,1,0:T(32,128)(4,1)} %get-tuple-element.18.packed_hbm, f8e4m3fn[16,512,256]{2,1,0:T(32,128)(4,1)S(1)} %get-tuple-element.19.kept_ref, ...), custom_call_target="tpu_custom_call" | custom-call | tf_op jit(solution)/shard_map/step/pallas_call | solution.py:595
  48.3 5.7 %all-to-all-start.3 = ((bf16[8,32,256]{2,1,0:T(8,128)(2,1)}), bf16[8,32,256]{2,1,0:T(8,128)(2,1)S(1)}, u32[]{:S(2)}, u32[]{:S(2)}) async-start(bf16[8,32,256]{2,1,0:T(8,128)(2,1)} %get-tuple-element.24), calls=%async_computation.3 | async-start | bytes 262144 | tf_op jit(solution)/shard_map/all_to_all | solution.py:537
  54.0 3.8 %near.6.base_ref = f32[32,2048]{1,0:T(8,128)S(1)} custom-call(s32[96]{0:T(128)} %rows_ref.7, s32[96]{0:T(128)} %slots_ref.7, bf16[96,256,256]{2,1,0:T(8,128)(2,1)} %real_hbm.9, bf16[96,256,256]{2,1,0:T(8,128)(2,1)} %imag_hbm.9, f32[8,2048]{1,0:T(8,128)S(1)} %get-tuple-element.20.scale_ref, f32[32,2048]{1,0:T(8,128)S(1)} %get-tuple-element.23.now_ref.before_ref, ...), custom_call_target="tpu_custom_call" | custom-call | flops 268435456 | bytes 2097152 | tf_op jit(solution)/shard_map/near/pallas_call | solution.py:579
  57.8 3.7 %step.6 = (f32[32,2048]{1,0:T(8,128)S(1)}, bf16[8,32,256]{2,1,0:T(8,128)(2,1)}) custom-call(s32[128]{0:T(128)} %get-tuple-element.17.plan_ref, s32[8,1,8]{2,1,0:T(1,128)S(1)} %all-to-all-done.wanted_ref, f8e4m3fn[64,512,256]{2,1,0:T(32,128)(4,1)} %get-tuple-element.18.packed_hbm, f8e4m3fn[16,512,256]{2,1,0:T(32,128)(4,1)S(1)} %get-tuple-element.19.kept_ref, ...), custom_call_target="tpu_custom_call" | custom-call | tf_op jit(solution)/shard_map/step/pallas_call | solution.py:595
  61.5 5.7 %all-to-all-start.4 = ((bf16[8,32,256]{2,1,0:T(8,128)(2,1)}), bf16[8,32,256]{2,1,0:T(8,128)(2,1)S(1)}, u32[]{:S(2)}, u32[]{:S(2)}) async-start(bf16[8,32,256]{2,1,0:T(8,128)(2,1)} %get-tuple-element.26), calls=%async_computation.4 | async-start | bytes 262144 | tf_op jit(solution)/shard_map/all_to_all | solution.py:537
  67.3 3.7 %near.7.base_ref = f32[32,2048]{1,0:T(8,128)S(1)} custom-call(s32[96]{0:T(128)} %rows_ref.7, s32[96]{0:T(128)} %slots_ref.7, bf16[96,256,256]{2,1,0:T(8,128)(2,1)} %real_hbm.9, bf16[96,256,256]{2,1,0:T(8,128)(2,1)} %imag_hbm.9, f32[8,2048]{1,0:T(8,128)S(1)} %get-tuple-element.20.scale_ref, f32[32,2048]{1,0:T(8,128)S(1)} %get-tuple-element.25.now_ref, ...), custom_call_target="tpu_custom_call" | custom-call | flops 268435456 | bytes 2097152 | tf_op jit(solution)/shard_map/near/pallas_call | solution.py:579
  71.0 3.0 %step.7.own_ref = f32[32,2048]{1,0:T(8,128)S(1)} custom-call(s32[128]{0:T(128)} %get-tuple-element.17.plan_ref, s32[8,1,8]{2,1,0:T(1,128)S(1)} %all-to-all-done.wanted_ref, f8e4m3fn[64,512,256]{2,1,0:T(32,128)(4,1)} %get-tuple-element.18.packed_hbm, f8e4m3fn[16,512,256]{2,1,0:T(32,128)(4,1)S(1)} %get-tuple-element.19.kept_ref, ...), custom_call_target="tpu_custom_call" | custom-call | tf_op jit(solution)/shard_map/step/pallas_call | solution.py:595
  74.0 1.6 %collective-permute-start.1 = (bf16[32,2048]{1,0:T(8,128)(2,1)S(1)}, bf16[32,2048]{1,0:T(8,128)(2,1)S(1)}, u32[]{:S(2)}, u32[]{:S(2)}) collective-permute-start(bf16[32,2048]{1,0:T(8,128)(2,1)S(1)} %convert_element_type.3), channel_id=1, source_target_pairs={{0,2},{1,3},{2,0},{3,1},{4,6},{5,7},{6,4},{7,5},{8,10},{9,11},{10,... | collective-permute-start | bytes 393224 | tf_op jit(solution)/shard_map/ppermute | solution.py:542
  75.6 3.5 %collective-permute-done.1.refs_1_ = bf16[32,2048]{1,0:T(8,128)(2,1)S(1)} collective-permute-done((bf16[32,2048]{1,0:T(8,128)(2,1)S(1)}, bf16[32,2048]{1,0:T(8,128)(2,1)S(1)}, u32[]{:S(2)}, u32[]{:S(2)}) %collective-permute-start.1) | collective-permute-done | bytes 131104 | tf_op jit(solution)/shard_map/ppermute | solution.py:542
  79.1 1.3 %collective-permute-done.2.refs_2_ = bf16[32,2048]{1,0:T(8,128)(2,1)S(1)} collective-permute-done((bf16[32,2048]{1,0:T(8,128)(2,1)S(1)}, bf16[32,2048]{1,0:T(8,128)(2,1)S(1)}, u32[]{:S(2)}, u32[]{:S(2)}) %collective-permute-start.2) | collective-permute-done | bytes 131104 | tf_op jit(solution)/shard_map/ppermute | solution.py:542
  80.8 2.2 %collective-permute-start.3 = (f32[64,128]{1,0:T(8,128)S(1)}, f32[64,128]{1,0:T(8,128)S(1)}, u32[]{:S(2)}, u32[]{:S(2)}) collective-permute-start(f32[64,128]{1,0:T(8,128)S(1)} %get-tuple-element.28), channel_id=1, source_target_pairs={{0,4},{4,0},{8,12},{12,8},{16,20},{20,16},{24,28},{28,24},{1,5},{5... | collective-permute-start | bytes 98312 | tf_op jit(solution)/shard_map/ppermute | solution.py:542
  83.0 1.9 %collective-permute-done.3 = f32[64,128]{1,0:T(8,128)S(1)} collective-permute-done((f32[64,128]{1,0:T(8,128)S(1)}, f32[64,128]{1,0:T(8,128)S(1)}, u32[]{:S(2)}, u32[]{:S(2)}) %collective-permute-start.3) | collective-permute-done | bytes 32800 | tf_op jit(solution)/shard_map/ppermute | solution.py:542
  84.9 2.4 %collective-permute-start.6 = (f32[64,128]{1,0:T(8,128)S(1)}, f32[64,128]{1,0:T(8,128)S(1)}, u32[]{:S(2)}, u32[]{:S(2)}) collective-permute-start(f32[64,128]{1,0:T(8,128)S(1)} %add.3.refs_0_), channel_id=1, source_target_pairs={{0,24},{4,28},{8,16},{12,20},{16,8},{20,12},{24,0},{28,4},{1,25},{... | collective-permute-start | bytes 98312 | tf_op jit(solution)/shard_map/ppermute | solution.py:542
  87.7 1.6 %collective-permute-start.4 = (f32[64,128]{1,0:T(8,128)S(1)}, f32[64,128]{1,0:T(8,128)S(1)}, u32[]{:S(2)}, u32[]{:S(2)}) collective-permute-start(f32[64,128]{1,0:T(8,128)S(1)} %add.3.refs_0_), channel_id=1, source_target_pairs={{0,8},{4,12},{8,0},{12,4},{16,24},{20,28},{24,16},{28,20},{1,9},{5... | collective-permute-start | bytes 98312 | tf_op jit(solution)/shard_map/ppermute | solution.py:542
  90.6 1.7 %collective-permute-done.5.refs_2_ = f32[64,128]{1,0:T(8,128)S(1)} collective-permute-done((f32[64,128]{1,0:T(8,128)S(1)}, f32[64,128]{1,0:T(8,128)S(1)}, u32[]{:S(2)}, u32[]{:S(2)}) %collective-permute-start.5) | collective-permute-done | bytes 32800 | tf_op jit(solution)/shard_map/ppermute | solution.py:542
  92.3 4.8 %factor.1 = f32[32,2048]{1,0:T(8,128)} custom-call(f32[32,2048]{1,0:T(8,128)S(1)} %step.7.own_ref, bf16[4,32,2048]{2,1,0:T(8,128)(2,1)S(1)} %get-tuple-element.27.all_ref, f32[64,128]{1,0:T(8,128)S(1)} %add.3.refs_0_, f32[64,128]{1,0:T(8,128)S(1)} %collective-permute-done.4.refs_1_, f32[64,128]{1,0:T(8,128)S(1)} %collective-permute-done.5.refs_2_, ...), custom_call_target="tpu_custom_call" | custom-call | tf_op jit(solution)/shard_map/factor/pallas_call | solution.py:631
  (17 shorter events, 3.4 us)
Async XLA Ops:
  1.2 19.9 %all-to-all-start = ((s32[8,1,8]{2,1,0:T(1,128)}), s32[8,1,8]{2,1,0:T(1,128)S(1)}, u32[]{:S(2)}, u32[]{:S(2)}) async-start(s32[8,1,8]{2,1,0:T(1,128)} %broadcast_in_dim.9), calls=%async_computation | async-start | bytes 8192 | tf_op jit(solution)/shard_map/all_to_all | solution.py:537
  9.5 11.7 %copy-start = (f32[32,2048]{1,0:T(8,128)S(1)}, f32[32,2048]{1,0:T(8,128)}, u32[]{:S(2)}) copy-start(f32[32,2048]{1,0:T(8,128)} %before_ref.3) | copy-start | bytes 786436
  22.5 8.9 %all-to-all-start.1 = ((bf16[8,32,256]{2,1,0:T(8,128)(2,1)}), bf16[8,32,256]{2,1,0:T(8,128)(2,1)S(1)}, u32[]{:S(2)}, u32[]{:S(2)}) async-start(bf16[8,32,256]{2,1,0:T(8,128)(2,1)} %first.1), calls=%async_computation.1 | async-start | bytes 262144 | tf_op jit(solution)/shard_map/all_to_all | solution.py:537
  35.1 9.5 %all-to-all-start.2 = ((bf16[8,32,256]{2,1,0:T(8,128)(2,1)}), bf16[8,32,256]{2,1,0:T(8,128)(2,1)S(1)}, u32[]{:S(2)}, u32[]{:S(2)}) async-start(bf16[8,32,256]{2,1,0:T(8,128)(2,1)} %get-tuple-element.22), calls=%async_computation.2 | async-start | bytes 262144 | tf_op jit(solution)/shard_map/all_to_all | solution.py:537
  48.3 9.5 %all-to-all-start.3 = ((bf16[8,32,256]{2,1,0:T(8,128)(2,1)}), bf16[8,32,256]{2,1,0:T(8,128)(2,1)S(1)}, u32[]{:S(2)}, u32[]{:S(2)}) async-start(bf16[8,32,256]{2,1,0:T(8,128)(2,1)} %get-tuple-element.24), calls=%async_computation.3 | async-start | bytes 262144 | tf_op jit(solution)/shard_map/all_to_all | solution.py:537
  61.5 9.5 %all-to-all-start.4 = ((bf16[8,32,256]{2,1,0:T(8,128)(2,1)}), bf16[8,32,256]{2,1,0:T(8,128)(2,1)S(1)}, u32[]{:S(2)}, u32[]{:S(2)}) async-start(bf16[8,32,256]{2,1,0:T(8,128)(2,1)} %get-tuple-element.26), calls=%async_computation.4 | async-start | bytes 262144 | tf_op jit(solution)/shard_map/all_to_all | solution.py:537
  74.0 5.0 %collective-permute-start.1 = (bf16[32,2048]{1,0:T(8,128)(2,1)S(1)}, bf16[32,2048]{1,0:T(8,128)(2,1)S(1)}, u32[]{:S(2)}, u32[]{:S(2)}) collective-permute-start(bf16[32,2048]{1,0:T(8,128)(2,1)S(1)} %convert_element_type.3), channel_id=1, source_target_pairs={{0,2},{1,3},{2,0},{3,1},{4,6},{5,7},{6,4},{7,5},{8,10},{9,11},{10,... | collective-permute-start | bytes 393224 | tf_op jit(solution)/shard_map/ppermute | solution.py:542
  75.6 3.5 %collective-permute-start = (bf16[32,2048]{1,0:T(8,128)(2,1)S(1)}, bf16[32,2048]{1,0:T(8,128)(2,1)S(1)}, u32[]{:S(2)}, u32[]{:S(2)}) collective-permute-start(bf16[32,2048]{1,0:T(8,128)(2,1)S(1)} %convert_element_type.3), channel_id=1, source_target_pairs={{0,1},{1,0},{2,3},{3,2},{4,5},{5,4},{6,7},{7,6},{8,9},{9,8},{10,11... | collective-permute-start | bytes 393224 | tf_op jit(solution)/shard_map/ppermute | solution.py:542
  79.1 1.3 %collective-permute-start.2 = (bf16[32,2048]{1,0:T(8,128)(2,1)S(1)}, bf16[32,2048]{1,0:T(8,128)(2,1)S(1)}, u32[]{:S(2)}, u32[]{:S(2)}) collective-permute-start(bf16[32,2048]{1,0:T(8,128)(2,1)S(1)} %collective-permute-done.1.refs_1_), channel_id=1, source_target_pairs={{0,1},{1,0},{2,3},{3,2},{4,5},{5,4},{6,7},{7,6},{8,9},{9,8},{10,11... | collective-permute-start | bytes 393224 | tf_op jit(solution)/shard_map/ppermute | solution.py:542
  80.8 4.1 %collective-permute-start.3 = (f32[64,128]{1,0:T(8,128)S(1)}, f32[64,128]{1,0:T(8,128)S(1)}, u32[]{:S(2)}, u32[]{:S(2)}) collective-permute-start(f32[64,128]{1,0:T(8,128)S(1)} %get-tuple-element.28), channel_id=1, source_target_pairs={{0,4},{4,0},{8,12},{12,8},{16,20},{20,16},{24,28},{28,24},{1,5},{5... | collective-permute-start | bytes 98312 | tf_op jit(solution)/shard_map/ppermute | solution.py:542
  84.9 5.7 %collective-permute-start.6 = (f32[64,128]{1,0:T(8,128)S(1)}, f32[64,128]{1,0:T(8,128)S(1)}, u32[]{:S(2)}, u32[]{:S(2)}) collective-permute-start(f32[64,128]{1,0:T(8,128)S(1)} %add.3.refs_0_), channel_id=1, source_target_pairs={{0,24},{4,28},{8,16},{12,20},{16,8},{20,12},{24,0},{28,4},{1,25},{... | collective-permute-start | bytes 98312 | tf_op jit(solution)/shard_map/ppermute | solution.py:542
  87.3 5.0 %collective-permute-start.5 = (f32[64,128]{1,0:T(8,128)S(1)}, f32[64,128]{1,0:T(8,128)S(1)}, u32[]{:S(2)}, u32[]{:S(2)}) collective-permute-start(f32[64,128]{1,0:T(8,128)S(1)} %add.3.refs_0_), channel_id=1, source_target_pairs={{0,16},{4,20},{8,24},{12,28},{16,0},{20,4},{24,8},{28,12},{1,17},{... | collective-permute-start | bytes 98312 | tf_op jit(solution)/shard_map/ppermute | solution.py:542
  87.7 4.6 %collective-permute-start.4 = (f32[64,128]{1,0:T(8,128)S(1)}, f32[64,128]{1,0:T(8,128)S(1)}, u32[]{:S(2)}, u32[]{:S(2)}) collective-permute-start(f32[64,128]{1,0:T(8,128)S(1)} %add.3.refs_0_), channel_id=1, source_target_pairs={{0,8},{4,12},{8,0},{12,4},{16,24},{20,28},{24,16},{28,20},{1,9},{5... | collective-permute-start | bytes 98312 | tf_op jit(solution)/shard_map/ppermute | solution.py:542
